TPU v7x, 32 devices: a whole 2x2x4 slice. The times are simulated.
32 devices in a mesh: pb: 4 (over x, core), lab: 8 (over z, y).
Axes of the slice: x: 2, y: 2, z: 4, core: 2. Of those that a mesh axis runs over, the one named last changes fastest.
Arguments:
- queries: bfloat16 [1024, 768], P(('pb', 'lab')), may hold values from -6 to 6
- label_weights: bfloat16 [8192, 768], P('lab'), may hold values from -0.21875 to 0.21875
- sibling_blocks: int32 [1024, 8], P('pb'), may hold values from 0 to 63, as said below
- positive_slot: int32 [1024], P('pb'), may hold values from 0 to 1023
Outputs:
- query_grad: float32 [1024, 768], P(('pb', 'lab'))
- weight_grad: bfloat16 [8192, 768], P('lab')
Inputs may be any that keep to these rules, and one draw needn't show every extreme that they name: `sibling_blocks`: each row names 8 different cluster blocks, lying in 8 different runs of 8 blocks (block // 8 differs). Rows are taken in aligned runs of 32 (one device's queries): within each run, exactly 32 rows name a block of each run of 8 blocks. Within each query group (aligned blocks of 256 rows) no block is named by more than 32 rows, and some block is named by exactly 32 rows.
All inputs are finite; a program needn't handle non-finite values.
Results may differ from a plain program's by a relative error of at most 0.0047.
Values may be sent and summed in bfloat16 or wider, within the bound.
No kernel may reach another device: no remote copies, remote signals or barrier semaphores. Data moves between devices by JAX's collectives and lax.ppermute only.
A program may use at most 64 MiB of HBM per device.

v0:
```python
import jax
import jax.numpy as jnp
from jax import lax
from jax.sharding import PartitionSpec as P

BLOCK = 128
K = 8


def pack_index(touched, width_slots, fill_value):
    homes, count = touched.shape
    rank = jnp.cumsum(touched.astype(jnp.int32), axis=1) - 1
    place = jnp.where(touched, rank, width_slots)
    home_ids = jnp.broadcast_to(jnp.arange(homes, dtype=jnp.int32)[:, None], touched.shape)
    row_ids = jnp.broadcast_to(jnp.arange(count, dtype=jnp.int32)[None, :], touched.shape)
    table = (
        jnp.full((homes, width_slots + 1), fill_value, jnp.int32).at[home_ids, place].set(row_ids)
    )
    return table[:, :width_slots]


def shards(queries, label_weights, sibling_blocks, positive_slot):
    width = queries.shape[1]
    qcount = sibling_blocks.shape[0]
    lab_dev = label_weights.shape[0]
    blocks_dev = lab_dev // BLOCK
    first = lax.axis_index("lab") * blocks_dev
    local_ids = first + jnp.arange(blocks_dev, dtype=jnp.int32)
    pblock = jnp.take_along_axis(sibling_blocks, (positive_slot // BLOCK)[:, None], axis=1)[:, 0]
    positive = pblock * BLOCK + positive_slot % BLOCK
    label_ids = local_ids[:, None] * BLOCK + jnp.arange(BLOCK, dtype=jnp.int32)[None, :]
    chosen_all = jnp.any(sibling_blocks[:, :, None] == local_ids[None, None, :], axis=1)
    piece = lax.all_gather(queries, "lab", axis=0, tiled=True)
    count = piece.shape[0]
    scores = jnp.dot(piece, label_weights.T, preferred_element_type=jnp.float32)
    scores = scores.reshape(count, blocks_dev, BLOCK)
    target = (label_ids[None, :, :] == positive[:, None, None]).astype(jnp.float32)
    slope = jnp.where(chosen_all[:, :, None], jax.nn.sigmoid(scores) - target, 0.0)
    slope = slope.astype(jnp.bfloat16).reshape(count, lab_dev)
    dq_rows = jnp.dot(slope, label_weights, preferred_element_type=jnp.float32)
    dq_all = dq_rows
    w_acc = lax.dot_general(
        slope, piece, (((0,), (0,)), ((), ())), preferred_element_type=jnp.float32
    )
    dq_all, w_acc = (dq_all, w_acc)
    homes = lax.axis_size("lab")
    q_home = qcount // homes
    slots = q_home * K // homes
    touched = jnp.any(chosen_all, axis=1).reshape(homes, q_home)
    send_idx = pack_index(touched, slots, q_home)
    padded = jnp.concatenate(
        [dq_all.reshape(homes, q_home, width), jnp.zeros((homes, 1, width), jnp.float32)], axis=1
    )
    outgoing = jnp.take_along_axis(padded, send_idx[:, :, None], axis=1)
    incoming = lax.all_to_all(outgoing, "lab", split_axis=0, concat_axis=0, tiled=True)
    own_blocks = lax.dynamic_slice_in_dim(sibling_blocks, lax.axis_index("lab") * q_home, q_home, 0)
    source_ids = jnp.arange(homes, dtype=jnp.int32)
    own_touch = jnp.any(
        (own_blocks // blocks_dev)[:, :, None] == source_ids[None, None, :], axis=1
    ).T
    recv_idx = pack_index(own_touch, slots, q_home)
    query_grad = (
        jnp.zeros((q_home + 1, width), jnp.float32)
        .at[recv_idx.reshape(-1)]
        .add(incoming.reshape(-1, width))[:q_home]
    )
    groups = lax.axis_size("pb")
    total = lax.psum(w_acc, "pb")
    weight_grad = (total / groups).astype(jnp.bfloat16)
    return (query_grad, weight_grad)


def solution(mesh):
    in_specs = (P(("pb", "lab"), None), P("lab", None), P("pb", None), P("pb"))
    out_specs = (P(("pb", "lab"), None), P("lab", None))
    return jax.shard_map(shards, mesh=mesh, in_specs=in_specs, out_specs=out_specs, check_vma=False)
```

profile of v0, /device:TPU:0, one launch (start us, length us, event | category | flops | bytes accessed | tf_op | source)
XLA Modules:
  0.0 128.3 jit_solution(11595944490526725456)
XLA Ops:
  7.2 0.8 compare_select_fusion.4
  8.1 2.3 %gather_fusion = s32[256]{0:T(256)S(1)} fusion(s32[256,8]{0,1:T(8,128)} %param.6, s32[256]{0:T(256)S(1)} %bitcast.42), kind=kCustom, calls=%fused_computation | custom fusion | bytes 4096 | tf_op jit(solution)/shard_map/jit(take_along_axis)/gather | solution.py:29
  10.4 0.7 fusion.23
  11.0 0.8 compare_reduce_fusion.1
  11.9 0.2 copy.18
  12.1 33.0 %all_gather.3 = bf16[256,768]{1,0:T(8,128)(2,1)S(1)} all-gather(bf16[32,768]{1,0:T(8,128)(2,1)} %param.4), channel_id=1, replica_groups=mesh['pb'=4,'lab'=8] {'lab'}, dimensions={0}, use_global_device_ids=true | all-gather | bytes 442368 | tf_op jit(solution)/shard_map/all_gather | solution.py:33
  45.1 0.3 broadcast_in_dim.88
  45.4 0.8 fusion.7
  46.2 2.3 %fusion.28 = f32[1024,768]{1,0:T(8,128)} fusion(bf16[256,1024]{1,0:T(8,128)(2,1)S(1)} %fusion.7, bf16[256,768]{1,0:T(8,128)(2,1)S(1)} %all_gather.3), kind=kOutput, calls=%fused_computation.71 | convolution fusion | flops 402653184 | bytes 4063232 | tf_op jit(solution)/shard_map/dot_general | solution.py:42
  48.7 0.1 copy.16
  48.9 1.9 %fusion.27 = s32[8,32,1]{2,0,1:T(8,128)S(1)} fusion(s32[8,32,1]{2,0,1:T(8,128)S(1)} %copy.16), kind=kOutput, calls=%fused_computation.70 | output fusion | flops 7936 | bytes 2048 | tf_op jit(solution)/shard_map/jit(cumsum)/reduce_window_sum | solution.py:12
  51.0 11.2 %scatter_fusion.1 = s32[8,33]{1,0:T(8,128)S(1)} fusion(s32[8,33]{1,0:T(8,128)S(1)} %broadcast.170.clone.1, s32[256]{0:T(256)S(1)} %reshape.180, s32[256]{0:T(256)S(1)} %reshape.176), kind=kCustom, calls=%fused_computation.3 | custom fusion | bytes 5120 | tf_op jit(solution)/shard_map/scatter | solution.py:17
  62.3 0.6 fusion
  62.9 0.5 copy.20
  63.4 1.7 %gather_fusion.1 = f32[256,768]{1,0:T(8,128)S(1)} fusion(f32[8,33,768]{2,0,1:T(8,128)S(1)} %concatenate.11.clone, s32[256]{0:T(256)S(1)} %reshape.168), kind=kCustom, calls=%fused_computation.1 | custom fusion | bytes 1574912 | tf_op jit(solution)/shard_map/jit(take_along_axis)/gather | solution.py:54
  65.1 1.0 broadcast_select_fusion
  66.1 5.7 %all-to-all-start = ((f32[8,32,768]{2,1,0:T(8,128)}), f32[8,32,768]{2,1,0:T(8,128)S(1)}, u32[]{:S(2)}, u32[]{:S(2)}) async-start(f32[8,32,768]{2,1,0:T(8,128)} %broadcast_select_fusion), calls=%async_computation | async-start | bytes 1572864 | tf_op jit(solution)/shard_map/all_to_all | solution.py:55
  71.9 0.2 reduce_window_sum.17
  72.2 11.2 %scatter_fusion = s32[8,33]{1,0:T(8,128)S(1)} fusion(s32[8,33]{1,0:T(8,128)S(1)} %broadcast.170.clone, s32[256]{0:T(256)S(1)} %reshape.174, s32[256]{0:T(256)S(1)} %reshape.176), kind=kCustom, calls=%fused_computation.2 | custom fusion | bytes 5120 | tf_op jit(solution)/shard_map/scatter | solution.py:17
  83.5 2.2 %all-to-all-done = f32[8,32,768]{2,1,0:T(8,128)S(1)} async-done(((f32[8,32,768]{2,1,0:T(8,128)}), f32[8,32,768]{2,1,0:T(8,128)S(1)}, u32[]{:S(2)}, u32[]{:S(2)}) %all-to-all-start) | async-done | bytes 786464 | tf_op jit(solution)/shard_map/all_to_all | solution.py:55
  85.7 2.2 %scatter_custom_fusion.2 = f32[33,768]{1,0:T(8,128)S(1)} fusion(s32[256]{0:T(256)S(1)} %bitcast.49, f32[256,768]{1,0:T(8,128)S(1)} %bitcast.45, f32[]{:T(128)} %constant.84.clone.1), kind=kCustom, calls=%fused_computation.18 | custom fusion | flops 196608 | bytes 101380 | tf_op jit(solution)/shard_map/scatter-add | solution.py:65
  87.9 0.6 slice.22
  88.6 29.6 %all-reduce.3.cloned.1.call-done = f32[1024,768]{1,0:T(8,128)} async-done(((f32[1024,768]{1,0:T(8,128)}), f32[1024,768]{1,0:T(8,128)}) %all-reduce.3.cloned.1.call-update) | async-done | bytes 3145744 | tf_op jit(solution)/shard_map/psum | solution.py:68
  118.2 3.3 %multiply_convert_fusion = bf16[1024,768]{1,0:T(8,128)(2,1)} fusion(f32[1024,768]{1,0:T(8,128)} %all-reduce.3.cloned.1.call-done), kind=kLoop, calls=%fused_computation.5 | loop fusion | flops 1572864 | bytes 4718592 | tf_op jit(solution)/shard_map/convert_element_type | solution.py:69
  (32 shorter events, 1.0 us)
Async XLA Ops:
  7.2 38.2 %copy-start = (bf16[1024,768]{1,0:T(8,128)(2,1)S(1)}, bf16[1024,768]{1,0:T(8,128)(2,1)}, u32[]{:S(2)}) copy-start(bf16[1024,768]{1,0:T(8,128)(2,1)} %param.5) | copy-start | bytes 4718596
  7.2 111.0 %all-reduce.3.cloned.1.call-start = ((), (), s32[]{:S(2)}) async-start(), calls=%async_computation.1 | async-start | bytes 6291456 | tf_op jit(solution)/shard_map/psum | solution.py:68
  65.1 6.7 %copy-start.1 = (s32[256,8]{0,1:T(8,128)S(1)}, s32[256,8]{0,1:T(8,128)}, u32[]{:S(2)}) copy-start(s32[256,8]{0,1:T(8,128)} %param.6) | copy-start | bytes 24580
  66.1 19.5 %all-to-all-start = ((f32[8,32,768]{2,1,0:T(8,128)}), f32[8,32,768]{2,1,0:T(8,128)S(1)}, u32[]{:S(2)}, u32[]{:S(2)}) async-start(f32[8,32,768]{2,1,0:T(8,128)} %broadcast_select_fusion), calls=%async_computation | async-start | bytes 1572864 | tf_op jit(solution)/shard_map/all_to_all | solution.py:55
Sparse Core Ops, SparseCore 0:
  48.7 69.5 all-reduce.2
where the time goes:
time: 129 us; the launch traced here: 128 us
  blocking collectives  33 us (26%)
  waiting for transfers between devices  31.8 us (25%)
  local copies, waits for them, and re-layouts  28.9 us (22%)
  between operations  14.2 us (11%)
  other arithmetic  11.1 us (9%)
  starting transfers between devices  5.7 us (4%)
  matrix products  3.7 us (3%)
    all_gather x1, blocking collectives, shards(): piece = lax.all_gather(queries, 'lab', axis=0, tiled=True)  33 us
    psum x1, waiting for transfers between devices, shards(): total = lax.psum(w_acc, 'pb')  29.6 us
    scatter x2, local copies, waits for them, and re-layouts, pack_index(): jnp.full((homes, width_slots + 1), fill_value, jnp.int32)  22.4 us
    all_to_all x1, starting transfers between devices, shards(): lax.all_to_all(outgoing, 'lab', split_axis=0, concat_axis=0, tiled=True)  5.66 us
    convert_element_type x1, other arithmetic, shards(): weight_grad = (total / groups).astype(jnp.bfloat16)  3.27 us
  transfers between devices with their start and end apart: 2, of which 2 were waited for; matrix products, arithmetic and copies ran while one was open for 25% of the time, Pallas kernels for 0%

commit v1 on v0

--- a/solution.py
+++ b/solution.py
@@ -19,7 +19,7 @@
     return table[:, :width_slots]
 
 
-def shards(queries, label_weights, sibling_blocks, positive_slot):
+def sparse_shards(queries, label_weights, sibling_blocks, positive_slot):
     width = queries.shape[1]
     qcount = sibling_blocks.shape[0]
     lab_dev = label_weights.shape[0]
@@ -37,12 +37,10 @@
     target = (label_ids[None, :, :] == positive[:, None, None]).astype(jnp.float32)
     slope = jnp.where(chosen_all[:, :, None], jax.nn.sigmoid(scores) - target, 0.0)
     slope = slope.astype(jnp.bfloat16).reshape(count, lab_dev)
-    dq_rows = jnp.dot(slope, label_weights, preferred_element_type=jnp.float32)
-    dq_all = dq_rows
+    dq_all = jnp.dot(slope, label_weights, preferred_element_type=jnp.float32)
     w_acc = lax.dot_general(
         slope, piece, (((0,), (0,)), ((), ())), preferred_element_type=jnp.float32
     )
-    dq_all, w_acc = (dq_all, w_acc)
     homes = lax.axis_size("lab")
     q_home = qcount // homes
     slots = q_home * K // homes
@@ -70,7 +68,73 @@
     return (query_grad, weight_grad)
 
 
+def swap(value, axis, bit):
+    count = lax.axis_size(axis)
+    return lax.ppermute(value, axis, [(i, i ^ bit) for i in range(count)])
+
+
+def codes(sibling_blocks, positive_slot, blocks_dev):
+    first = lax.axis_index("lab") * blocks_dev
+    local = sibling_blocks.T - first
+    inside = (local >= 0) & (local < blocks_dev)
+    chosen = jnp.max(jnp.where(inside, local, -1), axis=0)
+    steps = jnp.arange(local.shape[0], dtype=jnp.int32)[:, None]
+    pblock = jnp.sum(jnp.where(steps == (positive_slot // BLOCK)[None, :], local, 0), axis=0)
+    return jnp.stack([chosen, pblock * BLOCK + positive_slot % BLOCK])
+
+
+def slopes(rows, weights, code):
+    lab_dev = weights.shape[0]
+    scores = lax.dot_general(
+        weights, rows, (((1,), (1,)), ((), ())), preferred_element_type=jnp.float32
+    )
+    ids = jnp.arange(lab_dev, dtype=jnp.int32)[:, None]
+    target = (ids == code[1][None, :]).astype(jnp.float32)
+    slope = jnp.where(ids // BLOCK == code[0][None, :], jax.nn.sigmoid(scores) - target, 0.0)
+    return slope.astype(jnp.bfloat16)
+
+
+def dense_shards(queries, label_weights, sibling_blocks, positive_slot):
+    q_home, width = queries.shape
+    blocks_dev = label_weights.shape[0] // BLOCK
+    homes = lax.axis_size("lab")
+    groups = lax.axis_size("pb")
+    code = codes(sibling_blocks, positive_slot, blocks_dev)
+    copies = jnp.broadcast_to(queries[None], (homes, q_home, width))
+    own = lax.all_to_all(copies, "lab", split_axis=0, concat_axis=0, tiled=True)
+    parts = [own.reshape(homes * q_home, width)]
+    notes = [code]
+    bit = groups // 2
+    while bit:
+        parts = parts + [swap(part, "pb", bit) for part in parts]
+        notes = notes + [swap(note, "pb", bit) for note in notes]
+        bit //= 2
+    slope = slopes(parts[0], label_weights, notes[0])
+    dq = lax.dot_general(
+        slope, label_weights, (((0,), (0,)), ((), ())), preferred_element_type=jnp.float32
+    )
+    dq = dq.astype(jnp.bfloat16).reshape(homes, q_home, width)
+    incoming = lax.all_to_all(dq, "lab", split_axis=0, concat_axis=0, tiled=True)
+    query_grad = jnp.sum(incoming.astype(jnp.float32), axis=0)
+    rows = jnp.concatenate(parts, axis=0)
+    note = jnp.concatenate(notes, axis=1)
+    every = slopes(rows, label_weights, note)
+    total = jnp.dot(every, rows, preferred_element_type=jnp.float32)
+    weight_grad = (total / groups).astype(jnp.bfloat16)
+    return (query_grad, weight_grad)
+
+
 def solution(mesh):
+    groups, homes = mesh.shape["pb"], mesh.shape["lab"]
+
+    def shards(queries, label_weights, sibling_blocks, positive_slot):
+        every_row_everywhere = homes == K
+        few = groups * sibling_blocks.shape[0] <= 2 * label_weights.shape[0]
+        paired = groups & (groups - 1) == 0
+        one_block = label_weights.shape[0] // BLOCK <= K
+        plan = dense_shards if every_row_everywhere and few and paired and one_block else sparse_shards
+        return plan(queries, label_weights, sibling_blocks, positive_slot)
+
     in_specs = (P(("pb", "lab"), None), P("lab", None), P("pb", None), P("pb"))
     out_specs = (P(("pb", "lab"), None), P("lab", None))
     return jax.shard_map(shards, mesh=mesh, in_specs=in_specs, out_specs=out_specs, check_vma=False)

time: 129 us -> 46.3 us (0.36)
  blocking collectives: 33 us -> 0 us
  local copies, waits for them, and re-layouts: 28.9 us -> 1.71 us
  between operations: 14.2 us -> 0.66 us
  waiting for transfers between devices: 31.8 us -> 19.7 us
  other arithmetic: 11.1 us -> 2.81 us
  starting transfers between devices: 5.7 us -> 13.5 us
  matrix products: 3.7 us -> 7.5 us
    all_gather x1 -> x0, blocking collectives: 33 us -> none  [shards(): piece = lax.all_gather(queries, 'lab', axis=0, tiled=True)]
    psum x1 -> x0, waiting for transfers between devices: 29.6 us -> none  [shards(): total = lax.psum(w_acc, 'pb')]
    scatter x2 -> x0, local copies, waits for them, and re-layouts: 22.4 us -> none  [pack_index(): jnp.full((homes, width_slots + 1), fill_value, jnp.int32)]
    all_to_all x1 -> x2, waiting for transfers between devices: 2.18 us -> 16.1 us  [the longest x1 9.59 us: dense_shards(): own = lax.all_to_all(copies, 'lab', split_axis=0, concat_axis=0, tiled=True)]
    all_to_all x1 -> x2, starting transfers between devices: 5.66 us -> 10.9 us  [the longest x1 7.28 us: dense_shards(): own = lax.all_to_all(copies, 'lab', split_axis=0, concat_axis=0, tiled=True)]
    gather x3 -> x0, local copies, waits for them, and re-layouts: 4.07 us -> none  [the longest x1 2.28 us: shards(): jnp.take_along_axis(sibling_blocks, (positive_slot // BLOCK)[:, None], ax...]
    dot_general x3 -> x2, matrix products: 3.7 us -> 7.5 us  [the longest x1 4.97 us: dense_shards(): total = jnp.dot(every, rows, preferred_element_type=jnp.float32)]
    ppermute x0 -> x6, waiting for transfers between devices: none -> 3.69 us  [swap(): return lax.ppermute(value, axis, [(i, i ^ bit) for i in range(count)])]
  transfers between devices with their start and end apart: 2 -> 8, of which waited for: 2 -> 4; matrix products, arithmetic and copies ran while one was open for 25% -> 12% of each run, Pallas kernels for 0% -> 0%
where the time goes in v1:
time: 46.3 us; the launch traced here: 45.9 us
  waiting for transfers between devices  19.7 us (43%)
  starting transfers between devices  13.5 us (29%)
  matrix products  7.5 us (16%)
  other arithmetic  2.81 us (6%)
  local copies, waits for them, and re-layouts  1.71 us (4%)
  between operations  0.66 us (1%)
    all_to_all x1, waiting for transfers between devices, dense_shards(): own = lax.all_to_all(copies, 'lab', split_axis=0, concat_axis=0, tiled=True)  9.59 us
    all_to_all x1, starting transfers between devices, dense_shards(): own = lax.all_to_all(copies, 'lab', split_axis=0, concat_axis=0, tiled=True)  7.28 us
    all_to_all x1, waiting for transfers between devices, dense_shards(): lax.all_to_all(dq, 'lab', split_axis=0, concat_axis=0, tiled=True)  6.47 us
    dot_general x1, matrix products, dense_shards(): total = jnp.dot(every, rows, preferred_element_type=jnp.float32)  4.97 us
    ppermute x6, waiting for transfers between devices, swap(): return lax.ppermute(value, axis, [(i, i ^ bit) for i in range(count)])  3.69 us
    all_to_all x1, starting transfers between devices, dense_shards(): lax.all_to_all(dq, 'lab', split_axis=0, concat_axis=0, tiled=True)  3.62 us
    ppermute x6, starting transfers between devices, swap(): return lax.ppermute(value, axis, [(i, i ^ bit) for i in range(count)])  2.61 us
    dot_general x1, matrix products, dense_shards(): lax.dot_general(slope, label_weights, (((0,), (0,)), ((), ())), preferred...  2.53 us
  transfers between devices with their start and end apart: 8, of which 4 were waited for; matrix products, arithmetic and copies ran while one was open for 12% of the time, Pallas kernels for 0%

profile of v1, /device:TPU:0, one launch (start us, length us, event | category | flops | bytes accessed | tf_op | source)
XLA Modules:
  0.0 45.9 jit_solution(14574432730644628149)
XLA Ops:
  0.6 0.0 copy-start
  0.6 1.7 %broadcast_in_dim.24 = bf16[8,32,768]{2,1,0:T(8,128)(2,1)} broadcast(bf16[32,768]{1,0:T(8,128)(2,1)} %param.4), dimensions={1,2} | broadcast | bytes 442368 | tf_op jit(solution)/shard_map/broadcast_in_dim | solution.py:103
  2.3 7.3 %all-to-all-start = ((bf16[8,32,768]{2,1,0:T(8,128)(2,1)}), bf16[8,32,768]{2,1,0:T(8,128)(2,1)S(1)}, u32[]{:S(2)}, u32[]{:S(2)}) async-start(bf16[8,32,768]{2,1,0:T(8,128)(2,1)} %broadcast_in_dim.24), calls=%async_computation | async-start | bytes 786432 | tf_op jit(solution)/shard_map/all_to_all | solution.py:104
  9.6 0.7 %and_select_fusion.1 = s32[256]{0:T(256)S(1)} fusion(s32[256]{0:T(256)} %param.7), kind=kLoop, calls=%fused_computation.41 | loop fusion | flops 3840 | bytes 2048 | tf_op jit(solution)/shard_map/jit(floor_divide)/jit(_where)/select_n | solution.py:82
  10.3 0.7 %fusion.15 = (s32[256]{0:T(256)S(1)}, s32[256]{0:T(256)S(1)}) fusion(s32[256,8]{0,1:T(8,128)} %param.6, s32[]{:T(128)S(6)} %mul.7, s32[256]{0:T(256)S(1)} %and_select_fusion.1), kind=kLoop, calls=%fused_computation.28 | loop fusion | flops 17920 | bytes 11268 | tf_op jit(solution)/shard_map/reduce_max | solution.py:80
  11.0 0.7 %fusion.21 = s32[256]{0:T(256)S(1)} fusion(s32[256]{0:T(256)S(1)} %get-tuple-element.3, s32[256]{0:T(256)} %param.7), kind=kLoop, calls=%fused_computation.45 | loop fusion | flops 3328 | bytes 3072 | tf_op jit(solution)/shard_map/add | solution.py:83
  11.7 9.6 %all-to-all-done = bf16[8,32,768]{2,1,0:T(8,128)(2,1)S(1)} async-done(((bf16[8,32,768]{2,1,0:T(8,128)(2,1)}), bf16[8,32,768]{2,1,0:T(8,128)(2,1)S(1)}, u32[]{:S(2)}, u32[]{:S(2)}) %all-to-all-start) | async-done | bytes 393248 | tf_op jit(solution)/shard_map/all_to_all | solution.py:104
  21.3 1.5 %collective-permute-start.3 = (bf16[256,768]{1,0:T(8,128)(2,1)S(1)}, bf16[256,768]{1,0:T(8,128)(2,1)S(1)}, u32[]{:S(2)}, u32[]{:S(2)}) collective-permute-start(bf16[256,768]{1,0:T(8,128)(2,1)S(1)} %bitcast.33), channel_id=1, source_target_pairs={{0,16},{8,24},{16,0},{24,8},{1,17},{9,25},{17,1},{25,9},{2,18},{10... | collective-permute-start | bytes 1179656 | tf_op jit(solution)/shard_map/ppermute | solution.py:73
  22.8 2.5 %convolution_convert_fusion = bf16[256,768]{1,0:T(8,128)(2,1)} fusion(bf16[1024,768]{1,0:T(8,128)(2,1)S(1)} %copy-done, bf16[256,768]{1,0:T(8,128)(2,1)S(1)} %bitcast.34, s32[256]{0:T(256)S(1)} %fusion.21, s32[256]{0:T(256)S(1)} %get-tuple-element.2, s32[1024]{0:T(1024)S(1)} %add_select_fusion), kind=kOutput, calls=%fused_computation.11 | convolution fusion | flops 807862272 | bytes 2365440 | tf_op jit(solution)/shard_map/dot_general | solution.py:113
  25.3 3.6 %all-to-all-start.1 = ((bf16[8,32,768]{2,1,0:T(8,128)(2,1)}), bf16[8,32,768]{2,1,0:T(8,128)(2,1)S(1)}, u32[]{:S(2)}, u32[]{:S(2)}) async-start(bf16[8,32,768]{2,1,0:T(8,128)(2,1)} %bitcast.2), calls=%async_computation.1 | async-start | bytes 786432 | tf_op jit(solution)/shard_map/all_to_all | solution.py:117
  29.0 0.6 %collective-permute-start = (s32[2,256]{1,0:T(2,128)S(1)}, s32[2,256]{1,0:T(2,128)S(1)}, u32[]{:S(2)}, u32[]{:S(2)}) collective-permute-start(s32[2,256]{1,0:T(2,128)S(1)} %pad_add_fusion.1), channel_id=1, source_target_pairs={{0,16},{8,24},{16,0},{24,8},{1,17},{9,25},{17,1},{25,9},{2,18},{10... | collective-permute-start | bytes 6152 | tf_op jit(solution)/shard_map/ppermute | solution.py:73
  29.6 0.0 collective-permute-start.1
  29.6 3.0 %collective-permute-done = s32[2,256]{1,0:T(2,128)S(1)} collective-permute-done((s32[2,256]{1,0:T(2,128)S(1)}, s32[2,256]{1,0:T(2,128)S(1)}, u32[]{:S(2)}, u32[]{:S(2)}) %collective-permute-start) | collective-permute-done | bytes 2080 | tf_op jit(solution)/shard_map/ppermute | solution.py:73
  32.6 0.0 collective-permute-start.2
  32.6 0.5 %collective-permute-start.4 = (bf16[256,768]{1,0:T(8,128)(2,1)S(1)}, bf16[256,768]{1,0:T(8,128)(2,1)S(1)}, u32[]{:S(2)}, u32[]{:S(2)}) collective-permute-start(bf16[256,768]{1,0:T(8,128)(2,1)S(1)} %bitcast.35), channel_id=1, source_target_pairs={{0,8},{8,0},{16,24},{24,16},{1,9},{9,1},{17,25},{25,17},{2,10},{10... | collective-permute-start | bytes 1179656 | tf_op jit(solution)/shard_map/ppermute | solution.py:73
  33.1 0.0 collective-permute-done.3
  33.1 0.0 collective-permute-start.5
  33.1 0.0 collective-permute-done.1
  33.1 0.6 %collective-permute-done.2 = s32[2,256]{1,0:T(2,128)S(1)} collective-permute-done((s32[2,256]{1,0:T(2,128)S(1)}, s32[2,256]{1,0:T(2,128)S(1)}, u32[]{:S(2)}, u32[]{:S(2)}) %collective-permute-start.2) | collective-permute-done | bytes 2080 | tf_op jit(solution)/shard_map/ppermute | solution.py:73
  33.8 6.5 %all-to-all-done.1 = bf16[8,32,768]{2,1,0:T(8,128)(2,1)S(1)} async-done(((bf16[8,32,768]{2,1,0:T(8,128)(2,1)}), bf16[8,32,768]{2,1,0:T(8,128)(2,1)S(1)}, u32[]{:S(2)}, u32[]{:S(2)}) %all-to-all-start.1) | async-done | bytes 393248 | tf_op jit(solution)/shard_map/all_to_all | solution.py:117
  40.3 0.7 %convert_reduce_fusion = f32[32,768]{1,0:T(8,128)} fusion(bf16[8,32,768]{2,1,0:T(8,128)(2,1)S(1)} %all-to-all-done.1), kind=kLoop, calls=%fused_computation.17 | loop fusion | flops 368640 | bytes 491520 | tf_op jit(solution)/shard_map/reduce_sum | solution.py:118
  41.0 0.0 collective-permute-done.4
  41.0 0.0 collective-permute-done.5
  41.0 5.0 %multiply_convert_fusion = bf16[1024,768]{1,0:T(8,128)(2,1)} fusion(bf16[1024,768]{1,0:T(8,128)(2,1)S(1)} %copy-done, s32[1024]{0:T(1024)S(1)} %bitcast.42, s32[1024]{0:T(1024)S(1)} %bitcast.41, s32[1024]{0:T(1024)S(1)} %add_select_fusion, bf16[256,768]{1,0:T(8,128)(2,1)S(1)} %collective-permute-done.5, bf16[256,768]{1,0:T(8,128)(2,1)S(1)} %collective-permute-done.4, ...), kind=kOutput, calls=%fused_computation.4 | convolution fusion | flops 3244818432 | bytes 4730880 | tf_op jit(solution)/shard_map/dot_general | solution.py:122
  (5 shorter events, 0.0 us)
Async XLA Ops:
  0.6 22.2 %copy-start = (bf16[1024,768]{1,0:T(8,128)(2,1)S(1)}, bf16[1024,768]{1,0:T(8,128)(2,1)}, u32[]{:S(2)}) copy-start(bf16[1024,768]{1,0:T(8,128)(2,1)} %param.5) | copy-start | bytes 4718596
  2.3 19.0 %all-to-all-start = ((bf16[8,32,768]{2,1,0:T(8,128)(2,1)}), bf16[8,32,768]{2,1,0:T(8,128)(2,1)S(1)}, u32[]{:S(2)}, u32[]{:S(2)}) async-start(bf16[8,32,768]{2,1,0:T(8,128)(2,1)} %broadcast_in_dim.24), calls=%async_computation | async-start | bytes 786432 | tf_op jit(solution)/shard_map/all_to_all | solution.py:104
  21.3 11.8 %collective-permute-start.3 = (bf16[256,768]{1,0:T(8,128)(2,1)S(1)}, bf16[256,768]{1,0:T(8,128)(2,1)S(1)}, u32[]{:S(2)}, u32[]{:S(2)}) collective-permute-start(bf16[256,768]{1,0:T(8,128)(2,1)S(1)} %bitcast.33), channel_id=1, source_target_pairs={{0,16},{8,24},{16,0},{24,8},{1,17},{9,25},{17,1},{25,9},{2,18},{10... | collective-permute-start | bytes 1179656 | tf_op jit(solution)/shard_map/ppermute | solution.py:73
  25.3 14.9 %all-to-all-start.1 = ((bf16[8,32,768]{2,1,0:T(8,128)(2,1)}), bf16[8,32,768]{2,1,0:T(8,128)(2,1)S(1)}, u32[]{:S(2)}, u32[]{:S(2)}) async-start(bf16[8,32,768]{2,1,0:T(8,128)(2,1)} %bitcast.2), calls=%async_computation.1 | async-start | bytes 786432 | tf_op jit(solution)/shard_map/all_to_all | solution.py:117
  29.0 3.7 %collective-permute-start = (s32[2,256]{1,0:T(2,128)S(1)}, s32[2,256]{1,0:T(2,128)S(1)}, u32[]{:S(2)}, u32[]{:S(2)}) collective-permute-start(s32[2,256]{1,0:T(2,128)S(1)} %pad_add_fusion.1), channel_id=1, source_target_pairs={{0,16},{8,24},{16,0},{24,8},{1,17},{9,25},{17,1},{25,9},{2,18},{10... | collective-permute-start | bytes 6152 | tf_op jit(solution)/shard_map/ppermute | solution.py:73
  29.6 3.6 %collective-permute-start.1 = (s32[2,256]{1,0:T(2,128)S(1)}, s32[2,256]{1,0:T(2,128)S(1)}, u32[]{:S(2)}, u32[]{:S(2)}) collective-permute-start(s32[2,256]{1,0:T(2,128)S(1)} %pad_add_fusion.1), channel_id=1, source_target_pairs={{0,8},{8,0},{16,24},{24,16},{1,9},{9,1},{17,25},{25,17},{2,10},{10... | collective-permute-start | bytes 6152 | tf_op jit(solution)/shard_map/ppermute | solution.py:73
  32.6 1.2 %collective-permute-start.2 = (s32[2,256]{1,0:T(2,128)S(1)}, s32[2,256]{1,0:T(2,128)S(1)}, u32[]{:S(2)}, u32[]{:S(2)}) collective-permute-start(s32[2,256]{1,0:T(2,128)S(1)} %collective-permute-done), channel_id=1, source_target_pairs={{0,8},{8,0},{16,24},{24,16},{1,9},{9,1},{17,25},{25,17},{2,10},{10... | collective-permute-start | bytes 6152 | tf_op jit(solution)/shard_map/ppermute | solution.py:73
  32.6 8.3 %collective-permute-start.4 = (bf16[256,768]{1,0:T(8,128)(2,1)S(1)}, bf16[256,768]{1,0:T(8,128)(2,1)S(1)}, u32[]{:S(2)}, u32[]{:S(2)}) collective-permute-start(bf16[256,768]{1,0:T(8,128)(2,1)S(1)} %bitcast.35), channel_id=1, source_target_pairs={{0,8},{8,0},{16,24},{24,16},{1,9},{9,1},{17,25},{25,17},{2,10},{10... | collective-permute-start | bytes 1179656 | tf_op jit(solution)/shard_map/ppermute | solution.py:73
  33.1 7.8 %collective-permute-start.5 = (bf16[256,768]{1,0:T(8,128)(2,1)S(1)}, bf16[256,768]{1,0:T(8,128)(2,1)S(1)}, u32[]{:S(2)}, u32[]{:S(2)}) collective-permute-start(bf16[256,768]{1,0:T(8,128)(2,1)S(1)} %collective-permute-done.3), channel_id=1, source_target_pairs={{0,8},{8,0},{16,24},{24,16},{1,9},{9,1},{17,25},{25,17},{2,10},{10... | collective-permute-start | bytes 1179656 | tf_op jit(solution)/shard_map/ppermute | solution.py:73

commit v2 on v1

--- a/solution.py
+++ b/solution.py
@@ -94,15 +94,27 @@
     return slope.astype(jnp.bfloat16)
 
 
+def flip_to(value, index, count):
+    bit = 1
+    while bit < count:
+        split = value.reshape((count // (2 * bit), 2, bit) + value.shape[1:])
+        turned = jnp.concatenate([split[:, 1:], split[:, :1]], axis=1)
+        value = jnp.where((index & bit) != 0, turned, split).reshape(value.shape)
+        bit *= 2
+    return value
+
+
 def dense_shards(queries, label_weights, sibling_blocks, positive_slot):
     q_home, width = queries.shape
     blocks_dev = label_weights.shape[0] // BLOCK
     homes = lax.axis_size("lab")
     groups = lax.axis_size("pb")
-    code = codes(sibling_blocks, positive_slot, blocks_dev)
-    copies = jnp.broadcast_to(queries[None], (homes, q_home, width))
-    own = lax.all_to_all(copies, "lab", split_axis=0, concat_axis=0, tiled=True)
-    parts = [own.reshape(homes * q_home, width)]
+    me = lax.axis_index("lab")
+    arrived = [queries] + [swap(queries, "lab", step) for step in range(1, homes)]
+    sibling = flip_to(sibling_blocks.reshape(homes, q_home, -1), me, homes)
+    slot = flip_to(positive_slot.reshape(homes, q_home), me, homes)
+    code = codes(sibling.reshape(sibling_blocks.shape), slot.reshape(-1), blocks_dev)
+    parts = [jnp.concatenate(arrived, axis=0)]
     notes = [code]
     bit = groups // 2
     while bit:
@@ -113,14 +125,19 @@
     dq = lax.dot_general(
         slope, label_weights, (((0,), (0,)), ((), ())), preferred_element_type=jnp.float32
     )
-    dq = dq.astype(jnp.bfloat16).reshape(homes, q_home, width)
-    incoming = lax.all_to_all(dq, "lab", split_axis=0, concat_axis=0, tiled=True)
-    query_grad = jnp.sum(incoming.astype(jnp.float32), axis=0)
+    dq = dq.reshape(homes, q_home, width)
+    incoming = [dq[0]]
+    for step in range(1, homes):
+        incoming.append(swap(dq[step].astype(jnp.bfloat16), "lab", step))
     rows = jnp.concatenate(parts, axis=0)
     note = jnp.concatenate(notes, axis=1)
     every = slopes(rows, label_weights, note)
     total = jnp.dot(every, rows, preferred_element_type=jnp.float32)
     weight_grad = (total / groups).astype(jnp.bfloat16)
+    *incoming, weight_grad = lax.optimization_barrier((*incoming, weight_grad))
+    query_grad = incoming[0]
+    for term in incoming[1:]:
+        query_grad = query_grad + term.astype(jnp.float32)
     return (query_grad, weight_grad)
 
 

time: 46.3 us -> 62.6 us (1.35)
  starting transfers between devices: 13.5 us -> 26.7 us
  local copies, waits for them, and re-layouts: 1.71 us -> 14.7 us
  waiting for transfers between devices: 19.7 us -> 7.06 us
  matrix products: 7.5 us -> 10.5 us
    ppermute x6 -> x20, starting transfers between devices: 2.61 us -> 26.7 us  [swap(): return lax.ppermute(value, axis, [(i, i ^ bit) for i in range(count)])]
    all_to_all x2 -> x0, waiting for transfers between devices: 16.1 us -> none  [the longest x1 9.59 us: dense_shards(): own = lax.all_to_all(copies, 'lab', split_axis=0, concat_axis=0, tiled=True)]
    all_to_all x2 -> x0, starting transfers between devices: 10.9 us -> none  [the longest x1 7.28 us: dense_shards(): own = lax.all_to_all(copies, 'lab', split_axis=0, concat_axis=0, tiled=True)]
    unnamed x2 -> x12, local copies, waits for them, and re-layouts: 0.01 us -> 7.63 us
    another operation x0 -> x6, local copies, waits for them, and re-layouts: none -> 4.75 us  [flip_to(): split = value.reshape((count // (2 * bit), 2, bit) + value.shape[1:])]
    ppermute x6 -> x20, waiting for transfers between devices: 3.69 us -> 7.06 us  [swap(): return lax.ppermute(value, axis, [(i, i ^ bit) for i in range(count)])]
    dot_general x1, matrix products: 4.97 us -> 6.84 us  [dense_shards(): total = jnp.dot(every, rows, preferred_element_type=jnp.float32)]
    broadcast_in_dim x1 -> x0, local copies, waits for them, and re-layouts: 1.69 us -> none  [dense_shards(): copies = jnp.broadcast_to(queries[None], (homes, q_home, width))]
  transfers between devices with their start and end apart: 8 -> 20, of which waited for: 4 -> 2; matrix products, arithmetic and copies ran while one was open for 12% -> 31% of each run, Pallas kernels for 0% -> 0%
where the time goes in v2:
time: 62.6 us; the launch traced here: 62.1 us
  starting transfers between devices  26.7 us (43%)
  local copies, waits for them, and re-layouts  14.7 us (23%)
  matrix products  10.5 us (17%)
  waiting for transfers between devices  7.06 us (11%)
  other arithmetic  2.26 us (4%)
  between operations  0.85 us (1%)
    ppermute x20, starting transfers between devices, swap(): return lax.ppermute(value, axis, [(i, i ^ bit) for i in range(count)])  26.7 us
    unnamed x12, local copies, waits for them, and re-layouts  7.63 us
    ppermute x20, waiting for transfers between devices, swap(): return lax.ppermute(value, axis, [(i, i ^ bit) for i in range(count)])  7.06 us
    dot_general x1, matrix products, dense_shards(): total = jnp.dot(every, rows, preferred_element_type=jnp.float32)  6.84 us
    another operation x6, local copies, waits for them, and re-layouts, flip_to(): split = value.reshape((count // (2 * bit), 2, bit) + value.shape[1:])  4.75 us
    dot_general x1, matrix products, dense_shards(): lax.dot_general(slope, label_weights, (((0,), (0,)), ((), ())), preferred...  3.69 us
  transfers between devices with their start and end apart: 20, of which 2 were waited for; matrix products, arithmetic and copies ran while one was open for 31% of the time, Pallas kernels for 0%

profile of v2, /device:TPU:0, one launch (start us, length us, event | category | flops | bytes accessed | tf_op | source)
XLA Modules:
  0.0 62.1 jit_solution(9633188920386343172)
XLA Ops:
  0.6 0.9 %reshape_reshape.23 = s32[4,2,1,32]{3,1,0,2:T(2,128)S(1)} reshape(s32[256]{0:T(256)} %param.7) | data formatting | bytes 2048 | tf_op jit(solution)/shard_map/reshape;reshape | solution.py:100
  3.0 0.8 %reshape_reshape.20 = s32[4,2,1,32,8]{3,1,0,4,2:T(2,128)S(1)} reshape(s32[256,8]{0,1:T(8,128)} %param.6) | data formatting | bytes 16384 | tf_op jit(solution)/shard_map/reshape;reshape | solution.py:100
  3.8 0.8 %reshape_reshape.21 = s32[2,2,2,32,8]{3,2,1,0,4:T(2,128)S(1)} reshape(s32[256,8]{0,1:T(8,128)} %param.6) | data formatting | bytes 16384 | tf_op jit(solution)/shard_map/reshape;reshape | solution.py:100
  4.6 0.8 %reshape_reshape.22 = s32[1,2,4,32,8]{3,2,1,4,0:T(4,128)S(1)} reshape(s32[256,8]{0,1:T(8,128)} %param.6) | data formatting | bytes 16384 | tf_op jit(solution)/shard_map/reshape;reshape | solution.py:100
  7.7 3.0 %collective-permute-start.14 = (s32[2,256]{1,0:T(2,128)S(1)}, s32[2,256]{1,0:T(2,128)S(1)}, u32[]{:S(2)}, u32[]{:S(2)}) collective-permute-start(s32[2,256]{1,0:T(2,128)S(1)} %pad_add_fusion.7), channel_id=1, source_target_pairs={{0,16},{8,24},{16,0},{24,8},{1,17},{9,25},{17,1},{25,9},{2,18},{10... | collective-permute-start | bytes 6152 | tf_op jit(solution)/shard_map/ppermute | solution.py:73
  10.9 1.6 %collective-permute-start.1 = (bf16[32,768]{1,0:T(8,128)(2,1)}, bf16[32,768]{1,0:T(8,128)(2,1)S(1)}, u32[]{:S(2)}, u32[]{:S(2)}) collective-permute-start(bf16[32,768]{1,0:T(8,128)(2,1)} %param.4), channel_id=1, source_target_pairs={{0,2},{1,3},{2,0},{3,1},{4,6},{5,7},{6,4},{7,5},{8,10},{9,11},{10,... | collective-permute-start | bytes 147464 | tf_op jit(solution)/shard_map/ppermute | solution.py:73
  12.4 1.7 %collective-permute-start.2 = (bf16[32,768]{1,0:T(8,128)(2,1)}, bf16[32,768]{1,0:T(8,128)(2,1)S(1)}, u32[]{:S(2)}, u32[]{:S(2)}) collective-permute-start(bf16[32,768]{1,0:T(8,128)(2,1)} %param.4), channel_id=1, source_target_pairs={{0,3},{1,2},{2,1},{3,0},{4,7},{5,6},{6,5},{7,4},{8,11},{9,10},{10,... | collective-permute-start | bytes 147464 | tf_op jit(solution)/shard_map/ppermute | solution.py:73
  14.2 1.5 %constant_dynamic-update-slice_fusion.18 = (bf16[1024,768]{1,0:T(8,128)(2,1)}, bf16[256,768]{1,0:T(8,128)(2,1)}) fusion(bf16[32,768]{1,0:T(8,128)(2,1)} %param.4), kind=kLoop, calls=%fused_computation.41 | loop fusion | bytes 147456
  15.7 2.7 %collective-permute-start.3 = (bf16[32,768]{1,0:T(8,128)(2,1)}, bf16[32,768]{1,0:T(8,128)(2,1)S(1)}, u32[]{:S(2)}, u32[]{:S(2)}) collective-permute-start(bf16[32,768]{1,0:T(8,128)(2,1)} %param.4), channel_id=1, source_target_pairs={{0,4},{1,5},{2,6},{3,7},{4,0},{5,1},{6,2},{7,3},{8,12},{9,13},{10,... | collective-permute-start | bytes 147464 | tf_op jit(solution)/shard_map/ppermute | solution.py:73
  19.1 2.9 %collective-permute-start.5 = (bf16[32,768]{1,0:T(8,128)(2,1)}, bf16[32,768]{1,0:T(8,128)(2,1)S(1)}, u32[]{:S(2)}, u32[]{:S(2)}) collective-permute-start(bf16[32,768]{1,0:T(8,128)(2,1)} %param.4), channel_id=1, source_target_pairs={{0,6},{1,7},{2,4},{3,5},{4,2},{5,3},{6,0},{7,1},{8,14},{9,15},{10,... | collective-permute-start | bytes 147464 | tf_op jit(solution)/shard_map/ppermute | solution.py:73
  22.6 2.3 %collective-permute-start.6 = (bf16[32,768]{1,0:T(8,128)(2,1)}, bf16[32,768]{1,0:T(8,128)(2,1)S(1)}, u32[]{:S(2)}, u32[]{:S(2)}) collective-permute-start(bf16[32,768]{1,0:T(8,128)(2,1)} %param.4), channel_id=1, source_target_pairs={{0,7},{1,6},{2,5},{3,4},{4,3},{5,2},{6,1},{7,0},{8,15},{9,14},{10,... | collective-permute-start | bytes 147464 | tf_op jit(solution)/shard_map/ppermute | solution.py:73
  28.2 1.5 %collective-permute-done.6 = bf16[32,768]{1,0:T(8,128)(2,1)S(1)} collective-permute-done((bf16[32,768]{1,0:T(8,128)(2,1)}, bf16[32,768]{1,0:T(8,128)(2,1)S(1)}, u32[]{:S(2)}, u32[]{:S(2)}) %collective-permute-start.6) | collective-permute-done | bytes 49184 | tf_op jit(solution)/shard_map/ppermute | solution.py:73
  30.9 3.7 %fusion.36 = (bf16[256,768]{1,0:T(8,128)(2,1)S(1)}, f32[256,768]{1,0:T(8,128)}) fusion(bf16[1024,768]{1,0:T(8,128)(2,1)S(1)} %copy-done, bf16[256,768]{1,0:T(8,128)(2,1)} %get-tuple-element.32, s32[256]{0:T(256)S(1)} %fusion.23, s32[256]{0:T(256)S(1)} %get-tuple-element.20, s32[1024]{0:T(1024)S(1)} %add_select_fusion), kind=kOutput, calls=%fused_computation.91 | convolution fusion | flops 807862272 | bytes 3151872 | tf_op jit(solution)/shard_map/dot_general | solution.py:125
  34.6 5.5 %collective-permute-done.17 = bf16[256,768]{1,0:T(8,128)(2,1)S(1)} collective-permute-done((bf16[256,768]{1,0:T(8,128)(2,1)}, bf16[256,768]{1,0:T(8,128)(2,1)S(1)}, u32[]{:S(2)}, u32[]{:S(2)}) %collective-permute-start.17) | collective-permute-done | bytes 393248 | tf_op jit(solution)/shard_map/ppermute | solution.py:73
  40.1 2.3 %collective-permute-start.10 = (bf16[32,768]{1,0:T(8,128)(2,1)S(1)}, bf16[32,768]{1,0:T(8,128)(2,1)S(1)}, u32[]{:S(2)}, u32[]{:S(2)}) collective-permute-start(bf16[32,768]{1,0:T(8,128)(2,1)S(1)} %get-tuple-element.27), channel_id=1, source_target_pairs={{0,4},{1,5},{2,6},{3,7},{4,0},{5,1},{6,2},{7,3},{8,12},{9,13},{10,... | collective-permute-start | bytes 147464 | tf_op jit(solution)/shard_map/ppermute | solution.py:73
  42.4 1.9 %collective-permute-start.11 = (bf16[32,768]{1,0:T(8,128)(2,1)S(1)}, bf16[32,768]{1,0:T(8,128)(2,1)S(1)}, u32[]{:S(2)}, u32[]{:S(2)}) collective-permute-start(bf16[32,768]{1,0:T(8,128)(2,1)S(1)} %get-tuple-element.26), channel_id=1, source_target_pairs={{0,5},{1,4},{2,7},{3,6},{4,1},{5,0},{6,3},{7,2},{8,13},{9,12},{10,... | collective-permute-start | bytes 147464 | tf_op jit(solution)/shard_map/ppermute | solution.py:73
  44.3 1.6 %collective-permute-start.12 = (bf16[32,768]{1,0:T(8,128)(2,1)S(1)}, bf16[32,768]{1,0:T(8,128)(2,1)S(1)}, u32[]{:S(2)}, u32[]{:S(2)}) collective-permute-start(bf16[32,768]{1,0:T(8,128)(2,1)S(1)} %get-tuple-element.25), channel_id=1, source_target_pairs={{0,6},{1,7},{2,4},{3,5},{4,2},{5,3},{6,0},{7,1},{8,14},{9,15},{10,... | collective-permute-start | bytes 147464 | tf_op jit(solution)/shard_map/ppermute | solution.py:73
  45.9 0.9 %slice.115 = f32[32,768]{1,0:T(8,128)S(1)} slice(f32[256,768]{1,0:T(8,128)} %get-tuple-element.66), slice={[0:32], [0:768]} | slice | bytes 196608 | tf_op jit(solution)/shard_map/slice | solution.py:129
  46.8 0.8 %constant_dynamic-update-slice_fusion.10 = bf16[1024,768]{1,0:T(8,128)(2,1)} fusion(bf16[1024,768]{1,0:T(8,128)(2,1)} %get-tuple-element.31, bf16[256,768]{1,0:T(8,128)(2,1)S(1)} %collective-permute-done.17), kind=kLoop, calls=%fused_computation.33 | loop fusion | bytes 786432
  47.5 2.0 %collective-permute-start.13 = (bf16[32,768]{1,0:T(8,128)(2,1)S(1)}, bf16[32,768]{1,0:T(8,128)(2,1)S(1)}, u32[]{:S(2)}, u32[]{:S(2)}) collective-permute-start(bf16[32,768]{1,0:T(8,128)(2,1)S(1)} %get-tuple-element.24), channel_id=1, source_target_pairs={{0,7},{1,6},{2,5},{3,4},{4,3},{5,2},{6,1},{7,0},{8,15},{9,14},{10,... | collective-permute-start | bytes 147464 | tf_op jit(solution)/shard_map/ppermute | solution.py:73
  49.5 0.8 %constant_dynamic-update-slice_fusion.9 = bf16[1024,768]{1,0:T(8,128)(2,1)} fusion(bf16[1024,768]{1,0:T(8,128)(2,1)} %constant_dynamic-update-slice_fusion.10, bf16[256,768]{1,0:T(8,128)(2,1)S(1)} %collective-permute-done.18), kind=kLoop, calls=%fused_computation.32 | loop fusion | bytes 786432
  50.3 1.8 %collective-permute-start.7 = (bf16[32,768]{1,0:T(8,128)(2,1)S(1)}, bf16[32,768]{1,0:T(8,128)(2,1)S(1)}, u32[]{:S(2)}, u32[]{:S(2)}) collective-permute-start(bf16[32,768]{1,0:T(8,128)(2,1)S(1)} %get-tuple-element.30), channel_id=1, source_target_pairs={{0,1},{1,0},{2,3},{3,2},{4,5},{5,4},{6,7},{7,6},{8,9},{9,8},{10,11... | collective-permute-start | bytes 147464 | tf_op jit(solution)/shard_map/ppermute | solution.py:73
  52.8 1.7 %collective-permute-start.9 = (bf16[32,768]{1,0:T(8,128)(2,1)S(1)}, bf16[32,768]{1,0:T(8,128)(2,1)S(1)}, u32[]{:S(2)}, u32[]{:S(2)}) collective-permute-start(bf16[32,768]{1,0:T(8,128)(2,1)S(1)} %get-tuple-element.28), channel_id=1, source_target_pairs={{0,3},{1,2},{2,1},{3,0},{4,7},{5,6},{6,5},{7,4},{8,11},{9,10},{10,... | collective-permute-start | bytes 147464 | tf_op jit(solution)/shard_map/ppermute | solution.py:73
  54.6 6.8 %multiply_convert_fusion = bf16[1024,768]{1,0:T(8,128)(2,1)} fusion(bf16[1024,768]{1,0:T(8,128)(2,1)} %constant_dynamic-update-slice_fusion.8, bf16[1024,768]{1,0:T(8,128)(2,1)S(1)} %copy-done, s32[1024]{0:T(1024)S(1)} %bitcast.90, s32[1024]{0:T(1024)S(1)} %bitcast.89, s32[1024]{0:T(1024)S(1)} %add_select_fusion), kind=kOutput, calls=%fused_computation.4 | convolution fusion | flops 3232235520 | bytes 4730880 | tf_op jit(solution)/shard_map/dot_general | solution.py:135
  (69 shorter events, 11.2 us)
Async XLA Ops:
  0.6 30.3 %copy-start = (bf16[1024,768]{1,0:T(8,128)(2,1)S(1)}, bf16[1024,768]{1,0:T(8,128)(2,1)}, u32[]{:S(2)}) copy-start(bf16[1024,768]{1,0:T(8,128)(2,1)} %param.5) | copy-start | bytes 4718596
  7.7 8.0 %collective-permute-start.14 = (s32[2,256]{1,0:T(2,128)S(1)}, s32[2,256]{1,0:T(2,128)S(1)}, u32[]{:S(2)}, u32[]{:S(2)}) collective-permute-start(s32[2,256]{1,0:T(2,128)S(1)} %pad_add_fusion.7), channel_id=1, source_target_pairs={{0,16},{8,24},{16,0},{24,8},{1,17},{9,25},{17,1},{25,9},{2,18},{10... | collective-permute-start | bytes 6152 | tf_op jit(solution)/shard_map/ppermute | solution.py:73
  10.7 5.0 %collective-permute-start.15 = (s32[2,256]{1,0:T(2,128)S(1)}, s32[2,256]{1,0:T(2,128)S(1)}, u32[]{:S(2)}, u32[]{:S(2)}) collective-permute-start(s32[2,256]{1,0:T(2,128)S(1)} %pad_add_fusion.7), channel_id=1, source_target_pairs={{0,8},{8,0},{16,24},{24,16},{1,9},{9,1},{17,25},{25,17},{2,10},{10... | collective-permute-start | bytes 6152 | tf_op jit(solution)/shard_map/ppermute | solution.py:73
  10.7 8.4 %collective-permute-start = (bf16[32,768]{1,0:T(8,128)(2,1)}, bf16[32,768]{1,0:T(8,128)(2,1)S(1)}, u32[]{:S(2)}, u32[]{:S(2)}) collective-permute-start(bf16[32,768]{1,0:T(8,128)(2,1)} %param.4), channel_id=1, source_target_pairs={{0,1},{1,0},{2,3},{3,2},{4,5},{5,4},{6,7},{7,6},{8,9},{9,8},{10,11... | collective-permute-start | bytes 147464 | tf_op jit(solution)/shard_map/ppermute | solution.py:73
  10.9 11.8 %collective-permute-start.1 = (bf16[32,768]{1,0:T(8,128)(2,1)}, bf16[32,768]{1,0:T(8,128)(2,1)S(1)}, u32[]{:S(2)}, u32[]{:S(2)}) collective-permute-start(bf16[32,768]{1,0:T(8,128)(2,1)} %param.4), channel_id=1, source_target_pairs={{0,2},{1,3},{2,0},{3,1},{4,6},{5,7},{6,4},{7,5},{8,10},{9,11},{10,... | collective-permute-start | bytes 147464 | tf_op jit(solution)/shard_map/ppermute | solution.py:73
  12.4 13.1 %collective-permute-start.2 = (bf16[32,768]{1,0:T(8,128)(2,1)}, bf16[32,768]{1,0:T(8,128)(2,1)S(1)}, u32[]{:S(2)}, u32[]{:S(2)}) collective-permute-start(bf16[32,768]{1,0:T(8,128)(2,1)} %param.4), channel_id=1, source_target_pairs={{0,3},{1,2},{2,1},{3,0},{4,7},{5,6},{6,5},{7,4},{8,11},{9,10},{10,... | collective-permute-start | bytes 147464 | tf_op jit(solution)/shard_map/ppermute | solution.py:73
  15.7 2.7 %collective-permute-start.16 = (s32[2,256]{1,0:T(2,128)S(1)}, s32[2,256]{1,0:T(2,128)S(1)}, u32[]{:S(2)}, u32[]{:S(2)}) collective-permute-start(s32[2,256]{1,0:T(2,128)S(1)} %collective-permute-done.14), channel_id=1, source_target_pairs={{0,8},{8,0},{16,24},{24,16},{1,9},{9,1},{17,25},{25,17},{2,10},{10... | collective-permute-start | bytes 6152 | tf_op jit(solution)/shard_map/ppermute | solution.py:73
  15.7 10.5 %collective-permute-start.3 = (bf16[32,768]{1,0:T(8,128)(2,1)}, bf16[32,768]{1,0:T(8,128)(2,1)S(1)}, u32[]{:S(2)}, u32[]{:S(2)}) collective-permute-start(bf16[32,768]{1,0:T(8,128)(2,1)} %param.4), channel_id=1, source_target_pairs={{0,4},{1,5},{2,6},{3,7},{4,0},{5,1},{6,2},{7,3},{8,12},{9,13},{10,... | collective-permute-start | bytes 147464 | tf_op jit(solution)/shard_map/ppermute | solution.py:73
  18.3 8.5 %collective-permute-start.4 = (bf16[32,768]{1,0:T(8,128)(2,1)}, bf16[32,768]{1,0:T(8,128)(2,1)S(1)}, u32[]{:S(2)}, u32[]{:S(2)}) collective-permute-start(bf16[32,768]{1,0:T(8,128)(2,1)} %param.4), channel_id=1, source_target_pairs={{0,5},{1,4},{2,7},{3,6},{4,1},{5,0},{6,3},{7,2},{8,13},{9,12},{10,... | collective-permute-start | bytes 147464 | tf_op jit(solution)/shard_map/ppermute | solution.py:73
  19.1 8.5 %collective-permute-start.5 = (bf16[32,768]{1,0:T(8,128)(2,1)}, bf16[32,768]{1,0:T(8,128)(2,1)S(1)}, u32[]{:S(2)}, u32[]{:S(2)}) collective-permute-start(bf16[32,768]{1,0:T(8,128)(2,1)} %param.4), channel_id=1, source_target_pairs={{0,6},{1,7},{2,4},{3,5},{4,2},{5,3},{6,0},{7,1},{8,14},{9,15},{10,... | collective-permute-start | bytes 147464 | tf_op jit(solution)/shard_map/ppermute | solution.py:73
  22.6 7.1 %collective-permute-start.6 = (bf16[32,768]{1,0:T(8,128)(2,1)}, bf16[32,768]{1,0:T(8,128)(2,1)S(1)}, u32[]{:S(2)}, u32[]{:S(2)}) collective-permute-start(bf16[32,768]{1,0:T(8,128)(2,1)} %param.4), channel_id=1, source_target_pairs={{0,7},{1,6},{2,5},{3,4},{4,3},{5,2},{6,1},{7,0},{8,15},{9,14},{10,... | collective-permute-start | bytes 147464 | tf_op jit(solution)/shard_map/ppermute | solution.py:73
  30.4 9.7 %collective-permute-start.17 = (bf16[256,768]{1,0:T(8,128)(2,1)}, bf16[256,768]{1,0:T(8,128)(2,1)S(1)}, u32[]{:S(2)}, u32[]{:S(2)}) collective-permute-start(bf16[256,768]{1,0:T(8,128)(2,1)} %get-tuple-element.32), channel_id=1, source_target_pairs={{0,16},{8,24},{16,0},{24,8},{1,17},{9,25},{17,1},{25,9},{2,18},{10... | collective-permute-start | bytes 1179656 | tf_op jit(solution)/shard_map/ppermute | solution.py:73
  30.9 16.6 %collective-permute-start.18 = (bf16[256,768]{1,0:T(8,128)(2,1)}, bf16[256,768]{1,0:T(8,128)(2,1)S(1)}, u32[]{:S(2)}, u32[]{:S(2)}) collective-permute-start(bf16[256,768]{1,0:T(8,128)(2,1)} %get-tuple-element.32), channel_id=1, source_target_pairs={{0,8},{8,0},{16,24},{24,16},{1,9},{9,1},{17,25},{25,17},{2,10},{10... | collective-permute-start | bytes 1179656 | tf_op jit(solution)/shard_map/ppermute | solution.py:73
  40.1 10.2 %collective-permute-start.19 = (bf16[256,768]{1,0:T(8,128)(2,1)S(1)}, bf16[256,768]{1,0:T(8,128)(2,1)S(1)}, u32[]{:S(2)}, u32[]{:S(2)}) collective-permute-start(bf16[256,768]{1,0:T(8,128)(2,1)S(1)} %collective-permute-done.17), channel_id=1, source_target_pairs={{0,8},{8,0},{16,24},{24,16},{1,9},{9,1},{17,25},{25,17},{2,10},{10... | collective-permute-start | bytes 1179656 | tf_op jit(solution)/shard_map/ppermute | solution.py:73
  40.1 12.7 %collective-permute-start.10 = (bf16[32,768]{1,0:T(8,128)(2,1)S(1)}, bf16[32,768]{1,0:T(8,128)(2,1)S(1)}, u32[]{:S(2)}, u32[]{:S(2)}) collective-permute-start(bf16[32,768]{1,0:T(8,128)(2,1)S(1)} %get-tuple-element.27), channel_id=1, source_target_pairs={{0,4},{1,5},{2,6},{3,7},{4,0},{5,1},{6,2},{7,3},{8,12},{9,13},{10,... | collective-permute-start | bytes 147464 | tf_op jit(solution)/shard_map/ppermute | solution.py:73
  42.4 10.4 %collective-permute-start.11 = (bf16[32,768]{1,0:T(8,128)(2,1)S(1)}, bf16[32,768]{1,0:T(8,128)(2,1)S(1)}, u32[]{:S(2)}, u32[]{:S(2)}) collective-permute-start(bf16[32,768]{1,0:T(8,128)(2,1)S(1)} %get-tuple-element.26), channel_id=1, source_target_pairs={{0,5},{1,4},{2,7},{3,6},{4,1},{5,0},{6,3},{7,2},{8,13},{9,12},{10,... | collective-permute-start | bytes 147464 | tf_op jit(solution)/shard_map/ppermute | solution.py:73
  44.3 17.1 %collective-permute-start.12 = (bf16[32,768]{1,0:T(8,128)(2,1)S(1)}, bf16[32,768]{1,0:T(8,128)(2,1)S(1)}, u32[]{:S(2)}, u32[]{:S(2)}) collective-permute-start(bf16[32,768]{1,0:T(8,128)(2,1)S(1)} %get-tuple-element.25), channel_id=1, source_target_pairs={{0,6},{1,7},{2,4},{3,5},{4,2},{5,3},{6,0},{7,1},{8,14},{9,15},{10,... | collective-permute-start | bytes 147464 | tf_op jit(solution)/shard_map/ppermute | solution.py:73
  47.5 13.9 %collective-permute-start.13 = (bf16[32,768]{1,0:T(8,128)(2,1)S(1)}, bf16[32,768]{1,0:T(8,128)(2,1)S(1)}, u32[]{:S(2)}, u32[]{:S(2)}) collective-permute-start(bf16[32,768]{1,0:T(8,128)(2,1)S(1)} %get-tuple-element.24), channel_id=1, source_target_pairs={{0,7},{1,6},{2,5},{3,4},{4,3},{5,2},{6,1},{7,0},{8,15},{9,14},{10,... | collective-permute-start | bytes 147464 | tf_op jit(solution)/shard_map/ppermute | solution.py:73
  50.3 11.1 %collective-permute-start.7 = (bf16[32,768]{1,0:T(8,128)(2,1)S(1)}, bf16[32,768]{1,0:T(8,128)(2,1)S(1)}, u32[]{:S(2)}, u32[]{:S(2)}) collective-permute-start(bf16[32,768]{1,0:T(8,128)(2,1)S(1)} %get-tuple-element.30), channel_id=1, source_target_pairs={{0,1},{1,0},{2,3},{3,2},{4,5},{5,4},{6,7},{7,6},{8,9},{9,8},{10,11... | collective-permute-start | bytes 147464 | tf_op jit(solution)/shard_map/ppermute | solution.py:73
  52.8 8.6 %collective-permute-start.8 = (bf16[32,768]{1,0:T(8,128)(2,1)S(1)}, bf16[32,768]{1,0:T(8,128)(2,1)S(1)}, u32[]{:S(2)}, u32[]{:S(2)}) collective-permute-start(bf16[32,768]{1,0:T(8,128)(2,1)S(1)} %get-tuple-element.29), channel_id=1, source_target_pairs={{0,2},{1,3},{2,0},{3,1},{4,6},{5,7},{6,4},{7,5},{8,10},{9,11},{10,... | collective-permute-start | bytes 147464 | tf_op jit(solution)/shard_map/ppermute | solution.py:73
  52.8 8.6 %collective-permute-start.9 = (bf16[32,768]{1,0:T(8,128)(2,1)S(1)}, bf16[32,768]{1,0:T(8,128)(2,1)S(1)}, u32[]{:S(2)}, u32[]{:S(2)}) collective-permute-start(bf16[32,768]{1,0:T(8,128)(2,1)S(1)} %get-tuple-element.28), channel_id=1, source_target_pairs={{0,3},{1,2},{2,1},{3,0},{4,7},{5,6},{6,5},{7,4},{8,11},{9,10},{10,... | collective-permute-start | bytes 147464 | tf_op jit(solution)/shard_map/ppermute | solution.py:73

commit v3 on v1

--- a/solution.py
+++ b/solution.py
@@ -68,21 +68,6 @@
     return (query_grad, weight_grad)
 
 
-def swap(value, axis, bit):
-    count = lax.axis_size(axis)
-    return lax.ppermute(value, axis, [(i, i ^ bit) for i in range(count)])
-
-
-def codes(sibling_blocks, positive_slot, blocks_dev):
-    first = lax.axis_index("lab") * blocks_dev
-    local = sibling_blocks.T - first
-    inside = (local >= 0) & (local < blocks_dev)
-    chosen = jnp.max(jnp.where(inside, local, -1), axis=0)
-    steps = jnp.arange(local.shape[0], dtype=jnp.int32)[:, None]
-    pblock = jnp.sum(jnp.where(steps == (positive_slot // BLOCK)[None, :], local, 0), axis=0)
-    return jnp.stack([chosen, pblock * BLOCK + positive_slot % BLOCK])
-
-
 def slopes(rows, weights, code):
     lab_dev = weights.shape[0]
     scores = lax.dot_general(
@@ -96,30 +81,32 @@
 
 def dense_shards(queries, label_weights, sibling_blocks, positive_slot):
     q_home, width = queries.shape
+    qcount, picks = sibling_blocks.shape
     blocks_dev = label_weights.shape[0] // BLOCK
     homes = lax.axis_size("lab")
     groups = lax.axis_size("pb")
-    code = codes(sibling_blocks, positive_slot, blocks_dev)
-    copies = jnp.broadcast_to(queries[None], (homes, q_home, width))
-    own = lax.all_to_all(copies, "lab", split_axis=0, concat_axis=0, tiled=True)
-    parts = [own.reshape(homes * q_home, width)]
-    notes = [code]
-    bit = groups // 2
-    while bit:
-        parts = parts + [swap(part, "pb", bit) for part in parts]
-        notes = notes + [swap(note, "pb", bit) for note in notes]
-        bit //= 2
-    slope = slopes(parts[0], label_weights, notes[0])
+    me = lax.axis_index("lab")
+    own_blocks = lax.dynamic_slice_in_dim(sibling_blocks, me * q_home, q_home, 0)
+    own_slot = lax.dynamic_slice_in_dim(positive_slot, me * q_home, q_home, 0)[:, None]
+    columns = jnp.concatenate([own_blocks, own_slot // BLOCK, own_slot % BLOCK], axis=1)
+    columns = jnp.pad(columns, ((0, 0), (0, BLOCK - columns.shape[1])))
+    carried = jnp.concatenate([queries, columns.astype(jnp.bfloat16)], axis=1)
+    every = lax.all_gather(carried, ("pb", "lab"), axis=0, tiled=True)
+    rows = every[:, :width]
+    ints = every[:, width : width + picks + 2].astype(jnp.int32).T
+    local = ints[:picks] - me * blocks_dev
+    inside = (local >= 0) & (local < blocks_dev)
+    chosen = jnp.max(jnp.where(inside, local, -1), axis=0)
+    steps = jnp.arange(picks, dtype=jnp.int32)[:, None]
+    pblock = jnp.sum(jnp.where(steps == ints[picks], local, 0), axis=0)
+    code = jnp.stack([chosen, pblock * BLOCK + ints[picks + 1]])
+    slope = slopes(rows, label_weights, code)
+    mine = lax.dynamic_slice_in_dim(slope, lax.axis_index("pb") * qcount, qcount, 1)
     dq = lax.dot_general(
-        slope, label_weights, (((0,), (0,)), ((), ())), preferred_element_type=jnp.float32
+        mine, label_weights, (((0,), (0,)), ((), ())), preferred_element_type=jnp.float32
     )
-    dq = dq.astype(jnp.bfloat16).reshape(homes, q_home, width)
-    incoming = lax.all_to_all(dq, "lab", split_axis=0, concat_axis=0, tiled=True)
-    query_grad = jnp.sum(incoming.astype(jnp.float32), axis=0)
-    rows = jnp.concatenate(parts, axis=0)
-    note = jnp.concatenate(notes, axis=1)
-    every = slopes(rows, label_weights, note)
-    total = jnp.dot(every, rows, preferred_element_type=jnp.float32)
+    query_grad = lax.psum_scatter(dq, "lab", scatter_dimension=0, tiled=True)
+    total = jnp.dot(slope, rows, preferred_element_type=jnp.float32)
     weight_grad = (total / groups).astype(jnp.bfloat16)
     return (query_grad, weight_grad)
 

time: 46.3 us -> 147 us (3.17)
  waiting for transfers between devices: 19.7 us -> 116 us
  between operations: 0.66 us -> 14.1 us
  starting transfers between devices: 13.5 us -> 0.08 us
  matrix products: 7.5 us -> 10 us
  local copies, waits for them, and re-layouts: 1.71 us -> 3.49 us
    all_gather x0 -> x1, waiting for transfers between devices: none -> 59.4 us  [dense_shards(): every = lax.all_gather(carried, ('pb', 'lab'), axis=0, tiled=True)]
    reduce_scatter x0 -> x1, waiting for transfers between devices: none -> 56.9 us  [dense_shards(): query_grad = lax.psum_scatter(dq, 'lab', scatter_dimension=0, tiled=True)]
    all_to_all x2 -> x0, waiting for transfers between devices: 16.1 us -> none  [the longest x1 9.59 us: dense_shards(): own = lax.all_to_all(copies, 'lab', split_axis=0, concat_axis=0, tiled=True)]
    all_to_all x2 -> x0, starting transfers between devices: 10.9 us -> none  [the longest x1 7.28 us: dense_shards(): own = lax.all_to_all(copies, 'lab', split_axis=0, concat_axis=0, tiled=True)]
    ppermute x6 -> x0, waiting for transfers between devices: 3.69 us -> none  [swap(): return lax.ppermute(value, axis, [(i, i ^ bit) for i in range(count)])]
    ppermute x6 -> x0, starting transfers between devices: 2.61 us -> none  [swap(): return lax.ppermute(value, axis, [(i, i ^ bit) for i in range(count)])]
    dot_general x2 -> x3, matrix products: 7.5 us -> 10 us  [the longest x1 4.6 us: dense_shards(): total = jnp.dot(slope, rows, preferred_element_type=jnp.float32)]
    broadcast_in_dim x1 -> x0, local copies, waits for them, and re-layouts: 1.69 us -> none  [dense_shards(): copies = jnp.broadcast_to(queries[None], (homes, q_home, width))]
  transfers between devices with their start and end apart: 8 -> 2, of which waited for: 4 -> 2; matrix products, arithmetic and copies ran while one was open for 12% -> 3% of each run, Pallas kernels for 0% -> 0%
where the time goes in v3:
time: 147 us
  waiting for transfers between devices  116 us (79%)
  between operations  14.1 us (10%)
  matrix products  10 us (7%)
  local copies, waits for them, and re-layouts  3.49 us (2%)
  other arithmetic  2.47 us (2%)
    all_gather x1, waiting for transfers between devices, dense_shards(): every = lax.all_gather(carried, ('pb', 'lab'), axis=0, tiled=True)  59.4 us
    reduce_scatter x1, waiting for transfers between devices, dense_shards(): query_grad = lax.psum_scatter(dq, 'lab', scatter_dimension=0, tiled=True)  56.9 us
    dot_general x1, matrix products, dense_shards(): total = jnp.dot(slope, rows, preferred_element_type=jnp.float32)  4.6 us
    dot_general x1, matrix products, slopes(): lax.dot_general(weights, rows, (((1,), (1,)), ((), ())), preferred_elemen...  3.96 us
  transfers between devices with their start and end apart: 2, of which 2 were waited for; matrix products, arithmetic and copies ran while one was open for 3% of the time, Pallas kernels for 0%

profile of v3, /device:TPU:0, one launch (start us, length us, event | category | flops | bytes accessed | tf_op | source)
XLA Modules:
  0.0 146.5 jit_solution(18032159164753579003)
XLA Ops:
  7.2 0.0 copy-start
  7.2 0.0 all-gather.2.cloned.1.call-start
  7.2 0.9 convert_bitcast_fusion.1
  8.1 0.8 constant_dynamic-slice_fusion
  8.9 0.1 copy.10
  9.0 0.1 copy.9
  9.1 0.1 copy.12
  9.2 0.1 fusion.10
  9.2 1.4 pad_maximum_fusion
  10.7 0.0 all-gather.2.cloned.1.call-update
  10.7 0.0 reduce-scatter.2.cloned.1.call-start
  10.8 59.4 %all-gather.2.cloned.1.call-done = bf16[1024,896]{1,0:T(8,128)(2,1)} async-done(((bf16[32,896]{1,0:T(8,128)(2,1)}), bf16[1024,896]{1,0:T(8,128)(2,1)}) %all-gather.2.cloned.1.call-update) | async-done | bytes 1835024 | tf_op jit(solution)/shard_map/all_gather | solution.py:94
  70.2 1.0 slice.20
  71.1 0.1 copy.13
  71.4 0.0 copy-done
  71.4 4.0 %fusion.1 = bf16[1024,1024]{0,1:T(8,128)(2,1)S(1)} fusion(bf16[1024,768]{1,0:T(8,128)(2,1)S(1)} %copy-done, s32[1024]{0:T(1024)S(1)} %bitcast.20, s32[1024]{0:T(1024)S(1)} %add_select_fusion, s32[1024]{0:T(1024)S(1)} %get-tuple-element.2, bf16[1024,896]{1,0:T(8,128)(2,1)} %all-gather.2.cloned.1.call-done), kind=kOutput, calls=%fused_computation.2 | convolution fusion | flops 1620049920 | bytes 5255168 | tf_op jit(solution)/shard_map/dot_general | solution.py:73
  75.3 0.0 copy-start.1
  75.4 1.3 copy-done.1
  76.7 0.0 copy-start.2
  76.7 1.5 %fusion.4 = f32[256,768]{1,0:T(8,128)} fusion(bf16[1024,768]{1,0:T(8,128)(2,1)S(1)} %copy-done, bf16[1024,1024]{0,1:T(8,128)(2,1)S(1)} %fusion.1, s32[]{:T(128)S(6)} %select_n.55), kind=kOutput, calls=%fused_computation.7 | convolution fusion | flops 402653184 | bytes 2883588 | tf_op jit(solution)/shard_map/dot_general | solution.py:105
  78.2 0.0 reduce-scatter.2.cloned.1.call-update
  78.2 0.0 copy-done.2
  78.2 4.6 %multiply_convert_fusion = bf16[1024,768]{1,0:T(8,128)(2,1)} fusion(bf16[1024,1024]{0,1:T(8,128)(2,1)} %copy-done.1, bf16[1024,896]{1,0:T(8,128)(2,1)S(1)} %copy-done.2), kind=kOutput, calls=%fused_computation.4 | convolution fusion | flops 1612185600 | bytes 5242880 | tf_op jit(solution)/shard_map/dot_general | solution.py:109
  82.8 56.9 %reduce-scatter.2.cloned.1.call-done = f32[32,768]{1,0:T(8,128)} async-done(((f32[256,768]{1,0:T(8,128)}), f32[32,768]{1,0:T(8,128)}) %reduce-scatter.2.cloned.1.call-update) | async-done | bytes 98320 | tf_op jit(solution)/shard_map/reduce_scatter | solution.py:108
  (8 shorter events, 0.1 us)
Async XLA Ops:
  7.2 64.2 %copy-start = (bf16[1024,768]{1,0:T(8,128)(2,1)S(1)}, bf16[1024,768]{1,0:T(8,128)(2,1)}, u32[]{:S(2)}) copy-start(bf16[1024,768]{1,0:T(8,128)(2,1)} %param.5) | copy-start | bytes 4718596
  7.2 63.0 %all-gather.2.cloned.1.call-start = ((), (), s32[]{:S(2)}) async-start(), calls=%async_computation.1 | async-start | bytes 1892352 | tf_op jit(solution)/shard_map/all_gather | solution.py:94
  10.7 129.0 %reduce-scatter.2.cloned.1.call-start = ((), (), s32[]{:S(2)}) async-start(), calls=%async_computation.2 | async-start | bytes 884736 | tf_op jit(solution)/shard_map/reduce_scatter | solution.py:108
  75.3 1.3 copy-start.1
  76.7 1.5 %copy-start.2 = (bf16[1024,896]{1,0:T(8,128)(2,1)S(1)}, bf16[1024,896]{1,0:T(8,128)(2,1)}, u32[]{:S(2)}) copy-start(bf16[1024,896]{1,0:T(8,128)(2,1)} %all-gather.2.cloned.1.call-done) | copy-start | bytes 5505028
Sparse Core Ops, SparseCore 0:
  11.5 58.6 all-gather.1
  78.3 61.3 reduce-scatter.1

commit v4 on v0

--- a/solution.py
+++ b/solution.py
@@ -1,10 +1,14 @@
 import jax
 import jax.numpy as jnp
 from jax import lax
+from jax.experimental import pallas as pl
+from jax.experimental.pallas import tpu as pltpu
 from jax.sharding import PartitionSpec as P
 
 BLOCK = 128
 K = 8
+NOTE = 16
+VMEM_LIMIT = 24 * 1024 * 1024
 
 
 def pack_index(touched, width_slots, fill_value):
@@ -19,7 +23,7 @@
     return table[:, :width_slots]
 
 
-def shards(queries, label_weights, sibling_blocks, positive_slot):
+def sparse_shards(queries, label_weights, sibling_blocks, positive_slot):
     width = queries.shape[1]
     qcount = sibling_blocks.shape[0]
     lab_dev = label_weights.shape[0]
@@ -37,12 +41,10 @@
     target = (label_ids[None, :, :] == positive[:, None, None]).astype(jnp.float32)
     slope = jnp.where(chosen_all[:, :, None], jax.nn.sigmoid(scores) - target, 0.0)
     slope = slope.astype(jnp.bfloat16).reshape(count, lab_dev)
-    dq_rows = jnp.dot(slope, label_weights, preferred_element_type=jnp.float32)
-    dq_all = dq_rows
+    dq_all = jnp.dot(slope, label_weights, preferred_element_type=jnp.float32)
     w_acc = lax.dot_general(
         slope, piece, (((0,), (0,)), ((), ())), preferred_element_type=jnp.float32
     )
-    dq_all, w_acc = (dq_all, w_acc)
     homes = lax.axis_size("lab")
     q_home = qcount // homes
     slots = q_home * K // homes
@@ -70,7 +72,237 @@
     return (query_grad, weight_grad)
 
 
+def swap(value, axis, bit):
+    count = lax.axis_size(axis)
+    return lax.ppermute(value, axis, [(i, i ^ bit) for i in range(count)])
+
+
+def local_call(body, outs, args, flops=0):
+    scalars = [arg for arg in args if arg.dtype == jnp.int32]
+    size = sum(a.size * a.dtype.itemsize for a in list(args) + list(outs))
+    specs = [
+        pl.BlockSpec(memory_space=pltpu.SMEM if arg.dtype == jnp.int32 else pltpu.VMEM)
+        for arg in args
+    ]
+    del scalars
+    return pl.pallas_call(
+        body,
+        out_shape=outs,
+        in_specs=specs,
+        out_specs=[pl.BlockSpec(memory_space=pltpu.VMEM)] * len(outs),
+        cost_estimate=pl.CostEstimate(flops=flops, bytes_accessed=size, transcendentals=0),
+        compiler_params=pltpu.CompilerParams(vmem_limit_bytes=VMEM_LIMIT),
+    )(*args)
+
+
+def like(rows, width, dtype):
+    return jax.ShapeDtypeStruct((rows, width), dtype)
+
+
+def join_body(side_ref, own_ref, came_ref, out_ref):
+    rows = own_ref.shape[0]
+    side = side_ref[0]
+    out_ref[pl.ds(pl.multiple_of(side * rows, rows), rows), :] = own_ref[...]
+    out_ref[pl.ds(pl.multiple_of((1 - side) * rows, rows), rows), :] = came_ref[...]
+
+
+def join_note_body(side_ref, own_ref, came_ref, note_ref, out_ref, noted_ref):
+    rows = own_ref.shape[0]
+    join_body(side_ref, own_ref, came_ref, out_ref)
+    noted_ref[: 2 * rows, :] = out_ref[...]
+    noted_ref[2 * rows :, :] = note_ref[...]
+
+
+def slope_of(rows, weights_ref, chosen, place):
+    count = rows.shape[0]
+    blocks = weights_ref.shape[0] // BLOCK
+    scores = lax.dot_general(
+        weights_ref[...], rows, (((1,), (1,)), ((), ())), preferred_element_type=jnp.float32
+    )
+    named = jnp.zeros((BLOCK, count), jnp.float32)
+    for block in range(blocks):
+        named = jnp.where(chosen == block, scores[block * BLOCK : (block + 1) * BLOCK], named)
+    ids = lax.broadcasted_iota(jnp.int32, (BLOCK, count), 0)
+    slope = jax.nn.sigmoid(named) - jnp.where(ids == place, 1.0, 0.0)
+    parts = [jnp.where(chosen == block, slope, 0.0).astype(jnp.bfloat16) for block in range(blocks)]
+    return jnp.concatenate(parts, axis=0)
+
+
+def read_note(note, which, count):
+    chosen = note[2 * which : 2 * which + 1, :count].astype(jnp.int32)
+    place = note[2 * which + 1 : 2 * which + 2, :count].astype(jnp.int32)
+    return chosen, place
+
+
+def grad_body(which, rows_ref, weights_ref, note_ref, dq_ref, slope_ref):
+    rows = rows_ref[...]
+    note = note_ref[...].astype(jnp.float32)
+    slope = slope_of(rows, weights_ref, *read_note(note, which, rows.shape[0]))
+    slope_ref[...] = slope
+    dq = lax.dot_general(
+        slope, weights_ref[...], (((0,), (0,)), ((), ())), preferred_element_type=jnp.float32
+    )
+    dq_ref[...] = dq.astype(dq_ref.dtype)
+
+
+def near_body(rows_ref, weights_ref, note_ref, dq_ref, slope_ref):
+    grad_body(0, rows_ref, weights_ref, note_ref, dq_ref, slope_ref)
+
+
+def far_body(near_ref, rows_ref, weights_ref, note_ref, dq_ref, slope_ref, all_ref):
+    grad_body(1, rows_ref, weights_ref, note_ref, dq_ref, slope_ref)
+    noted = near_ref.shape[0]
+    all_ref[:noted, :] = near_ref[...]
+    all_ref[noted:, :] = rows_ref[...]
+
+
+def fold_body(side_ref, kept_ref, came_ref, keep_ref, send_ref):
+    rows = keep_ref.shape[0]
+    side = side_ref[0]
+    mine = pl.ds(pl.multiple_of(side * rows, rows), rows)
+    other = pl.ds(pl.multiple_of((1 - side) * rows, rows), rows)
+    keep_ref[...] = kept_ref[mine, :] + came_ref[mine, :].astype(jnp.float32)
+    send = kept_ref[other, :] + came_ref[other, :].astype(jnp.float32)
+    send_ref[...] = send.astype(send_ref.dtype)
+
+
+def last_body(kept_ref, came_ref, out_ref):
+    out_ref[...] = kept_ref[...] + came_ref[...].astype(jnp.float32)
+
+
+def slopes_of_set(near_rows, far_rows, note, weights_ref):
+    half = near_rows.shape[0]
+    rows = jnp.concatenate([near_rows, far_rows], axis=0)
+    codes = [read_note(note, which, half) for which in range(2)]
+    chosen = jnp.concatenate([codes[0][0], codes[1][0]], axis=1)
+    place = jnp.concatenate([codes[0][1], codes[1][1]], axis=1)
+    return rows, slope_of(rows, weights_ref, chosen, place)
+
+
+def early_body(near_ref, far_ref, near_slope_ref, far_slope_ref, set_ref, weights_ref, acc_ref):
+    half = near_ref.shape[0]
+    note = set_ref[half : half + NOTE, :].astype(jnp.float32)
+    rows, slope = slopes_of_set(set_ref[:half, :], set_ref[half + NOTE :, :], note, weights_ref)
+    rows = jnp.concatenate([near_ref[...], far_ref[...], rows], axis=0)
+    slope = jnp.concatenate([near_slope_ref[...], far_slope_ref[...], slope], axis=1)
+    acc_ref[...] = jnp.dot(slope, rows, preferred_element_type=jnp.float32)
+
+
+def late_body(groups, *refs):
+    *set_refs, weights_ref, acc_ref, out_ref = refs
+    rows, slopes = [], []
+    for near_ref, far_ref in zip(set_refs[::2], set_refs[1::2]):
+        half = far_ref.shape[0]
+        note = near_ref[half:, :].astype(jnp.float32)
+        part, slope = slopes_of_set(near_ref[:half, :], far_ref[...], note, weights_ref)
+        rows.append(part)
+        slopes.append(slope)
+    total = acc_ref[...] + jnp.dot(
+        jnp.concatenate(slopes, axis=1),
+        jnp.concatenate(rows, axis=0),
+        preferred_element_type=jnp.float32,
+    )
+    out_ref[...] = (total / groups).astype(out_ref.dtype)
+
+
+def make_note(sibling_blocks, positive_slot, blocks_dev, homes, width):
+    me = lax.axis_index("lab")
+    local = sibling_blocks.T - me * blocks_dev
+    inside = (local >= 0) & (local < blocks_dev)
+    chosen = jnp.max(jnp.where(inside, local, -1), axis=0)
+    steps = jnp.arange(local.shape[0], dtype=jnp.int32)[:, None]
+    pblock = jnp.sum(jnp.where(steps == (positive_slot // BLOCK)[None, :], local, 0), axis=0)
+    place = jnp.where(pblock == chosen, positive_slot % BLOCK, -1)
+    code = jnp.stack([chosen, place]).astype(jnp.bfloat16)
+    bits = homes.bit_length() - 1
+    code = code.reshape((2,) + (2,) * bits + (-1,))
+    code = code.transpose((bits, 0) + tuple(range(bits - 1, 0, -1)) + (bits + 1,))
+    code = code.reshape(2, 2, -1)
+    code = jnp.where(me % 2 == 0, code, code[::-1]).reshape(4, -1)
+    return jnp.pad(code, ((0, NOTE - 4), (0, width - code.shape[1])))
+
+
+def dense_shards(queries, label_weights, sibling_blocks, positive_slot):
+    q_home, width = queries.shape
+    qcount = sibling_blocks.shape[0]
+    half = qcount // 2
+    lab_dev = label_weights.shape[0]
+    homes = lax.axis_size("lab")
+    groups = lax.axis_size("pb")
+    me = lax.axis_index("lab")
+    f32, bf16 = jnp.float32, jnp.bfloat16
+
+    def side(bit):
+        return jnp.reshape((me // bit) % 2, (1,)).astype(jnp.int32)
+
+    note = make_note(sibling_blocks, positive_slot, lab_dev // BLOCK, homes, width)
+    near, bit = queries, homes // 2
+    while bit > 2:
+        near = local_call(
+            join_body, [like(2 * near.shape[0], width, bf16)], [side(bit), near, swap(near, "lab", bit)]
+        )[0]
+        bit //= 2
+    near, noted = local_call(
+        join_note_body,
+        [like(half, width, bf16), like(half + NOTE, width, bf16)],
+        [side(2), near, swap(near, "lab", 2), note],
+    )
+    far = swap(near, "lab", 1)
+    work = 4 * half * lab_dev * width
+    near_dq, near_slope = local_call(
+        near_body,
+        [like(half, width, f32), like(lab_dev, half, bf16)],
+        [near, label_weights, note],
+        work,
+    )
+    far_dq, far_slope, whole = local_call(
+        far_body,
+        [like(half, width, bf16), like(lab_dev, half, bf16), like(qcount + NOTE, width, bf16)],
+        [noted, far, label_weights, note],
+        work,
+    )
+    kept, came, bit = near_dq, swap(far_dq, "lab", 1), 2
+    while bit < homes:
+        rows = kept.shape[0] // 2
+        kept, send = local_call(
+            fold_body, [like(rows, width, f32), like(rows, width, bf16)], [side(bit), kept, came]
+        )
+        came = swap(send, "lab", bit)
+        bit *= 2
+    query_grad = local_call(last_body, [like(q_home, width, f32)], [kept, came])[0]
+    sets = [(swap(noted, "pb", groups // 2), swap(far, "pb", groups // 2))]
+    bit = groups // 4
+    mate = swap(whole, "pb", 1)
+    while bit:
+        sets = sets + [(swap(a, "pb", bit), swap(b, "pb", bit)) for a, b in sets]
+        bit //= 2
+    acc = local_call(
+        early_body,
+        [like(lab_dev, width, f32)],
+        [near, far, near_slope, far_slope, mate, label_weights],
+        3 * work,
+    )[0]
+    flat = [part for pair in sets for part in pair]
+    weight_grad = local_call(
+        lambda *refs: late_body(groups, *refs),
+        [like(lab_dev, width, bf16)],
+        flat + [label_weights, acc],
+        4 * work,
+    )[0]
+    return (query_grad, weight_grad)
+
+
 def solution(mesh):
+    groups, homes = mesh.shape["pb"], mesh.shape["lab"]
+
+    def shards(queries, label_weights, sibling_blocks, positive_slot):
+        every_row_everywhere = homes == K
+        few = groups * sibling_blocks.shape[0] <= 2 * label_weights.shape[0]
+        paired = groups == 4 and homes & (homes - 1) == 0
+        one_block = label_weights.shape[0] // BLOCK <= K
+        plan = dense_shards if every_row_everywhere and few and paired and one_block else sparse_shards
+        return plan(queries, label_weights, sibling_blocks, positive_slot)
+
     in_specs = (P(("pb", "lab"), None), P("lab", None), P("pb", None), P("pb"))
     out_specs = (P(("pb", "lab"), None), P("lab", None))
     return jax.shard_map(shards, mesh=mesh, in_specs=in_specs, out_specs=out_specs, check_vma=False)

time: 129 us -> 46.7 us (0.36)
  blocking collectives: 33 us -> 0 us
  local copies, waits for them, and re-layouts: 28.9 us -> 2.48 us
  waiting for transfers between devices: 31.8 us -> 17.3 us
  between operations: 14.2 us -> 0.76 us
  starting transfers between devices: 5.7 us -> 15 us
  other arithmetic: 11.1 us -> 2.11 us
  Pallas kernels: 0 us -> 8.86 us
  matrix products: 3.7 us -> 0 us
    all_gather x1 -> x0, blocking collectives: 33 us -> none  [shards(): piece = lax.all_gather(queries, 'lab', axis=0, tiled=True)]
    psum x1 -> x0, waiting for transfers between devices: 29.6 us -> none  [shards(): total = lax.psum(w_acc, 'pb')]
    scatter x2 -> x0, local copies, waits for them, and re-layouts: 22.4 us -> none  [pack_index(): jnp.full((homes, width_slots + 1), fill_value, jnp.int32)]
    ppermute x0 -> x11, waiting for transfers between devices: none -> 17.3 us  [swap(): return lax.ppermute(value, axis, [(i, i ^ bit) for i in range(count)])]
    ppermute x0 -> x11, starting transfers between devices: none -> 15 us  [swap(): return lax.ppermute(value, axis, [(i, i ^ bit) for i in range(count)])]
    pallas_call x0 -> x9, Pallas kernels: none -> 8.86 us  [local_call(): pl.pallas_call(body, out_shape=outs, in_specs=specs, out_specs=[pl.BlockS...]
    all_to_all x1 -> x0, starting transfers between devices: 5.66 us -> none  [shards(): lax.all_to_all(outgoing, 'lab', split_axis=0, concat_axis=0, tiled=True)]
    gather x3 -> x0, local copies, waits for them, and re-layouts: 4.07 us -> none  [the longest x1 2.28 us: shards(): jnp.take_along_axis(sibling_blocks, (positive_slot // BLOCK)[:, None], ax...]
  transfers between devices with their start and end apart: 2 -> 11, of which waited for: 2 -> 7; matrix products, arithmetic and copies ran while one was open for 25% -> 5% of each run, Pallas kernels for 0% -> 9%
where the time goes in v4:
time: 46.7 us; the launch traced here: 46.4 us
  waiting for transfers between devices  17.3 us (37%)
  starting transfers between devices  15 us (32%)
  Pallas kernels  8.86 us (19%)
  local copies, waits for them, and re-layouts  2.48 us (5%)
  other arithmetic  2.11 us (5%)
  between operations  0.76 us (2%)
    ppermute x11, waiting for transfers between devices, swap(): return lax.ppermute(value, axis, [(i, i ^ bit) for i in range(count)])  17.3 us
    ppermute x11, starting transfers between devices, swap(): return lax.ppermute(value, axis, [(i, i ^ bit) for i in range(count)])  15 us
    pallas_call x9, Pallas kernels, local_call(): pl.pallas_call(body, out_shape=outs, in_specs=specs, out_specs=[pl.BlockS...  8.86 us
    unnamed x6, local copies, waits for them, and re-layouts  2.21 us
  transfers between devices with their start and end apart: 11, of which 7 were waited for; matrix products, arithmetic and copies ran while one was open for 5% of the time, Pallas kernels for 9%

profile of v4, /device:TPU:0, one launch (start us, length us, event | category | flops | bytes accessed | tf_op | source)
XLA Modules:
  0.0 46.4 jit_solution(6954562322805077705)
XLA Ops:
  0.6 4.1 %collective-permute-start = (bf16[32,768]{1,0:T(8,128)(2,1)}, bf16[32,768]{1,0:T(8,128)(2,1)S(1)}, u32[]{:S(2)}, u32[]{:S(2)}) collective-permute-start(bf16[32,768]{1,0:T(8,128)(2,1)} %own_ref.1), channel_id=1, source_target_pairs={{0,4},{1,5},{2,6},{3,7},{4,0},{5,1},{6,2},{7,3},{8,12},{9,13},{10,... | collective-permute-start | bytes 147464 | tf_op jit(solution)/shard_map/ppermute | solution.py:77
  4.7 0.7 %and_select_fusion.1 = s32[256]{0:T(256)S(1)} fusion(s32[256]{0:T(256)} %param.7), kind=kLoop, calls=%fused_computation.11 | loop fusion | flops 3840 | bytes 2048 | tf_op jit(solution)/shard_map/jit(floor_divide)/jit(_where)/select_n | solution.py:214
  5.4 0.7 %fusion = (s32[256]{0:T(256)S(1)}, s32[256]{0:T(256)S(1)}) fusion(s32[256,8]{0,1:T(8,128)} %param.6, s32[]{:T(128)S(6)} %mul.3, s32[256]{0:T(256)S(1)} %and_select_fusion.1), kind=kLoop, calls=%fused_computation.4 | loop fusion | flops 17920 | bytes 11268 | tf_op jit(solution)/shard_map/reduce_max | solution.py:212
  6.1 0.7 %fusion.4 = (bf16[256]{0:T(256)(128)(2,1)S(1)}, bf16[256]{0:T(256)(128)(2,1)S(1)}) fusion(s32[256]{0:T(256)S(1)} %get-tuple-element.24, s32[256]{0:T(256)} %param.7, s32[256]{0:T(256)S(1)} %get-tuple-element.25), kind=kLoop, calls=%fused_computation.19 | loop fusion | flops 3840 | bytes 4096 | tf_op jit(solution)/shard_map/convert.3
  7.5 0.8 %copy-done.2 = bf16[32,768]{1,0:T(8,128)(2,1)S(1)} copy-done((bf16[32,768]{1,0:T(8,128)(2,1)S(1)}, bf16[32,768]{1,0:T(8,128)(2,1)}, u32[]{:S(2)}) %copy-start.2) | copy-done | bytes 49176
  8.4 1.4 %collective-permute-start.1 = (bf16[64,768]{1,0:T(8,128)(2,1)S(1)}, bf16[64,768]{1,0:T(8,128)(2,1)S(1)}, u32[]{:S(2)}, u32[]{:S(2)}) collective-permute-start(bf16[64,768]{1,0:T(8,128)(2,1)S(1)} %shard_map.59.own_ref), channel_id=1, source_target_pairs={{0,2},{1,3},{2,0},{3,1},{4,6},{5,7},{6,4},{7,5},{8,10},{9,11},{10,... | collective-permute-start | bytes 294920 | tf_op jit(solution)/shard_map/ppermute | solution.py:77
  9.8 3.2 %collective-permute-done.1.came_ref = bf16[64,768]{1,0:T(8,128)(2,1)S(1)} collective-permute-done((bf16[64,768]{1,0:T(8,128)(2,1)S(1)}, bf16[64,768]{1,0:T(8,128)(2,1)S(1)}, u32[]{:S(2)}, u32[]{:S(2)}) %collective-permute-start.1) | collective-permute-done | bytes 98336 | tf_op jit(solution)/shard_map/ppermute | solution.py:77
  13.1 1.8 %collective-permute-start.2 = (bf16[128,768]{1,0:T(8,128)(2,1)S(1)}, bf16[128,768]{1,0:T(8,128)(2,1)S(1)}, u32[]{:S(2)}, u32[]{:S(2)}) collective-permute-start(bf16[128,768]{1,0:T(8,128)(2,1)S(1)} %get-tuple-element.13.rows_ref.near_ref), channel_id=1, source_target_pairs={{0,1},{1,0},{2,3},{3,2},{4,5},{5,4},{6,7},{7,6},{8,9},{9,8},{10,11... | collective-permute-start | bytes 589832 | tf_op jit(solution)/shard_map/ppermute | solution.py:77
  14.9 3.9 %collective-permute-done.2.rows_ref.far_ref = bf16[128,768]{1,0:T(8,128)(2,1)S(1)} collective-permute-done((bf16[128,768]{1,0:T(8,128)(2,1)S(1)}, bf16[128,768]{1,0:T(8,128)(2,1)S(1)}, u32[]{:S(2)}, u32[]{:S(2)}) %collective-permute-start.2) | collective-permute-done | bytes 196640 | tf_op jit(solution)/shard_map/ppermute | solution.py:77
  18.8 1.4 %copy-done = bf16[1024,768]{1,0:T(8,128)(2,1)S(1)} copy-done((bf16[1024,768]{1,0:T(8,128)(2,1)S(1)}, bf16[1024,768]{1,0:T(8,128)(2,1)}, u32[]{:S(2)}) %copy-start) | copy-done | bytes 1572888
  20.2 1.3 %shard_map.62 = (bf16[128,768]{1,0:T(8,128)(2,1)S(1)}, bf16[1024,128]{1,0:T(8,128)(2,1)S(1)}, bf16[272,768]{1,0:T(8,128)(2,1)S(1)}) custom-call(bf16[144,768]{1,0:T(8,128)(2,1)S(1)} %get-tuple-element.15.near_ref, bf16[128,768]{1,0:T(8,128)(2,1)S(1)} %collective-permute-done.2.rows_ref.far_ref, bf16[1024,768]{1,0:T(8,128)(2,1)S(1)} %copy-done, ...), custom_call_target="tpu_custom_call" | custom-call | flops 402653184 | bytes 2891776 | tf_op jit(solution)/shard_map/pallas_call | solution.py:88
  21.6 1.8 %collective-permute-start.3 = (bf16[128,768]{1,0:T(8,128)(2,1)S(1)}, bf16[128,768]{1,0:T(8,128)(2,1)S(1)}, u32[]{:S(2)}, u32[]{:S(2)}) collective-permute-start(bf16[128,768]{1,0:T(8,128)(2,1)S(1)} %get-tuple-element.16), channel_id=1, source_target_pairs={{0,1},{1,0},{2,3},{3,2},{4,5},{5,4},{6,7},{7,6},{8,9},{9,8},{10,11... | collective-permute-start | bytes 589832 | tf_op jit(solution)/shard_map/ppermute | solution.py:77
  23.4 1.5 %collective-permute-start.6 = (bf16[144,768]{1,0:T(8,128)(2,1)S(1)}, bf16[144,768]{1,0:T(8,128)(2,1)S(1)}, u32[]{:S(2)}, u32[]{:S(2)}) collective-permute-start(bf16[144,768]{1,0:T(8,128)(2,1)S(1)} %get-tuple-element.15.near_ref), channel_id=1, source_target_pairs={{0,16},{8,24},{16,0},{24,8},{1,17},{9,25},{17,1},{25,9},{2,18},{10... | collective-permute-start | bytes 663560 | tf_op jit(solution)/shard_map/ppermute | solution.py:77
  24.9 0.5 %collective-permute-start.7 = (bf16[128,768]{1,0:T(8,128)(2,1)S(1)}, bf16[128,768]{1,0:T(8,128)(2,1)S(1)}, u32[]{:S(2)}, u32[]{:S(2)}) collective-permute-start(bf16[128,768]{1,0:T(8,128)(2,1)S(1)} %collective-permute-done.2.rows_ref.far_ref), channel_id=1, source_target_pairs={{0,16},{8,24},{16,0},{24,8},{1,17},{9,25},{17,1},{25,9},{2,18},{10... | collective-permute-start | bytes 589832 | tf_op jit(solution)/shard_map/ppermute | solution.py:77
  25.5 1.3 %shard_map.61 = (f32[128,768]{1,0:T(8,128)S(1)}, bf16[1024,128]{1,0:T(8,128)(2,1)S(1)}) custom-call(bf16[128,768]{1,0:T(8,128)(2,1)S(1)} %get-tuple-element.13.rows_ref.near_ref, bf16[1024,768]{1,0:T(8,128)(2,1)S(1)} %copy-done.1, bf16[16,768]{1,0:T(8,128)(2,1)S(1)} %pad.4.note_ref), custom_call_target="tpu_custom_call" | custom-call | flops 402653184 | bytes 2449408 | tf_op jit(solution)/shard_map/pallas_call | solution.py:88
  26.8 2.2 %collective-permute-done.3.came_ref = bf16[128,768]{1,0:T(8,128)(2,1)S(1)} collective-permute-done((bf16[128,768]{1,0:T(8,128)(2,1)S(1)}, bf16[128,768]{1,0:T(8,128)(2,1)S(1)}, u32[]{:S(2)}, u32[]{:S(2)}) %collective-permute-start.3) | collective-permute-done | bytes 196640 | tf_op jit(solution)/shard_map/ppermute | solution.py:77
  29.0 1.4 %collective-permute-start.4 = (bf16[64,768]{1,0:T(8,128)(2,1)S(1)}, bf16[64,768]{1,0:T(8,128)(2,1)S(1)}, u32[]{:S(2)}, u32[]{:S(2)}) collective-permute-start(bf16[64,768]{1,0:T(8,128)(2,1)S(1)} %get-tuple-element.18), channel_id=1, source_target_pairs={{0,2},{1,3},{2,0},{3,1},{4,6},{5,7},{6,4},{7,5},{8,10},{9,11},{10,... | collective-permute-start | bytes 294920 | tf_op jit(solution)/shard_map/ppermute | solution.py:77
  30.4 1.3 %collective-permute-done.6.refs_0_ = bf16[144,768]{1,0:T(8,128)(2,1)S(1)} collective-permute-done((bf16[144,768]{1,0:T(8,128)(2,1)S(1)}, bf16[144,768]{1,0:T(8,128)(2,1)S(1)}, u32[]{:S(2)}, u32[]{:S(2)}) %collective-permute-start.6) | collective-permute-done | bytes 221216 | tf_op jit(solution)/shard_map/ppermute | solution.py:77
  31.7 3.4 %collective-permute-done.7.refs_1_ = bf16[128,768]{1,0:T(8,128)(2,1)S(1)} collective-permute-done((bf16[128,768]{1,0:T(8,128)(2,1)S(1)}, bf16[128,768]{1,0:T(8,128)(2,1)S(1)}, u32[]{:S(2)}, u32[]{:S(2)}) %collective-permute-start.7) | collective-permute-done | bytes 196640 | tf_op jit(solution)/shard_map/ppermute | solution.py:77
  35.2 2.3 %collective-permute-start.5 = (bf16[32,768]{1,0:T(8,128)(2,1)S(1)}, bf16[32,768]{1,0:T(8,128)(2,1)S(1)}, u32[]{:S(2)}, u32[]{:S(2)}) collective-permute-start(bf16[32,768]{1,0:T(8,128)(2,1)S(1)} %get-tuple-element.20), channel_id=1, source_target_pairs={{0,4},{1,5},{2,6},{3,7},{4,0},{5,1},{6,2},{7,3},{8,12},{9,13},{10,... | collective-permute-start | bytes 147464 | tf_op jit(solution)/shard_map/ppermute | solution.py:77
  37.5 2.8 %collective-permute-done.5.came_ref = bf16[32,768]{1,0:T(8,128)(2,1)S(1)} collective-permute-done((bf16[32,768]{1,0:T(8,128)(2,1)S(1)}, bf16[32,768]{1,0:T(8,128)(2,1)S(1)}, u32[]{:S(2)}, u32[]{:S(2)}) %collective-permute-start.5) | collective-permute-done | bytes 49184 | tf_op jit(solution)/shard_map/ppermute | solution.py:77
  40.3 0.7 %shard_map.65 = f32[32,768]{1,0:T(8,128)} custom-call(f32[32,768]{1,0:T(8,128)S(1)} %get-tuple-element.19.kept_ref, bf16[32,768]{1,0:T(8,128)(2,1)S(1)} %collective-permute-done.5.came_ref), custom_call_target="tpu_custom_call" | custom-call | bytes 245760 | tf_op jit(solution)/shard_map/pallas_call | solution.py:88
  41.0 2.1 %shard_map.66.refs_5_ = f32[1024,768]{1,0:T(8,128)S(1)} custom-call(bf16[128,768]{1,0:T(8,128)(2,1)S(1)} %get-tuple-element.13.rows_ref.near_ref, bf16[128,768]{1,0:T(8,128)(2,1)S(1)} %collective-permute-done.2.rows_ref.far_ref, bf16[1024,128]{1,0:T(8,128)(2,1)S(1)} %get-tuple-element.21.near_slope_ref, ...), custom_call_target="tpu_custom_call" | custom-call | flops 1207959552 | bytes 6053888 | tf_op jit(solution)/shard_map/pallas_call | solution.py:88
  43.0 3.4 %shard_map.67 = bf16[1024,768]{1,0:T(8,128)(2,1)} custom-call(bf16[144,768]{1,0:T(8,128)(2,1)S(1)} %collective-permute-done.6.refs_0_, bf16[128,768]{1,0:T(8,128)(2,1)S(1)} %collective-permute-done.7.refs_1_, bf16[144,768]{1,0:T(8,128)(2,1)S(1)} %collective-permute-done.8.refs_2_, bf16[128,768]{1,0:T(8,128)(2,1)S(1)} %collective-permute-done.9.refs_3_, ...), custom_call_target="tpu_custom_call" | custom-call | flops 1610612736 | bytes 7127040 | tf_op jit(solution)/shard_map/pallas_call | solution.py:88
  (23 shorter events, 0.9 us)
Async XLA Ops:
  0.6 6.9 %collective-permute-start = (bf16[32,768]{1,0:T(8,128)(2,1)}, bf16[32,768]{1,0:T(8,128)(2,1)S(1)}, u32[]{:S(2)}, u32[]{:S(2)}) collective-permute-start(bf16[32,768]{1,0:T(8,128)(2,1)} %own_ref.1), channel_id=1, source_target_pairs={{0,4},{1,5},{2,6},{3,7},{4,0},{5,1},{6,2},{7,3},{8,12},{9,13},{10,... | collective-permute-start | bytes 147464 | tf_op jit(solution)/shard_map/ppermute | solution.py:77
  7.5 0.8 %copy-start.2 = (bf16[32,768]{1,0:T(8,128)(2,1)S(1)}, bf16[32,768]{1,0:T(8,128)(2,1)}, u32[]{:S(2)}) copy-start(bf16[32,768]{1,0:T(8,128)(2,1)} %own_ref.1) | copy-start | bytes 147460
  8.4 4.7 %collective-permute-start.1 = (bf16[64,768]{1,0:T(8,128)(2,1)S(1)}, bf16[64,768]{1,0:T(8,128)(2,1)S(1)}, u32[]{:S(2)}, u32[]{:S(2)}) collective-permute-start(bf16[64,768]{1,0:T(8,128)(2,1)S(1)} %shard_map.59.own_ref), channel_id=1, source_target_pairs={{0,2},{1,3},{2,0},{3,1},{4,6},{5,7},{6,4},{7,5},{8,10},{9,11},{10,... | collective-permute-start | bytes 294920 | tf_op jit(solution)/shard_map/ppermute | solution.py:77
  13.1 5.7 %collective-permute-start.2 = (bf16[128,768]{1,0:T(8,128)(2,1)S(1)}, bf16[128,768]{1,0:T(8,128)(2,1)S(1)}, u32[]{:S(2)}, u32[]{:S(2)}) collective-permute-start(bf16[128,768]{1,0:T(8,128)(2,1)S(1)} %get-tuple-element.13.rows_ref.near_ref), channel_id=1, source_target_pairs={{0,1},{1,0},{2,3},{3,2},{4,5},{5,4},{6,7},{7,6},{8,9},{9,8},{10,11... | collective-permute-start | bytes 589832 | tf_op jit(solution)/shard_map/ppermute | solution.py:77
  18.8 1.4 %copy-start = (bf16[1024,768]{1,0:T(8,128)(2,1)S(1)}, bf16[1024,768]{1,0:T(8,128)(2,1)}, u32[]{:S(2)}) copy-start(bf16[1024,768]{1,0:T(8,128)(2,1)} %refs_4_.1) | copy-start | bytes 4718596
  20.2 5.2 %copy-start.1 = (bf16[1024,768]{1,0:T(8,128)(2,1)S(1)}, bf16[1024,768]{1,0:T(8,128)(2,1)}, u32[]{:S(2)}) copy-start(bf16[1024,768]{1,0:T(8,128)(2,1)} %refs_4_.1) | copy-start | bytes 4718596
  21.6 19.4 %collective-permute-start.10 = (bf16[272,768]{1,0:T(8,128)(2,1)S(1)}, bf16[272,768]{1,0:T(8,128)(2,1)S(1)}, u32[]{:S(2)}, u32[]{:S(2)}) collective-permute-start(bf16[272,768]{1,0:T(8,128)(2,1)S(1)} %get-tuple-element.23), channel_id=1, source_target_pairs={{0,8},{8,0},{16,24},{24,16},{1,9},{9,1},{17,25},{25,17},{2,10},{10... | collective-permute-start | bytes 1253384 | tf_op jit(solution)/shard_map/ppermute | solution.py:77
  21.6 7.3 %collective-permute-start.3 = (bf16[128,768]{1,0:T(8,128)(2,1)S(1)}, bf16[128,768]{1,0:T(8,128)(2,1)S(1)}, u32[]{:S(2)}, u32[]{:S(2)}) collective-permute-start(bf16[128,768]{1,0:T(8,128)(2,1)S(1)} %get-tuple-element.16), channel_id=1, source_target_pairs={{0,1},{1,0},{2,3},{3,2},{4,5},{5,4},{6,7},{7,6},{8,9},{9,8},{10,11... | collective-permute-start | bytes 589832 | tf_op jit(solution)/shard_map/ppermute | solution.py:77
  23.4 8.3 %collective-permute-start.6 = (bf16[144,768]{1,0:T(8,128)(2,1)S(1)}, bf16[144,768]{1,0:T(8,128)(2,1)S(1)}, u32[]{:S(2)}, u32[]{:S(2)}) collective-permute-start(bf16[144,768]{1,0:T(8,128)(2,1)S(1)} %get-tuple-element.15.near_ref), channel_id=1, source_target_pairs={{0,16},{8,24},{16,0},{24,8},{1,17},{9,25},{17,1},{25,9},{2,18},{10... | collective-permute-start | bytes 663560 | tf_op jit(solution)/shard_map/ppermute | solution.py:77
  24.9 10.2 %collective-permute-start.7 = (bf16[128,768]{1,0:T(8,128)(2,1)S(1)}, bf16[128,768]{1,0:T(8,128)(2,1)S(1)}, u32[]{:S(2)}, u32[]{:S(2)}) collective-permute-start(bf16[128,768]{1,0:T(8,128)(2,1)S(1)} %collective-permute-done.2.rows_ref.far_ref), channel_id=1, source_target_pairs={{0,16},{8,24},{16,0},{24,8},{1,17},{9,25},{17,1},{25,9},{2,18},{10... | collective-permute-start | bytes 589832 | tf_op jit(solution)/shard_map/ppermute | solution.py:77
  29.0 6.2 %collective-permute-start.4 = (bf16[64,768]{1,0:T(8,128)(2,1)S(1)}, bf16[64,768]{1,0:T(8,128)(2,1)S(1)}, u32[]{:S(2)}, u32[]{:S(2)}) collective-permute-start(bf16[64,768]{1,0:T(8,128)(2,1)S(1)} %get-tuple-element.18), channel_id=1, source_target_pairs={{0,2},{1,3},{2,0},{3,1},{4,6},{5,7},{6,4},{7,5},{8,10},{9,11},{10,... | collective-permute-start | bytes 294920 | tf_op jit(solution)/shard_map/ppermute | solution.py:77
  31.7 11.3 %collective-permute-start.8 = (bf16[144,768]{1,0:T(8,128)(2,1)S(1)}, bf16[144,768]{1,0:T(8,128)(2,1)S(1)}, u32[]{:S(2)}, u32[]{:S(2)}) collective-permute-start(bf16[144,768]{1,0:T(8,128)(2,1)S(1)} %collective-permute-done.6.refs_0_), channel_id=1, source_target_pairs={{0,8},{8,0},{16,24},{24,16},{1,9},{9,1},{17,25},{25,17},{2,10},{10... | collective-permute-start | bytes 663560 | tf_op jit(solution)/shard_map/ppermute | solution.py:77
  35.1 7.9 %collective-permute-start.9 = (bf16[128,768]{1,0:T(8,128)(2,1)S(1)}, bf16[128,768]{1,0:T(8,128)(2,1)S(1)}, u32[]{:S(2)}, u32[]{:S(2)}) collective-permute-start(bf16[128,768]{1,0:T(8,128)(2,1)S(1)} %collective-permute-done.7.refs_1_), channel_id=1, source_target_pairs={{0,8},{8,0},{16,24},{24,16},{1,9},{9,1},{17,25},{25,17},{2,10},{10... | collective-permute-start | bytes 589832 | tf_op jit(solution)/shard_map/ppermute | solution.py:77
  35.2 5.1 %collective-permute-start.5 = (bf16[32,768]{1,0:T(8,128)(2,1)S(1)}, bf16[32,768]{1,0:T(8,128)(2,1)S(1)}, u32[]{:S(2)}, u32[]{:S(2)}) collective-permute-start(bf16[32,768]{1,0:T(8,128)(2,1)S(1)} %get-tuple-element.20), channel_id=1, source_target_pairs={{0,4},{1,5},{2,6},{3,7},{4,0},{5,1},{6,2},{7,3},{8,12},{9,13},{10,... | collective-permute-start | bytes 147464 | tf_op jit(solution)/shard_map/ppermute | solution.py:77

commit v5 on v4

--- a/solution.py
+++ b/solution.py
@@ -77,22 +77,20 @@
     return lax.ppermute(value, axis, [(i, i ^ bit) for i in range(count)])
 
 
-def local_call(body, outs, args, flops=0):
-    scalars = [arg for arg in args if arg.dtype == jnp.int32]
-    size = sum(a.size * a.dtype.itemsize for a in list(args) + list(outs))
+def local_call(body, outs, args, flops=0, follows=()):
     specs = [
         pl.BlockSpec(memory_space=pltpu.SMEM if arg.dtype == jnp.int32 else pltpu.VMEM)
         for arg in args
     ]
-    del scalars
+    given, later = len(args), len(args) + len(follows)
     return pl.pallas_call(
-        body,
+        lambda *refs: body(*refs[:given], *refs[later:]),
         out_shape=outs,
-        in_specs=specs,
+        in_specs=specs + [pl.BlockSpec(memory_space=pl.ANY)] * len(follows),
         out_specs=[pl.BlockSpec(memory_space=pltpu.VMEM)] * len(outs),
-        cost_estimate=pl.CostEstimate(flops=flops, bytes_accessed=size, transcendentals=0),
+        cost_estimate=pl.CostEstimate(flops=flops, bytes_accessed=0, transcendentals=0),
         compiler_params=pltpu.CompilerParams(vmem_limit_bytes=VMEM_LIMIT),
-    )(*args)
+    )(*args, *follows)
 
 
 def like(rows, width, dtype):
@@ -106,11 +104,13 @@
     out_ref[pl.ds(pl.multiple_of((1 - side) * rows, rows), rows), :] = came_ref[...]
 
 
-def join_note_body(side_ref, own_ref, came_ref, note_ref, out_ref, noted_ref):
-    rows = own_ref.shape[0]
+def hold_body(rows_ref, held_ref):
+    held_ref[...] = rows_ref[...]
+
+
+def join_mark_body(side_ref, own_ref, came_ref, out_ref, mark_ref):
     join_body(side_ref, own_ref, came_ref, out_ref)
-    noted_ref[: 2 * rows, :] = out_ref[...]
-    noted_ref[2 * rows :, :] = note_ref[...]
+    mark_ref[...] = jnp.zeros_like(mark_ref)
 
 
 def slope_of(rows, weights_ref, chosen, place):
@@ -145,15 +145,17 @@
     dq_ref[...] = dq.astype(dq_ref.dtype)
 
 
-def near_body(rows_ref, weights_ref, note_ref, dq_ref, slope_ref):
+def near_body(rows_ref, weights_ref, note_ref, dq_ref, slope_ref, noted_ref, held_ref):
+    held_ref[...] = weights_ref[...]
     grad_body(0, rows_ref, weights_ref, note_ref, dq_ref, slope_ref)
-
-
-def far_body(near_ref, rows_ref, weights_ref, note_ref, dq_ref, slope_ref, all_ref):
+    half = rows_ref.shape[0]
+    noted_ref[:half, :] = rows_ref[...]
+    noted_ref[half:, :] = note_ref[...]
+
+
+def far_body(rows_ref, weights_ref, note_ref, dq_ref, slope_ref, far_out):
     grad_body(1, rows_ref, weights_ref, note_ref, dq_ref, slope_ref)
-    noted = near_ref.shape[0]
-    all_ref[:noted, :] = near_ref[...]
-    all_ref[noted:, :] = rows_ref[...]
+    far_out[...] = rows_ref[...]
 
 
 def fold_body(side_ref, kept_ref, came_ref, keep_ref, send_ref):
@@ -179,33 +181,52 @@
     return rows, slope_of(rows, weights_ref, chosen, place)
 
 
-def early_body(near_ref, far_ref, near_slope_ref, far_slope_ref, set_ref, weights_ref, acc_ref):
-    half = near_ref.shape[0]
-    note = set_ref[half : half + NOTE, :].astype(jnp.float32)
-    rows, slope = slopes_of_set(set_ref[:half, :], set_ref[half + NOTE :, :], note, weights_ref)
-    rows = jnp.concatenate([near_ref[...], far_ref[...], rows], axis=0)
-    slope = jnp.concatenate([near_slope_ref[...], far_slope_ref[...], slope], axis=1)
+def own_body(near_ref, far_ref, near_slope_ref, far_slope_ref, noted_ref, acc_ref, whole_ref):
+    noted = noted_ref.shape[0]
+    whole_ref[:noted, :] = noted_ref[...]
+    whole_ref[noted:, :] = far_ref[...]
+    rows = jnp.concatenate([near_ref[...], far_ref[...]], axis=0)
+    slope = jnp.concatenate([near_slope_ref[...], far_slope_ref[...]], axis=1)
     acc_ref[...] = jnp.dot(slope, rows, preferred_element_type=jnp.float32)
 
 
-def late_body(groups, *refs):
-    *set_refs, weights_ref, acc_ref, out_ref = refs
+def split_set(set_ref):
+    half = (set_ref.shape[0] - NOTE) // 2
+    return set_ref[:half, :], set_ref[half + NOTE :, :], set_ref[half : half + NOTE, :]
+
+
+def pack_body(near_ref, far_ref, out_ref):
+    noted = near_ref.shape[0]
+    out_ref[:noted, :] = near_ref[...]
+    out_ref[noted:, :] = far_ref[...]
+
+
+def add_sets(acc_ref, weights_ref, set_refs):
     rows, slopes = [], []
-    for near_ref, far_ref in zip(set_refs[::2], set_refs[1::2]):
-        half = far_ref.shape[0]
-        note = near_ref[half:, :].astype(jnp.float32)
-        part, slope = slopes_of_set(near_ref[:half, :], far_ref[...], note, weights_ref)
+    for set_ref in set_refs:
+        near, far, note = split_set(set_ref)
+        part, slope = slopes_of_set(near, far, note.astype(jnp.float32), weights_ref)
         rows.append(part)
         slopes.append(slope)
-    total = acc_ref[...] + jnp.dot(
+    return acc_ref[...] + jnp.dot(
         jnp.concatenate(slopes, axis=1),
         jnp.concatenate(rows, axis=0),
         preferred_element_type=jnp.float32,
     )
+
+
+def mate_body(set_ref, weights_ref, acc_ref, out_ref):
+    out_ref[...] = add_sets(acc_ref, weights_ref, [set_ref])
+
+
+def late_body(groups, one_ref, two_ref, weights_ref, acc_ref, out_ref, mark_ref):
+    mark_ref[...] = jnp.zeros_like(mark_ref)
+    total = add_sets(acc_ref, weights_ref, [one_ref, two_ref])
     out_ref[...] = (total / groups).astype(out_ref.dtype)
 
 
-def make_note(sibling_blocks, positive_slot, blocks_dev, homes, width):
+def make_note(sibling_blocks, positive_slot, mark, blocks_dev, homes, width):
+    sibling_blocks, positive_slot = sibling_blocks + mark, positive_slot + mark
     me = lax.axis_index("lab")
     local = sibling_blocks.T - me * blocks_dev
     inside = (local >= 0) & (local < blocks_dev)
@@ -235,59 +256,87 @@
     def side(bit):
         return jnp.reshape((me // bit) % 2, (1,)).astype(jnp.int32)
 
-    note = make_note(sibling_blocks, positive_slot, lab_dev // BLOCK, homes, width)
-    near, bit = queries, homes // 2
-    while bit > 2:
-        near = local_call(
-            join_body, [like(2 * near.shape[0], width, bf16)], [side(bit), near, swap(near, "lab", bit)]
-        )[0]
+    far_bit = groups // 2
+    bit = homes // 2
+    came = swap(queries, "lab", bit)
+    near = local_call(hold_body, [like(q_home, width, bf16)], [queries])[0]
+    while True:
+        near, mark = local_call(
+            join_mark_body,
+            [like(2 * near.shape[0], width, bf16), like(1, BLOCK, jnp.int32)],
+            [side(bit), near, came],
+        )
         bit //= 2
-    near, noted = local_call(
-        join_note_body,
-        [like(half, width, bf16), like(half + NOTE, width, bf16)],
-        [side(2), near, swap(near, "lab", 2), note],
-    )
+        if bit == 1:
+            break
+        note = make_note(
+            sibling_blocks, positive_slot, mark[0, 0], lab_dev // BLOCK, homes, width
+        )
+        came = swap(near, "lab", bit)
     far = swap(near, "lab", 1)
     work = 4 * half * lab_dev * width
-    near_dq, near_slope = local_call(
+    near_dq, near_slope, noted, weights = local_call(
         near_body,
-        [like(half, width, f32), like(lab_dev, half, bf16)],
+        [
+            like(half, width, f32),
+            like(lab_dev, half, bf16),
+            like(half + NOTE, width, bf16),
+            like(lab_dev, width, bf16),
+        ],
         [near, label_weights, note],
         work,
     )
-    far_dq, far_slope, whole = local_call(
+    cross_near = swap(noted, "pb", far_bit)
+    far_dq, far_slope, far_copy = local_call(
         far_body,
-        [like(half, width, bf16), like(lab_dev, half, bf16), like(qcount + NOTE, width, bf16)],
-        [noted, far, label_weights, note],
+        [like(half, width, bf16), like(lab_dev, half, bf16), like(half, width, bf16)],
+        [far, weights, note],
         work,
-    )
-    kept, came, bit = near_dq, swap(far_dq, "lab", 1), 2
+        [near_dq],
+    )
+    came = swap(far_dq, "lab", 1)
+    acc, whole = local_call(
+        own_body,
+        [like(lab_dev, width, f32), like(qcount + NOTE, width, bf16)],
+        [near, far, near_slope, far_slope, noted],
+        work,
+        [cross_near],
+    )
+    cross_far = swap(far_copy, "pb", far_bit)
+    mate = swap(whole, "pb", 1)
+    rows = half // 2
+    kept, send = local_call(
+        fold_body, [like(rows, width, f32), like(rows, width, bf16)], [side(2), near_dq, came], 0, [acc]
+    )
+    came = swap(send, "lab", 2)
+    cross = local_call(
+        pack_body, [like(qcount + NOTE, width, bf16)], [cross_near, cross_far], 0, [kept]
+    )[0]
+    acc = local_call(
+        mate_body, [like(lab_dev, width, f32)], [mate, weights, acc], 40 * work, [cross]
+    )[0]
+    cross_mate = swap(cross, "pb", 1)
+    bit = 4
     while bit < homes:
-        rows = kept.shape[0] // 2
+        rows //= 2
         kept, send = local_call(
-            fold_body, [like(rows, width, f32), like(rows, width, bf16)], [side(bit), kept, came]
+            fold_body,
+            [like(rows, width, f32), like(rows, width, bf16)],
+            [side(bit), kept, came],
+            0,
+            [acc],
         )
         came = swap(send, "lab", bit)
         bit *= 2
-    query_grad = local_call(last_body, [like(q_home, width, f32)], [kept, came])[0]
-    sets = [(swap(noted, "pb", groups // 2), swap(far, "pb", groups // 2))]
-    bit = groups // 4
-    mate = swap(whole, "pb", 1)
-    while bit:
-        sets = sets + [(swap(a, "pb", bit), swap(b, "pb", bit)) for a, b in sets]
-        bit //= 2
-    acc = local_call(
-        early_body,
-        [like(lab_dev, width, f32)],
-        [near, far, near_slope, far_slope, mate, label_weights],
-        3 * work,
-    )[0]
-    flat = [part for pair in sets for part in pair]
-    weight_grad = local_call(
+    weight_grad, mark = local_call(
         lambda *refs: late_body(groups, *refs),
-        [like(lab_dev, width, bf16)],
-        flat + [label_weights, acc],
+        [like(lab_dev, width, bf16), like(1, BLOCK, jnp.int32)],
+        [cross, cross_mate, weights, acc],
         4 * work,
+        [kept],
+    )
+    query_grad = local_call(
+        last_body, [like(q_home, width, f32)], [kept, came], 0, [mark]
     )[0]
     return (query_grad, weight_grad)
 

time: 46.7 us -> 42.7 us (0.914)
  waiting for transfers between devices: 17.3 us -> 12.5 us
  Pallas kernels: 8.86 us -> 9.91 us
    ppermute x11 -> x10, waiting for transfers between devices: 17.3 us -> 12.5 us  [swap(): return lax.ppermute(value, axis, [(i, i ^ bit) for i in range(count)])]
    pallas_call x9 -> x12, Pallas kernels: 8.86 us -> 9.91 us  [local_call(): pl.pallas_call(lambda *refs: body(*refs[:given], *refs[later:]), out_shap...]
    ppermute x11 -> x10, starting transfers between devices: 15 us -> 14.6 us  [swap(): return lax.ppermute(value, axis, [(i, i ^ bit) for i in range(count)])]
    unnamed x6 -> x4, local copies, waits for them, and re-layouts: 2.21 us -> 2.24 us
  transfers between devices with their start and end apart: 11 -> 10, of which waited for: 7 -> 5; matrix products, arithmetic and copies ran while one was open for 5% -> 6% of each run, Pallas kernels for 9% -> 19%
where the time goes in v5:
time: 42.7 us; the launch traced here: 42.4 us
  starting transfers between devices  14.6 us (34%)
  waiting for transfers between devices  12.5 us (29%)
  Pallas kernels  9.91 us (23%)
  local copies, waits for them, and re-layouts  2.51 us (6%)
  other arithmetic  2.22 us (5%)
  between operations  0.72 us (2%)
    ppermute x10, starting transfers between devices, swap(): return lax.ppermute(value, axis, [(i, i ^ bit) for i in range(count)])  14.6 us
    ppermute x10, waiting for transfers between devices, swap(): return lax.ppermute(value, axis, [(i, i ^ bit) for i in range(count)])  12.5 us
    pallas_call x12, Pallas kernels, local_call(): pl.pallas_call(lambda *refs: body(*refs[:given], *refs[later:]), out_shap...  9.91 us
    unnamed x4, local copies, waits for them, and re-layouts  2.24 us
  transfers between devices with their start and end apart: 10, of which 5 were waited for; matrix products, arithmetic and copies ran while one was open for 6% of the time, Pallas kernels for 19%

profile of v5, /device:TPU:0, one launch (start us, length us, event | category | flops | bytes accessed | tf_op | source)
XLA Modules:
  0.0 42.4 jit_solution(14157332413859138371)
XLA Ops:
  0.6 4.1 %collective-permute-start = (bf16[32,768]{1,0:T(8,128)(2,1)}, bf16[32,768]{1,0:T(8,128)(2,1)S(1)}, u32[]{:S(2)}, u32[]{:S(2)}) collective-permute-start(bf16[32,768]{1,0:T(8,128)(2,1)} %refs_0_.1), channel_id=1, source_target_pairs={{0,4},{1,5},{2,6},{3,7},{4,0},{5,1},{6,2},{7,3},{8,12},{9,13},{10,... | collective-permute-start | bytes 147464 | tf_op jit(solution)/shard_map/ppermute | solution.py:77
  4.7 0.8 %copy-done.1 = bf16[32,768]{1,0:T(8,128)(2,1)S(1)} copy-done((bf16[32,768]{1,0:T(8,128)(2,1)S(1)}, bf16[32,768]{1,0:T(8,128)(2,1)}, u32[]{:S(2)}) %copy-start.1) | copy-done | bytes 49176
  5.6 2.0 %collective-permute-done.refs_2_ = bf16[32,768]{1,0:T(8,128)(2,1)S(1)} collective-permute-done((bf16[32,768]{1,0:T(8,128)(2,1)}, bf16[32,768]{1,0:T(8,128)(2,1)S(1)}, u32[]{:S(2)}, u32[]{:S(2)}) %collective-permute-start) | collective-permute-done | bytes 49184 | tf_op jit(solution)/shard_map/ppermute | solution.py:77
  7.6 1.4 %collective-permute-start.1 = (bf16[64,768]{1,0:T(8,128)(2,1)S(1)}, bf16[64,768]{1,0:T(8,128)(2,1)S(1)}, u32[]{:S(2)}, u32[]{:S(2)}) collective-permute-start(bf16[64,768]{1,0:T(8,128)(2,1)S(1)} %get-tuple-element.20.refs_1_), channel_id=1, source_target_pairs={{0,2},{1,3},{2,0},{3,1},{4,6},{5,7},{6,4},{7,5},{8,10},{9,11},{10,... | collective-permute-start | bytes 294920 | tf_op jit(solution)/shard_map/ppermute | solution.py:77
  9.0 0.7 %and_select_fusion.1 = s32[256]{0:T(256)S(1)} fusion(s32[256]{0:T(256)} %param.7, s32[]{:T(128)S(1)} %bitcast.22), kind=kLoop, calls=%fused_computation.12 | loop fusion | flops 4096 | bytes 2052 | tf_op jit(solution)/shard_map/jit(floor_divide)/jit(_where)/select_n | solution.py:235
  9.7 0.7 %fusion = (s32[256]{0:T(256)S(1)}, s32[256]{0:T(256)S(1)}) fusion(s32[256,8]{0,1:T(8,128)} %param.6, s32[]{:T(128)S(6)} %mul.3, s32[]{:T(128)S(1)} %bitcast.23, s32[256]{0:T(256)S(1)} %and_select_fusion.1), kind=kLoop, calls=%fused_computation.4 | loop fusion | flops 19968 | bytes 11272 | tf_op jit(solution)/shard_map/reduce_max | solution.py:233
  10.5 0.7 %fusion.4 = (bf16[256]{0:T(256)(128)(2,1)S(1)}, bf16[256]{0:T(256)(128)(2,1)S(1)}) fusion(s32[256]{0:T(256)S(1)} %get-tuple-element.38, s32[256]{0:T(256)} %param.7, s32[]{:T(128)S(1)} %bitcast.24, s32[256]{0:T(256)S(1)} %get-tuple-element.39), kind=kLoop, calls=%fused_computation.20 | loop fusion | flops 4096 | bytes 4100 | tf_op jit(solution)/shard_map/convert.3
  11.5 0.7 %collective-permute-done.1.refs_2_ = bf16[64,768]{1,0:T(8,128)(2,1)S(1)} collective-permute-done((bf16[64,768]{1,0:T(8,128)(2,1)S(1)}, bf16[64,768]{1,0:T(8,128)(2,1)S(1)}, u32[]{:S(2)}, u32[]{:S(2)}) %collective-permute-start.1) | collective-permute-done | bytes 98336 | tf_op jit(solution)/shard_map/ppermute | solution.py:77
  12.2 0.5 %shard_map.61 = (bf16[128,768]{1,0:T(8,128)(2,1)S(1)}, s32[1,128]{1,0:T(1,128)}) custom-call(s32[1]{0:T(128)} %bitcast.1.refs_0_, bf16[64,768]{1,0:T(8,128)(2,1)S(1)} %get-tuple-element.20.refs_1_, bf16[64,768]{1,0:T(8,128)(2,1)S(1)} %collective-permute-done.1.refs_2_), custom_call_target="tpu_custom_call" | custom-call | tf_op jit(solution)/shard_map/pallas_call | solution.py:86
  12.8 1.7 %collective-permute-start.2 = (bf16[128,768]{1,0:T(8,128)(2,1)S(1)}, bf16[128,768]{1,0:T(8,128)(2,1)S(1)}, u32[]{:S(2)}, u32[]{:S(2)}) collective-permute-start(bf16[128,768]{1,0:T(8,128)(2,1)S(1)} %get-tuple-element.21.refs_0_), channel_id=1, source_target_pairs={{0,1},{1,0},{2,3},{3,2},{4,5},{5,4},{6,7},{7,6},{8,9},{9,8},{10,11... | collective-permute-start | bytes 589832 | tf_op jit(solution)/shard_map/ppermute | solution.py:77
  14.5 1.4 %copy-done = bf16[1024,768]{1,0:T(8,128)(2,1)S(1)} copy-done((bf16[1024,768]{1,0:T(8,128)(2,1)S(1)}, bf16[1024,768]{1,0:T(8,128)(2,1)}, u32[]{:S(2)}) %copy-start) | copy-done | bytes 1572888
  15.9 1.4 %shard_map.62 = (f32[128,768]{1,0:T(8,128)S(1)}, bf16[1024,128]{1,0:T(8,128)(2,1)S(1)}, bf16[144,768]{1,0:T(8,128)(2,1)S(1)}, bf16[1024,768]{1,0:T(8,128)(2,1)S(1)}) custom-call(bf16[128,768]{1,0:T(8,128)(2,1)S(1)} %get-tuple-element.21.refs_0_, bf16[1024,768]{1,0:T(8,128)(2,1)S(1)} %copy-done, bf16[16,768]{1,0:T(8,128)(2,1)S(1)} %pad.4.refs_2_), custom_call_target="tpu_custom_call" | custom-call | flops 402653184 | tf_op jit(solution)/shard_map/pallas_call | solution.py:86
  17.3 1.6 %collective-permute-start.4 = (bf16[144,768]{1,0:T(8,128)(2,1)S(1)}, bf16[144,768]{1,0:T(8,128)(2,1)S(1)}, u32[]{:S(2)}, u32[]{:S(2)}) collective-permute-start(bf16[144,768]{1,0:T(8,128)(2,1)S(1)} %get-tuple-element.28.refs_4_), channel_id=1, source_target_pairs={{0,16},{8,24},{16,0},{24,8},{1,17},{9,25},{17,1},{25,9},{2,18},{10... | collective-permute-start | bytes 663560 | tf_op jit(solution)/shard_map/ppermute | solution.py:77
  18.9 1.3 %shard_map.63 = (bf16[128,768]{1,0:T(8,128)(2,1)S(1)}, bf16[1024,128]{1,0:T(8,128)(2,1)S(1)}, bf16[128,768]{1,0:T(8,128)(2,1)S(1)}) custom-call(bf16[128,768]{1,0:T(8,128)(2,1)S(1)} %collective-permute-done.2.refs_0_.refs_1_, bf16[1024,768]{1,0:T(8,128)(2,1)S(1)} %get-tuple-element.24.refs_1_.refs_2_, bf16[16,768]{1,0:T(8,128)(2,1)S(1)} %pad.4.refs_2_, ...), custom_call_target="tpu_custom_call" | custom-call | flops 402653184 | tf_op jit(solution)/shard_map/pallas_call | solution.py:86
  20.2 3.1 %collective-permute-done.4.refs_5_.refs_0_ = bf16[144,768]{1,0:T(8,128)(2,1)S(1)} collective-permute-done((bf16[144,768]{1,0:T(8,128)(2,1)S(1)}, bf16[144,768]{1,0:T(8,128)(2,1)S(1)}, u32[]{:S(2)}, u32[]{:S(2)}) %collective-permute-start.4) | collective-permute-done | bytes 221216 | tf_op jit(solution)/shard_map/ppermute | solution.py:77
  23.3 0.6 %shard_map.64 = (f32[1024,768]{1,0:T(8,128)S(1)}, bf16[272,768]{1,0:T(8,128)(2,1)S(1)}) custom-call(bf16[128,768]{1,0:T(8,128)(2,1)S(1)} %get-tuple-element.21.refs_0_, bf16[128,768]{1,0:T(8,128)(2,1)S(1)} %collective-permute-done.2.refs_0_.refs_1_, bf16[1024,128]{1,0:T(8,128)(2,1)S(1)} %get-tuple-element.26.refs_2_, ...), custom_call_target="tpu_custom_call" | custom-call | flops 402653184 | tf_op jit(solution)/shard_map/pallas_call | solution.py:86
  24.4 1.7 %collective-permute-start.7 = (bf16[128,768]{1,0:T(8,128)(2,1)S(1)}, bf16[128,768]{1,0:T(8,128)(2,1)S(1)}, u32[]{:S(2)}, u32[]{:S(2)}) collective-permute-start(bf16[128,768]{1,0:T(8,128)(2,1)S(1)} %get-tuple-element.33), channel_id=1, source_target_pairs={{0,16},{8,24},{16,0},{24,8},{1,17},{9,25},{17,1},{25,9},{2,18},{10... | collective-permute-start | bytes 589832 | tf_op jit(solution)/shard_map/ppermute | solution.py:77
  26.1 5.3 %collective-permute-done.3.refs_2_ = bf16[128,768]{1,0:T(8,128)(2,1)S(1)} collective-permute-done((bf16[128,768]{1,0:T(8,128)(2,1)S(1)}, bf16[128,768]{1,0:T(8,128)(2,1)S(1)}, u32[]{:S(2)}, u32[]{:S(2)}) %collective-permute-start.3) | collective-permute-done | bytes 196640 | tf_op jit(solution)/shard_map/ppermute | solution.py:77
  31.4 1.2 %collective-permute-start.5 = (bf16[64,768]{1,0:T(8,128)(2,1)S(1)}, bf16[64,768]{1,0:T(8,128)(2,1)S(1)}, u32[]{:S(2)}, u32[]{:S(2)}) collective-permute-start(bf16[64,768]{1,0:T(8,128)(2,1)S(1)} %get-tuple-element.31), channel_id=1, source_target_pairs={{0,2},{1,3},{2,0},{3,1},{4,6},{5,7},{6,4},{7,5},{8,10},{9,11},{10,... | collective-permute-start | bytes 294920 | tf_op jit(solution)/shard_map/ppermute | solution.py:77
  32.7 1.9 %shard_map.67.refs_3_ = f32[1024,768]{1,0:T(8,128)S(1)} custom-call(bf16[272,768]{1,0:T(8,128)(2,1)S(1)} %collective-permute-done.6.refs_0_, bf16[1024,768]{1,0:T(8,128)(2,1)S(1)} %get-tuple-element.24.refs_1_.refs_2_, f32[1024,768]{1,0:T(8,128)S(1)} %get-tuple-element.29.refs_3_.refs_2_, bf16[272,768]{1,0:T(8,128)(2,1)S(1)} %shard_map.66.refs_3_.refs_0_), custom_call_target="tpu_custom_call" | custom-call | flops 16106127360 | tf_op jit(solution)/shard_map/pallas_call | solution.py:86
  34.6 1.4 %collective-permute-done.5.refs_2_ = bf16[64,768]{1,0:T(8,128)(2,1)S(1)} collective-permute-done((bf16[64,768]{1,0:T(8,128)(2,1)S(1)}, bf16[64,768]{1,0:T(8,128)(2,1)S(1)}, u32[]{:S(2)}, u32[]{:S(2)}) %collective-permute-start.5) | collective-permute-done | bytes 98336 | tf_op jit(solution)/shard_map/ppermute | solution.py:77
  36.1 2.3 %collective-permute-start.8 = (bf16[32,768]{1,0:T(8,128)(2,1)S(1)}, bf16[32,768]{1,0:T(8,128)(2,1)S(1)}, u32[]{:S(2)}, u32[]{:S(2)}) collective-permute-start(bf16[32,768]{1,0:T(8,128)(2,1)S(1)} %get-tuple-element.35), channel_id=1, source_target_pairs={{0,4},{1,5},{2,6},{3,7},{4,0},{5,1},{6,2},{7,3},{8,12},{9,13},{10,... | collective-permute-start | bytes 147464 | tf_op jit(solution)/shard_map/ppermute | solution.py:77
  38.4 3.4 %shard_map.69 = (bf16[1024,768]{1,0:T(8,128)(2,1)}, s32[1,128]{1,0:T(1,128)S(1)}) custom-call(bf16[272,768]{1,0:T(8,128)(2,1)S(1)} %shard_map.66.refs_3_.refs_0_, bf16[272,768]{1,0:T(8,128)(2,1)S(1)} %collective-permute-done.9.refs_1_, bf16[1024,768]{1,0:T(8,128)(2,1)S(1)} %get-tuple-element.24.refs_1_.refs_2_, f32[1024,768]{1,0:T(8,128)S(1)} %shard_map.67.refs_3_, ...), custom_call_target="tpu_custom_call" | custom-call | flops 1610612736 | tf_op jit(solution)/shard_map/pallas_call | solution.py:86
  41.7 0.7 %shard_map.70 = f32[32,768]{1,0:T(8,128)} custom-call(f32[32,768]{1,0:T(8,128)S(1)} %get-tuple-element.34.refs_4_.refs_0_, bf16[32,768]{1,0:T(8,128)(2,1)S(1)} %collective-permute-done.8.refs_1_, s32[1,128]{1,0:T(1,128)S(1)} %get-tuple-element.36.refs_2_), custom_call_target="tpu_custom_call" | custom-call | tf_op jit(solution)/shard_map/pallas_call | solution.py:86
  (22 shorter events, 0.9 us)
Async XLA Ops:
  0.6 6.9 %collective-permute-start = (bf16[32,768]{1,0:T(8,128)(2,1)}, bf16[32,768]{1,0:T(8,128)(2,1)S(1)}, u32[]{:S(2)}, u32[]{:S(2)}) collective-permute-start(bf16[32,768]{1,0:T(8,128)(2,1)} %refs_0_.1), channel_id=1, source_target_pairs={{0,4},{1,5},{2,6},{3,7},{4,0},{5,1},{6,2},{7,3},{8,12},{9,13},{10,... | collective-permute-start | bytes 147464 | tf_op jit(solution)/shard_map/ppermute | solution.py:77
  4.7 0.8 %copy-start.1 = (bf16[32,768]{1,0:T(8,128)(2,1)S(1)}, bf16[32,768]{1,0:T(8,128)(2,1)}, u32[]{:S(2)}) copy-start(bf16[32,768]{1,0:T(8,128)(2,1)} %refs_0_.1) | copy-start | bytes 147460
  7.6 4.7 %collective-permute-start.1 = (bf16[64,768]{1,0:T(8,128)(2,1)S(1)}, bf16[64,768]{1,0:T(8,128)(2,1)S(1)}, u32[]{:S(2)}, u32[]{:S(2)}) collective-permute-start(bf16[64,768]{1,0:T(8,128)(2,1)S(1)} %get-tuple-element.20.refs_1_), channel_id=1, source_target_pairs={{0,2},{1,3},{2,0},{3,1},{4,6},{5,7},{6,4},{7,5},{8,10},{9,11},{10,... | collective-permute-start | bytes 294920 | tf_op jit(solution)/shard_map/ppermute | solution.py:77
  12.8 6.1 %collective-permute-start.2 = (bf16[128,768]{1,0:T(8,128)(2,1)S(1)}, bf16[128,768]{1,0:T(8,128)(2,1)S(1)}, u32[]{:S(2)}, u32[]{:S(2)}) collective-permute-start(bf16[128,768]{1,0:T(8,128)(2,1)S(1)} %get-tuple-element.21.refs_0_), channel_id=1, source_target_pairs={{0,1},{1,0},{2,3},{3,2},{4,5},{5,4},{6,7},{7,6},{8,9},{9,8},{10,11... | collective-permute-start | bytes 589832 | tf_op jit(solution)/shard_map/ppermute | solution.py:77
  14.5 1.4 %copy-start = (bf16[1024,768]{1,0:T(8,128)(2,1)S(1)}, bf16[1024,768]{1,0:T(8,128)(2,1)}, u32[]{:S(2)}) copy-start(bf16[1024,768]{1,0:T(8,128)(2,1)} %refs_1_.1) | copy-start | bytes 4718596
  17.3 6.0 %collective-permute-start.4 = (bf16[144,768]{1,0:T(8,128)(2,1)S(1)}, bf16[144,768]{1,0:T(8,128)(2,1)S(1)}, u32[]{:S(2)}, u32[]{:S(2)}) collective-permute-start(bf16[144,768]{1,0:T(8,128)(2,1)S(1)} %get-tuple-element.28.refs_4_), channel_id=1, source_target_pairs={{0,16},{8,24},{16,0},{24,8},{1,17},{9,25},{17,1},{25,9},{2,18},{10... | collective-permute-start | bytes 663560 | tf_op jit(solution)/shard_map/ppermute | solution.py:77
  23.9 8.8 %collective-permute-start.6 = (bf16[272,768]{1,0:T(8,128)(2,1)S(1)}, bf16[272,768]{1,0:T(8,128)(2,1)S(1)}, u32[]{:S(2)}, u32[]{:S(2)}) collective-permute-start(bf16[272,768]{1,0:T(8,128)(2,1)S(1)} %get-tuple-element.32), channel_id=1, source_target_pairs={{0,8},{8,0},{16,24},{24,16},{1,9},{9,1},{17,25},{25,17},{2,10},{10... | collective-permute-start | bytes 1253384 | tf_op jit(solution)/shard_map/ppermute | solution.py:77
  24.0 7.3 %collective-permute-start.3 = (bf16[128,768]{1,0:T(8,128)(2,1)S(1)}, bf16[128,768]{1,0:T(8,128)(2,1)S(1)}, u32[]{:S(2)}, u32[]{:S(2)}) collective-permute-start(bf16[128,768]{1,0:T(8,128)(2,1)S(1)} %get-tuple-element.25), channel_id=1, source_target_pairs={{0,1},{1,0},{2,3},{3,2},{4,5},{5,4},{6,7},{7,6},{8,9},{9,8},{10,11... | collective-permute-start | bytes 589832 | tf_op jit(solution)/shard_map/ppermute | solution.py:77
  24.4 8.2 %collective-permute-start.7 = (bf16[128,768]{1,0:T(8,128)(2,1)S(1)}, bf16[128,768]{1,0:T(8,128)(2,1)S(1)}, u32[]{:S(2)}, u32[]{:S(2)}) collective-permute-start(bf16[128,768]{1,0:T(8,128)(2,1)S(1)} %get-tuple-element.33), channel_id=1, source_target_pairs={{0,16},{8,24},{16,0},{24,8},{1,17},{9,25},{17,1},{25,9},{2,18},{10... | collective-permute-start | bytes 589832 | tf_op jit(solution)/shard_map/ppermute | solution.py:77
  31.4 4.7 %collective-permute-start.5 = (bf16[64,768]{1,0:T(8,128)(2,1)S(1)}, bf16[64,768]{1,0:T(8,128)(2,1)S(1)}, u32[]{:S(2)}, u32[]{:S(2)}) collective-permute-start(bf16[64,768]{1,0:T(8,128)(2,1)S(1)} %get-tuple-element.31), channel_id=1, source_target_pairs={{0,2},{1,3},{2,0},{3,1},{4,6},{5,7},{6,4},{7,5},{8,10},{9,11},{10,... | collective-permute-start | bytes 294920 | tf_op jit(solution)/shard_map/ppermute | solution.py:77
  32.6 5.7 %collective-permute-start.9 = (bf16[272,768]{1,0:T(8,128)(2,1)S(1)}, bf16[272,768]{1,0:T(8,128)(2,1)S(1)}, u32[]{:S(2)}, u32[]{:S(2)}) collective-permute-start(bf16[272,768]{1,0:T(8,128)(2,1)S(1)} %shard_map.66.refs_3_.refs_0_), channel_id=1, source_target_pairs={{0,8},{8,0},{16,24},{24,16},{1,9},{9,1},{17,25},{25,17},{2,10},{10... | collective-permute-start | bytes 1253384 | tf_op jit(solution)/shard_map/ppermute | solution.py:77
  36.1 5.7 %collective-permute-start.8 = (bf16[32,768]{1,0:T(8,128)(2,1)S(1)}, bf16[32,768]{1,0:T(8,128)(2,1)S(1)}, u32[]{:S(2)}, u32[]{:S(2)}) collective-permute-start(bf16[32,768]{1,0:T(8,128)(2,1)S(1)} %get-tuple-element.35), channel_id=1, source_target_pairs={{0,4},{1,5},{2,6},{3,7},{4,0},{5,1},{6,2},{7,3},{8,12},{9,13},{10,... | collective-permute-start | bytes 147464 | tf_op jit(solution)/shard_map/ppermute | solution.py:77

commit v6 on v5

--- a/solution.py
+++ b/solution.py
@@ -113,6 +113,13 @@
     mark_ref[...] = jnp.zeros_like(mark_ref)
 
 
+def join_note_body(side_ref, own_ref, came_ref, note_ref, out_ref, noted_ref):
+    rows = out_ref.shape[0]
+    join_body(side_ref, own_ref, came_ref, out_ref)
+    noted_ref[:rows, :] = out_ref[...]
+    noted_ref[rows:, :] = note_ref[...]
+
+
 def slope_of(rows, weights_ref, chosen, place):
     count = rows.shape[0]
     blocks = weights_ref.shape[0] // BLOCK
@@ -145,12 +152,9 @@
     dq_ref[...] = dq.astype(dq_ref.dtype)
 
 
-def near_body(rows_ref, weights_ref, note_ref, dq_ref, slope_ref, noted_ref, held_ref):
+def near_body(rows_ref, weights_ref, note_ref, dq_ref, slope_ref, held_ref):
     held_ref[...] = weights_ref[...]
     grad_body(0, rows_ref, weights_ref, note_ref, dq_ref, slope_ref)
-    half = rows_ref.shape[0]
-    noted_ref[:half, :] = rows_ref[...]
-    noted_ref[half:, :] = note_ref[...]
 
 
 def far_body(rows_ref, weights_ref, note_ref, dq_ref, slope_ref, far_out):
@@ -195,10 +199,11 @@
     return set_ref[:half, :], set_ref[half + NOTE :, :], set_ref[half : half + NOTE, :]
 
 
-def pack_body(near_ref, far_ref, out_ref):
+def fold_pack_body(side_ref, kept_ref, came_ref, near_ref, far_ref, keep_ref, send_ref, set_ref):
     noted = near_ref.shape[0]
-    out_ref[:noted, :] = near_ref[...]
-    out_ref[noted:, :] = far_ref[...]
+    fold_body(side_ref, kept_ref, came_ref, keep_ref, send_ref)
+    set_ref[:noted, :] = near_ref[...]
+    set_ref[noted:, :] = far_ref[...]
 
 
 def add_sets(acc_ref, weights_ref, set_refs):
@@ -260,29 +265,25 @@
     bit = homes // 2
     came = swap(queries, "lab", bit)
     near = local_call(hold_body, [like(q_home, width, bf16)], [queries])[0]
-    while True:
+    while bit > 2:
         near, mark = local_call(
             join_mark_body,
             [like(2 * near.shape[0], width, bf16), like(1, BLOCK, jnp.int32)],
             [side(bit), near, came],
         )
         bit //= 2
-        if bit == 1:
-            break
-        note = make_note(
-            sibling_blocks, positive_slot, mark[0, 0], lab_dev // BLOCK, homes, width
-        )
         came = swap(near, "lab", bit)
+    note = make_note(sibling_blocks, positive_slot, mark[0, 0], lab_dev // BLOCK, homes, width)
+    near, noted = local_call(
+        join_note_body,
+        [like(half, width, bf16), like(half + NOTE, width, bf16)],
+        [side(bit), near, came, note],
+    )
     far = swap(near, "lab", 1)
     work = 4 * half * lab_dev * width
-    near_dq, near_slope, noted, weights = local_call(
+    near_dq, near_slope, weights = local_call(
         near_body,
-        [
-            like(half, width, f32),
-            like(lab_dev, half, bf16),
-            like(half + NOTE, width, bf16),
-            like(lab_dev, width, bf16),
-        ],
+        [like(half, width, f32), like(lab_dev, half, bf16), like(lab_dev, width, bf16)],
         [near, label_weights, note],
         work,
     )
@@ -305,15 +306,16 @@
     cross_far = swap(far_copy, "pb", far_bit)
     mate = swap(whole, "pb", 1)
     rows = half // 2
-    kept, send = local_call(
-        fold_body, [like(rows, width, f32), like(rows, width, bf16)], [side(2), near_dq, came], 0, [acc]
+    kept, send, cross = local_call(
+        fold_pack_body,
+        [like(rows, width, f32), like(rows, width, bf16), like(qcount + NOTE, width, bf16)],
+        [side(2), near_dq, came, cross_near, cross_far],
+        0,
+        [acc],
     )
     came = swap(send, "lab", 2)
-    cross = local_call(
-        pack_body, [like(qcount + NOTE, width, bf16)], [cross_near, cross_far], 0, [kept]
-    )[0]
     acc = local_call(
-        mate_body, [like(lab_dev, width, f32)], [mate, weights, acc], 40 * work, [cross]
+        mate_body, [like(lab_dev, width, f32)], [mate, weights, acc], 2 * work, [kept]
     )[0]
     cross_mate = swap(cross, "pb", 1)
     bit = 4

time: 42.7 us -> 41.4 us (0.970)
  waiting for transfers between devices: 12.5 us -> 10.8 us
  starting transfers between devices: 14.6 us -> 15.5 us
  Pallas kernels: 9.91 us -> 9.38 us
    ppermute x10, waiting for transfers between devices: 12.5 us -> 10.8 us  [swap(): return lax.ppermute(value, axis, [(i, i ^ bit) for i in range(count)])]
    ppermute x10, starting transfers between devices: 14.6 us -> 15.5 us  [swap(): return lax.ppermute(value, axis, [(i, i ^ bit) for i in range(count)])]
    pallas_call x12 -> x11, Pallas kernels: 9.91 us -> 9.38 us  [local_call(): pl.pallas_call(lambda *refs: body(*refs[:given], *refs[later:]), out_shap...]
  transfers between devices with their start and end apart: 10 -> 10, of which waited for: 5 -> 5; matrix products, arithmetic and copies ran while one was open for 6% -> 0% of each run, Pallas kernels for 19% -> 21%
where the time goes in v6:
time: 41.4 us; the launch traced here: 41.1 us
  starting transfers between devices  15.5 us (37%)
  waiting for transfers between devices  10.8 us (26%)
  Pallas kernels  9.38 us (23%)
  local copies, waits for them, and re-layouts  2.51 us (6%)
  other arithmetic  2.22 us (5%)
  between operations  0.72 us (2%)
    ppermute x10, starting transfers between devices, swap(): return lax.ppermute(value, axis, [(i, i ^ bit) for i in range(count)])  15.5 us
    ppermute x10, waiting for transfers between devices, swap(): return lax.ppermute(value, axis, [(i, i ^ bit) for i in range(count)])  10.8 us
    pallas_call x11, Pallas kernels, local_call(): pl.pallas_call(lambda *refs: body(*refs[:given], *refs[later:]), out_shap...  9.38 us
    unnamed x4, local copies, waits for them, and re-layouts  2.24 us
  transfers between devices with their start and end apart: 10, of which 5 were waited for; matrix products, arithmetic and copies ran while one was open for 0% of the time, Pallas kernels for 21%

profile of v6, /device:TPU:0, one launch (start us, length us, event | category | flops | bytes accessed | tf_op | source)
XLA Modules:
  0.0 41.1 jit_solution(4782176267389740714)
XLA Ops:
  0.6 4.1 %collective-permute-start = (bf16[32,768]{1,0:T(8,128)(2,1)}, bf16[32,768]{1,0:T(8,128)(2,1)S(1)}, u32[]{:S(2)}, u32[]{:S(2)}) collective-permute-start(bf16[32,768]{1,0:T(8,128)(2,1)} %refs_0_.1), channel_id=1, source_target_pairs={{0,4},{1,5},{2,6},{3,7},{4,0},{5,1},{6,2},{7,3},{8,12},{9,13},{10,... | collective-permute-start | bytes 147464 | tf_op jit(solution)/shard_map/ppermute | solution.py:77
  4.7 0.8 %copy-done.1 = bf16[32,768]{1,0:T(8,128)(2,1)S(1)} copy-done((bf16[32,768]{1,0:T(8,128)(2,1)S(1)}, bf16[32,768]{1,0:T(8,128)(2,1)}, u32[]{:S(2)}) %copy-start.1) | copy-done | bytes 49176
  5.6 2.0 %collective-permute-done.refs_2_ = bf16[32,768]{1,0:T(8,128)(2,1)S(1)} collective-permute-done((bf16[32,768]{1,0:T(8,128)(2,1)}, bf16[32,768]{1,0:T(8,128)(2,1)S(1)}, u32[]{:S(2)}, u32[]{:S(2)}) %collective-permute-start) | collective-permute-done | bytes 49184 | tf_op jit(solution)/shard_map/ppermute | solution.py:77
  7.6 0.7 %and_select_fusion.1 = s32[256]{0:T(256)S(1)} fusion(s32[256]{0:T(256)} %param.7, s32[]{:T(128)S(1)} %bitcast.22), kind=kLoop, calls=%fused_computation.12 | loop fusion | flops 4096 | bytes 2052 | tf_op jit(solution)/shard_map/jit(floor_divide)/jit(_where)/select_n | solution.py:240
  8.3 0.7 %fusion = (s32[256]{0:T(256)S(1)}, s32[256]{0:T(256)S(1)}) fusion(s32[256,8]{0,1:T(8,128)} %param.6, s32[]{:T(128)S(6)} %mul.3, s32[]{:T(128)S(1)} %bitcast.23, s32[256]{0:T(256)S(1)} %and_select_fusion.1), kind=kLoop, calls=%fused_computation.4 | loop fusion | flops 19968 | bytes 11272 | tf_op jit(solution)/shard_map/reduce_max | solution.py:238
  9.0 0.7 %fusion.4 = (bf16[256]{0:T(256)(128)(2,1)S(1)}, bf16[256]{0:T(256)(128)(2,1)S(1)}) fusion(s32[256]{0:T(256)S(1)} %get-tuple-element.40, s32[256]{0:T(256)} %param.7, s32[]{:T(128)S(1)} %bitcast.24, s32[256]{0:T(256)S(1)} %get-tuple-element.41), kind=kLoop, calls=%fused_computation.20 | loop fusion | flops 4096 | bytes 4100 | tf_op jit(solution)/shard_map/convert.3
  10.0 1.4 %collective-permute-start.1 = (bf16[64,768]{1,0:T(8,128)(2,1)S(1)}, bf16[64,768]{1,0:T(8,128)(2,1)S(1)}, u32[]{:S(2)}, u32[]{:S(2)}) collective-permute-start(bf16[64,768]{1,0:T(8,128)(2,1)S(1)} %get-tuple-element.21.refs_1_), channel_id=1, source_target_pairs={{0,2},{1,3},{2,0},{3,1},{4,6},{5,7},{6,4},{7,5},{8,10},{9,11},{10,... | collective-permute-start | bytes 294920 | tf_op jit(solution)/shard_map/ppermute | solution.py:77
  11.4 3.2 %collective-permute-done.1.refs_2_ = bf16[64,768]{1,0:T(8,128)(2,1)S(1)} collective-permute-done((bf16[64,768]{1,0:T(8,128)(2,1)S(1)}, bf16[64,768]{1,0:T(8,128)(2,1)S(1)}, u32[]{:S(2)}, u32[]{:S(2)}) %collective-permute-start.1) | collective-permute-done | bytes 98336 | tf_op jit(solution)/shard_map/ppermute | solution.py:77
  14.7 1.8 %collective-permute-start.2 = (bf16[128,768]{1,0:T(8,128)(2,1)S(1)}, bf16[128,768]{1,0:T(8,128)(2,1)S(1)}, u32[]{:S(2)}, u32[]{:S(2)}) collective-permute-start(bf16[128,768]{1,0:T(8,128)(2,1)S(1)} %get-tuple-element.23.refs_0_), channel_id=1, source_target_pairs={{0,1},{1,0},{2,3},{3,2},{4,5},{5,4},{6,7},{7,6},{8,9},{9,8},{10,11... | collective-permute-start | bytes 589832 | tf_op jit(solution)/shard_map/ppermute | solution.py:77
  16.5 1.5 %collective-permute-start.4 = (bf16[144,768]{1,0:T(8,128)(2,1)S(1)}, bf16[144,768]{1,0:T(8,128)(2,1)S(1)}, u32[]{:S(2)}, u32[]{:S(2)}) collective-permute-start(bf16[144,768]{1,0:T(8,128)(2,1)S(1)} %get-tuple-element.27.refs_4_), channel_id=1, source_target_pairs={{0,16},{8,24},{16,0},{24,8},{1,17},{9,25},{17,1},{25,9},{2,18},{10... | collective-permute-start | bytes 663560 | tf_op jit(solution)/shard_map/ppermute | solution.py:77
  18.0 1.4 %copy-done = bf16[1024,768]{1,0:T(8,128)(2,1)S(1)} copy-done((bf16[1024,768]{1,0:T(8,128)(2,1)S(1)}, bf16[1024,768]{1,0:T(8,128)(2,1)}, u32[]{:S(2)}) %copy-start) | copy-done | bytes 1572888
  19.4 1.4 %shard_map.62 = (f32[128,768]{1,0:T(8,128)S(1)}, bf16[1024,128]{1,0:T(8,128)(2,1)S(1)}, bf16[1024,768]{1,0:T(8,128)(2,1)S(1)}) custom-call(bf16[128,768]{1,0:T(8,128)(2,1)S(1)} %get-tuple-element.23.refs_0_, bf16[1024,768]{1,0:T(8,128)(2,1)S(1)} %copy-done, bf16[16,768]{1,0:T(8,128)(2,1)S(1)} %pad.4.refs_3_.refs_2_), custom_call_target="tpu_custom_call" | custom-call | flops 402653184 | tf_op jit(solution)/shard_map/pallas_call | solution.py:86
  20.8 1.3 %shard_map.63 = (bf16[128,768]{1,0:T(8,128)(2,1)S(1)}, bf16[1024,128]{1,0:T(8,128)(2,1)S(1)}, bf16[128,768]{1,0:T(8,128)(2,1)S(1)}) custom-call(bf16[128,768]{1,0:T(8,128)(2,1)S(1)} %collective-permute-done.2.refs_0_.refs_1_, bf16[1024,768]{1,0:T(8,128)(2,1)S(1)} %get-tuple-element.25.refs_1_.refs_2_, bf16[16,768]{1,0:T(8,128)(2,1)S(1)} %pad.4.refs_3_.refs_2_, ...), custom_call_target="tpu_custom_call" | custom-call | flops 402653184 | tf_op jit(solution)/shard_map/pallas_call | solution.py:86
  22.1 1.4 %collective-permute-start.3 = (bf16[128,768]{1,0:T(8,128)(2,1)S(1)}, bf16[128,768]{1,0:T(8,128)(2,1)S(1)}, u32[]{:S(2)}, u32[]{:S(2)}) collective-permute-start(bf16[128,768]{1,0:T(8,128)(2,1)S(1)} %get-tuple-element.26), channel_id=1, source_target_pairs={{0,1},{1,0},{2,3},{3,2},{4,5},{5,4},{6,7},{7,6},{8,9},{9,8},{10,11... | collective-permute-start | bytes 589832 | tf_op jit(solution)/shard_map/ppermute | solution.py:77
  23.6 1.5 %collective-permute-start.5 = (bf16[128,768]{1,0:T(8,128)(2,1)S(1)}, bf16[128,768]{1,0:T(8,128)(2,1)S(1)}, u32[]{:S(2)}, u32[]{:S(2)}) collective-permute-start(bf16[128,768]{1,0:T(8,128)(2,1)S(1)} %get-tuple-element.28), channel_id=1, source_target_pairs={{0,16},{8,24},{16,0},{24,8},{1,17},{9,25},{17,1},{25,9},{2,18},{10... | collective-permute-start | bytes 589832 | tf_op jit(solution)/shard_map/ppermute | solution.py:77
  25.1 0.6 %shard_map.64 = (f32[1024,768]{1,0:T(8,128)S(1)}, bf16[272,768]{1,0:T(8,128)(2,1)S(1)}) custom-call(bf16[128,768]{1,0:T(8,128)(2,1)S(1)} %get-tuple-element.23.refs_0_, bf16[128,768]{1,0:T(8,128)(2,1)S(1)} %collective-permute-done.2.refs_0_.refs_1_, bf16[1024,128]{1,0:T(8,128)(2,1)S(1)} %get-tuple-element.29.refs_2_, ...), custom_call_target="tpu_custom_call" | custom-call | flops 402653184 | tf_op jit(solution)/shard_map/pallas_call | solution.py:86
  25.7 2.1 %collective-permute-done.3.refs_2_ = bf16[128,768]{1,0:T(8,128)(2,1)S(1)} collective-permute-done((bf16[128,768]{1,0:T(8,128)(2,1)S(1)}, bf16[128,768]{1,0:T(8,128)(2,1)S(1)}, u32[]{:S(2)}, u32[]{:S(2)}) %collective-permute-start.3) | collective-permute-done | bytes 196640 | tf_op jit(solution)/shard_map/ppermute | solution.py:77
  27.9 1.4 %collective-permute-done.5.refs_4_ = bf16[128,768]{1,0:T(8,128)(2,1)S(1)} collective-permute-done((bf16[128,768]{1,0:T(8,128)(2,1)S(1)}, bf16[128,768]{1,0:T(8,128)(2,1)S(1)}, u32[]{:S(2)}, u32[]{:S(2)}) %collective-permute-start.5) | collective-permute-done | bytes 196640 | tf_op jit(solution)/shard_map/ppermute | solution.py:77
  29.4 1.2 %collective-permute-start.6 = (bf16[64,768]{1,0:T(8,128)(2,1)S(1)}, bf16[64,768]{1,0:T(8,128)(2,1)S(1)}, u32[]{:S(2)}, u32[]{:S(2)}) collective-permute-start(bf16[64,768]{1,0:T(8,128)(2,1)S(1)} %get-tuple-element.33), channel_id=1, source_target_pairs={{0,2},{1,3},{2,0},{3,1},{4,6},{5,7},{6,4},{7,5},{8,10},{9,11},{10,... | collective-permute-start | bytes 294920 | tf_op jit(solution)/shard_map/ppermute | solution.py:77
  30.6 1.9 %shard_map.66.refs_3_ = f32[1024,768]{1,0:T(8,128)S(1)} custom-call(bf16[272,768]{1,0:T(8,128)(2,1)S(1)} %collective-permute-done.7.refs_0_, bf16[1024,768]{1,0:T(8,128)(2,1)S(1)} %get-tuple-element.25.refs_1_.refs_2_, f32[1024,768]{1,0:T(8,128)S(1)} %get-tuple-element.31.refs_5_.refs_2_, f32[64,768]{1,0:T(8,128)S(1)} %get-tuple-element.32.refs_3_.refs_1_), custom_call_target="tpu_custom_call" | custom-call | flops 805306368 | tf_op jit(solution)/shard_map/pallas_call | solution.py:86
  32.5 2.1 %collective-permute-done.6.refs_2_ = bf16[64,768]{1,0:T(8,128)(2,1)S(1)} collective-permute-done((bf16[64,768]{1,0:T(8,128)(2,1)S(1)}, bf16[64,768]{1,0:T(8,128)(2,1)S(1)}, u32[]{:S(2)}, u32[]{:S(2)}) %collective-permute-start.6) | collective-permute-done | bytes 98336 | tf_op jit(solution)/shard_map/ppermute | solution.py:77
  34.6 2.5 %collective-permute-start.8 = (bf16[32,768]{1,0:T(8,128)(2,1)S(1)}, bf16[32,768]{1,0:T(8,128)(2,1)S(1)}, u32[]{:S(2)}, u32[]{:S(2)}) collective-permute-start(bf16[32,768]{1,0:T(8,128)(2,1)S(1)} %get-tuple-element.36), channel_id=1, source_target_pairs={{0,4},{1,5},{2,6},{3,7},{4,0},{5,1},{6,2},{7,3},{8,12},{9,13},{10,... | collective-permute-start | bytes 147464 | tf_op jit(solution)/shard_map/ppermute | solution.py:77
  37.1 3.4 %shard_map.68 = (bf16[1024,768]{1,0:T(8,128)(2,1)}, s32[1,128]{1,0:T(1,128)S(1)}) custom-call(bf16[272,768]{1,0:T(8,128)(2,1)S(1)} %get-tuple-element.37.refs_0_, bf16[272,768]{1,0:T(8,128)(2,1)S(1)} %collective-permute-done.9.refs_1_, bf16[1024,768]{1,0:T(8,128)(2,1)S(1)} %get-tuple-element.25.refs_1_.refs_2_, f32[1024,768]{1,0:T(8,128)S(1)} %shard_map.66.refs_3_, ...), custom_call_target="tpu_custom_call" | custom-call | flops 1610612736 | tf_op jit(solution)/shard_map/pallas_call | solution.py:86
  40.5 0.7 %shard_map.69 = f32[32,768]{1,0:T(8,128)} custom-call(f32[32,768]{1,0:T(8,128)S(1)} %get-tuple-element.35.refs_4_.refs_0_, bf16[32,768]{1,0:T(8,128)(2,1)S(1)} %collective-permute-done.8.refs_1_, s32[1,128]{1,0:T(1,128)S(1)} %get-tuple-element.38.refs_2_), custom_call_target="tpu_custom_call" | custom-call | tf_op jit(solution)/shard_map/pallas_call | solution.py:86
  (21 shorter events, 0.6 us)
Async XLA Ops:
  0.6 6.9 %collective-permute-start = (bf16[32,768]{1,0:T(8,128)(2,1)}, bf16[32,768]{1,0:T(8,128)(2,1)S(1)}, u32[]{:S(2)}, u32[]{:S(2)}) collective-permute-start(bf16[32,768]{1,0:T(8,128)(2,1)} %refs_0_.1), channel_id=1, source_target_pairs={{0,4},{1,5},{2,6},{3,7},{4,0},{5,1},{6,2},{7,3},{8,12},{9,13},{10,... | collective-permute-start | bytes 147464 | tf_op jit(solution)/shard_map/ppermute | solution.py:77
  4.7 0.8 %copy-start.1 = (bf16[32,768]{1,0:T(8,128)(2,1)S(1)}, bf16[32,768]{1,0:T(8,128)(2,1)}, u32[]{:S(2)}) copy-start(bf16[32,768]{1,0:T(8,128)(2,1)} %refs_0_.1) | copy-start | bytes 147460
  10.0 4.6 %collective-permute-start.1 = (bf16[64,768]{1,0:T(8,128)(2,1)S(1)}, bf16[64,768]{1,0:T(8,128)(2,1)S(1)}, u32[]{:S(2)}, u32[]{:S(2)}) collective-permute-start(bf16[64,768]{1,0:T(8,128)(2,1)S(1)} %get-tuple-element.21.refs_1_), channel_id=1, source_target_pairs={{0,2},{1,3},{2,0},{3,1},{4,6},{5,7},{6,4},{7,5},{8,10},{9,11},{10,... | collective-permute-start | bytes 294920 | tf_op jit(solution)/shard_map/ppermute | solution.py:77
  14.7 6.1 %collective-permute-start.2 = (bf16[128,768]{1,0:T(8,128)(2,1)S(1)}, bf16[128,768]{1,0:T(8,128)(2,1)S(1)}, u32[]{:S(2)}, u32[]{:S(2)}) collective-permute-start(bf16[128,768]{1,0:T(8,128)(2,1)S(1)} %get-tuple-element.23.refs_0_), channel_id=1, source_target_pairs={{0,1},{1,0},{2,3},{3,2},{4,5},{5,4},{6,7},{7,6},{8,9},{9,8},{10,11... | collective-permute-start | bytes 589832 | tf_op jit(solution)/shard_map/ppermute | solution.py:77
  16.5 8.6 %collective-permute-start.4 = (bf16[144,768]{1,0:T(8,128)(2,1)S(1)}, bf16[144,768]{1,0:T(8,128)(2,1)S(1)}, u32[]{:S(2)}, u32[]{:S(2)}) collective-permute-start(bf16[144,768]{1,0:T(8,128)(2,1)S(1)} %get-tuple-element.27.refs_4_), channel_id=1, source_target_pairs={{0,16},{8,24},{16,0},{24,8},{1,17},{9,25},{17,1},{25,9},{2,18},{10... | collective-permute-start | bytes 663560 | tf_op jit(solution)/shard_map/ppermute | solution.py:77
  18.0 1.4 %copy-start = (bf16[1024,768]{1,0:T(8,128)(2,1)S(1)}, bf16[1024,768]{1,0:T(8,128)(2,1)}, u32[]{:S(2)}) copy-start(bf16[1024,768]{1,0:T(8,128)(2,1)} %refs_1_.1) | copy-start | bytes 4718596
  22.1 5.7 %collective-permute-start.3 = (bf16[128,768]{1,0:T(8,128)(2,1)S(1)}, bf16[128,768]{1,0:T(8,128)(2,1)S(1)}, u32[]{:S(2)}, u32[]{:S(2)}) collective-permute-start(bf16[128,768]{1,0:T(8,128)(2,1)S(1)} %get-tuple-element.26), channel_id=1, source_target_pairs={{0,1},{1,0},{2,3},{3,2},{4,5},{5,4},{6,7},{7,6},{8,9},{9,8},{10,11... | collective-permute-start | bytes 589832 | tf_op jit(solution)/shard_map/ppermute | solution.py:77
  23.6 5.7 %collective-permute-start.5 = (bf16[128,768]{1,0:T(8,128)(2,1)S(1)}, bf16[128,768]{1,0:T(8,128)(2,1)S(1)}, u32[]{:S(2)}, u32[]{:S(2)}) collective-permute-start(bf16[128,768]{1,0:T(8,128)(2,1)S(1)} %get-tuple-element.28), channel_id=1, source_target_pairs={{0,16},{8,24},{16,0},{24,8},{1,17},{9,25},{17,1},{25,9},{2,18},{10... | collective-permute-start | bytes 589832 | tf_op jit(solution)/shard_map/ppermute | solution.py:77
  25.7 5.0 %collective-permute-start.7 = (bf16[272,768]{1,0:T(8,128)(2,1)S(1)}, bf16[272,768]{1,0:T(8,128)(2,1)S(1)}, u32[]{:S(2)}, u32[]{:S(2)}) collective-permute-start(bf16[272,768]{1,0:T(8,128)(2,1)S(1)} %get-tuple-element.34), channel_id=1, source_target_pairs={{0,8},{8,0},{16,24},{24,16},{1,9},{9,1},{17,25},{25,17},{2,10},{10... | collective-permute-start | bytes 1253384 | tf_op jit(solution)/shard_map/ppermute | solution.py:77
  29.3 7.8 %collective-permute-start.9 = (bf16[272,768]{1,0:T(8,128)(2,1)S(1)}, bf16[272,768]{1,0:T(8,128)(2,1)S(1)}, u32[]{:S(2)}, u32[]{:S(2)}) collective-permute-start(bf16[272,768]{1,0:T(8,128)(2,1)S(1)} %get-tuple-element.37.refs_0_), channel_id=1, source_target_pairs={{0,8},{8,0},{16,24},{24,16},{1,9},{9,1},{17,25},{25,17},{2,10},{10... | collective-permute-start | bytes 1253384 | tf_op jit(solution)/shard_map/ppermute | solution.py:77
  29.4 5.2 %collective-permute-start.6 = (bf16[64,768]{1,0:T(8,128)(2,1)S(1)}, bf16[64,768]{1,0:T(8,128)(2,1)S(1)}, u32[]{:S(2)}, u32[]{:S(2)}) collective-permute-start(bf16[64,768]{1,0:T(8,128)(2,1)S(1)} %get-tuple-element.33), channel_id=1, source_target_pairs={{0,2},{1,3},{2,0},{3,1},{4,6},{5,7},{6,4},{7,5},{8,10},{9,11},{10,... | collective-permute-start | bytes 294920 | tf_op jit(solution)/shard_map/ppermute | solution.py:77
  34.6 5.9 %collective-permute-start.8 = (bf16[32,768]{1,0:T(8,128)(2,1)S(1)}, bf16[32,768]{1,0:T(8,128)(2,1)S(1)}, u32[]{:S(2)}, u32[]{:S(2)}) collective-permute-start(bf16[32,768]{1,0:T(8,128)(2,1)S(1)} %get-tuple-element.36), channel_id=1, source_target_pairs={{0,4},{1,5},{2,6},{3,7},{4,0},{5,1},{6,2},{7,3},{8,12},{9,13},{10,... | collective-permute-start | bytes 147464 | tf_op jit(solution)/shard_map/ppermute | solution.py:77

commit v7 on v6

--- a/solution.py
+++ b/solution.py
@@ -77,6 +77,16 @@
     return lax.ppermute(value, axis, [(i, i ^ bit) for i in range(count)])
 
 
+def diagonal(value, group_bit, home_bit):
+    groups, homes = lax.axis_size("pb"), lax.axis_size("lab")
+    pairs = [
+        (g * homes + h, (g ^ group_bit) * homes + (h ^ home_bit))
+        for g in range(groups)
+        for h in range(homes)
+    ]
+    return lax.ppermute(value, ("pb", "lab"), pairs)
+
+
 def local_call(body, outs, args, flops=0, follows=()):
     specs = [
         pl.BlockSpec(memory_space=pltpu.SMEM if arg.dtype == jnp.int32 else pltpu.VMEM)
@@ -97,27 +107,19 @@
     return jax.ShapeDtypeStruct((rows, width), dtype)
 
 
-def join_body(side_ref, own_ref, came_ref, out_ref):
-    rows = own_ref.shape[0]
-    side = side_ref[0]
-    out_ref[pl.ds(pl.multiple_of(side * rows, rows), rows), :] = own_ref[...]
-    out_ref[pl.ds(pl.multiple_of((1 - side) * rows, rows), rows), :] = came_ref[...]
+def join_body(place_ref, own_ref, *refs):
+    *came_refs, note_ref, out_ref, noted_ref = refs
+    rows, place = own_ref.shape[0], place_ref[0]
+    for step, ref in enumerate([own_ref, *came_refs]):
+        start = pl.multiple_of((place ^ step) * rows, rows)
+        out_ref[pl.ds(start, rows), :] = ref[...]
+    half = out_ref.shape[0]
+    noted_ref[:half, :] = out_ref[...]
+    noted_ref[half:, :] = note_ref[...]
 
 
 def hold_body(rows_ref, held_ref):
     held_ref[...] = rows_ref[...]
-
-
-def join_mark_body(side_ref, own_ref, came_ref, out_ref, mark_ref):
-    join_body(side_ref, own_ref, came_ref, out_ref)
-    mark_ref[...] = jnp.zeros_like(mark_ref)
-
-
-def join_note_body(side_ref, own_ref, came_ref, note_ref, out_ref, noted_ref):
-    rows = out_ref.shape[0]
-    join_body(side_ref, own_ref, came_ref, out_ref)
-    noted_ref[:rows, :] = out_ref[...]
-    noted_ref[rows:, :] = note_ref[...]
 
 
 def slope_of(rows, weights_ref, chosen, place):
@@ -157,23 +159,29 @@
     grad_body(0, rows_ref, weights_ref, note_ref, dq_ref, slope_ref)
 
 
-def far_body(rows_ref, weights_ref, note_ref, dq_ref, slope_ref, far_out):
-    grad_body(1, rows_ref, weights_ref, note_ref, dq_ref, slope_ref)
-    far_out[...] = rows_ref[...]
-
-
-def fold_body(side_ref, kept_ref, came_ref, keep_ref, send_ref):
-    rows = keep_ref.shape[0]
+def far_body(side_ref, rows_ref, weights_ref, note_ref, near_ref, dq_ref, slope_ref):
+    rows = rows_ref[...]
+    half = rows.shape[0]
+    planes, homes, q_home = 2, dq_ref.shape[0], dq_ref.shape[1]
     side = side_ref[0]
-    mine = pl.ds(pl.multiple_of(side * rows, rows), rows)
-    other = pl.ds(pl.multiple_of((1 - side) * rows, rows), rows)
-    keep_ref[...] = kept_ref[mine, :] + came_ref[mine, :].astype(jnp.float32)
-    send = kept_ref[other, :] + came_ref[other, :].astype(jnp.float32)
-    send_ref[...] = send.astype(send_ref.dtype)
-
-
-def last_body(kept_ref, came_ref, out_ref):
-    out_ref[...] = kept_ref[...] + came_ref[...].astype(jnp.float32)
+    note = note_ref[...].astype(jnp.float32)
+    slope = slope_of(rows, weights_ref, *read_note(note, 1, half))
+    slope_ref[...] = slope
+    far = lax.dot_general(
+        slope, weights_ref[...], (((0,), (0,)), ((), ())), preferred_element_type=jnp.float32
+    ).astype(dq_ref.dtype)
+    near = near_ref[...]
+    for z in range(homes // planes):
+        part = slice(z * q_home, (z + 1) * q_home)
+        dq_ref[planes * z + side] = near[part, :]
+        dq_ref[planes * z + 1 - side] = far[part, :]
+
+
+def sum_body(terms_ref, out_ref):
+    total = terms_ref[0].astype(jnp.float32)
+    for source in range(1, terms_ref.shape[0]):
+        total = total + terms_ref[source].astype(jnp.float32)
+    out_ref[...] = total
 
 
 def slopes_of_set(near_rows, far_rows, note, weights_ref):
@@ -199,11 +207,10 @@
     return set_ref[:half, :], set_ref[half + NOTE :, :], set_ref[half : half + NOTE, :]
 
 
-def fold_pack_body(side_ref, kept_ref, came_ref, near_ref, far_ref, keep_ref, send_ref, set_ref):
+def pack_body(near_ref, far_ref, out_ref):
     noted = near_ref.shape[0]
-    fold_body(side_ref, kept_ref, came_ref, keep_ref, send_ref)
-    set_ref[:noted, :] = near_ref[...]
-    set_ref[noted:, :] = far_ref[...]
+    out_ref[:noted, :] = near_ref[...]
+    out_ref[noted:, :] = far_ref[...]
 
 
 def add_sets(acc_ref, weights_ref, set_refs):
@@ -230,8 +237,7 @@
     out_ref[...] = (total / groups).astype(out_ref.dtype)
 
 
-def make_note(sibling_blocks, positive_slot, mark, blocks_dev, homes, width):
-    sibling_blocks, positive_slot = sibling_blocks + mark, positive_slot + mark
+def make_note(sibling_blocks, positive_slot, blocks_dev, homes, width):
     me = lax.axis_index("lab")
     local = sibling_blocks.T - me * blocks_dev
     inside = (local >= 0) & (local < blocks_dev)
@@ -240,10 +246,7 @@
     pblock = jnp.sum(jnp.where(steps == (positive_slot // BLOCK)[None, :], local, 0), axis=0)
     place = jnp.where(pblock == chosen, positive_slot % BLOCK, -1)
     code = jnp.stack([chosen, place]).astype(jnp.bfloat16)
-    bits = homes.bit_length() - 1
-    code = code.reshape((2,) + (2,) * bits + (-1,))
-    code = code.transpose((bits, 0) + tuple(range(bits - 1, 0, -1)) + (bits + 1,))
-    code = code.reshape(2, 2, -1)
+    code = code.reshape(2, homes // 2, 2, -1).transpose(2, 0, 1, 3).reshape(2, 2, -1)
     code = jnp.where(me % 2 == 0, code, code[::-1]).reshape(4, -1)
     return jnp.pad(code, ((0, NOTE - 4), (0, width - code.shape[1])))
 
@@ -258,88 +261,56 @@
     me = lax.axis_index("lab")
     f32, bf16 = jnp.float32, jnp.bfloat16
 
-    def side(bit):
-        return jnp.reshape((me // bit) % 2, (1,)).astype(jnp.int32)
-
+    place = jnp.reshape(me // 2, (1,)).astype(jnp.int32)
+    side = jnp.reshape(me % 2, (1,)).astype(jnp.int32)
     far_bit = groups // 2
-    bit = homes // 2
-    came = swap(queries, "lab", bit)
-    near = local_call(hold_body, [like(q_home, width, bf16)], [queries])[0]
-    while bit > 2:
-        near, mark = local_call(
-            join_mark_body,
-            [like(2 * near.shape[0], width, bf16), like(1, BLOCK, jnp.int32)],
-            [side(bit), near, came],
-        )
-        bit //= 2
-        came = swap(near, "lab", bit)
-    note = make_note(sibling_blocks, positive_slot, mark[0, 0], lab_dev // BLOCK, homes, width)
+    came = [swap(queries, "lab", 2 * step) for step in range(1, homes // 2)]
+    held = local_call(hold_body, [like(q_home, width, bf16)], [queries])[0]
+    note = make_note(sibling_blocks, positive_slot, lab_dev // BLOCK, homes, width)
     near, noted = local_call(
-        join_note_body,
+        join_body,
         [like(half, width, bf16), like(half + NOTE, width, bf16)],
-        [side(bit), near, came, note],
+        [place, held, *came, note],
     )
     far = swap(near, "lab", 1)
     work = 4 * half * lab_dev * width
     near_dq, near_slope, weights = local_call(
         near_body,
-        [like(half, width, f32), like(lab_dev, half, bf16), like(lab_dev, width, bf16)],
+        [like(half, width, bf16), like(lab_dev, half, bf16), like(lab_dev, width, bf16)],
         [near, label_weights, note],
         work,
     )
     cross_near = swap(noted, "pb", far_bit)
-    far_dq, far_slope, far_copy = local_call(
+    cross_far = diagonal(near, far_bit, 1)
+    dq, far_slope = local_call(
         far_body,
-        [like(half, width, bf16), like(lab_dev, half, bf16), like(half, width, bf16)],
-        [far, weights, note],
+        [jax.ShapeDtypeStruct((homes, q_home, width), bf16), like(lab_dev, half, bf16)],
+        [side, far, weights, note, near_dq],
         work,
-        [near_dq],
-    )
-    came = swap(far_dq, "lab", 1)
+    )
+    terms = lax.all_to_all(dq, "lab", split_axis=0, concat_axis=0, tiled=True)
     acc, whole = local_call(
         own_body,
         [like(lab_dev, width, f32), like(qcount + NOTE, width, bf16)],
         [near, far, near_slope, far_slope, noted],
         work,
-        [cross_near],
-    )
-    cross_far = swap(far_copy, "pb", far_bit)
+        [],
+    )
     mate = swap(whole, "pb", 1)
-    rows = half // 2
-    kept, send, cross = local_call(
-        fold_pack_body,
-        [like(rows, width, f32), like(rows, width, bf16), like(qcount + NOTE, width, bf16)],
-        [side(2), near_dq, came, cross_near, cross_far],
-        0,
-        [acc],
-    )
-    came = swap(send, "lab", 2)
-    acc = local_call(
-        mate_body, [like(lab_dev, width, f32)], [mate, weights, acc], 2 * work, [kept]
+    cross = local_call(
+        pack_body, [like(qcount + NOTE, width, bf16)], [cross_near, cross_far], 0, [acc]
     )[0]
     cross_mate = swap(cross, "pb", 1)
-    bit = 4
-    while bit < homes:
-        rows //= 2
-        kept, send = local_call(
-            fold_body,
-            [like(rows, width, f32), like(rows, width, bf16)],
-            [side(bit), kept, came],
-            0,
-            [acc],
-        )
-        came = swap(send, "lab", bit)
-        bit *= 2
+    acc = local_call(
+        mate_body, [like(lab_dev, width, f32)], [mate, weights, acc], 2 * work, [cross]
+    )[0]
     weight_grad, mark = local_call(
         lambda *refs: late_body(groups, *refs),
         [like(lab_dev, width, bf16), like(1, BLOCK, jnp.int32)],
         [cross, cross_mate, weights, acc],
         4 * work,
-        [kept],
-    )
-    query_grad = local_call(
-        last_body, [like(q_home, width, f32)], [kept, came], 0, [mark]
-    )[0]
+    )
+    query_grad = local_call(sum_body, [like(q_home, width, f32)], [terms], 0, [mark])[0]
     return (query_grad, weight_grad)
 
 

time: 41.4 us -> 35.9 us (0.87)
  waiting for transfers between devices: 10.8 us -> 6.84 us
  starting transfers between devices: 15.5 us -> 13.3 us
  Pallas kernels: 9.38 us -> 10.1 us
    ppermute x10 -> x7, starting transfers between devices: 15.5 us -> 9.37 us  [swap(): return lax.ppermute(value, axis, [(i, i ^ bit) for i in range(count)])]
    ppermute x10 -> x7, waiting for transfers between devices: 10.8 us -> 5.39 us  [swap(): return lax.ppermute(value, axis, [(i, i ^ bit) for i in range(count)])]
    all_to_all x0 -> x1, starting transfers between devices: none -> 3.45 us  [dense_shards(): terms = lax.all_to_all(dq, 'lab', split_axis=0, concat_axis=0, tiled=True)]
    all_to_all x0 -> x1, waiting for transfers between devices: none -> 1.45 us  [dense_shards(): terms = lax.all_to_all(dq, 'lab', split_axis=0, concat_axis=0, tiled=True)]
    pallas_call x11 -> x9, Pallas kernels: 9.38 us -> 10.1 us  [local_call(): pl.pallas_call(lambda *refs: body(*refs[:given], *refs[later:]), out_shap...]
    ppermute x0 -> x1, starting transfers between devices: none -> 0.48 us  [diagonal(): return lax.ppermute(value, ('pb', 'lab'), pairs)]
  transfers between devices with their start and end apart: 10 -> 9, of which waited for: 5 -> 5; matrix products, arithmetic and copies ran while one was open for 0% -> 7% of each run, Pallas kernels for 21% -> 26%
where the time goes in v7:
time: 35.9 us; the launch traced here: 35.5 us
  starting transfers between devices  13.3 us (37%)
  Pallas kernels  10.1 us (28%)
  waiting for transfers between devices  6.84 us (19%)
  local copies, waits for them, and re-layouts  2.47 us (7%)
  other arithmetic  2.12 us (6%)
  between operations  0.74 us (2%)
    pallas_call x9, Pallas kernels, local_call(): pl.pallas_call(lambda *refs: body(*refs[:given], *refs[later:]), out_shap...  10.1 us
    ppermute x7, starting transfers between devices, swap(): return lax.ppermute(value, axis, [(i, i ^ bit) for i in range(count)])  9.37 us
    ppermute x7, waiting for transfers between devices, swap(): return lax.ppermute(value, axis, [(i, i ^ bit) for i in range(count)])  5.39 us
    all_to_all x1, starting transfers between devices, dense_shards(): terms = lax.all_to_all(dq, 'lab', split_axis=0, concat_axis=0, tiled=True)  3.45 us
    unnamed x4, local copies, waits for them, and re-layouts  2.21 us
    all_to_all x1, waiting for transfers between devices, dense_shards(): terms = lax.all_to_all(dq, 'lab', split_axis=0, concat_axis=0, tiled=True)  1.45 us
  transfers between devices with their start and end apart: 9, of which 5 were waited for; matrix products, arithmetic and copies ran while one was open for 7% of the time, Pallas kernels for 26%

profile of v7, /device:TPU:0, one launch (start us, length us, event | category | flops | bytes accessed | tf_op | source)
XLA Modules:
  0.0 35.5 jit_solution(10837082981572951992)
XLA Ops:
  0.6 3.1 %collective-permute-start = (bf16[32,768]{1,0:T(8,128)(2,1)}, bf16[32,768]{1,0:T(8,128)(2,1)S(1)}, u32[]{:S(2)}, u32[]{:S(2)}) collective-permute-start(bf16[32,768]{1,0:T(8,128)(2,1)} %refs_0_.1), channel_id=1, source_target_pairs={{0,2},{1,3},{2,0},{3,1},{4,6},{5,7},{6,4},{7,5},{8,10},{9,11},{10,... | collective-permute-start | bytes 147464 | tf_op jit(solution)/shard_map/ppermute | solution.py:77
  3.7 2.6 %collective-permute-start.1 = (bf16[32,768]{1,0:T(8,128)(2,1)}, bf16[32,768]{1,0:T(8,128)(2,1)S(1)}, u32[]{:S(2)}, u32[]{:S(2)}) collective-permute-start(bf16[32,768]{1,0:T(8,128)(2,1)} %refs_0_.1), channel_id=1, source_target_pairs={{0,4},{1,5},{2,6},{3,7},{4,0},{5,1},{6,2},{7,3},{8,12},{9,13},{10,... | collective-permute-start | bytes 147464 | tf_op jit(solution)/shard_map/ppermute | solution.py:77
  6.3 0.7 %and_select_fusion.1 = s32[256]{0:T(256)S(1)} fusion(s32[256]{0:T(256)} %param.7), kind=kLoop, calls=%fused_computation.11 | loop fusion | flops 3840 | bytes 2048 | tf_op jit(solution)/shard_map/jit(floor_divide)/jit(_where)/select_n | solution.py:246
  7.0 0.7 %fusion = (s32[256]{0:T(256)S(1)}, s32[256]{0:T(256)S(1)}) fusion(s32[256,8]{0,1:T(8,128)} %param.6, s32[]{:T(128)S(6)} %mul.3, s32[256]{0:T(256)S(1)} %and_select_fusion.1), kind=kLoop, calls=%fused_computation.4 | loop fusion | flops 17920 | bytes 11268 | tf_op jit(solution)/shard_map/reduce_max | solution.py:244
  7.7 0.7 %fusion.4 = (bf16[256]{0:T(256)(128)(2,1)S(1)}, bf16[256]{0:T(256)(128)(2,1)S(1)}) fusion(s32[256]{0:T(256)S(1)} %get-tuple-element.24, s32[256]{0:T(256)} %param.7, s32[256]{0:T(256)S(1)} %get-tuple-element.25), kind=kLoop, calls=%fused_computation.19 | loop fusion | flops 3840 | bytes 4096 | tf_op jit(solution)/shard_map/convert.3
  8.4 0.1 stack.10
  8.7 0.8 %copy-done.1 = bf16[32,768]{1,0:T(8,128)(2,1)S(1)} copy-done((bf16[32,768]{1,0:T(8,128)(2,1)S(1)}, bf16[32,768]{1,0:T(8,128)(2,1)}, u32[]{:S(2)}) %copy-start.1) | copy-done | bytes 49176
  9.5 0.3 collective-permute-done.1.refs_3_
  9.9 2.6 %collective-permute-done.2.refs_4_ = bf16[32,768]{1,0:T(8,128)(2,1)S(1)} collective-permute-done((bf16[32,768]{1,0:T(8,128)(2,1)}, bf16[32,768]{1,0:T(8,128)(2,1)S(1)}, u32[]{:S(2)}, u32[]{:S(2)}) %collective-permute-start.2) | collective-permute-done | bytes 49184 | tf_op jit(solution)/shard_map/ppermute | solution.py:77
  12.4 1.6 %collective-permute-start.3 = (bf16[128,768]{1,0:T(8,128)(2,1)S(1)}, bf16[128,768]{1,0:T(8,128)(2,1)S(1)}, u32[]{:S(2)}, u32[]{:S(2)}) collective-permute-start(bf16[128,768]{1,0:T(8,128)(2,1)S(1)} %get-tuple-element.13.refs_0_), channel_id=1, source_target_pairs={{0,1},{1,0},{2,3},{3,2},{4,5},{5,4},{6,7},{7,6},{8,9},{9,8},{10,11... | collective-permute-start | bytes 589832 | tf_op jit(solution)/shard_map/ppermute | solution.py:77
  14.0 1.5 %collective-permute-start.4 = (bf16[144,768]{1,0:T(8,128)(2,1)S(1)}, bf16[144,768]{1,0:T(8,128)(2,1)S(1)}, u32[]{:S(2)}, u32[]{:S(2)}) collective-permute-start(bf16[144,768]{1,0:T(8,128)(2,1)S(1)} %get-tuple-element.17.refs_4_), channel_id=1, source_target_pairs={{0,16},{8,24},{16,0},{24,8},{1,17},{9,25},{17,1},{25,9},{2,18},{10... | collective-permute-start | bytes 663560 | tf_op jit(solution)/shard_map/ppermute | solution.py:77
  15.5 0.5 %collective-permute-start.5 = (bf16[128,768]{1,0:T(8,128)(2,1)S(1)}, bf16[128,768]{1,0:T(8,128)(2,1)S(1)}, u32[]{:S(2)}, u32[]{:S(2)}) collective-permute-start(bf16[128,768]{1,0:T(8,128)(2,1)S(1)} %get-tuple-element.13.refs_0_), channel_id=1, source_target_pairs={{0,17},{1,16},{2,19},{3,18},{4,21},{5,20},{6,23},{7,22},{8,25},{9,... | collective-permute-start | bytes 589832 | tf_op jit(solution)/shard_map/ppermute | solution.py:87
  16.0 1.4 %copy-done = bf16[1024,768]{1,0:T(8,128)(2,1)S(1)} copy-done((bf16[1024,768]{1,0:T(8,128)(2,1)S(1)}, bf16[1024,768]{1,0:T(8,128)(2,1)}, u32[]{:S(2)}) %copy-start) | copy-done | bytes 1572888
  17.4 1.4 %shard_map.61 = (bf16[128,768]{1,0:T(8,128)(2,1)S(1)}, bf16[1024,128]{1,0:T(8,128)(2,1)S(1)}, bf16[1024,768]{1,0:T(8,128)(2,1)S(1)}) custom-call(bf16[128,768]{1,0:T(8,128)(2,1)S(1)} %get-tuple-element.13.refs_0_, bf16[1024,768]{1,0:T(8,128)(2,1)S(1)} %copy-done, bf16[16,768]{1,0:T(8,128)(2,1)S(1)} %pad.4.refs_5_.refs_2_.refs_3_), custom_call_target="tpu_custom_call" | custom-call | flops 402653184 | tf_op jit(solution)/shard_map/pallas_call | solution.py:96
  18.8 1.4 %collective-permute-done.3.refs_1_ = bf16[128,768]{1,0:T(8,128)(2,1)S(1)} collective-permute-done((bf16[128,768]{1,0:T(8,128)(2,1)S(1)}, bf16[128,768]{1,0:T(8,128)(2,1)S(1)}, u32[]{:S(2)}, u32[]{:S(2)}) %collective-permute-start.3) | collective-permute-done | bytes 196640 | tf_op jit(solution)/shard_map/ppermute | solution.py:77
  20.2 2.1 %shard_map.62 = (bf16[8,32,768]{2,1,0:T(8,128)(2,1)}, bf16[1024,128]{1,0:T(8,128)(2,1)S(1)}) custom-call(s32[1]{0:T(128)} %bitcast.refs_0_, bf16[128,768]{1,0:T(8,128)(2,1)S(1)} %collective-permute-done.3.refs_1_, bf16[1024,768]{1,0:T(8,128)(2,1)S(1)} %get-tuple-element.14.refs_2_.refs_1_, bf16[16,768]{1,0:T(8,128)(2,1)S(1)} %pad.4.refs_5_.refs_2_.refs_3_, ...), custom_call_target="tpu_custom_call" | custom-call | flops 402653184 | tf_op jit(solution)/shard_map/pallas_call | solution.py:96
  22.3 3.5 %all-to-all-start = ((bf16[8,32,768]{2,1,0:T(8,128)(2,1)}), bf16[8,32,768]{2,1,0:T(8,128)(2,1)S(1)}, u32[]{:S(2)}, u32[]{:S(2)}) async-start(bf16[8,32,768]{2,1,0:T(8,128)(2,1)} %get-tuple-element.16), calls=%async_computation | async-start | bytes 786432 | tf_op jit(solution)/shard_map/all_to_all | solution.py:291
  25.7 0.6 %shard_map.63 = (f32[1024,768]{1,0:T(8,128)S(1)}, bf16[272,768]{1,0:T(8,128)(2,1)S(1)}) custom-call(bf16[128,768]{1,0:T(8,128)(2,1)S(1)} %get-tuple-element.13.refs_0_, bf16[128,768]{1,0:T(8,128)(2,1)S(1)} %collective-permute-done.3.refs_1_, bf16[1024,128]{1,0:T(8,128)(2,1)S(1)} %get-tuple-element.18.refs_2_, ...), custom_call_target="tpu_custom_call" | custom-call | flops 402653184 | tf_op jit(solution)/shard_map/pallas_call | solution.py:96
  26.4 0.5 %collective-permute-start.6 = (bf16[272,768]{1,0:T(8,128)(2,1)S(1)}, bf16[272,768]{1,0:T(8,128)(2,1)S(1)}, u32[]{:S(2)}, u32[]{:S(2)}) collective-permute-start(bf16[272,768]{1,0:T(8,128)(2,1)S(1)} %shard_map.64.refs_3_.refs_0_), channel_id=1, source_target_pairs={{0,8},{8,0},{16,24},{24,16},{1,9},{9,1},{17,25},{25,17},{2,10},{10... | collective-permute-start | bytes 1253384 | tf_op jit(solution)/shard_map/ppermute | solution.py:77
  27.0 1.1 %collective-permute-done.7.refs_0_ = bf16[272,768]{1,0:T(8,128)(2,1)S(1)} collective-permute-done((bf16[272,768]{1,0:T(8,128)(2,1)S(1)}, bf16[272,768]{1,0:T(8,128)(2,1)S(1)}, u32[]{:S(2)}, u32[]{:S(2)}) %collective-permute-start.7) | collective-permute-done | bytes 417824 | tf_op jit(solution)/shard_map/ppermute | solution.py:77
  28.1 1.9 %shard_map.65.refs_3_ = f32[1024,768]{1,0:T(8,128)S(1)} custom-call(bf16[272,768]{1,0:T(8,128)(2,1)S(1)} %collective-permute-done.7.refs_0_, bf16[1024,768]{1,0:T(8,128)(2,1)S(1)} %get-tuple-element.14.refs_2_.refs_1_, f32[1024,768]{1,0:T(8,128)S(1)} %get-tuple-element.20.refs_2_, bf16[272,768]{1,0:T(8,128)(2,1)S(1)} %shard_map.64.refs_3_.refs_0_), custom_call_target="tpu_custom_call" | custom-call | flops 805306368 | tf_op jit(solution)/shard_map/pallas_call | solution.py:96
  30.0 3.4 %shard_map.66 = (bf16[1024,768]{1,0:T(8,128)(2,1)}, s32[1,128]{1,0:T(1,128)S(1)}) custom-call(bf16[272,768]{1,0:T(8,128)(2,1)S(1)} %shard_map.64.refs_3_.refs_0_, bf16[272,768]{1,0:T(8,128)(2,1)S(1)} %collective-permute-done.6.refs_1_, bf16[1024,768]{1,0:T(8,128)(2,1)S(1)} %get-tuple-element.14.refs_2_.refs_1_, f32[1024,768]{1,0:T(8,128)S(1)} %shard_map.65.refs_3_), custom_call_target="tpu_custom_call" | custom-call | flops 1610612736 | tf_op jit(solution)/shard_map/pallas_call | solution.py:96
  33.4 1.4 %all-to-all-done.refs_0_ = bf16[8,32,768]{2,1,0:T(8,128)(2,1)S(1)} async-done(((bf16[8,32,768]{2,1,0:T(8,128)(2,1)}), bf16[8,32,768]{2,1,0:T(8,128)(2,1)S(1)}, u32[]{:S(2)}, u32[]{:S(2)}) %all-to-all-start) | async-done | bytes 393248 | tf_op jit(solution)/shard_map/all_to_all | solution.py:291
  34.9 0.7 %shard_map.67 = f32[32,768]{1,0:T(8,128)} custom-call(bf16[8,32,768]{2,1,0:T(8,128)(2,1)S(1)} %all-to-all-done.refs_0_, s32[1,128]{1,0:T(1,128)S(1)} %get-tuple-element.22.refs_1_), custom_call_target="tpu_custom_call" | custom-call | tf_op jit(solution)/shard_map/pallas_call | solution.py:96
  (17 shorter events, 0.4 us)
Async XLA Ops:
  0.6 8.9 %collective-permute-start = (bf16[32,768]{1,0:T(8,128)(2,1)}, bf16[32,768]{1,0:T(8,128)(2,1)S(1)}, u32[]{:S(2)}, u32[]{:S(2)}) collective-permute-start(bf16[32,768]{1,0:T(8,128)(2,1)} %refs_0_.1), channel_id=1, source_target_pairs={{0,2},{1,3},{2,0},{3,1},{4,6},{5,7},{6,4},{7,5},{8,10},{9,11},{10,... | collective-permute-start | bytes 147464 | tf_op jit(solution)/shard_map/ppermute | solution.py:77
  3.7 6.1 %collective-permute-start.1 = (bf16[32,768]{1,0:T(8,128)(2,1)}, bf16[32,768]{1,0:T(8,128)(2,1)S(1)}, u32[]{:S(2)}, u32[]{:S(2)}) collective-permute-start(bf16[32,768]{1,0:T(8,128)(2,1)} %refs_0_.1), channel_id=1, source_target_pairs={{0,4},{1,5},{2,6},{3,7},{4,0},{5,1},{6,2},{7,3},{8,12},{9,13},{10,... | collective-permute-start | bytes 147464 | tf_op jit(solution)/shard_map/ppermute | solution.py:77
  6.3 6.1 %collective-permute-start.2 = (bf16[32,768]{1,0:T(8,128)(2,1)}, bf16[32,768]{1,0:T(8,128)(2,1)S(1)}, u32[]{:S(2)}, u32[]{:S(2)}) collective-permute-start(bf16[32,768]{1,0:T(8,128)(2,1)} %refs_0_.1), channel_id=1, source_target_pairs={{0,6},{1,7},{2,4},{3,5},{4,2},{5,3},{6,0},{7,1},{8,14},{9,15},{10,... | collective-permute-start | bytes 147464 | tf_op jit(solution)/shard_map/ppermute | solution.py:77
  8.7 0.8 %copy-start.1 = (bf16[32,768]{1,0:T(8,128)(2,1)S(1)}, bf16[32,768]{1,0:T(8,128)(2,1)}, u32[]{:S(2)}) copy-start(bf16[32,768]{1,0:T(8,128)(2,1)} %refs_0_.1) | copy-start | bytes 147460
  12.4 7.7 %collective-permute-start.3 = (bf16[128,768]{1,0:T(8,128)(2,1)S(1)}, bf16[128,768]{1,0:T(8,128)(2,1)S(1)}, u32[]{:S(2)}, u32[]{:S(2)}) collective-permute-start(bf16[128,768]{1,0:T(8,128)(2,1)S(1)} %get-tuple-element.13.refs_0_), channel_id=1, source_target_pairs={{0,1},{1,0},{2,3},{3,2},{4,5},{5,4},{6,7},{7,6},{8,9},{9,8},{10,11... | collective-permute-start | bytes 589832 | tf_op jit(solution)/shard_map/ppermute | solution.py:77
  14.0 12.4 %collective-permute-start.4 = (bf16[144,768]{1,0:T(8,128)(2,1)S(1)}, bf16[144,768]{1,0:T(8,128)(2,1)S(1)}, u32[]{:S(2)}, u32[]{:S(2)}) collective-permute-start(bf16[144,768]{1,0:T(8,128)(2,1)S(1)} %get-tuple-element.17.refs_4_), channel_id=1, source_target_pairs={{0,16},{8,24},{16,0},{24,8},{1,17},{9,25},{17,1},{25,9},{2,18},{10... | collective-permute-start | bytes 663560 | tf_op jit(solution)/shard_map/ppermute | solution.py:77
  15.5 10.9 %collective-permute-start.5 = (bf16[128,768]{1,0:T(8,128)(2,1)S(1)}, bf16[128,768]{1,0:T(8,128)(2,1)S(1)}, u32[]{:S(2)}, u32[]{:S(2)}) collective-permute-start(bf16[128,768]{1,0:T(8,128)(2,1)S(1)} %get-tuple-element.13.refs_0_), channel_id=1, source_target_pairs={{0,17},{1,16},{2,19},{3,18},{4,21},{5,20},{6,23},{7,22},{8,25},{9,... | collective-permute-start | bytes 589832 | tf_op jit(solution)/shard_map/ppermute | solution.py:87
  16.0 1.4 %copy-start = (bf16[1024,768]{1,0:T(8,128)(2,1)S(1)}, bf16[1024,768]{1,0:T(8,128)(2,1)}, u32[]{:S(2)}) copy-start(bf16[1024,768]{1,0:T(8,128)(2,1)} %refs_1_.1) | copy-start | bytes 4718596
  22.3 12.6 %all-to-all-start = ((bf16[8,32,768]{2,1,0:T(8,128)(2,1)}), bf16[8,32,768]{2,1,0:T(8,128)(2,1)S(1)}, u32[]{:S(2)}, u32[]{:S(2)}) async-start(bf16[8,32,768]{2,1,0:T(8,128)(2,1)} %get-tuple-element.16), calls=%async_computation | async-start | bytes 786432 | tf_op jit(solution)/shard_map/all_to_all | solution.py:291
  26.3 1.8 %collective-permute-start.7 = (bf16[272,768]{1,0:T(8,128)(2,1)S(1)}, bf16[272,768]{1,0:T(8,128)(2,1)S(1)}, u32[]{:S(2)}, u32[]{:S(2)}) collective-permute-start(bf16[272,768]{1,0:T(8,128)(2,1)S(1)} %get-tuple-element.21), channel_id=1, source_target_pairs={{0,8},{8,0},{16,24},{24,16},{1,9},{9,1},{17,25},{25,17},{2,10},{10... | collective-permute-start | bytes 1253384 | tf_op jit(solution)/shard_map/ppermute | solution.py:77
  26.4 3.6 %collective-permute-start.6 = (bf16[272,768]{1,0:T(8,128)(2,1)S(1)}, bf16[272,768]{1,0:T(8,128)(2,1)S(1)}, u32[]{:S(2)}, u32[]{:S(2)}) collective-permute-start(bf16[272,768]{1,0:T(8,128)(2,1)S(1)} %shard_map.64.refs_3_.refs_0_), channel_id=1, source_target_pairs={{0,8},{8,0},{16,24},{24,16},{1,9},{9,1},{17,25},{25,17},{2,10},{10... | collective-permute-start | bytes 1253384 | tf_op jit(solution)/shard_map/ppermute | solution.py:77

commit v8 on v0

--- a/solution.py
+++ b/solution.py
@@ -1,10 +1,14 @@
 import jax
 import jax.numpy as jnp
 from jax import lax
+from jax.experimental import pallas as pl
+from jax.experimental.pallas import tpu as pltpu
 from jax.sharding import PartitionSpec as P
 
 BLOCK = 128
 K = 8
+NOTE = 16
+VMEM_LIMIT = 24 * 1024 * 1024
 
 
 def pack_index(touched, width_slots, fill_value):
@@ -19,7 +23,7 @@
     return table[:, :width_slots]
 
 
-def shards(queries, label_weights, sibling_blocks, positive_slot):
+def sparse_shards(queries, label_weights, sibling_blocks, positive_slot):
     width = queries.shape[1]
     qcount = sibling_blocks.shape[0]
     lab_dev = label_weights.shape[0]
@@ -37,12 +41,10 @@
     target = (label_ids[None, :, :] == positive[:, None, None]).astype(jnp.float32)
     slope = jnp.where(chosen_all[:, :, None], jax.nn.sigmoid(scores) - target, 0.0)
     slope = slope.astype(jnp.bfloat16).reshape(count, lab_dev)
-    dq_rows = jnp.dot(slope, label_weights, preferred_element_type=jnp.float32)
-    dq_all = dq_rows
+    dq_all = jnp.dot(slope, label_weights, preferred_element_type=jnp.float32)
     w_acc = lax.dot_general(
         slope, piece, (((0,), (0,)), ((), ())), preferred_element_type=jnp.float32
     )
-    dq_all, w_acc = (dq_all, w_acc)
     homes = lax.axis_size("lab")
     q_home = qcount // homes
     slots = q_home * K // homes
@@ -70,7 +72,273 @@
     return (query_grad, weight_grad)
 
 
+def swap(value, axis, bit):
+    count = lax.axis_size(axis)
+    return lax.ppermute(value, axis, [(i, i ^ bit) for i in range(count)])
+
+
+def local_call(body, outs, args, flops=0, follows=()):
+    specs = [
+        pl.BlockSpec(memory_space=pltpu.SMEM if arg.dtype == jnp.int32 else pltpu.VMEM)
+        for arg in args
+    ]
+    given, later = len(args), len(args) + len(follows)
+    return pl.pallas_call(
+        lambda *refs: body(*refs[:given], *refs[later:]),
+        out_shape=outs,
+        in_specs=specs + [pl.BlockSpec(memory_space=pl.ANY)] * len(follows),
+        out_specs=[pl.BlockSpec(memory_space=pltpu.VMEM)] * len(outs),
+        cost_estimate=pl.CostEstimate(flops=flops, bytes_accessed=0, transcendentals=0),
+        compiler_params=pltpu.CompilerParams(vmem_limit_bytes=VMEM_LIMIT),
+    )(*args, *follows)
+
+
+def like(rows, width, dtype):
+    return jax.ShapeDtypeStruct((rows, width), dtype)
+
+
+def join_body(*refs):
+    *came_refs, note_ref, out_ref, noted_ref = refs
+    rows = came_refs[0].shape[0]
+    for step, ref in enumerate(came_refs):
+        out_ref[step * rows : (step + 1) * rows, :] = ref[...]
+    half = out_ref.shape[0]
+    noted_ref[:half, :] = out_ref[...]
+    noted_ref[half:, :] = note_ref[...]
+
+
+def prep_body(
+    me_ref, queries_ref, weights_ref, sibling_ref, slot_ref,
+    own_ref, held_ref, note_ref, sibling, slot, sems,
+):
+    pairs = [(sibling_ref, sibling), (slot_ref, slot), (queries_ref, own_ref), (weights_ref, held_ref)]
+    copies = [pltpu.make_async_copy(*pair, sems.at[i]) for i, pair in enumerate(pairs)]
+    for copy in copies:
+        copy.start()
+    for copy in copies[:2]:
+        copy.wait()
+    me, q_home = me_ref[0], queries_ref.shape[0]
+    blocks_dev = weights_ref.shape[0] // BLOCK
+    count = slot.shape[1]
+    local = sibling[...] - me * blocks_dev
+    inside = (local >= 0) & (local < blocks_dev)
+    chosen = jnp.max(jnp.where(inside, local, -1), axis=0, keepdims=True)
+    steps = lax.broadcasted_iota(jnp.int32, local.shape, 0)
+    named = steps == lax.shift_right_logical(slot[...], BLOCK.bit_length() - 1)
+    pblock = jnp.sum(jnp.where(named, local, 0), axis=0, keepdims=True)
+    place = jnp.where(pblock == chosen, slot[...] & (BLOCK - 1), -1)
+    rows = lax.broadcasted_iota(jnp.int32, (NOTE, count), 0)
+    code = jnp.where(rows == 0, chosen, jnp.where(rows == 1, place, 0))
+    shift, half = q_home.bit_length() - 1, count // 2
+    lane = lax.broadcasted_iota(jnp.int32, (count, count), 1)
+    source = lax.broadcasted_iota(jnp.int32, (count, count), 0)
+    plane = (lane >= half).astype(jnp.int32)
+    step = lax.shift_right_logical(lane & (half - 1), shift)
+    home = (2 * step + plane) ^ me
+    wanted = home * q_home + (lane & (q_home - 1))
+    order = jnp.where(source == wanted, 1.0, 0.0).astype(jnp.bfloat16)
+    note = jnp.dot(code.astype(jnp.bfloat16), order, preferred_element_type=jnp.float32)
+    note_ref[...] = jnp.zeros_like(note_ref)
+    note_ref[:, :count] = note.astype(note_ref.dtype)
+    for copy in copies[2:]:
+        copy.wait()
+
+
+def prepare(me, queries, weights, sibling, slot):
+    return pl.pallas_call(
+        prep_body,
+        out_shape=[
+            like(*queries.shape, queries.dtype),
+            like(*weights.shape, weights.dtype),
+            like(NOTE, queries.shape[1], jnp.bfloat16),
+        ],
+        in_specs=[pl.BlockSpec(memory_space=pltpu.SMEM)] + [pl.BlockSpec(memory_space=pl.ANY)] * 4,
+        out_specs=[pl.BlockSpec(memory_space=pltpu.VMEM)] * 3,
+        scratch_shapes=[
+            pltpu.VMEM(sibling.shape, jnp.int32),
+            pltpu.VMEM(slot.shape, jnp.int32),
+            pltpu.SemaphoreType.DMA((4,)),
+        ],
+        cost_estimate=pl.CostEstimate(flops=0, bytes_accessed=0, transcendentals=0),
+    )(me, queries, weights, sibling, slot)
+
+
+def slope_of(rows, weights_ref, chosen, place):
+    count = rows.shape[0]
+    blocks = weights_ref.shape[0] // BLOCK
+    scores = lax.dot_general(
+        weights_ref[...], rows, (((1,), (1,)), ((), ())), preferred_element_type=jnp.float32
+    )
+    named = jnp.zeros((BLOCK, count), jnp.float32)
+    for block in range(blocks):
+        named = jnp.where(chosen == block, scores[block * BLOCK : (block + 1) * BLOCK], named)
+    ids = lax.broadcasted_iota(jnp.int32, (BLOCK, count), 0)
+    slope = jax.nn.sigmoid(named) - jnp.where(ids == place, 1.0, 0.0)
+    parts = [jnp.where(chosen == block, slope, 0.0).astype(jnp.bfloat16) for block in range(blocks)]
+    return jnp.concatenate(parts, axis=0)
+
+
+def read_note(note, first, count):
+    code = note[:2, first : first + count].astype(jnp.float32).astype(jnp.int32)
+    return code[:1], code[1:]
+
+
+def grad_terms(first, rows_ref, weights_ref, note_ref, slope_ref):
+    rows = rows_ref[...]
+    slope = slope_of(rows, weights_ref, *read_note(note_ref[...], first, rows.shape[0]))
+    slope_ref[...] = slope
+    return lax.dot_general(
+        slope, weights_ref[...], (((0,), (0,)), ((), ())), preferred_element_type=jnp.float32
+    )
+
+
+def near_body(place_ref, rows_ref, weights_ref, note_ref, slope_ref, terms_ref):
+    dq = grad_terms(0, rows_ref, weights_ref, note_ref, slope_ref).astype(terms_ref.dtype)
+    count = terms_ref.shape[1]
+    for step in range(terms_ref.shape[0]):
+        terms_ref[step ^ place_ref[0]] = dq[step * count : (step + 1) * count]
+
+
+def far_body(rows_ref, weights_ref, note_ref, slope_ref, *term_refs):
+    dq = grad_terms(rows_ref.shape[0], rows_ref, weights_ref, note_ref, slope_ref)
+    count = term_refs[0].shape[0]
+    for step, ref in enumerate(term_refs):
+        ref[...] = dq[step * count : (step + 1) * count].astype(ref.dtype)
+
+
+def sum_body(near_ref, *refs):
+    *term_refs, out_ref, mark_ref = refs
+    mark_ref[...] = jnp.zeros_like(mark_ref)
+    total = near_ref[0].astype(jnp.float32)
+    for step in range(1, near_ref.shape[0]):
+        total = total + near_ref[step].astype(jnp.float32)
+    for ref in term_refs:
+        total = total + ref[...].astype(jnp.float32)
+    out_ref[...] = total
+
+
+def slopes_of_set(near_rows, far_rows, note, weights_ref):
+    rows = jnp.concatenate([near_rows, far_rows], axis=0)
+    return rows, slope_of(rows, weights_ref, *read_note(note, 0, rows.shape[0]))
+
+
+def own_body(near_ref, far_ref, near_slope_ref, far_slope_ref, acc_ref):
+    rows = jnp.concatenate([near_ref[...], far_ref[...]], axis=0)
+    slope = jnp.concatenate([near_slope_ref[...], far_slope_ref[...]], axis=1)
+    acc_ref[...] = jnp.dot(slope, rows, preferred_element_type=jnp.float32)
+
+
+def pack_body(own_near_ref, own_far_ref, near_ref, far_ref, out_ref):
+    start = 0
+    for ref in (own_near_ref, own_far_ref, near_ref, far_ref):
+        out_ref[start : start + ref.shape[0], :] = ref[...]
+        start += ref.shape[0]
+
+
+def add_set(acc_ref, weights_ref, set_ref, start):
+    half = (set_ref.shape[0] // 2 - NOTE) // 2
+    middle = start + half + NOTE
+    rows, slope = slopes_of_set(
+        set_ref[start : start + half, :],
+        set_ref[middle : middle + half, :],
+        set_ref[start + half : middle, :],
+        weights_ref,
+    )
+    return acc_ref[...] + jnp.dot(slope, rows, preferred_element_type=jnp.float32)
+
+
+def add_body(start, set_ref, weights_ref, acc_ref, out_ref):
+    out_ref[...] = add_set(acc_ref, weights_ref, set_ref, start)
+
+
+def late_body(groups, start, set_ref, weights_ref, acc_ref, out_ref):
+    total = add_set(acc_ref, weights_ref, set_ref, start)
+    out_ref[...] = (total / groups).astype(out_ref.dtype)
+
+
+def dense_shards(queries, label_weights, sibling_blocks, positive_slot):
+    q_home, width = queries.shape
+    qcount = sibling_blocks.shape[0]
+    half = qcount // 2
+    lab_dev = label_weights.shape[0]
+    homes = lax.axis_size("lab")
+    groups = lax.axis_size("pb")
+    f32, bf16 = jnp.float32, jnp.bfloat16
+    far_bit = groups // 2
+    me = jnp.reshape(lax.axis_index("lab"), (1,)).astype(jnp.int32)
+    came = [swap(queries, "lab", step) for step in range(2, homes, 2)]
+    held, weights, note = prepare(
+        me, queries, label_weights, sibling_blocks.T, positive_slot.reshape(1, qcount)
+    )
+    near, noted = local_call(
+        join_body, [like(half, width, bf16), like(half + NOTE, width, bf16)], [held, *came, note]
+    )
+    far = swap(near, "lab", 1)
+    cross_near = swap(noted, "pb", far_bit)
+    work = 4 * half * lab_dev * width
+    slope = like(lab_dev, half, bf16)
+    near_slope, near_dq = local_call(
+        near_body,
+        [slope, jax.ShapeDtypeStruct((homes // 2, q_home, width), bf16)],
+        [me // 2, near, weights, note],
+        work,
+    )
+    planes = [list(range(plane, homes, 2)) for plane in range(2)]
+    near_terms = lax.all_to_all(
+        near_dq, "lab", split_axis=0, concat_axis=0, axis_index_groups=planes, tiled=True
+    )
+    cross_far = swap(far, "pb", far_bit)
+    far_slope, *far_terms = local_call(
+        far_body,
+        [slope] + [like(q_home, width, bf16)] * (homes // 2),
+        [far, weights, note],
+        work,
+        [near_dq],
+    )
+    terms = [swap(out, "lab", 2 * step + 1) for step, out in enumerate(far_terms)]
+    acc = local_call(
+        own_body, [like(lab_dev, width, f32)], [near, far, near_slope, far_slope], work
+    )[0]
+    span = qcount + NOTE
+    pack = local_call(
+        pack_body, [like(2 * span, width, bf16)], [noted, far, cross_near, cross_far], 0, [acc]
+    )[0]
+    mate = swap(pack, "pb", 1)
+    grown = like(lab_dev, width, f32)
+    acc = local_call(
+        lambda *refs: add_body(span, *refs), [grown], [pack, weights, acc], 100 * work
+    )[0]
+    acc = local_call(
+        lambda *refs: add_body(0, *refs), [grown], [mate, weights, acc], 2 * work
+    )[0]
+    query_grad, mark = local_call(
+        sum_body,
+        [like(q_home, width, f32), like(1, BLOCK, jnp.int32)],
+        [near_terms, *terms],
+        0,
+        [acc],
+    )
+    weight_grad = local_call(
+        lambda *refs: late_body(groups, span, *refs),
+        [like(lab_dev, width, bf16)],
+        [mate, weights, acc],
+        2 * work,
+        [mark],
+    )[0]
+    return (query_grad, weight_grad)
+
+
 def solution(mesh):
+    groups, homes = mesh.shape["pb"], mesh.shape["lab"]
+
+    def shards(queries, label_weights, sibling_blocks, positive_slot):
+        every_row_everywhere = homes == K
+        few = groups * sibling_blocks.shape[0] <= 2 * label_weights.shape[0]
+        paired = groups == 4 and homes & (homes - 1) == 0
+        one_block = label_weights.shape[0] // BLOCK <= K
+        plan = dense_shards if every_row_everywhere and few and paired and one_block else sparse_shards
+        return plan(queries, label_weights, sibling_blocks, positive_slot)
+
     in_specs = (P(("pb", "lab"), None), P("lab", None), P("pb", None), P("pb"))
     out_specs = (P(("pb", "lab"), None), P("lab", None))
     return jax.shard_map(shards, mesh=mesh, in_specs=in_specs, out_specs=out_specs, check_vma=False)

time: 129 us -> 51.8 us (0.40)
  blocking collectives: 33 us -> 0 us
  waiting for transfers between devices: 31.8 us -> 7.2 us
  local copies, waits for them, and re-layouts: 28.9 us -> 7.95 us
  starting transfers between devices: 5.7 us -> 21 us
  Pallas kernels: 0 us -> 14.2 us
  between operations: 14.2 us -> 0.79 us
  other arithmetic: 11.1 us -> 0 us
  matrix products: 3.7 us -> 0 us
    all_gather x1 -> x0, blocking collectives: 33 us -> none  [shards(): piece = lax.all_gather(queries, 'lab', axis=0, tiled=True)]
    psum x1 -> x0, waiting for transfers between devices: 29.6 us -> none  [shards(): total = lax.psum(w_acc, 'pb')]
    scatter x2 -> x0, local copies, waits for them, and re-layouts: 22.4 us -> none  [pack_index(): jnp.full((homes, width_slots + 1), fill_value, jnp.int32)]
    ppermute x0 -> x11, starting transfers between devices: none -> 17.3 us  [swap(): return lax.ppermute(value, axis, [(i, i ^ bit) for i in range(count)])]
    pallas_call x0 -> x10, Pallas kernels: none -> 14.2 us  [the longest x9 11.6 us: local_call(): pl.pallas_call(lambda *refs: body(*refs[:given], *refs[later:]), out_shap...]
    unnamed x6 -> x20, local copies, waits for them, and re-layouts: 0.48 us -> 7.95 us
    ppermute x0 -> x11, waiting for transfers between devices: none -> 7.2 us  [swap(): return lax.ppermute(value, axis, [(i, i ^ bit) for i in range(count)])]
    gather x3 -> x0, local copies, waits for them, and re-layouts: 4.07 us -> none  [the longest x1 2.28 us: shards(): jnp.take_along_axis(sibling_blocks, (positive_slot // BLOCK)[:, None], ax...]
  transfers between devices with their start and end apart: 2 -> 12, of which waited for: 2 -> 4; matrix products, arithmetic and copies ran while one was open for 25% -> 0% of each run, Pallas kernels for 0% -> 20%
where the time goes in v8:
time: 51.8 us; the launch traced here: 51.2 us
  starting transfers between devices  21 us (41%)
  Pallas kernels  14.2 us (27%)
  local copies, waits for them, and re-layouts  7.95 us (15%)
  waiting for transfers between devices  7.2 us (14%)
  between operations  0.79 us (2%)
    ppermute x11, starting transfers between devices, swap(): return lax.ppermute(value, axis, [(i, i ^ bit) for i in range(count)])  17.3 us
    pallas_call x9, Pallas kernels, local_call(): pl.pallas_call(lambda *refs: body(*refs[:given], *refs[later:]), out_shap...  11.6 us
    unnamed x20, local copies, waits for them, and re-layouts  7.95 us
    ppermute x11, waiting for transfers between devices, swap(): return lax.ppermute(value, axis, [(i, i ^ bit) for i in range(count)])  7.2 us
    all_to_all x1, starting transfers between devices, dense_shards(): lax.all_to_all(near_dq, 'lab', split_axis=0, concat_axis=0, axis_index_gr...  3.77 us
    pallas_call x1, Pallas kernels, prepare(): pl.pallas_call(prep_body, out_shape=[like(*queries.shape, queries.dtype),...  2.65 us
  transfers between devices with their start and end apart: 12, of which 4 were waited for; matrix products, arithmetic and copies ran while one was open for 0% of the time, Pallas kernels for 20%

profile of v8, /device:TPU:0, one launch (start us, length us, event | category | flops | bytes accessed | tf_op | source)
XLA Modules:
  0.0 51.2 jit_solution(17493651256768543759)
XLA Ops:
  0.6 3.1 %collective-permute-start = (bf16[32,768]{1,0:T(8,128)(2,1)}, bf16[32,768]{1,0:T(8,128)(2,1)S(1)}, u32[]{:S(2)}, u32[]{:S(2)}) collective-permute-start(bf16[32,768]{1,0:T(8,128)(2,1)} %queries_ref.1), channel_id=1, source_target_pairs={{0,2},{1,3},{2,0},{3,1},{4,6},{5,7},{6,4},{7,5},{8,10},{9,11},{10,... | collective-permute-start | bytes 147464 | tf_op jit(solution)/shard_map/ppermute | solution.py:77
  3.7 2.5 %collective-permute-start.2 = (bf16[32,768]{1,0:T(8,128)(2,1)}, bf16[32,768]{1,0:T(8,128)(2,1)S(1)}, u32[]{:S(2)}, u32[]{:S(2)}) collective-permute-start(bf16[32,768]{1,0:T(8,128)(2,1)} %queries_ref.1), channel_id=1, source_target_pairs={{0,6},{1,7},{2,4},{3,5},{4,2},{5,3},{6,0},{7,1},{8,14},{9,15},{10,... | collective-permute-start | bytes 147464 | tf_op jit(solution)/shard_map/ppermute | solution.py:77
  6.3 2.6 %shard_map.59 = (bf16[32,768]{1,0:T(8,128)(2,1)}, bf16[1024,768]{1,0:T(8,128)(2,1)}, bf16[16,768]{1,0:T(8,128)(2,1)}) custom-call(s32[1]{0:T(128)} %bitcast.me_ref, bf16[32,768]{1,0:T(8,128)(2,1)} %queries_ref.1, bf16[1024,768]{1,0:T(8,128)(2,1)} %weights_ref.1, s32[8,256]{1,0:T(8,128)} %bitcast.3, s32[1,256]{1,0:T(1,128)} %bitcast.4), custom_call_target="tpu_custom_call" | custom-call | tf_op jit(solution)/shard_map/pallas_call | solution.py:148
  9.0 1.5 %collective-permute-done.2.refs_3_ = bf16[32,768]{1,0:T(8,128)(2,1)S(1)} collective-permute-done((bf16[32,768]{1,0:T(8,128)(2,1)}, bf16[32,768]{1,0:T(8,128)(2,1)S(1)}, u32[]{:S(2)}, u32[]{:S(2)}) %collective-permute-start.2) | collective-permute-done | bytes 49184 | tf_op jit(solution)/shard_map/ppermute | solution.py:77
  10.4 1.5 %collective-permute-done.1.refs_2_ = bf16[32,768]{1,0:T(8,128)(2,1)S(1)} collective-permute-done((bf16[32,768]{1,0:T(8,128)(2,1)}, bf16[32,768]{1,0:T(8,128)(2,1)S(1)}, u32[]{:S(2)}, u32[]{:S(2)}) %collective-permute-start.1) | collective-permute-done | bytes 49184 | tf_op jit(solution)/shard_map/ppermute | solution.py:77
  12.7 0.8 %copy-done.9 = bf16[32,768]{1,0:T(8,128)(2,1)S(1)} copy-done((bf16[32,768]{1,0:T(8,128)(2,1)S(1)}, bf16[32,768]{1,0:T(8,128)(2,1)}, u32[]{:S(2)}) %copy-start.9) | copy-done | bytes 49176
  13.5 1.6 %collective-permute-start.3 = (bf16[128,768]{1,0:T(8,128)(2,1)S(1)}, bf16[128,768]{1,0:T(8,128)(2,1)S(1)}, u32[]{:S(2)}, u32[]{:S(2)}) collective-permute-start(bf16[128,768]{1,0:T(8,128)(2,1)S(1)} %get-tuple-element.18.refs_1_.refs_0_), channel_id=1, source_target_pairs={{0,1},{1,0},{2,3},{3,2},{4,5},{5,4},{6,7},{7,6},{8,9},{9,8},{10,11... | collective-permute-start | bytes 589832 | tf_op jit(solution)/shard_map/ppermute | solution.py:77
  15.1 1.5 %collective-permute-start.8 = (bf16[144,768]{1,0:T(8,128)(2,1)S(1)}, bf16[144,768]{1,0:T(8,128)(2,1)S(1)}, u32[]{:S(2)}, u32[]{:S(2)}) collective-permute-start(bf16[144,768]{1,0:T(8,128)(2,1)S(1)} %get-tuple-element.25.refs_0_), channel_id=1, source_target_pairs={{0,16},{8,24},{16,0},{24,8},{1,17},{9,25},{17,1},{25,9},{2,18},{10... | collective-permute-start | bytes 663560 | tf_op jit(solution)/shard_map/ppermute | solution.py:77
  16.6 2.7 %collective-permute-done.3.refs_0_.refs_1_ = bf16[128,768]{1,0:T(8,128)(2,1)S(1)} collective-permute-done((bf16[128,768]{1,0:T(8,128)(2,1)S(1)}, bf16[128,768]{1,0:T(8,128)(2,1)S(1)}, u32[]{:S(2)}, u32[]{:S(2)}) %collective-permute-start.3) | collective-permute-done | bytes 196640 | tf_op jit(solution)/shard_map/ppermute | solution.py:77
  19.2 1.5 %collective-permute-start.9 = (bf16[128,768]{1,0:T(8,128)(2,1)S(1)}, bf16[128,768]{1,0:T(8,128)(2,1)S(1)}, u32[]{:S(2)}, u32[]{:S(2)}) collective-permute-start(bf16[128,768]{1,0:T(8,128)(2,1)S(1)} %collective-permute-done.3.refs_0_.refs_1_), channel_id=1, source_target_pairs={{0,16},{8,24},{16,0},{24,8},{1,17},{9,25},{17,1},{25,9},{2,18},{10... | collective-permute-start | bytes 589832 | tf_op jit(solution)/shard_map/ppermute | solution.py:77
  20.7 1.4 %copy-done = bf16[1024,768]{1,0:T(8,128)(2,1)S(1)} copy-done((bf16[1024,768]{1,0:T(8,128)(2,1)S(1)}, bf16[1024,768]{1,0:T(8,128)(2,1)}, u32[]{:S(2)}) %copy-start) | copy-done | bytes 1572888
  22.9 2.0 %shard_map.61 = (bf16[1024,128]{1,0:T(8,128)(2,1)S(1)}, bf16[4,32,768]{2,1,0:T(8,128)(2,1)}) custom-call(s32[1]{0:T(128)S(6)} %select_n.5.refs_0_, bf16[128,768]{1,0:T(8,128)(2,1)S(1)} %get-tuple-element.18.refs_1_.refs_0_, bf16[1024,768]{1,0:T(8,128)(2,1)S(1)} %copy-done, bf16[16,768]{1,0:T(8,128)(2,1)S(1)} %copy-done.7), custom_call_target="tpu_custom_call" | custom-call | flops 402653184 | tf_op jit(solution)/shard_map/pallas_call | solution.py:86
  24.9 3.8 %all-to-all-start = ((bf16[4,32,768]{2,1,0:T(8,128)(2,1)}), bf16[4,32,768]{2,1,0:T(8,128)(2,1)S(1)}, u32[]{:S(2)}, u32[]{:S(2)}) async-start(bf16[4,32,768]{2,1,0:T(8,128)(2,1)} %get-tuple-element.20.refs_3_), calls=%async_computation | async-start | bytes 393216 | tf_op jit(solution)/shard_map/all_to_all | solution.py:287
  28.7 1.4 %copy-done.1 = bf16[1024,768]{1,0:T(8,128)(2,1)S(1)} copy-done((bf16[1024,768]{1,0:T(8,128)(2,1)S(1)}, bf16[1024,768]{1,0:T(8,128)(2,1)}, u32[]{:S(2)}) %copy-start.1) | copy-done | bytes 1572888
  30.8 1.3 %shard_map.62 = (bf16[1024,128]{1,0:T(8,128)(2,1)S(1)}, bf16[32,768]{1,0:T(8,128)(2,1)S(1)}, bf16[32,768]{1,0:T(8,128)(2,1)S(1)}, bf16[32,768]{1,0:T(8,128)(2,1)S(1)}, bf16[32,768]{1,0:T(8,128)(2,1)S(1)}) custom-call(bf16[128,768]{1,0:T(8,128)(2,1)S(1)} %collective-permute-done.3.refs_0_.refs_1_, bf16[1024,768]{1,0:T(8,128)(2,1)S(1)} %copy-done.1, ...), custom_call_target="tpu_custom_call" | custom-call | flops 402653184 | tf_op jit(solution)/shard_map/pallas_call | solution.py:86
  32.1 1.6 %collective-permute-start.4 = (bf16[32,768]{1,0:T(8,128)(2,1)S(1)}, bf16[32,768]{1,0:T(8,128)(2,1)S(1)}, u32[]{:S(2)}, u32[]{:S(2)}) collective-permute-start(bf16[32,768]{1,0:T(8,128)(2,1)S(1)} %get-tuple-element.21), channel_id=1, source_target_pairs={{0,1},{1,0},{2,3},{3,2},{4,5},{5,4},{6,7},{7,6},{8,9},{9,8},{10,11... | collective-permute-start | bytes 147464 | tf_op jit(solution)/shard_map/ppermute | solution.py:77
  33.7 2.0 %collective-permute-start.5 = (bf16[32,768]{1,0:T(8,128)(2,1)S(1)}, bf16[32,768]{1,0:T(8,128)(2,1)S(1)}, u32[]{:S(2)}, u32[]{:S(2)}) collective-permute-start(bf16[32,768]{1,0:T(8,128)(2,1)S(1)} %get-tuple-element.22), channel_id=1, source_target_pairs={{0,3},{1,2},{2,1},{3,0},{4,7},{5,6},{6,5},{7,4},{8,11},{9,10},{10,... | collective-permute-start | bytes 147464 | tf_op jit(solution)/shard_map/ppermute | solution.py:77
  35.7 3.3 %collective-permute-start.6 = (bf16[32,768]{1,0:T(8,128)(2,1)S(1)}, bf16[32,768]{1,0:T(8,128)(2,1)S(1)}, u32[]{:S(2)}, u32[]{:S(2)}) collective-permute-start(bf16[32,768]{1,0:T(8,128)(2,1)S(1)} %get-tuple-element.23), channel_id=1, source_target_pairs={{0,5},{1,4},{2,7},{3,6},{4,1},{5,0},{6,3},{7,2},{8,13},{9,12},{10,... | collective-permute-start | bytes 147464 | tf_op jit(solution)/shard_map/ppermute | solution.py:77
  39.8 1.2 %copy-done.2 = bf16[1024,768]{1,0:T(8,128)(2,1)S(1)} copy-done((bf16[1024,768]{1,0:T(8,128)(2,1)S(1)}, bf16[1024,768]{1,0:T(8,128)(2,1)}, u32[]{:S(2)}) %copy-start.2) | copy-done | bytes 1572888
  41.0 1.9 %shard_map.65.refs_2_ = f32[1024,768]{1,0:T(8,128)S(1)} custom-call(bf16[544,768]{1,0:T(8,128)(2,1)S(1)} %shard_map.64.refs_0_, bf16[1024,768]{1,0:T(8,128)(2,1)S(1)} %copy-done.2, f32[1024,768]{1,0:T(8,128)S(1)} %shard_map.63.refs_4_.refs_2_), custom_call_target="tpu_custom_call" | custom-call | flops 40265318400 | tf_op jit(solution)/shard_map/pallas_call | solution.py:86
  42.9 1.9 %shard_map.66.refs_5_.refs_2_ = f32[1024,768]{1,0:T(8,128)S(1)} custom-call(bf16[544,768]{1,0:T(8,128)(2,1)S(1)} %collective-permute-done.10.refs_0_, bf16[1024,768]{1,0:T(8,128)(2,1)S(1)} %copy-done.2, f32[1024,768]{1,0:T(8,128)S(1)} %shard_map.65.refs_2_), custom_call_target="tpu_custom_call" | custom-call | flops 805306368 | tf_op jit(solution)/shard_map/pallas_call | solution.py:86
  44.9 1.6 %collective-permute-done.7.refs_4_ = bf16[32,768]{1,0:T(8,128)(2,1)S(1)} collective-permute-done((bf16[32,768]{1,0:T(8,128)(2,1)S(1)}, bf16[32,768]{1,0:T(8,128)(2,1)S(1)}, u32[]{:S(2)}, u32[]{:S(2)}) %collective-permute-start.7) | collective-permute-done | bytes 49184 | tf_op jit(solution)/shard_map/ppermute | solution.py:77
  47.2 0.7 %copy-done.3 = bf16[1024,768]{1,0:T(8,128)(2,1)S(1)} copy-done((bf16[1024,768]{1,0:T(8,128)(2,1)S(1)}, bf16[1024,768]{1,0:T(8,128)(2,1)}, u32[]{:S(2)}) %copy-start.3) | copy-done | bytes 1572888
  48.1 3.1 %shard_map.68 = bf16[1024,768]{1,0:T(8,128)(2,1)} custom-call(bf16[544,768]{1,0:T(8,128)(2,1)S(1)} %copy-done.5, bf16[1024,768]{1,0:T(8,128)(2,1)S(1)} %copy-done.3, f32[1024,768]{1,0:T(8,128)S(1)} %shard_map.66.refs_5_.refs_2_, s32[1,128]{1,0:T(1,128)S(1)} %get-tuple-element.29.refs_3_), custom_call_target="tpu_custom_call" | custom-call | flops 805306368 | tf_op jit(solution)/shard_map/pallas_call | solution.py:86
  (30 shorter events, 4.1 us)
Async XLA Ops:
  0.6 8.3 %collective-permute-start = (bf16[32,768]{1,0:T(8,128)(2,1)}, bf16[32,768]{1,0:T(8,128)(2,1)S(1)}, u32[]{:S(2)}, u32[]{:S(2)}) collective-permute-start(bf16[32,768]{1,0:T(8,128)(2,1)} %queries_ref.1), channel_id=1, source_target_pairs={{0,2},{1,3},{2,0},{3,1},{4,6},{5,7},{6,4},{7,5},{8,10},{9,11},{10,... | collective-permute-start | bytes 147464 | tf_op jit(solution)/shard_map/ppermute | solution.py:77
  3.7 6.7 %collective-permute-start.2 = (bf16[32,768]{1,0:T(8,128)(2,1)}, bf16[32,768]{1,0:T(8,128)(2,1)S(1)}, u32[]{:S(2)}, u32[]{:S(2)}) collective-permute-start(bf16[32,768]{1,0:T(8,128)(2,1)} %queries_ref.1), channel_id=1, source_target_pairs={{0,6},{1,7},{2,4},{3,5},{4,2},{5,3},{6,0},{7,1},{8,14},{9,15},{10,... | collective-permute-start | bytes 147464 | tf_op jit(solution)/shard_map/ppermute | solution.py:77
  6.2 5.7 %collective-permute-start.1 = (bf16[32,768]{1,0:T(8,128)(2,1)}, bf16[32,768]{1,0:T(8,128)(2,1)S(1)}, u32[]{:S(2)}, u32[]{:S(2)}) collective-permute-start(bf16[32,768]{1,0:T(8,128)(2,1)} %queries_ref.1), channel_id=1, source_target_pairs={{0,4},{1,5},{2,6},{3,7},{4,0},{5,1},{6,2},{7,3},{8,12},{9,13},{10,... | collective-permute-start | bytes 147464 | tf_op jit(solution)/shard_map/ppermute | solution.py:77
  11.9 0.7 %copy-start.6 = (bf16[16,768]{1,0:T(8,128)(2,1)S(1)}, bf16[16,768]{1,0:T(8,128)(2,1)}, u32[]{:S(2)}) copy-start(bf16[16,768]{1,0:T(8,128)(2,1)} %get-tuple-element.17.refs_4_.refs_3_.refs_2_) | copy-start | bytes 73732
  12.7 0.8 %copy-start.9 = (bf16[32,768]{1,0:T(8,128)(2,1)S(1)}, bf16[32,768]{1,0:T(8,128)(2,1)}, u32[]{:S(2)}) copy-start(bf16[32,768]{1,0:T(8,128)(2,1)} %get-tuple-element.16.refs_0_) | copy-start | bytes 147460
  13.5 5.7 %collective-permute-start.3 = (bf16[128,768]{1,0:T(8,128)(2,1)S(1)}, bf16[128,768]{1,0:T(8,128)(2,1)S(1)}, u32[]{:S(2)}, u32[]{:S(2)}) collective-permute-start(bf16[128,768]{1,0:T(8,128)(2,1)S(1)} %get-tuple-element.18.refs_1_.refs_0_), channel_id=1, source_target_pairs={{0,1},{1,0},{2,3},{3,2},{4,5},{5,4},{6,7},{7,6},{8,9},{9,8},{10,11... | collective-permute-start | bytes 589832 | tf_op jit(solution)/shard_map/ppermute | solution.py:77
  15.1 24.5 %collective-permute-start.8 = (bf16[144,768]{1,0:T(8,128)(2,1)S(1)}, bf16[144,768]{1,0:T(8,128)(2,1)S(1)}, u32[]{:S(2)}, u32[]{:S(2)}) collective-permute-start(bf16[144,768]{1,0:T(8,128)(2,1)S(1)} %get-tuple-element.25.refs_0_), channel_id=1, source_target_pairs={{0,16},{8,24},{16,0},{24,8},{1,17},{9,25},{17,1},{25,9},{2,18},{10... | collective-permute-start | bytes 663560 | tf_op jit(solution)/shard_map/ppermute | solution.py:77
  19.2 20.5 %collective-permute-start.9 = (bf16[128,768]{1,0:T(8,128)(2,1)S(1)}, bf16[128,768]{1,0:T(8,128)(2,1)S(1)}, u32[]{:S(2)}, u32[]{:S(2)}) collective-permute-start(bf16[128,768]{1,0:T(8,128)(2,1)S(1)} %collective-permute-done.3.refs_0_.refs_1_), channel_id=1, source_target_pairs={{0,16},{8,24},{16,0},{24,8},{1,17},{9,25},{17,1},{25,9},{2,18},{10... | collective-permute-start | bytes 589832 | tf_op jit(solution)/shard_map/ppermute | solution.py:77
  20.7 1.4 %copy-start = (bf16[1024,768]{1,0:T(8,128)(2,1)S(1)}, bf16[1024,768]{1,0:T(8,128)(2,1)}, u32[]{:S(2)}) copy-start(bf16[1024,768]{1,0:T(8,128)(2,1)} %get-tuple-element.19.refs_2_.refs_1_) | copy-start | bytes 4718596
  22.1 0.7 %copy-start.7 = (bf16[16,768]{1,0:T(8,128)(2,1)S(1)}, bf16[16,768]{1,0:T(8,128)(2,1)}, u32[]{:S(2)}) copy-start(bf16[16,768]{1,0:T(8,128)(2,1)} %get-tuple-element.17.refs_4_.refs_3_.refs_2_) | copy-start | bytes 73732
  24.9 21.6 %all-to-all-start = ((bf16[4,32,768]{2,1,0:T(8,128)(2,1)}), bf16[4,32,768]{2,1,0:T(8,128)(2,1)S(1)}, u32[]{:S(2)}, u32[]{:S(2)}) async-start(bf16[4,32,768]{2,1,0:T(8,128)(2,1)} %get-tuple-element.20.refs_3_), calls=%async_computation | async-start | bytes 393216 | tf_op jit(solution)/shard_map/all_to_all | solution.py:287
  28.7 1.4 %copy-start.1 = (bf16[1024,768]{1,0:T(8,128)(2,1)S(1)}, bf16[1024,768]{1,0:T(8,128)(2,1)}, u32[]{:S(2)}) copy-start(bf16[1024,768]{1,0:T(8,128)(2,1)} %get-tuple-element.19.refs_2_.refs_1_) | copy-start | bytes 4718596
  30.1 0.7 %copy-start.8 = (bf16[16,768]{1,0:T(8,128)(2,1)S(1)}, bf16[16,768]{1,0:T(8,128)(2,1)}, u32[]{:S(2)}) copy-start(bf16[16,768]{1,0:T(8,128)(2,1)} %get-tuple-element.17.refs_4_.refs_3_.refs_2_) | copy-start | bytes 73732
  32.1 12.7 %collective-permute-start.4 = (bf16[32,768]{1,0:T(8,128)(2,1)S(1)}, bf16[32,768]{1,0:T(8,128)(2,1)S(1)}, u32[]{:S(2)}, u32[]{:S(2)}) collective-permute-start(bf16[32,768]{1,0:T(8,128)(2,1)S(1)} %get-tuple-element.21), channel_id=1, source_target_pairs={{0,1},{1,0},{2,3},{3,2},{4,5},{5,4},{6,7},{7,6},{8,9},{9,8},{10,11... | collective-permute-start | bytes 147464 | tf_op jit(solution)/shard_map/ppermute | solution.py:77
  33.7 11.1 %collective-permute-start.5 = (bf16[32,768]{1,0:T(8,128)(2,1)S(1)}, bf16[32,768]{1,0:T(8,128)(2,1)S(1)}, u32[]{:S(2)}, u32[]{:S(2)}) collective-permute-start(bf16[32,768]{1,0:T(8,128)(2,1)S(1)} %get-tuple-element.22), channel_id=1, source_target_pairs={{0,3},{1,2},{2,1},{3,0},{4,7},{5,6},{6,5},{7,4},{8,11},{9,10},{10,... | collective-permute-start | bytes 147464 | tf_op jit(solution)/shard_map/ppermute | solution.py:77
  35.7 9.2 %collective-permute-start.6 = (bf16[32,768]{1,0:T(8,128)(2,1)S(1)}, bf16[32,768]{1,0:T(8,128)(2,1)S(1)}, u32[]{:S(2)}, u32[]{:S(2)}) collective-permute-start(bf16[32,768]{1,0:T(8,128)(2,1)S(1)} %get-tuple-element.23), channel_id=1, source_target_pairs={{0,5},{1,4},{2,7},{3,6},{4,1},{5,0},{6,3},{7,2},{8,13},{9,12},{10,... | collective-permute-start | bytes 147464 | tf_op jit(solution)/shard_map/ppermute | solution.py:77
  39.6 1.4 %copy-start.2 = (bf16[1024,768]{1,0:T(8,128)(2,1)S(1)}, bf16[1024,768]{1,0:T(8,128)(2,1)}, u32[]{:S(2)}) copy-start(bf16[1024,768]{1,0:T(8,128)(2,1)} %get-tuple-element.19.refs_2_.refs_1_) | copy-start | bytes 4718596
  39.6 6.9 %collective-permute-start.7 = (bf16[32,768]{1,0:T(8,128)(2,1)S(1)}, bf16[32,768]{1,0:T(8,128)(2,1)S(1)}, u32[]{:S(2)}, u32[]{:S(2)}) collective-permute-start(bf16[32,768]{1,0:T(8,128)(2,1)S(1)} %get-tuple-element.24), channel_id=1, source_target_pairs={{0,7},{1,6},{2,5},{3,4},{4,3},{5,2},{6,1},{7,0},{8,15},{9,14},{10,... | collective-permute-start | bytes 147464 | tf_op jit(solution)/shard_map/ppermute | solution.py:77
  39.8 3.1 %collective-permute-start.10 = (bf16[544,768]{1,0:T(8,128)(2,1)S(1)}, bf16[544,768]{1,0:T(8,128)(2,1)S(1)}, u32[]{:S(2)}, u32[]{:S(2)}) collective-permute-start(bf16[544,768]{1,0:T(8,128)(2,1)S(1)} %shard_map.64.refs_0_), channel_id=1, source_target_pairs={{0,8},{8,0},{16,24},{24,16},{1,9},{9,1},{17,25},{25,17},{2,10},{10... | collective-permute-start | bytes 2506760 | tf_op jit(solution)/shard_map/ppermute | solution.py:77
  42.9 1.9 %copy-start.4 = (bf16[544,768]{1,0:T(8,128)(2,1)}, bf16[544,768]{1,0:T(8,128)(2,1)S(1)}, u32[]{:S(2)}) copy-start(bf16[544,768]{1,0:T(8,128)(2,1)S(1)} %collective-permute-done.10.refs_0_) | copy-start | bytes 2506756
  46.5 1.4 %copy-start.3 = (bf16[1024,768]{1,0:T(8,128)(2,1)S(1)}, bf16[1024,768]{1,0:T(8,128)(2,1)}, u32[]{:S(2)}) copy-start(bf16[1024,768]{1,0:T(8,128)(2,1)} %get-tuple-element.19.refs_2_.refs_1_) | copy-start | bytes 4718596
  46.5 1.7 %copy-start.5 = (bf16[544,768]{1,0:T(8,128)(2,1)S(1)}, bf16[544,768]{1,0:T(8,128)(2,1)}, u32[]{:S(2)}) copy-start(bf16[544,768]{1,0:T(8,128)(2,1)} %copy-done.4) | copy-start | bytes 2506756

commit v9 on v0

--- a/solution.py
+++ b/solution.py
@@ -1,10 +1,14 @@
 import jax
 import jax.numpy as jnp
 from jax import lax
+from jax.experimental import pallas as pl
+from jax.experimental.pallas import tpu as pltpu
 from jax.sharding import PartitionSpec as P
 
 BLOCK = 128
 K = 8
+NOTE = 16
+VMEM_LIMIT = 24 * 1024 * 1024
 
 
 def pack_index(touched, width_slots, fill_value):
@@ -19,7 +23,7 @@
     return table[:, :width_slots]
 
 
-def shards(queries, label_weights, sibling_blocks, positive_slot):
+def sparse_shards(queries, label_weights, sibling_blocks, positive_slot):
     width = queries.shape[1]
     qcount = sibling_blocks.shape[0]
     lab_dev = label_weights.shape[0]
@@ -37,12 +41,10 @@
     target = (label_ids[None, :, :] == positive[:, None, None]).astype(jnp.float32)
     slope = jnp.where(chosen_all[:, :, None], jax.nn.sigmoid(scores) - target, 0.0)
     slope = slope.astype(jnp.bfloat16).reshape(count, lab_dev)
-    dq_rows = jnp.dot(slope, label_weights, preferred_element_type=jnp.float32)
-    dq_all = dq_rows
+    dq_all = jnp.dot(slope, label_weights, preferred_element_type=jnp.float32)
     w_acc = lax.dot_general(
         slope, piece, (((0,), (0,)), ((), ())), preferred_element_type=jnp.float32
     )
-    dq_all, w_acc = (dq_all, w_acc)
     homes = lax.axis_size("lab")
     q_home = qcount // homes
     slots = q_home * K // homes
@@ -70,7 +72,251 @@
     return (query_grad, weight_grad)
 
 
+def swap(value, axis, bit):
+    count = lax.axis_size(axis)
+    return lax.ppermute(value, axis, [(i, i ^ bit) for i in range(count)])
+
+
+def local_call(body, outs, args, flops=0, follows=()):
+    specs = [
+        pl.BlockSpec(memory_space=pltpu.SMEM if arg.dtype == jnp.int32 else pltpu.VMEM)
+        for arg in args
+    ]
+    given, later = len(args), len(args) + len(follows)
+    return pl.pallas_call(
+        lambda *refs: body(*refs[:given], *refs[later:]),
+        out_shape=outs,
+        in_specs=specs + [pl.BlockSpec(memory_space=pl.ANY)] * len(follows),
+        out_specs=[pl.BlockSpec(memory_space=pltpu.VMEM)] * len(outs),
+        cost_estimate=pl.CostEstimate(flops=flops, bytes_accessed=0, transcendentals=0),
+        compiler_params=pltpu.CompilerParams(vmem_limit_bytes=VMEM_LIMIT),
+    )(*args, *follows)
+
+
+def like(rows, width, dtype):
+    return jax.ShapeDtypeStruct((rows, width), dtype)
+
+
+def stack_body(*refs):
+    *came_refs, out_ref = refs
+    start = 0
+    for ref in came_refs:
+        out_ref[start : start + ref.shape[0], : ref.shape[1]] = ref[...]
+        start += ref.shape[0]
+
+
+def grad_body(near_ref, far_ref, weights_ref, note_ref, kept_ref, slope_ref, *term_refs):
+    rows = jnp.concatenate([near_ref[...], far_ref[...]], axis=0)
+    weights = weights_ref[...]
+    count, blocks = rows.shape[0], weights.shape[0] // BLOCK
+    code = note_ref[:2, :count].astype(jnp.float32).astype(jnp.int32)
+    chosen, place = code[:1], code[1:]
+    scores = lax.dot_general(
+        weights, rows, (((1,), (1,)), ((), ())), preferred_element_type=jnp.float32
+    )
+    named = jnp.zeros((BLOCK, count), jnp.float32)
+    for block in range(blocks):
+        named = jnp.where(chosen == block, scores[block * BLOCK : (block + 1) * BLOCK], named)
+    ids = lax.broadcasted_iota(jnp.int32, (BLOCK, count), 0)
+    slope = (jax.nn.sigmoid(named) - jnp.where(ids == place, 1.0, 0.0)).astype(jnp.bfloat16)
+    slope_ref[:BLOCK, :] = slope
+    slope_ref[BLOCK:, :] = note_ref[:, :count]
+    dq = lax.dot_general(
+        spread(slope, chosen, range(blocks)),
+        weights,
+        (((0,), (0,)), ((), ())),
+        preferred_element_type=jnp.float32,
+    )
+    q_home = kept_ref.shape[0]
+    kept_ref[...] = dq[:q_home]
+    half = count // q_home // 2
+    for step, ref in enumerate(term_refs, 1):
+        start = (step // 2 + (step % 2) * half) * q_home
+        ref[...] = dq[start : start + q_home].astype(ref.dtype)
+
+
+def spread(slope, chosen, blocks):
+    wide = slope.astype(jnp.float32)
+    parts = [jnp.where(chosen == block, wide, 0.0).astype(slope.dtype) for block in blocks]
+    return jnp.concatenate(parts, axis=0)
+
+
+def read_slope(slope):
+    chosen = slope[BLOCK : BLOCK + 1].astype(jnp.float32).astype(jnp.int32)
+    return slope[:BLOCK], chosen
+
+
+def own_body(near_ref, far_ref, slope_ref, acc_ref):
+    rows = jnp.concatenate([near_ref[...], far_ref[...]], axis=0)
+    wide = spread(*read_slope(slope_ref[...]), range(acc_ref.shape[0] // BLOCK))
+    acc_ref[...] = jnp.dot(wide, rows, preferred_element_type=jnp.float32)
+
+
+def add_body(near_ref, far_ref, slope_ref, acc_ref, out_ref):
+    own_body(near_ref, far_ref, slope_ref, out_ref)
+    out_ref[...] += acc_ref[...]
+
+
+def late_body(groups, set_ref, acc_ref, out_ref, held, sems):
+    count = set_ref.shape[0] - BLOCK - NOTE
+    rows = set_ref[:count, :]
+    slope, chosen = read_slope(set_ref[count:, :count])
+    blocks = acc_ref.shape[0] // BLOCK
+    chunk = blocks // sems.shape[0]
+    copies = []
+    for part in range(sems.shape[0]):
+        here = pl.ds(part * chunk * BLOCK, chunk * BLOCK)
+        wide = spread(slope, chosen, range(part * chunk, (part + 1) * chunk))
+        total = acc_ref[here, :] + jnp.dot(wide, rows, preferred_element_type=jnp.float32)
+        held[here, :] = (total / groups).astype(held.dtype)
+        copy = pltpu.make_async_copy(held.at[here, :], out_ref.at[here, :], sems.at[part])
+        copy.start()
+        copies.append(copy)
+    for copy in copies:
+        copy.wait()
+
+
+def late(groups, swapped, acc, mark):
+    lab_dev, width = acc.shape
+    out = like(lab_dev, width, swapped.dtype)
+    chunks = 4
+    return pl.pallas_call(
+        lambda set_ref, acc_ref, mark_ref, *refs: late_body(groups, set_ref, acc_ref, *refs),
+        out_shape=out,
+        in_specs=[pl.BlockSpec(memory_space=pltpu.VMEM)] * 2 + [pl.BlockSpec(memory_space=pl.ANY)],
+        out_specs=pl.BlockSpec(memory_space=pl.ANY),
+        scratch_shapes=[pltpu.VMEM(out.shape, out.dtype), pltpu.SemaphoreType.DMA((chunks,))],
+        cost_estimate=pl.CostEstimate(flops=0, bytes_accessed=0, transcendentals=0),
+        compiler_params=pltpu.CompilerParams(vmem_limit_bytes=VMEM_LIMIT),
+    )(swapped, acc, mark)
+
+
+def sum_body(kept_ref, *refs):
+    *term_refs, out_ref, mark_ref = refs
+    mark_ref[...] = jnp.zeros_like(mark_ref)
+    total = kept_ref[...]
+    for ref in term_refs:
+        total = total + ref[...].astype(jnp.float32)
+    out_ref[...] = total
+
+
+def make_note(sibling_blocks, positive_slot, blocks_dev, homes, width):
+    me = lax.axis_index("lab")
+    local = sibling_blocks.T - me * blocks_dev
+    inside = (local >= 0) & (local < blocks_dev)
+    chosen = jnp.max(jnp.where(inside, local, -1), axis=0)
+    steps = jnp.arange(local.shape[0], dtype=jnp.int32)[:, None]
+    pblock = jnp.sum(jnp.where(steps == (positive_slot // BLOCK)[None, :], local, 0), axis=0)
+    place = jnp.where(pblock == chosen, positive_slot % BLOCK, -1)
+    code = jnp.stack([chosen, place]).astype(jnp.bfloat16)
+    return jnp.pad(code, ((0, NOTE - 2), (0, width - code.shape[1])))
+
+
+def order_body(me_ref, note_ref, q_home_ref, out_ref):
+    q_home, count = q_home_ref.shape[0], note_ref.shape[1]
+    half = count // 2
+    lane = lax.broadcasted_iota(jnp.int32, (count, count), 1)
+    source = lax.broadcasted_iota(jnp.int32, (count, count), 0)
+    plane = (lane >= half).astype(jnp.int32)
+    step = lax.shift_right_logical(lane & (half - 1), q_home.bit_length() - 1)
+    wanted = ((2 * step + plane) ^ me_ref[0]) * q_home + (lane & (q_home - 1))
+    order = jnp.where(source == wanted, 1.0, 0.0).astype(jnp.bfloat16)
+    note = jnp.dot(note_ref[...], order, preferred_element_type=jnp.float32)
+    out_ref[...] = note.astype(out_ref.dtype)
+
+
+def hold_body(rows_ref, held_ref):
+    held_ref[...] = rows_ref[...]
+
+
+def dense_shards(queries, label_weights, sibling_blocks, positive_slot):
+    q_home, width = queries.shape
+    qcount = sibling_blocks.shape[0]
+    half = qcount // 2
+    lab_dev = label_weights.shape[0]
+    homes = lax.axis_size("lab")
+    groups = lax.axis_size("pb")
+    f32, bf16 = jnp.float32, jnp.bfloat16
+    cross = groups // 2
+    me = jnp.reshape(lax.axis_index("lab"), (1,)).astype(jnp.int32)
+    came = {step: swap(queries, "lab", step) for step in range(2, homes, 2)}
+    came.update({step: swap(queries, "lab", step) for step in range(homes - 1, 0, -2)})
+    held = local_call(hold_body, [like(q_home, width, bf16)], [queries])[0]
+    note = make_note(sibling_blocks, positive_slot, lab_dev // BLOCK, homes, qcount)
+    note = local_call(order_body, [like(NOTE, qcount, bf16)], [me, note, held])[0]
+    near = [held] + [came[step] for step in range(2, homes, 2)]
+    near = local_call(stack_body, [like(half, width, bf16)], near)[0]
+    far = [came[step] for step in range(1, homes, 2)]
+    far = local_call(stack_body, [like(half, width, bf16)], far, 0, [near])[0]
+    work = 4 * half * lab_dev * width
+    slope_like = like(BLOCK + NOTE, qcount, bf16)
+    kept, slope, *terms = local_call(
+        grad_body,
+        [like(q_home, width, f32), slope_like] + [like(q_home, width, bf16)] * (homes - 1),
+        [near, far, label_weights, note],
+        2 * work,
+    )
+    terms = {step: swap(term, "lab", step) for step, term in enumerate(terms, 1)}
+    cross_near, cross_far = swap(near, "pb", cross), swap(far, "pb", cross)
+    cross_slope = swap(slope, "pb", cross)
+    grown = like(lab_dev, width, f32)
+    acc = local_call(own_body, [grown], [near, far, slope], 10 * work, [cross_near])[0]
+    part = local_call(
+        sum_part_body,
+        [like(q_home, width, f32)],
+        [kept] + [terms[step] for step in range(2, homes, 2)],
+        0,
+        [acc],
+    )[0]
+    pack = local_call(
+        pack_body,
+        [like(2 * qcount + BLOCK + NOTE, width, bf16)],
+        [slope, cross_slope, near, far, cross_near, cross_far],
+        0,
+        [part],
+    )[0]
+    mate = swap(pack, "pb", 1)
+    acc = local_call(
+        add_body, [grown], [cross_near, cross_far, cross_slope, acc], 100 * work, [part]
+    )[0]
+    query_grad, mark = local_call(
+        sum_body,
+        [like(q_home, width, f32), like(1, BLOCK, jnp.int32)],
+        [part] + [terms[step] for step in range(1, homes, 2)],
+        0,
+        [acc],
+    )
+    weight_grad = late(groups, mate, acc, mark)
+    return (query_grad, weight_grad)
+
+
+def pack_body(slope_ref, came_ref, *refs):
+    *rows_refs, out_ref = refs
+    stack_body(*rows_refs, out_ref)
+    start, count = out_ref.shape[0] - slope_ref.shape[0], slope_ref.shape[1]
+    out_ref[start:, :count] = slope_ref[...]
+    out_ref[start:, count : 2 * count] = came_ref[...]
+
+
+def sum_part_body(kept_ref, *refs):
+    *term_refs, out_ref = refs
+    total = kept_ref[...]
+    for ref in term_refs:
+        total = total + ref[...].astype(jnp.float32)
+    out_ref[...] = total
+
+
 def solution(mesh):
+    groups, homes = mesh.shape["pb"], mesh.shape["lab"]
+
+    def shards(queries, label_weights, sibling_blocks, positive_slot):
+        every_row_everywhere = homes == K
+        few = groups * sibling_blocks.shape[0] <= 2 * label_weights.shape[0]
+        paired = groups == 4 and homes & (homes - 1) == 0
+        one_block = label_weights.shape[0] // BLOCK <= K
+        plan = dense_shards if every_row_everywhere and few and paired and one_block else sparse_shards
+        return plan(queries, label_weights, sibling_blocks, positive_slot)
+
     in_specs = (P(("pb", "lab"), None), P("lab", None), P("pb", None), P("pb"))
     out_specs = (P(("pb", "lab"), None), P("lab", None))
     return jax.shard_map(shards, mesh=mesh, in_specs=in_specs, out_specs=out_specs, check_vma=False)

time: 129 us -> 45.7 us (0.35)
  blocking collectives: 33 us -> 0 us
  local copies, waits for them, and re-layouts: 28.9 us -> 2.21 us
  waiting for transfers between devices: 31.8 us -> 7.82 us
  starting transfers between devices: 5.7 us -> 26.6 us
  between operations: 14.2 us -> 0.75 us
  other arithmetic: 11.1 us -> 2.1 us
  Pallas kernels: 0 us -> 5.92 us
  matrix products: 3.7 us -> 0 us
    all_gather x1 -> x0, blocking collectives: 33 us -> none  [shards(): piece = lax.all_gather(queries, 'lab', axis=0, tiled=True)]
    psum x1 -> x0, waiting for transfers between devices: 29.6 us -> none  [shards(): total = lax.psum(w_acc, 'pb')]
    ppermute x0 -> x18, starting transfers between devices: none -> 26.6 us  [swap(): return lax.ppermute(value, axis, [(i, i ^ bit) for i in range(count)])]
    scatter x2 -> x0, local copies, waits for them, and re-layouts: 22.4 us -> none  [pack_index(): jnp.full((homes, width_slots + 1), fill_value, jnp.int32)]
    ppermute x0 -> x18, waiting for transfers between devices: none -> 7.82 us  [swap(): return lax.ppermute(value, axis, [(i, i ^ bit) for i in range(count)])]
    pallas_call x0 -> x11, Pallas kernels: none -> 5.92 us  [the longest x10 4.08 us: local_call(): pl.pallas_call(lambda *refs: body(*refs[:given], *refs[later:]), out_shap...]
    all_to_all x1 -> x0, starting transfers between devices: 5.66 us -> none  [shards(): lax.all_to_all(outgoing, 'lab', split_axis=0, concat_axis=0, tiled=True)]
    gather x3 -> x0, local copies, waits for them, and re-layouts: 4.07 us -> none  [the longest x1 2.28 us: shards(): jnp.take_along_axis(sibling_blocks, (positive_slot // BLOCK)[:, None], ax...]
  transfers between devices with their start and end apart: 2 -> 18, of which waited for: 2 -> 5; matrix products, arithmetic and copies ran while one was open for 25% -> 5% of each run, Pallas kernels for 0% -> 9%
where the time goes in v9:
time: 45.7 us; the launch traced here: 45.4 us
  starting transfers between devices  26.6 us (58%)
  waiting for transfers between devices  7.82 us (17%)
  Pallas kernels  5.92 us (13%)
  local copies, waits for them, and re-layouts  2.21 us (5%)
  other arithmetic  2.1 us (5%)
  between operations  0.75 us (2%)
    ppermute x18, starting transfers between devices, swap(): return lax.ppermute(value, axis, [(i, i ^ bit) for i in range(count)])  26.6 us
    ppermute x18, waiting for transfers between devices, swap(): return lax.ppermute(value, axis, [(i, i ^ bit) for i in range(count)])  7.82 us
    pallas_call x10, Pallas kernels, local_call(): pl.pallas_call(lambda *refs: body(*refs[:given], *refs[later:]), out_shap...  4.08 us
    unnamed x4, local copies, waits for them, and re-layouts  2.2 us
    pallas_call x1, Pallas kernels, late(): pl.pallas_call(lambda set_ref, acc_ref, mark_ref, *refs: late_body(groups...  1.84 us
  transfers between devices with their start and end apart: 18, of which 5 were waited for; matrix products, arithmetic and copies ran while one was open for 5% of the time, Pallas kernels for 9%

profile of v9, /device:TPU:0, one launch (start us, length us, event | category | flops | bytes accessed | tf_op | source)
XLA Modules:
  0.0 45.4 jit_solution(558326122698543734)
XLA Ops:
  0.6 4.0 %collective-permute-start.4 = (bf16[32,768]{1,0:T(8,128)(2,1)}, bf16[32,768]{1,0:T(8,128)(2,1)S(1)}, u32[]{:S(2)}, u32[]{:S(2)}) collective-permute-start(bf16[32,768]{1,0:T(8,128)(2,1)} %refs_0_.1), channel_id=1, source_target_pairs={{0,3},{1,2},{2,1},{3,0},{4,7},{5,6},{6,5},{7,4},{8,11},{9,10},{10,... | collective-permute-start | bytes 147464 | tf_op jit(solution)/shard_map/ppermute | solution.py:77
  5.2 2.5 %collective-permute-start.2 = (bf16[32,768]{1,0:T(8,128)(2,1)}, bf16[32,768]{1,0:T(8,128)(2,1)S(1)}, u32[]{:S(2)}, u32[]{:S(2)}) collective-permute-start(bf16[32,768]{1,0:T(8,128)(2,1)} %refs_0_.1), channel_id=1, source_target_pairs={{0,6},{1,7},{2,4},{3,5},{4,2},{5,3},{6,0},{7,1},{8,14},{9,15},{10,... | collective-permute-start | bytes 147464 | tf_op jit(solution)/shard_map/ppermute | solution.py:77
  7.8 1.8 %collective-permute-start = (bf16[32,768]{1,0:T(8,128)(2,1)}, bf16[32,768]{1,0:T(8,128)(2,1)S(1)}, u32[]{:S(2)}, u32[]{:S(2)}) collective-permute-start(bf16[32,768]{1,0:T(8,128)(2,1)} %refs_0_.1), channel_id=1, source_target_pairs={{0,2},{1,3},{2,0},{3,1},{4,6},{5,7},{6,4},{7,5},{8,10},{9,11},{10,... | collective-permute-start | bytes 147464 | tf_op jit(solution)/shard_map/ppermute | solution.py:77
  9.6 0.7 %and_select_fusion.1 = s32[256]{0:T(256)S(1)} fusion(s32[256]{0:T(256)} %param.7), kind=kLoop, calls=%fused_computation.14 | loop fusion | flops 3840 | bytes 2048 | tf_op jit(solution)/shard_map/jit(floor_divide)/jit(_where)/select_n | solution.py:209
  10.3 0.7 %fusion.3 = (s32[256]{0:T(256)S(1)}, s32[256]{0:T(256)S(1)}) fusion(s32[256,8]{0,1:T(8,128)} %param.6, s32[]{:T(128)S(6)} %mul.3, s32[256]{0:T(256)S(1)} %and_select_fusion.1), kind=kLoop, calls=%fused_computation.8 | loop fusion | flops 17920 | bytes 11268 | tf_op jit(solution)/shard_map/reduce_max | solution.py:207
  11.0 0.8 %copy-done = bf16[32,768]{1,0:T(8,128)(2,1)S(1)} copy-done((bf16[32,768]{1,0:T(8,128)(2,1)S(1)}, bf16[32,768]{1,0:T(8,128)(2,1)}, u32[]{:S(2)}) %copy-start) | copy-done | bytes 49176
  11.8 3.5 %collective-permute-start.6 = (bf16[32,768]{1,0:T(8,128)(2,1)}, bf16[32,768]{1,0:T(8,128)(2,1)S(1)}, u32[]{:S(2)}, u32[]{:S(2)}) collective-permute-start(bf16[32,768]{1,0:T(8,128)(2,1)} %refs_0_.1), channel_id=1, source_target_pairs={{0,7},{1,6},{2,5},{3,4},{4,3},{5,2},{6,1},{7,0},{8,15},{9,14},{10,... | collective-permute-start | bytes 147464 | tf_op jit(solution)/shard_map/ppermute | solution.py:77
  15.3 1.6 %collective-permute-start.10 = (bf16[128,768]{1,0:T(8,128)(2,1)S(1)}, bf16[128,768]{1,0:T(8,128)(2,1)S(1)}, u32[]{:S(2)}, u32[]{:S(2)}) collective-permute-start(bf16[128,768]{1,0:T(8,128)(2,1)S(1)} %shard_map.60.refs_4_.refs_0_.refs_2_), channel_id=1, source_target_pairs={{0,16},{8,24},{16,0},{24,8},{1,17},{9,25},{17,1},{25,9},{2,18},{10... | collective-permute-start | bytes 589832 | tf_op jit(solution)/shard_map/ppermute | solution.py:77
  16.9 0.7 %fusion.7 = (bf16[256]{0:T(256)(128)(2,1)S(1)}, bf16[256]{0:T(256)(128)(2,1)S(1)}) fusion(s32[256]{0:T(256)S(1)} %get-tuple-element.24, s32[256]{0:T(256)} %param.7, s32[256]{0:T(256)S(1)} %get-tuple-element.25), kind=kLoop, calls=%fused_computation.21 | loop fusion | flops 3840 | bytes 4096 | tf_op jit(solution)/shard_map/convert.3
  17.8 1.2 %collective-permute-done.6.refs_3_ = bf16[32,768]{1,0:T(8,128)(2,1)S(1)} collective-permute-done((bf16[32,768]{1,0:T(8,128)(2,1)}, bf16[32,768]{1,0:T(8,128)(2,1)S(1)}, u32[]{:S(2)}, u32[]{:S(2)}) %collective-permute-start.6) | collective-permute-done | bytes 49184 | tf_op jit(solution)/shard_map/ppermute | solution.py:77
  18.9 2.4 %collective-permute-done.5.refs_2_ = bf16[32,768]{1,0:T(8,128)(2,1)S(1)} collective-permute-done((bf16[32,768]{1,0:T(8,128)(2,1)}, bf16[32,768]{1,0:T(8,128)(2,1)S(1)}, u32[]{:S(2)}, u32[]{:S(2)}) %collective-permute-start.5) | collective-permute-done | bytes 49184 | tf_op jit(solution)/shard_map/ppermute | solution.py:77
  21.4 1.6 %collective-permute-start.15 = (bf16[128,768]{1,0:T(8,128)(2,1)S(1)}, bf16[128,768]{1,0:T(8,128)(2,1)S(1)}, u32[]{:S(2)}, u32[]{:S(2)}) collective-permute-start(bf16[128,768]{1,0:T(8,128)(2,1)S(1)} %shard_map.61.refs_1_.refs_3_), channel_id=1, source_target_pairs={{0,16},{8,24},{16,0},{24,8},{1,17},{9,25},{17,1},{25,9},{2,18},{10... | collective-permute-start | bytes 589832 | tf_op jit(solution)/shard_map/ppermute | solution.py:77
  23.0 1.4 %copy-done.1 = bf16[1024,768]{1,0:T(8,128)(2,1)S(1)} copy-done((bf16[1024,768]{1,0:T(8,128)(2,1)S(1)}, bf16[1024,768]{1,0:T(8,128)(2,1)}, u32[]{:S(2)}) %copy-start.1) | copy-done | bytes 1572888
  24.4 2.0 %shard_map.63 = (f32[32,768]{1,0:T(8,128)S(1)}, bf16[144,256]{1,0:T(8,128)(2,1)S(1)}, bf16[32,768]{1,0:T(8,128)(2,1)S(1)}, bf16[32,768]{1,0:T(8,128)(2,1)S(1)}, ...) custom-call(bf16[128,768]{1,0:T(8,128)(2,1)S(1)} %shard_map.60.refs_, ...), custom_call_target="tpu_custom_call" | custom-call | flops 805306368 | tf_op jit(solution)/shard_map/pallas_call | solution.py:86
  26.4 1.9 %collective-permute-start.8 = (bf16[32,768]{1,0:T(8,128)(2,1)S(1)}, bf16[32,768]{1,0:T(8,128)(2,1)S(1)}, u32[]{:S(2)}, u32[]{:S(2)}) collective-permute-start(bf16[32,768]{1,0:T(8,128)(2,1)S(1)} %get-tuple-element.15), channel_id=1, source_target_pairs={{0,4},{1,5},{2,6},{3,7},{4,0},{5,1},{6,2},{7,3},{8,12},{9,13},{10,... | collective-permute-start | bytes 147464 | tf_op jit(solution)/shard_map/ppermute | solution.py:77
  28.3 2.5 %collective-permute-start.9 = (bf16[32,768]{1,0:T(8,128)(2,1)S(1)}, bf16[32,768]{1,0:T(8,128)(2,1)S(1)}, u32[]{:S(2)}, u32[]{:S(2)}) collective-permute-start(bf16[32,768]{1,0:T(8,128)(2,1)S(1)} %get-tuple-element.16), channel_id=1, source_target_pairs={{0,6},{1,7},{2,4},{3,5},{4,2},{5,3},{6,0},{7,1},{8,14},{9,15},{10,... | collective-permute-start | bytes 147464 | tf_op jit(solution)/shard_map/ppermute | solution.py:77
  32.5 1.2 %collective-permute-start.12 = (bf16[32,768]{1,0:T(8,128)(2,1)S(1)}, bf16[32,768]{1,0:T(8,128)(2,1)S(1)}, u32[]{:S(2)}, u32[]{:S(2)}) collective-permute-start(bf16[32,768]{1,0:T(8,128)(2,1)S(1)} %get-tuple-element.19), channel_id=1, source_target_pairs={{0,3},{1,2},{2,1},{3,0},{4,7},{5,6},{6,5},{7,4},{8,11},{9,10},{10,... | collective-permute-start | bytes 147464 | tf_op jit(solution)/shard_map/ppermute | solution.py:77
  33.7 0.9 %collective-permute-done.9.refs_3_ = bf16[32,768]{1,0:T(8,128)(2,1)S(1)} collective-permute-done((bf16[32,768]{1,0:T(8,128)(2,1)S(1)}, bf16[32,768]{1,0:T(8,128)(2,1)S(1)}, u32[]{:S(2)}, u32[]{:S(2)}) %collective-permute-start.9) | collective-permute-done | bytes 49184 | tf_op jit(solution)/shard_map/ppermute | solution.py:77
  34.6 1.4 %collective-permute-start.13 = (bf16[32,768]{1,0:T(8,128)(2,1)S(1)}, bf16[32,768]{1,0:T(8,128)(2,1)S(1)}, u32[]{:S(2)}, u32[]{:S(2)}) collective-permute-start(bf16[32,768]{1,0:T(8,128)(2,1)S(1)} %get-tuple-element.20), channel_id=1, source_target_pairs={{0,5},{1,4},{2,7},{3,6},{4,1},{5,0},{6,3},{7,2},{8,13},{9,12},{10,... | collective-permute-start | bytes 147464 | tf_op jit(solution)/shard_map/ppermute | solution.py:77
  36.0 2.8 %collective-permute-start.14 = (bf16[32,768]{1,0:T(8,128)(2,1)S(1)}, bf16[32,768]{1,0:T(8,128)(2,1)S(1)}, u32[]{:S(2)}, u32[]{:S(2)}) collective-permute-start(bf16[32,768]{1,0:T(8,128)(2,1)S(1)} %get-tuple-element.21), channel_id=1, source_target_pairs={{0,7},{1,6},{2,5},{3,4},{4,3},{5,2},{6,1},{7,0},{8,15},{9,14},{10,... | collective-permute-start | bytes 147464 | tf_op jit(solution)/shard_map/ppermute | solution.py:77
  39.6 1.4 %collective-permute-done.13.refs_3_ = bf16[32,768]{1,0:T(8,128)(2,1)S(1)} collective-permute-done((bf16[32,768]{1,0:T(8,128)(2,1)S(1)}, bf16[32,768]{1,0:T(8,128)(2,1)S(1)}, u32[]{:S(2)}, u32[]{:S(2)}) %collective-permute-start.13) | collective-permute-done | bytes 49184 | tf_op jit(solution)/shard_map/ppermute | solution.py:77
  41.0 1.8 %collective-permute-done.14.refs_4_ = bf16[32,768]{1,0:T(8,128)(2,1)S(1)} collective-permute-done((bf16[32,768]{1,0:T(8,128)(2,1)S(1)}, bf16[32,768]{1,0:T(8,128)(2,1)S(1)}, u32[]{:S(2)}, u32[]{:S(2)}) %collective-permute-start.14) | collective-permute-done | bytes 49184 | tf_op jit(solution)/shard_map/ppermute | solution.py:77
  42.9 0.7 %shard_map.67 = (f32[32,768]{1,0:T(8,128)}, s32[1,128]{1,0:T(1,128)S(1)}) custom-call(f32[32,768]{1,0:T(8,128)S(1)} %shard_map.65.refs_4_.refs_0_.refs_6_, bf16[32,768]{1,0:T(8,128)(2,1)S(1)} %collective-permute-done.11.refs_1_, bf16[32,768]{1,0:T(8,128)(2,1)S(1)} %collective-permute-done.12.refs_2_, bf16[32,768]{1,0:T(8,128)(2,1)S(1)} %collective-permute-done.13.refs_3_, ...), custom_call_target="tpu_custom_call" | custom-call | tf_op jit(solution)/shard_map/pallas_call | solution.py:86
  43.5 1.8 %shard_map.69 = bf16[1024,768]{1,0:T(8,128)(2,1)} custom-call(bf16[656,768]{1,0:T(8,128)(2,1)S(1)} %collective-permute-done.17.set_ref, f32[1024,768]{1,0:T(8,128)S(1)} %shard_map.66.refs_5_.acc_ref, s32[1,128]{1,0:T(1,128)S(1)} %get-tuple-element.23.mark_ref), custom_call_target="tpu_custom_call" | custom-call | tf_op jit(solution)/shard_map/pallas_call | solution.py:183
  (33 shorter events, 3.4 us)
Async XLA Ops:
  0.6 17.1 %collective-permute-start.4 = (bf16[32,768]{1,0:T(8,128)(2,1)}, bf16[32,768]{1,0:T(8,128)(2,1)S(1)}, u32[]{:S(2)}, u32[]{:S(2)}) collective-permute-start(bf16[32,768]{1,0:T(8,128)(2,1)} %refs_0_.1), channel_id=1, source_target_pairs={{0,3},{1,2},{2,1},{3,0},{4,7},{5,6},{6,5},{7,4},{8,11},{9,10},{10,... | collective-permute-start | bytes 147464 | tf_op jit(solution)/shard_map/ppermute | solution.py:77
  4.7 13.1 %collective-permute-start.3 = (bf16[32,768]{1,0:T(8,128)(2,1)}, bf16[32,768]{1,0:T(8,128)(2,1)S(1)}, u32[]{:S(2)}, u32[]{:S(2)}) collective-permute-start(bf16[32,768]{1,0:T(8,128)(2,1)} %refs_0_.1), channel_id=1, source_target_pairs={{0,1},{1,0},{2,3},{3,2},{4,5},{5,4},{6,7},{7,6},{8,9},{9,8},{10,11... | collective-permute-start | bytes 147464 | tf_op jit(solution)/shard_map/ppermute | solution.py:77
  5.2 6.6 %collective-permute-start.2 = (bf16[32,768]{1,0:T(8,128)(2,1)}, bf16[32,768]{1,0:T(8,128)(2,1)S(1)}, u32[]{:S(2)}, u32[]{:S(2)}) collective-permute-start(bf16[32,768]{1,0:T(8,128)(2,1)} %refs_0_.1), channel_id=1, source_target_pairs={{0,6},{1,7},{2,4},{3,5},{4,2},{5,3},{6,0},{7,1},{8,14},{9,15},{10,... | collective-permute-start | bytes 147464 | tf_op jit(solution)/shard_map/ppermute | solution.py:77
  7.7 7.6 %collective-permute-start.1 = (bf16[32,768]{1,0:T(8,128)(2,1)}, bf16[32,768]{1,0:T(8,128)(2,1)S(1)}, u32[]{:S(2)}, u32[]{:S(2)}) collective-permute-start(bf16[32,768]{1,0:T(8,128)(2,1)} %refs_0_.1), channel_id=1, source_target_pairs={{0,4},{1,5},{2,6},{3,7},{4,0},{5,1},{6,2},{7,3},{8,12},{9,13},{10,... | collective-permute-start | bytes 147464 | tf_op jit(solution)/shard_map/ppermute | solution.py:77
  7.8 7.5 %collective-permute-start = (bf16[32,768]{1,0:T(8,128)(2,1)}, bf16[32,768]{1,0:T(8,128)(2,1)S(1)}, u32[]{:S(2)}, u32[]{:S(2)}) collective-permute-start(bf16[32,768]{1,0:T(8,128)(2,1)} %refs_0_.1), channel_id=1, source_target_pairs={{0,2},{1,3},{2,0},{3,1},{4,6},{5,7},{6,4},{7,5},{8,10},{9,11},{10,... | collective-permute-start | bytes 147464 | tf_op jit(solution)/shard_map/ppermute | solution.py:77
  11.0 0.8 %copy-start = (bf16[32,768]{1,0:T(8,128)(2,1)S(1)}, bf16[32,768]{1,0:T(8,128)(2,1)}, u32[]{:S(2)}) copy-start(bf16[32,768]{1,0:T(8,128)(2,1)} %refs_0_.1) | copy-start | bytes 147460
  11.8 7.2 %collective-permute-start.6 = (bf16[32,768]{1,0:T(8,128)(2,1)}, bf16[32,768]{1,0:T(8,128)(2,1)S(1)}, u32[]{:S(2)}, u32[]{:S(2)}) collective-permute-start(bf16[32,768]{1,0:T(8,128)(2,1)} %refs_0_.1), channel_id=1, source_target_pairs={{0,7},{1,6},{2,5},{3,4},{4,3},{5,2},{6,1},{7,0},{8,15},{9,14},{10,... | collective-permute-start | bytes 147464 | tf_op jit(solution)/shard_map/ppermute | solution.py:77
  15.3 6.1 %collective-permute-start.5 = (bf16[32,768]{1,0:T(8,128)(2,1)}, bf16[32,768]{1,0:T(8,128)(2,1)S(1)}, u32[]{:S(2)}, u32[]{:S(2)}) collective-permute-start(bf16[32,768]{1,0:T(8,128)(2,1)} %refs_0_.1), channel_id=1, source_target_pairs={{0,5},{1,4},{2,7},{3,6},{4,1},{5,0},{6,3},{7,2},{8,13},{9,12},{10,... | collective-permute-start | bytes 147464 | tf_op jit(solution)/shard_map/ppermute | solution.py:77
  15.3 15.5 %collective-permute-start.10 = (bf16[128,768]{1,0:T(8,128)(2,1)S(1)}, bf16[128,768]{1,0:T(8,128)(2,1)S(1)}, u32[]{:S(2)}, u32[]{:S(2)}) collective-permute-start(bf16[128,768]{1,0:T(8,128)(2,1)S(1)} %shard_map.60.refs_4_.refs_0_.refs_2_), channel_id=1, source_target_pairs={{0,16},{8,24},{16,0},{24,8},{1,17},{9,25},{17,1},{25,9},{2,18},{10... | collective-permute-start | bytes 589832 | tf_op jit(solution)/shard_map/ppermute | solution.py:77
  21.4 17.5 %collective-permute-start.15 = (bf16[128,768]{1,0:T(8,128)(2,1)S(1)}, bf16[128,768]{1,0:T(8,128)(2,1)S(1)}, u32[]{:S(2)}, u32[]{:S(2)}) collective-permute-start(bf16[128,768]{1,0:T(8,128)(2,1)S(1)} %shard_map.61.refs_1_.refs_3_), channel_id=1, source_target_pairs={{0,16},{8,24},{16,0},{24,8},{1,17},{9,25},{17,1},{25,9},{2,18},{10... | collective-permute-start | bytes 589832 | tf_op jit(solution)/shard_map/ppermute | solution.py:77
  23.0 1.4 %copy-start.1 = (bf16[1024,768]{1,0:T(8,128)(2,1)S(1)}, bf16[1024,768]{1,0:T(8,128)(2,1)}, u32[]{:S(2)}) copy-start(bf16[1024,768]{1,0:T(8,128)(2,1)} %refs_2_.1) | copy-start | bytes 4718596
  26.3 5.6 %collective-permute-start.7 = (bf16[32,768]{1,0:T(8,128)(2,1)S(1)}, bf16[32,768]{1,0:T(8,128)(2,1)S(1)}, u32[]{:S(2)}, u32[]{:S(2)}) collective-permute-start(bf16[32,768]{1,0:T(8,128)(2,1)S(1)} %get-tuple-element.14), channel_id=1, source_target_pairs={{0,2},{1,3},{2,0},{3,1},{4,6},{5,7},{6,4},{7,5},{8,10},{9,11},{10,... | collective-permute-start | bytes 147464 | tf_op jit(solution)/shard_map/ppermute | solution.py:77
  26.4 6.0 %collective-permute-start.8 = (bf16[32,768]{1,0:T(8,128)(2,1)S(1)}, bf16[32,768]{1,0:T(8,128)(2,1)S(1)}, u32[]{:S(2)}, u32[]{:S(2)}) collective-permute-start(bf16[32,768]{1,0:T(8,128)(2,1)S(1)} %get-tuple-element.15), channel_id=1, source_target_pairs={{0,4},{1,5},{2,6},{3,7},{4,0},{5,1},{6,2},{7,3},{8,12},{9,13},{10,... | collective-permute-start | bytes 147464 | tf_op jit(solution)/shard_map/ppermute | solution.py:77
  28.3 6.3 %collective-permute-start.9 = (bf16[32,768]{1,0:T(8,128)(2,1)S(1)}, bf16[32,768]{1,0:T(8,128)(2,1)S(1)}, u32[]{:S(2)}, u32[]{:S(2)}) collective-permute-start(bf16[32,768]{1,0:T(8,128)(2,1)S(1)} %get-tuple-element.16), channel_id=1, source_target_pairs={{0,6},{1,7},{2,4},{3,5},{4,2},{5,3},{6,0},{7,1},{8,14},{9,15},{10,... | collective-permute-start | bytes 147464 | tf_op jit(solution)/shard_map/ppermute | solution.py:77
  30.8 5.2 %collective-permute-start.16 = (bf16[144,256]{1,0:T(8,128)(2,1)S(1)}, bf16[144,256]{1,0:T(8,128)(2,1)S(1)}, u32[]{:S(2)}, u32[]{:S(2)}) collective-permute-start(bf16[144,256]{1,0:T(8,128)(2,1)S(1)} %get-tuple-element.17.refs_2_.refs_0_), channel_id=1, source_target_pairs={{0,16},{8,24},{16,0},{24,8},{1,17},{9,25},{17,1},{25,9},{2,18},{10... | collective-permute-start | bytes 221192 | tf_op jit(solution)/shard_map/ppermute | solution.py:77
  31.9 7.7 %collective-permute-start.11 = (bf16[32,768]{1,0:T(8,128)(2,1)S(1)}, bf16[32,768]{1,0:T(8,128)(2,1)S(1)}, u32[]{:S(2)}, u32[]{:S(2)}) collective-permute-start(bf16[32,768]{1,0:T(8,128)(2,1)S(1)} %get-tuple-element.18), channel_id=1, source_target_pairs={{0,1},{1,0},{2,3},{3,2},{4,5},{5,4},{6,7},{7,6},{8,9},{9,8},{10,11... | collective-permute-start | bytes 147464 | tf_op jit(solution)/shard_map/ppermute | solution.py:77
  32.5 7.1 %collective-permute-start.12 = (bf16[32,768]{1,0:T(8,128)(2,1)S(1)}, bf16[32,768]{1,0:T(8,128)(2,1)S(1)}, u32[]{:S(2)}, u32[]{:S(2)}) collective-permute-start(bf16[32,768]{1,0:T(8,128)(2,1)S(1)} %get-tuple-element.19), channel_id=1, source_target_pairs={{0,3},{1,2},{2,1},{3,0},{4,7},{5,6},{6,5},{7,4},{8,11},{9,10},{10,... | collective-permute-start | bytes 147464 | tf_op jit(solution)/shard_map/ppermute | solution.py:77
  34.6 6.4 %collective-permute-start.13 = (bf16[32,768]{1,0:T(8,128)(2,1)S(1)}, bf16[32,768]{1,0:T(8,128)(2,1)S(1)}, u32[]{:S(2)}, u32[]{:S(2)}) collective-permute-start(bf16[32,768]{1,0:T(8,128)(2,1)S(1)} %get-tuple-element.20), channel_id=1, source_target_pairs={{0,5},{1,4},{2,7},{3,6},{4,1},{5,0},{6,3},{7,2},{8,13},{9,12},{10,... | collective-permute-start | bytes 147464 | tf_op jit(solution)/shard_map/ppermute | solution.py:77
  36.0 6.9 %collective-permute-start.14 = (bf16[32,768]{1,0:T(8,128)(2,1)S(1)}, bf16[32,768]{1,0:T(8,128)(2,1)S(1)}, u32[]{:S(2)}, u32[]{:S(2)}) collective-permute-start(bf16[32,768]{1,0:T(8,128)(2,1)S(1)} %get-tuple-element.21), channel_id=1, source_target_pairs={{0,7},{1,6},{2,5},{3,4},{4,3},{5,2},{6,1},{7,0},{8,15},{9,14},{10,... | collective-permute-start | bytes 147464 | tf_op jit(solution)/shard_map/ppermute | solution.py:77
  38.9 4.6 %collective-permute-start.17 = (bf16[656,768]{1,0:T(8,128)(2,1)S(1)}, bf16[656,768]{1,0:T(8,128)(2,1)S(1)}, u32[]{:S(2)}, u32[]{:S(2)}) collective-permute-start(bf16[656,768]{1,0:T(8,128)(2,1)S(1)} %shard_map.68), channel_id=1, source_target_pairs={{0,8},{8,0},{16,24},{24,16},{1,9},{9,1},{17,25},{25,17},{2,10},{10... | collective-permute-start | bytes 3022856 | tf_op jit(solution)/shard_map/ppermute | solution.py:77

commit v10 on v7

--- a/solution.py
+++ b/solution.py
@@ -122,18 +122,21 @@
     held_ref[...] = rows_ref[...]
 
 
-def slope_of(rows, weights_ref, chosen, place):
-    count = rows.shape[0]
-    blocks = weights_ref.shape[0] // BLOCK
+def slope_of(rows, weights, chosen, place):
+    count, blocks = rows.shape[0], weights.shape[0] // BLOCK
     scores = lax.dot_general(
-        weights_ref[...], rows, (((1,), (1,)), ((), ())), preferred_element_type=jnp.float32
+        weights, rows, (((1,), (1,)), ((), ())), preferred_element_type=jnp.float32
     )
     named = jnp.zeros((BLOCK, count), jnp.float32)
     for block in range(blocks):
         named = jnp.where(chosen == block, scores[block * BLOCK : (block + 1) * BLOCK], named)
     ids = lax.broadcasted_iota(jnp.int32, (BLOCK, count), 0)
-    slope = jax.nn.sigmoid(named) - jnp.where(ids == place, 1.0, 0.0)
-    parts = [jnp.where(chosen == block, slope, 0.0).astype(jnp.bfloat16) for block in range(blocks)]
+    return (jax.nn.sigmoid(named) - jnp.where(ids == place, 1.0, 0.0)).astype(jnp.bfloat16)
+
+
+def spread(slope, chosen, blocks):
+    wide = slope.astype(jnp.float32)
+    parts = [jnp.where(chosen == block, wide, 0.0).astype(slope.dtype) for block in blocks]
     return jnp.concatenate(parts, axis=0)
 
 
@@ -144,37 +147,37 @@
 
 
 def grad_body(which, rows_ref, weights_ref, note_ref, dq_ref, slope_ref):
-    rows = rows_ref[...]
+    rows, weights = rows_ref[...], weights_ref[...]
     note = note_ref[...].astype(jnp.float32)
-    slope = slope_of(rows, weights_ref, *read_note(note, which, rows.shape[0]))
-    slope_ref[...] = slope
+    chosen, place = read_note(note, which, rows.shape[0])
+    slope = slope_of(rows, weights, chosen, place)
+    slope_ref[:BLOCK, :] = slope
+    slope_ref[BLOCK:, :] = jnp.broadcast_to(chosen, (NOTE, rows.shape[0])).astype(slope.dtype)
     dq = lax.dot_general(
-        slope, weights_ref[...], (((0,), (0,)), ((), ())), preferred_element_type=jnp.float32
+        spread(slope, chosen, range(weights.shape[0] // BLOCK)),
+        weights,
+        (((0,), (0,)), ((), ())),
+        preferred_element_type=jnp.float32,
     )
     dq_ref[...] = dq.astype(dq_ref.dtype)
 
 
-def near_body(rows_ref, weights_ref, note_ref, dq_ref, slope_ref, held_ref):
+def near_body(rows_ref, weights_ref, note_ref, dq_ref, slope_ref, held_ref, copy_ref):
     held_ref[...] = weights_ref[...]
+    copy_ref[...] = rows_ref[...]
     grad_body(0, rows_ref, weights_ref, note_ref, dq_ref, slope_ref)
 
 
-def far_body(side_ref, rows_ref, weights_ref, note_ref, near_ref, dq_ref, slope_ref):
-    rows = rows_ref[...]
-    half = rows.shape[0]
-    planes, homes, q_home = 2, dq_ref.shape[0], dq_ref.shape[1]
-    side = side_ref[0]
-    note = note_ref[...].astype(jnp.float32)
-    slope = slope_of(rows, weights_ref, *read_note(note, 1, half))
-    slope_ref[...] = slope
-    far = lax.dot_general(
-        slope, weights_ref[...], (((0,), (0,)), ((), ())), preferred_element_type=jnp.float32
-    ).astype(dq_ref.dtype)
-    near = near_ref[...]
-    for z in range(homes // planes):
+def far_body(rows_ref, weights_ref, note_ref, dq_ref, slope_ref):
+    grad_body(1, rows_ref, weights_ref, note_ref, dq_ref, slope_ref)
+
+
+def order_body(side_ref, near_ref, far_ref, out_ref):
+    side, q_home = side_ref[0], out_ref.shape[1]
+    for z in range(out_ref.shape[0] // 2):
         part = slice(z * q_home, (z + 1) * q_home)
-        dq_ref[planes * z + side] = near[part, :]
-        dq_ref[planes * z + 1 - side] = far[part, :]
+        out_ref[2 * z + side] = near_ref[part, :]
+        out_ref[2 * z + 1 - side] = far_ref[part, :]
 
 
 def sum_body(terms_ref, out_ref):
@@ -184,57 +187,84 @@
     out_ref[...] = total
 
 
-def slopes_of_set(near_rows, far_rows, note, weights_ref):
-    half = near_rows.shape[0]
-    rows = jnp.concatenate([near_rows, far_rows], axis=0)
+def stack_body(*refs):
+    *came_refs, out_ref = refs
+    start = 0
+    for ref in came_refs:
+        out_ref[start : start + ref.shape[0], : ref.shape[1]] = ref[...]
+        start += ref.shape[0]
+
+
+def read_slope(slope):
+    chosen = slope[BLOCK : BLOCK + 1].astype(jnp.float32).astype(jnp.int32)
+    return slope[:BLOCK], chosen
+
+
+def own_body(near_ref, far_ref, near_slope_ref, far_slope_ref, acc_ref, set_ref):
+    rows = jnp.concatenate([near_ref[...], far_ref[...]], axis=0)
+    slope = jnp.concatenate([near_slope_ref[...], far_slope_ref[...]], axis=1)
+    count = rows.shape[0]
+    set_ref[:count, :] = rows
+    set_ref[count:, :count] = slope
+    wide = spread(*read_slope(slope), range(acc_ref.shape[0] // BLOCK))
+    acc_ref[...] = jnp.dot(wide, rows, preferred_element_type=jnp.float32)
+
+
+def mate_body(set_ref, acc_ref, out_ref):
+    count = set_ref.shape[0] - BLOCK - NOTE
+    slope, chosen = read_slope(set_ref[count:, :count])
+    wide = spread(slope, chosen, range(acc_ref.shape[0] // BLOCK))
+    out_ref[...] = acc_ref[...] + jnp.dot(
+        wide, set_ref[:count, :], preferred_element_type=jnp.float32
+    )
+
+
+def set_slope(set_ref, weights):
+    half = (set_ref.shape[0] - NOTE) // 2
+    rows = jnp.concatenate([set_ref[:half, :], set_ref[half + NOTE :, :]], axis=0)
+    note = set_ref[half : half + NOTE, :].astype(jnp.float32)
     codes = [read_note(note, which, half) for which in range(2)]
     chosen = jnp.concatenate([codes[0][0], codes[1][0]], axis=1)
     place = jnp.concatenate([codes[0][1], codes[1][1]], axis=1)
-    return rows, slope_of(rows, weights_ref, chosen, place)
-
-
-def own_body(near_ref, far_ref, near_slope_ref, far_slope_ref, noted_ref, acc_ref, whole_ref):
-    noted = noted_ref.shape[0]
-    whole_ref[:noted, :] = noted_ref[...]
-    whole_ref[noted:, :] = far_ref[...]
-    rows = jnp.concatenate([near_ref[...], far_ref[...]], axis=0)
-    slope = jnp.concatenate([near_slope_ref[...], far_slope_ref[...]], axis=1)
-    acc_ref[...] = jnp.dot(slope, rows, preferred_element_type=jnp.float32)
-
-
-def split_set(set_ref):
-    half = (set_ref.shape[0] - NOTE) // 2
-    return set_ref[:half, :], set_ref[half + NOTE :, :], set_ref[half : half + NOTE, :]
-
-
-def pack_body(near_ref, far_ref, out_ref):
-    noted = near_ref.shape[0]
-    out_ref[:noted, :] = near_ref[...]
-    out_ref[noted:, :] = far_ref[...]
-
-
-def add_sets(acc_ref, weights_ref, set_refs):
-    rows, slopes = [], []
-    for set_ref in set_refs:
-        near, far, note = split_set(set_ref)
-        part, slope = slopes_of_set(near, far, note.astype(jnp.float32), weights_ref)
-        rows.append(part)
-        slopes.append(slope)
-    return acc_ref[...] + jnp.dot(
-        jnp.concatenate(slopes, axis=1),
-        jnp.concatenate(rows, axis=0),
-        preferred_element_type=jnp.float32,
-    )
-
-
-def mate_body(set_ref, weights_ref, acc_ref, out_ref):
-    out_ref[...] = add_sets(acc_ref, weights_ref, [set_ref])
-
-
-def late_body(groups, one_ref, two_ref, weights_ref, acc_ref, out_ref, mark_ref):
+    return rows, slope_of(rows, weights, chosen, place), chosen
+
+
+def cross_body(set_ref, weights_ref, acc_ref, out_ref):
+    rows, slope, chosen = set_slope(set_ref, weights_ref[...])
+    wide = spread(slope, chosen, range(acc_ref.shape[0] // BLOCK))
+    out_ref[...] = acc_ref[...] + jnp.dot(wide, rows, preferred_element_type=jnp.float32)
+
+
+def late_body(groups, set_ref, weights_ref, acc_ref, out_ref, mark_ref, held, sems):
     mark_ref[...] = jnp.zeros_like(mark_ref)
-    total = add_sets(acc_ref, weights_ref, [one_ref, two_ref])
-    out_ref[...] = (total / groups).astype(out_ref.dtype)
+    rows, slope, chosen = set_slope(set_ref, weights_ref[...])
+    blocks = acc_ref.shape[0] // BLOCK
+    chunk = blocks // sems.shape[0]
+    copies = []
+    for part in range(sems.shape[0]):
+        here = pl.ds(part * chunk * BLOCK, chunk * BLOCK)
+        wide = spread(slope, chosen, range(part * chunk, (part + 1) * chunk))
+        total = acc_ref[here, :] + jnp.dot(wide, rows, preferred_element_type=jnp.float32)
+        held[here, :] = (total / groups).astype(held.dtype)
+        copy = pltpu.make_async_copy(held.at[here, :], out_ref.at[here, :], sems.at[part])
+        copy.start()
+        copies.append(copy)
+    for copy in copies:
+        copy.wait()
+
+
+def late(groups, crossed, weights, acc):
+    out = like(*weights.shape, weights.dtype)
+    chunks = 4
+    return pl.pallas_call(
+        lambda *refs: late_body(groups, *refs),
+        out_shape=[out, like(1, BLOCK, jnp.int32)],
+        in_specs=[pl.BlockSpec(memory_space=pltpu.VMEM)] * 3,
+        out_specs=[pl.BlockSpec(memory_space=pl.ANY), pl.BlockSpec(memory_space=pltpu.VMEM)],
+        scratch_shapes=[pltpu.VMEM(out.shape, out.dtype), pltpu.SemaphoreType.DMA((chunks,))],
+        cost_estimate=pl.CostEstimate(flops=0, bytes_accessed=0, transcendentals=0),
+        compiler_params=pltpu.CompilerParams(vmem_limit_bytes=VMEM_LIMIT),
+    )(crossed, weights, acc)
 
 
 def make_note(sibling_blocks, positive_slot, blocks_dev, homes, width):
@@ -274,42 +304,42 @@
     )
     far = swap(near, "lab", 1)
     work = 4 * half * lab_dev * width
-    near_dq, near_slope, weights = local_call(
+    slope_like = like(BLOCK + NOTE, half, bf16)
+    near_dq, near_slope, weights, near_copy = local_call(
         near_body,
-        [like(half, width, bf16), like(lab_dev, half, bf16), like(lab_dev, width, bf16)],
+        [like(half, width, bf16), slope_like, like(lab_dev, width, bf16), like(half, width, bf16)],
         [near, label_weights, note],
         work,
     )
     cross_near = swap(noted, "pb", far_bit)
-    cross_far = diagonal(near, far_bit, 1)
-    dq, far_slope = local_call(
+    cross_far = diagonal(near_copy, far_bit, 1)
+    far_dq, far_slope = local_call(
         far_body,
-        [jax.ShapeDtypeStruct((homes, q_home, width), bf16), like(lab_dev, half, bf16)],
-        [side, far, weights, note, near_dq],
+        [like(half, width, bf16), slope_like],
+        [far, weights, note],
         work,
-    )
+        [near_dq],
+    )
+    dq = local_call(
+        order_body, [jax.ShapeDtypeStruct((homes, q_home, width), bf16)], [side, near_dq, far_dq]
+    )[0]
     terms = lax.all_to_all(dq, "lab", split_axis=0, concat_axis=0, tiled=True)
-    acc, whole = local_call(
+    acc, own = local_call(
         own_body,
-        [like(lab_dev, width, f32), like(qcount + NOTE, width, bf16)],
-        [near, far, near_slope, far_slope, noted],
+        [like(lab_dev, width, f32), like(qcount + BLOCK + NOTE, width, bf16)],
+        [near, far, near_slope, far_slope],
         work,
-        [],
-    )
-    mate = swap(whole, "pb", 1)
+        [dq],
+    )
+    mate = swap(own, "pb", 1)
     cross = local_call(
-        pack_body, [like(qcount + NOTE, width, bf16)], [cross_near, cross_far], 0, [acc]
+        stack_body, [like(qcount + NOTE, width, bf16)], [cross_near, cross_far], 0, [acc]
     )[0]
     cross_mate = swap(cross, "pb", 1)
-    acc = local_call(
-        mate_body, [like(lab_dev, width, f32)], [mate, weights, acc], 2 * work, [cross]
-    )[0]
-    weight_grad, mark = local_call(
-        lambda *refs: late_body(groups, *refs),
-        [like(lab_dev, width, bf16), like(1, BLOCK, jnp.int32)],
-        [cross, cross_mate, weights, acc],
-        4 * work,
-    )
+    grown = like(lab_dev, width, f32)
+    acc = local_call(mate_body, [grown], [mate, acc], work, [cross])[0]
+    acc = local_call(cross_body, [grown], [cross, weights, acc], 2 * work)[0]
+    weight_grad, mark = late(groups, cross_mate, weights, acc)
     query_grad = local_call(sum_body, [like(q_home, width, f32)], [terms], 0, [mark])[0]
     return (query_grad, weight_grad)
 

time: 35.9 us -> 48.6 us (1.35)
  waiting for transfers between devices: 6.84 us -> 15 us
  local copies, waits for them, and re-layouts: 2.47 us -> 6.02 us
  starting transfers between devices: 13.3 us -> 14.2 us
    ppermute x1, waiting for transfers between devices: 0.01 us -> 10.8 us  [diagonal(): return lax.ppermute(value, ('pb', 'lab'), pairs)]
    unnamed x4 -> x10, local copies, waits for them, and re-layouts: 2.21 us -> 5.76 us
    pallas_call x9 -> x10, Pallas kernels: 10.1 us -> 7.34 us  [local_call(): pl.pallas_call(lambda *refs: body(*refs[:given], *refs[later:]), out_shap...]
    pallas_call x0 -> x1, Pallas kernels: none -> 2.71 us  [late(): pl.pallas_call(lambda *refs: late_body(groups, *refs), out_shape=[out, li...]
    all_to_all x1, waiting for transfers between devices: 1.45 us -> 0.01 us  [dense_shards(): terms = lax.all_to_all(dq, 'lab', split_axis=0, concat_axis=0, tiled=True)]
    ppermute x1, starting transfers between devices: 0.48 us -> 1.82 us  [diagonal(): return lax.ppermute(value, ('pb', 'lab'), pairs)]
    ppermute x7, waiting for transfers between devices: 5.39 us -> 4.19 us  [swap(): return lax.ppermute(value, axis, [(i, i ^ bit) for i in range(count)])]
  transfers between devices with their start and end apart: 9 -> 9, of which waited for: 5 -> 4; matrix products, arithmetic and copies ran while one was open for 7% -> 5% of each run, Pallas kernels for 26% -> 14%
where the time goes in v10:
time: 48.6 us; the launch traced here: 48.1 us
  waiting for transfers between devices  15 us (31%)
  starting transfers between devices  14.2 us (29%)
  Pallas kernels  10 us (21%)
  local copies, waits for them, and re-layouts  6.02 us (12%)
  other arithmetic  2.12 us (4%)
  between operations  0.78 us (2%)
    ppermute x1, waiting for transfers between devices, diagonal(): return lax.ppermute(value, ('pb', 'lab'), pairs)  10.8 us
    ppermute x7, starting transfers between devices, swap(): return lax.ppermute(value, axis, [(i, i ^ bit) for i in range(count)])  8.9 us
    pallas_call x10, Pallas kernels, local_call(): pl.pallas_call(lambda *refs: body(*refs[:given], *refs[later:]), out_shap...  7.34 us
    unnamed x10, local copies, waits for them, and re-layouts  5.76 us
    ppermute x7, waiting for transfers between devices, swap(): return lax.ppermute(value, axis, [(i, i ^ bit) for i in range(count)])  4.19 us
    all_to_all x1, starting transfers between devices, dense_shards(): terms = lax.all_to_all(dq, 'lab', split_axis=0, concat_axis=0, tiled=True)  3.45 us
    pallas_call x1, Pallas kernels, late(): pl.pallas_call(lambda *refs: late_body(groups, *refs), out_shape=[out, li...  2.71 us
    ppermute x1, starting transfers between devices, diagonal(): return lax.ppermute(value, ('pb', 'lab'), pairs)  1.82 us
  transfers between devices with their start and end apart: 9, of which 4 were waited for; matrix products, arithmetic and copies ran while one was open for 5% of the time, Pallas kernels for 14%

profile of v10, /device:TPU:0, one launch (start us, length us, event | category | flops | bytes accessed | tf_op | source)
XLA Modules:
  0.0 48.1 jit_solution(13871391598605665564)
XLA Ops:
  0.6 3.1 %collective-permute-start = (bf16[32,768]{1,0:T(8,128)(2,1)}, bf16[32,768]{1,0:T(8,128)(2,1)S(1)}, u32[]{:S(2)}, u32[]{:S(2)}) collective-permute-start(bf16[32,768]{1,0:T(8,128)(2,1)} %refs_0_.1), channel_id=1, source_target_pairs={{0,2},{1,3},{2,0},{3,1},{4,6},{5,7},{6,4},{7,5},{8,10},{9,11},{10,... | collective-permute-start | bytes 147464 | tf_op jit(solution)/shard_map/ppermute | solution.py:77
  3.7 2.6 %collective-permute-start.1 = (bf16[32,768]{1,0:T(8,128)(2,1)}, bf16[32,768]{1,0:T(8,128)(2,1)S(1)}, u32[]{:S(2)}, u32[]{:S(2)}) collective-permute-start(bf16[32,768]{1,0:T(8,128)(2,1)} %refs_0_.1), channel_id=1, source_target_pairs={{0,4},{1,5},{2,6},{3,7},{4,0},{5,1},{6,2},{7,3},{8,12},{9,13},{10,... | collective-permute-start | bytes 147464 | tf_op jit(solution)/shard_map/ppermute | solution.py:77
  6.3 0.7 %and_select_fusion.1 = s32[256]{0:T(256)S(1)} fusion(s32[256]{0:T(256)} %param.7), kind=kLoop, calls=%fused_computation.11 | loop fusion | flops 3840 | bytes 2048 | tf_op jit(solution)/shard_map/jit(floor_divide)/jit(_where)/select_n | solution.py:276
  7.0 0.7 %fusion = (s32[256]{0:T(256)S(1)}, s32[256]{0:T(256)S(1)}) fusion(s32[256,8]{0,1:T(8,128)} %param.6, s32[]{:T(128)S(6)} %mul.3, s32[256]{0:T(256)S(1)} %and_select_fusion.1), kind=kLoop, calls=%fused_computation.4 | loop fusion | flops 17920 | bytes 11268 | tf_op jit(solution)/shard_map/reduce_max | solution.py:274
  7.7 0.7 %fusion.4 = (bf16[256]{0:T(256)(128)(2,1)S(1)}, bf16[256]{0:T(256)(128)(2,1)S(1)}) fusion(s32[256]{0:T(256)S(1)} %get-tuple-element.26, s32[256]{0:T(256)} %param.7, s32[256]{0:T(256)S(1)} %get-tuple-element.27), kind=kLoop, calls=%fused_computation.19 | loop fusion | flops 3840 | bytes 4096 | tf_op jit(solution)/shard_map/convert.3
  8.7 0.8 %copy-done.3 = bf16[32,768]{1,0:T(8,128)(2,1)S(1)} copy-done((bf16[32,768]{1,0:T(8,128)(2,1)S(1)}, bf16[32,768]{1,0:T(8,128)(2,1)}, u32[]{:S(2)}) %copy-start.3) | copy-done | bytes 49176
  9.9 2.6 %collective-permute-done.2.refs_4_ = bf16[32,768]{1,0:T(8,128)(2,1)S(1)} collective-permute-done((bf16[32,768]{1,0:T(8,128)(2,1)}, bf16[32,768]{1,0:T(8,128)(2,1)S(1)}, u32[]{:S(2)}, u32[]{:S(2)}) %collective-permute-start.2) | collective-permute-done | bytes 49184 | tf_op jit(solution)/shard_map/ppermute | solution.py:77
  12.4 1.6 %collective-permute-start.3 = (bf16[128,768]{1,0:T(8,128)(2,1)S(1)}, bf16[128,768]{1,0:T(8,128)(2,1)S(1)}, u32[]{:S(2)}, u32[]{:S(2)}) collective-permute-start(bf16[128,768]{1,0:T(8,128)(2,1)S(1)} %get-tuple-element.14.refs_0_), channel_id=1, source_target_pairs={{0,1},{1,0},{2,3},{3,2},{4,5},{5,4},{6,7},{7,6},{8,9},{9,8},{10,11... | collective-permute-start | bytes 589832 | tf_op jit(solution)/shard_map/ppermute | solution.py:77
  14.0 1.4 %copy-done.2 = bf16[1024,768]{1,0:T(8,128)(2,1)S(1)} copy-done((bf16[1024,768]{1,0:T(8,128)(2,1)S(1)}, bf16[1024,768]{1,0:T(8,128)(2,1)}, u32[]{:S(2)}) %copy-start.2) | copy-done | bytes 1572888
  15.4 1.4 %shard_map.61 = (bf16[128,768]{1,0:T(8,128)(2,1)S(1)}, bf16[144,128]{1,0:T(8,128)(2,1)S(1)}, bf16[1024,768]{1,0:T(8,128)(2,1)S(1)}, bf16[128,768]{1,0:T(8,128)(2,1)S(1)}) custom-call(bf16[128,768]{1,0:T(8,128)(2,1)S(1)} %get-tuple-element.14.refs_0_, bf16[1024,768]{1,0:T(8,128)(2,1)S(1)} %copy-done.2, bf16[16,768]{1,0:T(8,128)(2,1)S(1)} %pad.4.refs_5_.refs_2_), custom_call_target="tpu_custom_call" | custom-call | flops 402653184 | tf_op jit(solution)/shard_map/pallas_call | solution.py:96
  16.9 1.3 %collective-permute-done.3.refs_0_.refs_1_ = bf16[128,768]{1,0:T(8,128)(2,1)S(1)} collective-permute-done((bf16[128,768]{1,0:T(8,128)(2,1)S(1)}, bf16[128,768]{1,0:T(8,128)(2,1)S(1)}, u32[]{:S(2)}, u32[]{:S(2)}) %collective-permute-start.3) | collective-permute-done | bytes 196640 | tf_op jit(solution)/shard_map/ppermute | solution.py:77
  18.2 1.3 %shard_map.62 = (bf16[128,768]{1,0:T(8,128)(2,1)S(1)}, bf16[144,128]{1,0:T(8,128)(2,1)S(1)}) custom-call(bf16[128,768]{1,0:T(8,128)(2,1)S(1)} %collective-permute-done.3.refs_0_.refs_1_, bf16[1024,768]{1,0:T(8,128)(2,1)S(1)} %get-tuple-element.16.refs_1_, bf16[16,768]{1,0:T(8,128)(2,1)S(1)} %pad.4.refs_5_.refs_2_, ...), custom_call_target="tpu_custom_call" | custom-call | flops 402653184 | tf_op jit(solution)/shard_map/pallas_call | solution.py:96
  19.5 0.8 %shard_map.63.refs_4_ = bf16[8,32,768]{2,1,0:T(8,128)(2,1)} custom-call(s32[1]{0:T(128)} %bitcast.refs_0_, bf16[128,768]{1,0:T(8,128)(2,1)S(1)} %get-tuple-element.15.refs_3_.refs_1_, bf16[128,768]{1,0:T(8,128)(2,1)S(1)} %get-tuple-element.17.refs_2_), custom_call_target="tpu_custom_call" | custom-call | tf_op jit(solution)/shard_map/pallas_call | solution.py:96
  20.3 0.6 %shard_map.64 = (f32[1024,768]{1,0:T(8,128)S(1)}, bf16[400,768]{1,0:T(8,128)(2,1)S(1)}) custom-call(bf16[128,768]{1,0:T(8,128)(2,1)S(1)} %get-tuple-element.14.refs_0_, bf16[128,768]{1,0:T(8,128)(2,1)S(1)} %collective-permute-done.3.refs_0_.refs_1_, bf16[144,128]{1,0:T(8,128)(2,1)S(1)} %get-tuple-element.20.refs_2_, ...), custom_call_target="tpu_custom_call" | custom-call | flops 402653184 | tf_op jit(solution)/shard_map/pallas_call | solution.py:96
  20.9 1.7 %copy-done = f32[1024,768]{1,0:T(8,128)} copy-done((f32[1024,768]{1,0:T(8,128)}, f32[1024,768]{1,0:T(8,128)S(1)}, u32[]{:S(2)}) %copy-start) | copy-done | bytes 3145752
  22.5 3.5 %all-to-all-start = ((bf16[8,32,768]{2,1,0:T(8,128)(2,1)}), bf16[8,32,768]{2,1,0:T(8,128)(2,1)S(1)}, u32[]{:S(2)}, u32[]{:S(2)}) async-start(bf16[8,32,768]{2,1,0:T(8,128)(2,1)} %shard_map.63.refs_4_), calls=%async_computation | async-start | bytes 786432 | tf_op jit(solution)/shard_map/all_to_all | solution.py:326
  26.0 1.6 %collective-permute-start.4 = (bf16[144,768]{1,0:T(8,128)(2,1)S(1)}, bf16[144,768]{1,0:T(8,128)(2,1)S(1)}, u32[]{:S(2)}, u32[]{:S(2)}) collective-permute-start(bf16[144,768]{1,0:T(8,128)(2,1)S(1)} %get-tuple-element.18), channel_id=1, source_target_pairs={{0,16},{8,24},{16,0},{24,8},{1,17},{9,25},{17,1},{25,9},{2,18},{10... | collective-permute-start | bytes 663560 | tf_op jit(solution)/shard_map/ppermute | solution.py:77
  27.6 1.8 %collective-permute-start.5 = (bf16[128,768]{1,0:T(8,128)(2,1)}, bf16[128,768]{1,0:T(8,128)(2,1)S(1)}, u32[]{:S(2)}, u32[]{:S(2)}) collective-permute-start(bf16[128,768]{1,0:T(8,128)(2,1)} %copy-done.4), channel_id=1, source_target_pairs={{0,17},{1,16},{2,19},{3,18},{4,21},{5,20},{6,23},{7,22},{8,25},{9,... | collective-permute-start | bytes 589832 | tf_op jit(solution)/shard_map/ppermute | solution.py:87
  29.4 10.8 %collective-permute-done.5.refs_1_ = bf16[128,768]{1,0:T(8,128)(2,1)S(1)} collective-permute-done((bf16[128,768]{1,0:T(8,128)(2,1)}, bf16[128,768]{1,0:T(8,128)(2,1)S(1)}, u32[]{:S(2)}, u32[]{:S(2)}) %collective-permute-start.5) | collective-permute-done | bytes 196640 | tf_op jit(solution)/shard_map/ppermute | solution.py:87
  40.2 1.9 %copy-done.1 = f32[1024,768]{1,0:T(8,128)S(1)} copy-done((f32[1024,768]{1,0:T(8,128)S(1)}, f32[1024,768]{1,0:T(8,128)}, u32[]{:S(2)}) %copy-start.1) | copy-done | bytes 3145752
  42.2 0.6 %shard_map.66.refs_2_ = f32[1024,768]{1,0:T(8,128)S(1)} custom-call(bf16[400,768]{1,0:T(8,128)(2,1)S(1)} %collective-permute-done.7.refs_0_, f32[1024,768]{1,0:T(8,128)S(1)} %copy-done.1, bf16[272,768]{1,0:T(8,128)(2,1)S(1)} %shard_map.65.refs_2_.refs_0_), custom_call_target="tpu_custom_call" | custom-call | flops 402653184 | tf_op jit(solution)/shard_map/pallas_call | solution.py:96
  42.8 1.9 %shard_map.67.refs_2_ = f32[1024,768]{1,0:T(8,128)S(1)} custom-call(bf16[272,768]{1,0:T(8,128)(2,1)S(1)} %shard_map.65.refs_2_.refs_0_, bf16[1024,768]{1,0:T(8,128)(2,1)S(1)} %get-tuple-element.16.refs_1_, f32[1024,768]{1,0:T(8,128)S(1)} %shard_map.66.refs_2_), custom_call_target="tpu_custom_call" | custom-call | flops 805306368 | tf_op jit(solution)/shard_map/pallas_call | solution.py:96
  44.7 2.7 %shard_map.68 = (bf16[1024,768]{1,0:T(8,128)(2,1)}, s32[1,128]{1,0:T(1,128)S(1)}) custom-call(bf16[272,768]{1,0:T(8,128)(2,1)S(1)} %collective-permute-done.6.refs_0_, bf16[1024,768]{1,0:T(8,128)(2,1)S(1)} %get-tuple-element.16.refs_1_, f32[1024,768]{1,0:T(8,128)S(1)} %shard_map.67.refs_2_), custom_call_target="tpu_custom_call" | custom-call | tf_op jit(solution)/shard_map/pallas_call | solution.py:259
  47.4 0.7 %shard_map.69 = f32[32,768]{1,0:T(8,128)} custom-call(bf16[8,32,768]{2,1,0:T(8,128)(2,1)S(1)} %all-to-all-done.refs_0_, s32[1,128]{1,0:T(1,128)S(1)} %get-tuple-element.24.refs_1_), custom_call_target="tpu_custom_call" | custom-call | tf_op jit(solution)/shard_map/pallas_call | solution.py:96
  (25 shorter events, 0.8 us)
Async XLA Ops:
  0.6 8.9 %collective-permute-start = (bf16[32,768]{1,0:T(8,128)(2,1)}, bf16[32,768]{1,0:T(8,128)(2,1)S(1)}, u32[]{:S(2)}, u32[]{:S(2)}) collective-permute-start(bf16[32,768]{1,0:T(8,128)(2,1)} %refs_0_.1), channel_id=1, source_target_pairs={{0,2},{1,3},{2,0},{3,1},{4,6},{5,7},{6,4},{7,5},{8,10},{9,11},{10,... | collective-permute-start | bytes 147464 | tf_op jit(solution)/shard_map/ppermute | solution.py:77
  3.7 6.1 %collective-permute-start.1 = (bf16[32,768]{1,0:T(8,128)(2,1)}, bf16[32,768]{1,0:T(8,128)(2,1)S(1)}, u32[]{:S(2)}, u32[]{:S(2)}) collective-permute-start(bf16[32,768]{1,0:T(8,128)(2,1)} %refs_0_.1), channel_id=1, source_target_pairs={{0,4},{1,5},{2,6},{3,7},{4,0},{5,1},{6,2},{7,3},{8,12},{9,13},{10,... | collective-permute-start | bytes 147464 | tf_op jit(solution)/shard_map/ppermute | solution.py:77
  6.3 6.1 %collective-permute-start.2 = (bf16[32,768]{1,0:T(8,128)(2,1)}, bf16[32,768]{1,0:T(8,128)(2,1)S(1)}, u32[]{:S(2)}, u32[]{:S(2)}) collective-permute-start(bf16[32,768]{1,0:T(8,128)(2,1)} %refs_0_.1), channel_id=1, source_target_pairs={{0,6},{1,7},{2,4},{3,5},{4,2},{5,3},{6,0},{7,1},{8,14},{9,15},{10,... | collective-permute-start | bytes 147464 | tf_op jit(solution)/shard_map/ppermute | solution.py:77
  8.7 0.8 %copy-start.3 = (bf16[32,768]{1,0:T(8,128)(2,1)S(1)}, bf16[32,768]{1,0:T(8,128)(2,1)}, u32[]{:S(2)}) copy-start(bf16[32,768]{1,0:T(8,128)(2,1)} %refs_0_.1) | copy-start | bytes 147460
  12.4 5.7 %collective-permute-start.3 = (bf16[128,768]{1,0:T(8,128)(2,1)S(1)}, bf16[128,768]{1,0:T(8,128)(2,1)S(1)}, u32[]{:S(2)}, u32[]{:S(2)}) collective-permute-start(bf16[128,768]{1,0:T(8,128)(2,1)S(1)} %get-tuple-element.14.refs_0_), channel_id=1, source_target_pairs={{0,1},{1,0},{2,3},{3,2},{4,5},{5,4},{6,7},{7,6},{8,9},{9,8},{10,11... | collective-permute-start | bytes 589832 | tf_op jit(solution)/shard_map/ppermute | solution.py:77
  14.0 1.4 %copy-start.2 = (bf16[1024,768]{1,0:T(8,128)(2,1)S(1)}, bf16[1024,768]{1,0:T(8,128)(2,1)}, u32[]{:S(2)}) copy-start(bf16[1024,768]{1,0:T(8,128)(2,1)} %refs_1_.1) | copy-start | bytes 4718596
  16.8 3.5 %copy-start.4 = (bf16[128,768]{1,0:T(8,128)(2,1)}, bf16[128,768]{1,0:T(8,128)(2,1)S(1)}, u32[]{:S(2)}) copy-start(bf16[128,768]{1,0:T(8,128)(2,1)S(1)} %get-tuple-element.19) | copy-start | bytes 589828
  20.9 1.7 %copy-start = (f32[1024,768]{1,0:T(8,128)}, f32[1024,768]{1,0:T(8,128)S(1)}, u32[]{:S(2)}) copy-start(f32[1024,768]{1,0:T(8,128)S(1)} %get-tuple-element.22.refs_2_.refs_1_) | copy-start | bytes 9437188
  22.5 19.7 %collective-permute-start.7 = (bf16[400,768]{1,0:T(8,128)(2,1)S(1)}, bf16[400,768]{1,0:T(8,128)(2,1)S(1)}, u32[]{:S(2)}, u32[]{:S(2)}) collective-permute-start(bf16[400,768]{1,0:T(8,128)(2,1)S(1)} %get-tuple-element.23), channel_id=1, source_target_pairs={{0,8},{8,0},{16,24},{24,16},{1,9},{9,1},{17,25},{25,17},{2,10},{10... | collective-permute-start | bytes 1843208 | tf_op jit(solution)/shard_map/ppermute | solution.py:77
  22.5 24.9 %all-to-all-start = ((bf16[8,32,768]{2,1,0:T(8,128)(2,1)}), bf16[8,32,768]{2,1,0:T(8,128)(2,1)S(1)}, u32[]{:S(2)}, u32[]{:S(2)}) async-start(bf16[8,32,768]{2,1,0:T(8,128)(2,1)} %shard_map.63.refs_4_), calls=%async_computation | async-start | bytes 786432 | tf_op jit(solution)/shard_map/all_to_all | solution.py:326
  26.0 14.2 %collective-permute-start.4 = (bf16[144,768]{1,0:T(8,128)(2,1)S(1)}, bf16[144,768]{1,0:T(8,128)(2,1)S(1)}, u32[]{:S(2)}, u32[]{:S(2)}) collective-permute-start(bf16[144,768]{1,0:T(8,128)(2,1)S(1)} %get-tuple-element.18), channel_id=1, source_target_pairs={{0,16},{8,24},{16,0},{24,8},{1,17},{9,25},{17,1},{25,9},{2,18},{10... | collective-permute-start | bytes 663560 | tf_op jit(solution)/shard_map/ppermute | solution.py:77
  27.6 12.6 %collective-permute-start.5 = (bf16[128,768]{1,0:T(8,128)(2,1)}, bf16[128,768]{1,0:T(8,128)(2,1)S(1)}, u32[]{:S(2)}, u32[]{:S(2)}) collective-permute-start(bf16[128,768]{1,0:T(8,128)(2,1)} %copy-done.4), channel_id=1, source_target_pairs={{0,17},{1,16},{2,19},{3,18},{4,21},{5,20},{6,23},{7,22},{8,25},{9,... | collective-permute-start | bytes 589832 | tf_op jit(solution)/shard_map/ppermute | solution.py:87
  40.2 1.9 %copy-start.1 = (f32[1024,768]{1,0:T(8,128)S(1)}, f32[1024,768]{1,0:T(8,128)}, u32[]{:S(2)}) copy-start(f32[1024,768]{1,0:T(8,128)} %copy-done) | copy-start | bytes 9437188
  42.1 2.6 %collective-permute-start.6 = (bf16[272,768]{1,0:T(8,128)(2,1)S(1)}, bf16[272,768]{1,0:T(8,128)(2,1)S(1)}, u32[]{:S(2)}, u32[]{:S(2)}) collective-permute-start(bf16[272,768]{1,0:T(8,128)(2,1)S(1)} %shard_map.65.refs_2_.refs_0_), channel_id=1, source_target_pairs={{0,8},{8,0},{16,24},{24,16},{1,9},{9,1},{17,25},{25,17},{2,10},{10... | collective-permute-start | bytes 1253384 | tf_op jit(solution)/shard_map/ppermute | solution.py:77

commit v11 on v10

--- a/solution.py
+++ b/solution.py
@@ -329,7 +329,6 @@
         [like(lab_dev, width, f32), like(qcount + BLOCK + NOTE, width, bf16)],
         [near, far, near_slope, far_slope],
         work,
-        [dq],
     )
     mate = swap(own, "pb", 1)
     cross = local_call(
@@ -337,8 +336,8 @@
     )[0]
     cross_mate = swap(cross, "pb", 1)
     grown = like(lab_dev, width, f32)
-    acc = local_call(mate_body, [grown], [mate, acc], work, [cross])[0]
-    acc = local_call(cross_body, [grown], [cross, weights, acc], 2 * work)[0]
+    acc = local_call(cross_body, [grown], [cross, weights, acc], 20 * work)[0]
+    acc = local_call(mate_body, [grown], [mate, acc], work)[0]
     weight_grad, mark = late(groups, cross_mate, weights, acc)
     query_grad = local_call(sum_body, [like(q_home, width, f32)], [terms], 0, [mark])[0]
     return (query_grad, weight_grad)

time: 48.6 us -> 36.2 us (0.74)
  waiting for transfers between devices: 15 us -> 6.18 us
  local copies, waits for them, and re-layouts: 6.02 us -> 2.47 us
    ppermute x1, waiting for transfers between devices: 10.8 us -> 0.01 us  [diagonal(): return lax.ppermute(value, ('pb', 'lab'), pairs)]
    all_to_all x1, waiting for transfers between devices: 0.01 us -> 3.77 us  [dense_shards(): terms = lax.all_to_all(dq, 'lab', split_axis=0, concat_axis=0, tiled=True)]
    unnamed x10 -> x4, local copies, waits for them, and re-layouts: 5.76 us -> 2.21 us
    ppermute x7, waiting for transfers between devices: 4.19 us -> 2.41 us  [swap(): return lax.ppermute(value, axis, [(i, i ^ bit) for i in range(count)])]
    ppermute x1, starting transfers between devices: 1.82 us -> 0.54 us  [diagonal(): return lax.ppermute(value, ('pb', 'lab'), pairs)]
    all_to_all x1, starting transfers between devices: 3.45 us -> 4.35 us  [dense_shards(): terms = lax.all_to_all(dq, 'lab', split_axis=0, concat_axis=0, tiled=True)]
  transfers between devices with their start and end apart: 9 -> 9, of which waited for: 4 -> 3; matrix products, arithmetic and copies ran while one was open for 5% -> 7% of each run, Pallas kernels for 14% -> 26%
where the time goes in v11:
time: 36.2 us; the launch traced here: 35.8 us
  starting transfers between devices  14.3 us (40%)
  Pallas kernels  10 us (28%)
  waiting for transfers between devices  6.18 us (17%)
  local copies, waits for them, and re-layouts  2.47 us (7%)
  other arithmetic  2.12 us (6%)
  between operations  0.75 us (2%)
    ppermute x7, starting transfers between devices, swap(): return lax.ppermute(value, axis, [(i, i ^ bit) for i in range(count)])  9.37 us
    pallas_call x10, Pallas kernels, local_call(): pl.pallas_call(lambda *refs: body(*refs[:given], *refs[later:]), out_shap...  7.32 us
    all_to_all x1, starting transfers between devices, dense_shards(): terms = lax.all_to_all(dq, 'lab', split_axis=0, concat_axis=0, tiled=True)  4.35 us
    all_to_all x1, waiting for transfers between devices, dense_shards(): terms = lax.all_to_all(dq, 'lab', split_axis=0, concat_axis=0, tiled=True)  3.77 us
    pallas_call x1, Pallas kernels, late(): pl.pallas_call(lambda *refs: late_body(groups, *refs), out_shape=[out, li...  2.7 us
    ppermute x7, waiting for transfers between devices, swap(): return lax.ppermute(value, axis, [(i, i ^ bit) for i in range(count)])  2.41 us
    unnamed x4, local copies, waits for them, and re-layouts  2.21 us
  transfers between devices with their start and end apart: 9, of which 3 were waited for; matrix products, arithmetic and copies ran while one was open for 7% of the time, Pallas kernels for 26%

profile of v11, /device:TPU:0, one launch (start us, length us, event | category | flops | bytes accessed | tf_op | source)
XLA Modules:
  0.0 35.8 jit_solution(10014764442104712412)
XLA Ops:
  0.6 3.1 %collective-permute-start = (bf16[32,768]{1,0:T(8,128)(2,1)}, bf16[32,768]{1,0:T(8,128)(2,1)S(1)}, u32[]{:S(2)}, u32[]{:S(2)}) collective-permute-start(bf16[32,768]{1,0:T(8,128)(2,1)} %refs_0_.1), channel_id=1, source_target_pairs={{0,2},{1,3},{2,0},{3,1},{4,6},{5,7},{6,4},{7,5},{8,10},{9,11},{10,... | collective-permute-start | bytes 147464 | tf_op jit(solution)/shard_map/ppermute | solution.py:77
  3.7 2.5 %collective-permute-start.2 = (bf16[32,768]{1,0:T(8,128)(2,1)}, bf16[32,768]{1,0:T(8,128)(2,1)S(1)}, u32[]{:S(2)}, u32[]{:S(2)}) collective-permute-start(bf16[32,768]{1,0:T(8,128)(2,1)} %refs_0_.1), channel_id=1, source_target_pairs={{0,6},{1,7},{2,4},{3,5},{4,2},{5,3},{6,0},{7,1},{8,14},{9,15},{10,... | collective-permute-start | bytes 147464 | tf_op jit(solution)/shard_map/ppermute | solution.py:77
  6.2 0.1 collective-permute-start.1
  6.3 0.7 %and_select_fusion.1 = s32[256]{0:T(256)S(1)} fusion(s32[256]{0:T(256)} %param.7), kind=kLoop, calls=%fused_computation.11 | loop fusion | flops 3840 | bytes 2048 | tf_op jit(solution)/shard_map/jit(floor_divide)/jit(_where)/select_n | solution.py:276
  7.0 0.7 %fusion = (s32[256]{0:T(256)S(1)}, s32[256]{0:T(256)S(1)}) fusion(s32[256,8]{0,1:T(8,128)} %param.6, s32[]{:T(128)S(6)} %mul.3, s32[256]{0:T(256)S(1)} %and_select_fusion.1), kind=kLoop, calls=%fused_computation.4 | loop fusion | flops 17920 | bytes 11268 | tf_op jit(solution)/shard_map/reduce_max | solution.py:274
  7.7 0.7 %fusion.4 = (bf16[256]{0:T(256)(128)(2,1)S(1)}, bf16[256]{0:T(256)(128)(2,1)S(1)}) fusion(s32[256]{0:T(256)S(1)} %get-tuple-element.26, s32[256]{0:T(256)} %param.7, s32[256]{0:T(256)S(1)} %get-tuple-element.27), kind=kLoop, calls=%fused_computation.19 | loop fusion | flops 3840 | bytes 4096 | tf_op jit(solution)/shard_map/convert.3
  8.7 0.8 %copy-done.1 = bf16[32,768]{1,0:T(8,128)(2,1)S(1)} copy-done((bf16[32,768]{1,0:T(8,128)(2,1)S(1)}, bf16[32,768]{1,0:T(8,128)(2,1)}, u32[]{:S(2)}) %copy-start.1) | copy-done | bytes 49176
  9.5 0.9 %collective-permute-done.2.refs_4_ = bf16[32,768]{1,0:T(8,128)(2,1)S(1)} collective-permute-done((bf16[32,768]{1,0:T(8,128)(2,1)}, bf16[32,768]{1,0:T(8,128)(2,1)S(1)}, u32[]{:S(2)}, u32[]{:S(2)}) %collective-permute-start.2) | collective-permute-done | bytes 49184 | tf_op jit(solution)/shard_map/ppermute | solution.py:77
  10.4 1.5 %collective-permute-done.1.refs_3_ = bf16[32,768]{1,0:T(8,128)(2,1)S(1)} collective-permute-done((bf16[32,768]{1,0:T(8,128)(2,1)}, bf16[32,768]{1,0:T(8,128)(2,1)S(1)}, u32[]{:S(2)}, u32[]{:S(2)}) %collective-permute-start.1) | collective-permute-done | bytes 49184 | tf_op jit(solution)/shard_map/ppermute | solution.py:77
  12.0 1.6 %collective-permute-start.3 = (bf16[128,768]{1,0:T(8,128)(2,1)S(1)}, bf16[128,768]{1,0:T(8,128)(2,1)S(1)}, u32[]{:S(2)}, u32[]{:S(2)}) collective-permute-start(bf16[128,768]{1,0:T(8,128)(2,1)S(1)} %get-tuple-element.14.refs_0_), channel_id=1, source_target_pairs={{0,1},{1,0},{2,3},{3,2},{4,5},{5,4},{6,7},{7,6},{8,9},{9,8},{10,11... | collective-permute-start | bytes 589832 | tf_op jit(solution)/shard_map/ppermute | solution.py:77
  13.5 1.5 %collective-permute-start.4 = (bf16[144,768]{1,0:T(8,128)(2,1)S(1)}, bf16[144,768]{1,0:T(8,128)(2,1)S(1)}, u32[]{:S(2)}, u32[]{:S(2)}) collective-permute-start(bf16[144,768]{1,0:T(8,128)(2,1)S(1)} %get-tuple-element.18), channel_id=1, source_target_pairs={{0,16},{8,24},{16,0},{24,8},{1,17},{9,25},{17,1},{25,9},{2,18},{10... | collective-permute-start | bytes 663560 | tf_op jit(solution)/shard_map/ppermute | solution.py:77
  15.0 1.4 %copy-done = bf16[1024,768]{1,0:T(8,128)(2,1)S(1)} copy-done((bf16[1024,768]{1,0:T(8,128)(2,1)S(1)}, bf16[1024,768]{1,0:T(8,128)(2,1)}, u32[]{:S(2)}) %copy-start) | copy-done | bytes 1572888
  16.4 1.4 %shard_map.61 = (bf16[128,768]{1,0:T(8,128)(2,1)S(1)}, bf16[144,128]{1,0:T(8,128)(2,1)S(1)}, bf16[1024,768]{1,0:T(8,128)(2,1)S(1)}, bf16[128,768]{1,0:T(8,128)(2,1)S(1)}) custom-call(bf16[128,768]{1,0:T(8,128)(2,1)S(1)} %get-tuple-element.14.refs_0_, bf16[1024,768]{1,0:T(8,128)(2,1)S(1)} %copy-done, bf16[16,768]{1,0:T(8,128)(2,1)S(1)} %pad.4.refs_5_.refs_2_), custom_call_target="tpu_custom_call" | custom-call | flops 402653184 | tf_op jit(solution)/shard_map/pallas_call | solution.py:96
  17.9 0.5 %collective-permute-start.5 = (bf16[128,768]{1,0:T(8,128)(2,1)S(1)}, bf16[128,768]{1,0:T(8,128)(2,1)S(1)}, u32[]{:S(2)}, u32[]{:S(2)}) collective-permute-start(bf16[128,768]{1,0:T(8,128)(2,1)S(1)} %get-tuple-element.19), channel_id=1, source_target_pairs={{0,17},{1,16},{2,19},{3,18},{4,21},{5,20},{6,23},{7,22},{8,25},{9,... | collective-permute-start | bytes 589832 | tf_op jit(solution)/shard_map/ppermute | solution.py:87
  18.4 1.3 %shard_map.62 = (bf16[128,768]{1,0:T(8,128)(2,1)S(1)}, bf16[144,128]{1,0:T(8,128)(2,1)S(1)}) custom-call(bf16[128,768]{1,0:T(8,128)(2,1)S(1)} %collective-permute-done.3.refs_0_.refs_1_, bf16[1024,768]{1,0:T(8,128)(2,1)S(1)} %get-tuple-element.16.refs_1_, bf16[16,768]{1,0:T(8,128)(2,1)S(1)} %pad.4.refs_5_.refs_2_, ...), custom_call_target="tpu_custom_call" | custom-call | flops 402653184 | tf_op jit(solution)/shard_map/pallas_call | solution.py:96
  19.7 0.8 %shard_map.63 = bf16[8,32,768]{2,1,0:T(8,128)(2,1)} custom-call(s32[1]{0:T(128)} %bitcast.refs_0_, bf16[128,768]{1,0:T(8,128)(2,1)S(1)} %get-tuple-element.15.refs_3_.refs_1_, bf16[128,768]{1,0:T(8,128)(2,1)S(1)} %get-tuple-element.17.refs_2_), custom_call_target="tpu_custom_call" | custom-call | tf_op jit(solution)/shard_map/pallas_call | solution.py:96
  20.5 4.4 %all-to-all-start = ((bf16[8,32,768]{2,1,0:T(8,128)(2,1)}), bf16[8,32,768]{2,1,0:T(8,128)(2,1)S(1)}, u32[]{:S(2)}, u32[]{:S(2)}) async-start(bf16[8,32,768]{2,1,0:T(8,128)(2,1)} %shard_map.63), calls=%async_computation | async-start | bytes 786432 | tf_op jit(solution)/shard_map/all_to_all | solution.py:326
  24.9 0.6 %shard_map.64 = (f32[1024,768]{1,0:T(8,128)S(1)}, bf16[400,768]{1,0:T(8,128)(2,1)S(1)}) custom-call(bf16[128,768]{1,0:T(8,128)(2,1)S(1)} %get-tuple-element.14.refs_0_, bf16[128,768]{1,0:T(8,128)(2,1)S(1)} %collective-permute-done.3.refs_0_.refs_1_, bf16[144,128]{1,0:T(8,128)(2,1)S(1)} %get-tuple-element.20.refs_2_, ...), custom_call_target="tpu_custom_call" | custom-call | flops 402653184 | tf_op jit(solution)/shard_map/pallas_call | solution.py:96
  25.6 0.5 %collective-permute-start.6 = (bf16[272,768]{1,0:T(8,128)(2,1)S(1)}, bf16[272,768]{1,0:T(8,128)(2,1)S(1)}, u32[]{:S(2)}, u32[]{:S(2)}) collective-permute-start(bf16[272,768]{1,0:T(8,128)(2,1)S(1)} %shard_map.65.refs_0_), channel_id=1, source_target_pairs={{0,8},{8,0},{16,24},{24,16},{1,9},{9,1},{17,25},{25,17},{2,10},{10... | collective-permute-start | bytes 1253384 | tf_op jit(solution)/shard_map/ppermute | solution.py:77
  26.1 1.9 %shard_map.66.refs_1_ = f32[1024,768]{1,0:T(8,128)S(1)} custom-call(bf16[272,768]{1,0:T(8,128)(2,1)S(1)} %shard_map.65.refs_0_, bf16[1024,768]{1,0:T(8,128)(2,1)S(1)} %get-tuple-element.16.refs_1_, f32[1024,768]{1,0:T(8,128)S(1)} %get-tuple-element.22.refs_2_), custom_call_target="tpu_custom_call" | custom-call | flops 8053063680 | tf_op jit(solution)/shard_map/pallas_call | solution.py:96
  28.0 0.6 %shard_map.67.refs_2_ = f32[1024,768]{1,0:T(8,128)S(1)} custom-call(bf16[400,768]{1,0:T(8,128)(2,1)S(1)} %collective-permute-done.7.refs_0_, f32[1024,768]{1,0:T(8,128)S(1)} %shard_map.66.refs_1_), custom_call_target="tpu_custom_call" | custom-call | flops 402653184 | tf_op jit(solution)/shard_map/pallas_call | solution.py:96
  28.6 2.7 %shard_map.68 = (bf16[1024,768]{1,0:T(8,128)(2,1)}, s32[1,128]{1,0:T(1,128)S(1)}) custom-call(bf16[272,768]{1,0:T(8,128)(2,1)S(1)} %collective-permute-done.6.refs_0_, bf16[1024,768]{1,0:T(8,128)(2,1)S(1)} %get-tuple-element.16.refs_1_, f32[1024,768]{1,0:T(8,128)S(1)} %shard_map.67.refs_2_), custom_call_target="tpu_custom_call" | custom-call | tf_op jit(solution)/shard_map/pallas_call | solution.py:259
  31.3 3.8 %all-to-all-done.refs_0_ = bf16[8,32,768]{2,1,0:T(8,128)(2,1)S(1)} async-done(((bf16[8,32,768]{2,1,0:T(8,128)(2,1)}), bf16[8,32,768]{2,1,0:T(8,128)(2,1)S(1)}, u32[]{:S(2)}, u32[]{:S(2)}) %all-to-all-start) | async-done | bytes 393248 | tf_op jit(solution)/shard_map/all_to_all | solution.py:326
  35.1 0.7 %shard_map.69 = f32[32,768]{1,0:T(8,128)} custom-call(bf16[8,32,768]{2,1,0:T(8,128)(2,1)S(1)} %all-to-all-done.refs_0_, s32[1,128]{1,0:T(1,128)S(1)} %get-tuple-element.24.refs_1_), custom_call_target="tpu_custom_call" | custom-call | tf_op jit(solution)/shard_map/pallas_call | solution.py:96
  (19 shorter events, 0.4 us)
Async XLA Ops:
  0.6 8.9 %collective-permute-start = (bf16[32,768]{1,0:T(8,128)(2,1)}, bf16[32,768]{1,0:T(8,128)(2,1)S(1)}, u32[]{:S(2)}, u32[]{:S(2)}) collective-permute-start(bf16[32,768]{1,0:T(8,128)(2,1)} %refs_0_.1), channel_id=1, source_target_pairs={{0,2},{1,3},{2,0},{3,1},{4,6},{5,7},{6,4},{7,5},{8,10},{9,11},{10,... | collective-permute-start | bytes 147464 | tf_op jit(solution)/shard_map/ppermute | solution.py:77
  3.7 6.7 %collective-permute-start.2 = (bf16[32,768]{1,0:T(8,128)(2,1)}, bf16[32,768]{1,0:T(8,128)(2,1)S(1)}, u32[]{:S(2)}, u32[]{:S(2)}) collective-permute-start(bf16[32,768]{1,0:T(8,128)(2,1)} %refs_0_.1), channel_id=1, source_target_pairs={{0,6},{1,7},{2,4},{3,5},{4,2},{5,3},{6,0},{7,1},{8,14},{9,15},{10,... | collective-permute-start | bytes 147464 | tf_op jit(solution)/shard_map/ppermute | solution.py:77
  6.2 5.7 %collective-permute-start.1 = (bf16[32,768]{1,0:T(8,128)(2,1)}, bf16[32,768]{1,0:T(8,128)(2,1)S(1)}, u32[]{:S(2)}, u32[]{:S(2)}) collective-permute-start(bf16[32,768]{1,0:T(8,128)(2,1)} %refs_0_.1), channel_id=1, source_target_pairs={{0,4},{1,5},{2,6},{3,7},{4,0},{5,1},{6,2},{7,3},{8,12},{9,13},{10,... | collective-permute-start | bytes 147464 | tf_op jit(solution)/shard_map/ppermute | solution.py:77
  8.7 0.8 %copy-start.1 = (bf16[32,768]{1,0:T(8,128)(2,1)S(1)}, bf16[32,768]{1,0:T(8,128)(2,1)}, u32[]{:S(2)}) copy-start(bf16[32,768]{1,0:T(8,128)(2,1)} %refs_0_.1) | copy-start | bytes 147460
  12.0 6.4 %collective-permute-start.3 = (bf16[128,768]{1,0:T(8,128)(2,1)S(1)}, bf16[128,768]{1,0:T(8,128)(2,1)S(1)}, u32[]{:S(2)}, u32[]{:S(2)}) collective-permute-start(bf16[128,768]{1,0:T(8,128)(2,1)S(1)} %get-tuple-element.14.refs_0_), channel_id=1, source_target_pairs={{0,1},{1,0},{2,3},{3,2},{4,5},{5,4},{6,7},{7,6},{8,9},{9,8},{10,11... | collective-permute-start | bytes 589832 | tf_op jit(solution)/shard_map/ppermute | solution.py:77
  13.5 12.0 %collective-permute-start.4 = (bf16[144,768]{1,0:T(8,128)(2,1)S(1)}, bf16[144,768]{1,0:T(8,128)(2,1)S(1)}, u32[]{:S(2)}, u32[]{:S(2)}) collective-permute-start(bf16[144,768]{1,0:T(8,128)(2,1)S(1)} %get-tuple-element.18), channel_id=1, source_target_pairs={{0,16},{8,24},{16,0},{24,8},{1,17},{9,25},{17,1},{25,9},{2,18},{10... | collective-permute-start | bytes 663560 | tf_op jit(solution)/shard_map/ppermute | solution.py:77
  15.0 1.4 %copy-start = (bf16[1024,768]{1,0:T(8,128)(2,1)S(1)}, bf16[1024,768]{1,0:T(8,128)(2,1)}, u32[]{:S(2)}) copy-start(bf16[1024,768]{1,0:T(8,128)(2,1)} %refs_1_.1) | copy-start | bytes 4718596
  17.9 7.7 %collective-permute-start.5 = (bf16[128,768]{1,0:T(8,128)(2,1)S(1)}, bf16[128,768]{1,0:T(8,128)(2,1)S(1)}, u32[]{:S(2)}, u32[]{:S(2)}) collective-permute-start(bf16[128,768]{1,0:T(8,128)(2,1)S(1)} %get-tuple-element.19), channel_id=1, source_target_pairs={{0,17},{1,16},{2,19},{3,18},{4,21},{5,20},{6,23},{7,22},{8,25},{9,... | collective-permute-start | bytes 589832 | tf_op jit(solution)/shard_map/ppermute | solution.py:87
  20.5 14.6 %all-to-all-start = ((bf16[8,32,768]{2,1,0:T(8,128)(2,1)}), bf16[8,32,768]{2,1,0:T(8,128)(2,1)S(1)}, u32[]{:S(2)}, u32[]{:S(2)}) async-start(bf16[8,32,768]{2,1,0:T(8,128)(2,1)} %shard_map.63), calls=%async_computation | async-start | bytes 786432 | tf_op jit(solution)/shard_map/all_to_all | solution.py:326
  25.4 2.6 %collective-permute-start.7 = (bf16[400,768]{1,0:T(8,128)(2,1)S(1)}, bf16[400,768]{1,0:T(8,128)(2,1)S(1)}, u32[]{:S(2)}, u32[]{:S(2)}) collective-permute-start(bf16[400,768]{1,0:T(8,128)(2,1)S(1)} %get-tuple-element.23), channel_id=1, source_target_pairs={{0,8},{8,0},{16,24},{24,16},{1,9},{9,1},{17,25},{25,17},{2,10},{10... | collective-permute-start | bytes 1843208 | tf_op jit(solution)/shard_map/ppermute | solution.py:77
  25.6 3.0 %collective-permute-start.6 = (bf16[272,768]{1,0:T(8,128)(2,1)S(1)}, bf16[272,768]{1,0:T(8,128)(2,1)S(1)}, u32[]{:S(2)}, u32[]{:S(2)}) collective-permute-start(bf16[272,768]{1,0:T(8,128)(2,1)S(1)} %shard_map.65.refs_0_), channel_id=1, source_target_pairs={{0,8},{8,0},{16,24},{24,16},{1,9},{9,1},{17,25},{25,17},{2,10},{10... | collective-permute-start | bytes 1253384 | tf_op jit(solution)/shard_map/ppermute | solution.py:77

commit v12 on v11

--- a/solution.py
+++ b/solution.py
@@ -118,8 +118,9 @@
     noted_ref[half:, :] = note_ref[...]
 
 
-def hold_body(rows_ref, held_ref):
-    held_ref[...] = rows_ref[...]
+def hold_body(*refs):
+    for source, held in zip(refs[: len(refs) // 2], refs[len(refs) // 2 :]):
+        held[...] = source[...]
 
 
 def slope_of(rows, weights, chosen, place):
@@ -162,8 +163,7 @@
     dq_ref[...] = dq.astype(dq_ref.dtype)
 
 
-def near_body(rows_ref, weights_ref, note_ref, dq_ref, slope_ref, held_ref, copy_ref):
-    held_ref[...] = weights_ref[...]
+def near_body(rows_ref, weights_ref, note_ref, dq_ref, slope_ref, copy_ref):
     copy_ref[...] = rows_ref[...]
     grad_body(0, rows_ref, weights_ref, note_ref, dq_ref, slope_ref)
 
@@ -172,18 +172,18 @@
     grad_body(1, rows_ref, weights_ref, note_ref, dq_ref, slope_ref)
 
 
-def order_body(side_ref, near_ref, far_ref, out_ref):
-    side, q_home = side_ref[0], out_ref.shape[1]
-    for z in range(out_ref.shape[0] // 2):
-        part = slice(z * q_home, (z + 1) * q_home)
-        out_ref[2 * z + side] = near_ref[part, :]
-        out_ref[2 * z + 1 - side] = far_ref[part, :]
-
-
-def sum_body(terms_ref, out_ref):
-    total = terms_ref[0].astype(jnp.float32)
-    for source in range(1, terms_ref.shape[0]):
-        total = total + terms_ref[source].astype(jnp.float32)
+def fold_body(place_ref, near_ref, came_ref, kept_ref, *send_refs):
+    rows, place = kept_ref.shape[0], place_ref[0]
+    for step, ref in enumerate([kept_ref, *send_refs]):
+        part = pl.ds(pl.multiple_of((place ^ step) * rows, rows), rows)
+        ref[...] = (near_ref[part, :] + came_ref[part, :].astype(jnp.float32)).astype(ref.dtype)
+
+
+def sum_body(kept_ref, *refs):
+    *term_refs, out_ref = refs
+    total = kept_ref[...]
+    for ref in term_refs:
+        total = total + ref[...].astype(jnp.float32)
     out_ref[...] = total
 
 
@@ -267,18 +267,30 @@
     )(crossed, weights, acc)
 
 
-def make_note(sibling_blocks, positive_slot, blocks_dev, homes, width):
-    me = lax.axis_index("lab")
-    local = sibling_blocks.T - me * blocks_dev
+def note_body(blocks_dev, q_home, me_ref, choice_ref, note_ref):
+    choice = choice_ref[...].astype(jnp.int32)
+    me, picks, count = me_ref[0], choice.shape[0] - 1, choice.shape[1]
+    local, slot = choice[:picks] - me * blocks_dev, choice[picks:]
     inside = (local >= 0) & (local < blocks_dev)
-    chosen = jnp.max(jnp.where(inside, local, -1), axis=0)
-    steps = jnp.arange(local.shape[0], dtype=jnp.int32)[:, None]
-    pblock = jnp.sum(jnp.where(steps == (positive_slot // BLOCK)[None, :], local, 0), axis=0)
-    place = jnp.where(pblock == chosen, positive_slot % BLOCK, -1)
-    code = jnp.stack([chosen, place]).astype(jnp.bfloat16)
-    code = code.reshape(2, homes // 2, 2, -1).transpose(2, 0, 1, 3).reshape(2, 2, -1)
-    code = jnp.where(me % 2 == 0, code, code[::-1]).reshape(4, -1)
-    return jnp.pad(code, ((0, NOTE - 4), (0, width - code.shape[1])))
+    chosen = jnp.max(jnp.where(inside, local, -1), axis=0, keepdims=True)
+    steps = lax.broadcasted_iota(jnp.int32, local.shape, 0)
+    named = steps == lax.shift_right_logical(slot, BLOCK.bit_length() - 1)
+    pblock = jnp.sum(jnp.where(named, local, 0), axis=0, keepdims=True)
+    place = jnp.where(pblock == chosen, slot & (BLOCK - 1), -1)
+    row = lax.broadcasted_iota(jnp.int32, (NOTE, count), 0)
+    code = jnp.where(row == 0, chosen, jnp.where(row == 1, place, 0))
+    half = count // 2
+    lane = lax.broadcasted_iota(jnp.int32, (count, count), 1)
+    source = lax.broadcasted_iota(jnp.int32, (count, count), 0)
+    plane = (lane >= half).astype(jnp.int32) ^ (me & 1)
+    step = lax.shift_right_logical(lane & (half - 1), q_home.bit_length() - 1)
+    wanted = (2 * step + plane) * q_home + (lane & (q_home - 1))
+    order = jnp.where(source == wanted, 1.0, 0.0).astype(jnp.bfloat16)
+    code = jnp.dot(code.astype(jnp.bfloat16), order, preferred_element_type=jnp.float32)
+    rest = jnp.zeros((NOTE - 4, half), jnp.float32)
+    note = jnp.concatenate([code[:2, :half], code[:2, half:], rest], axis=0)
+    note_ref[...] = jnp.zeros_like(note_ref)
+    note_ref[:, :half] = note.astype(note_ref.dtype)
 
 
 def dense_shards(queries, label_weights, sibling_blocks, positive_slot):
@@ -292,23 +304,33 @@
     f32, bf16 = jnp.float32, jnp.bfloat16
 
     place = jnp.reshape(me // 2, (1,)).astype(jnp.int32)
-    side = jnp.reshape(me % 2, (1,)).astype(jnp.int32)
     far_bit = groups // 2
     came = [swap(queries, "lab", 2 * step) for step in range(1, homes // 2)]
-    held = local_call(hold_body, [like(q_home, width, bf16)], [queries])[0]
-    note = make_note(sibling_blocks, positive_slot, lab_dev // BLOCK, homes, width)
+    held, weights = local_call(
+        hold_body,
+        [like(q_home, width, bf16), like(lab_dev, width, bf16)],
+        [queries, label_weights],
+    )
+    choice = jnp.concatenate([sibling_blocks.T, positive_slot[None]], axis=0).astype(f32)
+    note = local_call(
+        lambda *refs: note_body(lab_dev // BLOCK, q_home, *refs),
+        [like(NOTE, width, bf16)],
+        [jnp.reshape(me, (1,)).astype(jnp.int32), choice],
+    )[0]
     near, noted = local_call(
         join_body,
         [like(half, width, bf16), like(half + NOTE, width, bf16)],
         [place, held, *came, note],
+        0,
+        [weights],
     )
     far = swap(near, "lab", 1)
     work = 4 * half * lab_dev * width
     slope_like = like(BLOCK + NOTE, half, bf16)
-    near_dq, near_slope, weights, near_copy = local_call(
+    near_dq, near_slope, near_copy = local_call(
         near_body,
-        [like(half, width, bf16), slope_like, like(lab_dev, width, bf16), like(half, width, bf16)],
-        [near, label_weights, note],
+        [like(half, width, f32), slope_like, like(half, width, bf16)],
+        [near, weights, note],
         work,
     )
     cross_near = swap(noted, "pb", far_bit)
@@ -320,10 +342,7 @@
         work,
         [near_dq],
     )
-    dq = local_call(
-        order_body, [jax.ShapeDtypeStruct((homes, q_home, width), bf16)], [side, near_dq, far_dq]
-    )[0]
-    terms = lax.all_to_all(dq, "lab", split_axis=0, concat_axis=0, tiled=True)
+    came = swap(far_dq, "lab", 1)
     acc, own = local_call(
         own_body,
         [like(lab_dev, width, f32), like(qcount + BLOCK + NOTE, width, bf16)],
@@ -331,15 +350,25 @@
         work,
     )
     mate = swap(own, "pb", 1)
+    kept, *terms = local_call(
+        fold_body,
+        [like(q_home, width, f32)] + [like(q_home, width, bf16)] * (homes // 2 - 1),
+        [place, near_dq, came],
+        0,
+        [acc],
+    )
+    terms = [swap(term, "lab", 2 * step) for step, term in enumerate(terms, 1)]
     cross = local_call(
-        stack_body, [like(qcount + NOTE, width, bf16)], [cross_near, cross_far], 0, [acc]
+        stack_body, [like(qcount + NOTE, width, bf16)], [cross_near, cross_far], 0, []
     )[0]
     cross_mate = swap(cross, "pb", 1)
     grown = like(lab_dev, width, f32)
     acc = local_call(cross_body, [grown], [cross, weights, acc], 20 * work)[0]
     acc = local_call(mate_body, [grown], [mate, acc], work)[0]
     weight_grad, mark = late(groups, cross_mate, weights, acc)
-    query_grad = local_call(sum_body, [like(q_home, width, f32)], [terms], 0, [mark])[0]
+    query_grad = local_call(
+        sum_body, [like(q_home, width, f32)], [kept, *terms], 0, [mark]
+    )[0]
     return (query_grad, weight_grad)
 
 

time: 36.2 us -> 37.7 us (1.041)
  waiting for transfers between devices: 6.18 us -> 8.12 us
  starting transfers between devices: 14.3 us -> 16.2 us
  other arithmetic: 2.12 us -> 0.72 us
  Pallas kernels: 10 us -> 9.45 us
    ppermute x7 -> x11, starting transfers between devices: 9.37 us -> 15.7 us  [swap(): return lax.ppermute(value, axis, [(i, i ^ bit) for i in range(count)])]
    all_to_all x1 -> x0, starting transfers between devices: 4.35 us -> none  [dense_shards(): terms = lax.all_to_all(dq, 'lab', split_axis=0, concat_axis=0, tiled=True)]
    ppermute x7 -> x11, waiting for transfers between devices: 2.41 us -> 6.38 us  [swap(): return lax.ppermute(value, axis, [(i, i ^ bit) for i in range(count)])]
    all_to_all x1 -> x0, waiting for transfers between devices: 3.77 us -> none  [dense_shards(): terms = lax.all_to_all(dq, 'lab', split_axis=0, concat_axis=0, tiled=True)]
    ppermute x1, waiting for transfers between devices: 0.01 us -> 1.74 us  [diagonal(): return lax.ppermute(value, ('pb', 'lab'), pairs)]
    convert_element_type x0 -> x1, other arithmetic: none -> 0.72 us  [dense_shards(): jnp.concatenate([sibling_blocks.T, positive_slot[None]], axis=0).astype(f32)]
    reduce_max x1 -> x0, other arithmetic: 0.71 us -> none  [make_note(): chosen = jnp.max(jnp.where(inside, local, -1), axis=0)]
    select_n x2 -> x0, other arithmetic: 0.69 us -> none  [the longest x1 0.69 us: make_note(): positive_slot // BLOCK]
  transfers between devices with their start and end apart: 9 -> 12, of which waited for: 3 -> 5; matrix products, arithmetic and copies ran while one was open for 7% -> 2% of each run, Pallas kernels for 26% -> 23%
where the time goes in v12:
time: 37.7 us; the launch traced here: 37.5 us
  starting transfers between devices  16.2 us (43%)
  Pallas kernels  9.45 us (25%)
  waiting for transfers between devices  8.12 us (22%)
  local copies, waits for them, and re-layouts  2.21 us (6%)
  between operations  0.76 us (2%)
  other arithmetic  0.72 us (2%)
    ppermute x11, starting transfers between devices, swap(): return lax.ppermute(value, axis, [(i, i ^ bit) for i in range(count)])  15.7 us
    pallas_call x11, Pallas kernels, local_call(): pl.pallas_call(lambda *refs: body(*refs[:given], *refs[later:]), out_shap...  6.75 us
    ppermute x11, waiting for transfers between devices, swap(): return lax.ppermute(value, axis, [(i, i ^ bit) for i in range(count)])  6.38 us
    pallas_call x1, Pallas kernels, late(): pl.pallas_call(lambda *refs: late_body(groups, *refs), out_shape=[out, li...  2.7 us
    unnamed x4, local copies, waits for them, and re-layouts  2.21 us
    ppermute x1, waiting for transfers between devices, diagonal(): return lax.ppermute(value, ('pb', 'lab'), pairs)  1.74 us
  transfers between devices with their start and end apart: 12, of which 5 were waited for; matrix products, arithmetic and copies ran while one was open for 2% of the time, Pallas kernels for 23%

profile of v12, /device:TPU:0, one launch (start us, length us, event | category | flops | bytes accessed | tf_op | source)
XLA Modules:
  0.0 37.5 jit_solution(8064390961660723525)
XLA Ops:
  0.6 3.1 %collective-permute-start = (bf16[32,768]{1,0:T(8,128)(2,1)}, bf16[32,768]{1,0:T(8,128)(2,1)S(1)}, u32[]{:S(2)}, u32[]{:S(2)}) collective-permute-start(bf16[32,768]{1,0:T(8,128)(2,1)} %refs_0_.1), channel_id=1, source_target_pairs={{0,2},{1,3},{2,0},{3,1},{4,6},{5,7},{6,4},{7,5},{8,10},{9,11},{10,... | collective-permute-start | bytes 147464 | tf_op jit(solution)/shard_map/ppermute | solution.py:77
  3.7 2.5 %collective-permute-start.2 = (bf16[32,768]{1,0:T(8,128)(2,1)}, bf16[32,768]{1,0:T(8,128)(2,1)S(1)}, u32[]{:S(2)}, u32[]{:S(2)}) collective-permute-start(bf16[32,768]{1,0:T(8,128)(2,1)} %refs_0_.1), channel_id=1, source_target_pairs={{0,6},{1,7},{2,4},{3,5},{4,2},{5,3},{6,0},{7,1},{8,14},{9,15},{10,... | collective-permute-start | bytes 147464 | tf_op jit(solution)/shard_map/ppermute | solution.py:77
  6.3 0.7 %add_convert_fusion.refs_1_ = f32[9,256]{1,0:T(8,128)S(1)} fusion(s32[1,256]{1,0:T(1,128)} %bitcast.5, s32[8,256]{1,0:T(8,128)} %bitcast.4), kind=kLoop, calls=%fused_computation | loop fusion | flops 4608 | bytes 18432 | tf_op jit(solution)/shard_map/convert_element_type | solution.py:314
  7.0 1.4 %copy-done = bf16[1024,768]{1,0:T(8,128)(2,1)S(1)} copy-done((bf16[1024,768]{1,0:T(8,128)(2,1)S(1)}, bf16[1024,768]{1,0:T(8,128)(2,1)}, u32[]{:S(2)}) %copy-start) | copy-done | bytes 1572888
  8.4 0.8 %copy-done.1 = bf16[32,768]{1,0:T(8,128)(2,1)S(1)} copy-done((bf16[32,768]{1,0:T(8,128)(2,1)S(1)}, bf16[32,768]{1,0:T(8,128)(2,1)}, u32[]{:S(2)}) %copy-start.1) | copy-done | bytes 49176
  9.5 0.9 %collective-permute-done.2.refs_4_ = bf16[32,768]{1,0:T(8,128)(2,1)S(1)} collective-permute-done((bf16[32,768]{1,0:T(8,128)(2,1)}, bf16[32,768]{1,0:T(8,128)(2,1)S(1)}, u32[]{:S(2)}, u32[]{:S(2)}) %collective-permute-start.2) | collective-permute-done | bytes 49184 | tf_op jit(solution)/shard_map/ppermute | solution.py:77
  10.4 1.5 %collective-permute-done.1.refs_3_ = bf16[32,768]{1,0:T(8,128)(2,1)S(1)} collective-permute-done((bf16[32,768]{1,0:T(8,128)(2,1)}, bf16[32,768]{1,0:T(8,128)(2,1)S(1)}, u32[]{:S(2)}, u32[]{:S(2)}) %collective-permute-start.1) | collective-permute-done | bytes 49184 | tf_op jit(solution)/shard_map/ppermute | solution.py:77
  12.0 1.6 %collective-permute-start.3 = (bf16[128,768]{1,0:T(8,128)(2,1)S(1)}, bf16[128,768]{1,0:T(8,128)(2,1)S(1)}, u32[]{:S(2)}, u32[]{:S(2)}) collective-permute-start(bf16[128,768]{1,0:T(8,128)(2,1)S(1)} %get-tuple-element.21.refs_0_), channel_id=1, source_target_pairs={{0,1},{1,0},{2,3},{3,2},{4,5},{5,4},{6,7},{7,6},{8,9},{9,8},{10,11... | collective-permute-start | bytes 589832 | tf_op jit(solution)/shard_map/ppermute | solution.py:77
  13.5 1.5 %collective-permute-start.8 = (bf16[144,768]{1,0:T(8,128)(2,1)S(1)}, bf16[144,768]{1,0:T(8,128)(2,1)S(1)}, u32[]{:S(2)}, u32[]{:S(2)}) collective-permute-start(bf16[144,768]{1,0:T(8,128)(2,1)S(1)} %get-tuple-element.31), channel_id=1, source_target_pairs={{0,16},{8,24},{16,0},{24,8},{1,17},{9,25},{17,1},{25,9},{2,18},{10... | collective-permute-start | bytes 663560 | tf_op jit(solution)/shard_map/ppermute | solution.py:77
  15.0 1.3 %shard_map.62 = (f32[128,768]{1,0:T(8,128)S(1)}, bf16[144,128]{1,0:T(8,128)(2,1)S(1)}, bf16[128,768]{1,0:T(8,128)(2,1)S(1)}) custom-call(bf16[128,768]{1,0:T(8,128)(2,1)S(1)} %get-tuple-element.21.refs_0_, bf16[1024,768]{1,0:T(8,128)(2,1)S(1)} %get-tuple-element.20.refs_6_.refs_1_, bf16[16,768]{1,0:T(8,128)(2,1)S(1)} %shard_map.60.refs_5_.refs_2_), custom_call_target="tpu_custom_call" | custom-call | flops 402653184 | tf_op jit(solution)/shard_map/pallas_call | solution.py:96
  16.4 0.5 %collective-permute-start.9 = (bf16[128,768]{1,0:T(8,128)(2,1)S(1)}, bf16[128,768]{1,0:T(8,128)(2,1)S(1)}, u32[]{:S(2)}, u32[]{:S(2)}) collective-permute-start(bf16[128,768]{1,0:T(8,128)(2,1)S(1)} %get-tuple-element.32), channel_id=1, source_target_pairs={{0,17},{1,16},{2,19},{3,18},{4,21},{5,20},{6,23},{7,22},{8,25},{9,... | collective-permute-start | bytes 589832 | tf_op jit(solution)/shard_map/ppermute | solution.py:87
  16.9 0.8 %collective-permute-done.3.refs_0_.refs_1_ = bf16[128,768]{1,0:T(8,128)(2,1)S(1)} collective-permute-done((bf16[128,768]{1,0:T(8,128)(2,1)S(1)}, bf16[128,768]{1,0:T(8,128)(2,1)S(1)}, u32[]{:S(2)}, u32[]{:S(2)}) %collective-permute-start.3) | collective-permute-done | bytes 196640 | tf_op jit(solution)/shard_map/ppermute | solution.py:77
  17.7 1.3 %shard_map.63 = (bf16[128,768]{1,0:T(8,128)(2,1)S(1)}, bf16[144,128]{1,0:T(8,128)(2,1)S(1)}) custom-call(bf16[128,768]{1,0:T(8,128)(2,1)S(1)} %collective-permute-done.3.refs_0_.refs_1_, bf16[1024,768]{1,0:T(8,128)(2,1)S(1)} %get-tuple-element.20.refs_6_.refs_1_, bf16[16,768]{1,0:T(8,128)(2,1)S(1)} %shard_map.60.refs_5_.refs_2_, ...), custom_call_target="tpu_custom_call" | custom-call | flops 402653184 | tf_op jit(solution)/shard_map/pallas_call | solution.py:96
  19.0 2.3 %collective-permute-start.4 = (bf16[128,768]{1,0:T(8,128)(2,1)S(1)}, bf16[128,768]{1,0:T(8,128)(2,1)S(1)}, u32[]{:S(2)}, u32[]{:S(2)}) collective-permute-start(bf16[128,768]{1,0:T(8,128)(2,1)S(1)} %get-tuple-element.23), channel_id=1, source_target_pairs={{0,1},{1,0},{2,3},{3,2},{4,5},{5,4},{6,7},{7,6},{8,9},{9,8},{10,11... | collective-permute-start | bytes 589832 | tf_op jit(solution)/shard_map/ppermute | solution.py:77
  21.3 0.6 %shard_map.64 = (f32[1024,768]{1,0:T(8,128)S(1)}, bf16[400,768]{1,0:T(8,128)(2,1)S(1)}) custom-call(bf16[128,768]{1,0:T(8,128)(2,1)S(1)} %get-tuple-element.21.refs_0_, bf16[128,768]{1,0:T(8,128)(2,1)S(1)} %collective-permute-done.3.refs_0_.refs_1_, bf16[144,128]{1,0:T(8,128)(2,1)S(1)} %get-tuple-element.24.refs_2_, ...), custom_call_target="tpu_custom_call" | custom-call | flops 402653184 | tf_op jit(solution)/shard_map/pallas_call | solution.py:96
  22.0 1.7 %collective-permute-done.9.refs_1_ = bf16[128,768]{1,0:T(8,128)(2,1)S(1)} collective-permute-done((bf16[128,768]{1,0:T(8,128)(2,1)S(1)}, bf16[128,768]{1,0:T(8,128)(2,1)S(1)}, u32[]{:S(2)}, u32[]{:S(2)}) %collective-permute-start.9) | collective-permute-done | bytes 196640 | tf_op jit(solution)/shard_map/ppermute | solution.py:87
  23.9 3.2 %collective-permute-done.4.refs_2_ = bf16[128,768]{1,0:T(8,128)(2,1)S(1)} collective-permute-done((bf16[128,768]{1,0:T(8,128)(2,1)S(1)}, bf16[128,768]{1,0:T(8,128)(2,1)S(1)}, u32[]{:S(2)}, u32[]{:S(2)}) %collective-permute-start.4) | collective-permute-done | bytes 196640 | tf_op jit(solution)/shard_map/ppermute | solution.py:77
  27.1 0.3 collective-permute-start.5
  27.4 3.4 %collective-permute-start.6 = (bf16[32,768]{1,0:T(8,128)(2,1)S(1)}, bf16[32,768]{1,0:T(8,128)(2,1)S(1)}, u32[]{:S(2)}, u32[]{:S(2)}) collective-permute-start(bf16[32,768]{1,0:T(8,128)(2,1)S(1)} %get-tuple-element.29), channel_id=1, source_target_pairs={{0,4},{1,5},{2,6},{3,7},{4,0},{5,1},{6,2},{7,3},{8,12},{9,13},{10,... | collective-permute-start | bytes 147464 | tf_op jit(solution)/shard_map/ppermute | solution.py:77
  30.8 0.8 %collective-permute-start.7 = (bf16[32,768]{1,0:T(8,128)(2,1)S(1)}, bf16[32,768]{1,0:T(8,128)(2,1)S(1)}, u32[]{:S(2)}, u32[]{:S(2)}) collective-permute-start(bf16[32,768]{1,0:T(8,128)(2,1)S(1)} %get-tuple-element.30), channel_id=1, source_target_pairs={{0,6},{1,7},{2,4},{3,5},{4,2},{5,3},{6,0},{7,1},{8,14},{9,15},{10,... | collective-permute-start | bytes 147464 | tf_op jit(solution)/shard_map/ppermute | solution.py:77
  31.5 1.9 %shard_map.67.refs_1_ = f32[1024,768]{1,0:T(8,128)S(1)} custom-call(bf16[272,768]{1,0:T(8,128)(2,1)S(1)} %shard_map.66.refs_0_, bf16[1024,768]{1,0:T(8,128)(2,1)S(1)} %get-tuple-element.20.refs_6_.refs_1_, f32[1024,768]{1,0:T(8,128)S(1)} %get-tuple-element.26.refs_3_.refs_2_), custom_call_target="tpu_custom_call" | custom-call | flops 8053063680 | tf_op jit(solution)/shard_map/pallas_call | solution.py:96
  33.5 0.6 %shard_map.68.refs_2_ = f32[1024,768]{1,0:T(8,128)S(1)} custom-call(bf16[400,768]{1,0:T(8,128)(2,1)S(1)} %collective-permute-done.11.refs_0_, f32[1024,768]{1,0:T(8,128)S(1)} %shard_map.67.refs_1_), custom_call_target="tpu_custom_call" | custom-call | flops 402653184 | tf_op jit(solution)/shard_map/pallas_call | solution.py:96
  34.0 2.7 %shard_map.69 = (bf16[1024,768]{1,0:T(8,128)(2,1)}, s32[1,128]{1,0:T(1,128)S(1)}) custom-call(bf16[272,768]{1,0:T(8,128)(2,1)S(1)} %collective-permute-done.10.refs_0_, bf16[1024,768]{1,0:T(8,128)(2,1)S(1)} %get-tuple-element.20.refs_6_.refs_1_, f32[1024,768]{1,0:T(8,128)S(1)} %shard_map.68.refs_2_), custom_call_target="tpu_custom_call" | custom-call | tf_op jit(solution)/shard_map/pallas_call | solution.py:259
  36.8 0.7 %shard_map.70 = f32[32,768]{1,0:T(8,128)} custom-call(f32[32,768]{1,0:T(8,128)S(1)} %get-tuple-element.27.refs_0_, bf16[32,768]{1,0:T(8,128)(2,1)S(1)} %collective-permute-done.5.refs_1_, bf16[32,768]{1,0:T(8,128)(2,1)S(1)} %collective-permute-done.6.refs_2_, bf16[32,768]{1,0:T(8,128)(2,1)S(1)} %collective-permute-done.7.refs_3_, ...), custom_call_target="tpu_custom_call" | custom-call | tf_op jit(solution)/shard_map/pallas_call | solution.py:96
  (17 shorter events, 0.7 us)
Async XLA Ops:
  0.6 8.9 %collective-permute-start = (bf16[32,768]{1,0:T(8,128)(2,1)}, bf16[32,768]{1,0:T(8,128)(2,1)S(1)}, u32[]{:S(2)}, u32[]{:S(2)}) collective-permute-start(bf16[32,768]{1,0:T(8,128)(2,1)} %refs_0_.1), channel_id=1, source_target_pairs={{0,2},{1,3},{2,0},{3,1},{4,6},{5,7},{6,4},{7,5},{8,10},{9,11},{10,... | collective-permute-start | bytes 147464 | tf_op jit(solution)/shard_map/ppermute | solution.py:77
  3.7 6.7 %collective-permute-start.2 = (bf16[32,768]{1,0:T(8,128)(2,1)}, bf16[32,768]{1,0:T(8,128)(2,1)S(1)}, u32[]{:S(2)}, u32[]{:S(2)}) collective-permute-start(bf16[32,768]{1,0:T(8,128)(2,1)} %refs_0_.1), channel_id=1, source_target_pairs={{0,6},{1,7},{2,4},{3,5},{4,2},{5,3},{6,0},{7,1},{8,14},{9,15},{10,... | collective-permute-start | bytes 147464 | tf_op jit(solution)/shard_map/ppermute | solution.py:77
  6.2 5.7 %collective-permute-start.1 = (bf16[32,768]{1,0:T(8,128)(2,1)}, bf16[32,768]{1,0:T(8,128)(2,1)S(1)}, u32[]{:S(2)}, u32[]{:S(2)}) collective-permute-start(bf16[32,768]{1,0:T(8,128)(2,1)} %refs_0_.1), channel_id=1, source_target_pairs={{0,4},{1,5},{2,6},{3,7},{4,0},{5,1},{6,2},{7,3},{8,12},{9,13},{10,... | collective-permute-start | bytes 147464 | tf_op jit(solution)/shard_map/ppermute | solution.py:77
  7.0 1.4 %copy-start = (bf16[1024,768]{1,0:T(8,128)(2,1)S(1)}, bf16[1024,768]{1,0:T(8,128)(2,1)}, u32[]{:S(2)}) copy-start(bf16[1024,768]{1,0:T(8,128)(2,1)} %refs_1_.1) | copy-start | bytes 4718596
  8.4 0.8 %copy-start.1 = (bf16[32,768]{1,0:T(8,128)(2,1)S(1)}, bf16[32,768]{1,0:T(8,128)(2,1)}, u32[]{:S(2)}) copy-start(bf16[32,768]{1,0:T(8,128)(2,1)} %refs_0_.1) | copy-start | bytes 147460
  12.0 5.7 %collective-permute-start.3 = (bf16[128,768]{1,0:T(8,128)(2,1)S(1)}, bf16[128,768]{1,0:T(8,128)(2,1)S(1)}, u32[]{:S(2)}, u32[]{:S(2)}) collective-permute-start(bf16[128,768]{1,0:T(8,128)(2,1)S(1)} %get-tuple-element.21.refs_0_), channel_id=1, source_target_pairs={{0,1},{1,0},{2,3},{3,2},{4,5},{5,4},{6,7},{7,6},{8,9},{9,8},{10,11... | collective-permute-start | bytes 589832 | tf_op jit(solution)/shard_map/ppermute | solution.py:77
  13.5 10.2 %collective-permute-start.8 = (bf16[144,768]{1,0:T(8,128)(2,1)S(1)}, bf16[144,768]{1,0:T(8,128)(2,1)S(1)}, u32[]{:S(2)}, u32[]{:S(2)}) collective-permute-start(bf16[144,768]{1,0:T(8,128)(2,1)S(1)} %get-tuple-element.31), channel_id=1, source_target_pairs={{0,16},{8,24},{16,0},{24,8},{1,17},{9,25},{17,1},{25,9},{2,18},{10... | collective-permute-start | bytes 663560 | tf_op jit(solution)/shard_map/ppermute | solution.py:77
  16.4 7.4 %collective-permute-start.9 = (bf16[128,768]{1,0:T(8,128)(2,1)S(1)}, bf16[128,768]{1,0:T(8,128)(2,1)S(1)}, u32[]{:S(2)}, u32[]{:S(2)}) collective-permute-start(bf16[128,768]{1,0:T(8,128)(2,1)S(1)} %get-tuple-element.32), channel_id=1, source_target_pairs={{0,17},{1,16},{2,19},{3,18},{4,21},{5,20},{6,23},{7,22},{8,25},{9,... | collective-permute-start | bytes 589832 | tf_op jit(solution)/shard_map/ppermute | solution.py:87
  19.0 8.0 %collective-permute-start.4 = (bf16[128,768]{1,0:T(8,128)(2,1)S(1)}, bf16[128,768]{1,0:T(8,128)(2,1)S(1)}, u32[]{:S(2)}, u32[]{:S(2)}) collective-permute-start(bf16[128,768]{1,0:T(8,128)(2,1)S(1)} %get-tuple-element.23), channel_id=1, source_target_pairs={{0,1},{1,0},{2,3},{3,2},{4,5},{5,4},{6,7},{7,6},{8,9},{9,8},{10,11... | collective-permute-start | bytes 589832 | tf_op jit(solution)/shard_map/ppermute | solution.py:77
  21.9 11.5 %collective-permute-start.11 = (bf16[400,768]{1,0:T(8,128)(2,1)S(1)}, bf16[400,768]{1,0:T(8,128)(2,1)S(1)}, u32[]{:S(2)}, u32[]{:S(2)}) collective-permute-start(bf16[400,768]{1,0:T(8,128)(2,1)S(1)} %get-tuple-element.33), channel_id=1, source_target_pairs={{0,8},{8,0},{16,24},{24,16},{1,9},{9,1},{17,25},{25,17},{2,10},{10... | collective-permute-start | bytes 1843208 | tf_op jit(solution)/shard_map/ppermute | solution.py:77
  23.8 10.3 %collective-permute-start.10 = (bf16[272,768]{1,0:T(8,128)(2,1)S(1)}, bf16[272,768]{1,0:T(8,128)(2,1)S(1)}, u32[]{:S(2)}, u32[]{:S(2)}) collective-permute-start(bf16[272,768]{1,0:T(8,128)(2,1)S(1)} %shard_map.66.refs_0_), channel_id=1, source_target_pairs={{0,8},{8,0},{16,24},{24,16},{1,9},{9,1},{17,25},{25,17},{2,10},{10... | collective-permute-start | bytes 1253384 | tf_op jit(solution)/shard_map/ppermute | solution.py:77
  27.1 9.7 %collective-permute-start.5 = (bf16[32,768]{1,0:T(8,128)(2,1)S(1)}, bf16[32,768]{1,0:T(8,128)(2,1)S(1)}, u32[]{:S(2)}, u32[]{:S(2)}) collective-permute-start(bf16[32,768]{1,0:T(8,128)(2,1)S(1)} %get-tuple-element.28), channel_id=1, source_target_pairs={{0,2},{1,3},{2,0},{3,1},{4,6},{5,7},{6,4},{7,5},{8,10},{9,11},{10,... | collective-permute-start | bytes 147464 | tf_op jit(solution)/shard_map/ppermute | solution.py:77
  27.4 9.4 %collective-permute-start.6 = (bf16[32,768]{1,0:T(8,128)(2,1)S(1)}, bf16[32,768]{1,0:T(8,128)(2,1)S(1)}, u32[]{:S(2)}, u32[]{:S(2)}) collective-permute-start(bf16[32,768]{1,0:T(8,128)(2,1)S(1)} %get-tuple-element.29), channel_id=1, source_target_pairs={{0,4},{1,5},{2,6},{3,7},{4,0},{5,1},{6,2},{7,3},{8,12},{9,13},{10,... | collective-permute-start | bytes 147464 | tf_op jit(solution)/shard_map/ppermute | solution.py:77
  30.8 6.0 %collective-permute-start.7 = (bf16[32,768]{1,0:T(8,128)(2,1)S(1)}, bf16[32,768]{1,0:T(8,128)(2,1)S(1)}, u32[]{:S(2)}, u32[]{:S(2)}) collective-permute-start(bf16[32,768]{1,0:T(8,128)(2,1)S(1)} %get-tuple-element.30), channel_id=1, source_target_pairs={{0,6},{1,7},{2,4},{3,5},{4,2},{5,3},{6,0},{7,1},{8,14},{9,15},{10,... | collective-permute-start | bytes 147464 | tf_op jit(solution)/shard_map/ppermute | solution.py:77

commit v13 on v12

--- a/solution.py
+++ b/solution.py
@@ -350,14 +350,6 @@
         work,
     )
     mate = swap(own, "pb", 1)
-    kept, *terms = local_call(
-        fold_body,
-        [like(q_home, width, f32)] + [like(q_home, width, bf16)] * (homes // 2 - 1),
-        [place, near_dq, came],
-        0,
-        [acc],
-    )
-    terms = [swap(term, "lab", 2 * step) for step, term in enumerate(terms, 1)]
     cross = local_call(
         stack_body, [like(qcount + NOTE, width, bf16)], [cross_near, cross_far], 0, []
     )[0]
@@ -365,6 +357,14 @@
     grown = like(lab_dev, width, f32)
     acc = local_call(cross_body, [grown], [cross, weights, acc], 20 * work)[0]
     acc = local_call(mate_body, [grown], [mate, acc], work)[0]
+    kept, *terms = local_call(
+        fold_body,
+        [like(q_home, width, f32)] + [like(q_home, width, bf16)] * (homes // 2 - 1),
+        [place, near_dq, came],
+        0,
+        [acc],
+    )
+    terms = [swap(term, "lab", 2 * step) for step, term in enumerate(terms, 1)]
     weight_grad, mark = late(groups, cross_mate, weights, acc)
     query_grad = local_call(
         sum_body, [like(q_home, width, f32)], [kept, *terms], 0, [mark]

time: 37.7 us -> 37.5 us (level)
  waiting for transfers between devices: 8.12 us -> 6.85 us
  starting transfers between devices: 16.2 us -> 17.3 us
    ppermute x1, waiting for transfers between devices: 1.74 us -> 0.66 us  [diagonal(): return lax.ppermute(value, ('pb', 'lab'), pairs)]
    ppermute x11, starting transfers between devices: 15.7 us -> 16.7 us  [swap(): return lax.ppermute(value, axis, [(i, i ^ bit) for i in range(count)])]
  transfers between devices with their start and end apart: 12 -> 12, of which waited for: 5 -> 6; matrix products, arithmetic and copies ran while one was open for 2% -> 2% of each run, Pallas kernels for 23% -> 24%
where the time goes in v13:
time: 37.5 us; the launch traced here: 37.3 us
  starting transfers between devices  17.3 us (46%)
  Pallas kernels  9.47 us (25%)
  waiting for transfers between devices  6.85 us (18%)
  local copies, waits for them, and re-layouts  2.21 us (6%)
  between operations  0.75 us (2%)
  other arithmetic  0.72 us (2%)
    ppermute x11, starting transfers between devices, swap(): return lax.ppermute(value, axis, [(i, i ^ bit) for i in range(count)])  16.7 us
    pallas_call x11, Pallas kernels, local_call(): pl.pallas_call(lambda *refs: body(*refs[:given], *refs[later:]), out_shap...  6.75 us
    ppermute x11, waiting for transfers between devices, swap(): return lax.ppermute(value, axis, [(i, i ^ bit) for i in range(count)])  6.19 us
    pallas_call x1, Pallas kernels, late(): pl.pallas_call(lambda *refs: late_body(groups, *refs), out_shape=[out, li...  2.71 us
    unnamed x4, local copies, waits for them, and re-layouts  2.21 us
  transfers between devices with their start and end apart: 12, of which 6 were waited for; matrix products, arithmetic and copies ran while one was open for 2% of the time, Pallas kernels for 24%

profile of v13, /device:TPU:0, one launch (start us, length us, event | category | flops | bytes accessed | tf_op | source)
XLA Modules:
  0.0 37.3 jit_solution(13760457195384817958)
XLA Ops:
  0.6 3.1 %collective-permute-start = (bf16[32,768]{1,0:T(8,128)(2,1)}, bf16[32,768]{1,0:T(8,128)(2,1)S(1)}, u32[]{:S(2)}, u32[]{:S(2)}) collective-permute-start(bf16[32,768]{1,0:T(8,128)(2,1)} %refs_0_.1), channel_id=1, source_target_pairs={{0,2},{1,3},{2,0},{3,1},{4,6},{5,7},{6,4},{7,5},{8,10},{9,11},{10,... | collective-permute-start | bytes 147464 | tf_op jit(solution)/shard_map/ppermute | solution.py:77
  3.7 2.6 %collective-permute-start.1 = (bf16[32,768]{1,0:T(8,128)(2,1)}, bf16[32,768]{1,0:T(8,128)(2,1)S(1)}, u32[]{:S(2)}, u32[]{:S(2)}) collective-permute-start(bf16[32,768]{1,0:T(8,128)(2,1)} %refs_0_.1), channel_id=1, source_target_pairs={{0,4},{1,5},{2,6},{3,7},{4,0},{5,1},{6,2},{7,3},{8,12},{9,13},{10,... | collective-permute-start | bytes 147464 | tf_op jit(solution)/shard_map/ppermute | solution.py:77
  6.3 0.7 %add_convert_fusion.refs_1_ = f32[9,256]{1,0:T(8,128)S(1)} fusion(s32[1,256]{1,0:T(1,128)} %bitcast.5, s32[8,256]{1,0:T(8,128)} %bitcast.4), kind=kLoop, calls=%fused_computation | loop fusion | flops 4608 | bytes 18432 | tf_op jit(solution)/shard_map/convert_element_type | solution.py:314
  7.0 1.4 %copy-done = bf16[1024,768]{1,0:T(8,128)(2,1)S(1)} copy-done((bf16[1024,768]{1,0:T(8,128)(2,1)S(1)}, bf16[1024,768]{1,0:T(8,128)(2,1)}, u32[]{:S(2)}) %copy-start) | copy-done | bytes 1572888
  8.4 0.8 %copy-done.1 = bf16[32,768]{1,0:T(8,128)(2,1)S(1)} copy-done((bf16[32,768]{1,0:T(8,128)(2,1)S(1)}, bf16[32,768]{1,0:T(8,128)(2,1)}, u32[]{:S(2)}) %copy-start.1) | copy-done | bytes 49176
  9.5 0.3 collective-permute-done.1.refs_3_
  9.9 2.6 %collective-permute-done.2.refs_4_ = bf16[32,768]{1,0:T(8,128)(2,1)S(1)} collective-permute-done((bf16[32,768]{1,0:T(8,128)(2,1)}, bf16[32,768]{1,0:T(8,128)(2,1)S(1)}, u32[]{:S(2)}, u32[]{:S(2)}) %collective-permute-start.2) | collective-permute-done | bytes 49184 | tf_op jit(solution)/shard_map/ppermute | solution.py:77
  12.4 1.6 %collective-permute-start.3 = (bf16[128,768]{1,0:T(8,128)(2,1)S(1)}, bf16[128,768]{1,0:T(8,128)(2,1)S(1)}, u32[]{:S(2)}, u32[]{:S(2)}) collective-permute-start(bf16[128,768]{1,0:T(8,128)(2,1)S(1)} %get-tuple-element.21.refs_0_), channel_id=1, source_target_pairs={{0,1},{1,0},{2,3},{3,2},{4,5},{5,4},{6,7},{7,6},{8,9},{9,8},{10,11... | collective-permute-start | bytes 589832 | tf_op jit(solution)/shard_map/ppermute | solution.py:77
  14.0 1.5 %collective-permute-start.6 = (bf16[144,768]{1,0:T(8,128)(2,1)S(1)}, bf16[144,768]{1,0:T(8,128)(2,1)S(1)}, u32[]{:S(2)}, u32[]{:S(2)}) collective-permute-start(bf16[144,768]{1,0:T(8,128)(2,1)S(1)} %get-tuple-element.27), channel_id=1, source_target_pairs={{0,16},{8,24},{16,0},{24,8},{1,17},{9,25},{17,1},{25,9},{2,18},{10... | collective-permute-start | bytes 663560 | tf_op jit(solution)/shard_map/ppermute | solution.py:77
  15.5 1.3 %shard_map.62 = (f32[128,768]{1,0:T(8,128)S(1)}, bf16[144,128]{1,0:T(8,128)(2,1)S(1)}, bf16[128,768]{1,0:T(8,128)(2,1)S(1)}) custom-call(bf16[128,768]{1,0:T(8,128)(2,1)S(1)} %get-tuple-element.21.refs_0_, bf16[1024,768]{1,0:T(8,128)(2,1)S(1)} %get-tuple-element.20.refs_6_.refs_1_, bf16[16,768]{1,0:T(8,128)(2,1)S(1)} %shard_map.60.refs_5_.refs_2_), custom_call_target="tpu_custom_call" | custom-call | flops 402653184 | tf_op jit(solution)/shard_map/pallas_call | solution.py:96
  16.9 0.5 %collective-permute-start.7 = (bf16[128,768]{1,0:T(8,128)(2,1)S(1)}, bf16[128,768]{1,0:T(8,128)(2,1)S(1)}, u32[]{:S(2)}, u32[]{:S(2)}) collective-permute-start(bf16[128,768]{1,0:T(8,128)(2,1)S(1)} %get-tuple-element.28), channel_id=1, source_target_pairs={{0,17},{1,16},{2,19},{3,18},{4,21},{5,20},{6,23},{7,22},{8,25},{9,... | collective-permute-start | bytes 589832 | tf_op jit(solution)/shard_map/ppermute | solution.py:87
  17.4 1.2 %collective-permute-done.3.refs_0_.refs_1_ = bf16[128,768]{1,0:T(8,128)(2,1)S(1)} collective-permute-done((bf16[128,768]{1,0:T(8,128)(2,1)S(1)}, bf16[128,768]{1,0:T(8,128)(2,1)S(1)}, u32[]{:S(2)}, u32[]{:S(2)}) %collective-permute-start.3) | collective-permute-done | bytes 196640 | tf_op jit(solution)/shard_map/ppermute | solution.py:77
  18.6 1.3 %shard_map.63 = (bf16[128,768]{1,0:T(8,128)(2,1)S(1)}, bf16[144,128]{1,0:T(8,128)(2,1)S(1)}) custom-call(bf16[128,768]{1,0:T(8,128)(2,1)S(1)} %collective-permute-done.3.refs_0_.refs_1_, bf16[1024,768]{1,0:T(8,128)(2,1)S(1)} %get-tuple-element.20.refs_6_.refs_1_, bf16[16,768]{1,0:T(8,128)(2,1)S(1)} %shard_map.60.refs_5_.refs_2_, ...), custom_call_target="tpu_custom_call" | custom-call | flops 402653184 | tf_op jit(solution)/shard_map/pallas_call | solution.py:96
  19.9 3.0 %collective-permute-start.4 = (bf16[128,768]{1,0:T(8,128)(2,1)S(1)}, bf16[128,768]{1,0:T(8,128)(2,1)S(1)}, u32[]{:S(2)}, u32[]{:S(2)}) collective-permute-start(bf16[128,768]{1,0:T(8,128)(2,1)S(1)} %get-tuple-element.23), channel_id=1, source_target_pairs={{0,1},{1,0},{2,3},{3,2},{4,5},{5,4},{6,7},{7,6},{8,9},{9,8},{10,11... | collective-permute-start | bytes 589832 | tf_op jit(solution)/shard_map/ppermute | solution.py:77
  22.9 0.6 %shard_map.64 = (f32[1024,768]{1,0:T(8,128)S(1)}, bf16[400,768]{1,0:T(8,128)(2,1)S(1)}) custom-call(bf16[128,768]{1,0:T(8,128)(2,1)S(1)} %get-tuple-element.21.refs_0_, bf16[128,768]{1,0:T(8,128)(2,1)S(1)} %collective-permute-done.3.refs_0_.refs_1_, bf16[144,128]{1,0:T(8,128)(2,1)S(1)} %get-tuple-element.24.refs_2_, ...), custom_call_target="tpu_custom_call" | custom-call | flops 402653184 | tf_op jit(solution)/shard_map/pallas_call | solution.py:96
  23.5 0.7 %collective-permute-done.7.refs_1_ = bf16[128,768]{1,0:T(8,128)(2,1)S(1)} collective-permute-done((bf16[128,768]{1,0:T(8,128)(2,1)S(1)}, bf16[128,768]{1,0:T(8,128)(2,1)S(1)}, u32[]{:S(2)}, u32[]{:S(2)}) %collective-permute-start.7) | collective-permute-done | bytes 196640 | tf_op jit(solution)/shard_map/ppermute | solution.py:87
  24.3 1.9 %shard_map.66.refs_1_ = f32[1024,768]{1,0:T(8,128)S(1)} custom-call(bf16[272,768]{1,0:T(8,128)(2,1)S(1)} %shard_map.65.refs_0_, bf16[1024,768]{1,0:T(8,128)(2,1)S(1)} %get-tuple-element.20.refs_6_.refs_1_, f32[1024,768]{1,0:T(8,128)S(1)} %get-tuple-element.29.refs_2_), custom_call_target="tpu_custom_call" | custom-call | flops 8053063680 | tf_op jit(solution)/shard_map/pallas_call | solution.py:96
  26.2 0.6 %shard_map.67.refs_3_.refs_2_ = f32[1024,768]{1,0:T(8,128)S(1)} custom-call(bf16[400,768]{1,0:T(8,128)(2,1)S(1)} %collective-permute-done.5.refs_0_, f32[1024,768]{1,0:T(8,128)S(1)} %shard_map.66.refs_1_), custom_call_target="tpu_custom_call" | custom-call | flops 402653184 | tf_op jit(solution)/shard_map/pallas_call | solution.py:96
  26.8 0.3 collective-permute-done.4.refs_2_
  27.2 3.4 %collective-permute-start.9 = (bf16[32,768]{1,0:T(8,128)(2,1)S(1)}, bf16[32,768]{1,0:T(8,128)(2,1)S(1)}, u32[]{:S(2)}, u32[]{:S(2)}) collective-permute-start(bf16[32,768]{1,0:T(8,128)(2,1)S(1)} %get-tuple-element.32), channel_id=1, source_target_pairs={{0,4},{1,5},{2,6},{3,7},{4,0},{5,1},{6,2},{7,3},{8,12},{9,13},{10,... | collective-permute-start | bytes 147464 | tf_op jit(solution)/shard_map/ppermute | solution.py:77
  30.6 1.4 %collective-permute-start.10 = (bf16[32,768]{1,0:T(8,128)(2,1)S(1)}, bf16[32,768]{1,0:T(8,128)(2,1)S(1)}, u32[]{:S(2)}, u32[]{:S(2)}) collective-permute-start(bf16[32,768]{1,0:T(8,128)(2,1)S(1)} %get-tuple-element.33), channel_id=1, source_target_pairs={{0,6},{1,7},{2,4},{3,5},{4,2},{5,3},{6,0},{7,1},{8,14},{9,15},{10,... | collective-permute-start | bytes 147464 | tf_op jit(solution)/shard_map/ppermute | solution.py:77
  32.0 2.7 %shard_map.69 = (bf16[1024,768]{1,0:T(8,128)(2,1)}, s32[1,128]{1,0:T(1,128)S(1)}) custom-call(bf16[272,768]{1,0:T(8,128)(2,1)S(1)} %collective-permute-done.11.refs_0_, bf16[1024,768]{1,0:T(8,128)(2,1)S(1)} %get-tuple-element.20.refs_6_.refs_1_, f32[1024,768]{1,0:T(8,128)S(1)} %shard_map.67.refs_3_.refs_2_), custom_call_target="tpu_custom_call" | custom-call | tf_op jit(solution)/shard_map/pallas_call | solution.py:259
  34.7 1.9 %collective-permute-done.10.refs_3_ = bf16[32,768]{1,0:T(8,128)(2,1)S(1)} collective-permute-done((bf16[32,768]{1,0:T(8,128)(2,1)S(1)}, bf16[32,768]{1,0:T(8,128)(2,1)S(1)}, u32[]{:S(2)}, u32[]{:S(2)}) %collective-permute-start.10) | collective-permute-done | bytes 49184 | tf_op jit(solution)/shard_map/ppermute | solution.py:77
  36.6 0.7 %shard_map.70 = f32[32,768]{1,0:T(8,128)} custom-call(f32[32,768]{1,0:T(8,128)S(1)} %get-tuple-element.30.refs_0_, bf16[32,768]{1,0:T(8,128)(2,1)S(1)} %collective-permute-done.8.refs_1_, bf16[32,768]{1,0:T(8,128)(2,1)S(1)} %collective-permute-done.9.refs_2_, bf16[32,768]{1,0:T(8,128)(2,1)S(1)} %collective-permute-done.10.refs_3_, ...), custom_call_target="tpu_custom_call" | custom-call | tf_op jit(solution)/shard_map/pallas_call | solution.py:96
  (17 shorter events, 0.6 us)
Async XLA Ops:
  0.6 8.9 %collective-permute-start = (bf16[32,768]{1,0:T(8,128)(2,1)}, bf16[32,768]{1,0:T(8,128)(2,1)S(1)}, u32[]{:S(2)}, u32[]{:S(2)}) collective-permute-start(bf16[32,768]{1,0:T(8,128)(2,1)} %refs_0_.1), channel_id=1, source_target_pairs={{0,2},{1,3},{2,0},{3,1},{4,6},{5,7},{6,4},{7,5},{8,10},{9,11},{10,... | collective-permute-start | bytes 147464 | tf_op jit(solution)/shard_map/ppermute | solution.py:77
  3.7 6.1 %collective-permute-start.1 = (bf16[32,768]{1,0:T(8,128)(2,1)}, bf16[32,768]{1,0:T(8,128)(2,1)S(1)}, u32[]{:S(2)}, u32[]{:S(2)}) collective-permute-start(bf16[32,768]{1,0:T(8,128)(2,1)} %refs_0_.1), channel_id=1, source_target_pairs={{0,4},{1,5},{2,6},{3,7},{4,0},{5,1},{6,2},{7,3},{8,12},{9,13},{10,... | collective-permute-start | bytes 147464 | tf_op jit(solution)/shard_map/ppermute | solution.py:77
  6.3 6.1 %collective-permute-start.2 = (bf16[32,768]{1,0:T(8,128)(2,1)}, bf16[32,768]{1,0:T(8,128)(2,1)S(1)}, u32[]{:S(2)}, u32[]{:S(2)}) collective-permute-start(bf16[32,768]{1,0:T(8,128)(2,1)} %refs_0_.1), channel_id=1, source_target_pairs={{0,6},{1,7},{2,4},{3,5},{4,2},{5,3},{6,0},{7,1},{8,14},{9,15},{10,... | collective-permute-start | bytes 147464 | tf_op jit(solution)/shard_map/ppermute | solution.py:77
  7.0 1.4 %copy-start = (bf16[1024,768]{1,0:T(8,128)(2,1)S(1)}, bf16[1024,768]{1,0:T(8,128)(2,1)}, u32[]{:S(2)}) copy-start(bf16[1024,768]{1,0:T(8,128)(2,1)} %refs_1_.1) | copy-start | bytes 4718596
  8.4 0.8 %copy-start.1 = (bf16[32,768]{1,0:T(8,128)(2,1)S(1)}, bf16[32,768]{1,0:T(8,128)(2,1)}, u32[]{:S(2)}) copy-start(bf16[32,768]{1,0:T(8,128)(2,1)} %refs_0_.1) | copy-start | bytes 147460
  12.4 6.1 %collective-permute-start.3 = (bf16[128,768]{1,0:T(8,128)(2,1)S(1)}, bf16[128,768]{1,0:T(8,128)(2,1)S(1)}, u32[]{:S(2)}, u32[]{:S(2)}) collective-permute-start(bf16[128,768]{1,0:T(8,128)(2,1)S(1)} %get-tuple-element.21.refs_0_), channel_id=1, source_target_pairs={{0,1},{1,0},{2,3},{3,2},{4,5},{5,4},{6,7},{7,6},{8,9},{9,8},{10,11... | collective-permute-start | bytes 589832 | tf_op jit(solution)/shard_map/ppermute | solution.py:77
  14.0 10.2 %collective-permute-start.6 = (bf16[144,768]{1,0:T(8,128)(2,1)S(1)}, bf16[144,768]{1,0:T(8,128)(2,1)S(1)}, u32[]{:S(2)}, u32[]{:S(2)}) collective-permute-start(bf16[144,768]{1,0:T(8,128)(2,1)S(1)} %get-tuple-element.27), channel_id=1, source_target_pairs={{0,16},{8,24},{16,0},{24,8},{1,17},{9,25},{17,1},{25,9},{2,18},{10... | collective-permute-start | bytes 663560 | tf_op jit(solution)/shard_map/ppermute | solution.py:77
  16.9 7.3 %collective-permute-start.7 = (bf16[128,768]{1,0:T(8,128)(2,1)S(1)}, bf16[128,768]{1,0:T(8,128)(2,1)S(1)}, u32[]{:S(2)}, u32[]{:S(2)}) collective-permute-start(bf16[128,768]{1,0:T(8,128)(2,1)S(1)} %get-tuple-element.28), channel_id=1, source_target_pairs={{0,17},{1,16},{2,19},{3,18},{4,21},{5,20},{6,23},{7,22},{8,25},{9,... | collective-permute-start | bytes 589832 | tf_op jit(solution)/shard_map/ppermute | solution.py:87
  19.9 7.2 %collective-permute-start.4 = (bf16[128,768]{1,0:T(8,128)(2,1)S(1)}, bf16[128,768]{1,0:T(8,128)(2,1)S(1)}, u32[]{:S(2)}, u32[]{:S(2)}) collective-permute-start(bf16[128,768]{1,0:T(8,128)(2,1)S(1)} %get-tuple-element.23), channel_id=1, source_target_pairs={{0,1},{1,0},{2,3},{3,2},{4,5},{5,4},{6,7},{7,6},{8,9},{9,8},{10,11... | collective-permute-start | bytes 589832 | tf_op jit(solution)/shard_map/ppermute | solution.py:77
  23.4 2.8 %collective-permute-start.5 = (bf16[400,768]{1,0:T(8,128)(2,1)S(1)}, bf16[400,768]{1,0:T(8,128)(2,1)S(1)}, u32[]{:S(2)}, u32[]{:S(2)}) collective-permute-start(bf16[400,768]{1,0:T(8,128)(2,1)S(1)} %get-tuple-element.26), channel_id=1, source_target_pairs={{0,8},{8,0},{16,24},{24,16},{1,9},{9,1},{17,25},{25,17},{2,10},{10... | collective-permute-start | bytes 1843208 | tf_op jit(solution)/shard_map/ppermute | solution.py:77
  24.2 7.8 %collective-permute-start.11 = (bf16[272,768]{1,0:T(8,128)(2,1)S(1)}, bf16[272,768]{1,0:T(8,128)(2,1)S(1)}, u32[]{:S(2)}, u32[]{:S(2)}) collective-permute-start(bf16[272,768]{1,0:T(8,128)(2,1)S(1)} %shard_map.65.refs_0_), channel_id=1, source_target_pairs={{0,8},{8,0},{16,24},{24,16},{1,9},{9,1},{17,25},{25,17},{2,10},{10... | collective-permute-start | bytes 1253384 | tf_op jit(solution)/shard_map/ppermute | solution.py:77
  27.1 7.6 %collective-permute-start.8 = (bf16[32,768]{1,0:T(8,128)(2,1)S(1)}, bf16[32,768]{1,0:T(8,128)(2,1)S(1)}, u32[]{:S(2)}, u32[]{:S(2)}) collective-permute-start(bf16[32,768]{1,0:T(8,128)(2,1)S(1)} %get-tuple-element.31), channel_id=1, source_target_pairs={{0,2},{1,3},{2,0},{3,1},{4,6},{5,7},{6,4},{7,5},{8,10},{9,11},{10,... | collective-permute-start | bytes 147464 | tf_op jit(solution)/shard_map/ppermute | solution.py:77
  27.2 7.5 %collective-permute-start.9 = (bf16[32,768]{1,0:T(8,128)(2,1)S(1)}, bf16[32,768]{1,0:T(8,128)(2,1)S(1)}, u32[]{:S(2)}, u32[]{:S(2)}) collective-permute-start(bf16[32,768]{1,0:T(8,128)(2,1)S(1)} %get-tuple-element.32), channel_id=1, source_target_pairs={{0,4},{1,5},{2,6},{3,7},{4,0},{5,1},{6,2},{7,3},{8,12},{9,13},{10,... | collective-permute-start | bytes 147464 | tf_op jit(solution)/shard_map/ppermute | solution.py:77
  30.6 6.0 %collective-permute-start.10 = (bf16[32,768]{1,0:T(8,128)(2,1)S(1)}, bf16[32,768]{1,0:T(8,128)(2,1)S(1)}, u32[]{:S(2)}, u32[]{:S(2)}) collective-permute-start(bf16[32,768]{1,0:T(8,128)(2,1)S(1)} %get-tuple-element.33), channel_id=1, source_target_pairs={{0,6},{1,7},{2,4},{3,5},{4,2},{5,3},{6,0},{7,1},{8,14},{9,15},{10,... | collective-permute-start | bytes 147464 | tf_op jit(solution)/shard_map/ppermute | solution.py:77

commit v14 on v13

--- a/solution.py
+++ b/solution.py
@@ -160,30 +160,57 @@
         (((0,), (0,)), ((), ())),
         preferred_element_type=jnp.float32,
     )
-    dq_ref[...] = dq.astype(dq_ref.dtype)
-
-
-def near_body(rows_ref, weights_ref, note_ref, dq_ref, slope_ref, copy_ref):
+    q_home = dq_ref.shape[1]
+    for z in range(dq_ref.shape[0]):
+        dq_ref[z] = dq[z * q_home : (z + 1) * q_home].astype(dq_ref.dtype)
+
+
+def write_home(plane, staged, out_ref, sems):
+    copies = [
+        pltpu.make_async_copy(staged.at[z], out_ref.at[2 * z + plane], sems.at[z])
+        for z in range(staged.shape[0])
+    ]
+    for copy in copies:
+        copy.start()
+    for copy in copies:
+        copy.wait()
+
+
+def near_body(side_ref, rows_ref, weights_ref, note_ref, slope_ref, copy_ref, out_ref, staged, sems):
     copy_ref[...] = rows_ref[...]
-    grad_body(0, rows_ref, weights_ref, note_ref, dq_ref, slope_ref)
-
-
-def far_body(rows_ref, weights_ref, note_ref, dq_ref, slope_ref):
-    grad_body(1, rows_ref, weights_ref, note_ref, dq_ref, slope_ref)
-
-
-def fold_body(place_ref, near_ref, came_ref, kept_ref, *send_refs):
-    rows, place = kept_ref.shape[0], place_ref[0]
-    for step, ref in enumerate([kept_ref, *send_refs]):
-        part = pl.ds(pl.multiple_of((place ^ step) * rows, rows), rows)
-        ref[...] = (near_ref[part, :] + came_ref[part, :].astype(jnp.float32)).astype(ref.dtype)
-
-
-def sum_body(kept_ref, *refs):
-    *term_refs, out_ref = refs
-    total = kept_ref[...]
-    for ref in term_refs:
-        total = total + ref[...].astype(jnp.float32)
+    grad_body(0, rows_ref, weights_ref, note_ref, staged, slope_ref)
+    write_home(side_ref[0], staged, out_ref, sems)
+
+
+def far_body(side_ref, rows_ref, weights_ref, note_ref, near_ref, slope_ref, out_ref, staged, sems):
+    del near_ref
+    grad_body(1, rows_ref, weights_ref, note_ref, staged, slope_ref)
+    write_home(1 - side_ref[0], staged, out_ref, sems)
+
+
+def grad_call(body, homes, q_home, outs, args, aliases, flops):
+    width = args[1].shape[1]
+    vmem = pl.BlockSpec(memory_space=pltpu.VMEM)
+    specs = [pl.BlockSpec(memory_space=pltpu.SMEM), vmem, vmem, vmem]
+    return pl.pallas_call(
+        body,
+        out_shape=outs + [jax.ShapeDtypeStruct((homes, q_home, width), jnp.bfloat16)],
+        in_specs=specs + [pl.BlockSpec(memory_space=pl.ANY)] * len(aliases),
+        out_specs=[vmem] * len(outs) + [pl.BlockSpec(memory_space=pl.ANY)],
+        scratch_shapes=[
+            pltpu.VMEM((homes // 2, q_home, width), jnp.bfloat16),
+            pltpu.SemaphoreType.DMA((homes // 2,)),
+        ],
+        input_output_aliases=aliases,
+        cost_estimate=pl.CostEstimate(flops=flops, bytes_accessed=0, transcendentals=0),
+        compiler_params=pltpu.CompilerParams(vmem_limit_bytes=VMEM_LIMIT),
+    )(*args)
+
+
+def sum_body(terms_ref, out_ref):
+    total = terms_ref[0].astype(jnp.float32)
+    for source in range(1, terms_ref.shape[0]):
+        total = total + terms_ref[source].astype(jnp.float32)
     out_ref[...] = total
 
 
@@ -304,6 +331,7 @@
     f32, bf16 = jnp.float32, jnp.bfloat16
 
     place = jnp.reshape(me // 2, (1,)).astype(jnp.int32)
+    side = jnp.reshape(me % 2, (1,)).astype(jnp.int32)
     far_bit = groups // 2
     came = [swap(queries, "lab", 2 * step) for step in range(1, homes // 2)]
     held, weights = local_call(
@@ -327,22 +355,21 @@
     far = swap(near, "lab", 1)
     work = 4 * half * lab_dev * width
     slope_like = like(BLOCK + NOTE, half, bf16)
-    near_dq, near_slope, near_copy = local_call(
+    near_slope, near_copy, dq = grad_call(
         near_body,
-        [like(half, width, f32), slope_like, like(half, width, bf16)],
-        [near, weights, note],
+        homes,
+        q_home,
+        [slope_like, like(half, width, bf16)],
+        [side, near, weights, note],
+        {},
         work,
     )
     cross_near = swap(noted, "pb", far_bit)
     cross_far = diagonal(near_copy, far_bit, 1)
-    far_dq, far_slope = local_call(
-        far_body,
-        [like(half, width, bf16), slope_like],
-        [far, weights, note],
-        work,
-        [near_dq],
-    )
-    came = swap(far_dq, "lab", 1)
+    far_slope, dq = grad_call(
+        far_body, homes, q_home, [slope_like], [side, far, weights, note, dq], {4: 1}, work
+    )
+    terms = lax.all_to_all(dq, "lab", split_axis=0, concat_axis=0, tiled=True)
     acc, own = local_call(
         own_body,
         [like(lab_dev, width, f32), like(qcount + BLOCK + NOTE, width, bf16)],
@@ -351,24 +378,14 @@
     )
     mate = swap(own, "pb", 1)
     cross = local_call(
-        stack_body, [like(qcount + NOTE, width, bf16)], [cross_near, cross_far], 0, []
+        stack_body, [like(qcount + NOTE, width, bf16)], [cross_near, cross_far], 0, [acc]
     )[0]
     cross_mate = swap(cross, "pb", 1)
     grown = like(lab_dev, width, f32)
     acc = local_call(cross_body, [grown], [cross, weights, acc], 20 * work)[0]
     acc = local_call(mate_body, [grown], [mate, acc], work)[0]
-    kept, *terms = local_call(
-        fold_body,
-        [like(q_home, width, f32)] + [like(q_home, width, bf16)] * (homes // 2 - 1),
-        [place, near_dq, came],
-        0,
-        [acc],
-    )
-    terms = [swap(term, "lab", 2 * step) for step, term in enumerate(terms, 1)]
     weight_grad, mark = late(groups, cross_mate, weights, acc)
-    query_grad = local_call(
-        sum_body, [like(q_home, width, f32)], [kept, *terms], 0, [mark]
-    )[0]
+    query_grad = local_call(sum_body, [like(q_home, width, f32)], [terms], 0, [mark])[0]
     return (query_grad, weight_grad)
 
 

time: 37.5 us -> 35.7 us (0.952)
  starting transfers between devices: 17.3 us -> 14.7 us
  Pallas kernels: 9.47 us -> 10.9 us
  waiting for transfers between devices: 6.85 us -> 6.15 us
    ppermute x11 -> x7, starting transfers between devices: 16.7 us -> 9.37 us  [swap(): return lax.ppermute(value, axis, [(i, i ^ bit) for i in range(count)])]
    all_to_all x0 -> x1, starting transfers between devices: none -> 4.75 us  [dense_shards(): terms = lax.all_to_all(dq, 'lab', split_axis=0, concat_axis=0, tiled=True)]
    pallas_call x0 -> x2, Pallas kernels: none -> 4.12 us  [grad_call(): pl.pallas_call(body, out_shape=outs + [jax.ShapeDtypeStruct((homes, q_hom...]
    ppermute x11 -> x7, waiting for transfers between devices: 6.19 us -> 2.46 us  [swap(): return lax.ppermute(value, axis, [(i, i ^ bit) for i in range(count)])]
    all_to_all x0 -> x1, waiting for transfers between devices: none -> 3.69 us  [dense_shards(): terms = lax.all_to_all(dq, 'lab', split_axis=0, concat_axis=0, tiled=True)]
    pallas_call x11 -> x8, Pallas kernels: 6.75 us -> 4.07 us  [local_call(): pl.pallas_call(lambda *refs: body(*refs[:given], *refs[later:]), out_shap...]
    ppermute x1, waiting for transfers between devices: 0.66 us -> 0.01 us  [diagonal(): return lax.ppermute(value, ('pb', 'lab'), pairs)]
  transfers between devices with their start and end apart: 12 -> 9, of which waited for: 6 -> 3; matrix products, arithmetic and copies ran while one was open for 2% -> 2% of each run, Pallas kernels for 24% -> 29%
where the time goes in v14:
time: 35.7 us; the launch traced here: 35.4 us
  starting transfers between devices  14.7 us (41%)
  Pallas kernels  10.9 us (31%)
  waiting for transfers between devices  6.15 us (17%)
  local copies, waits for them, and re-layouts  2.21 us (6%)
  between operations  0.74 us (2%)
  other arithmetic  0.72 us (2%)
    ppermute x7, starting transfers between devices, swap(): return lax.ppermute(value, axis, [(i, i ^ bit) for i in range(count)])  9.37 us
    all_to_all x1, starting transfers between devices, dense_shards(): terms = lax.all_to_all(dq, 'lab', split_axis=0, concat_axis=0, tiled=True)  4.75 us
    pallas_call x2, Pallas kernels, grad_call(): pl.pallas_call(body, out_shape=outs + [jax.ShapeDtypeStruct((homes, q_hom...  4.12 us
    pallas_call x8, Pallas kernels, local_call(): pl.pallas_call(lambda *refs: body(*refs[:given], *refs[later:]), out_shap...  4.07 us
    all_to_all x1, waiting for transfers between devices, dense_shards(): terms = lax.all_to_all(dq, 'lab', split_axis=0, concat_axis=0, tiled=True)  3.69 us
    pallas_call x1, Pallas kernels, late(): pl.pallas_call(lambda *refs: late_body(groups, *refs), out_shape=[out, li...  2.7 us
    ppermute x7, waiting for transfers between devices, swap(): return lax.ppermute(value, axis, [(i, i ^ bit) for i in range(count)])  2.46 us
    unnamed x4, local copies, waits for them, and re-layouts  2.21 us
  transfers between devices with their start and end apart: 9, of which 3 were waited for; matrix products, arithmetic and copies ran while one was open for 2% of the time, Pallas kernels for 29%

profile of v14, /device:TPU:0, one launch (start us, length us, event | category | flops | bytes accessed | tf_op | source)
XLA Modules:
  0.0 35.4 jit_solution(16705780925671005743)
XLA Ops:
  0.6 3.1 %collective-permute-start = (bf16[32,768]{1,0:T(8,128)(2,1)}, bf16[32,768]{1,0:T(8,128)(2,1)S(1)}, u32[]{:S(2)}, u32[]{:S(2)}) collective-permute-start(bf16[32,768]{1,0:T(8,128)(2,1)} %refs_0_.1), channel_id=1, source_target_pairs={{0,2},{1,3},{2,0},{3,1},{4,6},{5,7},{6,4},{7,5},{8,10},{9,11},{10,... | collective-permute-start | bytes 147464 | tf_op jit(solution)/shard_map/ppermute | solution.py:77
  3.7 2.5 %collective-permute-start.2 = (bf16[32,768]{1,0:T(8,128)(2,1)}, bf16[32,768]{1,0:T(8,128)(2,1)S(1)}, u32[]{:S(2)}, u32[]{:S(2)}) collective-permute-start(bf16[32,768]{1,0:T(8,128)(2,1)} %refs_0_.1), channel_id=1, source_target_pairs={{0,6},{1,7},{2,4},{3,5},{4,2},{5,3},{6,0},{7,1},{8,14},{9,15},{10,... | collective-permute-start | bytes 147464 | tf_op jit(solution)/shard_map/ppermute | solution.py:77
  6.2 0.1 collective-permute-start.1
  6.3 0.7 %add_convert_fusion.refs_1_ = f32[9,256]{1,0:T(8,128)S(1)} fusion(s32[1,256]{1,0:T(1,128)} %bitcast.6, s32[8,256]{1,0:T(8,128)} %bitcast.5), kind=kLoop, calls=%fused_computation | loop fusion | flops 4608 | bytes 18432 | tf_op jit(solution)/shard_map/convert_element_type | solution.py:342
  7.0 1.4 %copy-done = bf16[1024,768]{1,0:T(8,128)(2,1)S(1)} copy-done((bf16[1024,768]{1,0:T(8,128)(2,1)S(1)}, bf16[1024,768]{1,0:T(8,128)(2,1)}, u32[]{:S(2)}) %copy-start) | copy-done | bytes 1572888
  8.4 0.8 %copy-done.1 = bf16[32,768]{1,0:T(8,128)(2,1)S(1)} copy-done((bf16[32,768]{1,0:T(8,128)(2,1)S(1)}, bf16[32,768]{1,0:T(8,128)(2,1)}, u32[]{:S(2)}) %copy-start.1) | copy-done | bytes 49176
  9.2 0.1 shard_map.59
  9.4 0.2 shard_map.60.refs_5_.note_ref
  9.5 0.9 %collective-permute-done.2.refs_4_ = bf16[32,768]{1,0:T(8,128)(2,1)S(1)} collective-permute-done((bf16[32,768]{1,0:T(8,128)(2,1)}, bf16[32,768]{1,0:T(8,128)(2,1)S(1)}, u32[]{:S(2)}, u32[]{:S(2)}) %collective-permute-start.2) | collective-permute-done | bytes 49184 | tf_op jit(solution)/shard_map/ppermute | solution.py:77
  10.4 1.5 %collective-permute-done.1.refs_3_ = bf16[32,768]{1,0:T(8,128)(2,1)S(1)} collective-permute-done((bf16[32,768]{1,0:T(8,128)(2,1)}, bf16[32,768]{1,0:T(8,128)(2,1)S(1)}, u32[]{:S(2)}, u32[]{:S(2)}) %collective-permute-start.1) | collective-permute-done | bytes 49184 | tf_op jit(solution)/shard_map/ppermute | solution.py:77
  12.0 1.6 %collective-permute-start.3 = (bf16[128,768]{1,0:T(8,128)(2,1)S(1)}, bf16[128,768]{1,0:T(8,128)(2,1)S(1)}, u32[]{:S(2)}, u32[]{:S(2)}) collective-permute-start(bf16[128,768]{1,0:T(8,128)(2,1)S(1)} %get-tuple-element.17.rows_ref.refs_0_), channel_id=1, source_target_pairs={{0,1},{1,0},{2,3},{3,2},{4,5},{5,4},{6,7},{7,6},{8,9},{9,8},{10,11... | collective-permute-start | bytes 589832 | tf_op jit(solution)/shard_map/ppermute | solution.py:77
  13.5 1.5 %collective-permute-start.4 = (bf16[144,768]{1,0:T(8,128)(2,1)S(1)}, bf16[144,768]{1,0:T(8,128)(2,1)S(1)}, u32[]{:S(2)}, u32[]{:S(2)}) collective-permute-start(bf16[144,768]{1,0:T(8,128)(2,1)S(1)} %get-tuple-element.20), channel_id=1, source_target_pairs={{0,16},{8,24},{16,0},{24,8},{1,17},{9,25},{17,1},{25,9},{2,18},{10... | collective-permute-start | bytes 663560 | tf_op jit(solution)/shard_map/ppermute | solution.py:77
  15.0 2.1 %shard_map.62 = (bf16[144,128]{1,0:T(8,128)(2,1)S(1)}, bf16[128,768]{1,0:T(8,128)(2,1)S(1)}, bf16[8,32,768]{2,1,0:T(8,128)(2,1)}) custom-call(s32[1]{0:T(128)} %bitcast.side_ref, bf16[128,768]{1,0:T(8,128)(2,1)S(1)} %get-tuple-element.17.rows_ref.refs_0_, bf16[1024,768]{1,0:T(8,128)(2,1)S(1)} %get-tuple-element.16.refs_6_.weights_ref.refs_1_, ...), custom_call_target="tpu_custom_call" | custom-call | flops 402653184 | tf_op jit(solution)/shard_map/pallas_call | solution.py:195
  17.1 0.5 %collective-permute-start.5 = (bf16[128,768]{1,0:T(8,128)(2,1)S(1)}, bf16[128,768]{1,0:T(8,128)(2,1)S(1)}, u32[]{:S(2)}, u32[]{:S(2)}) collective-permute-start(bf16[128,768]{1,0:T(8,128)(2,1)S(1)} %get-tuple-element.21), channel_id=1, source_target_pairs={{0,17},{1,16},{2,19},{3,18},{4,21},{5,20},{6,23},{7,22},{8,25},{9,... | collective-permute-start | bytes 589832 | tf_op jit(solution)/shard_map/ppermute | solution.py:87
  17.7 2.1 %shard_map.63 = (bf16[144,128]{1,0:T(8,128)(2,1)S(1)}, bf16[8,32,768]{2,1,0:T(8,128)(2,1)}) custom-call(s32[1]{0:T(128)} %bitcast.side_ref, bf16[128,768]{1,0:T(8,128)(2,1)S(1)} %collective-permute-done.3.rows_ref.refs_1_, bf16[1024,768]{1,0:T(8,128)(2,1)S(1)} %get-tuple-element.16.refs_6_.weights_ref.refs_1_, ...), custom_call_target="tpu_custom_call", output_to_operand_aliasing={{1}: (4, {})} | custom-call | flops 402653184 | tf_op jit(solution)/shard_map/pallas_call | solution.py:195
  19.8 4.7 %all-to-all-start = ((bf16[8,32,768]{2,1,0:T(8,128)(2,1)}), bf16[8,32,768]{2,1,0:T(8,128)(2,1)S(1)}, u32[]{:S(2)}, u32[]{:S(2)}) async-start(bf16[8,32,768]{2,1,0:T(8,128)(2,1)} %get-tuple-element.19), calls=%async_computation | async-start | bytes 786432 | tf_op jit(solution)/shard_map/all_to_all | solution.py:372
  24.5 0.6 %shard_map.64 = (f32[1024,768]{1,0:T(8,128)S(1)}, bf16[400,768]{1,0:T(8,128)(2,1)S(1)}) custom-call(bf16[128,768]{1,0:T(8,128)(2,1)S(1)} %get-tuple-element.17.rows_ref.refs_0_, bf16[128,768]{1,0:T(8,128)(2,1)S(1)} %collective-permute-done.3.rows_ref.refs_1_, bf16[144,128]{1,0:T(8,128)(2,1)S(1)} %get-tuple-element.22.refs_2_, ...), custom_call_target="tpu_custom_call" | custom-call | flops 402653184 | tf_op jit(solution)/shard_map/pallas_call | solution.py:96
  25.1 0.1 collective-permute-start.7
  25.2 0.5 %collective-permute-start.6 = (bf16[272,768]{1,0:T(8,128)(2,1)S(1)}, bf16[272,768]{1,0:T(8,128)(2,1)S(1)}, u32[]{:S(2)}, u32[]{:S(2)}) collective-permute-start(bf16[272,768]{1,0:T(8,128)(2,1)S(1)} %shard_map.65.refs_0_), channel_id=1, source_target_pairs={{0,8},{8,0},{16,24},{24,16},{1,9},{9,1},{17,25},{25,17},{2,10},{10... | collective-permute-start | bytes 1253384 | tf_op jit(solution)/shard_map/ppermute | solution.py:77
  25.8 1.9 %shard_map.66.refs_1_ = f32[1024,768]{1,0:T(8,128)S(1)} custom-call(bf16[272,768]{1,0:T(8,128)(2,1)S(1)} %shard_map.65.refs_0_, bf16[1024,768]{1,0:T(8,128)(2,1)S(1)} %get-tuple-element.16.refs_6_.weights_ref.refs_1_, f32[1024,768]{1,0:T(8,128)S(1)} %get-tuple-element.24.refs_2_), custom_call_target="tpu_custom_call" | custom-call | flops 8053063680 | tf_op jit(solution)/shard_map/pallas_call | solution.py:96
  27.7 0.6 %shard_map.67.refs_2_ = f32[1024,768]{1,0:T(8,128)S(1)} custom-call(bf16[400,768]{1,0:T(8,128)(2,1)S(1)} %collective-permute-done.7.refs_0_, f32[1024,768]{1,0:T(8,128)S(1)} %shard_map.66.refs_1_), custom_call_target="tpu_custom_call" | custom-call | flops 402653184 | tf_op jit(solution)/shard_map/pallas_call | solution.py:96
  28.3 2.7 %shard_map.68 = (bf16[1024,768]{1,0:T(8,128)(2,1)}, s32[1,128]{1,0:T(1,128)S(1)}) custom-call(bf16[272,768]{1,0:T(8,128)(2,1)S(1)} %collective-permute-done.6.refs_0_, bf16[1024,768]{1,0:T(8,128)(2,1)S(1)} %get-tuple-element.16.refs_6_.weights_ref.refs_1_, f32[1024,768]{1,0:T(8,128)S(1)} %shard_map.67.refs_2_), custom_call_target="tpu_custom_call" | custom-call | tf_op jit(solution)/shard_map/pallas_call | solution.py:286
  31.0 3.7 %all-to-all-done.refs_0_ = bf16[8,32,768]{2,1,0:T(8,128)(2,1)S(1)} async-done(((bf16[8,32,768]{2,1,0:T(8,128)(2,1)}), bf16[8,32,768]{2,1,0:T(8,128)(2,1)S(1)}, u32[]{:S(2)}, u32[]{:S(2)}) %all-to-all-start) | async-done | bytes 393248 | tf_op jit(solution)/shard_map/all_to_all | solution.py:372
  34.7 0.7 %shard_map.69 = f32[32,768]{1,0:T(8,128)} custom-call(bf16[8,32,768]{2,1,0:T(8,128)(2,1)S(1)} %all-to-all-done.refs_0_, s32[1,128]{1,0:T(1,128)S(1)} %get-tuple-element.26.refs_1_), custom_call_target="tpu_custom_call" | custom-call | tf_op jit(solution)/shard_map/pallas_call | solution.py:96
  (10 shorter events, 0.1 us)
Async XLA Ops:
  0.6 8.9 %collective-permute-start = (bf16[32,768]{1,0:T(8,128)(2,1)}, bf16[32,768]{1,0:T(8,128)(2,1)S(1)}, u32[]{:S(2)}, u32[]{:S(2)}) collective-permute-start(bf16[32,768]{1,0:T(8,128)(2,1)} %refs_0_.1), channel_id=1, source_target_pairs={{0,2},{1,3},{2,0},{3,1},{4,6},{5,7},{6,4},{7,5},{8,10},{9,11},{10,... | collective-permute-start | bytes 147464 | tf_op jit(solution)/shard_map/ppermute | solution.py:77
  3.7 6.7 %collective-permute-start.2 = (bf16[32,768]{1,0:T(8,128)(2,1)}, bf16[32,768]{1,0:T(8,128)(2,1)S(1)}, u32[]{:S(2)}, u32[]{:S(2)}) collective-permute-start(bf16[32,768]{1,0:T(8,128)(2,1)} %refs_0_.1), channel_id=1, source_target_pairs={{0,6},{1,7},{2,4},{3,5},{4,2},{5,3},{6,0},{7,1},{8,14},{9,15},{10,... | collective-permute-start | bytes 147464 | tf_op jit(solution)/shard_map/ppermute | solution.py:77
  6.2 5.7 %collective-permute-start.1 = (bf16[32,768]{1,0:T(8,128)(2,1)}, bf16[32,768]{1,0:T(8,128)(2,1)S(1)}, u32[]{:S(2)}, u32[]{:S(2)}) collective-permute-start(bf16[32,768]{1,0:T(8,128)(2,1)} %refs_0_.1), channel_id=1, source_target_pairs={{0,4},{1,5},{2,6},{3,7},{4,0},{5,1},{6,2},{7,3},{8,12},{9,13},{10,... | collective-permute-start | bytes 147464 | tf_op jit(solution)/shard_map/ppermute | solution.py:77
  7.0 1.4 %copy-start = (bf16[1024,768]{1,0:T(8,128)(2,1)S(1)}, bf16[1024,768]{1,0:T(8,128)(2,1)}, u32[]{:S(2)}) copy-start(bf16[1024,768]{1,0:T(8,128)(2,1)} %refs_1_.1) | copy-start | bytes 4718596
  8.4 0.8 %copy-start.1 = (bf16[32,768]{1,0:T(8,128)(2,1)S(1)}, bf16[32,768]{1,0:T(8,128)(2,1)}, u32[]{:S(2)}) copy-start(bf16[32,768]{1,0:T(8,128)(2,1)} %refs_0_.1) | copy-start | bytes 147460
  12.0 5.7 %collective-permute-start.3 = (bf16[128,768]{1,0:T(8,128)(2,1)S(1)}, bf16[128,768]{1,0:T(8,128)(2,1)S(1)}, u32[]{:S(2)}, u32[]{:S(2)}) collective-permute-start(bf16[128,768]{1,0:T(8,128)(2,1)S(1)} %get-tuple-element.17.rows_ref.refs_0_), channel_id=1, source_target_pairs={{0,1},{1,0},{2,3},{3,2},{4,5},{5,4},{6,7},{7,6},{8,9},{9,8},{10,11... | collective-permute-start | bytes 589832 | tf_op jit(solution)/shard_map/ppermute | solution.py:77
  13.5 11.6 %collective-permute-start.4 = (bf16[144,768]{1,0:T(8,128)(2,1)S(1)}, bf16[144,768]{1,0:T(8,128)(2,1)S(1)}, u32[]{:S(2)}, u32[]{:S(2)}) collective-permute-start(bf16[144,768]{1,0:T(8,128)(2,1)S(1)} %get-tuple-element.20), channel_id=1, source_target_pairs={{0,16},{8,24},{16,0},{24,8},{1,17},{9,25},{17,1},{25,9},{2,18},{10... | collective-permute-start | bytes 663560 | tf_op jit(solution)/shard_map/ppermute | solution.py:77
  17.1 8.1 %collective-permute-start.5 = (bf16[128,768]{1,0:T(8,128)(2,1)S(1)}, bf16[128,768]{1,0:T(8,128)(2,1)S(1)}, u32[]{:S(2)}, u32[]{:S(2)}) collective-permute-start(bf16[128,768]{1,0:T(8,128)(2,1)S(1)} %get-tuple-element.21), channel_id=1, source_target_pairs={{0,17},{1,16},{2,19},{3,18},{4,21},{5,20},{6,23},{7,22},{8,25},{9,... | collective-permute-start | bytes 589832 | tf_op jit(solution)/shard_map/ppermute | solution.py:87
  19.8 14.9 %all-to-all-start = ((bf16[8,32,768]{2,1,0:T(8,128)(2,1)}), bf16[8,32,768]{2,1,0:T(8,128)(2,1)S(1)}, u32[]{:S(2)}, u32[]{:S(2)}) async-start(bf16[8,32,768]{2,1,0:T(8,128)(2,1)} %get-tuple-element.19), calls=%async_computation | async-start | bytes 786432 | tf_op jit(solution)/shard_map/all_to_all | solution.py:372
  25.1 2.6 %collective-permute-start.7 = (bf16[400,768]{1,0:T(8,128)(2,1)S(1)}, bf16[400,768]{1,0:T(8,128)(2,1)S(1)}, u32[]{:S(2)}, u32[]{:S(2)}) collective-permute-start(bf16[400,768]{1,0:T(8,128)(2,1)S(1)} %get-tuple-element.25), channel_id=1, source_target_pairs={{0,8},{8,0},{16,24},{24,16},{1,9},{9,1},{17,25},{25,17},{2,10},{10... | collective-permute-start | bytes 1843208 | tf_op jit(solution)/shard_map/ppermute | solution.py:77
  25.2 3.0 %collective-permute-start.6 = (bf16[272,768]{1,0:T(8,128)(2,1)S(1)}, bf16[272,768]{1,0:T(8,128)(2,1)S(1)}, u32[]{:S(2)}, u32[]{:S(2)}) collective-permute-start(bf16[272,768]{1,0:T(8,128)(2,1)S(1)} %shard_map.65.refs_0_), channel_id=1, source_target_pairs={{0,8},{8,0},{16,24},{24,16},{1,9},{9,1},{17,25},{25,17},{2,10},{10... | collective-permute-start | bytes 1253384 | tf_op jit(solution)/shard_map/ppermute | solution.py:77

commit v15 on v14

--- a/solution.py
+++ b/solution.py
@@ -107,15 +107,11 @@
     return jax.ShapeDtypeStruct((rows, width), dtype)
 
 
-def join_body(place_ref, own_ref, *refs):
-    *came_refs, note_ref, out_ref, noted_ref = refs
-    rows, place = own_ref.shape[0], place_ref[0]
-    for step, ref in enumerate([own_ref, *came_refs]):
-        start = pl.multiple_of((place ^ step) * rows, rows)
-        out_ref[pl.ds(start, rows), :] = ref[...]
-    half = out_ref.shape[0]
-    noted_ref[:half, :] = out_ref[...]
-    noted_ref[half:, :] = note_ref[...]
+def join_body(*refs):
+    *came_refs, note_ref, out_ref, noted_ref, others_ref = refs
+    stack_body(*came_refs, out_ref)
+    stack_body(*came_refs, note_ref, noted_ref)
+    stack_body(*came_refs[1:], others_ref)
 
 
 def hold_body(*refs):
@@ -147,8 +143,8 @@
     return chosen, place
 
 
-def grad_body(which, rows_ref, weights_ref, note_ref, dq_ref, slope_ref):
-    rows, weights = rows_ref[...], weights_ref[...]
+def grad_body(which, rows, weights_ref, note_ref, dq_ref, slope_ref):
+    weights = weights_ref[...]
     note = note_ref[...].astype(jnp.float32)
     chosen, place = read_note(note, which, rows.shape[0])
     slope = slope_of(rows, weights, chosen, place)
@@ -161,47 +157,49 @@
         preferred_element_type=jnp.float32,
     )
     q_home = dq_ref.shape[1]
-    for z in range(dq_ref.shape[0]):
-        dq_ref[z] = dq[z * q_home : (z + 1) * q_home].astype(dq_ref.dtype)
-
-
-def write_home(plane, staged, out_ref, sems):
-    copies = [
-        pltpu.make_async_copy(staged.at[z], out_ref.at[2 * z + plane], sems.at[z])
-        for z in range(staged.shape[0])
+    for step in range(dq_ref.shape[0]):
+        dq_ref[step] = dq[step * q_home : (step + 1) * q_home].astype(dq_ref.dtype)
+
+
+def near_body(rows_ref, weights_ref, note_ref, dq_ref, slope_ref, copy_ref):
+    copy_ref[...] = rows_ref[...]
+    grad_body(0, rows_ref[...], weights_ref, note_ref, dq_ref, slope_ref)
+
+
+def far_body(
+    me_ref, near_ref, first_ref, others_ref, weights_ref, note_ref, slope_ref, out_ref, staged, sems
+):
+    me, steps = me_ref[0], near_ref.shape[0]
+    near = [
+        pltpu.make_async_copy(near_ref.at[step], out_ref.at[me ^ (2 * step)], sems.at[0, step])
+        for step in range(steps)
     ]
-    for copy in copies:
+    for copy in near:
         copy.start()
-    for copy in copies:
+    rows = jnp.concatenate([first_ref[...], others_ref[...]], axis=0)
+    grad_body(1, rows, weights_ref, note_ref, staged, slope_ref)
+    far = [
+        pltpu.make_async_copy(staged.at[step], out_ref.at[me ^ (2 * step + 1)], sems.at[1, step])
+        for step in range(steps)
+    ]
+    for copy in far:
+        copy.start()
+    for copy in near + far:
         copy.wait()
 
 
-def near_body(side_ref, rows_ref, weights_ref, note_ref, slope_ref, copy_ref, out_ref, staged, sems):
-    copy_ref[...] = rows_ref[...]
-    grad_body(0, rows_ref, weights_ref, note_ref, staged, slope_ref)
-    write_home(side_ref[0], staged, out_ref, sems)
-
-
-def far_body(side_ref, rows_ref, weights_ref, note_ref, near_ref, slope_ref, out_ref, staged, sems):
-    del near_ref
-    grad_body(1, rows_ref, weights_ref, note_ref, staged, slope_ref)
-    write_home(1 - side_ref[0], staged, out_ref, sems)
-
-
-def grad_call(body, homes, q_home, outs, args, aliases, flops):
-    width = args[1].shape[1]
+def far_call(slope_like, args, flops):
+    steps, q_home, width = args[1].shape
     vmem = pl.BlockSpec(memory_space=pltpu.VMEM)
-    specs = [pl.BlockSpec(memory_space=pltpu.SMEM), vmem, vmem, vmem]
     return pl.pallas_call(
-        body,
-        out_shape=outs + [jax.ShapeDtypeStruct((homes, q_home, width), jnp.bfloat16)],
-        in_specs=specs + [pl.BlockSpec(memory_space=pl.ANY)] * len(aliases),
-        out_specs=[vmem] * len(outs) + [pl.BlockSpec(memory_space=pl.ANY)],
+        far_body,
+        out_shape=[slope_like, jax.ShapeDtypeStruct((2 * steps, q_home, width), jnp.bfloat16)],
+        in_specs=[pl.BlockSpec(memory_space=pltpu.SMEM)] + [vmem] * (len(args) - 1),
+        out_specs=[vmem, pl.BlockSpec(memory_space=pl.ANY)],
         scratch_shapes=[
-            pltpu.VMEM((homes // 2, q_home, width), jnp.bfloat16),
-            pltpu.SemaphoreType.DMA((homes // 2,)),
+            pltpu.VMEM((steps, q_home, width), jnp.bfloat16),
+            pltpu.SemaphoreType.DMA((2, steps)),
         ],
-        input_output_aliases=aliases,
         cost_estimate=pl.CostEstimate(flops=flops, bytes_accessed=0, transcendentals=0),
         compiler_params=pltpu.CompilerParams(vmem_limit_bytes=VMEM_LIMIT),
     )(*args)
@@ -227,8 +225,8 @@
     return slope[:BLOCK], chosen
 
 
-def own_body(near_ref, far_ref, near_slope_ref, far_slope_ref, acc_ref, set_ref):
-    rows = jnp.concatenate([near_ref[...], far_ref[...]], axis=0)
+def own_body(near_ref, first_ref, others_ref, near_slope_ref, far_slope_ref, acc_ref, set_ref):
+    rows = jnp.concatenate([near_ref[...], first_ref[...], others_ref[...]], axis=0)
     slope = jnp.concatenate([near_slope_ref[...], far_slope_ref[...]], axis=1)
     count = rows.shape[0]
     set_ref[:count, :] = rows
@@ -309,9 +307,9 @@
     half = count // 2
     lane = lax.broadcasted_iota(jnp.int32, (count, count), 1)
     source = lax.broadcasted_iota(jnp.int32, (count, count), 0)
-    plane = (lane >= half).astype(jnp.int32) ^ (me & 1)
+    plane = (lane >= half).astype(jnp.int32)
     step = lax.shift_right_logical(lane & (half - 1), q_home.bit_length() - 1)
-    wanted = (2 * step + plane) * q_home + (lane & (q_home - 1))
+    wanted = ((2 * step + plane) ^ me) * q_home + (lane & (q_home - 1))
     order = jnp.where(source == wanted, 1.0, 0.0).astype(jnp.bfloat16)
     code = jnp.dot(code.astype(jnp.bfloat16), order, preferred_element_type=jnp.float32)
     rest = jnp.zeros((NOTE - 4, half), jnp.float32)
@@ -327,13 +325,11 @@
     lab_dev = label_weights.shape[0]
     homes = lax.axis_size("lab")
     groups = lax.axis_size("pb")
-    me = lax.axis_index("lab")
     f32, bf16 = jnp.float32, jnp.bfloat16
-
-    place = jnp.reshape(me // 2, (1,)).astype(jnp.int32)
-    side = jnp.reshape(me % 2, (1,)).astype(jnp.int32)
+    me = jnp.reshape(lax.axis_index("lab"), (1,)).astype(jnp.int32)
     far_bit = groups // 2
-    came = [swap(queries, "lab", 2 * step) for step in range(1, homes // 2)]
+    came = [swap(queries, "lab", step) for step in range(2, homes, 2)]
+    far_first = swap(queries, "lab", 1)
     held, weights = local_call(
         hold_body,
         [like(q_home, width, bf16), like(lab_dev, width, bf16)],
@@ -343,37 +339,38 @@
     note = local_call(
         lambda *refs: note_body(lab_dev // BLOCK, q_home, *refs),
         [like(NOTE, width, bf16)],
-        [jnp.reshape(me, (1,)).astype(jnp.int32), choice],
+        [me, choice],
     )[0]
-    near, noted = local_call(
+    near, noted, others = local_call(
         join_body,
-        [like(half, width, bf16), like(half + NOTE, width, bf16)],
-        [place, held, *came, note],
+        [like(half, width, bf16), like(half + NOTE, width, bf16), like(half - q_home, width, bf16)],
+        [held, *came, note],
         0,
-        [weights],
-    )
-    far = swap(near, "lab", 1)
+        [weights, far_first],
+    )
+    far_others = swap(others, "lab", 1)
     work = 4 * half * lab_dev * width
     slope_like = like(BLOCK + NOTE, half, bf16)
-    near_slope, near_copy, dq = grad_call(
+    near_dq, near_slope, near_copy = local_call(
         near_body,
-        homes,
-        q_home,
-        [slope_like, like(half, width, bf16)],
-        [side, near, weights, note],
-        {},
+        [
+            jax.ShapeDtypeStruct((homes // 2, q_home, width), bf16),
+            slope_like,
+            like(half, width, bf16),
+        ],
+        [near, weights, note],
         work,
     )
     cross_near = swap(noted, "pb", far_bit)
     cross_far = diagonal(near_copy, far_bit, 1)
-    far_slope, dq = grad_call(
-        far_body, homes, q_home, [slope_like], [side, far, weights, note, dq], {4: 1}, work
+    far_slope, dq = far_call(
+        slope_like, [me, near_dq, far_first, far_others, weights, note], work
     )
     terms = lax.all_to_all(dq, "lab", split_axis=0, concat_axis=0, tiled=True)
     acc, own = local_call(
         own_body,
         [like(lab_dev, width, f32), like(qcount + BLOCK + NOTE, width, bf16)],
-        [near, far, near_slope, far_slope],
+        [near, far_first, far_others, near_slope, far_slope],
         work,
     )
     mate = swap(own, "pb", 1)

time: 35.7 us -> 36.6 us (1.025)
  waiting for transfers between devices: 6.15 us -> 7.26 us
  Pallas kernels: 10.9 us -> 10.2 us
  starting transfers between devices: 14.7 us -> 15.1 us
    ppermute x7 -> x8, waiting for transfers between devices: 2.46 us -> 4.6 us  [swap(): return lax.ppermute(value, axis, [(i, i ^ bit) for i in range(count)])]
    pallas_call x2 -> x1, Pallas kernels: 4.12 us -> 2.09 us  [far_call(): pl.pallas_call(far_body, out_shape=[slope_like, jax.ShapeDtypeStruct((2 *...]
    pallas_call x8 -> x9, Pallas kernels: 4.07 us -> 5.41 us  [local_call(): pl.pallas_call(lambda *refs: body(*refs[:given], *refs[later:]), out_shap...]
    all_to_all x1, starting transfers between devices: 4.75 us -> 3.46 us  [dense_shards(): terms = lax.all_to_all(dq, 'lab', split_axis=0, concat_axis=0, tiled=True)]
    all_to_all x1, waiting for transfers between devices: 3.69 us -> 2.66 us  [dense_shards(): terms = lax.all_to_all(dq, 'lab', split_axis=0, concat_axis=0, tiled=True)]
    ppermute x1, starting transfers between devices: 0.55 us -> 1.56 us  [diagonal(): return lax.ppermute(value, ('pb', 'lab'), pairs)]
    ppermute x7 -> x8, starting transfers between devices: 9.37 us -> 10.1 us  [swap(): return lax.ppermute(value, axis, [(i, i ^ bit) for i in range(count)])]
  transfers between devices with their start and end apart: 9 -> 10, of which waited for: 3 -> 3; matrix products, arithmetic and copies ran while one was open for 2% -> 2% of each run, Pallas kernels for 29% -> 26%
where the time goes in v15:
time: 36.6 us; the launch traced here: 36.2 us
  starting transfers between devices  15.1 us (41%)
  Pallas kernels  10.2 us (28%)
  waiting for transfers between devices  7.26 us (20%)
  local copies, waits for them, and re-layouts  2.21 us (6%)
  between operations  0.75 us (2%)
  other arithmetic  0.72 us (2%)
    ppermute x8, starting transfers between devices, swap(): return lax.ppermute(value, axis, [(i, i ^ bit) for i in range(count)])  10.1 us
    pallas_call x9, Pallas kernels, local_call(): pl.pallas_call(lambda *refs: body(*refs[:given], *refs[later:]), out_shap...  5.41 us
    ppermute x8, waiting for transfers between devices, swap(): return lax.ppermute(value, axis, [(i, i ^ bit) for i in range(count)])  4.6 us
    all_to_all x1, starting transfers between devices, dense_shards(): terms = lax.all_to_all(dq, 'lab', split_axis=0, concat_axis=0, tiled=True)  3.46 us
    pallas_call x1, Pallas kernels, late(): pl.pallas_call(lambda *refs: late_body(groups, *refs), out_shape=[out, li...  2.7 us
    all_to_all x1, waiting for transfers between devices, dense_shards(): terms = lax.all_to_all(dq, 'lab', split_axis=0, concat_axis=0, tiled=True)  2.66 us
    unnamed x4, local copies, waits for them, and re-layouts  2.21 us
    pallas_call x1, Pallas kernels, far_call(): pl.pallas_call(far_body, out_shape=[slope_like, jax.ShapeDtypeStruct((2 *...  2.09 us
  transfers between devices with their start and end apart: 10, of which 3 were waited for; matrix products, arithmetic and copies ran while one was open for 2% of the time, Pallas kernels for 26%

profile of v15, /device:TPU:0, one launch (start us, length us, event | category | flops | bytes accessed | tf_op | source)
XLA Modules:
  0.0 36.2 jit_solution(1564786126953408025)
XLA Ops:
  0.6 4.1 %collective-permute-start.1 = (bf16[32,768]{1,0:T(8,128)(2,1)}, bf16[32,768]{1,0:T(8,128)(2,1)S(1)}, u32[]{:S(2)}, u32[]{:S(2)}) collective-permute-start(bf16[32,768]{1,0:T(8,128)(2,1)} %refs_0_.1), channel_id=1, source_target_pairs={{0,4},{1,5},{2,6},{3,7},{4,0},{5,1},{6,2},{7,3},{8,12},{9,13},{10,... | collective-permute-start | bytes 147464 | tf_op jit(solution)/shard_map/ppermute | solution.py:77
  4.7 1.6 %collective-permute-start = (bf16[32,768]{1,0:T(8,128)(2,1)}, bf16[32,768]{1,0:T(8,128)(2,1)S(1)}, u32[]{:S(2)}, u32[]{:S(2)}) collective-permute-start(bf16[32,768]{1,0:T(8,128)(2,1)} %refs_0_.1), channel_id=1, source_target_pairs={{0,2},{1,3},{2,0},{3,1},{4,6},{5,7},{6,4},{7,5},{8,10},{9,11},{10,... | collective-permute-start | bytes 147464 | tf_op jit(solution)/shard_map/ppermute | solution.py:77
  6.3 1.5 %collective-permute-start.3 = (bf16[32,768]{1,0:T(8,128)(2,1)}, bf16[32,768]{1,0:T(8,128)(2,1)S(1)}, u32[]{:S(2)}, u32[]{:S(2)}) collective-permute-start(bf16[32,768]{1,0:T(8,128)(2,1)} %refs_0_.1), channel_id=1, source_target_pairs={{0,1},{1,0},{2,3},{3,2},{4,5},{5,4},{6,7},{7,6},{8,9},{9,8},{10,11... | collective-permute-start | bytes 147464 | tf_op jit(solution)/shard_map/ppermute | solution.py:77
  7.8 0.2 collective-permute-start.2
  8.1 0.7 %add_convert_fusion.refs_1_ = f32[9,256]{1,0:T(8,128)S(1)} fusion(s32[1,256]{1,0:T(1,128)} %bitcast.4, s32[8,256]{1,0:T(8,128)} %bitcast.3), kind=kLoop, calls=%fused_computation | loop fusion | flops 4608 | bytes 18432 | tf_op jit(solution)/shard_map/convert_element_type | solution.py:338
  8.8 1.4 %copy-done = bf16[1024,768]{1,0:T(8,128)(2,1)S(1)} copy-done((bf16[1024,768]{1,0:T(8,128)(2,1)S(1)}, bf16[1024,768]{1,0:T(8,128)(2,1)}, u32[]{:S(2)}) %copy-start) | copy-done | bytes 1572888
  10.2 0.8 %copy-done.1 = bf16[32,768]{1,0:T(8,128)(2,1)S(1)} copy-done((bf16[32,768]{1,0:T(8,128)(2,1)S(1)}, bf16[32,768]{1,0:T(8,128)(2,1)}, u32[]{:S(2)}) %copy-start.1) | copy-done | bytes 49176
  11.0 0.1 shard_map.59
  11.1 0.2 shard_map.60.refs_4_.refs_2_.note_ref
  11.3 2.7 %collective-permute-done.2.refs_3_ = bf16[32,768]{1,0:T(8,128)(2,1)S(1)} collective-permute-done((bf16[32,768]{1,0:T(8,128)(2,1)}, bf16[32,768]{1,0:T(8,128)(2,1)S(1)}, u32[]{:S(2)}, u32[]{:S(2)}) %collective-permute-start.2) | collective-permute-done | bytes 49184 | tf_op jit(solution)/shard_map/ppermute | solution.py:77
  14.0 0.6 %collective-permute-start.4 = (bf16[96,768]{1,0:T(8,128)(2,1)S(1)}, bf16[96,768]{1,0:T(8,128)(2,1)S(1)}, u32[]{:S(2)}, u32[]{:S(2)}) collective-permute-start(bf16[96,768]{1,0:T(8,128)(2,1)S(1)} %get-tuple-element.20), channel_id=1, source_target_pairs={{0,1},{1,0},{2,3},{3,2},{4,5},{5,4},{6,7},{7,6},{8,9},{9,8},{10,11... | collective-permute-start | bytes 442376 | tf_op jit(solution)/shard_map/ppermute | solution.py:77
  14.5 1.5 %collective-permute-start.5 = (bf16[144,768]{1,0:T(8,128)(2,1)S(1)}, bf16[144,768]{1,0:T(8,128)(2,1)S(1)}, u32[]{:S(2)}, u32[]{:S(2)}) collective-permute-start(bf16[144,768]{1,0:T(8,128)(2,1)S(1)} %get-tuple-element.22), channel_id=1, source_target_pairs={{0,16},{8,24},{16,0},{24,8},{1,17},{9,25},{17,1},{25,9},{2,18},{10... | collective-permute-start | bytes 663560 | tf_op jit(solution)/shard_map/ppermute | solution.py:77
  16.0 1.3 %shard_map.62 = (bf16[4,32,768]{2,1,0:T(8,128)(2,1)S(1)}, bf16[144,128]{1,0:T(8,128)(2,1)S(1)}, bf16[128,768]{1,0:T(8,128)(2,1)S(1)}) custom-call(bf16[128,768]{1,0:T(8,128)(2,1)S(1)} %get-tuple-element.18.refs_0_, bf16[1024,768]{1,0:T(8,128)(2,1)S(1)} %get-tuple-element.17.refs_5_.refs_1_.weights_ref, bf16[16,768]{1,0:T(8,128)(2,1)S(1)} %shard_map.60.refs_4_.refs_2_.note_ref), custom_call_target="tpu_custom_call" | custom-call | flops 402653184 | tf_op jit(solution)/shard_map/pallas_call | solution.py:96
  17.4 1.6 %collective-permute-start.6 = (bf16[128,768]{1,0:T(8,128)(2,1)S(1)}, bf16[128,768]{1,0:T(8,128)(2,1)S(1)}, u32[]{:S(2)}, u32[]{:S(2)}) collective-permute-start(bf16[128,768]{1,0:T(8,128)(2,1)S(1)} %get-tuple-element.23), channel_id=1, source_target_pairs={{0,17},{1,16},{2,19},{3,18},{4,21},{5,20},{6,23},{7,22},{8,25},{9,... | collective-permute-start | bytes 589832 | tf_op jit(solution)/shard_map/ppermute | solution.py:87
  18.9 1.9 %collective-permute-done.4.others_ref.refs_2_ = bf16[96,768]{1,0:T(8,128)(2,1)S(1)} collective-permute-done((bf16[96,768]{1,0:T(8,128)(2,1)S(1)}, bf16[96,768]{1,0:T(8,128)(2,1)S(1)}, u32[]{:S(2)}, u32[]{:S(2)}) %collective-permute-start.4) | collective-permute-done | bytes 147488 | tf_op jit(solution)/shard_map/ppermute | solution.py:77
  20.9 2.1 %shard_map.63 = (bf16[144,128]{1,0:T(8,128)(2,1)S(1)}, bf16[8,32,768]{2,1,0:T(8,128)(2,1)}) custom-call(s32[1]{0:T(128)} %bitcast.refs_0_.me_ref, bf16[4,32,768]{2,1,0:T(8,128)(2,1)S(1)} %get-tuple-element.19.near_ref, bf16[32,768]{1,0:T(8,128)(2,1)S(1)} %collective-permute-done.3.refs_6_.first_ref.refs_1_, ...), custom_call_target="tpu_custom_call" | custom-call | flops 402653184 | tf_op jit(solution)/shard_map/pallas_call | solution.py:194
  22.9 3.5 %all-to-all-start = ((bf16[8,32,768]{2,1,0:T(8,128)(2,1)}), bf16[8,32,768]{2,1,0:T(8,128)(2,1)S(1)}, u32[]{:S(2)}, u32[]{:S(2)}) async-start(bf16[8,32,768]{2,1,0:T(8,128)(2,1)} %get-tuple-element.21), calls=%async_computation | async-start | bytes 786432 | tf_op jit(solution)/shard_map/all_to_all | solution.py:369
  26.4 0.6 %shard_map.64 = (f32[1024,768]{1,0:T(8,128)S(1)}, bf16[400,768]{1,0:T(8,128)(2,1)S(1)}) custom-call(bf16[128,768]{1,0:T(8,128)(2,1)S(1)} %get-tuple-element.18.refs_0_, bf16[32,768]{1,0:T(8,128)(2,1)S(1)} %collective-permute-done.3.refs_6_.first_ref.refs_1_, bf16[96,768]{1,0:T(8,128)(2,1)S(1)} %collective-permute-done.4.others_ref.refs_2_, ...), custom_call_target="tpu_custom_call" | custom-call | flops 402653184 | tf_op jit(solution)/shard_map/pallas_call | solution.py:96
  27.1 0.5 %collective-permute-start.7 = (bf16[272,768]{1,0:T(8,128)(2,1)S(1)}, bf16[272,768]{1,0:T(8,128)(2,1)S(1)}, u32[]{:S(2)}, u32[]{:S(2)}) collective-permute-start(bf16[272,768]{1,0:T(8,128)(2,1)S(1)} %shard_map.65.refs_0_), channel_id=1, source_target_pairs={{0,8},{8,0},{16,24},{24,16},{1,9},{9,1},{17,25},{25,17},{2,10},{10... | collective-permute-start | bytes 1253384 | tf_op jit(solution)/shard_map/ppermute | solution.py:77
  27.7 1.9 %shard_map.66.refs_1_ = f32[1024,768]{1,0:T(8,128)S(1)} custom-call(bf16[272,768]{1,0:T(8,128)(2,1)S(1)} %shard_map.65.refs_0_, bf16[1024,768]{1,0:T(8,128)(2,1)S(1)} %get-tuple-element.17.refs_5_.refs_1_.weights_ref, f32[1024,768]{1,0:T(8,128)S(1)} %get-tuple-element.26.refs_2_), custom_call_target="tpu_custom_call" | custom-call | flops 8053063680 | tf_op jit(solution)/shard_map/pallas_call | solution.py:96
  29.6 0.6 %shard_map.67.refs_2_ = f32[1024,768]{1,0:T(8,128)S(1)} custom-call(bf16[400,768]{1,0:T(8,128)(2,1)S(1)} %collective-permute-done.8.refs_0_, f32[1024,768]{1,0:T(8,128)S(1)} %shard_map.66.refs_1_), custom_call_target="tpu_custom_call" | custom-call | flops 402653184 | tf_op jit(solution)/shard_map/pallas_call | solution.py:96
  30.2 2.7 %shard_map.68 = (bf16[1024,768]{1,0:T(8,128)(2,1)}, s32[1,128]{1,0:T(1,128)S(1)}) custom-call(bf16[272,768]{1,0:T(8,128)(2,1)S(1)} %collective-permute-done.7.refs_0_, bf16[1024,768]{1,0:T(8,128)(2,1)S(1)} %get-tuple-element.17.refs_5_.refs_1_.weights_ref, f32[1024,768]{1,0:T(8,128)S(1)} %shard_map.67.refs_2_), custom_call_target="tpu_custom_call" | custom-call | tf_op jit(solution)/shard_map/pallas_call | solution.py:284
  32.9 2.7 %all-to-all-done.refs_0_ = bf16[8,32,768]{2,1,0:T(8,128)(2,1)S(1)} async-done(((bf16[8,32,768]{2,1,0:T(8,128)(2,1)}), bf16[8,32,768]{2,1,0:T(8,128)(2,1)S(1)}, u32[]{:S(2)}, u32[]{:S(2)}) %all-to-all-start) | async-done | bytes 393248 | tf_op jit(solution)/shard_map/all_to_all | solution.py:369
  35.6 0.7 %shard_map.69 = f32[32,768]{1,0:T(8,128)} custom-call(bf16[8,32,768]{2,1,0:T(8,128)(2,1)S(1)} %all-to-all-done.refs_0_, s32[1,128]{1,0:T(1,128)S(1)} %get-tuple-element.28.refs_1_), custom_call_target="tpu_custom_call" | custom-call | tf_op jit(solution)/shard_map/pallas_call | solution.py:96
  (12 shorter events, 0.2 us)
Async XLA Ops:
  0.6 10.6 %collective-permute-start.1 = (bf16[32,768]{1,0:T(8,128)(2,1)}, bf16[32,768]{1,0:T(8,128)(2,1)S(1)}, u32[]{:S(2)}, u32[]{:S(2)}) collective-permute-start(bf16[32,768]{1,0:T(8,128)(2,1)} %refs_0_.1), channel_id=1, source_target_pairs={{0,4},{1,5},{2,6},{3,7},{4,0},{5,1},{6,2},{7,3},{8,12},{9,13},{10,... | collective-permute-start | bytes 147464 | tf_op jit(solution)/shard_map/ppermute | solution.py:77
  4.7 6.5 %collective-permute-start = (bf16[32,768]{1,0:T(8,128)(2,1)}, bf16[32,768]{1,0:T(8,128)(2,1)S(1)}, u32[]{:S(2)}, u32[]{:S(2)}) collective-permute-start(bf16[32,768]{1,0:T(8,128)(2,1)} %refs_0_.1), channel_id=1, source_target_pairs={{0,2},{1,3},{2,0},{3,1},{4,6},{5,7},{6,4},{7,5},{8,10},{9,11},{10,... | collective-permute-start | bytes 147464 | tf_op jit(solution)/shard_map/ppermute | solution.py:77
  6.3 5.0 %collective-permute-start.3 = (bf16[32,768]{1,0:T(8,128)(2,1)}, bf16[32,768]{1,0:T(8,128)(2,1)S(1)}, u32[]{:S(2)}, u32[]{:S(2)}) collective-permute-start(bf16[32,768]{1,0:T(8,128)(2,1)} %refs_0_.1), channel_id=1, source_target_pairs={{0,1},{1,0},{2,3},{3,2},{4,5},{5,4},{6,7},{7,6},{8,9},{9,8},{10,11... | collective-permute-start | bytes 147464 | tf_op jit(solution)/shard_map/ppermute | solution.py:77
  7.8 6.1 %collective-permute-start.2 = (bf16[32,768]{1,0:T(8,128)(2,1)}, bf16[32,768]{1,0:T(8,128)(2,1)S(1)}, u32[]{:S(2)}, u32[]{:S(2)}) collective-permute-start(bf16[32,768]{1,0:T(8,128)(2,1)} %refs_0_.1), channel_id=1, source_target_pairs={{0,6},{1,7},{2,4},{3,5},{4,2},{5,3},{6,0},{7,1},{8,14},{9,15},{10,... | collective-permute-start | bytes 147464 | tf_op jit(solution)/shard_map/ppermute | solution.py:77
  8.8 1.4 %copy-start = (bf16[1024,768]{1,0:T(8,128)(2,1)S(1)}, bf16[1024,768]{1,0:T(8,128)(2,1)}, u32[]{:S(2)}) copy-start(bf16[1024,768]{1,0:T(8,128)(2,1)} %refs_1_.1) | copy-start | bytes 4718596
  10.2 0.8 %copy-start.1 = (bf16[32,768]{1,0:T(8,128)(2,1)S(1)}, bf16[32,768]{1,0:T(8,128)(2,1)}, u32[]{:S(2)}) copy-start(bf16[32,768]{1,0:T(8,128)(2,1)} %refs_0_.1) | copy-start | bytes 147460
  14.0 6.9 %collective-permute-start.4 = (bf16[96,768]{1,0:T(8,128)(2,1)S(1)}, bf16[96,768]{1,0:T(8,128)(2,1)S(1)}, u32[]{:S(2)}, u32[]{:S(2)}) collective-permute-start(bf16[96,768]{1,0:T(8,128)(2,1)S(1)} %get-tuple-element.20), channel_id=1, source_target_pairs={{0,1},{1,0},{2,3},{3,2},{4,5},{5,4},{6,7},{7,6},{8,9},{9,8},{10,11... | collective-permute-start | bytes 442376 | tf_op jit(solution)/shard_map/ppermute | solution.py:77
  14.5 12.6 %collective-permute-start.5 = (bf16[144,768]{1,0:T(8,128)(2,1)S(1)}, bf16[144,768]{1,0:T(8,128)(2,1)S(1)}, u32[]{:S(2)}, u32[]{:S(2)}) collective-permute-start(bf16[144,768]{1,0:T(8,128)(2,1)S(1)} %get-tuple-element.22), channel_id=1, source_target_pairs={{0,16},{8,24},{16,0},{24,8},{1,17},{9,25},{17,1},{25,9},{2,18},{10... | collective-permute-start | bytes 663560 | tf_op jit(solution)/shard_map/ppermute | solution.py:77
  17.4 9.7 %collective-permute-start.6 = (bf16[128,768]{1,0:T(8,128)(2,1)S(1)}, bf16[128,768]{1,0:T(8,128)(2,1)S(1)}, u32[]{:S(2)}, u32[]{:S(2)}) collective-permute-start(bf16[128,768]{1,0:T(8,128)(2,1)S(1)} %get-tuple-element.23), channel_id=1, source_target_pairs={{0,17},{1,16},{2,19},{3,18},{4,21},{5,20},{6,23},{7,22},{8,25},{9,... | collective-permute-start | bytes 589832 | tf_op jit(solution)/shard_map/ppermute | solution.py:87
  22.9 12.6 %all-to-all-start = ((bf16[8,32,768]{2,1,0:T(8,128)(2,1)}), bf16[8,32,768]{2,1,0:T(8,128)(2,1)S(1)}, u32[]{:S(2)}, u32[]{:S(2)}) async-start(bf16[8,32,768]{2,1,0:T(8,128)(2,1)} %get-tuple-element.21), calls=%async_computation | async-start | bytes 786432 | tf_op jit(solution)/shard_map/all_to_all | solution.py:369
  27.0 2.6 %collective-permute-start.8 = (bf16[400,768]{1,0:T(8,128)(2,1)S(1)}, bf16[400,768]{1,0:T(8,128)(2,1)S(1)}, u32[]{:S(2)}, u32[]{:S(2)}) collective-permute-start(bf16[400,768]{1,0:T(8,128)(2,1)S(1)} %get-tuple-element.27), channel_id=1, source_target_pairs={{0,8},{8,0},{16,24},{24,16},{1,9},{9,1},{17,25},{25,17},{2,10},{10... | collective-permute-start | bytes 1843208 | tf_op jit(solution)/shard_map/ppermute | solution.py:77
  27.1 3.0 %collective-permute-start.7 = (bf16[272,768]{1,0:T(8,128)(2,1)S(1)}, bf16[272,768]{1,0:T(8,128)(2,1)S(1)}, u32[]{:S(2)}, u32[]{:S(2)}) collective-permute-start(bf16[272,768]{1,0:T(8,128)(2,1)S(1)} %shard_map.65.refs_0_), channel_id=1, source_target_pairs={{0,8},{8,0},{16,24},{24,16},{1,9},{9,1},{17,25},{25,17},{2,10},{10... | collective-permute-start | bytes 1253384 | tf_op jit(solution)/shard_map/ppermute | solution.py:77

commit v16 on v13

--- a/solution.py
+++ b/solution.py
@@ -107,15 +107,10 @@
     return jax.ShapeDtypeStruct((rows, width), dtype)
 
 
-def join_body(place_ref, own_ref, *refs):
+def join_body(*refs):
     *came_refs, note_ref, out_ref, noted_ref = refs
-    rows, place = own_ref.shape[0], place_ref[0]
-    for step, ref in enumerate([own_ref, *came_refs]):
-        start = pl.multiple_of((place ^ step) * rows, rows)
-        out_ref[pl.ds(start, rows), :] = ref[...]
-    half = out_ref.shape[0]
-    noted_ref[:half, :] = out_ref[...]
-    noted_ref[half:, :] = note_ref[...]
+    stack_body(*came_refs, out_ref)
+    stack_body(*came_refs, note_ref, noted_ref)
 
 
 def hold_body(*refs):
@@ -147,7 +142,7 @@
     return chosen, place
 
 
-def grad_body(which, rows_ref, weights_ref, note_ref, dq_ref, slope_ref):
+def grad_body(which, rows_ref, weights_ref, note_ref, kept_ref, sent_ref, slope_ref):
     rows, weights = rows_ref[...], weights_ref[...]
     note = note_ref[...].astype(jnp.float32)
     chosen, place = read_note(note, which, rows.shape[0])
@@ -160,23 +155,28 @@
         (((0,), (0,)), ((), ())),
         preferred_element_type=jnp.float32,
     )
-    dq_ref[...] = dq.astype(dq_ref.dtype)
-
-
-def near_body(rows_ref, weights_ref, note_ref, dq_ref, slope_ref, copy_ref):
+    halve(dq, kept_ref, sent_ref, kept_ref.shape[0] // 2)
+
+
+def halve(terms, kept_ref, sent_ref, span):
+    for start in range(0, kept_ref.shape[0], span):
+        kept_ref[start : start + span, :] = terms[2 * start : 2 * start + span]
+        sent = terms[2 * start + span : 2 * start + 2 * span]
+        sent_ref[start : start + span, :] = sent.astype(sent_ref.dtype)
+
+
+def near_body(rows_ref, weights_ref, note_ref, kept_ref, sent_ref, slope_ref, copy_ref):
     copy_ref[...] = rows_ref[...]
-    grad_body(0, rows_ref, weights_ref, note_ref, dq_ref, slope_ref)
-
-
-def far_body(rows_ref, weights_ref, note_ref, dq_ref, slope_ref):
-    grad_body(1, rows_ref, weights_ref, note_ref, dq_ref, slope_ref)
-
-
-def fold_body(place_ref, near_ref, came_ref, kept_ref, *send_refs):
-    rows, place = kept_ref.shape[0], place_ref[0]
-    for step, ref in enumerate([kept_ref, *send_refs]):
-        part = pl.ds(pl.multiple_of((place ^ step) * rows, rows), rows)
-        ref[...] = (near_ref[part, :] + came_ref[part, :].astype(jnp.float32)).astype(ref.dtype)
+    grad_body(0, rows_ref, weights_ref, note_ref, kept_ref, sent_ref, slope_ref)
+
+
+def far_body(rows_ref, weights_ref, note_ref, kept_ref, sent_ref, slope_ref):
+    grad_body(1, rows_ref, weights_ref, note_ref, kept_ref, sent_ref, slope_ref)
+
+
+def fold_body(terms_ref, came_ref, kept_ref, sent_ref):
+    terms = terms_ref[...] + came_ref[...].astype(jnp.float32)
+    halve(terms, kept_ref, sent_ref, kept_ref.shape[0])
 
 
 def sum_body(kept_ref, *refs):
@@ -184,7 +184,7 @@
     total = kept_ref[...]
     for ref in term_refs:
         total = total + ref[...].astype(jnp.float32)
-    out_ref[...] = total
+    out_ref[...] = total.astype(out_ref.dtype)
 
 
 def stack_body(*refs):
@@ -282,9 +282,9 @@
     half = count // 2
     lane = lax.broadcasted_iota(jnp.int32, (count, count), 1)
     source = lax.broadcasted_iota(jnp.int32, (count, count), 0)
-    plane = (lane >= half).astype(jnp.int32) ^ (me & 1)
+    plane = (lane >= half).astype(jnp.int32)
     step = lax.shift_right_logical(lane & (half - 1), q_home.bit_length() - 1)
-    wanted = (2 * step + plane) * q_home + (lane & (q_home - 1))
+    wanted = ((2 * step + plane) ^ me) * q_home + (lane & (q_home - 1))
     order = jnp.where(source == wanted, 1.0, 0.0).astype(jnp.bfloat16)
     code = jnp.dot(code.astype(jnp.bfloat16), order, preferred_element_type=jnp.float32)
     rest = jnp.zeros((NOTE - 4, half), jnp.float32)
@@ -300,12 +300,10 @@
     lab_dev = label_weights.shape[0]
     homes = lax.axis_size("lab")
     groups = lax.axis_size("pb")
-    me = lax.axis_index("lab")
     f32, bf16 = jnp.float32, jnp.bfloat16
-
-    place = jnp.reshape(me // 2, (1,)).astype(jnp.int32)
+    me = jnp.reshape(lax.axis_index("lab"), (1,)).astype(jnp.int32)
     far_bit = groups // 2
-    came = [swap(queries, "lab", 2 * step) for step in range(1, homes // 2)]
+    came = [swap(queries, "lab", step) for step in range(2, homes, 2)]
     held, weights = local_call(
         hold_body,
         [like(q_home, width, bf16), like(lab_dev, width, bf16)],
@@ -315,34 +313,32 @@
     note = local_call(
         lambda *refs: note_body(lab_dev // BLOCK, q_home, *refs),
         [like(NOTE, width, bf16)],
-        [jnp.reshape(me, (1,)).astype(jnp.int32), choice],
+        [me, choice],
     )[0]
     near, noted = local_call(
         join_body,
         [like(half, width, bf16), like(half + NOTE, width, bf16)],
-        [place, held, *came, note],
+        [held, *came, note],
         0,
         [weights],
     )
     far = swap(near, "lab", 1)
     work = 4 * half * lab_dev * width
     slope_like = like(BLOCK + NOTE, half, bf16)
-    near_dq, near_slope, near_copy = local_call(
+    pair = [like(half // 2, width, f32), like(half // 2, width, bf16)]
+    single = [like(q_home, width, f32), like(q_home, width, bf16)]
+    near_kept, near_sent, near_slope, near_copy = local_call(
         near_body,
-        [like(half, width, f32), slope_like, like(half, width, bf16)],
+        pair + [slope_like, like(half, width, bf16)],
         [near, weights, note],
         work,
     )
     cross_near = swap(noted, "pb", far_bit)
     cross_far = diagonal(near_copy, far_bit, 1)
-    far_dq, far_slope = local_call(
-        far_body,
-        [like(half, width, bf16), slope_like],
-        [far, weights, note],
-        work,
-        [near_dq],
-    )
-    came = swap(far_dq, "lab", 1)
+    far_kept, far_sent, far_slope = local_call(
+        far_body, pair + [slope_like], [far, weights, note], work, [near_slope]
+    )
+    far_came, near_came = swap(far_sent, "lab", 2), swap(near_sent, "lab", 2)
     acc, own = local_call(
         own_body,
         [like(lab_dev, width, f32), like(qcount + BLOCK + NOTE, width, bf16)],
@@ -350,24 +346,24 @@
         work,
     )
     mate = swap(own, "pb", 1)
+    far_kept, far_sent = local_call(fold_body, single, [far_kept, far_came], 0, [acc])
+    far_came = swap(far_sent, "lab", 4)
+    near_kept, near_sent = local_call(fold_body, single, [near_kept, near_came], 0, [far_kept])
+    near_came = swap(near_sent, "lab", 4)
     cross = local_call(
-        stack_body, [like(qcount + NOTE, width, bf16)], [cross_near, cross_far], 0, []
+        stack_body, [like(qcount + NOTE, width, bf16)], [cross_near, cross_far], 0, [far_kept]
     )[0]
     cross_mate = swap(cross, "pb", 1)
     grown = like(lab_dev, width, f32)
-    acc = local_call(cross_body, [grown], [cross, weights, acc], 20 * work)[0]
-    acc = local_call(mate_body, [grown], [mate, acc], work)[0]
-    kept, *terms = local_call(
-        fold_body,
-        [like(q_home, width, f32)] + [like(q_home, width, bf16)] * (homes // 2 - 1),
-        [place, near_dq, came],
-        0,
-        [acc],
-    )
-    terms = [swap(term, "lab", 2 * step) for step, term in enumerate(terms, 1)]
+    acc = local_call(cross_body, [grown], [cross, weights, acc], 20 * work, [near_kept])[0]
+    far_sent = local_call(
+        sum_body, [like(q_home, width, bf16)], [far_kept, far_came], 0, [acc]
+    )[0]
+    far_came = swap(far_sent, "lab", 1)
+    acc = local_call(mate_body, [grown], [mate, acc], work, [far_sent])[0]
     weight_grad, mark = late(groups, cross_mate, weights, acc)
     query_grad = local_call(
-        sum_body, [like(q_home, width, f32)], [kept, *terms], 0, [mark]
+        sum_body, [like(q_home, width, f32)], [near_kept, near_came, far_came], 0, [mark]
     )[0]
     return (query_grad, weight_grad)
 

time: 37.5 us -> 35.6 us (0.949)
  waiting for transfers between devices: 6.85 us -> 5.15 us
    ppermute x11 -> x12, waiting for transfers between devices: 6.19 us -> 5.15 us  [swap(): return lax.ppermute(value, axis, [(i, i ^ bit) for i in range(count)])]
    ppermute x1, waiting for transfers between devices: 0.66 us -> 0.01 us  [diagonal(): return lax.ppermute(value, ('pb', 'lab'), pairs)]
    ppermute x11 -> x12, starting transfers between devices: 16.7 us -> 16.5 us  [swap(): return lax.ppermute(value, axis, [(i, i ^ bit) for i in range(count)])]
    pallas_call x11 -> x13, Pallas kernels: 6.75 us -> 6.76 us  [local_call(): pl.pallas_call(lambda *refs: body(*refs[:given], *refs[later:]), out_shap...]
  transfers between devices with their start and end apart: 12 -> 13, of which waited for: 6 -> 4; matrix products, arithmetic and copies ran while one was open for 2% -> 2% of each run, Pallas kernels for 24% -> 25%
where the time goes in v16:
time: 35.6 us; the launch traced here: 35.3 us
  starting transfers between devices  17 us (48%)
  Pallas kernels  9.47 us (27%)
  waiting for transfers between devices  5.15 us (14%)
  local copies, waits for them, and re-layouts  2.21 us (6%)
  between operations  0.75 us (2%)
  other arithmetic  0.72 us (2%)
    ppermute x12, starting transfers between devices, swap(): return lax.ppermute(value, axis, [(i, i ^ bit) for i in range(count)])  16.5 us
    pallas_call x13, Pallas kernels, local_call(): pl.pallas_call(lambda *refs: body(*refs[:given], *refs[later:]), out_shap...  6.76 us
    ppermute x12, waiting for transfers between devices, swap(): return lax.ppermute(value, axis, [(i, i ^ bit) for i in range(count)])  5.15 us
    pallas_call x1, Pallas kernels, late(): pl.pallas_call(lambda *refs: late_body(groups, *refs), out_shape=[out, li...  2.72 us
    unnamed x4, local copies, waits for them, and re-layouts  2.21 us
    convert_element_type x1, other arithmetic, dense_shards(): jnp.concatenate([sibling_blocks.T, positive_slot[None]], axis=0).astype(f32)  0.72 us
  transfers between devices with their start and end apart: 13, of which 4 were waited for; matrix products, arithmetic and copies ran while one was open for 2% of the time, Pallas kernels for 25%

profile of v16, /device:TPU:0, one launch (start us, length us, event | category | flops | bytes accessed | tf_op | source)
XLA Modules:
  0.0 35.3 jit_solution(2940903855193388081)
XLA Ops:
  0.6 3.1 %collective-permute-start = (bf16[32,768]{1,0:T(8,128)(2,1)}, bf16[32,768]{1,0:T(8,128)(2,1)S(1)}, u32[]{:S(2)}, u32[]{:S(2)}) collective-permute-start(bf16[32,768]{1,0:T(8,128)(2,1)} %refs_0_.1), channel_id=1, source_target_pairs={{0,2},{1,3},{2,0},{3,1},{4,6},{5,7},{6,4},{7,5},{8,10},{9,11},{10,... | collective-permute-start | bytes 147464 | tf_op jit(solution)/shard_map/ppermute | solution.py:77
  3.7 2.5 %collective-permute-start.2 = (bf16[32,768]{1,0:T(8,128)(2,1)}, bf16[32,768]{1,0:T(8,128)(2,1)S(1)}, u32[]{:S(2)}, u32[]{:S(2)}) collective-permute-start(bf16[32,768]{1,0:T(8,128)(2,1)} %refs_0_.1), channel_id=1, source_target_pairs={{0,6},{1,7},{2,4},{3,5},{4,2},{5,3},{6,0},{7,1},{8,14},{9,15},{10,... | collective-permute-start | bytes 147464 | tf_op jit(solution)/shard_map/ppermute | solution.py:77
  6.3 0.7 %add_convert_fusion.refs_1_ = f32[9,256]{1,0:T(8,128)S(1)} fusion(s32[1,256]{1,0:T(1,128)} %bitcast.4, s32[8,256]{1,0:T(8,128)} %bitcast.3), kind=kLoop, calls=%fused_computation | loop fusion | flops 4608 | bytes 18432 | tf_op jit(solution)/shard_map/convert_element_type | solution.py:312
  7.0 1.4 %copy-done = bf16[1024,768]{1,0:T(8,128)(2,1)S(1)} copy-done((bf16[1024,768]{1,0:T(8,128)(2,1)S(1)}, bf16[1024,768]{1,0:T(8,128)(2,1)}, u32[]{:S(2)}) %copy-start) | copy-done | bytes 1572888
  8.4 0.8 %copy-done.1 = bf16[32,768]{1,0:T(8,128)(2,1)S(1)} copy-done((bf16[32,768]{1,0:T(8,128)(2,1)S(1)}, bf16[32,768]{1,0:T(8,128)(2,1)}, u32[]{:S(2)}) %copy-start.1) | copy-done | bytes 49176
  9.5 0.9 %collective-permute-done.2.refs_3_ = bf16[32,768]{1,0:T(8,128)(2,1)S(1)} collective-permute-done((bf16[32,768]{1,0:T(8,128)(2,1)}, bf16[32,768]{1,0:T(8,128)(2,1)S(1)}, u32[]{:S(2)}, u32[]{:S(2)}) %collective-permute-start.2) | collective-permute-done | bytes 49184 | tf_op jit(solution)/shard_map/ppermute | solution.py:77
  10.4 1.5 %collective-permute-done.1.refs_2_ = bf16[32,768]{1,0:T(8,128)(2,1)S(1)} collective-permute-done((bf16[32,768]{1,0:T(8,128)(2,1)}, bf16[32,768]{1,0:T(8,128)(2,1)S(1)}, u32[]{:S(2)}, u32[]{:S(2)}) %collective-permute-start.1) | collective-permute-done | bytes 49184 | tf_op jit(solution)/shard_map/ppermute | solution.py:77
  12.0 1.6 %collective-permute-start.4 = (bf16[128,768]{1,0:T(8,128)(2,1)S(1)}, bf16[128,768]{1,0:T(8,128)(2,1)S(1)}, u32[]{:S(2)}, u32[]{:S(2)}) collective-permute-start(bf16[128,768]{1,0:T(8,128)(2,1)S(1)} %get-tuple-element.23.refs_0_), channel_id=1, source_target_pairs={{0,1},{1,0},{2,3},{3,2},{4,5},{5,4},{6,7},{7,6},{8,9},{9,8},{10,11... | collective-permute-start | bytes 589832 | tf_op jit(solution)/shard_map/ppermute | solution.py:77
  13.5 1.5 %collective-permute-start.8 = (bf16[144,768]{1,0:T(8,128)(2,1)S(1)}, bf16[144,768]{1,0:T(8,128)(2,1)S(1)}, u32[]{:S(2)}, u32[]{:S(2)}) collective-permute-start(bf16[144,768]{1,0:T(8,128)(2,1)S(1)} %get-tuple-element.35), channel_id=1, source_target_pairs={{0,16},{8,24},{16,0},{24,8},{1,17},{9,25},{17,1},{25,9},{2,18},{10... | collective-permute-start | bytes 663560 | tf_op jit(solution)/shard_map/ppermute | solution.py:77
  15.0 1.3 %shard_map.62 = (f32[64,768]{1,0:T(8,128)S(1)}, bf16[64,768]{1,0:T(8,128)(2,1)S(1)}, bf16[144,128]{1,0:T(8,128)(2,1)S(1)}, bf16[128,768]{1,0:T(8,128)(2,1)S(1)}) custom-call(bf16[128,768]{1,0:T(8,128)(2,1)S(1)} %get-tuple-element.23.refs_0_, bf16[1024,768]{1,0:T(8,128)(2,1)S(1)} %get-tuple-element.22.refs_5_.refs_1_, ...), custom_call_target="tpu_custom_call" | custom-call | flops 402653184 | tf_op jit(solution)/shard_map/pallas_call | solution.py:96
  16.4 0.5 %collective-permute-start.9 = (bf16[128,768]{1,0:T(8,128)(2,1)S(1)}, bf16[128,768]{1,0:T(8,128)(2,1)S(1)}, u32[]{:S(2)}, u32[]{:S(2)}) collective-permute-start(bf16[128,768]{1,0:T(8,128)(2,1)S(1)} %get-tuple-element.36), channel_id=1, source_target_pairs={{0,17},{1,16},{2,19},{3,18},{4,21},{5,20},{6,23},{7,22},{8,25},{9,... | collective-permute-start | bytes 589832 | tf_op jit(solution)/shard_map/ppermute | solution.py:87
  16.9 0.8 %collective-permute-done.4.refs_0_.refs_1_ = bf16[128,768]{1,0:T(8,128)(2,1)S(1)} collective-permute-done((bf16[128,768]{1,0:T(8,128)(2,1)S(1)}, bf16[128,768]{1,0:T(8,128)(2,1)S(1)}, u32[]{:S(2)}, u32[]{:S(2)}) %collective-permute-start.4) | collective-permute-done | bytes 196640 | tf_op jit(solution)/shard_map/ppermute | solution.py:77
  17.7 1.3 %shard_map.63 = (f32[64,768]{1,0:T(8,128)S(1)}, bf16[64,768]{1,0:T(8,128)(2,1)S(1)}, bf16[144,128]{1,0:T(8,128)(2,1)S(1)}) custom-call(bf16[128,768]{1,0:T(8,128)(2,1)S(1)} %collective-permute-done.4.refs_0_.refs_1_, bf16[1024,768]{1,0:T(8,128)(2,1)S(1)} %get-tuple-element.22.refs_5_.refs_1_, bf16[16,768]{1,0:T(8,128)(2,1)S(1)} %shard_map.60.refs_4_.refs_2_, ...), custom_call_target="tpu_custom_call" | custom-call | flops 402653184 | tf_op jit(solution)/shard_map/pallas_call | solution.py:96
  19.0 0.3 collective-permute-start.5
  19.3 1.8 %collective-permute-start.3 = (bf16[64,768]{1,0:T(8,128)(2,1)S(1)}, bf16[64,768]{1,0:T(8,128)(2,1)S(1)}, u32[]{:S(2)}, u32[]{:S(2)}) collective-permute-start(bf16[64,768]{1,0:T(8,128)(2,1)S(1)} %get-tuple-element.25), channel_id=1, source_target_pairs={{0,2},{1,3},{2,0},{3,1},{4,6},{5,7},{6,4},{7,5},{8,10},{9,11},{10,... | collective-permute-start | bytes 294920 | tf_op jit(solution)/shard_map/ppermute | solution.py:77
  21.1 0.6 %shard_map.64 = (f32[1024,768]{1,0:T(8,128)S(1)}, bf16[400,768]{1,0:T(8,128)(2,1)S(1)}) custom-call(bf16[128,768]{1,0:T(8,128)(2,1)S(1)} %get-tuple-element.23.refs_0_, bf16[128,768]{1,0:T(8,128)(2,1)S(1)} %collective-permute-done.4.refs_0_.refs_1_, bf16[144,128]{1,0:T(8,128)(2,1)S(1)} %get-tuple-element.26.refs_3_.refs_2_, ...), custom_call_target="tpu_custom_call" | custom-call | flops 402653184 | tf_op jit(solution)/shard_map/pallas_call | solution.py:96
  21.8 1.9 %collective-permute-done.5.refs_1_ = bf16[64,768]{1,0:T(8,128)(2,1)S(1)} collective-permute-done((bf16[64,768]{1,0:T(8,128)(2,1)S(1)}, bf16[64,768]{1,0:T(8,128)(2,1)S(1)}, u32[]{:S(2)}, u32[]{:S(2)}) %collective-permute-start.5) | collective-permute-done | bytes 98336 | tf_op jit(solution)/shard_map/ppermute | solution.py:77
  23.7 1.3 %collective-permute-start.7 = (bf16[32,768]{1,0:T(8,128)(2,1)S(1)}, bf16[32,768]{1,0:T(8,128)(2,1)S(1)}, u32[]{:S(2)}, u32[]{:S(2)}) collective-permute-start(bf16[32,768]{1,0:T(8,128)(2,1)S(1)} %get-tuple-element.34), channel_id=1, source_target_pairs={{0,4},{1,5},{2,6},{3,7},{4,0},{5,1},{6,2},{7,3},{8,12},{9,13},{10,... | collective-permute-start | bytes 147464 | tf_op jit(solution)/shard_map/ppermute | solution.py:77
  25.2 1.9 %shard_map.68.refs_2_.refs_1_ = f32[1024,768]{1,0:T(8,128)S(1)} custom-call(bf16[272,768]{1,0:T(8,128)(2,1)S(1)} %shard_map.67.refs_0_, bf16[1024,768]{1,0:T(8,128)(2,1)S(1)} %get-tuple-element.22.refs_5_.refs_1_, f32[1024,768]{1,0:T(8,128)S(1)} %get-tuple-element.30.refs_2_, f32[32,768]{1,0:T(8,128)S(1)} %get-tuple-element.32.refs_3_.refs_0_), custom_call_target="tpu_custom_call" | custom-call | flops 8053063680 | tf_op jit(solution)/shard_map/pallas_call | solution.py:96
  27.1 2.2 %collective-permute-start.6 = (bf16[32,768]{1,0:T(8,128)(2,1)S(1)}, bf16[32,768]{1,0:T(8,128)(2,1)S(1)}, u32[]{:S(2)}, u32[]{:S(2)}) collective-permute-start(bf16[32,768]{1,0:T(8,128)(2,1)S(1)} %get-tuple-element.33), channel_id=1, source_target_pairs={{0,4},{1,5},{2,6},{3,7},{4,0},{5,1},{6,2},{7,3},{8,12},{9,13},{10,... | collective-permute-start | bytes 147464 | tf_op jit(solution)/shard_map/ppermute | solution.py:77
  29.3 2.0 %collective-permute-start.10 = (bf16[32,768]{1,0:T(8,128)(2,1)S(1)}, bf16[32,768]{1,0:T(8,128)(2,1)S(1)}, u32[]{:S(2)}, u32[]{:S(2)}) collective-permute-start(bf16[32,768]{1,0:T(8,128)(2,1)S(1)} %shard_map.69.refs_2_), channel_id=1, source_target_pairs={{0,1},{1,0},{2,3},{3,2},{4,5},{5,4},{6,7},{7,6},{8,9},{9,8},{10,11... | collective-permute-start | bytes 147464 | tf_op jit(solution)/shard_map/ppermute | solution.py:77
  31.3 0.6 %shard_map.70.refs_2_ = f32[1024,768]{1,0:T(8,128)S(1)} custom-call(bf16[400,768]{1,0:T(8,128)(2,1)S(1)} %collective-permute-done.12.refs_0_, f32[1024,768]{1,0:T(8,128)S(1)} %shard_map.68.refs_2_.refs_1_, bf16[32,768]{1,0:T(8,128)(2,1)S(1)} %shard_map.69.refs_2_), custom_call_target="tpu_custom_call" | custom-call | flops 402653184 | tf_op jit(solution)/shard_map/pallas_call | solution.py:96
  31.9 2.7 %shard_map.71 = (bf16[1024,768]{1,0:T(8,128)(2,1)}, s32[1,128]{1,0:T(1,128)S(1)}) custom-call(bf16[272,768]{1,0:T(8,128)(2,1)S(1)} %collective-permute-done.11.refs_0_, bf16[1024,768]{1,0:T(8,128)(2,1)S(1)} %get-tuple-element.22.refs_5_.refs_1_, f32[1024,768]{1,0:T(8,128)S(1)} %shard_map.70.refs_2_), custom_call_target="tpu_custom_call" | custom-call | tf_op jit(solution)/shard_map/pallas_call | solution.py:259
  34.7 0.7 %shard_map.72 = f32[32,768]{1,0:T(8,128)} custom-call(f32[32,768]{1,0:T(8,128)S(1)} %get-tuple-element.32.refs_3_.refs_0_, bf16[32,768]{1,0:T(8,128)(2,1)S(1)} %collective-permute-done.6.refs_1_, bf16[32,768]{1,0:T(8,128)(2,1)S(1)} %collective-permute-done.10.refs_2_, s32[1,128]{1,0:T(1,128)S(1)} %get-tuple-element.38.refs_3_), custom_call_target="tpu_custom_call" | custom-call | tf_op jit(solution)/shard_map/pallas_call | solution.py:96
  (21 shorter events, 0.7 us)
Async XLA Ops:
  0.6 8.9 %collective-permute-start = (bf16[32,768]{1,0:T(8,128)(2,1)}, bf16[32,768]{1,0:T(8,128)(2,1)S(1)}, u32[]{:S(2)}, u32[]{:S(2)}) collective-permute-start(bf16[32,768]{1,0:T(8,128)(2,1)} %refs_0_.1), channel_id=1, source_target_pairs={{0,2},{1,3},{2,0},{3,1},{4,6},{5,7},{6,4},{7,5},{8,10},{9,11},{10,... | collective-permute-start | bytes 147464 | tf_op jit(solution)/shard_map/ppermute | solution.py:77
  3.7 6.7 %collective-permute-start.2 = (bf16[32,768]{1,0:T(8,128)(2,1)}, bf16[32,768]{1,0:T(8,128)(2,1)S(1)}, u32[]{:S(2)}, u32[]{:S(2)}) collective-permute-start(bf16[32,768]{1,0:T(8,128)(2,1)} %refs_0_.1), channel_id=1, source_target_pairs={{0,6},{1,7},{2,4},{3,5},{4,2},{5,3},{6,0},{7,1},{8,14},{9,15},{10,... | collective-permute-start | bytes 147464 | tf_op jit(solution)/shard_map/ppermute | solution.py:77
  6.2 5.7 %collective-permute-start.1 = (bf16[32,768]{1,0:T(8,128)(2,1)}, bf16[32,768]{1,0:T(8,128)(2,1)S(1)}, u32[]{:S(2)}, u32[]{:S(2)}) collective-permute-start(bf16[32,768]{1,0:T(8,128)(2,1)} %refs_0_.1), channel_id=1, source_target_pairs={{0,4},{1,5},{2,6},{3,7},{4,0},{5,1},{6,2},{7,3},{8,12},{9,13},{10,... | collective-permute-start | bytes 147464 | tf_op jit(solution)/shard_map/ppermute | solution.py:77
  7.0 1.4 %copy-start = (bf16[1024,768]{1,0:T(8,128)(2,1)S(1)}, bf16[1024,768]{1,0:T(8,128)(2,1)}, u32[]{:S(2)}) copy-start(bf16[1024,768]{1,0:T(8,128)(2,1)} %refs_1_.1) | copy-start | bytes 4718596
  8.4 0.8 %copy-start.1 = (bf16[32,768]{1,0:T(8,128)(2,1)S(1)}, bf16[32,768]{1,0:T(8,128)(2,1)}, u32[]{:S(2)}) copy-start(bf16[32,768]{1,0:T(8,128)(2,1)} %refs_0_.1) | copy-start | bytes 147460
  12.0 5.7 %collective-permute-start.4 = (bf16[128,768]{1,0:T(8,128)(2,1)S(1)}, bf16[128,768]{1,0:T(8,128)(2,1)S(1)}, u32[]{:S(2)}, u32[]{:S(2)}) collective-permute-start(bf16[128,768]{1,0:T(8,128)(2,1)S(1)} %get-tuple-element.23.refs_0_), channel_id=1, source_target_pairs={{0,1},{1,0},{2,3},{3,2},{4,5},{5,4},{6,7},{7,6},{8,9},{9,8},{10,11... | collective-permute-start | bytes 589832 | tf_op jit(solution)/shard_map/ppermute | solution.py:77
  13.5 11.5 %collective-permute-start.8 = (bf16[144,768]{1,0:T(8,128)(2,1)S(1)}, bf16[144,768]{1,0:T(8,128)(2,1)S(1)}, u32[]{:S(2)}, u32[]{:S(2)}) collective-permute-start(bf16[144,768]{1,0:T(8,128)(2,1)S(1)} %get-tuple-element.35), channel_id=1, source_target_pairs={{0,16},{8,24},{16,0},{24,8},{1,17},{9,25},{17,1},{25,9},{2,18},{10... | collective-permute-start | bytes 663560 | tf_op jit(solution)/shard_map/ppermute | solution.py:77
  16.4 8.6 %collective-permute-start.9 = (bf16[128,768]{1,0:T(8,128)(2,1)S(1)}, bf16[128,768]{1,0:T(8,128)(2,1)S(1)}, u32[]{:S(2)}, u32[]{:S(2)}) collective-permute-start(bf16[128,768]{1,0:T(8,128)(2,1)S(1)} %get-tuple-element.36), channel_id=1, source_target_pairs={{0,17},{1,16},{2,19},{3,18},{4,21},{5,20},{6,23},{7,22},{8,25},{9,... | collective-permute-start | bytes 589832 | tf_op jit(solution)/shard_map/ppermute | solution.py:87
  19.0 4.7 %collective-permute-start.5 = (bf16[64,768]{1,0:T(8,128)(2,1)S(1)}, bf16[64,768]{1,0:T(8,128)(2,1)S(1)}, u32[]{:S(2)}, u32[]{:S(2)}) collective-permute-start(bf16[64,768]{1,0:T(8,128)(2,1)S(1)} %get-tuple-element.28), channel_id=1, source_target_pairs={{0,2},{1,3},{2,0},{3,1},{4,6},{5,7},{6,4},{7,5},{8,10},{9,11},{10,... | collective-permute-start | bytes 294920 | tf_op jit(solution)/shard_map/ppermute | solution.py:77
  19.3 5.8 %collective-permute-start.3 = (bf16[64,768]{1,0:T(8,128)(2,1)S(1)}, bf16[64,768]{1,0:T(8,128)(2,1)S(1)}, u32[]{:S(2)}, u32[]{:S(2)}) collective-permute-start(bf16[64,768]{1,0:T(8,128)(2,1)S(1)} %get-tuple-element.25), channel_id=1, source_target_pairs={{0,2},{1,3},{2,0},{3,1},{4,6},{5,7},{6,4},{7,5},{8,10},{9,11},{10,... | collective-permute-start | bytes 294920 | tf_op jit(solution)/shard_map/ppermute | solution.py:77
  21.7 9.7 %collective-permute-start.12 = (bf16[400,768]{1,0:T(8,128)(2,1)S(1)}, bf16[400,768]{1,0:T(8,128)(2,1)S(1)}, u32[]{:S(2)}, u32[]{:S(2)}) collective-permute-start(bf16[400,768]{1,0:T(8,128)(2,1)S(1)} %get-tuple-element.37), channel_id=1, source_target_pairs={{0,8},{8,0},{16,24},{24,16},{1,9},{9,1},{17,25},{25,17},{2,10},{10... | collective-permute-start | bytes 1843208 | tf_op jit(solution)/shard_map/ppermute | solution.py:77
  23.7 5.6 %collective-permute-start.7 = (bf16[32,768]{1,0:T(8,128)(2,1)S(1)}, bf16[32,768]{1,0:T(8,128)(2,1)S(1)}, u32[]{:S(2)}, u32[]{:S(2)}) collective-permute-start(bf16[32,768]{1,0:T(8,128)(2,1)S(1)} %get-tuple-element.34), channel_id=1, source_target_pairs={{0,4},{1,5},{2,6},{3,7},{4,0},{5,1},{6,2},{7,3},{8,12},{9,13},{10,... | collective-permute-start | bytes 147464 | tf_op jit(solution)/shard_map/ppermute | solution.py:77
  25.1 6.9 %collective-permute-start.11 = (bf16[272,768]{1,0:T(8,128)(2,1)S(1)}, bf16[272,768]{1,0:T(8,128)(2,1)S(1)}, u32[]{:S(2)}, u32[]{:S(2)}) collective-permute-start(bf16[272,768]{1,0:T(8,128)(2,1)S(1)} %shard_map.67.refs_0_), channel_id=1, source_target_pairs={{0,8},{8,0},{16,24},{24,16},{1,9},{9,1},{17,25},{25,17},{2,10},{10... | collective-permute-start | bytes 1253384 | tf_op jit(solution)/shard_map/ppermute | solution.py:77
  27.1 7.6 %collective-permute-start.6 = (bf16[32,768]{1,0:T(8,128)(2,1)S(1)}, bf16[32,768]{1,0:T(8,128)(2,1)S(1)}, u32[]{:S(2)}, u32[]{:S(2)}) collective-permute-start(bf16[32,768]{1,0:T(8,128)(2,1)S(1)} %get-tuple-element.33), channel_id=1, source_target_pairs={{0,4},{1,5},{2,6},{3,7},{4,0},{5,1},{6,2},{7,3},{8,12},{9,13},{10,... | collective-permute-start | bytes 147464 | tf_op jit(solution)/shard_map/ppermute | solution.py:77
  29.3 5.3 %collective-permute-start.10 = (bf16[32,768]{1,0:T(8,128)(2,1)S(1)}, bf16[32,768]{1,0:T(8,128)(2,1)S(1)}, u32[]{:S(2)}, u32[]{:S(2)}) collective-permute-start(bf16[32,768]{1,0:T(8,128)(2,1)S(1)} %shard_map.69.refs_2_), channel_id=1, source_target_pairs={{0,1},{1,0},{2,3},{3,2},{4,5},{5,4},{6,7},{7,6},{8,9},{9,8},{10,11... | collective-permute-start | bytes 147464 | tf_op jit(solution)/shard_map/ppermute | solution.py:77

commit v17 on v16

--- a/solution.py
+++ b/solution.py
@@ -174,9 +174,19 @@
     grad_body(1, rows_ref, weights_ref, note_ref, kept_ref, sent_ref, slope_ref)
 
 
-def fold_body(terms_ref, came_ref, kept_ref, sent_ref):
-    terms = terms_ref[...] + came_ref[...].astype(jnp.float32)
-    halve(terms, kept_ref, sent_ref, kept_ref.shape[0])
+def fold_body(far_ref, far_came_ref, near_ref, near_came_ref, far_kept, near_kept, sent_ref):
+    span = far_kept.shape[0]
+    far = far_ref[...] + far_came_ref[...].astype(jnp.float32)
+    near = near_ref[...] + near_came_ref[...].astype(jnp.float32)
+    halve(far, far_kept, sent_ref.at[:span], span)
+    halve(near, near_kept, sent_ref.at[span:], span)
+
+
+def home_body(far_ref, near_ref, came_ref, sent_ref, kept_ref):
+    span = far_ref.shape[0]
+    came = came_ref[...].astype(jnp.float32)
+    sent_ref[...] = (far_ref[...] + came[:span]).astype(sent_ref.dtype)
+    kept_ref[...] = near_ref[...] + came[span:]
 
 
 def sum_body(kept_ref, *refs):
@@ -326,7 +336,6 @@
     work = 4 * half * lab_dev * width
     slope_like = like(BLOCK + NOTE, half, bf16)
     pair = [like(half // 2, width, f32), like(half // 2, width, bf16)]
-    single = [like(q_home, width, f32), like(q_home, width, bf16)]
     near_kept, near_sent, near_slope, near_copy = local_call(
         near_body,
         pair + [slope_like, like(half, width, bf16)],
@@ -346,25 +355,28 @@
         work,
     )
     mate = swap(own, "pb", 1)
-    far_kept, far_sent = local_call(fold_body, single, [far_kept, far_came], 0, [acc])
-    far_came = swap(far_sent, "lab", 4)
-    near_kept, near_sent = local_call(fold_body, single, [near_kept, near_came], 0, [far_kept])
-    near_came = swap(near_sent, "lab", 4)
+    single = like(q_home, width, f32)
+    far_kept, near_kept, sent = local_call(
+        fold_body,
+        [single, single, like(2 * q_home, width, bf16)],
+        [far_kept, far_came, near_kept, near_came],
+        0,
+        [acc],
+    )
+    came = swap(sent, "lab", 4)
     cross = local_call(
         stack_body, [like(qcount + NOTE, width, bf16)], [cross_near, cross_far], 0, [far_kept]
     )[0]
     cross_mate = swap(cross, "pb", 1)
     grown = like(lab_dev, width, f32)
-    acc = local_call(cross_body, [grown], [cross, weights, acc], 20 * work, [near_kept])[0]
-    far_sent = local_call(
-        sum_body, [like(q_home, width, bf16)], [far_kept, far_came], 0, [acc]
-    )[0]
+    acc = local_call(cross_body, [grown], [cross, weights, acc], 20 * work)[0]
+    acc = local_call(mate_body, [grown], [mate, acc], work)[0]
+    far_sent, kept = local_call(
+        home_body, [like(q_home, width, bf16), single], [far_kept, near_kept, came], 0, [acc]
+    )
     far_came = swap(far_sent, "lab", 1)
-    acc = local_call(mate_body, [grown], [mate, acc], work, [far_sent])[0]
     weight_grad, mark = late(groups, cross_mate, weights, acc)
-    query_grad = local_call(
-        sum_body, [like(q_home, width, f32)], [near_kept, near_came, far_came], 0, [mark]
-    )[0]
+    query_grad = local_call(sum_body, [single], [kept, far_came], 0, [mark])[0]
     return (query_grad, weight_grad)
 
 

time: 35.6 us -> 37 us (1.039)
  waiting for transfers between devices: 5.15 us -> 9.94 us
  starting transfers between devices: 17 us -> 13.7 us
    ppermute x12 -> x11, waiting for transfers between devices: 5.15 us -> 9.93 us  [swap(): return lax.ppermute(value, axis, [(i, i ^ bit) for i in range(count)])]
    ppermute x12 -> x11, starting transfers between devices: 16.5 us -> 13.2 us  [swap(): return lax.ppermute(value, axis, [(i, i ^ bit) for i in range(count)])]
    pallas_call x13 -> x12, Pallas kernels: 6.76 us -> 6.76 us  [local_call(): pl.pallas_call(lambda *refs: body(*refs[:given], *refs[later:]), out_shap...]
  transfers between devices with their start and end apart: 13 -> 12, of which waited for: 4 -> 6; matrix products, arithmetic and copies ran while one was open for 2% -> 2% of each run, Pallas kernels for 25% -> 24%
where the time goes in v17:
time: 37 us; the launch traced here: 36.8 us
  starting transfers between devices  13.7 us (37%)
  waiting for transfers between devices  9.94 us (27%)
  Pallas kernels  9.45 us (26%)
  local copies, waits for them, and re-layouts  2.21 us (6%)
  between operations  0.73 us (2%)
  other arithmetic  0.72 us (2%)
    ppermute x11, starting transfers between devices, swap(): return lax.ppermute(value, axis, [(i, i ^ bit) for i in range(count)])  13.2 us
    ppermute x11, waiting for transfers between devices, swap(): return lax.ppermute(value, axis, [(i, i ^ bit) for i in range(count)])  9.93 us
    pallas_call x12, Pallas kernels, local_call(): pl.pallas_call(lambda *refs: body(*refs[:given], *refs[later:]), out_shap...  6.76 us
    pallas_call x1, Pallas kernels, late(): pl.pallas_call(lambda *refs: late_body(groups, *refs), out_shape=[out, li...  2.7 us
    unnamed x4, local copies, waits for them, and re-layouts  2.21 us
  transfers between devices with their start and end apart: 12, of which 6 were waited for; matrix products, arithmetic and copies ran while one was open for 2% of the time, Pallas kernels for 24%

profile of v17, /device:TPU:0, one launch (start us, length us, event | category | flops | bytes accessed | tf_op | source)
XLA Modules:
  0.0 36.8 jit_solution(7277938433953313213)
XLA Ops:
  0.6 3.1 %collective-permute-start = (bf16[32,768]{1,0:T(8,128)(2,1)}, bf16[32,768]{1,0:T(8,128)(2,1)S(1)}, u32[]{:S(2)}, u32[]{:S(2)}) collective-permute-start(bf16[32,768]{1,0:T(8,128)(2,1)} %refs_0_.1), channel_id=1, source_target_pairs={{0,2},{1,3},{2,0},{3,1},{4,6},{5,7},{6,4},{7,5},{8,10},{9,11},{10,... | collective-permute-start | bytes 147464 | tf_op jit(solution)/shard_map/ppermute | solution.py:77
  3.7 2.6 %collective-permute-start.1 = (bf16[32,768]{1,0:T(8,128)(2,1)}, bf16[32,768]{1,0:T(8,128)(2,1)S(1)}, u32[]{:S(2)}, u32[]{:S(2)}) collective-permute-start(bf16[32,768]{1,0:T(8,128)(2,1)} %refs_0_.1), channel_id=1, source_target_pairs={{0,4},{1,5},{2,6},{3,7},{4,0},{5,1},{6,2},{7,3},{8,12},{9,13},{10,... | collective-permute-start | bytes 147464 | tf_op jit(solution)/shard_map/ppermute | solution.py:77
  6.3 0.7 %add_convert_fusion.refs_1_ = f32[9,256]{1,0:T(8,128)S(1)} fusion(s32[1,256]{1,0:T(1,128)} %bitcast.4, s32[8,256]{1,0:T(8,128)} %bitcast.3), kind=kLoop, calls=%fused_computation | loop fusion | flops 4608 | bytes 18432 | tf_op jit(solution)/shard_map/convert_element_type | solution.py:322
  7.0 1.4 %copy-done = bf16[1024,768]{1,0:T(8,128)(2,1)S(1)} copy-done((bf16[1024,768]{1,0:T(8,128)(2,1)S(1)}, bf16[1024,768]{1,0:T(8,128)(2,1)}, u32[]{:S(2)}) %copy-start) | copy-done | bytes 1572888
  8.4 0.8 %copy-done.1 = bf16[32,768]{1,0:T(8,128)(2,1)S(1)} copy-done((bf16[32,768]{1,0:T(8,128)(2,1)S(1)}, bf16[32,768]{1,0:T(8,128)(2,1)}, u32[]{:S(2)}) %copy-start.1) | copy-done | bytes 49176
  9.5 0.3 collective-permute-done.1.refs_2_
  9.9 2.6 %collective-permute-done.2.refs_3_ = bf16[32,768]{1,0:T(8,128)(2,1)S(1)} collective-permute-done((bf16[32,768]{1,0:T(8,128)(2,1)}, bf16[32,768]{1,0:T(8,128)(2,1)S(1)}, u32[]{:S(2)}, u32[]{:S(2)}) %collective-permute-start.2) | collective-permute-done | bytes 49184 | tf_op jit(solution)/shard_map/ppermute | solution.py:77
  12.4 1.6 %collective-permute-start.3 = (bf16[128,768]{1,0:T(8,128)(2,1)S(1)}, bf16[128,768]{1,0:T(8,128)(2,1)S(1)}, u32[]{:S(2)}, u32[]{:S(2)}) collective-permute-start(bf16[128,768]{1,0:T(8,128)(2,1)S(1)} %get-tuple-element.24.refs_0_), channel_id=1, source_target_pairs={{0,1},{1,0},{2,3},{3,2},{4,5},{5,4},{6,7},{7,6},{8,9},{9,8},{10,11... | collective-permute-start | bytes 589832 | tf_op jit(solution)/shard_map/ppermute | solution.py:77
  14.0 1.5 %collective-permute-start.8 = (bf16[144,768]{1,0:T(8,128)(2,1)S(1)}, bf16[144,768]{1,0:T(8,128)(2,1)S(1)}, u32[]{:S(2)}, u32[]{:S(2)}) collective-permute-start(bf16[144,768]{1,0:T(8,128)(2,1)S(1)} %get-tuple-element.36), channel_id=1, source_target_pairs={{0,16},{8,24},{16,0},{24,8},{1,17},{9,25},{17,1},{25,9},{2,18},{10... | collective-permute-start | bytes 663560 | tf_op jit(solution)/shard_map/ppermute | solution.py:77
  15.5 1.3 %shard_map.62 = (f32[64,768]{1,0:T(8,128)S(1)}, bf16[64,768]{1,0:T(8,128)(2,1)S(1)}, bf16[144,128]{1,0:T(8,128)(2,1)S(1)}, bf16[128,768]{1,0:T(8,128)(2,1)S(1)}) custom-call(bf16[128,768]{1,0:T(8,128)(2,1)S(1)} %get-tuple-element.24.refs_0_, bf16[1024,768]{1,0:T(8,128)(2,1)S(1)} %get-tuple-element.23.refs_5_.refs_1_, ...), custom_call_target="tpu_custom_call" | custom-call | flops 402653184 | tf_op jit(solution)/shard_map/pallas_call | solution.py:96
  16.9 0.5 %collective-permute-start.9 = (bf16[128,768]{1,0:T(8,128)(2,1)S(1)}, bf16[128,768]{1,0:T(8,128)(2,1)S(1)}, u32[]{:S(2)}, u32[]{:S(2)}) collective-permute-start(bf16[128,768]{1,0:T(8,128)(2,1)S(1)} %get-tuple-element.37), channel_id=1, source_target_pairs={{0,17},{1,16},{2,19},{3,18},{4,21},{5,20},{6,23},{7,22},{8,25},{9,... | collective-permute-start | bytes 589832 | tf_op jit(solution)/shard_map/ppermute | solution.py:87
  17.4 1.2 %collective-permute-done.3.refs_0_.refs_1_ = bf16[128,768]{1,0:T(8,128)(2,1)S(1)} collective-permute-done((bf16[128,768]{1,0:T(8,128)(2,1)S(1)}, bf16[128,768]{1,0:T(8,128)(2,1)S(1)}, u32[]{:S(2)}, u32[]{:S(2)}) %collective-permute-start.3) | collective-permute-done | bytes 196640 | tf_op jit(solution)/shard_map/ppermute | solution.py:77
  18.6 1.3 %shard_map.63 = (f32[64,768]{1,0:T(8,128)S(1)}, bf16[64,768]{1,0:T(8,128)(2,1)S(1)}, bf16[144,128]{1,0:T(8,128)(2,1)S(1)}) custom-call(bf16[128,768]{1,0:T(8,128)(2,1)S(1)} %collective-permute-done.3.refs_0_.refs_1_, bf16[1024,768]{1,0:T(8,128)(2,1)S(1)} %get-tuple-element.23.refs_5_.refs_1_, bf16[16,768]{1,0:T(8,128)(2,1)S(1)} %shard_map.60.refs_4_.refs_2_, ...), custom_call_target="tpu_custom_call" | custom-call | flops 402653184 | tf_op jit(solution)/shard_map/pallas_call | solution.py:96
  19.9 0.9 %collective-permute-start.4 = (bf16[64,768]{1,0:T(8,128)(2,1)S(1)}, bf16[64,768]{1,0:T(8,128)(2,1)S(1)}, u32[]{:S(2)}, u32[]{:S(2)}) collective-permute-start(bf16[64,768]{1,0:T(8,128)(2,1)S(1)} %get-tuple-element.27), channel_id=1, source_target_pairs={{0,2},{1,3},{2,0},{3,1},{4,6},{5,7},{6,4},{7,5},{8,10},{9,11},{10,... | collective-permute-start | bytes 294920 | tf_op jit(solution)/shard_map/ppermute | solution.py:77
  20.8 0.6 %shard_map.64 = (f32[1024,768]{1,0:T(8,128)S(1)}, bf16[400,768]{1,0:T(8,128)(2,1)S(1)}) custom-call(bf16[128,768]{1,0:T(8,128)(2,1)S(1)} %get-tuple-element.24.refs_0_, bf16[128,768]{1,0:T(8,128)(2,1)S(1)} %collective-permute-done.3.refs_0_.refs_1_, bf16[144,128]{1,0:T(8,128)(2,1)S(1)} %get-tuple-element.25.refs_3_.refs_2_, ...), custom_call_target="tpu_custom_call" | custom-call | flops 402653184 | tf_op jit(solution)/shard_map/pallas_call | solution.py:96
  21.5 0.5 %collective-permute-done.5.refs_3_ = bf16[64,768]{1,0:T(8,128)(2,1)S(1)} collective-permute-done((bf16[64,768]{1,0:T(8,128)(2,1)S(1)}, bf16[64,768]{1,0:T(8,128)(2,1)S(1)}, u32[]{:S(2)}, u32[]{:S(2)}) %collective-permute-start.5) | collective-permute-done | bytes 98336 | tf_op jit(solution)/shard_map/ppermute | solution.py:77
  22.0 2.6 %collective-permute-done.4.refs_1_ = bf16[64,768]{1,0:T(8,128)(2,1)S(1)} collective-permute-done((bf16[64,768]{1,0:T(8,128)(2,1)S(1)}, bf16[64,768]{1,0:T(8,128)(2,1)S(1)}, u32[]{:S(2)}, u32[]{:S(2)}) %collective-permute-start.4) | collective-permute-done | bytes 98336 | tf_op jit(solution)/shard_map/ppermute | solution.py:77
  24.6 1.2 %collective-permute-start.6 = (bf16[64,768]{1,0:T(8,128)(2,1)S(1)}, bf16[64,768]{1,0:T(8,128)(2,1)S(1)}, u32[]{:S(2)}, u32[]{:S(2)}) collective-permute-start(bf16[64,768]{1,0:T(8,128)(2,1)S(1)} %get-tuple-element.34), channel_id=1, source_target_pairs={{0,4},{1,5},{2,6},{3,7},{4,0},{5,1},{6,2},{7,3},{8,12},{9,13},{10,... | collective-permute-start | bytes 294920 | tf_op jit(solution)/shard_map/ppermute | solution.py:77
  26.0 1.9 %shard_map.67.refs_1_ = f32[1024,768]{1,0:T(8,128)S(1)} custom-call(bf16[272,768]{1,0:T(8,128)(2,1)S(1)} %shard_map.66.refs_0_, bf16[1024,768]{1,0:T(8,128)(2,1)S(1)} %get-tuple-element.23.refs_5_.refs_1_, f32[1024,768]{1,0:T(8,128)S(1)} %get-tuple-element.31.refs_4_.refs_2_), custom_call_target="tpu_custom_call" | custom-call | flops 8053063680 | tf_op jit(solution)/shard_map/pallas_call | solution.py:96
  27.9 0.6 %shard_map.68.refs_3_.refs_2_ = f32[1024,768]{1,0:T(8,128)S(1)} custom-call(bf16[400,768]{1,0:T(8,128)(2,1)S(1)} %collective-permute-done.7.refs_0_, f32[1024,768]{1,0:T(8,128)S(1)} %shard_map.67.refs_1_), custom_call_target="tpu_custom_call" | custom-call | flops 402653184 | tf_op jit(solution)/shard_map/pallas_call | solution.py:96
  28.5 2.8 %collective-permute-done.6.refs_2_ = bf16[64,768]{1,0:T(8,128)(2,1)S(1)} collective-permute-done((bf16[64,768]{1,0:T(8,128)(2,1)S(1)}, bf16[64,768]{1,0:T(8,128)(2,1)S(1)}, u32[]{:S(2)}, u32[]{:S(2)}) %collective-permute-start.6) | collective-permute-done | bytes 98336 | tf_op jit(solution)/shard_map/ppermute | solution.py:77
  31.3 2.1 %collective-permute-start.10 = (bf16[32,768]{1,0:T(8,128)(2,1)S(1)}, bf16[32,768]{1,0:T(8,128)(2,1)S(1)}, u32[]{:S(2)}, u32[]{:S(2)}) collective-permute-start(bf16[32,768]{1,0:T(8,128)(2,1)S(1)} %get-tuple-element.39), channel_id=1, source_target_pairs={{0,1},{1,0},{2,3},{3,2},{4,5},{5,4},{6,7},{7,6},{8,9},{9,8},{10,11... | collective-permute-start | bytes 147464 | tf_op jit(solution)/shard_map/ppermute | solution.py:77
  33.4 2.7 %shard_map.70 = (bf16[1024,768]{1,0:T(8,128)(2,1)}, s32[1,128]{1,0:T(1,128)S(1)}) custom-call(bf16[272,768]{1,0:T(8,128)(2,1)S(1)} %collective-permute-done.11.refs_0_, bf16[1024,768]{1,0:T(8,128)(2,1)S(1)} %get-tuple-element.23.refs_5_.refs_1_, f32[1024,768]{1,0:T(8,128)S(1)} %shard_map.68.refs_3_.refs_2_), custom_call_target="tpu_custom_call" | custom-call | tf_op jit(solution)/shard_map/pallas_call | solution.py:269
  36.1 0.7 %shard_map.71 = f32[32,768]{1,0:T(8,128)} custom-call(f32[32,768]{1,0:T(8,128)S(1)} %get-tuple-element.38.refs_0_, bf16[32,768]{1,0:T(8,128)(2,1)S(1)} %collective-permute-done.10.refs_1_, s32[1,128]{1,0:T(1,128)S(1)} %get-tuple-element.40.refs_2_), custom_call_target="tpu_custom_call" | custom-call | tf_op jit(solution)/shard_map/pallas_call | solution.py:96
  (18 shorter events, 0.6 us)
Async XLA Ops:
  0.6 8.9 %collective-permute-start = (bf16[32,768]{1,0:T(8,128)(2,1)}, bf16[32,768]{1,0:T(8,128)(2,1)S(1)}, u32[]{:S(2)}, u32[]{:S(2)}) collective-permute-start(bf16[32,768]{1,0:T(8,128)(2,1)} %refs_0_.1), channel_id=1, source_target_pairs={{0,2},{1,3},{2,0},{3,1},{4,6},{5,7},{6,4},{7,5},{8,10},{9,11},{10,... | collective-permute-start | bytes 147464 | tf_op jit(solution)/shard_map/ppermute | solution.py:77
  3.7 6.1 %collective-permute-start.1 = (bf16[32,768]{1,0:T(8,128)(2,1)}, bf16[32,768]{1,0:T(8,128)(2,1)S(1)}, u32[]{:S(2)}, u32[]{:S(2)}) collective-permute-start(bf16[32,768]{1,0:T(8,128)(2,1)} %refs_0_.1), channel_id=1, source_target_pairs={{0,4},{1,5},{2,6},{3,7},{4,0},{5,1},{6,2},{7,3},{8,12},{9,13},{10,... | collective-permute-start | bytes 147464 | tf_op jit(solution)/shard_map/ppermute | solution.py:77
  6.3 6.1 %collective-permute-start.2 = (bf16[32,768]{1,0:T(8,128)(2,1)}, bf16[32,768]{1,0:T(8,128)(2,1)S(1)}, u32[]{:S(2)}, u32[]{:S(2)}) collective-permute-start(bf16[32,768]{1,0:T(8,128)(2,1)} %refs_0_.1), channel_id=1, source_target_pairs={{0,6},{1,7},{2,4},{3,5},{4,2},{5,3},{6,0},{7,1},{8,14},{9,15},{10,... | collective-permute-start | bytes 147464 | tf_op jit(solution)/shard_map/ppermute | solution.py:77
  7.0 1.4 %copy-start = (bf16[1024,768]{1,0:T(8,128)(2,1)S(1)}, bf16[1024,768]{1,0:T(8,128)(2,1)}, u32[]{:S(2)}) copy-start(bf16[1024,768]{1,0:T(8,128)(2,1)} %refs_1_.1) | copy-start | bytes 4718596
  8.4 0.8 %copy-start.1 = (bf16[32,768]{1,0:T(8,128)(2,1)S(1)}, bf16[32,768]{1,0:T(8,128)(2,1)}, u32[]{:S(2)}) copy-start(bf16[32,768]{1,0:T(8,128)(2,1)} %refs_0_.1) | copy-start | bytes 147460
  12.4 6.1 %collective-permute-start.3 = (bf16[128,768]{1,0:T(8,128)(2,1)S(1)}, bf16[128,768]{1,0:T(8,128)(2,1)S(1)}, u32[]{:S(2)}, u32[]{:S(2)}) collective-permute-start(bf16[128,768]{1,0:T(8,128)(2,1)S(1)} %get-tuple-element.24.refs_0_), channel_id=1, source_target_pairs={{0,1},{1,0},{2,3},{3,2},{4,5},{5,4},{6,7},{7,6},{8,9},{9,8},{10,11... | collective-permute-start | bytes 589832 | tf_op jit(solution)/shard_map/ppermute | solution.py:77
  14.0 11.8 %collective-permute-start.8 = (bf16[144,768]{1,0:T(8,128)(2,1)S(1)}, bf16[144,768]{1,0:T(8,128)(2,1)S(1)}, u32[]{:S(2)}, u32[]{:S(2)}) collective-permute-start(bf16[144,768]{1,0:T(8,128)(2,1)S(1)} %get-tuple-element.36), channel_id=1, source_target_pairs={{0,16},{8,24},{16,0},{24,8},{1,17},{9,25},{17,1},{25,9},{2,18},{10... | collective-permute-start | bytes 663560 | tf_op jit(solution)/shard_map/ppermute | solution.py:77
  16.9 9.0 %collective-permute-start.9 = (bf16[128,768]{1,0:T(8,128)(2,1)S(1)}, bf16[128,768]{1,0:T(8,128)(2,1)S(1)}, u32[]{:S(2)}, u32[]{:S(2)}) collective-permute-start(bf16[128,768]{1,0:T(8,128)(2,1)S(1)} %get-tuple-element.37), channel_id=1, source_target_pairs={{0,17},{1,16},{2,19},{3,18},{4,21},{5,20},{6,23},{7,22},{8,25},{9,... | collective-permute-start | bytes 589832 | tf_op jit(solution)/shard_map/ppermute | solution.py:87
  17.4 4.6 %collective-permute-start.5 = (bf16[64,768]{1,0:T(8,128)(2,1)S(1)}, bf16[64,768]{1,0:T(8,128)(2,1)S(1)}, u32[]{:S(2)}, u32[]{:S(2)}) collective-permute-start(bf16[64,768]{1,0:T(8,128)(2,1)S(1)} %get-tuple-element.29), channel_id=1, source_target_pairs={{0,2},{1,3},{2,0},{3,1},{4,6},{5,7},{6,4},{7,5},{8,10},{9,11},{10,... | collective-permute-start | bytes 294920 | tf_op jit(solution)/shard_map/ppermute | solution.py:77
  19.9 4.7 %collective-permute-start.4 = (bf16[64,768]{1,0:T(8,128)(2,1)S(1)}, bf16[64,768]{1,0:T(8,128)(2,1)S(1)}, u32[]{:S(2)}, u32[]{:S(2)}) collective-permute-start(bf16[64,768]{1,0:T(8,128)(2,1)S(1)} %get-tuple-element.27), channel_id=1, source_target_pairs={{0,2},{1,3},{2,0},{3,1},{4,6},{5,7},{6,4},{7,5},{8,10},{9,11},{10,... | collective-permute-start | bytes 294920 | tf_op jit(solution)/shard_map/ppermute | solution.py:77
  21.4 6.5 %collective-permute-start.7 = (bf16[400,768]{1,0:T(8,128)(2,1)S(1)}, bf16[400,768]{1,0:T(8,128)(2,1)S(1)}, u32[]{:S(2)}, u32[]{:S(2)}) collective-permute-start(bf16[400,768]{1,0:T(8,128)(2,1)S(1)} %get-tuple-element.35), channel_id=1, source_target_pairs={{0,8},{8,0},{16,24},{24,16},{1,9},{9,1},{17,25},{25,17},{2,10},{10... | collective-permute-start | bytes 1843208 | tf_op jit(solution)/shard_map/ppermute | solution.py:77
  24.6 6.6 %collective-permute-start.6 = (bf16[64,768]{1,0:T(8,128)(2,1)S(1)}, bf16[64,768]{1,0:T(8,128)(2,1)S(1)}, u32[]{:S(2)}, u32[]{:S(2)}) collective-permute-start(bf16[64,768]{1,0:T(8,128)(2,1)S(1)} %get-tuple-element.34), channel_id=1, source_target_pairs={{0,4},{1,5},{2,6},{3,7},{4,0},{5,1},{6,2},{7,3},{8,12},{9,13},{10,... | collective-permute-start | bytes 294920 | tf_op jit(solution)/shard_map/ppermute | solution.py:77
  25.9 7.5 %collective-permute-start.11 = (bf16[272,768]{1,0:T(8,128)(2,1)S(1)}, bf16[272,768]{1,0:T(8,128)(2,1)S(1)}, u32[]{:S(2)}, u32[]{:S(2)}) collective-permute-start(bf16[272,768]{1,0:T(8,128)(2,1)S(1)} %shard_map.66.refs_0_), channel_id=1, source_target_pairs={{0,8},{8,0},{16,24},{24,16},{1,9},{9,1},{17,25},{25,17},{2,10},{10... | collective-permute-start | bytes 1253384 | tf_op jit(solution)/shard_map/ppermute | solution.py:77
  31.3 4.8 %collective-permute-start.10 = (bf16[32,768]{1,0:T(8,128)(2,1)S(1)}, bf16[32,768]{1,0:T(8,128)(2,1)S(1)}, u32[]{:S(2)}, u32[]{:S(2)}) collective-permute-start(bf16[32,768]{1,0:T(8,128)(2,1)S(1)} %get-tuple-element.39), channel_id=1, source_target_pairs={{0,1},{1,0},{2,3},{3,2},{4,5},{5,4},{6,7},{7,6},{8,9},{9,8},{10,11... | collective-permute-start | bytes 147464 | tf_op jit(solution)/shard_map/ppermute | solution.py:77

commit v18 on v16

--- a/solution.py
+++ b/solution.py
@@ -360,10 +360,13 @@
         sum_body, [like(q_home, width, bf16)], [far_kept, far_came], 0, [acc]
     )[0]
     far_came = swap(far_sent, "lab", 1)
-    acc = local_call(mate_body, [grown], [mate, acc], work, [far_sent])[0]
+    near_most = local_call(
+        sum_body, [like(q_home, width, f32)], [near_kept, near_came], 0, [far_sent]
+    )[0]
+    acc = local_call(mate_body, [grown], [mate, acc], work, [near_most])[0]
     weight_grad, mark = late(groups, cross_mate, weights, acc)
     query_grad = local_call(
-        sum_body, [like(q_home, width, f32)], [near_kept, near_came, far_came], 0, [mark]
+        sum_body, [like(q_home, width, f32)], [near_most, far_came], 0, [mark]
     )[0]
     return (query_grad, weight_grad)
 

time: 35.6 us -> 38.8 us (1.090)
  waiting for transfers between devices: 5.15 us -> 9.23 us
  starting transfers between devices: 17 us -> 16.2 us
    ppermute x12, waiting for transfers between devices: 5.15 us -> 9.22 us  [swap(): return lax.ppermute(value, axis, [(i, i ^ bit) for i in range(count)])]
    ppermute x12, starting transfers between devices: 16.5 us -> 15.7 us  [swap(): return lax.ppermute(value, axis, [(i, i ^ bit) for i in range(count)])]
    pallas_call x13 -> x14, Pallas kernels: 6.76 us -> 6.76 us  [local_call(): pl.pallas_call(lambda *refs: body(*refs[:given], *refs[later:]), out_shap...]
  transfers between devices with their start and end apart: 13 -> 13, of which waited for: 4 -> 6; matrix products, arithmetic and copies ran while one was open for 2% -> 2% of each run, Pallas kernels for 25% -> 23%
where the time goes in v18:
time: 38.8 us; the launch traced here: 38.6 us
  starting transfers between devices  16.2 us (42%)
  Pallas kernels  9.48 us (24%)
  waiting for transfers between devices  9.23 us (24%)
  local copies, waits for them, and re-layouts  2.21 us (6%)
  between operations  0.74 us (2%)
  other arithmetic  0.72 us (2%)
    ppermute x12, starting transfers between devices, swap(): return lax.ppermute(value, axis, [(i, i ^ bit) for i in range(count)])  15.7 us
    ppermute x12, waiting for transfers between devices, swap(): return lax.ppermute(value, axis, [(i, i ^ bit) for i in range(count)])  9.22 us
    pallas_call x14, Pallas kernels, local_call(): pl.pallas_call(lambda *refs: body(*refs[:given], *refs[later:]), out_shap...  6.76 us
    pallas_call x1, Pallas kernels, late(): pl.pallas_call(lambda *refs: late_body(groups, *refs), out_shape=[out, li...  2.72 us
    unnamed x4, local copies, waits for them, and re-layouts  2.21 us
  transfers between devices with their start and end apart: 13, of which 6 were waited for; matrix products, arithmetic and copies ran while one was open for 2% of the time, Pallas kernels for 23%

profile of v18, /device:TPU:0, one launch (start us, length us, event | category | flops | bytes accessed | tf_op | source)
XLA Modules:
  0.0 38.6 jit_solution(5058796133749450907)
XLA Ops:
  0.6 3.1 %collective-permute-start = (bf16[32,768]{1,0:T(8,128)(2,1)}, bf16[32,768]{1,0:T(8,128)(2,1)S(1)}, u32[]{:S(2)}, u32[]{:S(2)}) collective-permute-start(bf16[32,768]{1,0:T(8,128)(2,1)} %refs_0_.1), channel_id=1, source_target_pairs={{0,2},{1,3},{2,0},{3,1},{4,6},{5,7},{6,4},{7,5},{8,10},{9,11},{10,... | collective-permute-start | bytes 147464 | tf_op jit(solution)/shard_map/ppermute | solution.py:77
  3.7 2.5 %collective-permute-start.2 = (bf16[32,768]{1,0:T(8,128)(2,1)}, bf16[32,768]{1,0:T(8,128)(2,1)S(1)}, u32[]{:S(2)}, u32[]{:S(2)}) collective-permute-start(bf16[32,768]{1,0:T(8,128)(2,1)} %refs_0_.1), channel_id=1, source_target_pairs={{0,6},{1,7},{2,4},{3,5},{4,2},{5,3},{6,0},{7,1},{8,14},{9,15},{10,... | collective-permute-start | bytes 147464 | tf_op jit(solution)/shard_map/ppermute | solution.py:77
  6.3 0.7 %add_convert_fusion.refs_1_ = f32[9,256]{1,0:T(8,128)S(1)} fusion(s32[1,256]{1,0:T(1,128)} %bitcast.4, s32[8,256]{1,0:T(8,128)} %bitcast.3), kind=kLoop, calls=%fused_computation | loop fusion | flops 4608 | bytes 18432 | tf_op jit(solution)/shard_map/convert_element_type | solution.py:312
  7.0 1.4 %copy-done = bf16[1024,768]{1,0:T(8,128)(2,1)S(1)} copy-done((bf16[1024,768]{1,0:T(8,128)(2,1)S(1)}, bf16[1024,768]{1,0:T(8,128)(2,1)}, u32[]{:S(2)}) %copy-start) | copy-done | bytes 1572888
  8.4 0.8 %copy-done.1 = bf16[32,768]{1,0:T(8,128)(2,1)S(1)} copy-done((bf16[32,768]{1,0:T(8,128)(2,1)S(1)}, bf16[32,768]{1,0:T(8,128)(2,1)}, u32[]{:S(2)}) %copy-start.1) | copy-done | bytes 49176
  9.5 0.9 %collective-permute-done.2.refs_3_ = bf16[32,768]{1,0:T(8,128)(2,1)S(1)} collective-permute-done((bf16[32,768]{1,0:T(8,128)(2,1)}, bf16[32,768]{1,0:T(8,128)(2,1)S(1)}, u32[]{:S(2)}, u32[]{:S(2)}) %collective-permute-start.2) | collective-permute-done | bytes 49184 | tf_op jit(solution)/shard_map/ppermute | solution.py:77
  10.4 1.5 %collective-permute-done.1.refs_2_ = bf16[32,768]{1,0:T(8,128)(2,1)S(1)} collective-permute-done((bf16[32,768]{1,0:T(8,128)(2,1)}, bf16[32,768]{1,0:T(8,128)(2,1)S(1)}, u32[]{:S(2)}, u32[]{:S(2)}) %collective-permute-start.1) | collective-permute-done | bytes 49184 | tf_op jit(solution)/shard_map/ppermute | solution.py:77
  12.0 1.6 %collective-permute-start.4 = (bf16[128,768]{1,0:T(8,128)(2,1)S(1)}, bf16[128,768]{1,0:T(8,128)(2,1)S(1)}, u32[]{:S(2)}, u32[]{:S(2)}) collective-permute-start(bf16[128,768]{1,0:T(8,128)(2,1)S(1)} %get-tuple-element.23.refs_0_), channel_id=1, source_target_pairs={{0,1},{1,0},{2,3},{3,2},{4,5},{5,4},{6,7},{7,6},{8,9},{9,8},{10,11... | collective-permute-start | bytes 589832 | tf_op jit(solution)/shard_map/ppermute | solution.py:77
  13.5 1.5 %collective-permute-start.8 = (bf16[144,768]{1,0:T(8,128)(2,1)S(1)}, bf16[144,768]{1,0:T(8,128)(2,1)S(1)}, u32[]{:S(2)}, u32[]{:S(2)}) collective-permute-start(bf16[144,768]{1,0:T(8,128)(2,1)S(1)} %get-tuple-element.35), channel_id=1, source_target_pairs={{0,16},{8,24},{16,0},{24,8},{1,17},{9,25},{17,1},{25,9},{2,18},{10... | collective-permute-start | bytes 663560 | tf_op jit(solution)/shard_map/ppermute | solution.py:77
  15.0 1.3 %shard_map.62 = (f32[64,768]{1,0:T(8,128)S(1)}, bf16[64,768]{1,0:T(8,128)(2,1)S(1)}, bf16[144,128]{1,0:T(8,128)(2,1)S(1)}, bf16[128,768]{1,0:T(8,128)(2,1)S(1)}) custom-call(bf16[128,768]{1,0:T(8,128)(2,1)S(1)} %get-tuple-element.23.refs_0_, bf16[1024,768]{1,0:T(8,128)(2,1)S(1)} %get-tuple-element.22.refs_5_.refs_1_, ...), custom_call_target="tpu_custom_call" | custom-call | flops 402653184 | tf_op jit(solution)/shard_map/pallas_call | solution.py:96
  16.4 0.5 %collective-permute-start.9 = (bf16[128,768]{1,0:T(8,128)(2,1)S(1)}, bf16[128,768]{1,0:T(8,128)(2,1)S(1)}, u32[]{:S(2)}, u32[]{:S(2)}) collective-permute-start(bf16[128,768]{1,0:T(8,128)(2,1)S(1)} %get-tuple-element.36), channel_id=1, source_target_pairs={{0,17},{1,16},{2,19},{3,18},{4,21},{5,20},{6,23},{7,22},{8,25},{9,... | collective-permute-start | bytes 589832 | tf_op jit(solution)/shard_map/ppermute | solution.py:87
  16.9 0.8 %collective-permute-done.4.refs_0_.refs_1_ = bf16[128,768]{1,0:T(8,128)(2,1)S(1)} collective-permute-done((bf16[128,768]{1,0:T(8,128)(2,1)S(1)}, bf16[128,768]{1,0:T(8,128)(2,1)S(1)}, u32[]{:S(2)}, u32[]{:S(2)}) %collective-permute-start.4) | collective-permute-done | bytes 196640 | tf_op jit(solution)/shard_map/ppermute | solution.py:77
  17.7 1.3 %shard_map.63 = (f32[64,768]{1,0:T(8,128)S(1)}, bf16[64,768]{1,0:T(8,128)(2,1)S(1)}, bf16[144,128]{1,0:T(8,128)(2,1)S(1)}) custom-call(bf16[128,768]{1,0:T(8,128)(2,1)S(1)} %collective-permute-done.4.refs_0_.refs_1_, bf16[1024,768]{1,0:T(8,128)(2,1)S(1)} %get-tuple-element.22.refs_5_.refs_1_, bf16[16,768]{1,0:T(8,128)(2,1)S(1)} %shard_map.60.refs_4_.refs_2_, ...), custom_call_target="tpu_custom_call" | custom-call | flops 402653184 | tf_op jit(solution)/shard_map/pallas_call | solution.py:96
  19.3 1.8 %collective-permute-start.3 = (bf16[64,768]{1,0:T(8,128)(2,1)S(1)}, bf16[64,768]{1,0:T(8,128)(2,1)S(1)}, u32[]{:S(2)}, u32[]{:S(2)}) collective-permute-start(bf16[64,768]{1,0:T(8,128)(2,1)S(1)} %get-tuple-element.25), channel_id=1, source_target_pairs={{0,2},{1,3},{2,0},{3,1},{4,6},{5,7},{6,4},{7,5},{8,10},{9,11},{10,... | collective-permute-start | bytes 294920 | tf_op jit(solution)/shard_map/ppermute | solution.py:77
  21.1 0.6 %shard_map.64 = (f32[1024,768]{1,0:T(8,128)S(1)}, bf16[400,768]{1,0:T(8,128)(2,1)S(1)}) custom-call(bf16[128,768]{1,0:T(8,128)(2,1)S(1)} %get-tuple-element.23.refs_0_, bf16[128,768]{1,0:T(8,128)(2,1)S(1)} %collective-permute-done.4.refs_0_.refs_1_, bf16[144,128]{1,0:T(8,128)(2,1)S(1)} %get-tuple-element.26.refs_3_.refs_2_, ...), custom_call_target="tpu_custom_call" | custom-call | flops 402653184 | tf_op jit(solution)/shard_map/pallas_call | solution.py:96
  21.8 1.9 %collective-permute-done.5.refs_1_ = bf16[64,768]{1,0:T(8,128)(2,1)S(1)} collective-permute-done((bf16[64,768]{1,0:T(8,128)(2,1)S(1)}, bf16[64,768]{1,0:T(8,128)(2,1)S(1)}, u32[]{:S(2)}, u32[]{:S(2)}) %collective-permute-start.5) | collective-permute-done | bytes 98336 | tf_op jit(solution)/shard_map/ppermute | solution.py:77
  23.7 1.0 %collective-permute-done.3.refs_1_ = bf16[64,768]{1,0:T(8,128)(2,1)S(1)} collective-permute-done((bf16[64,768]{1,0:T(8,128)(2,1)S(1)}, bf16[64,768]{1,0:T(8,128)(2,1)S(1)}, u32[]{:S(2)}, u32[]{:S(2)}) %collective-permute-start.3) | collective-permute-done | bytes 98336 | tf_op jit(solution)/shard_map/ppermute | solution.py:77
  24.8 2.6 %collective-permute-start.6 = (bf16[32,768]{1,0:T(8,128)(2,1)S(1)}, bf16[32,768]{1,0:T(8,128)(2,1)S(1)}, u32[]{:S(2)}, u32[]{:S(2)}) collective-permute-start(bf16[32,768]{1,0:T(8,128)(2,1)S(1)} %get-tuple-element.33), channel_id=1, source_target_pairs={{0,4},{1,5},{2,6},{3,7},{4,0},{5,1},{6,2},{7,3},{8,12},{9,13},{10,... | collective-permute-start | bytes 147464 | tf_op jit(solution)/shard_map/ppermute | solution.py:77
  27.9 1.9 %shard_map.68.refs_2_.refs_1_ = f32[1024,768]{1,0:T(8,128)S(1)} custom-call(bf16[272,768]{1,0:T(8,128)(2,1)S(1)} %shard_map.67.refs_0_, bf16[1024,768]{1,0:T(8,128)(2,1)S(1)} %get-tuple-element.22.refs_5_.refs_1_, f32[1024,768]{1,0:T(8,128)S(1)} %get-tuple-element.30.refs_2_, f32[32,768]{1,0:T(8,128)S(1)} %get-tuple-element.32.refs_3_.refs_0_), custom_call_target="tpu_custom_call" | custom-call | flops 8053063680 | tf_op jit(solution)/shard_map/pallas_call | solution.py:96
  29.8 3.1 %collective-permute-done.7.refs_1_ = bf16[32,768]{1,0:T(8,128)(2,1)S(1)} collective-permute-done((bf16[32,768]{1,0:T(8,128)(2,1)S(1)}, bf16[32,768]{1,0:T(8,128)(2,1)S(1)}, u32[]{:S(2)}, u32[]{:S(2)}) %collective-permute-start.7) | collective-permute-done | bytes 49184 | tf_op jit(solution)/shard_map/ppermute | solution.py:77
  32.9 1.7 %collective-permute-start.10 = (bf16[32,768]{1,0:T(8,128)(2,1)S(1)}, bf16[32,768]{1,0:T(8,128)(2,1)S(1)}, u32[]{:S(2)}, u32[]{:S(2)}) collective-permute-start(bf16[32,768]{1,0:T(8,128)(2,1)S(1)} %shard_map.69.refs_2_), channel_id=1, source_target_pairs={{0,1},{1,0},{2,3},{3,2},{4,5},{5,4},{6,7},{7,6},{8,9},{9,8},{10,11... | collective-permute-start | bytes 147464 | tf_op jit(solution)/shard_map/ppermute | solution.py:77
  34.6 0.6 %shard_map.71.refs_2_ = f32[1024,768]{1,0:T(8,128)S(1)} custom-call(bf16[400,768]{1,0:T(8,128)(2,1)S(1)} %collective-permute-done.12.refs_0_, f32[1024,768]{1,0:T(8,128)S(1)} %shard_map.68.refs_2_.refs_1_, f32[32,768]{1,0:T(8,128)S(1)} %shard_map.70.refs_2_.refs_0_), custom_call_target="tpu_custom_call" | custom-call | flops 402653184 | tf_op jit(solution)/shard_map/pallas_call | solution.py:96
  35.2 2.7 %shard_map.72 = (bf16[1024,768]{1,0:T(8,128)(2,1)}, s32[1,128]{1,0:T(1,128)S(1)}) custom-call(bf16[272,768]{1,0:T(8,128)(2,1)S(1)} %collective-permute-done.11.refs_0_, bf16[1024,768]{1,0:T(8,128)(2,1)S(1)} %get-tuple-element.22.refs_5_.refs_1_, f32[1024,768]{1,0:T(8,128)S(1)} %shard_map.71.refs_2_), custom_call_target="tpu_custom_call" | custom-call | tf_op jit(solution)/shard_map/pallas_call | solution.py:259
  37.9 0.7 %shard_map.73 = f32[32,768]{1,0:T(8,128)} custom-call(f32[32,768]{1,0:T(8,128)S(1)} %shard_map.70.refs_2_.refs_0_, bf16[32,768]{1,0:T(8,128)(2,1)S(1)} %collective-permute-done.10.refs_1_, s32[1,128]{1,0:T(1,128)S(1)} %get-tuple-element.38.refs_2_), custom_call_target="tpu_custom_call" | custom-call | tf_op jit(solution)/shard_map/pallas_call | solution.py:96
  (22 shorter events, 1.4 us)
Async XLA Ops:
  0.6 8.9 %collective-permute-start = (bf16[32,768]{1,0:T(8,128)(2,1)}, bf16[32,768]{1,0:T(8,128)(2,1)S(1)}, u32[]{:S(2)}, u32[]{:S(2)}) collective-permute-start(bf16[32,768]{1,0:T(8,128)(2,1)} %refs_0_.1), channel_id=1, source_target_pairs={{0,2},{1,3},{2,0},{3,1},{4,6},{5,7},{6,4},{7,5},{8,10},{9,11},{10,... | collective-permute-start | bytes 147464 | tf_op jit(solution)/shard_map/ppermute | solution.py:77
  3.7 6.7 %collective-permute-start.2 = (bf16[32,768]{1,0:T(8,128)(2,1)}, bf16[32,768]{1,0:T(8,128)(2,1)S(1)}, u32[]{:S(2)}, u32[]{:S(2)}) collective-permute-start(bf16[32,768]{1,0:T(8,128)(2,1)} %refs_0_.1), channel_id=1, source_target_pairs={{0,6},{1,7},{2,4},{3,5},{4,2},{5,3},{6,0},{7,1},{8,14},{9,15},{10,... | collective-permute-start | bytes 147464 | tf_op jit(solution)/shard_map/ppermute | solution.py:77
  6.2 5.7 %collective-permute-start.1 = (bf16[32,768]{1,0:T(8,128)(2,1)}, bf16[32,768]{1,0:T(8,128)(2,1)S(1)}, u32[]{:S(2)}, u32[]{:S(2)}) collective-permute-start(bf16[32,768]{1,0:T(8,128)(2,1)} %refs_0_.1), channel_id=1, source_target_pairs={{0,4},{1,5},{2,6},{3,7},{4,0},{5,1},{6,2},{7,3},{8,12},{9,13},{10,... | collective-permute-start | bytes 147464 | tf_op jit(solution)/shard_map/ppermute | solution.py:77
  7.0 1.4 %copy-start = (bf16[1024,768]{1,0:T(8,128)(2,1)S(1)}, bf16[1024,768]{1,0:T(8,128)(2,1)}, u32[]{:S(2)}) copy-start(bf16[1024,768]{1,0:T(8,128)(2,1)} %refs_1_.1) | copy-start | bytes 4718596
  8.4 0.8 %copy-start.1 = (bf16[32,768]{1,0:T(8,128)(2,1)S(1)}, bf16[32,768]{1,0:T(8,128)(2,1)}, u32[]{:S(2)}) copy-start(bf16[32,768]{1,0:T(8,128)(2,1)} %refs_0_.1) | copy-start | bytes 147460
  12.0 5.7 %collective-permute-start.4 = (bf16[128,768]{1,0:T(8,128)(2,1)S(1)}, bf16[128,768]{1,0:T(8,128)(2,1)S(1)}, u32[]{:S(2)}, u32[]{:S(2)}) collective-permute-start(bf16[128,768]{1,0:T(8,128)(2,1)S(1)} %get-tuple-element.23.refs_0_), channel_id=1, source_target_pairs={{0,1},{1,0},{2,3},{3,2},{4,5},{5,4},{6,7},{7,6},{8,9},{9,8},{10,11... | collective-permute-start | bytes 589832 | tf_op jit(solution)/shard_map/ppermute | solution.py:77
  13.5 14.2 %collective-permute-start.8 = (bf16[144,768]{1,0:T(8,128)(2,1)S(1)}, bf16[144,768]{1,0:T(8,128)(2,1)S(1)}, u32[]{:S(2)}, u32[]{:S(2)}) collective-permute-start(bf16[144,768]{1,0:T(8,128)(2,1)S(1)} %get-tuple-element.35), channel_id=1, source_target_pairs={{0,16},{8,24},{16,0},{24,8},{1,17},{9,25},{17,1},{25,9},{2,18},{10... | collective-permute-start | bytes 663560 | tf_op jit(solution)/shard_map/ppermute | solution.py:77
  16.4 11.4 %collective-permute-start.9 = (bf16[128,768]{1,0:T(8,128)(2,1)S(1)}, bf16[128,768]{1,0:T(8,128)(2,1)S(1)}, u32[]{:S(2)}, u32[]{:S(2)}) collective-permute-start(bf16[128,768]{1,0:T(8,128)(2,1)S(1)} %get-tuple-element.36), channel_id=1, source_target_pairs={{0,17},{1,16},{2,19},{3,18},{4,21},{5,20},{6,23},{7,22},{8,25},{9,... | collective-permute-start | bytes 589832 | tf_op jit(solution)/shard_map/ppermute | solution.py:87
  19.0 4.7 %collective-permute-start.5 = (bf16[64,768]{1,0:T(8,128)(2,1)S(1)}, bf16[64,768]{1,0:T(8,128)(2,1)S(1)}, u32[]{:S(2)}, u32[]{:S(2)}) collective-permute-start(bf16[64,768]{1,0:T(8,128)(2,1)S(1)} %get-tuple-element.28), channel_id=1, source_target_pairs={{0,2},{1,3},{2,0},{3,1},{4,6},{5,7},{6,4},{7,5},{8,10},{9,11},{10,... | collective-permute-start | bytes 294920 | tf_op jit(solution)/shard_map/ppermute | solution.py:77
  19.3 5.4 %collective-permute-start.3 = (bf16[64,768]{1,0:T(8,128)(2,1)S(1)}, bf16[64,768]{1,0:T(8,128)(2,1)S(1)}, u32[]{:S(2)}, u32[]{:S(2)}) collective-permute-start(bf16[64,768]{1,0:T(8,128)(2,1)S(1)} %get-tuple-element.25), channel_id=1, source_target_pairs={{0,2},{1,3},{2,0},{3,1},{4,6},{5,7},{6,4},{7,5},{8,10},{9,11},{10,... | collective-permute-start | bytes 294920 | tf_op jit(solution)/shard_map/ppermute | solution.py:77
  21.7 12.9 %collective-permute-start.12 = (bf16[400,768]{1,0:T(8,128)(2,1)S(1)}, bf16[400,768]{1,0:T(8,128)(2,1)S(1)}, u32[]{:S(2)}, u32[]{:S(2)}) collective-permute-start(bf16[400,768]{1,0:T(8,128)(2,1)S(1)} %get-tuple-element.37), channel_id=1, source_target_pairs={{0,8},{8,0},{16,24},{24,16},{1,9},{9,1},{17,25},{25,17},{2,10},{10... | collective-permute-start | bytes 1843208 | tf_op jit(solution)/shard_map/ppermute | solution.py:77
  24.8 9.8 %collective-permute-start.6 = (bf16[32,768]{1,0:T(8,128)(2,1)S(1)}, bf16[32,768]{1,0:T(8,128)(2,1)S(1)}, u32[]{:S(2)}, u32[]{:S(2)}) collective-permute-start(bf16[32,768]{1,0:T(8,128)(2,1)S(1)} %get-tuple-element.33), channel_id=1, source_target_pairs={{0,4},{1,5},{2,6},{3,7},{4,0},{5,1},{6,2},{7,3},{8,12},{9,13},{10,... | collective-permute-start | bytes 147464 | tf_op jit(solution)/shard_map/ppermute | solution.py:77
  27.4 5.5 %collective-permute-start.7 = (bf16[32,768]{1,0:T(8,128)(2,1)S(1)}, bf16[32,768]{1,0:T(8,128)(2,1)S(1)}, u32[]{:S(2)}, u32[]{:S(2)}) collective-permute-start(bf16[32,768]{1,0:T(8,128)(2,1)S(1)} %get-tuple-element.34), channel_id=1, source_target_pairs={{0,4},{1,5},{2,6},{3,7},{4,0},{5,1},{6,2},{7,3},{8,12},{9,13},{10,... | collective-permute-start | bytes 147464 | tf_op jit(solution)/shard_map/ppermute | solution.py:77
  27.8 7.4 %collective-permute-start.11 = (bf16[272,768]{1,0:T(8,128)(2,1)S(1)}, bf16[272,768]{1,0:T(8,128)(2,1)S(1)}, u32[]{:S(2)}, u32[]{:S(2)}) collective-permute-start(bf16[272,768]{1,0:T(8,128)(2,1)S(1)} %shard_map.67.refs_0_), channel_id=1, source_target_pairs={{0,8},{8,0},{16,24},{24,16},{1,9},{9,1},{17,25},{25,17},{2,10},{10... | collective-permute-start | bytes 1253384 | tf_op jit(solution)/shard_map/ppermute | solution.py:77
  32.9 5.1 %collective-permute-start.10 = (bf16[32,768]{1,0:T(8,128)(2,1)S(1)}, bf16[32,768]{1,0:T(8,128)(2,1)S(1)}, u32[]{:S(2)}, u32[]{:S(2)}) collective-permute-start(bf16[32,768]{1,0:T(8,128)(2,1)S(1)} %shard_map.69.refs_2_), channel_id=1, source_target_pairs={{0,1},{1,0},{2,3},{3,2},{4,5},{5,4},{6,7},{7,6},{8,9},{9,8},{10,11... | collective-permute-start | bytes 147464 | tf_op jit(solution)/shard_map/ppermute | solution.py:77

commit v19 on v16

--- a/solution.py
+++ b/solution.py
@@ -346,24 +346,29 @@
         work,
     )
     mate = swap(own, "pb", 1)
-    far_kept, far_sent = local_call(fold_body, single, [far_kept, far_came], 0, [acc])
+    near_kept, near_sent = local_call(fold_body, single, [near_kept, near_came], 0, [acc])
+    near_came = swap(near_sent, "lab", 4)
+    far_kept, far_sent = local_call(
+        fold_body, single, [far_kept, far_came], 0, [near_kept, acc]
+    )
     far_came = swap(far_sent, "lab", 4)
-    near_kept, near_sent = local_call(fold_body, single, [near_kept, near_came], 0, [far_kept])
-    near_came = swap(near_sent, "lab", 4)
+    near_most = local_call(
+        sum_body, [like(q_home, width, f32)], [near_kept, near_came], 0, [far_kept]
+    )[0]
     cross = local_call(
         stack_body, [like(qcount + NOTE, width, bf16)], [cross_near, cross_far], 0, [far_kept]
     )[0]
     cross_mate = swap(cross, "pb", 1)
     grown = like(lab_dev, width, f32)
-    acc = local_call(cross_body, [grown], [cross, weights, acc], 20 * work, [near_kept])[0]
+    acc = local_call(cross_body, [grown], [cross, weights, acc], 20 * work, [near_most])[0]
+    acc = local_call(mate_body, [grown], [mate, acc], work)[0]
     far_sent = local_call(
         sum_body, [like(q_home, width, bf16)], [far_kept, far_came], 0, [acc]
     )[0]
     far_came = swap(far_sent, "lab", 1)
-    acc = local_call(mate_body, [grown], [mate, acc], work, [far_sent])[0]
     weight_grad, mark = late(groups, cross_mate, weights, acc)
     query_grad = local_call(
-        sum_body, [like(q_home, width, f32)], [near_kept, near_came, far_came], 0, [mark]
+        sum_body, [like(q_home, width, f32)], [near_most, far_came], 0, [mark]
     )[0]
     return (query_grad, weight_grad)
 

time: 35.6 us -> 35.6 us (level)
    pallas_call x13 -> x14, Pallas kernels: 6.76 us -> 6.77 us  [local_call(): pl.pallas_call(lambda *refs: body(*refs[:given], *refs[later:]), out_shap...]
  transfers between devices with their start and end apart: 13 -> 13, of which waited for: 4 -> 6; matrix products, arithmetic and copies ran while one was open for 2% -> 2% of each run, Pallas kernels for 25% -> 25%
where the time goes in v19:
time: 35.6 us; the launch traced here: 35.4 us
  starting transfers between devices  17.1 us (48%)
  Pallas kernels  9.47 us (27%)
  waiting for transfers between devices  5.19 us (15%)
  local copies, waits for them, and re-layouts  2.21 us (6%)
  between operations  0.74 us (2%)
  other arithmetic  0.72 us (2%)
    ppermute x12, starting transfers between devices, swap(): return lax.ppermute(value, axis, [(i, i ^ bit) for i in range(count)])  16.5 us
    pallas_call x14, Pallas kernels, local_call(): pl.pallas_call(lambda *refs: body(*refs[:given], *refs[later:]), out_shap...  6.77 us
    ppermute x12, waiting for transfers between devices, swap(): return lax.ppermute(value, axis, [(i, i ^ bit) for i in range(count)])  5.18 us
    pallas_call x1, Pallas kernels, late(): pl.pallas_call(lambda *refs: late_body(groups, *refs), out_shape=[out, li...  2.7 us
    unnamed x4, local copies, waits for them, and re-layouts  2.21 us
    convert_element_type x1, other arithmetic, dense_shards(): jnp.concatenate([sibling_blocks.T, positive_slot[None]], axis=0).astype(f32)  0.72 us
  transfers between devices with their start and end apart: 13, of which 6 were waited for; matrix products, arithmetic and copies ran while one was open for 2% of the time, Pallas kernels for 25%

profile of v19, /device:TPU:0, one launch (start us, length us, event | category | flops | bytes accessed | tf_op | source)
XLA Modules:
  0.0 35.4 jit_solution(6231422456369398087)
XLA Ops:
  0.6 3.1 %collective-permute-start = (bf16[32,768]{1,0:T(8,128)(2,1)}, bf16[32,768]{1,0:T(8,128)(2,1)S(1)}, u32[]{:S(2)}, u32[]{:S(2)}) collective-permute-start(bf16[32,768]{1,0:T(8,128)(2,1)} %refs_0_.1), channel_id=1, source_target_pairs={{0,2},{1,3},{2,0},{3,1},{4,6},{5,7},{6,4},{7,5},{8,10},{9,11},{10,... | collective-permute-start | bytes 147464 | tf_op jit(solution)/shard_map/ppermute | solution.py:77
  3.7 2.5 %collective-permute-start.2 = (bf16[32,768]{1,0:T(8,128)(2,1)}, bf16[32,768]{1,0:T(8,128)(2,1)S(1)}, u32[]{:S(2)}, u32[]{:S(2)}) collective-permute-start(bf16[32,768]{1,0:T(8,128)(2,1)} %refs_0_.1), channel_id=1, source_target_pairs={{0,6},{1,7},{2,4},{3,5},{4,2},{5,3},{6,0},{7,1},{8,14},{9,15},{10,... | collective-permute-start | bytes 147464 | tf_op jit(solution)/shard_map/ppermute | solution.py:77
  6.3 0.7 %add_convert_fusion.refs_1_ = f32[9,256]{1,0:T(8,128)S(1)} fusion(s32[1,256]{1,0:T(1,128)} %bitcast.4, s32[8,256]{1,0:T(8,128)} %bitcast.3), kind=kLoop, calls=%fused_computation | loop fusion | flops 4608 | bytes 18432 | tf_op jit(solution)/shard_map/convert_element_type | solution.py:312
  7.0 1.4 %copy-done = bf16[1024,768]{1,0:T(8,128)(2,1)S(1)} copy-done((bf16[1024,768]{1,0:T(8,128)(2,1)S(1)}, bf16[1024,768]{1,0:T(8,128)(2,1)}, u32[]{:S(2)}) %copy-start) | copy-done | bytes 1572888
  8.4 0.8 %copy-done.1 = bf16[32,768]{1,0:T(8,128)(2,1)S(1)} copy-done((bf16[32,768]{1,0:T(8,128)(2,1)S(1)}, bf16[32,768]{1,0:T(8,128)(2,1)}, u32[]{:S(2)}) %copy-start.1) | copy-done | bytes 49176
  9.5 0.9 %collective-permute-done.2.refs_3_ = bf16[32,768]{1,0:T(8,128)(2,1)S(1)} collective-permute-done((bf16[32,768]{1,0:T(8,128)(2,1)}, bf16[32,768]{1,0:T(8,128)(2,1)S(1)}, u32[]{:S(2)}, u32[]{:S(2)}) %collective-permute-start.2) | collective-permute-done | bytes 49184 | tf_op jit(solution)/shard_map/ppermute | solution.py:77
  10.4 1.5 %collective-permute-done.1.refs_2_ = bf16[32,768]{1,0:T(8,128)(2,1)S(1)} collective-permute-done((bf16[32,768]{1,0:T(8,128)(2,1)}, bf16[32,768]{1,0:T(8,128)(2,1)S(1)}, u32[]{:S(2)}, u32[]{:S(2)}) %collective-permute-start.1) | collective-permute-done | bytes 49184 | tf_op jit(solution)/shard_map/ppermute | solution.py:77
  12.0 1.6 %collective-permute-start.4 = (bf16[128,768]{1,0:T(8,128)(2,1)S(1)}, bf16[128,768]{1,0:T(8,128)(2,1)S(1)}, u32[]{:S(2)}, u32[]{:S(2)}) collective-permute-start(bf16[128,768]{1,0:T(8,128)(2,1)S(1)} %get-tuple-element.23.refs_0_), channel_id=1, source_target_pairs={{0,1},{1,0},{2,3},{3,2},{4,5},{5,4},{6,7},{7,6},{8,9},{9,8},{10,11... | collective-permute-start | bytes 589832 | tf_op jit(solution)/shard_map/ppermute | solution.py:77
  13.5 1.5 %collective-permute-start.9 = (bf16[144,768]{1,0:T(8,128)(2,1)S(1)}, bf16[144,768]{1,0:T(8,128)(2,1)S(1)}, u32[]{:S(2)}, u32[]{:S(2)}) collective-permute-start(bf16[144,768]{1,0:T(8,128)(2,1)S(1)} %get-tuple-element.36), channel_id=1, source_target_pairs={{0,16},{8,24},{16,0},{24,8},{1,17},{9,25},{17,1},{25,9},{2,18},{10... | collective-permute-start | bytes 663560 | tf_op jit(solution)/shard_map/ppermute | solution.py:77
  15.0 1.3 %shard_map.62 = (f32[64,768]{1,0:T(8,128)S(1)}, bf16[64,768]{1,0:T(8,128)(2,1)S(1)}, bf16[144,128]{1,0:T(8,128)(2,1)S(1)}, bf16[128,768]{1,0:T(8,128)(2,1)S(1)}) custom-call(bf16[128,768]{1,0:T(8,128)(2,1)S(1)} %get-tuple-element.23.refs_0_, bf16[1024,768]{1,0:T(8,128)(2,1)S(1)} %get-tuple-element.22.refs_5_.refs_1_, ...), custom_call_target="tpu_custom_call" | custom-call | flops 402653184 | tf_op jit(solution)/shard_map/pallas_call | solution.py:96
  16.4 0.5 %collective-permute-start.10 = (bf16[128,768]{1,0:T(8,128)(2,1)S(1)}, bf16[128,768]{1,0:T(8,128)(2,1)S(1)}, u32[]{:S(2)}, u32[]{:S(2)}) collective-permute-start(bf16[128,768]{1,0:T(8,128)(2,1)S(1)} %get-tuple-element.37), channel_id=1, source_target_pairs={{0,17},{1,16},{2,19},{3,18},{4,21},{5,20},{6,23},{7,22},{8,25},{9,... | collective-permute-start | bytes 589832 | tf_op jit(solution)/shard_map/ppermute | solution.py:87
  17.7 1.3 %shard_map.63 = (f32[64,768]{1,0:T(8,128)S(1)}, bf16[64,768]{1,0:T(8,128)(2,1)S(1)}, bf16[144,128]{1,0:T(8,128)(2,1)S(1)}) custom-call(bf16[128,768]{1,0:T(8,128)(2,1)S(1)} %collective-permute-done.4.refs_0_.refs_1_, bf16[1024,768]{1,0:T(8,128)(2,1)S(1)} %get-tuple-element.22.refs_5_.refs_1_, bf16[16,768]{1,0:T(8,128)(2,1)S(1)} %shard_map.60.refs_4_.refs_2_, ...), custom_call_target="tpu_custom_call" | custom-call | flops 402653184 | tf_op jit(solution)/shard_map/pallas_call | solution.py:96
  19.0 1.3 %collective-permute-start.6 = (bf16[64,768]{1,0:T(8,128)(2,1)S(1)}, bf16[64,768]{1,0:T(8,128)(2,1)S(1)}, u32[]{:S(2)}, u32[]{:S(2)}) collective-permute-start(bf16[64,768]{1,0:T(8,128)(2,1)S(1)} %get-tuple-element.32), channel_id=1, source_target_pairs={{0,2},{1,3},{2,0},{3,1},{4,6},{5,7},{6,4},{7,5},{8,10},{9,11},{10,... | collective-permute-start | bytes 294920 | tf_op jit(solution)/shard_map/ppermute | solution.py:77
  20.3 0.6 %shard_map.64 = (f32[1024,768]{1,0:T(8,128)S(1)}, bf16[400,768]{1,0:T(8,128)(2,1)S(1)}) custom-call(bf16[128,768]{1,0:T(8,128)(2,1)S(1)} %get-tuple-element.23.refs_0_, bf16[128,768]{1,0:T(8,128)(2,1)S(1)} %collective-permute-done.4.refs_0_.refs_1_, bf16[144,128]{1,0:T(8,128)(2,1)S(1)} %get-tuple-element.26.refs_3_.refs_2_, ...), custom_call_target="tpu_custom_call" | custom-call | flops 402653184 | tf_op jit(solution)/shard_map/pallas_call | solution.py:96
  20.9 0.6 %collective-permute-done.3.refs_1_ = bf16[64,768]{1,0:T(8,128)(2,1)S(1)} collective-permute-done((bf16[64,768]{1,0:T(8,128)(2,1)S(1)}, bf16[64,768]{1,0:T(8,128)(2,1)S(1)}, u32[]{:S(2)}, u32[]{:S(2)}) %collective-permute-start.3) | collective-permute-done | bytes 98336 | tf_op jit(solution)/shard_map/ppermute | solution.py:77
  21.6 1.3 %collective-permute-start.5 = (bf16[32,768]{1,0:T(8,128)(2,1)S(1)}, bf16[32,768]{1,0:T(8,128)(2,1)S(1)}, u32[]{:S(2)}, u32[]{:S(2)}) collective-permute-start(bf16[32,768]{1,0:T(8,128)(2,1)S(1)} %get-tuple-element.30), channel_id=1, source_target_pairs={{0,4},{1,5},{2,6},{3,7},{4,0},{5,1},{6,2},{7,3},{8,12},{9,13},{10,... | collective-permute-start | bytes 147464 | tf_op jit(solution)/shard_map/ppermute | solution.py:77
  22.9 0.8 %collective-permute-done.6.refs_1_ = bf16[64,768]{1,0:T(8,128)(2,1)S(1)} collective-permute-done((bf16[64,768]{1,0:T(8,128)(2,1)S(1)}, bf16[64,768]{1,0:T(8,128)(2,1)S(1)}, u32[]{:S(2)}, u32[]{:S(2)}) %collective-permute-start.6) | collective-permute-done | bytes 98336 | tf_op jit(solution)/shard_map/ppermute | solution.py:77
  23.7 2.0 %collective-permute-start.7 = (bf16[32,768]{1,0:T(8,128)(2,1)S(1)}, bf16[32,768]{1,0:T(8,128)(2,1)S(1)}, u32[]{:S(2)}, u32[]{:S(2)}) collective-permute-start(bf16[32,768]{1,0:T(8,128)(2,1)S(1)} %get-tuple-element.34), channel_id=1, source_target_pairs={{0,4},{1,5},{2,6},{3,7},{4,0},{5,1},{6,2},{7,3},{8,12},{9,13},{10,... | collective-permute-start | bytes 147464 | tf_op jit(solution)/shard_map/ppermute | solution.py:77
  25.8 0.8 %collective-permute-done.5.refs_1_ = bf16[32,768]{1,0:T(8,128)(2,1)S(1)} collective-permute-done((bf16[32,768]{1,0:T(8,128)(2,1)S(1)}, bf16[32,768]{1,0:T(8,128)(2,1)S(1)}, u32[]{:S(2)}, u32[]{:S(2)}) %collective-permute-start.5) | collective-permute-done | bytes 49184 | tf_op jit(solution)/shard_map/ppermute | solution.py:77
  26.6 1.9 %shard_map.69.refs_1_ = f32[1024,768]{1,0:T(8,128)S(1)} custom-call(bf16[272,768]{1,0:T(8,128)(2,1)S(1)} %shard_map.68.refs_0_, bf16[1024,768]{1,0:T(8,128)(2,1)S(1)} %get-tuple-element.22.refs_5_.refs_1_, f32[1024,768]{1,0:T(8,128)S(1)} %get-tuple-element.28.refs_2_.refs_3_, f32[32,768]{1,0:T(8,128)S(1)} %shard_map.67.refs_3_.refs_0_), custom_call_target="tpu_custom_call" | custom-call | flops 8053063680 | tf_op jit(solution)/shard_map/pallas_call | solution.py:96
  28.6 0.6 %shard_map.70.refs_2_ = f32[1024,768]{1,0:T(8,128)S(1)} custom-call(bf16[400,768]{1,0:T(8,128)(2,1)S(1)} %collective-permute-done.8.refs_0_, f32[1024,768]{1,0:T(8,128)S(1)} %shard_map.69.refs_1_), custom_call_target="tpu_custom_call" | custom-call | flops 402653184 | tf_op jit(solution)/shard_map/pallas_call | solution.py:96
  29.2 2.8 %collective-permute-start.11 = (bf16[32,768]{1,0:T(8,128)(2,1)S(1)}, bf16[32,768]{1,0:T(8,128)(2,1)S(1)}, u32[]{:S(2)}, u32[]{:S(2)}) collective-permute-start(bf16[32,768]{1,0:T(8,128)(2,1)S(1)} %shard_map.71), channel_id=1, source_target_pairs={{0,1},{1,0},{2,3},{3,2},{4,5},{5,4},{6,7},{7,6},{8,9},{9,8},{10,11... | collective-permute-start | bytes 147464 | tf_op jit(solution)/shard_map/ppermute | solution.py:77
  32.0 2.7 %shard_map.72 = (bf16[1024,768]{1,0:T(8,128)(2,1)}, s32[1,128]{1,0:T(1,128)S(1)}) custom-call(bf16[272,768]{1,0:T(8,128)(2,1)S(1)} %collective-permute-done.12.refs_0_, bf16[1024,768]{1,0:T(8,128)(2,1)S(1)} %get-tuple-element.22.refs_5_.refs_1_, f32[1024,768]{1,0:T(8,128)S(1)} %shard_map.70.refs_2_), custom_call_target="tpu_custom_call" | custom-call | tf_op jit(solution)/shard_map/pallas_call | solution.py:259
  34.7 0.7 %shard_map.73 = f32[32,768]{1,0:T(8,128)} custom-call(f32[32,768]{1,0:T(8,128)S(1)} %shard_map.67.refs_3_.refs_0_, bf16[32,768]{1,0:T(8,128)(2,1)S(1)} %collective-permute-done.11.refs_1_, s32[1,128]{1,0:T(1,128)S(1)} %get-tuple-element.38.refs_2_), custom_call_target="tpu_custom_call" | custom-call | tf_op jit(solution)/shard_map/pallas_call | solution.py:96
  (22 shorter events, 1.4 us)
Async XLA Ops:
  0.6 8.9 %collective-permute-start = (bf16[32,768]{1,0:T(8,128)(2,1)}, bf16[32,768]{1,0:T(8,128)(2,1)S(1)}, u32[]{:S(2)}, u32[]{:S(2)}) collective-permute-start(bf16[32,768]{1,0:T(8,128)(2,1)} %refs_0_.1), channel_id=1, source_target_pairs={{0,2},{1,3},{2,0},{3,1},{4,6},{5,7},{6,4},{7,5},{8,10},{9,11},{10,... | collective-permute-start | bytes 147464 | tf_op jit(solution)/shard_map/ppermute | solution.py:77
  3.7 6.7 %collective-permute-start.2 = (bf16[32,768]{1,0:T(8,128)(2,1)}, bf16[32,768]{1,0:T(8,128)(2,1)S(1)}, u32[]{:S(2)}, u32[]{:S(2)}) collective-permute-start(bf16[32,768]{1,0:T(8,128)(2,1)} %refs_0_.1), channel_id=1, source_target_pairs={{0,6},{1,7},{2,4},{3,5},{4,2},{5,3},{6,0},{7,1},{8,14},{9,15},{10,... | collective-permute-start | bytes 147464 | tf_op jit(solution)/shard_map/ppermute | solution.py:77
  6.2 5.7 %collective-permute-start.1 = (bf16[32,768]{1,0:T(8,128)(2,1)}, bf16[32,768]{1,0:T(8,128)(2,1)S(1)}, u32[]{:S(2)}, u32[]{:S(2)}) collective-permute-start(bf16[32,768]{1,0:T(8,128)(2,1)} %refs_0_.1), channel_id=1, source_target_pairs={{0,4},{1,5},{2,6},{3,7},{4,0},{5,1},{6,2},{7,3},{8,12},{9,13},{10,... | collective-permute-start | bytes 147464 | tf_op jit(solution)/shard_map/ppermute | solution.py:77
  7.0 1.4 %copy-start = (bf16[1024,768]{1,0:T(8,128)(2,1)S(1)}, bf16[1024,768]{1,0:T(8,128)(2,1)}, u32[]{:S(2)}) copy-start(bf16[1024,768]{1,0:T(8,128)(2,1)} %refs_1_.1) | copy-start | bytes 4718596
  8.4 0.8 %copy-start.1 = (bf16[32,768]{1,0:T(8,128)(2,1)S(1)}, bf16[32,768]{1,0:T(8,128)(2,1)}, u32[]{:S(2)}) copy-start(bf16[32,768]{1,0:T(8,128)(2,1)} %refs_0_.1) | copy-start | bytes 147460
  12.0 5.7 %collective-permute-start.4 = (bf16[128,768]{1,0:T(8,128)(2,1)S(1)}, bf16[128,768]{1,0:T(8,128)(2,1)S(1)}, u32[]{:S(2)}, u32[]{:S(2)}) collective-permute-start(bf16[128,768]{1,0:T(8,128)(2,1)S(1)} %get-tuple-element.23.refs_0_), channel_id=1, source_target_pairs={{0,1},{1,0},{2,3},{3,2},{4,5},{5,4},{6,7},{7,6},{8,9},{9,8},{10,11... | collective-permute-start | bytes 589832 | tf_op jit(solution)/shard_map/ppermute | solution.py:77
  13.5 12.2 %collective-permute-start.9 = (bf16[144,768]{1,0:T(8,128)(2,1)S(1)}, bf16[144,768]{1,0:T(8,128)(2,1)S(1)}, u32[]{:S(2)}, u32[]{:S(2)}) collective-permute-start(bf16[144,768]{1,0:T(8,128)(2,1)S(1)} %get-tuple-element.36), channel_id=1, source_target_pairs={{0,16},{8,24},{16,0},{24,8},{1,17},{9,25},{17,1},{25,9},{2,18},{10... | collective-permute-start | bytes 663560 | tf_op jit(solution)/shard_map/ppermute | solution.py:77
  16.4 9.3 %collective-permute-start.10 = (bf16[128,768]{1,0:T(8,128)(2,1)S(1)}, bf16[128,768]{1,0:T(8,128)(2,1)S(1)}, u32[]{:S(2)}, u32[]{:S(2)}) collective-permute-start(bf16[128,768]{1,0:T(8,128)(2,1)S(1)} %get-tuple-element.37), channel_id=1, source_target_pairs={{0,17},{1,16},{2,19},{3,18},{4,21},{5,20},{6,23},{7,22},{8,25},{9,... | collective-permute-start | bytes 589832 | tf_op jit(solution)/shard_map/ppermute | solution.py:87
  16.9 4.6 %collective-permute-start.3 = (bf16[64,768]{1,0:T(8,128)(2,1)S(1)}, bf16[64,768]{1,0:T(8,128)(2,1)S(1)}, u32[]{:S(2)}, u32[]{:S(2)}) collective-permute-start(bf16[64,768]{1,0:T(8,128)(2,1)S(1)} %get-tuple-element.25), channel_id=1, source_target_pairs={{0,2},{1,3},{2,0},{3,1},{4,6},{5,7},{6,4},{7,5},{8,10},{9,11},{10,... | collective-permute-start | bytes 294920 | tf_op jit(solution)/shard_map/ppermute | solution.py:77
  19.0 4.7 %collective-permute-start.6 = (bf16[64,768]{1,0:T(8,128)(2,1)S(1)}, bf16[64,768]{1,0:T(8,128)(2,1)S(1)}, u32[]{:S(2)}, u32[]{:S(2)}) collective-permute-start(bf16[64,768]{1,0:T(8,128)(2,1)S(1)} %get-tuple-element.32), channel_id=1, source_target_pairs={{0,2},{1,3},{2,0},{3,1},{4,6},{5,7},{6,4},{7,5},{8,10},{9,11},{10,... | collective-permute-start | bytes 294920 | tf_op jit(solution)/shard_map/ppermute | solution.py:77
  21.6 5.1 %collective-permute-start.5 = (bf16[32,768]{1,0:T(8,128)(2,1)S(1)}, bf16[32,768]{1,0:T(8,128)(2,1)S(1)}, u32[]{:S(2)}, u32[]{:S(2)}) collective-permute-start(bf16[32,768]{1,0:T(8,128)(2,1)S(1)} %get-tuple-element.30), channel_id=1, source_target_pairs={{0,4},{1,5},{2,6},{3,7},{4,0},{5,1},{6,2},{7,3},{8,12},{9,13},{10,... | collective-permute-start | bytes 147464 | tf_op jit(solution)/shard_map/ppermute | solution.py:77
  22.9 5.7 %collective-permute-start.8 = (bf16[400,768]{1,0:T(8,128)(2,1)S(1)}, bf16[400,768]{1,0:T(8,128)(2,1)S(1)}, u32[]{:S(2)}, u32[]{:S(2)}) collective-permute-start(bf16[400,768]{1,0:T(8,128)(2,1)S(1)} %get-tuple-element.35), channel_id=1, source_target_pairs={{0,8},{8,0},{16,24},{24,16},{1,9},{9,1},{17,25},{25,17},{2,10},{10... | collective-permute-start | bytes 1843208 | tf_op jit(solution)/shard_map/ppermute | solution.py:77
  23.7 5.4 %collective-permute-start.7 = (bf16[32,768]{1,0:T(8,128)(2,1)S(1)}, bf16[32,768]{1,0:T(8,128)(2,1)S(1)}, u32[]{:S(2)}, u32[]{:S(2)}) collective-permute-start(bf16[32,768]{1,0:T(8,128)(2,1)S(1)} %get-tuple-element.34), channel_id=1, source_target_pairs={{0,4},{1,5},{2,6},{3,7},{4,0},{5,1},{6,2},{7,3},{8,12},{9,13},{10,... | collective-permute-start | bytes 147464 | tf_op jit(solution)/shard_map/ppermute | solution.py:77
  25.7 6.3 %collective-permute-start.12 = (bf16[272,768]{1,0:T(8,128)(2,1)S(1)}, bf16[272,768]{1,0:T(8,128)(2,1)S(1)}, u32[]{:S(2)}, u32[]{:S(2)}) collective-permute-start(bf16[272,768]{1,0:T(8,128)(2,1)S(1)} %shard_map.68.refs_0_), channel_id=1, source_target_pairs={{0,8},{8,0},{16,24},{24,16},{1,9},{9,1},{17,25},{25,17},{2,10},{10... | collective-permute-start | bytes 1253384 | tf_op jit(solution)/shard_map/ppermute | solution.py:77
  29.2 5.5 %collective-permute-start.11 = (bf16[32,768]{1,0:T(8,128)(2,1)S(1)}, bf16[32,768]{1,0:T(8,128)(2,1)S(1)}, u32[]{:S(2)}, u32[]{:S(2)}) collective-permute-start(bf16[32,768]{1,0:T(8,128)(2,1)S(1)} %shard_map.71), channel_id=1, source_target_pairs={{0,1},{1,0},{2,3},{3,2},{4,5},{5,4},{6,7},{7,6},{8,9},{9,8},{10,11... | collective-permute-start | bytes 147464 | tf_op jit(solution)/shard_map/ppermute | solution.py:77

commit v20 on v19

--- a/solution.py
+++ b/solution.py
@@ -108,7 +108,8 @@
 
 
 def join_body(*refs):
-    *came_refs, note_ref, out_ref, noted_ref = refs
+    own_ref, first_ref, *rest, note_ref, out_ref, noted_ref = refs
+    came_refs = [own_ref, first_ref, *rest[::-1]]
     stack_body(*came_refs, out_ref)
     stack_body(*came_refs, note_ref, noted_ref)
 
@@ -318,7 +319,7 @@
     near, noted = local_call(
         join_body,
         [like(half, width, bf16), like(half + NOTE, width, bf16)],
-        [held, *came, note],
+        [held, came[0], *came[:0:-1], note],
         0,
         [weights],
     )
@@ -360,8 +361,8 @@
     )[0]
     cross_mate = swap(cross, "pb", 1)
     grown = like(lab_dev, width, f32)
-    acc = local_call(cross_body, [grown], [cross, weights, acc], 20 * work, [near_most])[0]
-    acc = local_call(mate_body, [grown], [mate, acc], work)[0]
+    acc = local_call(cross_body, [grown], [cross, weights, acc], 20 * work, [far_kept])[0]
+    acc = local_call(mate_body, [grown], [mate, acc], work, [near_most])[0]
     far_sent = local_call(
         sum_body, [like(q_home, width, bf16)], [far_kept, far_came], 0, [acc]
     )[0]

time: 35.6 us -> 35.6 us (level)
  waiting for transfers between devices: 5.19 us -> 4.82 us
    ppermute x12, starting transfers between devices: 16.5 us -> 16.9 us  [swap(): return lax.ppermute(value, axis, [(i, i ^ bit) for i in range(count)])]
    ppermute x12, waiting for transfers between devices: 5.18 us -> 4.82 us  [swap(): return lax.ppermute(value, axis, [(i, i ^ bit) for i in range(count)])]
where the time goes in v20:
time: 35.6 us; the launch traced here: 35.4 us
  starting transfers between devices  17.4 us (49%)
  Pallas kernels  9.47 us (27%)
  waiting for transfers between devices  4.82 us (14%)
  local copies, waits for them, and re-layouts  2.21 us (6%)
  between operations  0.74 us (2%)
  other arithmetic  0.72 us (2%)
    ppermute x12, starting transfers between devices, swap(): return lax.ppermute(value, axis, [(i, i ^ bit) for i in range(count)])  16.9 us
    pallas_call x14, Pallas kernels, local_call(): pl.pallas_call(lambda *refs: body(*refs[:given], *refs[later:]), out_shap...  6.77 us
    ppermute x12, waiting for transfers between devices, swap(): return lax.ppermute(value, axis, [(i, i ^ bit) for i in range(count)])  4.82 us
    pallas_call x1, Pallas kernels, late(): pl.pallas_call(lambda *refs: late_body(groups, *refs), out_shape=[out, li...  2.7 us
    unnamed x4, local copies, waits for them, and re-layouts  2.21 us
    convert_element_type x1, other arithmetic, dense_shards(): jnp.concatenate([sibling_blocks.T, positive_slot[None]], axis=0).astype(f32)  0.72 us
  transfers between devices with their start and end apart: 13, of which 6 were waited for; matrix products, arithmetic and copies ran while one was open for 2% of the time, Pallas kernels for 25%

profile of v20, /device:TPU:0, one launch (start us, length us, event | category | flops | bytes accessed | tf_op | source)
XLA Modules:
  0.0 35.4 jit_solution(16472897517197589155)
XLA Ops:
  0.6 3.1 %collective-permute-start = (bf16[32,768]{1,0:T(8,128)(2,1)}, bf16[32,768]{1,0:T(8,128)(2,1)S(1)}, u32[]{:S(2)}, u32[]{:S(2)}) collective-permute-start(bf16[32,768]{1,0:T(8,128)(2,1)} %refs_0_.1), channel_id=1, source_target_pairs={{0,2},{1,3},{2,0},{3,1},{4,6},{5,7},{6,4},{7,5},{8,10},{9,11},{10,... | collective-permute-start | bytes 147464 | tf_op jit(solution)/shard_map/ppermute | solution.py:77
  3.7 2.5 %collective-permute-start.1 = (bf16[32,768]{1,0:T(8,128)(2,1)}, bf16[32,768]{1,0:T(8,128)(2,1)S(1)}, u32[]{:S(2)}, u32[]{:S(2)}) collective-permute-start(bf16[32,768]{1,0:T(8,128)(2,1)} %refs_0_.1), channel_id=1, source_target_pairs={{0,6},{1,7},{2,4},{3,5},{4,2},{5,3},{6,0},{7,1},{8,14},{9,15},{10,... | collective-permute-start | bytes 147464 | tf_op jit(solution)/shard_map/ppermute | solution.py:77
  6.3 0.7 %add_convert_fusion.refs_1_ = f32[9,256]{1,0:T(8,128)S(1)} fusion(s32[1,256]{1,0:T(1,128)} %bitcast.4, s32[8,256]{1,0:T(8,128)} %bitcast.3), kind=kLoop, calls=%fused_computation | loop fusion | flops 4608 | bytes 18432 | tf_op jit(solution)/shard_map/convert_element_type | solution.py:313
  7.0 1.4 %copy-done = bf16[1024,768]{1,0:T(8,128)(2,1)S(1)} copy-done((bf16[1024,768]{1,0:T(8,128)(2,1)S(1)}, bf16[1024,768]{1,0:T(8,128)(2,1)}, u32[]{:S(2)}) %copy-start) | copy-done | bytes 1572888
  8.4 0.8 %copy-done.1 = bf16[32,768]{1,0:T(8,128)(2,1)S(1)} copy-done((bf16[32,768]{1,0:T(8,128)(2,1)S(1)}, bf16[32,768]{1,0:T(8,128)(2,1)}, u32[]{:S(2)}) %copy-start.1) | copy-done | bytes 49176
  9.5 0.9 %collective-permute-done.1.refs_2_ = bf16[32,768]{1,0:T(8,128)(2,1)S(1)} collective-permute-done((bf16[32,768]{1,0:T(8,128)(2,1)}, bf16[32,768]{1,0:T(8,128)(2,1)S(1)}, u32[]{:S(2)}, u32[]{:S(2)}) %collective-permute-start.1) | collective-permute-done | bytes 49184 | tf_op jit(solution)/shard_map/ppermute | solution.py:77
  10.4 1.5 %collective-permute-done.2.refs_3_ = bf16[32,768]{1,0:T(8,128)(2,1)S(1)} collective-permute-done((bf16[32,768]{1,0:T(8,128)(2,1)}, bf16[32,768]{1,0:T(8,128)(2,1)S(1)}, u32[]{:S(2)}, u32[]{:S(2)}) %collective-permute-start.2) | collective-permute-done | bytes 49184 | tf_op jit(solution)/shard_map/ppermute | solution.py:77
  12.0 1.6 %collective-permute-start.4 = (bf16[128,768]{1,0:T(8,128)(2,1)S(1)}, bf16[128,768]{1,0:T(8,128)(2,1)S(1)}, u32[]{:S(2)}, u32[]{:S(2)}) collective-permute-start(bf16[128,768]{1,0:T(8,128)(2,1)S(1)} %get-tuple-element.23.refs_0_), channel_id=1, source_target_pairs={{0,1},{1,0},{2,3},{3,2},{4,5},{5,4},{6,7},{7,6},{8,9},{9,8},{10,11... | collective-permute-start | bytes 589832 | tf_op jit(solution)/shard_map/ppermute | solution.py:77
  13.5 1.5 %collective-permute-start.9 = (bf16[144,768]{1,0:T(8,128)(2,1)S(1)}, bf16[144,768]{1,0:T(8,128)(2,1)S(1)}, u32[]{:S(2)}, u32[]{:S(2)}) collective-permute-start(bf16[144,768]{1,0:T(8,128)(2,1)S(1)} %get-tuple-element.36), channel_id=1, source_target_pairs={{0,16},{8,24},{16,0},{24,8},{1,17},{9,25},{17,1},{25,9},{2,18},{10... | collective-permute-start | bytes 663560 | tf_op jit(solution)/shard_map/ppermute | solution.py:77
  15.0 1.3 %shard_map.62 = (f32[64,768]{1,0:T(8,128)S(1)}, bf16[64,768]{1,0:T(8,128)(2,1)S(1)}, bf16[144,128]{1,0:T(8,128)(2,1)S(1)}, bf16[128,768]{1,0:T(8,128)(2,1)S(1)}) custom-call(bf16[128,768]{1,0:T(8,128)(2,1)S(1)} %get-tuple-element.23.refs_0_, bf16[1024,768]{1,0:T(8,128)(2,1)S(1)} %get-tuple-element.22.refs_5_.refs_1_, ...), custom_call_target="tpu_custom_call" | custom-call | flops 402653184 | tf_op jit(solution)/shard_map/pallas_call | solution.py:96
  16.4 0.5 %collective-permute-start.10 = (bf16[128,768]{1,0:T(8,128)(2,1)S(1)}, bf16[128,768]{1,0:T(8,128)(2,1)S(1)}, u32[]{:S(2)}, u32[]{:S(2)}) collective-permute-start(bf16[128,768]{1,0:T(8,128)(2,1)S(1)} %get-tuple-element.37), channel_id=1, source_target_pairs={{0,17},{1,16},{2,19},{3,18},{4,21},{5,20},{6,23},{7,22},{8,25},{9,... | collective-permute-start | bytes 589832 | tf_op jit(solution)/shard_map/ppermute | solution.py:87
  17.2 0.5 %collective-permute-done.4.refs_0_.refs_1_ = bf16[128,768]{1,0:T(8,128)(2,1)S(1)} collective-permute-done((bf16[128,768]{1,0:T(8,128)(2,1)S(1)}, bf16[128,768]{1,0:T(8,128)(2,1)S(1)}, u32[]{:S(2)}, u32[]{:S(2)}) %collective-permute-start.4) | collective-permute-done | bytes 196640 | tf_op jit(solution)/shard_map/ppermute | solution.py:77
  17.7 1.3 %shard_map.63 = (f32[64,768]{1,0:T(8,128)S(1)}, bf16[64,768]{1,0:T(8,128)(2,1)S(1)}, bf16[144,128]{1,0:T(8,128)(2,1)S(1)}) custom-call(bf16[128,768]{1,0:T(8,128)(2,1)S(1)} %collective-permute-done.4.refs_0_.refs_1_, bf16[1024,768]{1,0:T(8,128)(2,1)S(1)} %get-tuple-element.22.refs_5_.refs_1_, bf16[16,768]{1,0:T(8,128)(2,1)S(1)} %shard_map.60.refs_4_.refs_2_, ...), custom_call_target="tpu_custom_call" | custom-call | flops 402653184 | tf_op jit(solution)/shard_map/pallas_call | solution.py:96
  19.0 1.3 %collective-permute-start.6 = (bf16[64,768]{1,0:T(8,128)(2,1)S(1)}, bf16[64,768]{1,0:T(8,128)(2,1)S(1)}, u32[]{:S(2)}, u32[]{:S(2)}) collective-permute-start(bf16[64,768]{1,0:T(8,128)(2,1)S(1)} %get-tuple-element.32), channel_id=1, source_target_pairs={{0,2},{1,3},{2,0},{3,1},{4,6},{5,7},{6,4},{7,5},{8,10},{9,11},{10,... | collective-permute-start | bytes 294920 | tf_op jit(solution)/shard_map/ppermute | solution.py:77
  20.3 0.6 %shard_map.64 = (f32[1024,768]{1,0:T(8,128)S(1)}, bf16[400,768]{1,0:T(8,128)(2,1)S(1)}) custom-call(bf16[128,768]{1,0:T(8,128)(2,1)S(1)} %get-tuple-element.23.refs_0_, bf16[128,768]{1,0:T(8,128)(2,1)S(1)} %collective-permute-done.4.refs_0_.refs_1_, bf16[144,128]{1,0:T(8,128)(2,1)S(1)} %get-tuple-element.26.refs_3_.refs_2_, ...), custom_call_target="tpu_custom_call" | custom-call | flops 402653184 | tf_op jit(solution)/shard_map/pallas_call | solution.py:96
  20.9 0.6 %collective-permute-done.3.refs_1_ = bf16[64,768]{1,0:T(8,128)(2,1)S(1)} collective-permute-done((bf16[64,768]{1,0:T(8,128)(2,1)S(1)}, bf16[64,768]{1,0:T(8,128)(2,1)S(1)}, u32[]{:S(2)}, u32[]{:S(2)}) %collective-permute-start.3) | collective-permute-done | bytes 98336 | tf_op jit(solution)/shard_map/ppermute | solution.py:77
  21.6 1.3 %collective-permute-start.5 = (bf16[32,768]{1,0:T(8,128)(2,1)S(1)}, bf16[32,768]{1,0:T(8,128)(2,1)S(1)}, u32[]{:S(2)}, u32[]{:S(2)}) collective-permute-start(bf16[32,768]{1,0:T(8,128)(2,1)S(1)} %get-tuple-element.30), channel_id=1, source_target_pairs={{0,4},{1,5},{2,6},{3,7},{4,0},{5,1},{6,2},{7,3},{8,12},{9,13},{10,... | collective-permute-start | bytes 147464 | tf_op jit(solution)/shard_map/ppermute | solution.py:77
  22.9 0.8 %collective-permute-done.6.refs_1_ = bf16[64,768]{1,0:T(8,128)(2,1)S(1)} collective-permute-done((bf16[64,768]{1,0:T(8,128)(2,1)S(1)}, bf16[64,768]{1,0:T(8,128)(2,1)S(1)}, u32[]{:S(2)}, u32[]{:S(2)}) %collective-permute-start.6) | collective-permute-done | bytes 98336 | tf_op jit(solution)/shard_map/ppermute | solution.py:77
  23.7 2.0 %collective-permute-start.7 = (bf16[32,768]{1,0:T(8,128)(2,1)S(1)}, bf16[32,768]{1,0:T(8,128)(2,1)S(1)}, u32[]{:S(2)}, u32[]{:S(2)}) collective-permute-start(bf16[32,768]{1,0:T(8,128)(2,1)S(1)} %get-tuple-element.34), channel_id=1, source_target_pairs={{0,4},{1,5},{2,6},{3,7},{4,0},{5,1},{6,2},{7,3},{8,12},{9,13},{10,... | collective-permute-start | bytes 147464 | tf_op jit(solution)/shard_map/ppermute | solution.py:77
  25.8 1.9 %shard_map.69.refs_1_ = f32[1024,768]{1,0:T(8,128)S(1)} custom-call(bf16[272,768]{1,0:T(8,128)(2,1)S(1)} %shard_map.68.refs_0_, bf16[1024,768]{1,0:T(8,128)(2,1)S(1)} %get-tuple-element.22.refs_5_.refs_1_, f32[1024,768]{1,0:T(8,128)S(1)} %get-tuple-element.28.refs_2_.refs_3_, f32[32,768]{1,0:T(8,128)S(1)} %get-tuple-element.33.refs_2_.refs_3_.refs_0_), custom_call_target="tpu_custom_call" | custom-call | flops 8053063680 | tf_op jit(solution)/shard_map/pallas_call | solution.py:96
  27.8 0.6 %shard_map.70.refs_2_ = f32[1024,768]{1,0:T(8,128)S(1)} custom-call(bf16[400,768]{1,0:T(8,128)(2,1)S(1)} %collective-permute-done.8.refs_0_, f32[1024,768]{1,0:T(8,128)S(1)} %shard_map.69.refs_1_, f32[32,768]{1,0:T(8,128)S(1)} %shard_map.67.refs_2_.refs_0_), custom_call_target="tpu_custom_call" | custom-call | flops 402653184 | tf_op jit(solution)/shard_map/pallas_call | solution.py:96
  28.8 3.2 %collective-permute-start.11 = (bf16[32,768]{1,0:T(8,128)(2,1)S(1)}, bf16[32,768]{1,0:T(8,128)(2,1)S(1)}, u32[]{:S(2)}, u32[]{:S(2)}) collective-permute-start(bf16[32,768]{1,0:T(8,128)(2,1)S(1)} %shard_map.71), channel_id=1, source_target_pairs={{0,1},{1,0},{2,3},{3,2},{4,5},{5,4},{6,7},{7,6},{8,9},{9,8},{10,11... | collective-permute-start | bytes 147464 | tf_op jit(solution)/shard_map/ppermute | solution.py:77
  32.0 2.7 %shard_map.72 = (bf16[1024,768]{1,0:T(8,128)(2,1)}, s32[1,128]{1,0:T(1,128)S(1)}) custom-call(bf16[272,768]{1,0:T(8,128)(2,1)S(1)} %collective-permute-done.12.refs_0_, bf16[1024,768]{1,0:T(8,128)(2,1)S(1)} %get-tuple-element.22.refs_5_.refs_1_, f32[1024,768]{1,0:T(8,128)S(1)} %shard_map.70.refs_2_), custom_call_target="tpu_custom_call" | custom-call | tf_op jit(solution)/shard_map/pallas_call | solution.py:260
  34.7 0.7 %shard_map.73 = f32[32,768]{1,0:T(8,128)} custom-call(f32[32,768]{1,0:T(8,128)S(1)} %shard_map.67.refs_2_.refs_0_, bf16[32,768]{1,0:T(8,128)(2,1)S(1)} %collective-permute-done.11.refs_1_, s32[1,128]{1,0:T(1,128)S(1)} %get-tuple-element.38.refs_2_), custom_call_target="tpu_custom_call" | custom-call | tf_op jit(solution)/shard_map/pallas_call | solution.py:96
  (22 shorter events, 1.3 us)
Async XLA Ops:
  0.6 8.9 %collective-permute-start = (bf16[32,768]{1,0:T(8,128)(2,1)}, bf16[32,768]{1,0:T(8,128)(2,1)S(1)}, u32[]{:S(2)}, u32[]{:S(2)}) collective-permute-start(bf16[32,768]{1,0:T(8,128)(2,1)} %refs_0_.1), channel_id=1, source_target_pairs={{0,2},{1,3},{2,0},{3,1},{4,6},{5,7},{6,4},{7,5},{8,10},{9,11},{10,... | collective-permute-start | bytes 147464 | tf_op jit(solution)/shard_map/ppermute | solution.py:77
  3.7 6.7 %collective-permute-start.1 = (bf16[32,768]{1,0:T(8,128)(2,1)}, bf16[32,768]{1,0:T(8,128)(2,1)S(1)}, u32[]{:S(2)}, u32[]{:S(2)}) collective-permute-start(bf16[32,768]{1,0:T(8,128)(2,1)} %refs_0_.1), channel_id=1, source_target_pairs={{0,6},{1,7},{2,4},{3,5},{4,2},{5,3},{6,0},{7,1},{8,14},{9,15},{10,... | collective-permute-start | bytes 147464 | tf_op jit(solution)/shard_map/ppermute | solution.py:77
  6.2 5.7 %collective-permute-start.2 = (bf16[32,768]{1,0:T(8,128)(2,1)}, bf16[32,768]{1,0:T(8,128)(2,1)S(1)}, u32[]{:S(2)}, u32[]{:S(2)}) collective-permute-start(bf16[32,768]{1,0:T(8,128)(2,1)} %refs_0_.1), channel_id=1, source_target_pairs={{0,4},{1,5},{2,6},{3,7},{4,0},{5,1},{6,2},{7,3},{8,12},{9,13},{10,... | collective-permute-start | bytes 147464 | tf_op jit(solution)/shard_map/ppermute | solution.py:77
  7.0 1.4 %copy-start = (bf16[1024,768]{1,0:T(8,128)(2,1)S(1)}, bf16[1024,768]{1,0:T(8,128)(2,1)}, u32[]{:S(2)}) copy-start(bf16[1024,768]{1,0:T(8,128)(2,1)} %refs_1_.1) | copy-start | bytes 4718596
  8.4 0.8 %copy-start.1 = (bf16[32,768]{1,0:T(8,128)(2,1)S(1)}, bf16[32,768]{1,0:T(8,128)(2,1)}, u32[]{:S(2)}) copy-start(bf16[32,768]{1,0:T(8,128)(2,1)} %refs_0_.1) | copy-start | bytes 147460
  12.0 5.7 %collective-permute-start.4 = (bf16[128,768]{1,0:T(8,128)(2,1)S(1)}, bf16[128,768]{1,0:T(8,128)(2,1)S(1)}, u32[]{:S(2)}, u32[]{:S(2)}) collective-permute-start(bf16[128,768]{1,0:T(8,128)(2,1)S(1)} %get-tuple-element.23.refs_0_), channel_id=1, source_target_pairs={{0,1},{1,0},{2,3},{3,2},{4,5},{5,4},{6,7},{7,6},{8,9},{9,8},{10,11... | collective-permute-start | bytes 589832 | tf_op jit(solution)/shard_map/ppermute | solution.py:77
  13.5 12.2 %collective-permute-start.9 = (bf16[144,768]{1,0:T(8,128)(2,1)S(1)}, bf16[144,768]{1,0:T(8,128)(2,1)S(1)}, u32[]{:S(2)}, u32[]{:S(2)}) collective-permute-start(bf16[144,768]{1,0:T(8,128)(2,1)S(1)} %get-tuple-element.36), channel_id=1, source_target_pairs={{0,16},{8,24},{16,0},{24,8},{1,17},{9,25},{17,1},{25,9},{2,18},{10... | collective-permute-start | bytes 663560 | tf_op jit(solution)/shard_map/ppermute | solution.py:77
  16.4 9.3 %collective-permute-start.10 = (bf16[128,768]{1,0:T(8,128)(2,1)S(1)}, bf16[128,768]{1,0:T(8,128)(2,1)S(1)}, u32[]{:S(2)}, u32[]{:S(2)}) collective-permute-start(bf16[128,768]{1,0:T(8,128)(2,1)S(1)} %get-tuple-element.37), channel_id=1, source_target_pairs={{0,17},{1,16},{2,19},{3,18},{4,21},{5,20},{6,23},{7,22},{8,25},{9,... | collective-permute-start | bytes 589832 | tf_op jit(solution)/shard_map/ppermute | solution.py:87
  16.9 4.6 %collective-permute-start.3 = (bf16[64,768]{1,0:T(8,128)(2,1)S(1)}, bf16[64,768]{1,0:T(8,128)(2,1)S(1)}, u32[]{:S(2)}, u32[]{:S(2)}) collective-permute-start(bf16[64,768]{1,0:T(8,128)(2,1)S(1)} %get-tuple-element.25), channel_id=1, source_target_pairs={{0,2},{1,3},{2,0},{3,1},{4,6},{5,7},{6,4},{7,5},{8,10},{9,11},{10,... | collective-permute-start | bytes 294920 | tf_op jit(solution)/shard_map/ppermute | solution.py:77
  19.0 4.7 %collective-permute-start.6 = (bf16[64,768]{1,0:T(8,128)(2,1)S(1)}, bf16[64,768]{1,0:T(8,128)(2,1)S(1)}, u32[]{:S(2)}, u32[]{:S(2)}) collective-permute-start(bf16[64,768]{1,0:T(8,128)(2,1)S(1)} %get-tuple-element.32), channel_id=1, source_target_pairs={{0,2},{1,3},{2,0},{3,1},{4,6},{5,7},{6,4},{7,5},{8,10},{9,11},{10,... | collective-permute-start | bytes 294920 | tf_op jit(solution)/shard_map/ppermute | solution.py:77
  21.6 6.2 %collective-permute-start.5 = (bf16[32,768]{1,0:T(8,128)(2,1)S(1)}, bf16[32,768]{1,0:T(8,128)(2,1)S(1)}, u32[]{:S(2)}, u32[]{:S(2)}) collective-permute-start(bf16[32,768]{1,0:T(8,128)(2,1)S(1)} %get-tuple-element.30), channel_id=1, source_target_pairs={{0,4},{1,5},{2,6},{3,7},{4,0},{5,1},{6,2},{7,3},{8,12},{9,13},{10,... | collective-permute-start | bytes 147464 | tf_op jit(solution)/shard_map/ppermute | solution.py:77
  22.9 4.9 %collective-permute-start.8 = (bf16[400,768]{1,0:T(8,128)(2,1)S(1)}, bf16[400,768]{1,0:T(8,128)(2,1)S(1)}, u32[]{:S(2)}, u32[]{:S(2)}) collective-permute-start(bf16[400,768]{1,0:T(8,128)(2,1)S(1)} %get-tuple-element.35), channel_id=1, source_target_pairs={{0,8},{8,0},{16,24},{24,16},{1,9},{9,1},{17,25},{25,17},{2,10},{10... | collective-permute-start | bytes 1843208 | tf_op jit(solution)/shard_map/ppermute | solution.py:77
  23.7 5.1 %collective-permute-start.7 = (bf16[32,768]{1,0:T(8,128)(2,1)S(1)}, bf16[32,768]{1,0:T(8,128)(2,1)S(1)}, u32[]{:S(2)}, u32[]{:S(2)}) collective-permute-start(bf16[32,768]{1,0:T(8,128)(2,1)S(1)} %get-tuple-element.34), channel_id=1, source_target_pairs={{0,4},{1,5},{2,6},{3,7},{4,0},{5,1},{6,2},{7,3},{8,12},{9,13},{10,... | collective-permute-start | bytes 147464 | tf_op jit(solution)/shard_map/ppermute | solution.py:77
  25.7 6.3 %collective-permute-start.12 = (bf16[272,768]{1,0:T(8,128)(2,1)S(1)}, bf16[272,768]{1,0:T(8,128)(2,1)S(1)}, u32[]{:S(2)}, u32[]{:S(2)}) collective-permute-start(bf16[272,768]{1,0:T(8,128)(2,1)S(1)} %shard_map.68.refs_0_), channel_id=1, source_target_pairs={{0,8},{8,0},{16,24},{24,16},{1,9},{9,1},{17,25},{25,17},{2,10},{10... | collective-permute-start | bytes 1253384 | tf_op jit(solution)/shard_map/ppermute | solution.py:77
  28.8 5.9 %collective-permute-start.11 = (bf16[32,768]{1,0:T(8,128)(2,1)S(1)}, bf16[32,768]{1,0:T(8,128)(2,1)S(1)}, u32[]{:S(2)}, u32[]{:S(2)}) collective-permute-start(bf16[32,768]{1,0:T(8,128)(2,1)S(1)} %shard_map.71), channel_id=1, source_target_pairs={{0,1},{1,0},{2,3},{3,2},{4,5},{5,4},{6,7},{7,6},{8,9},{9,8},{10,11... | collective-permute-start | bytes 147464 | tf_op jit(solution)/shard_map/ppermute | solution.py:77

commit v21 on v16

--- a/solution.py
+++ b/solution.py
@@ -174,9 +174,11 @@
     grad_body(1, rows_ref, weights_ref, note_ref, kept_ref, sent_ref, slope_ref)
 
 
-def fold_body(terms_ref, came_ref, kept_ref, sent_ref):
+def fold_body(terms_ref, came_ref, first_ref, second_ref):
     terms = terms_ref[...] + came_ref[...].astype(jnp.float32)
-    halve(terms, kept_ref, sent_ref, kept_ref.shape[0])
+    span = first_ref.shape[0]
+    first_ref[...] = terms[:span].astype(first_ref.dtype)
+    second_ref[...] = terms[span:].astype(second_ref.dtype)
 
 
 def sum_body(kept_ref, *refs):
@@ -326,7 +328,6 @@
     work = 4 * half * lab_dev * width
     slope_like = like(BLOCK + NOTE, half, bf16)
     pair = [like(half // 2, width, f32), like(half // 2, width, bf16)]
-    single = [like(q_home, width, f32), like(q_home, width, bf16)]
     near_kept, near_sent, near_slope, near_copy = local_call(
         near_body,
         pair + [slope_like, like(half, width, bf16)],
@@ -346,24 +347,25 @@
         work,
     )
     mate = swap(own, "pb", 1)
-    far_kept, far_sent = local_call(fold_body, single, [far_kept, far_came], 0, [acc])
-    far_came = swap(far_sent, "lab", 4)
-    near_kept, near_sent = local_call(fold_body, single, [near_kept, near_came], 0, [far_kept])
+    home, sent = like(q_home, width, f32), like(q_home, width, bf16)
+    near_kept, near_sent = local_call(
+        fold_body, [home, sent], [near_kept, near_came], 0, [acc]
+    )
     near_came = swap(near_sent, "lab", 4)
+    far_sent, far_across = local_call(
+        fold_body, [sent, sent], [far_kept, far_came], 0, [near_kept, acc]
+    )
+    far_came, far_across = swap(far_sent, "lab", 1), swap(far_across, "lab", 5)
     cross = local_call(
-        stack_body, [like(qcount + NOTE, width, bf16)], [cross_near, cross_far], 0, [far_kept]
+        stack_body, [like(qcount + NOTE, width, bf16)], [cross_near, cross_far], 0, [far_sent]
     )[0]
     cross_mate = swap(cross, "pb", 1)
     grown = like(lab_dev, width, f32)
-    acc = local_call(cross_body, [grown], [cross, weights, acc], 20 * work, [near_kept])[0]
-    far_sent = local_call(
-        sum_body, [like(q_home, width, bf16)], [far_kept, far_came], 0, [acc]
-    )[0]
-    far_came = swap(far_sent, "lab", 1)
-    acc = local_call(mate_body, [grown], [mate, acc], work, [far_sent])[0]
+    acc = local_call(cross_body, [grown], [cross, weights, acc], 20 * work)[0]
+    acc = local_call(mate_body, [grown], [mate, acc], work)[0]
     weight_grad, mark = late(groups, cross_mate, weights, acc)
     query_grad = local_call(
-        sum_body, [like(q_home, width, f32)], [near_kept, near_came, far_came], 0, [mark]
+        sum_body, [home], [near_kept, near_came, far_came, far_across], 0, [mark]
     )[0]
     return (query_grad, weight_grad)
 

time: 35.6 us -> 33.5 us (0.941)
  starting transfers between devices: 17 us -> 15.7 us
  waiting for transfers between devices: 5.15 us -> 4.39 us
    ppermute x12, starting transfers between devices: 16.5 us -> 15.2 us  [swap(): return lax.ppermute(value, axis, [(i, i ^ bit) for i in range(count)])]
    ppermute x12, waiting for transfers between devices: 5.15 us -> 4.39 us  [swap(): return lax.ppermute(value, axis, [(i, i ^ bit) for i in range(count)])]
    pallas_call x13 -> x12, Pallas kernels: 6.76 us -> 6.75 us  [local_call(): pl.pallas_call(lambda *refs: body(*refs[:given], *refs[later:]), out_shap...]
  transfers between devices with their start and end apart: 13 -> 13, of which waited for: 4 -> 5; matrix products, arithmetic and copies ran while one was open for 2% -> 2% of each run, Pallas kernels for 25% -> 26%
where the time goes in v21:
time: 33.5 us; the launch traced here: 33.2 us
  starting transfers between devices  15.7 us (47%)
  Pallas kernels  9.47 us (28%)
  waiting for transfers between devices  4.39 us (13%)
  local copies, waits for them, and re-layouts  2.21 us (7%)
  between operations  0.74 us (2%)
  other arithmetic  0.72 us (2%)
    ppermute x12, starting transfers between devices, swap(): return lax.ppermute(value, axis, [(i, i ^ bit) for i in range(count)])  15.2 us
    pallas_call x12, Pallas kernels, local_call(): pl.pallas_call(lambda *refs: body(*refs[:given], *refs[later:]), out_shap...  6.75 us
    ppermute x12, waiting for transfers between devices, swap(): return lax.ppermute(value, axis, [(i, i ^ bit) for i in range(count)])  4.39 us
    pallas_call x1, Pallas kernels, late(): pl.pallas_call(lambda *refs: late_body(groups, *refs), out_shape=[out, li...  2.71 us
    unnamed x4, local copies, waits for them, and re-layouts  2.21 us
    convert_element_type x1, other arithmetic, dense_shards(): jnp.concatenate([sibling_blocks.T, positive_slot[None]], axis=0).astype(f32)  0.72 us
  transfers between devices with their start and end apart: 13, of which 5 were waited for; matrix products, arithmetic and copies ran while one was open for 2% of the time, Pallas kernels for 26%

profile of v21, /device:TPU:0, one launch (start us, length us, event | category | flops | bytes accessed | tf_op | source)
XLA Modules:
  0.0 33.2 jit_solution(13918824389860873682)
XLA Ops:
  0.6 3.1 %collective-permute-start = (bf16[32,768]{1,0:T(8,128)(2,1)}, bf16[32,768]{1,0:T(8,128)(2,1)S(1)}, u32[]{:S(2)}, u32[]{:S(2)}) collective-permute-start(bf16[32,768]{1,0:T(8,128)(2,1)} %refs_0_.1), channel_id=1, source_target_pairs={{0,2},{1,3},{2,0},{3,1},{4,6},{5,7},{6,4},{7,5},{8,10},{9,11},{10,... | collective-permute-start | bytes 147464 | tf_op jit(solution)/shard_map/ppermute | solution.py:77
  3.7 2.5 %collective-permute-start.2 = (bf16[32,768]{1,0:T(8,128)(2,1)}, bf16[32,768]{1,0:T(8,128)(2,1)S(1)}, u32[]{:S(2)}, u32[]{:S(2)}) collective-permute-start(bf16[32,768]{1,0:T(8,128)(2,1)} %refs_0_.1), channel_id=1, source_target_pairs={{0,6},{1,7},{2,4},{3,5},{4,2},{5,3},{6,0},{7,1},{8,14},{9,15},{10,... | collective-permute-start | bytes 147464 | tf_op jit(solution)/shard_map/ppermute | solution.py:77
  6.3 0.7 %add_convert_fusion.refs_1_ = f32[9,256]{1,0:T(8,128)S(1)} fusion(s32[1,256]{1,0:T(1,128)} %bitcast.4, s32[8,256]{1,0:T(8,128)} %bitcast.3), kind=kLoop, calls=%fused_computation | loop fusion | flops 4608 | bytes 18432 | tf_op jit(solution)/shard_map/convert_element_type | solution.py:314
  7.0 1.4 %copy-done = bf16[1024,768]{1,0:T(8,128)(2,1)S(1)} copy-done((bf16[1024,768]{1,0:T(8,128)(2,1)S(1)}, bf16[1024,768]{1,0:T(8,128)(2,1)}, u32[]{:S(2)}) %copy-start) | copy-done | bytes 1572888
  8.4 0.8 %copy-done.1 = bf16[32,768]{1,0:T(8,128)(2,1)S(1)} copy-done((bf16[32,768]{1,0:T(8,128)(2,1)S(1)}, bf16[32,768]{1,0:T(8,128)(2,1)}, u32[]{:S(2)}) %copy-start.1) | copy-done | bytes 49176
  9.5 0.9 %collective-permute-done.2.refs_3_ = bf16[32,768]{1,0:T(8,128)(2,1)S(1)} collective-permute-done((bf16[32,768]{1,0:T(8,128)(2,1)}, bf16[32,768]{1,0:T(8,128)(2,1)S(1)}, u32[]{:S(2)}, u32[]{:S(2)}) %collective-permute-start.2) | collective-permute-done | bytes 49184 | tf_op jit(solution)/shard_map/ppermute | solution.py:77
  10.4 1.5 %collective-permute-done.1.refs_2_ = bf16[32,768]{1,0:T(8,128)(2,1)S(1)} collective-permute-done((bf16[32,768]{1,0:T(8,128)(2,1)}, bf16[32,768]{1,0:T(8,128)(2,1)S(1)}, u32[]{:S(2)}, u32[]{:S(2)}) %collective-permute-start.1) | collective-permute-done | bytes 49184 | tf_op jit(solution)/shard_map/ppermute | solution.py:77
  12.0 1.6 %collective-permute-start.4 = (bf16[128,768]{1,0:T(8,128)(2,1)S(1)}, bf16[128,768]{1,0:T(8,128)(2,1)S(1)}, u32[]{:S(2)}, u32[]{:S(2)}) collective-permute-start(bf16[128,768]{1,0:T(8,128)(2,1)S(1)} %get-tuple-element.23.refs_0_), channel_id=1, source_target_pairs={{0,1},{1,0},{2,3},{3,2},{4,5},{5,4},{6,7},{7,6},{8,9},{9,8},{10,11... | collective-permute-start | bytes 589832 | tf_op jit(solution)/shard_map/ppermute | solution.py:77
  13.5 1.5 %collective-permute-start.9 = (bf16[144,768]{1,0:T(8,128)(2,1)S(1)}, bf16[144,768]{1,0:T(8,128)(2,1)S(1)}, u32[]{:S(2)}, u32[]{:S(2)}) collective-permute-start(bf16[144,768]{1,0:T(8,128)(2,1)S(1)} %get-tuple-element.35), channel_id=1, source_target_pairs={{0,16},{8,24},{16,0},{24,8},{1,17},{9,25},{17,1},{25,9},{2,18},{10... | collective-permute-start | bytes 663560 | tf_op jit(solution)/shard_map/ppermute | solution.py:77
  15.0 1.3 %shard_map.62 = (f32[64,768]{1,0:T(8,128)S(1)}, bf16[64,768]{1,0:T(8,128)(2,1)S(1)}, bf16[144,128]{1,0:T(8,128)(2,1)S(1)}, bf16[128,768]{1,0:T(8,128)(2,1)S(1)}) custom-call(bf16[128,768]{1,0:T(8,128)(2,1)S(1)} %get-tuple-element.23.refs_0_, bf16[1024,768]{1,0:T(8,128)(2,1)S(1)} %get-tuple-element.22.refs_5_.refs_1_, ...), custom_call_target="tpu_custom_call" | custom-call | flops 402653184 | tf_op jit(solution)/shard_map/pallas_call | solution.py:96
  16.4 0.5 %collective-permute-start.10 = (bf16[128,768]{1,0:T(8,128)(2,1)S(1)}, bf16[128,768]{1,0:T(8,128)(2,1)S(1)}, u32[]{:S(2)}, u32[]{:S(2)}) collective-permute-start(bf16[128,768]{1,0:T(8,128)(2,1)S(1)} %get-tuple-element.36), channel_id=1, source_target_pairs={{0,17},{1,16},{2,19},{3,18},{4,21},{5,20},{6,23},{7,22},{8,25},{9,... | collective-permute-start | bytes 589832 | tf_op jit(solution)/shard_map/ppermute | solution.py:87
  17.2 0.5 %collective-permute-done.4.refs_0_.refs_1_ = bf16[128,768]{1,0:T(8,128)(2,1)S(1)} collective-permute-done((bf16[128,768]{1,0:T(8,128)(2,1)S(1)}, bf16[128,768]{1,0:T(8,128)(2,1)S(1)}, u32[]{:S(2)}, u32[]{:S(2)}) %collective-permute-start.4) | collective-permute-done | bytes 196640 | tf_op jit(solution)/shard_map/ppermute | solution.py:77
  17.7 1.3 %shard_map.63 = (f32[64,768]{1,0:T(8,128)S(1)}, bf16[64,768]{1,0:T(8,128)(2,1)S(1)}, bf16[144,128]{1,0:T(8,128)(2,1)S(1)}) custom-call(bf16[128,768]{1,0:T(8,128)(2,1)S(1)} %collective-permute-done.4.refs_0_.refs_1_, bf16[1024,768]{1,0:T(8,128)(2,1)S(1)} %get-tuple-element.22.refs_5_.refs_1_, bf16[16,768]{1,0:T(8,128)(2,1)S(1)} %shard_map.60.refs_4_.refs_2_, ...), custom_call_target="tpu_custom_call" | custom-call | flops 402653184 | tf_op jit(solution)/shard_map/pallas_call | solution.py:96
  19.0 1.3 %collective-permute-start.6 = (bf16[64,768]{1,0:T(8,128)(2,1)S(1)}, bf16[64,768]{1,0:T(8,128)(2,1)S(1)}, u32[]{:S(2)}, u32[]{:S(2)}) collective-permute-start(bf16[64,768]{1,0:T(8,128)(2,1)S(1)} %get-tuple-element.32), channel_id=1, source_target_pairs={{0,2},{1,3},{2,0},{3,1},{4,6},{5,7},{6,4},{7,5},{8,10},{9,11},{10,... | collective-permute-start | bytes 294920 | tf_op jit(solution)/shard_map/ppermute | solution.py:77
  20.3 0.6 %shard_map.64 = (f32[1024,768]{1,0:T(8,128)S(1)}, bf16[400,768]{1,0:T(8,128)(2,1)S(1)}) custom-call(bf16[128,768]{1,0:T(8,128)(2,1)S(1)} %get-tuple-element.23.refs_0_, bf16[128,768]{1,0:T(8,128)(2,1)S(1)} %collective-permute-done.4.refs_0_.refs_1_, bf16[144,128]{1,0:T(8,128)(2,1)S(1)} %get-tuple-element.26.refs_3_.refs_2_, ...), custom_call_target="tpu_custom_call" | custom-call | flops 402653184 | tf_op jit(solution)/shard_map/pallas_call | solution.py:96
  20.9 0.6 %collective-permute-done.3.refs_1_ = bf16[64,768]{1,0:T(8,128)(2,1)S(1)} collective-permute-done((bf16[64,768]{1,0:T(8,128)(2,1)S(1)}, bf16[64,768]{1,0:T(8,128)(2,1)S(1)}, u32[]{:S(2)}, u32[]{:S(2)}) %collective-permute-start.3) | collective-permute-done | bytes 98336 | tf_op jit(solution)/shard_map/ppermute | solution.py:77
  21.6 1.3 %collective-permute-start.5 = (bf16[32,768]{1,0:T(8,128)(2,1)S(1)}, bf16[32,768]{1,0:T(8,128)(2,1)S(1)}, u32[]{:S(2)}, u32[]{:S(2)}) collective-permute-start(bf16[32,768]{1,0:T(8,128)(2,1)S(1)} %get-tuple-element.30), channel_id=1, source_target_pairs={{0,4},{1,5},{2,6},{3,7},{4,0},{5,1},{6,2},{7,3},{8,12},{9,13},{10,... | collective-permute-start | bytes 147464 | tf_op jit(solution)/shard_map/ppermute | solution.py:77
  22.9 0.8 %collective-permute-done.6.refs_1_ = bf16[64,768]{1,0:T(8,128)(2,1)S(1)} collective-permute-done((bf16[64,768]{1,0:T(8,128)(2,1)S(1)}, bf16[64,768]{1,0:T(8,128)(2,1)S(1)}, u32[]{:S(2)}, u32[]{:S(2)}) %collective-permute-start.6) | collective-permute-done | bytes 98336 | tf_op jit(solution)/shard_map/ppermute | solution.py:77
  23.7 2.9 %collective-permute-start.8 = (bf16[32,768]{1,0:T(8,128)(2,1)S(1)}, bf16[32,768]{1,0:T(8,128)(2,1)S(1)}, u32[]{:S(2)}, u32[]{:S(2)}) collective-permute-start(bf16[32,768]{1,0:T(8,128)(2,1)S(1)} %get-tuple-element.34), channel_id=1, source_target_pairs={{0,5},{1,4},{2,7},{3,6},{4,1},{5,0},{6,3},{7,2},{8,13},{9,12},{10,... | collective-permute-start | bytes 147464 | tf_op jit(solution)/shard_map/ppermute | solution.py:77
  26.7 0.5 %collective-permute-start.7 = (bf16[32,768]{1,0:T(8,128)(2,1)S(1)}, bf16[32,768]{1,0:T(8,128)(2,1)S(1)}, u32[]{:S(2)}, u32[]{:S(2)}) collective-permute-start(bf16[32,768]{1,0:T(8,128)(2,1)S(1)} %get-tuple-element.33.refs_2_), channel_id=1, source_target_pairs={{0,1},{1,0},{2,3},{3,2},{4,5},{5,4},{6,7},{7,6},{8,9},{9,8},{10,11... | collective-permute-start | bytes 147464 | tf_op jit(solution)/shard_map/ppermute | solution.py:77
  27.3 1.9 %shard_map.68.refs_1_ = f32[1024,768]{1,0:T(8,128)S(1)} custom-call(bf16[272,768]{1,0:T(8,128)(2,1)S(1)} %shard_map.67.refs_0_, bf16[1024,768]{1,0:T(8,128)(2,1)S(1)} %get-tuple-element.22.refs_5_.refs_1_, f32[1024,768]{1,0:T(8,128)S(1)} %get-tuple-element.28.refs_2_.refs_3_), custom_call_target="tpu_custom_call" | custom-call | flops 8053063680 | tf_op jit(solution)/shard_map/pallas_call | solution.py:96
  29.2 0.6 %shard_map.69.refs_2_ = f32[1024,768]{1,0:T(8,128)S(1)} custom-call(bf16[400,768]{1,0:T(8,128)(2,1)S(1)} %collective-permute-done.12.refs_0_, f32[1024,768]{1,0:T(8,128)S(1)} %shard_map.68.refs_1_), custom_call_target="tpu_custom_call" | custom-call | flops 402653184 | tf_op jit(solution)/shard_map/pallas_call | solution.py:96
  29.8 2.7 %shard_map.70 = (bf16[1024,768]{1,0:T(8,128)(2,1)}, s32[1,128]{1,0:T(1,128)S(1)}) custom-call(bf16[272,768]{1,0:T(8,128)(2,1)S(1)} %collective-permute-done.11.refs_0_, bf16[1024,768]{1,0:T(8,128)(2,1)S(1)} %get-tuple-element.22.refs_5_.refs_1_, f32[1024,768]{1,0:T(8,128)S(1)} %shard_map.69.refs_2_), custom_call_target="tpu_custom_call" | custom-call | tf_op jit(solution)/shard_map/pallas_call | solution.py:261
  32.6 0.7 %shard_map.71 = f32[32,768]{1,0:T(8,128)} custom-call(f32[32,768]{1,0:T(8,128)S(1)} %get-tuple-element.29.refs_2_.refs_0_, bf16[32,768]{1,0:T(8,128)(2,1)S(1)} %collective-permute-done.5.refs_1_, bf16[32,768]{1,0:T(8,128)(2,1)S(1)} %collective-permute-done.7.refs_2_, bf16[32,768]{1,0:T(8,128)(2,1)S(1)} %collective-permute-done.8.refs_3_, ...), custom_call_target="tpu_custom_call" | custom-call | tf_op jit(solution)/shard_map/pallas_call | solution.py:96
  (20 shorter events, 0.8 us)
Async XLA Ops:
  0.6 8.9 %collective-permute-start = (bf16[32,768]{1,0:T(8,128)(2,1)}, bf16[32,768]{1,0:T(8,128)(2,1)S(1)}, u32[]{:S(2)}, u32[]{:S(2)}) collective-permute-start(bf16[32,768]{1,0:T(8,128)(2,1)} %refs_0_.1), channel_id=1, source_target_pairs={{0,2},{1,3},{2,0},{3,1},{4,6},{5,7},{6,4},{7,5},{8,10},{9,11},{10,... | collective-permute-start | bytes 147464 | tf_op jit(solution)/shard_map/ppermute | solution.py:77
  3.7 6.7 %collective-permute-start.2 = (bf16[32,768]{1,0:T(8,128)(2,1)}, bf16[32,768]{1,0:T(8,128)(2,1)S(1)}, u32[]{:S(2)}, u32[]{:S(2)}) collective-permute-start(bf16[32,768]{1,0:T(8,128)(2,1)} %refs_0_.1), channel_id=1, source_target_pairs={{0,6},{1,7},{2,4},{3,5},{4,2},{5,3},{6,0},{7,1},{8,14},{9,15},{10,... | collective-permute-start | bytes 147464 | tf_op jit(solution)/shard_map/ppermute | solution.py:77
  6.2 5.7 %collective-permute-start.1 = (bf16[32,768]{1,0:T(8,128)(2,1)}, bf16[32,768]{1,0:T(8,128)(2,1)S(1)}, u32[]{:S(2)}, u32[]{:S(2)}) collective-permute-start(bf16[32,768]{1,0:T(8,128)(2,1)} %refs_0_.1), channel_id=1, source_target_pairs={{0,4},{1,5},{2,6},{3,7},{4,0},{5,1},{6,2},{7,3},{8,12},{9,13},{10,... | collective-permute-start | bytes 147464 | tf_op jit(solution)/shard_map/ppermute | solution.py:77
  7.0 1.4 %copy-start = (bf16[1024,768]{1,0:T(8,128)(2,1)S(1)}, bf16[1024,768]{1,0:T(8,128)(2,1)}, u32[]{:S(2)}) copy-start(bf16[1024,768]{1,0:T(8,128)(2,1)} %refs_1_.1) | copy-start | bytes 4718596
  8.4 0.8 %copy-start.1 = (bf16[32,768]{1,0:T(8,128)(2,1)S(1)}, bf16[32,768]{1,0:T(8,128)(2,1)}, u32[]{:S(2)}) copy-start(bf16[32,768]{1,0:T(8,128)(2,1)} %refs_0_.1) | copy-start | bytes 147460
  12.0 5.7 %collective-permute-start.4 = (bf16[128,768]{1,0:T(8,128)(2,1)S(1)}, bf16[128,768]{1,0:T(8,128)(2,1)S(1)}, u32[]{:S(2)}, u32[]{:S(2)}) collective-permute-start(bf16[128,768]{1,0:T(8,128)(2,1)S(1)} %get-tuple-element.23.refs_0_), channel_id=1, source_target_pairs={{0,1},{1,0},{2,3},{3,2},{4,5},{5,4},{6,7},{7,6},{8,9},{9,8},{10,11... | collective-permute-start | bytes 589832 | tf_op jit(solution)/shard_map/ppermute | solution.py:77
  13.5 13.6 %collective-permute-start.9 = (bf16[144,768]{1,0:T(8,128)(2,1)S(1)}, bf16[144,768]{1,0:T(8,128)(2,1)S(1)}, u32[]{:S(2)}, u32[]{:S(2)}) collective-permute-start(bf16[144,768]{1,0:T(8,128)(2,1)S(1)} %get-tuple-element.35), channel_id=1, source_target_pairs={{0,16},{8,24},{16,0},{24,8},{1,17},{9,25},{17,1},{25,9},{2,18},{10... | collective-permute-start | bytes 663560 | tf_op jit(solution)/shard_map/ppermute | solution.py:77
  16.4 10.3 %collective-permute-start.10 = (bf16[128,768]{1,0:T(8,128)(2,1)S(1)}, bf16[128,768]{1,0:T(8,128)(2,1)S(1)}, u32[]{:S(2)}, u32[]{:S(2)}) collective-permute-start(bf16[128,768]{1,0:T(8,128)(2,1)S(1)} %get-tuple-element.36), channel_id=1, source_target_pairs={{0,17},{1,16},{2,19},{3,18},{4,21},{5,20},{6,23},{7,22},{8,25},{9,... | collective-permute-start | bytes 589832 | tf_op jit(solution)/shard_map/ppermute | solution.py:87
  16.9 4.6 %collective-permute-start.3 = (bf16[64,768]{1,0:T(8,128)(2,1)S(1)}, bf16[64,768]{1,0:T(8,128)(2,1)S(1)}, u32[]{:S(2)}, u32[]{:S(2)}) collective-permute-start(bf16[64,768]{1,0:T(8,128)(2,1)S(1)} %get-tuple-element.25), channel_id=1, source_target_pairs={{0,2},{1,3},{2,0},{3,1},{4,6},{5,7},{6,4},{7,5},{8,10},{9,11},{10,... | collective-permute-start | bytes 294920 | tf_op jit(solution)/shard_map/ppermute | solution.py:77
  19.0 4.7 %collective-permute-start.6 = (bf16[64,768]{1,0:T(8,128)(2,1)S(1)}, bf16[64,768]{1,0:T(8,128)(2,1)S(1)}, u32[]{:S(2)}, u32[]{:S(2)}) collective-permute-start(bf16[64,768]{1,0:T(8,128)(2,1)S(1)} %get-tuple-element.32), channel_id=1, source_target_pairs={{0,2},{1,3},{2,0},{3,1},{4,6},{5,7},{6,4},{7,5},{8,10},{9,11},{10,... | collective-permute-start | bytes 294920 | tf_op jit(solution)/shard_map/ppermute | solution.py:77
  21.6 11.0 %collective-permute-start.5 = (bf16[32,768]{1,0:T(8,128)(2,1)S(1)}, bf16[32,768]{1,0:T(8,128)(2,1)S(1)}, u32[]{:S(2)}, u32[]{:S(2)}) collective-permute-start(bf16[32,768]{1,0:T(8,128)(2,1)S(1)} %get-tuple-element.30), channel_id=1, source_target_pairs={{0,4},{1,5},{2,6},{3,7},{4,0},{5,1},{6,2},{7,3},{8,12},{9,13},{10,... | collective-permute-start | bytes 147464 | tf_op jit(solution)/shard_map/ppermute | solution.py:77
  22.9 6.3 %collective-permute-start.12 = (bf16[400,768]{1,0:T(8,128)(2,1)S(1)}, bf16[400,768]{1,0:T(8,128)(2,1)S(1)}, u32[]{:S(2)}, u32[]{:S(2)}) collective-permute-start(bf16[400,768]{1,0:T(8,128)(2,1)S(1)} %get-tuple-element.37), channel_id=1, source_target_pairs={{0,8},{8,0},{16,24},{24,16},{1,9},{9,1},{17,25},{25,17},{2,10},{10... | collective-permute-start | bytes 1843208 | tf_op jit(solution)/shard_map/ppermute | solution.py:77
  23.7 8.8 %collective-permute-start.8 = (bf16[32,768]{1,0:T(8,128)(2,1)S(1)}, bf16[32,768]{1,0:T(8,128)(2,1)S(1)}, u32[]{:S(2)}, u32[]{:S(2)}) collective-permute-start(bf16[32,768]{1,0:T(8,128)(2,1)S(1)} %get-tuple-element.34), channel_id=1, source_target_pairs={{0,5},{1,4},{2,7},{3,6},{4,1},{5,0},{6,3},{7,2},{8,13},{9,12},{10,... | collective-permute-start | bytes 147464 | tf_op jit(solution)/shard_map/ppermute | solution.py:77
  26.7 5.9 %collective-permute-start.7 = (bf16[32,768]{1,0:T(8,128)(2,1)S(1)}, bf16[32,768]{1,0:T(8,128)(2,1)S(1)}, u32[]{:S(2)}, u32[]{:S(2)}) collective-permute-start(bf16[32,768]{1,0:T(8,128)(2,1)S(1)} %get-tuple-element.33.refs_2_), channel_id=1, source_target_pairs={{0,1},{1,0},{2,3},{3,2},{4,5},{5,4},{6,7},{7,6},{8,9},{9,8},{10,11... | collective-permute-start | bytes 147464 | tf_op jit(solution)/shard_map/ppermute | solution.py:77
  27.2 2.6 %collective-permute-start.11 = (bf16[272,768]{1,0:T(8,128)(2,1)S(1)}, bf16[272,768]{1,0:T(8,128)(2,1)S(1)}, u32[]{:S(2)}, u32[]{:S(2)}) collective-permute-start(bf16[272,768]{1,0:T(8,128)(2,1)S(1)} %shard_map.67.refs_0_), channel_id=1, source_target_pairs={{0,8},{8,0},{16,24},{24,16},{1,9},{9,1},{17,25},{25,17},{2,10},{10... | collective-permute-start | bytes 1253384 | tf_op jit(solution)/shard_map/ppermute | solution.py:77

commit v22 on v21

--- a/solution.py
+++ b/solution.py
@@ -212,15 +212,6 @@
     acc_ref[...] = jnp.dot(wide, rows, preferred_element_type=jnp.float32)
 
 
-def mate_body(set_ref, acc_ref, out_ref):
-    count = set_ref.shape[0] - BLOCK - NOTE
-    slope, chosen = read_slope(set_ref[count:, :count])
-    wide = spread(slope, chosen, range(acc_ref.shape[0] // BLOCK))
-    out_ref[...] = acc_ref[...] + jnp.dot(
-        wide, set_ref[:count, :], preferred_element_type=jnp.float32
-    )
-
-
 def set_slope(set_ref, weights):
     half = (set_ref.shape[0] - NOTE) // 2
     rows = jnp.concatenate([set_ref[:half, :], set_ref[half + NOTE :, :]], axis=0)
@@ -237,9 +228,14 @@
     out_ref[...] = acc_ref[...] + jnp.dot(wide, rows, preferred_element_type=jnp.float32)
 
 
-def late_body(groups, set_ref, weights_ref, acc_ref, out_ref, mark_ref, held, sems):
+def late_body(groups, set_ref, mate_ref, weights_ref, acc_ref, out_ref, mark_ref, held, sems):
     mark_ref[...] = jnp.zeros_like(mark_ref)
     rows, slope, chosen = set_slope(set_ref, weights_ref[...])
+    count = mate_ref.shape[0] - BLOCK - NOTE
+    mate_slope, mate_chosen = read_slope(mate_ref[count:, :count])
+    rows = jnp.concatenate([rows, mate_ref[:count, :]], axis=0)
+    slope = jnp.concatenate([slope, mate_slope], axis=1)
+    chosen = jnp.concatenate([chosen, mate_chosen], axis=1)
     blocks = acc_ref.shape[0] // BLOCK
     chunk = blocks // sems.shape[0]
     copies = []
@@ -255,18 +251,18 @@
         copy.wait()
 
 
-def late(groups, crossed, weights, acc):
+def late(groups, crossed, mate, weights, acc):
     out = like(*weights.shape, weights.dtype)
     chunks = 4
     return pl.pallas_call(
         lambda *refs: late_body(groups, *refs),
         out_shape=[out, like(1, BLOCK, jnp.int32)],
-        in_specs=[pl.BlockSpec(memory_space=pltpu.VMEM)] * 3,
+        in_specs=[pl.BlockSpec(memory_space=pltpu.VMEM)] * 4,
         out_specs=[pl.BlockSpec(memory_space=pl.ANY), pl.BlockSpec(memory_space=pltpu.VMEM)],
         scratch_shapes=[pltpu.VMEM(out.shape, out.dtype), pltpu.SemaphoreType.DMA((chunks,))],
         cost_estimate=pl.CostEstimate(flops=0, bytes_accessed=0, transcendentals=0),
         compiler_params=pltpu.CompilerParams(vmem_limit_bytes=VMEM_LIMIT),
-    )(crossed, weights, acc)
+    )(crossed, mate, weights, acc)
 
 
 def note_body(blocks_dev, q_home, me_ref, choice_ref, note_ref):
@@ -362,8 +358,7 @@
     cross_mate = swap(cross, "pb", 1)
     grown = like(lab_dev, width, f32)
     acc = local_call(cross_body, [grown], [cross, weights, acc], 20 * work)[0]
-    acc = local_call(mate_body, [grown], [mate, acc], work)[0]
-    weight_grad, mark = late(groups, cross_mate, weights, acc)
+    weight_grad, mark = late(groups, cross_mate, mate, weights, acc)
     query_grad = local_call(
         sum_body, [home], [near_kept, near_came, far_came, far_across], 0, [mark]
     )[0]

time: 33.5 us -> 33.4 us (level)
    pallas_call x12 -> x11, Pallas kernels: 6.75 us -> 6.18 us  [local_call(): pl.pallas_call(lambda *refs: body(*refs[:given], *refs[later:]), out_shap...]
    pallas_call x1, Pallas kernels: 2.71 us -> 3.17 us  [late(): pl.pallas_call(lambda *refs: late_body(groups, *refs), out_shape=[out, li...]
where the time goes in v22:
time: 33.4 us; the launch traced here: 33.1 us
  starting transfers between devices  15.7 us (47%)
  Pallas kernels  9.35 us (28%)
  waiting for transfers between devices  4.39 us (13%)
  local copies, waits for them, and re-layouts  2.21 us (7%)
  between operations  0.74 us (2%)
  other arithmetic  0.72 us (2%)
    ppermute x12, starting transfers between devices, swap(): return lax.ppermute(value, axis, [(i, i ^ bit) for i in range(count)])  15.2 us
    pallas_call x11, Pallas kernels, local_call(): pl.pallas_call(lambda *refs: body(*refs[:given], *refs[later:]), out_shap...  6.18 us
    ppermute x12, waiting for transfers between devices, swap(): return lax.ppermute(value, axis, [(i, i ^ bit) for i in range(count)])  4.38 us
    pallas_call x1, Pallas kernels, late(): pl.pallas_call(lambda *refs: late_body(groups, *refs), out_shape=[out, li...  3.17 us
    unnamed x4, local copies, waits for them, and re-layouts  2.21 us
    convert_element_type x1, other arithmetic, dense_shards(): jnp.concatenate([sibling_blocks.T, positive_slot[None]], axis=0).astype(f32)  0.72 us
  transfers between devices with their start and end apart: 13, of which 5 were waited for; matrix products, arithmetic and copies ran while one was open for 2% of the time, Pallas kernels for 26%

profile of v22, /device:TPU:0, one launch (start us, length us, event | category | flops | bytes accessed | tf_op | source)
XLA Modules:
  0.0 33.1 jit_solution(7472571475602720161)
XLA Ops:
  0.6 3.1 %collective-permute-start = (bf16[32,768]{1,0:T(8,128)(2,1)}, bf16[32,768]{1,0:T(8,128)(2,1)S(1)}, u32[]{:S(2)}, u32[]{:S(2)}) collective-permute-start(bf16[32,768]{1,0:T(8,128)(2,1)} %refs_0_.1), channel_id=1, source_target_pairs={{0,2},{1,3},{2,0},{3,1},{4,6},{5,7},{6,4},{7,5},{8,10},{9,11},{10,... | collective-permute-start | bytes 147464 | tf_op jit(solution)/shard_map/ppermute | solution.py:77
  3.7 2.5 %collective-permute-start.2 = (bf16[32,768]{1,0:T(8,128)(2,1)}, bf16[32,768]{1,0:T(8,128)(2,1)S(1)}, u32[]{:S(2)}, u32[]{:S(2)}) collective-permute-start(bf16[32,768]{1,0:T(8,128)(2,1)} %refs_0_.1), channel_id=1, source_target_pairs={{0,6},{1,7},{2,4},{3,5},{4,2},{5,3},{6,0},{7,1},{8,14},{9,15},{10,... | collective-permute-start | bytes 147464 | tf_op jit(solution)/shard_map/ppermute | solution.py:77
  6.3 0.7 %add_convert_fusion.refs_1_ = f32[9,256]{1,0:T(8,128)S(1)} fusion(s32[1,256]{1,0:T(1,128)} %bitcast.4, s32[8,256]{1,0:T(8,128)} %bitcast.3), kind=kLoop, calls=%fused_computation | loop fusion | flops 4608 | bytes 18432 | tf_op jit(solution)/shard_map/convert_element_type | solution.py:310
  7.0 1.4 %copy-done = bf16[1024,768]{1,0:T(8,128)(2,1)S(1)} copy-done((bf16[1024,768]{1,0:T(8,128)(2,1)S(1)}, bf16[1024,768]{1,0:T(8,128)(2,1)}, u32[]{:S(2)}) %copy-start) | copy-done | bytes 1572888
  8.4 0.8 %copy-done.1 = bf16[32,768]{1,0:T(8,128)(2,1)S(1)} copy-done((bf16[32,768]{1,0:T(8,128)(2,1)S(1)}, bf16[32,768]{1,0:T(8,128)(2,1)}, u32[]{:S(2)}) %copy-start.1) | copy-done | bytes 49176
  9.5 0.9 %collective-permute-done.2.refs_3_ = bf16[32,768]{1,0:T(8,128)(2,1)S(1)} collective-permute-done((bf16[32,768]{1,0:T(8,128)(2,1)}, bf16[32,768]{1,0:T(8,128)(2,1)S(1)}, u32[]{:S(2)}, u32[]{:S(2)}) %collective-permute-start.2) | collective-permute-done | bytes 49184 | tf_op jit(solution)/shard_map/ppermute | solution.py:77
  10.4 1.5 %collective-permute-done.1.refs_2_ = bf16[32,768]{1,0:T(8,128)(2,1)S(1)} collective-permute-done((bf16[32,768]{1,0:T(8,128)(2,1)}, bf16[32,768]{1,0:T(8,128)(2,1)S(1)}, u32[]{:S(2)}, u32[]{:S(2)}) %collective-permute-start.1) | collective-permute-done | bytes 49184 | tf_op jit(solution)/shard_map/ppermute | solution.py:77
  12.0 1.6 %collective-permute-start.4 = (bf16[128,768]{1,0:T(8,128)(2,1)S(1)}, bf16[128,768]{1,0:T(8,128)(2,1)S(1)}, u32[]{:S(2)}, u32[]{:S(2)}) collective-permute-start(bf16[128,768]{1,0:T(8,128)(2,1)S(1)} %get-tuple-element.23.refs_0_), channel_id=1, source_target_pairs={{0,1},{1,0},{2,3},{3,2},{4,5},{5,4},{6,7},{7,6},{8,9},{9,8},{10,11... | collective-permute-start | bytes 589832 | tf_op jit(solution)/shard_map/ppermute | solution.py:77
  13.5 1.5 %collective-permute-start.9 = (bf16[144,768]{1,0:T(8,128)(2,1)S(1)}, bf16[144,768]{1,0:T(8,128)(2,1)S(1)}, u32[]{:S(2)}, u32[]{:S(2)}) collective-permute-start(bf16[144,768]{1,0:T(8,128)(2,1)S(1)} %get-tuple-element.35), channel_id=1, source_target_pairs={{0,16},{8,24},{16,0},{24,8},{1,17},{9,25},{17,1},{25,9},{2,18},{10... | collective-permute-start | bytes 663560 | tf_op jit(solution)/shard_map/ppermute | solution.py:77
  15.0 1.3 %shard_map.62 = (f32[64,768]{1,0:T(8,128)S(1)}, bf16[64,768]{1,0:T(8,128)(2,1)S(1)}, bf16[144,128]{1,0:T(8,128)(2,1)S(1)}, bf16[128,768]{1,0:T(8,128)(2,1)S(1)}) custom-call(bf16[128,768]{1,0:T(8,128)(2,1)S(1)} %get-tuple-element.23.refs_0_, bf16[1024,768]{1,0:T(8,128)(2,1)S(1)} %get-tuple-element.22.refs_5_.refs_1_.refs_2_, ...), custom_call_target="tpu_custom_call" | custom-call | flops 402653184 | tf_op jit(solution)/shard_map/pallas_call | solution.py:96
  16.4 0.5 %collective-permute-start.10 = (bf16[128,768]{1,0:T(8,128)(2,1)S(1)}, bf16[128,768]{1,0:T(8,128)(2,1)S(1)}, u32[]{:S(2)}, u32[]{:S(2)}) collective-permute-start(bf16[128,768]{1,0:T(8,128)(2,1)S(1)} %get-tuple-element.36), channel_id=1, source_target_pairs={{0,17},{1,16},{2,19},{3,18},{4,21},{5,20},{6,23},{7,22},{8,25},{9,... | collective-permute-start | bytes 589832 | tf_op jit(solution)/shard_map/ppermute | solution.py:87
  16.9 0.3 collective-permute-start.3
  17.2 0.5 %collective-permute-done.4.refs_0_.refs_1_ = bf16[128,768]{1,0:T(8,128)(2,1)S(1)} collective-permute-done((bf16[128,768]{1,0:T(8,128)(2,1)S(1)}, bf16[128,768]{1,0:T(8,128)(2,1)S(1)}, u32[]{:S(2)}, u32[]{:S(2)}) %collective-permute-start.4) | collective-permute-done | bytes 196640 | tf_op jit(solution)/shard_map/ppermute | solution.py:77
  17.7 1.3 %shard_map.63 = (f32[64,768]{1,0:T(8,128)S(1)}, bf16[64,768]{1,0:T(8,128)(2,1)S(1)}, bf16[144,128]{1,0:T(8,128)(2,1)S(1)}) custom-call(bf16[128,768]{1,0:T(8,128)(2,1)S(1)} %collective-permute-done.4.refs_0_.refs_1_, bf16[1024,768]{1,0:T(8,128)(2,1)S(1)} %get-tuple-element.22.refs_5_.refs_1_.refs_2_, bf16[16,768]{1,0:T(8,128)(2,1)S(1)} %shard_map.60.refs_4_.refs_2_, ...), custom_call_target="tpu_custom_call" | custom-call | flops 402653184 | tf_op jit(solution)/shard_map/pallas_call | solution.py:96
  19.0 1.3 %collective-permute-start.6 = (bf16[64,768]{1,0:T(8,128)(2,1)S(1)}, bf16[64,768]{1,0:T(8,128)(2,1)S(1)}, u32[]{:S(2)}, u32[]{:S(2)}) collective-permute-start(bf16[64,768]{1,0:T(8,128)(2,1)S(1)} %get-tuple-element.32), channel_id=1, source_target_pairs={{0,2},{1,3},{2,0},{3,1},{4,6},{5,7},{6,4},{7,5},{8,10},{9,11},{10,... | collective-permute-start | bytes 294920 | tf_op jit(solution)/shard_map/ppermute | solution.py:77
  20.3 0.6 %shard_map.64 = (f32[1024,768]{1,0:T(8,128)S(1)}, bf16[400,768]{1,0:T(8,128)(2,1)S(1)}) custom-call(bf16[128,768]{1,0:T(8,128)(2,1)S(1)} %get-tuple-element.23.refs_0_, bf16[128,768]{1,0:T(8,128)(2,1)S(1)} %collective-permute-done.4.refs_0_.refs_1_, bf16[144,128]{1,0:T(8,128)(2,1)S(1)} %get-tuple-element.26.refs_3_.refs_2_, ...), custom_call_target="tpu_custom_call" | custom-call | flops 402653184 | tf_op jit(solution)/shard_map/pallas_call | solution.py:96
  20.9 0.6 %collective-permute-done.3.refs_1_ = bf16[64,768]{1,0:T(8,128)(2,1)S(1)} collective-permute-done((bf16[64,768]{1,0:T(8,128)(2,1)S(1)}, bf16[64,768]{1,0:T(8,128)(2,1)S(1)}, u32[]{:S(2)}, u32[]{:S(2)}) %collective-permute-start.3) | collective-permute-done | bytes 98336 | tf_op jit(solution)/shard_map/ppermute | solution.py:77
  21.6 1.3 %collective-permute-start.5 = (bf16[32,768]{1,0:T(8,128)(2,1)S(1)}, bf16[32,768]{1,0:T(8,128)(2,1)S(1)}, u32[]{:S(2)}, u32[]{:S(2)}) collective-permute-start(bf16[32,768]{1,0:T(8,128)(2,1)S(1)} %get-tuple-element.30), channel_id=1, source_target_pairs={{0,4},{1,5},{2,6},{3,7},{4,0},{5,1},{6,2},{7,3},{8,12},{9,13},{10,... | collective-permute-start | bytes 147464 | tf_op jit(solution)/shard_map/ppermute | solution.py:77
  22.9 0.8 %collective-permute-done.6.refs_1_ = bf16[64,768]{1,0:T(8,128)(2,1)S(1)} collective-permute-done((bf16[64,768]{1,0:T(8,128)(2,1)S(1)}, bf16[64,768]{1,0:T(8,128)(2,1)S(1)}, u32[]{:S(2)}, u32[]{:S(2)}) %collective-permute-start.6) | collective-permute-done | bytes 98336 | tf_op jit(solution)/shard_map/ppermute | solution.py:77
  23.7 2.9 %collective-permute-start.8 = (bf16[32,768]{1,0:T(8,128)(2,1)S(1)}, bf16[32,768]{1,0:T(8,128)(2,1)S(1)}, u32[]{:S(2)}, u32[]{:S(2)}) collective-permute-start(bf16[32,768]{1,0:T(8,128)(2,1)S(1)} %get-tuple-element.34), channel_id=1, source_target_pairs={{0,5},{1,4},{2,7},{3,6},{4,1},{5,0},{6,3},{7,2},{8,13},{9,12},{10,... | collective-permute-start | bytes 147464 | tf_op jit(solution)/shard_map/ppermute | solution.py:77
  26.7 0.5 %collective-permute-start.7 = (bf16[32,768]{1,0:T(8,128)(2,1)S(1)}, bf16[32,768]{1,0:T(8,128)(2,1)S(1)}, u32[]{:S(2)}, u32[]{:S(2)}) collective-permute-start(bf16[32,768]{1,0:T(8,128)(2,1)S(1)} %get-tuple-element.33.refs_2_), channel_id=1, source_target_pairs={{0,1},{1,0},{2,3},{3,2},{4,5},{5,4},{6,7},{7,6},{8,9},{9,8},{10,11... | collective-permute-start | bytes 147464 | tf_op jit(solution)/shard_map/ppermute | solution.py:77
  27.3 1.9 %shard_map.68.refs_3_ = f32[1024,768]{1,0:T(8,128)S(1)} custom-call(bf16[272,768]{1,0:T(8,128)(2,1)S(1)} %shard_map.67.refs_0_, bf16[1024,768]{1,0:T(8,128)(2,1)S(1)} %get-tuple-element.22.refs_5_.refs_1_.refs_2_, f32[1024,768]{1,0:T(8,128)S(1)} %get-tuple-element.28.refs_2_.refs_3_), custom_call_target="tpu_custom_call" | custom-call | flops 8053063680 | tf_op jit(solution)/shard_map/pallas_call | solution.py:96
  29.2 3.2 %shard_map.69 = (bf16[1024,768]{1,0:T(8,128)(2,1)}, s32[1,128]{1,0:T(1,128)S(1)}) custom-call(bf16[272,768]{1,0:T(8,128)(2,1)S(1)} %collective-permute-done.11.refs_0_, bf16[400,768]{1,0:T(8,128)(2,1)S(1)} %collective-permute-done.12.refs_1_, bf16[1024,768]{1,0:T(8,128)(2,1)S(1)} %get-tuple-element.22.refs_5_.refs_1_.refs_2_, f32[1024,768]{1,0:T(8,128)S(1)} %shard_map.68.refs_3_), custom_call_target="tpu_custom_call" | custom-call | tf_op jit(solution)/shard_map/pallas_call | solution.py:257
  32.4 0.7 %shard_map.70 = f32[32,768]{1,0:T(8,128)} custom-call(f32[32,768]{1,0:T(8,128)S(1)} %get-tuple-element.29.refs_2_.refs_0_, bf16[32,768]{1,0:T(8,128)(2,1)S(1)} %collective-permute-done.5.refs_1_, bf16[32,768]{1,0:T(8,128)(2,1)S(1)} %collective-permute-done.7.refs_2_, bf16[32,768]{1,0:T(8,128)(2,1)S(1)} %collective-permute-done.8.refs_3_, ...), custom_call_target="tpu_custom_call" | custom-call | tf_op jit(solution)/shard_map/pallas_call | solution.py:96
  (19 shorter events, 0.6 us)
Async XLA Ops:
  0.6 8.9 %collective-permute-start = (bf16[32,768]{1,0:T(8,128)(2,1)}, bf16[32,768]{1,0:T(8,128)(2,1)S(1)}, u32[]{:S(2)}, u32[]{:S(2)}) collective-permute-start(bf16[32,768]{1,0:T(8,128)(2,1)} %refs_0_.1), channel_id=1, source_target_pairs={{0,2},{1,3},{2,0},{3,1},{4,6},{5,7},{6,4},{7,5},{8,10},{9,11},{10,... | collective-permute-start | bytes 147464 | tf_op jit(solution)/shard_map/ppermute | solution.py:77
  3.7 6.7 %collective-permute-start.2 = (bf16[32,768]{1,0:T(8,128)(2,1)}, bf16[32,768]{1,0:T(8,128)(2,1)S(1)}, u32[]{:S(2)}, u32[]{:S(2)}) collective-permute-start(bf16[32,768]{1,0:T(8,128)(2,1)} %refs_0_.1), channel_id=1, source_target_pairs={{0,6},{1,7},{2,4},{3,5},{4,2},{5,3},{6,0},{7,1},{8,14},{9,15},{10,... | collective-permute-start | bytes 147464 | tf_op jit(solution)/shard_map/ppermute | solution.py:77
  6.2 5.7 %collective-permute-start.1 = (bf16[32,768]{1,0:T(8,128)(2,1)}, bf16[32,768]{1,0:T(8,128)(2,1)S(1)}, u32[]{:S(2)}, u32[]{:S(2)}) collective-permute-start(bf16[32,768]{1,0:T(8,128)(2,1)} %refs_0_.1), channel_id=1, source_target_pairs={{0,4},{1,5},{2,6},{3,7},{4,0},{5,1},{6,2},{7,3},{8,12},{9,13},{10,... | collective-permute-start | bytes 147464 | tf_op jit(solution)/shard_map/ppermute | solution.py:77
  7.0 1.4 %copy-start = (bf16[1024,768]{1,0:T(8,128)(2,1)S(1)}, bf16[1024,768]{1,0:T(8,128)(2,1)}, u32[]{:S(2)}) copy-start(bf16[1024,768]{1,0:T(8,128)(2,1)} %refs_1_.1) | copy-start | bytes 4718596
  8.4 0.8 %copy-start.1 = (bf16[32,768]{1,0:T(8,128)(2,1)S(1)}, bf16[32,768]{1,0:T(8,128)(2,1)}, u32[]{:S(2)}) copy-start(bf16[32,768]{1,0:T(8,128)(2,1)} %refs_0_.1) | copy-start | bytes 147460
  12.0 5.7 %collective-permute-start.4 = (bf16[128,768]{1,0:T(8,128)(2,1)S(1)}, bf16[128,768]{1,0:T(8,128)(2,1)S(1)}, u32[]{:S(2)}, u32[]{:S(2)}) collective-permute-start(bf16[128,768]{1,0:T(8,128)(2,1)S(1)} %get-tuple-element.23.refs_0_), channel_id=1, source_target_pairs={{0,1},{1,0},{2,3},{3,2},{4,5},{5,4},{6,7},{7,6},{8,9},{9,8},{10,11... | collective-permute-start | bytes 589832 | tf_op jit(solution)/shard_map/ppermute | solution.py:77
  13.5 13.6 %collective-permute-start.9 = (bf16[144,768]{1,0:T(8,128)(2,1)S(1)}, bf16[144,768]{1,0:T(8,128)(2,1)S(1)}, u32[]{:S(2)}, u32[]{:S(2)}) collective-permute-start(bf16[144,768]{1,0:T(8,128)(2,1)S(1)} %get-tuple-element.35), channel_id=1, source_target_pairs={{0,16},{8,24},{16,0},{24,8},{1,17},{9,25},{17,1},{25,9},{2,18},{10... | collective-permute-start | bytes 663560 | tf_op jit(solution)/shard_map/ppermute | solution.py:77
  16.4 10.3 %collective-permute-start.10 = (bf16[128,768]{1,0:T(8,128)(2,1)S(1)}, bf16[128,768]{1,0:T(8,128)(2,1)S(1)}, u32[]{:S(2)}, u32[]{:S(2)}) collective-permute-start(bf16[128,768]{1,0:T(8,128)(2,1)S(1)} %get-tuple-element.36), channel_id=1, source_target_pairs={{0,17},{1,16},{2,19},{3,18},{4,21},{5,20},{6,23},{7,22},{8,25},{9,... | collective-permute-start | bytes 589832 | tf_op jit(solution)/shard_map/ppermute | solution.py:87
  16.9 4.6 %collective-permute-start.3 = (bf16[64,768]{1,0:T(8,128)(2,1)S(1)}, bf16[64,768]{1,0:T(8,128)(2,1)S(1)}, u32[]{:S(2)}, u32[]{:S(2)}) collective-permute-start(bf16[64,768]{1,0:T(8,128)(2,1)S(1)} %get-tuple-element.25), channel_id=1, source_target_pairs={{0,2},{1,3},{2,0},{3,1},{4,6},{5,7},{6,4},{7,5},{8,10},{9,11},{10,... | collective-permute-start | bytes 294920 | tf_op jit(solution)/shard_map/ppermute | solution.py:77
  19.0 4.7 %collective-permute-start.6 = (bf16[64,768]{1,0:T(8,128)(2,1)S(1)}, bf16[64,768]{1,0:T(8,128)(2,1)S(1)}, u32[]{:S(2)}, u32[]{:S(2)}) collective-permute-start(bf16[64,768]{1,0:T(8,128)(2,1)S(1)} %get-tuple-element.32), channel_id=1, source_target_pairs={{0,2},{1,3},{2,0},{3,1},{4,6},{5,7},{6,4},{7,5},{8,10},{9,11},{10,... | collective-permute-start | bytes 294920 | tf_op jit(solution)/shard_map/ppermute | solution.py:77
  21.6 10.8 %collective-permute-start.5 = (bf16[32,768]{1,0:T(8,128)(2,1)S(1)}, bf16[32,768]{1,0:T(8,128)(2,1)S(1)}, u32[]{:S(2)}, u32[]{:S(2)}) collective-permute-start(bf16[32,768]{1,0:T(8,128)(2,1)S(1)} %get-tuple-element.30), channel_id=1, source_target_pairs={{0,4},{1,5},{2,6},{3,7},{4,0},{5,1},{6,2},{7,3},{8,12},{9,13},{10,... | collective-permute-start | bytes 147464 | tf_op jit(solution)/shard_map/ppermute | solution.py:77
  22.9 6.3 %collective-permute-start.12 = (bf16[400,768]{1,0:T(8,128)(2,1)S(1)}, bf16[400,768]{1,0:T(8,128)(2,1)S(1)}, u32[]{:S(2)}, u32[]{:S(2)}) collective-permute-start(bf16[400,768]{1,0:T(8,128)(2,1)S(1)} %get-tuple-element.37), channel_id=1, source_target_pairs={{0,8},{8,0},{16,24},{24,16},{1,9},{9,1},{17,25},{25,17},{2,10},{10... | collective-permute-start | bytes 1843208 | tf_op jit(solution)/shard_map/ppermute | solution.py:77
  23.7 8.7 %collective-permute-start.8 = (bf16[32,768]{1,0:T(8,128)(2,1)S(1)}, bf16[32,768]{1,0:T(8,128)(2,1)S(1)}, u32[]{:S(2)}, u32[]{:S(2)}) collective-permute-start(bf16[32,768]{1,0:T(8,128)(2,1)S(1)} %get-tuple-element.34), channel_id=1, source_target_pairs={{0,5},{1,4},{2,7},{3,6},{4,1},{5,0},{6,3},{7,2},{8,13},{9,12},{10,... | collective-permute-start | bytes 147464 | tf_op jit(solution)/shard_map/ppermute | solution.py:77
  26.7 5.8 %collective-permute-start.7 = (bf16[32,768]{1,0:T(8,128)(2,1)S(1)}, bf16[32,768]{1,0:T(8,128)(2,1)S(1)}, u32[]{:S(2)}, u32[]{:S(2)}) collective-permute-start(bf16[32,768]{1,0:T(8,128)(2,1)S(1)} %get-tuple-element.33.refs_2_), channel_id=1, source_target_pairs={{0,1},{1,0},{2,3},{3,2},{4,5},{5,4},{6,7},{7,6},{8,9},{9,8},{10,11... | collective-permute-start | bytes 147464 | tf_op jit(solution)/shard_map/ppermute | solution.py:77
  27.2 2.0 %collective-permute-start.11 = (bf16[272,768]{1,0:T(8,128)(2,1)S(1)}, bf16[272,768]{1,0:T(8,128)(2,1)S(1)}, u32[]{:S(2)}, u32[]{:S(2)}) collective-permute-start(bf16[272,768]{1,0:T(8,128)(2,1)S(1)} %shard_map.67.refs_0_), channel_id=1, source_target_pairs={{0,8},{8,0},{16,24},{24,16},{1,9},{9,1},{17,25},{25,17},{2,10},{10... | collective-permute-start | bytes 1253384 | tf_op jit(solution)/shard_map/ppermute | solution.py:77

commit v23 on v22

--- a/solution.py
+++ b/solution.py
@@ -181,14 +181,6 @@
     second_ref[...] = terms[span:].astype(second_ref.dtype)
 
 
-def sum_body(kept_ref, *refs):
-    *term_refs, out_ref = refs
-    total = kept_ref[...]
-    for ref in term_refs:
-        total = total + ref[...].astype(jnp.float32)
-    out_ref[...] = total.astype(out_ref.dtype)
-
-
 def stack_body(*refs):
     *came_refs, out_ref = refs
     start = 0
@@ -228,22 +220,36 @@
     out_ref[...] = acc_ref[...] + jnp.dot(wide, rows, preferred_element_type=jnp.float32)
 
 
-def late_body(groups, set_ref, mate_ref, weights_ref, acc_ref, out_ref, mark_ref, held, sems):
-    mark_ref[...] = jnp.zeros_like(mark_ref)
-    rows, slope, chosen = set_slope(set_ref, weights_ref[...])
+def cross_slope_body(set_ref, weights_ref, slope_ref):
+    _, slope, chosen = set_slope(set_ref, weights_ref[...])
+    slope_ref[:BLOCK, :] = slope
+    slope_ref[BLOCK:, :] = jnp.broadcast_to(chosen, (NOTE, chosen.shape[1])).astype(slope.dtype)
+
+
+def late_body(
+    groups, set_ref, slope_ref, mate_ref, acc_ref, kept_ref, *refs
+):
+    *term_refs, out_ref, home_ref, held, total, sems, home_sem = refs
+    gathered = kept_ref[...]
+    for ref in term_refs:
+        gathered = gathered + ref[...].astype(jnp.float32)
+    total[...] = gathered
+    copies = [pltpu.make_async_copy(total, home_ref, home_sem)]
+    copies[0].start()
+    half = (set_ref.shape[0] - NOTE) // 2
     count = mate_ref.shape[0] - BLOCK - NOTE
-    mate_slope, mate_chosen = read_slope(mate_ref[count:, :count])
-    rows = jnp.concatenate([rows, mate_ref[:count, :]], axis=0)
-    slope = jnp.concatenate([slope, mate_slope], axis=1)
-    chosen = jnp.concatenate([chosen, mate_chosen], axis=1)
+    rows = jnp.concatenate(
+        [set_ref[:half, :], set_ref[half + NOTE :, :], mate_ref[:count, :]], axis=0
+    )
+    slope = jnp.concatenate([slope_ref[...], mate_ref[count:, :count]], axis=1)
+    slope, chosen = read_slope(slope)
     blocks = acc_ref.shape[0] // BLOCK
     chunk = blocks // sems.shape[0]
-    copies = []
     for part in range(sems.shape[0]):
         here = pl.ds(part * chunk * BLOCK, chunk * BLOCK)
         wide = spread(slope, chosen, range(part * chunk, (part + 1) * chunk))
-        total = acc_ref[here, :] + jnp.dot(wide, rows, preferred_element_type=jnp.float32)
-        held[here, :] = (total / groups).astype(held.dtype)
+        sums = acc_ref[here, :] + jnp.dot(wide, rows, preferred_element_type=jnp.float32)
+        held[here, :] = (sums / groups).astype(held.dtype)
         copy = pltpu.make_async_copy(held.at[here, :], out_ref.at[here, :], sems.at[part])
         copy.start()
         copies.append(copy)
@@ -251,18 +257,24 @@
         copy.wait()
 
 
-def late(groups, crossed, mate, weights, acc):
-    out = like(*weights.shape, weights.dtype)
+def late(groups, crossed, slope, mate, acc, kept, terms):
+    out = like(*acc.shape, crossed.dtype)
+    args = [crossed, slope, mate, acc, kept, *terms]
     chunks = 4
     return pl.pallas_call(
         lambda *refs: late_body(groups, *refs),
-        out_shape=[out, like(1, BLOCK, jnp.int32)],
-        in_specs=[pl.BlockSpec(memory_space=pltpu.VMEM)] * 4,
-        out_specs=[pl.BlockSpec(memory_space=pl.ANY), pl.BlockSpec(memory_space=pltpu.VMEM)],
-        scratch_shapes=[pltpu.VMEM(out.shape, out.dtype), pltpu.SemaphoreType.DMA((chunks,))],
+        out_shape=[out, like(*kept.shape, kept.dtype)],
+        in_specs=[pl.BlockSpec(memory_space=pltpu.VMEM)] * len(args),
+        out_specs=[pl.BlockSpec(memory_space=pl.ANY)] * 2,
+        scratch_shapes=[
+            pltpu.VMEM(out.shape, out.dtype),
+            pltpu.VMEM(kept.shape, kept.dtype),
+            pltpu.SemaphoreType.DMA((chunks,)),
+            pltpu.SemaphoreType.DMA,
+        ],
         cost_estimate=pl.CostEstimate(flops=0, bytes_accessed=0, transcendentals=0),
         compiler_params=pltpu.CompilerParams(vmem_limit_bytes=VMEM_LIMIT),
-    )(crossed, mate, weights, acc)
+    )(*args)
 
 
 def note_body(blocks_dev, q_home, me_ref, choice_ref, note_ref):
@@ -358,10 +370,16 @@
     cross_mate = swap(cross, "pb", 1)
     grown = like(lab_dev, width, f32)
     acc = local_call(cross_body, [grown], [cross, weights, acc], 20 * work)[0]
-    weight_grad, mark = late(groups, cross_mate, mate, weights, acc)
-    query_grad = local_call(
-        sum_body, [home], [near_kept, near_came, far_came, far_across], 0, [mark]
+    slope = local_call(
+        cross_slope_body,
+        [like(BLOCK + NOTE, qcount, bf16)],
+        [cross_mate, weights],
+        2 * work,
+        [acc],
     )[0]
+    weight_grad, query_grad = late(
+        groups, cross_mate, slope, mate, acc, near_kept, [near_came, far_came, far_across]
+    )
     return (query_grad, weight_grad)
 
 

time: 33.4 us -> 32.9 us (0.985)
  Pallas kernels: 9.35 us -> 8.01 us
  waiting for transfers between devices: 4.39 us -> 5.28 us
    pallas_call x1, Pallas kernels: 3.17 us -> 1.87 us  [late(): pl.pallas_call(lambda *refs: late_body(groups, *refs), out_shape=[out, li...]
    ppermute x12, waiting for transfers between devices: 4.38 us -> 5.28 us  [swap(): return lax.ppermute(value, axis, [(i, i ^ bit) for i in range(count)])]
  transfers between devices with their start and end apart: 13 -> 13, of which waited for: 5 -> 6; matrix products, arithmetic and copies ran while one was open for 2% -> 2% of each run, Pallas kernels for 26% -> 19%
where the time goes in v23:
time: 32.9 us; the launch traced here: 32.6 us
  starting transfers between devices  15.7 us (48%)
  Pallas kernels  8.01 us (24%)
  waiting for transfers between devices  5.28 us (16%)
  local copies, waits for them, and re-layouts  2.21 us (7%)
  other arithmetic  0.72 us (2%)
  between operations  0.72 us (2%)
    ppermute x12, starting transfers between devices, swap(): return lax.ppermute(value, axis, [(i, i ^ bit) for i in range(count)])  15.2 us
    pallas_call x11, Pallas kernels, local_call(): pl.pallas_call(lambda *refs: body(*refs[:given], *refs[later:]), out_shap...  6.14 us
    ppermute x12, waiting for transfers between devices, swap(): return lax.ppermute(value, axis, [(i, i ^ bit) for i in range(count)])  5.28 us
    unnamed x4, local copies, waits for them, and re-layouts  2.21 us
    pallas_call x1, Pallas kernels, late(): pl.pallas_call(lambda *refs: late_body(groups, *refs), out_shape=[out, li...  1.87 us
    convert_element_type x1, other arithmetic, dense_shards(): jnp.concatenate([sibling_blocks.T, positive_slot[None]], axis=0).astype(f32)  0.72 us
  transfers between devices with their start and end apart: 13, of which 6 were waited for; matrix products, arithmetic and copies ran while one was open for 2% of the time, Pallas kernels for 19%

profile of v23, /device:TPU:0, one launch (start us, length us, event | category | flops | bytes accessed | tf_op | source)
XLA Modules:
  0.0 32.6 jit_solution(18329513721331639484)
XLA Ops:
  0.6 3.1 %collective-permute-start = (bf16[32,768]{1,0:T(8,128)(2,1)}, bf16[32,768]{1,0:T(8,128)(2,1)S(1)}, u32[]{:S(2)}, u32[]{:S(2)}) collective-permute-start(bf16[32,768]{1,0:T(8,128)(2,1)} %refs_0_.1), channel_id=1, source_target_pairs={{0,2},{1,3},{2,0},{3,1},{4,6},{5,7},{6,4},{7,5},{8,10},{9,11},{10,... | collective-permute-start | bytes 147464 | tf_op jit(solution)/shard_map/ppermute | solution.py:77
  3.7 2.5 %collective-permute-start.2 = (bf16[32,768]{1,0:T(8,128)(2,1)}, bf16[32,768]{1,0:T(8,128)(2,1)S(1)}, u32[]{:S(2)}, u32[]{:S(2)}) collective-permute-start(bf16[32,768]{1,0:T(8,128)(2,1)} %refs_0_.1), channel_id=1, source_target_pairs={{0,6},{1,7},{2,4},{3,5},{4,2},{5,3},{6,0},{7,1},{8,14},{9,15},{10,... | collective-permute-start | bytes 147464 | tf_op jit(solution)/shard_map/ppermute | solution.py:77
  6.3 0.7 %add_convert_fusion.refs_1_ = f32[9,256]{1,0:T(8,128)S(1)} fusion(s32[1,256]{1,0:T(1,128)} %bitcast.4, s32[8,256]{1,0:T(8,128)} %bitcast.3), kind=kLoop, calls=%fused_computation | loop fusion | flops 4608 | bytes 18432 | tf_op jit(solution)/shard_map/convert_element_type | solution.py:322
  7.0 1.4 %copy-done = bf16[1024,768]{1,0:T(8,128)(2,1)S(1)} copy-done((bf16[1024,768]{1,0:T(8,128)(2,1)S(1)}, bf16[1024,768]{1,0:T(8,128)(2,1)}, u32[]{:S(2)}) %copy-start) | copy-done | bytes 1572888
  8.4 0.8 %copy-done.1 = bf16[32,768]{1,0:T(8,128)(2,1)S(1)} copy-done((bf16[32,768]{1,0:T(8,128)(2,1)S(1)}, bf16[32,768]{1,0:T(8,128)(2,1)}, u32[]{:S(2)}) %copy-start.1) | copy-done | bytes 49176
  9.5 0.9 %collective-permute-done.2.refs_3_ = bf16[32,768]{1,0:T(8,128)(2,1)S(1)} collective-permute-done((bf16[32,768]{1,0:T(8,128)(2,1)}, bf16[32,768]{1,0:T(8,128)(2,1)S(1)}, u32[]{:S(2)}, u32[]{:S(2)}) %collective-permute-start.2) | collective-permute-done | bytes 49184 | tf_op jit(solution)/shard_map/ppermute | solution.py:77
  10.4 1.5 %collective-permute-done.1.refs_2_ = bf16[32,768]{1,0:T(8,128)(2,1)S(1)} collective-permute-done((bf16[32,768]{1,0:T(8,128)(2,1)}, bf16[32,768]{1,0:T(8,128)(2,1)S(1)}, u32[]{:S(2)}, u32[]{:S(2)}) %collective-permute-start.1) | collective-permute-done | bytes 49184 | tf_op jit(solution)/shard_map/ppermute | solution.py:77
  12.0 1.6 %collective-permute-start.5 = (bf16[128,768]{1,0:T(8,128)(2,1)S(1)}, bf16[128,768]{1,0:T(8,128)(2,1)S(1)}, u32[]{:S(2)}, u32[]{:S(2)}) collective-permute-start(bf16[128,768]{1,0:T(8,128)(2,1)S(1)} %get-tuple-element.24.refs_0_), channel_id=1, source_target_pairs={{0,1},{1,0},{2,3},{3,2},{4,5},{5,4},{6,7},{7,6},{8,9},{9,8},{10,11... | collective-permute-start | bytes 589832 | tf_op jit(solution)/shard_map/ppermute | solution.py:77
  13.5 1.5 %collective-permute-start.3 = (bf16[144,768]{1,0:T(8,128)(2,1)S(1)}, bf16[144,768]{1,0:T(8,128)(2,1)S(1)}, u32[]{:S(2)}, u32[]{:S(2)}) collective-permute-start(bf16[144,768]{1,0:T(8,128)(2,1)S(1)} %get-tuple-element.23), channel_id=1, source_target_pairs={{0,16},{8,24},{16,0},{24,8},{1,17},{9,25},{17,1},{25,9},{2,18},{10... | collective-permute-start | bytes 663560 | tf_op jit(solution)/shard_map/ppermute | solution.py:77
  15.0 1.3 %shard_map.62 = (f32[64,768]{1,0:T(8,128)S(1)}, bf16[64,768]{1,0:T(8,128)(2,1)S(1)}, bf16[144,128]{1,0:T(8,128)(2,1)S(1)}, bf16[128,768]{1,0:T(8,128)(2,1)S(1)}) custom-call(bf16[128,768]{1,0:T(8,128)(2,1)S(1)} %get-tuple-element.24.refs_0_, bf16[1024,768]{1,0:T(8,128)(2,1)S(1)} %get-tuple-element.22.refs_5_.refs_1_, ...), custom_call_target="tpu_custom_call" | custom-call | flops 402653184 | tf_op jit(solution)/shard_map/pallas_call | solution.py:96
  16.4 0.5 %collective-permute-start.4 = (bf16[128,768]{1,0:T(8,128)(2,1)S(1)}, bf16[128,768]{1,0:T(8,128)(2,1)S(1)}, u32[]{:S(2)}, u32[]{:S(2)}) collective-permute-start(bf16[128,768]{1,0:T(8,128)(2,1)S(1)} %get-tuple-element.25), channel_id=1, source_target_pairs={{0,17},{1,16},{2,19},{3,18},{4,21},{5,20},{6,23},{7,22},{8,25},{9,... | collective-permute-start | bytes 589832 | tf_op jit(solution)/shard_map/ppermute | solution.py:87
  17.2 0.5 %collective-permute-done.5.refs_0_.refs_1_ = bf16[128,768]{1,0:T(8,128)(2,1)S(1)} collective-permute-done((bf16[128,768]{1,0:T(8,128)(2,1)S(1)}, bf16[128,768]{1,0:T(8,128)(2,1)S(1)}, u32[]{:S(2)}, u32[]{:S(2)}) %collective-permute-start.5) | collective-permute-done | bytes 196640 | tf_op jit(solution)/shard_map/ppermute | solution.py:77
  17.7 1.3 %shard_map.63 = (f32[64,768]{1,0:T(8,128)S(1)}, bf16[64,768]{1,0:T(8,128)(2,1)S(1)}, bf16[144,128]{1,0:T(8,128)(2,1)S(1)}) custom-call(bf16[128,768]{1,0:T(8,128)(2,1)S(1)} %collective-permute-done.5.refs_0_.refs_1_, bf16[1024,768]{1,0:T(8,128)(2,1)S(1)} %get-tuple-element.22.refs_5_.refs_1_, bf16[16,768]{1,0:T(8,128)(2,1)S(1)} %shard_map.60.refs_4_.refs_2_, ...), custom_call_target="tpu_custom_call" | custom-call | flops 402653184 | tf_op jit(solution)/shard_map/pallas_call | solution.py:96
  19.0 1.3 %collective-permute-start.6 = (bf16[64,768]{1,0:T(8,128)(2,1)S(1)}, bf16[64,768]{1,0:T(8,128)(2,1)S(1)}, u32[]{:S(2)}, u32[]{:S(2)}) collective-permute-start(bf16[64,768]{1,0:T(8,128)(2,1)S(1)} %get-tuple-element.28), channel_id=1, source_target_pairs={{0,2},{1,3},{2,0},{3,1},{4,6},{5,7},{6,4},{7,5},{8,10},{9,11},{10,... | collective-permute-start | bytes 294920 | tf_op jit(solution)/shard_map/ppermute | solution.py:77
  20.3 0.6 %shard_map.64 = (f32[1024,768]{1,0:T(8,128)S(1)}, bf16[400,768]{1,0:T(8,128)(2,1)S(1)}) custom-call(bf16[128,768]{1,0:T(8,128)(2,1)S(1)} %get-tuple-element.24.refs_0_, bf16[128,768]{1,0:T(8,128)(2,1)S(1)} %collective-permute-done.5.refs_0_.refs_1_, bf16[144,128]{1,0:T(8,128)(2,1)S(1)} %get-tuple-element.26.refs_3_.refs_2_, ...), custom_call_target="tpu_custom_call" | custom-call | flops 402653184 | tf_op jit(solution)/shard_map/pallas_call | solution.py:96
  20.9 0.6 %collective-permute-done.7.refs_1_ = bf16[64,768]{1,0:T(8,128)(2,1)S(1)} collective-permute-done((bf16[64,768]{1,0:T(8,128)(2,1)S(1)}, bf16[64,768]{1,0:T(8,128)(2,1)S(1)}, u32[]{:S(2)}, u32[]{:S(2)}) %collective-permute-start.7) | collective-permute-done | bytes 98336 | tf_op jit(solution)/shard_map/ppermute | solution.py:77
  21.6 1.3 %collective-permute-start.10 = (bf16[32,768]{1,0:T(8,128)(2,1)S(1)}, bf16[32,768]{1,0:T(8,128)(2,1)S(1)}, u32[]{:S(2)}, u32[]{:S(2)}) collective-permute-start(bf16[32,768]{1,0:T(8,128)(2,1)S(1)} %get-tuple-element.36), channel_id=1, source_target_pairs={{0,4},{1,5},{2,6},{3,7},{4,0},{5,1},{6,2},{7,3},{8,12},{9,13},{10,... | collective-permute-start | bytes 147464 | tf_op jit(solution)/shard_map/ppermute | solution.py:77
  22.9 0.8 %collective-permute-done.6.refs_1_ = bf16[64,768]{1,0:T(8,128)(2,1)S(1)} collective-permute-done((bf16[64,768]{1,0:T(8,128)(2,1)S(1)}, bf16[64,768]{1,0:T(8,128)(2,1)S(1)}, u32[]{:S(2)}, u32[]{:S(2)}) %collective-permute-start.6) | collective-permute-done | bytes 98336 | tf_op jit(solution)/shard_map/ppermute | solution.py:77
  23.7 2.9 %collective-permute-start.12 = (bf16[32,768]{1,0:T(8,128)(2,1)S(1)}, bf16[32,768]{1,0:T(8,128)(2,1)S(1)}, u32[]{:S(2)}, u32[]{:S(2)}) collective-permute-start(bf16[32,768]{1,0:T(8,128)(2,1)S(1)} %get-tuple-element.37), channel_id=1, source_target_pairs={{0,5},{1,4},{2,7},{3,6},{4,1},{5,0},{6,3},{7,2},{8,13},{9,12},{10,... | collective-permute-start | bytes 147464 | tf_op jit(solution)/shard_map/ppermute | solution.py:77
  26.7 0.5 %collective-permute-start.11 = (bf16[32,768]{1,0:T(8,128)(2,1)S(1)}, bf16[32,768]{1,0:T(8,128)(2,1)S(1)}, u32[]{:S(2)}, u32[]{:S(2)}) collective-permute-start(bf16[32,768]{1,0:T(8,128)(2,1)S(1)} %get-tuple-element.34.refs_2_), channel_id=1, source_target_pairs={{0,1},{1,0},{2,3},{3,2},{4,5},{5,4},{6,7},{7,6},{8,9},{9,8},{10,11... | collective-permute-start | bytes 147464 | tf_op jit(solution)/shard_map/ppermute | solution.py:77
  27.3 1.9 %shard_map.68.refs_2_.refs_3_ = f32[1024,768]{1,0:T(8,128)S(1)} custom-call(bf16[272,768]{1,0:T(8,128)(2,1)S(1)} %shard_map.67.refs_0_, bf16[1024,768]{1,0:T(8,128)(2,1)S(1)} %get-tuple-element.22.refs_5_.refs_1_, f32[1024,768]{1,0:T(8,128)S(1)} %get-tuple-element.32.refs_2_.refs_3_), custom_call_target="tpu_custom_call" | custom-call | flops 8053063680 | tf_op jit(solution)/shard_map/pallas_call | solution.py:96
  29.2 0.6 %shard_map.69.refs_1_ = bf16[144,256]{1,0:T(8,128)(2,1)S(1)} custom-call(bf16[272,768]{1,0:T(8,128)(2,1)S(1)} %collective-permute-done.8.refs_0_, bf16[1024,768]{1,0:T(8,128)(2,1)S(1)} %get-tuple-element.22.refs_5_.refs_1_, f32[1024,768]{1,0:T(8,128)S(1)} %shard_map.68.refs_2_.refs_3_), custom_call_target="tpu_custom_call" | custom-call | flops 805306368 | tf_op jit(solution)/shard_map/pallas_call | solution.py:96
  29.9 0.9 %collective-permute-done.11.refs_6_ = bf16[32,768]{1,0:T(8,128)(2,1)S(1)} collective-permute-done((bf16[32,768]{1,0:T(8,128)(2,1)S(1)}, bf16[32,768]{1,0:T(8,128)(2,1)S(1)}, u32[]{:S(2)}, u32[]{:S(2)}) %collective-permute-start.11) | collective-permute-done | bytes 49184 | tf_op jit(solution)/shard_map/ppermute | solution.py:77
  30.8 1.9 %shard_map.70 = (bf16[1024,768]{1,0:T(8,128)(2,1)}, f32[32,768]{1,0:T(8,128)}) custom-call(bf16[272,768]{1,0:T(8,128)(2,1)S(1)} %collective-permute-done.8.refs_0_, bf16[144,256]{1,0:T(8,128)(2,1)S(1)} %shard_map.69.refs_1_, bf16[400,768]{1,0:T(8,128)(2,1)S(1)} %collective-permute-done.9.refs_2_, f32[1024,768]{1,0:T(8,128)S(1)} %shard_map.68.refs_2_.refs_3_, ...), custom_call_target="tpu_custom_call" | custom-call | tf_op jit(solution)/shard_map/pallas_call | solution.py:264
  (19 shorter events, 0.8 us)
Async XLA Ops:
  0.6 8.9 %collective-permute-start = (bf16[32,768]{1,0:T(8,128)(2,1)}, bf16[32,768]{1,0:T(8,128)(2,1)S(1)}, u32[]{:S(2)}, u32[]{:S(2)}) collective-permute-start(bf16[32,768]{1,0:T(8,128)(2,1)} %refs_0_.1), channel_id=1, source_target_pairs={{0,2},{1,3},{2,0},{3,1},{4,6},{5,7},{6,4},{7,5},{8,10},{9,11},{10,... | collective-permute-start | bytes 147464 | tf_op jit(solution)/shard_map/ppermute | solution.py:77
  3.7 6.7 %collective-permute-start.2 = (bf16[32,768]{1,0:T(8,128)(2,1)}, bf16[32,768]{1,0:T(8,128)(2,1)S(1)}, u32[]{:S(2)}, u32[]{:S(2)}) collective-permute-start(bf16[32,768]{1,0:T(8,128)(2,1)} %refs_0_.1), channel_id=1, source_target_pairs={{0,6},{1,7},{2,4},{3,5},{4,2},{5,3},{6,0},{7,1},{8,14},{9,15},{10,... | collective-permute-start | bytes 147464 | tf_op jit(solution)/shard_map/ppermute | solution.py:77
  6.2 5.7 %collective-permute-start.1 = (bf16[32,768]{1,0:T(8,128)(2,1)}, bf16[32,768]{1,0:T(8,128)(2,1)S(1)}, u32[]{:S(2)}, u32[]{:S(2)}) collective-permute-start(bf16[32,768]{1,0:T(8,128)(2,1)} %refs_0_.1), channel_id=1, source_target_pairs={{0,4},{1,5},{2,6},{3,7},{4,0},{5,1},{6,2},{7,3},{8,12},{9,13},{10,... | collective-permute-start | bytes 147464 | tf_op jit(solution)/shard_map/ppermute | solution.py:77
  7.0 1.4 %copy-start = (bf16[1024,768]{1,0:T(8,128)(2,1)S(1)}, bf16[1024,768]{1,0:T(8,128)(2,1)}, u32[]{:S(2)}) copy-start(bf16[1024,768]{1,0:T(8,128)(2,1)} %refs_1_.1) | copy-start | bytes 4718596
  8.4 0.8 %copy-start.1 = (bf16[32,768]{1,0:T(8,128)(2,1)S(1)}, bf16[32,768]{1,0:T(8,128)(2,1)}, u32[]{:S(2)}) copy-start(bf16[32,768]{1,0:T(8,128)(2,1)} %refs_0_.1) | copy-start | bytes 147460
  12.0 5.7 %collective-permute-start.5 = (bf16[128,768]{1,0:T(8,128)(2,1)S(1)}, bf16[128,768]{1,0:T(8,128)(2,1)S(1)}, u32[]{:S(2)}, u32[]{:S(2)}) collective-permute-start(bf16[128,768]{1,0:T(8,128)(2,1)S(1)} %get-tuple-element.24.refs_0_), channel_id=1, source_target_pairs={{0,1},{1,0},{2,3},{3,2},{4,5},{5,4},{6,7},{7,6},{8,9},{9,8},{10,11... | collective-permute-start | bytes 589832 | tf_op jit(solution)/shard_map/ppermute | solution.py:77
  13.5 13.6 %collective-permute-start.3 = (bf16[144,768]{1,0:T(8,128)(2,1)S(1)}, bf16[144,768]{1,0:T(8,128)(2,1)S(1)}, u32[]{:S(2)}, u32[]{:S(2)}) collective-permute-start(bf16[144,768]{1,0:T(8,128)(2,1)S(1)} %get-tuple-element.23), channel_id=1, source_target_pairs={{0,16},{8,24},{16,0},{24,8},{1,17},{9,25},{17,1},{25,9},{2,18},{10... | collective-permute-start | bytes 663560 | tf_op jit(solution)/shard_map/ppermute | solution.py:77
  16.4 10.3 %collective-permute-start.4 = (bf16[128,768]{1,0:T(8,128)(2,1)S(1)}, bf16[128,768]{1,0:T(8,128)(2,1)S(1)}, u32[]{:S(2)}, u32[]{:S(2)}) collective-permute-start(bf16[128,768]{1,0:T(8,128)(2,1)S(1)} %get-tuple-element.25), channel_id=1, source_target_pairs={{0,17},{1,16},{2,19},{3,18},{4,21},{5,20},{6,23},{7,22},{8,25},{9,... | collective-permute-start | bytes 589832 | tf_op jit(solution)/shard_map/ppermute | solution.py:87
  16.9 4.6 %collective-permute-start.7 = (bf16[64,768]{1,0:T(8,128)(2,1)S(1)}, bf16[64,768]{1,0:T(8,128)(2,1)S(1)}, u32[]{:S(2)}, u32[]{:S(2)}) collective-permute-start(bf16[64,768]{1,0:T(8,128)(2,1)S(1)} %get-tuple-element.30), channel_id=1, source_target_pairs={{0,2},{1,3},{2,0},{3,1},{4,6},{5,7},{6,4},{7,5},{8,10},{9,11},{10,... | collective-permute-start | bytes 294920 | tf_op jit(solution)/shard_map/ppermute | solution.py:77
  19.0 4.7 %collective-permute-start.6 = (bf16[64,768]{1,0:T(8,128)(2,1)S(1)}, bf16[64,768]{1,0:T(8,128)(2,1)S(1)}, u32[]{:S(2)}, u32[]{:S(2)}) collective-permute-start(bf16[64,768]{1,0:T(8,128)(2,1)S(1)} %get-tuple-element.28), channel_id=1, source_target_pairs={{0,2},{1,3},{2,0},{3,1},{4,6},{5,7},{6,4},{7,5},{8,10},{9,11},{10,... | collective-permute-start | bytes 294920 | tf_op jit(solution)/shard_map/ppermute | solution.py:77
  21.6 8.3 %collective-permute-start.10 = (bf16[32,768]{1,0:T(8,128)(2,1)S(1)}, bf16[32,768]{1,0:T(8,128)(2,1)S(1)}, u32[]{:S(2)}, u32[]{:S(2)}) collective-permute-start(bf16[32,768]{1,0:T(8,128)(2,1)S(1)} %get-tuple-element.36), channel_id=1, source_target_pairs={{0,4},{1,5},{2,6},{3,7},{4,0},{5,1},{6,2},{7,3},{8,12},{9,13},{10,... | collective-permute-start | bytes 147464 | tf_op jit(solution)/shard_map/ppermute | solution.py:77
  22.9 7.9 %collective-permute-start.9 = (bf16[400,768]{1,0:T(8,128)(2,1)S(1)}, bf16[400,768]{1,0:T(8,128)(2,1)S(1)}, u32[]{:S(2)}, u32[]{:S(2)}) collective-permute-start(bf16[400,768]{1,0:T(8,128)(2,1)S(1)} %get-tuple-element.35), channel_id=1, source_target_pairs={{0,8},{8,0},{16,24},{24,16},{1,9},{9,1},{17,25},{25,17},{2,10},{10... | collective-permute-start | bytes 1843208 | tf_op jit(solution)/shard_map/ppermute | solution.py:77
  23.7 6.1 %collective-permute-start.12 = (bf16[32,768]{1,0:T(8,128)(2,1)S(1)}, bf16[32,768]{1,0:T(8,128)(2,1)S(1)}, u32[]{:S(2)}, u32[]{:S(2)}) collective-permute-start(bf16[32,768]{1,0:T(8,128)(2,1)S(1)} %get-tuple-element.37), channel_id=1, source_target_pairs={{0,5},{1,4},{2,7},{3,6},{4,1},{5,0},{6,3},{7,2},{8,13},{9,12},{10,... | collective-permute-start | bytes 147464 | tf_op jit(solution)/shard_map/ppermute | solution.py:77
  26.7 4.1 %collective-permute-start.11 = (bf16[32,768]{1,0:T(8,128)(2,1)S(1)}, bf16[32,768]{1,0:T(8,128)(2,1)S(1)}, u32[]{:S(2)}, u32[]{:S(2)}) collective-permute-start(bf16[32,768]{1,0:T(8,128)(2,1)S(1)} %get-tuple-element.34.refs_2_), channel_id=1, source_target_pairs={{0,1},{1,0},{2,3},{3,2},{4,5},{5,4},{6,7},{7,6},{8,9},{9,8},{10,11... | collective-permute-start | bytes 147464 | tf_op jit(solution)/shard_map/ppermute | solution.py:77
  27.2 2.0 %collective-permute-start.8 = (bf16[272,768]{1,0:T(8,128)(2,1)S(1)}, bf16[272,768]{1,0:T(8,128)(2,1)S(1)}, u32[]{:S(2)}, u32[]{:S(2)}) collective-permute-start(bf16[272,768]{1,0:T(8,128)(2,1)S(1)} %shard_map.67.refs_0_), channel_id=1, source_target_pairs={{0,8},{8,0},{16,24},{24,16},{1,9},{9,1},{17,25},{25,17},{2,10},{10... | collective-permute-start | bytes 1253384 | tf_op jit(solution)/shard_map/ppermute | solution.py:77

commit v24 on v22

--- a/solution.py
+++ b/solution.py
@@ -108,7 +108,8 @@
 
 
 def join_body(*refs):
-    *came_refs, note_ref, out_ref, noted_ref = refs
+    own_ref, first_ref, *rest, note_ref, out_ref, noted_ref = refs
+    came_refs = [own_ref, first_ref, *rest[::-1]]
     stack_body(*came_refs, out_ref)
     stack_body(*came_refs, note_ref, noted_ref)
 
@@ -181,14 +182,6 @@
     second_ref[...] = terms[span:].astype(second_ref.dtype)
 
 
-def sum_body(kept_ref, *refs):
-    *term_refs, out_ref = refs
-    total = kept_ref[...]
-    for ref in term_refs:
-        total = total + ref[...].astype(jnp.float32)
-    out_ref[...] = total.astype(out_ref.dtype)
-
-
 def stack_body(*refs):
     *came_refs, out_ref = refs
     start = 0
@@ -222,28 +215,36 @@
     return rows, slope_of(rows, weights, chosen, place), chosen
 
 
-def cross_body(set_ref, weights_ref, acc_ref, out_ref):
-    rows, slope, chosen = set_slope(set_ref, weights_ref[...])
-    wide = spread(slope, chosen, range(acc_ref.shape[0] // BLOCK))
+def cross_slope_body(set_ref, weights_ref, slope_ref):
+    _, slope, chosen = set_slope(set_ref, weights_ref[...])
+    slope_ref[:BLOCK, :] = slope
+    slope_ref[BLOCK:, :] = jnp.broadcast_to(chosen, (NOTE, chosen.shape[1])).astype(slope.dtype)
+
+
+def set_rows(set_ref):
+    half = (set_ref.shape[0] - NOTE) // 2
+    return jnp.concatenate([set_ref[:half, :], set_ref[half + NOTE :, :]], axis=0)
+
+
+def sets_body(cross_ref, slope_ref, mate_ref, acc_ref, out_ref):
+    count = mate_ref.shape[0] - BLOCK - NOTE
+    rows = jnp.concatenate([set_rows(cross_ref), mate_ref[:count, :]], axis=0)
+    slope = jnp.concatenate([slope_ref[...], mate_ref[count:, :count]], axis=1)
+    wide = spread(*read_slope(slope), range(acc_ref.shape[0] // BLOCK))
     out_ref[...] = acc_ref[...] + jnp.dot(wide, rows, preferred_element_type=jnp.float32)
 
 
-def late_body(groups, set_ref, mate_ref, weights_ref, acc_ref, out_ref, mark_ref, held, sems):
+def late_body(groups, set_ref, slope_ref, acc_ref, out_ref, mark_ref, held, sems):
     mark_ref[...] = jnp.zeros_like(mark_ref)
-    rows, slope, chosen = set_slope(set_ref, weights_ref[...])
-    count = mate_ref.shape[0] - BLOCK - NOTE
-    mate_slope, mate_chosen = read_slope(mate_ref[count:, :count])
-    rows = jnp.concatenate([rows, mate_ref[:count, :]], axis=0)
-    slope = jnp.concatenate([slope, mate_slope], axis=1)
-    chosen = jnp.concatenate([chosen, mate_chosen], axis=1)
+    rows, (slope, chosen) = set_rows(set_ref), read_slope(slope_ref[...])
     blocks = acc_ref.shape[0] // BLOCK
     chunk = blocks // sems.shape[0]
     copies = []
     for part in range(sems.shape[0]):
         here = pl.ds(part * chunk * BLOCK, chunk * BLOCK)
         wide = spread(slope, chosen, range(part * chunk, (part + 1) * chunk))
-        total = acc_ref[here, :] + jnp.dot(wide, rows, preferred_element_type=jnp.float32)
-        held[here, :] = (total / groups).astype(held.dtype)
+        sums = acc_ref[here, :] + jnp.dot(wide, rows, preferred_element_type=jnp.float32)
+        held[here, :] = (sums / groups).astype(held.dtype)
         copy = pltpu.make_async_copy(held.at[here, :], out_ref.at[here, :], sems.at[part])
         copy.start()
         copies.append(copy)
@@ -251,18 +252,26 @@
         copy.wait()
 
 
-def late(groups, crossed, mate, weights, acc):
-    out = like(*weights.shape, weights.dtype)
+def late(groups, crossed, slope, acc):
+    out = like(*acc.shape, crossed.dtype)
     chunks = 4
     return pl.pallas_call(
         lambda *refs: late_body(groups, *refs),
         out_shape=[out, like(1, BLOCK, jnp.int32)],
-        in_specs=[pl.BlockSpec(memory_space=pltpu.VMEM)] * 4,
+        in_specs=[pl.BlockSpec(memory_space=pltpu.VMEM)] * 3,
         out_specs=[pl.BlockSpec(memory_space=pl.ANY), pl.BlockSpec(memory_space=pltpu.VMEM)],
         scratch_shapes=[pltpu.VMEM(out.shape, out.dtype), pltpu.SemaphoreType.DMA((chunks,))],
         cost_estimate=pl.CostEstimate(flops=0, bytes_accessed=0, transcendentals=0),
         compiler_params=pltpu.CompilerParams(vmem_limit_bytes=VMEM_LIMIT),
-    )(crossed, mate, weights, acc)
+    )(crossed, slope, acc)
+
+
+def sum_body(kept_ref, *refs):
+    *term_refs, out_ref = refs
+    total = kept_ref[...]
+    for ref in term_refs:
+        total = total + ref[...].astype(jnp.float32)
+    out_ref[...] = total
 
 
 def note_body(blocks_dev, q_home, me_ref, choice_ref, note_ref):
@@ -316,7 +325,7 @@
     near, noted = local_call(
         join_body,
         [like(half, width, bf16), like(half + NOTE, width, bf16)],
-        [held, *came, note],
+        [held, came[0], *came[:0:-1], note],
         0,
         [weights],
     )
@@ -357,8 +366,15 @@
     )[0]
     cross_mate = swap(cross, "pb", 1)
     grown = like(lab_dev, width, f32)
-    acc = local_call(cross_body, [grown], [cross, weights, acc], 20 * work)[0]
-    weight_grad, mark = late(groups, cross_mate, mate, weights, acc)
+    slope_like = like(BLOCK + NOTE, qcount, bf16)
+    slope = local_call(
+        cross_slope_body, [slope_like], [cross, weights], 20 * work, [acc]
+    )[0]
+    acc = local_call(sets_body, [grown], [cross, slope, mate, acc], work)[0]
+    slope = local_call(
+        cross_slope_body, [slope_like], [cross_mate, weights], work, [acc]
+    )[0]
+    weight_grad, mark = late(groups, cross_mate, slope, acc)
     query_grad = local_call(
         sum_body, [home], [near_kept, near_came, far_came, far_across], 0, [mark]
     )[0]

time: 33.4 us -> 34.1 us (1.021)
  waiting for transfers between devices: 4.39 us -> 6.33 us
  Pallas kernels: 9.35 us -> 7.97 us
    ppermute x12, waiting for transfers between devices: 4.38 us -> 6.32 us  [swap(): return lax.ppermute(value, axis, [(i, i ^ bit) for i in range(count)])]
    pallas_call x1, Pallas kernels: 3.17 us -> 1.48 us  [late(): pl.pallas_call(lambda *refs: late_body(groups, *refs), out_shape=[out, li...]
    pallas_call x11 -> x13, Pallas kernels: 6.18 us -> 6.49 us  [local_call(): pl.pallas_call(lambda *refs: body(*refs[:given], *refs[later:]), out_shap...]
  transfers between devices with their start and end apart: 13 -> 13, of which waited for: 5 -> 6; matrix products, arithmetic and copies ran while one was open for 2% -> 2% of each run, Pallas kernels for 26% -> 22%
where the time goes in v24:
time: 34.1 us; the launch traced here: 33.8 us
  starting transfers between devices  15.9 us (47%)
  Pallas kernels  7.97 us (23%)
  waiting for transfers between devices  6.33 us (19%)
  local copies, waits for them, and re-layouts  2.21 us (6%)
  between operations  0.76 us (2%)
  other arithmetic  0.72 us (2%)
    ppermute x12, starting transfers between devices, swap(): return lax.ppermute(value, axis, [(i, i ^ bit) for i in range(count)])  15.3 us
    pallas_call x13, Pallas kernels, local_call(): pl.pallas_call(lambda *refs: body(*refs[:given], *refs[later:]), out_shap...  6.49 us
    ppermute x12, waiting for transfers between devices, swap(): return lax.ppermute(value, axis, [(i, i ^ bit) for i in range(count)])  6.32 us
    unnamed x4, local copies, waits for them, and re-layouts  2.21 us
    pallas_call x1, Pallas kernels, late(): pl.pallas_call(lambda *refs: late_body(groups, *refs), out_shape=[out, li...  1.48 us
    convert_element_type x1, other arithmetic, dense_shards(): jnp.concatenate([sibling_blocks.T, positive_slot[None]], axis=0).astype(f32)  0.72 us
  transfers between devices with their start and end apart: 13, of which 6 were waited for; matrix products, arithmetic and copies ran while one was open for 2% of the time, Pallas kernels for 22%

profile of v24, /device:TPU:0, one launch (start us, length us, event | category | flops | bytes accessed | tf_op | source)
XLA Modules:
  0.0 33.8 jit_solution(9379140718724215463)
XLA Ops:
  0.6 3.1 %collective-permute-start = (bf16[32,768]{1,0:T(8,128)(2,1)}, bf16[32,768]{1,0:T(8,128)(2,1)S(1)}, u32[]{:S(2)}, u32[]{:S(2)}) collective-permute-start(bf16[32,768]{1,0:T(8,128)(2,1)} %refs_0_.1), channel_id=1, source_target_pairs={{0,2},{1,3},{2,0},{3,1},{4,6},{5,7},{6,4},{7,5},{8,10},{9,11},{10,... | collective-permute-start | bytes 147464 | tf_op jit(solution)/shard_map/ppermute | solution.py:77
  3.7 2.5 %collective-permute-start.1 = (bf16[32,768]{1,0:T(8,128)(2,1)}, bf16[32,768]{1,0:T(8,128)(2,1)S(1)}, u32[]{:S(2)}, u32[]{:S(2)}) collective-permute-start(bf16[32,768]{1,0:T(8,128)(2,1)} %refs_0_.1), channel_id=1, source_target_pairs={{0,6},{1,7},{2,4},{3,5},{4,2},{5,3},{6,0},{7,1},{8,14},{9,15},{10,... | collective-permute-start | bytes 147464 | tf_op jit(solution)/shard_map/ppermute | solution.py:77
  6.3 0.7 %add_convert_fusion.refs_1_ = f32[9,256]{1,0:T(8,128)S(1)} fusion(s32[1,256]{1,0:T(1,128)} %bitcast.4, s32[8,256]{1,0:T(8,128)} %bitcast.3), kind=kLoop, calls=%fused_computation | loop fusion | flops 4608 | bytes 18432 | tf_op jit(solution)/shard_map/convert_element_type | solution.py:319
  7.0 1.4 %copy-done = bf16[1024,768]{1,0:T(8,128)(2,1)S(1)} copy-done((bf16[1024,768]{1,0:T(8,128)(2,1)S(1)}, bf16[1024,768]{1,0:T(8,128)(2,1)}, u32[]{:S(2)}) %copy-start) | copy-done | bytes 1572888
  8.4 0.8 %copy-done.1 = bf16[32,768]{1,0:T(8,128)(2,1)S(1)} copy-done((bf16[32,768]{1,0:T(8,128)(2,1)S(1)}, bf16[32,768]{1,0:T(8,128)(2,1)}, u32[]{:S(2)}) %copy-start.1) | copy-done | bytes 49176
  9.5 0.9 %collective-permute-done.1.refs_2_ = bf16[32,768]{1,0:T(8,128)(2,1)S(1)} collective-permute-done((bf16[32,768]{1,0:T(8,128)(2,1)}, bf16[32,768]{1,0:T(8,128)(2,1)S(1)}, u32[]{:S(2)}, u32[]{:S(2)}) %collective-permute-start.1) | collective-permute-done | bytes 49184 | tf_op jit(solution)/shard_map/ppermute | solution.py:77
  10.4 1.5 %collective-permute-done.2.refs_3_ = bf16[32,768]{1,0:T(8,128)(2,1)S(1)} collective-permute-done((bf16[32,768]{1,0:T(8,128)(2,1)}, bf16[32,768]{1,0:T(8,128)(2,1)S(1)}, u32[]{:S(2)}, u32[]{:S(2)}) %collective-permute-start.2) | collective-permute-done | bytes 49184 | tf_op jit(solution)/shard_map/ppermute | solution.py:77
  12.0 1.6 %collective-permute-start.4 = (bf16[128,768]{1,0:T(8,128)(2,1)S(1)}, bf16[128,768]{1,0:T(8,128)(2,1)S(1)}, u32[]{:S(2)}, u32[]{:S(2)}) collective-permute-start(bf16[128,768]{1,0:T(8,128)(2,1)S(1)} %get-tuple-element.23.refs_0_), channel_id=1, source_target_pairs={{0,1},{1,0},{2,3},{3,2},{4,5},{5,4},{6,7},{7,6},{8,9},{9,8},{10,11... | collective-permute-start | bytes 589832 | tf_op jit(solution)/shard_map/ppermute | solution.py:77
  13.5 1.5 %collective-permute-start.9 = (bf16[144,768]{1,0:T(8,128)(2,1)S(1)}, bf16[144,768]{1,0:T(8,128)(2,1)S(1)}, u32[]{:S(2)}, u32[]{:S(2)}) collective-permute-start(bf16[144,768]{1,0:T(8,128)(2,1)S(1)} %get-tuple-element.35), channel_id=1, source_target_pairs={{0,16},{8,24},{16,0},{24,8},{1,17},{9,25},{17,1},{25,9},{2,18},{10... | collective-permute-start | bytes 663560 | tf_op jit(solution)/shard_map/ppermute | solution.py:77
  15.0 1.3 %shard_map.62 = (f32[64,768]{1,0:T(8,128)S(1)}, bf16[64,768]{1,0:T(8,128)(2,1)S(1)}, bf16[144,128]{1,0:T(8,128)(2,1)S(1)}, bf16[128,768]{1,0:T(8,128)(2,1)S(1)}) custom-call(bf16[128,768]{1,0:T(8,128)(2,1)S(1)} %get-tuple-element.23.refs_0_, bf16[1024,768]{1,0:T(8,128)(2,1)S(1)} %get-tuple-element.22.refs_5_.refs_1_, ...), custom_call_target="tpu_custom_call" | custom-call | flops 402653184 | tf_op jit(solution)/shard_map/pallas_call | solution.py:96
  16.4 0.5 %collective-permute-start.10 = (bf16[128,768]{1,0:T(8,128)(2,1)S(1)}, bf16[128,768]{1,0:T(8,128)(2,1)S(1)}, u32[]{:S(2)}, u32[]{:S(2)}) collective-permute-start(bf16[128,768]{1,0:T(8,128)(2,1)S(1)} %get-tuple-element.36), channel_id=1, source_target_pairs={{0,17},{1,16},{2,19},{3,18},{4,21},{5,20},{6,23},{7,22},{8,25},{9,... | collective-permute-start | bytes 589832 | tf_op jit(solution)/shard_map/ppermute | solution.py:87
  17.7 1.3 %shard_map.63 = (f32[64,768]{1,0:T(8,128)S(1)}, bf16[64,768]{1,0:T(8,128)(2,1)S(1)}, bf16[144,128]{1,0:T(8,128)(2,1)S(1)}) custom-call(bf16[128,768]{1,0:T(8,128)(2,1)S(1)} %collective-permute-done.4.refs_0_.refs_1_, bf16[1024,768]{1,0:T(8,128)(2,1)S(1)} %get-tuple-element.22.refs_5_.refs_1_, bf16[16,768]{1,0:T(8,128)(2,1)S(1)} %shard_map.60.refs_4_.refs_2_, ...), custom_call_target="tpu_custom_call" | custom-call | flops 402653184 | tf_op jit(solution)/shard_map/pallas_call | solution.py:96
  19.0 1.3 %collective-permute-start.6 = (bf16[64,768]{1,0:T(8,128)(2,1)S(1)}, bf16[64,768]{1,0:T(8,128)(2,1)S(1)}, u32[]{:S(2)}, u32[]{:S(2)}) collective-permute-start(bf16[64,768]{1,0:T(8,128)(2,1)S(1)} %get-tuple-element.32), channel_id=1, source_target_pairs={{0,2},{1,3},{2,0},{3,1},{4,6},{5,7},{6,4},{7,5},{8,10},{9,11},{10,... | collective-permute-start | bytes 294920 | tf_op jit(solution)/shard_map/ppermute | solution.py:77
  20.3 0.6 %shard_map.64 = (f32[1024,768]{1,0:T(8,128)S(1)}, bf16[400,768]{1,0:T(8,128)(2,1)S(1)}) custom-call(bf16[128,768]{1,0:T(8,128)(2,1)S(1)} %get-tuple-element.23.refs_0_, bf16[128,768]{1,0:T(8,128)(2,1)S(1)} %collective-permute-done.4.refs_0_.refs_1_, bf16[144,128]{1,0:T(8,128)(2,1)S(1)} %get-tuple-element.26.refs_3_.refs_2_, ...), custom_call_target="tpu_custom_call" | custom-call | flops 402653184 | tf_op jit(solution)/shard_map/pallas_call | solution.py:96
  21.6 1.4 %collective-permute-start.5 = (bf16[32,768]{1,0:T(8,128)(2,1)S(1)}, bf16[32,768]{1,0:T(8,128)(2,1)S(1)}, u32[]{:S(2)}, u32[]{:S(2)}) collective-permute-start(bf16[32,768]{1,0:T(8,128)(2,1)S(1)} %get-tuple-element.30), channel_id=1, source_target_pairs={{0,4},{1,5},{2,6},{3,7},{4,0},{5,1},{6,2},{7,3},{8,12},{9,13},{10,... | collective-permute-start | bytes 147464 | tf_op jit(solution)/shard_map/ppermute | solution.py:77
  22.9 0.8 %collective-permute-done.6.refs_1_ = bf16[64,768]{1,0:T(8,128)(2,1)S(1)} collective-permute-done((bf16[64,768]{1,0:T(8,128)(2,1)S(1)}, bf16[64,768]{1,0:T(8,128)(2,1)S(1)}, u32[]{:S(2)}, u32[]{:S(2)}) %collective-permute-start.6) | collective-permute-done | bytes 98336 | tf_op jit(solution)/shard_map/ppermute | solution.py:77
  23.7 2.3 %collective-permute-start.7 = (bf16[32,768]{1,0:T(8,128)(2,1)S(1)}, bf16[32,768]{1,0:T(8,128)(2,1)S(1)}, u32[]{:S(2)}, u32[]{:S(2)}) collective-permute-start(bf16[32,768]{1,0:T(8,128)(2,1)S(1)} %get-tuple-element.33.refs_2_), channel_id=1, source_target_pairs={{0,1},{1,0},{2,3},{3,2},{4,5},{5,4},{6,7},{7,6},{8,9},{9,8},{10,11... | collective-permute-start | bytes 147464 | tf_op jit(solution)/shard_map/ppermute | solution.py:77
  26.2 1.2 %collective-permute-start.8 = (bf16[32,768]{1,0:T(8,128)(2,1)S(1)}, bf16[32,768]{1,0:T(8,128)(2,1)S(1)}, u32[]{:S(2)}, u32[]{:S(2)}) collective-permute-start(bf16[32,768]{1,0:T(8,128)(2,1)S(1)} %get-tuple-element.34), channel_id=1, source_target_pairs={{0,5},{1,4},{2,7},{3,6},{4,1},{5,0},{6,3},{7,2},{8,13},{9,12},{10,... | collective-permute-start | bytes 147464 | tf_op jit(solution)/shard_map/ppermute | solution.py:77
  27.3 0.6 %shard_map.68.refs_1_ = bf16[144,256]{1,0:T(8,128)(2,1)S(1)} custom-call(bf16[272,768]{1,0:T(8,128)(2,1)S(1)} %shard_map.67.refs_0_, bf16[1024,768]{1,0:T(8,128)(2,1)S(1)} %get-tuple-element.22.refs_5_.refs_1_, f32[1024,768]{1,0:T(8,128)S(1)} %get-tuple-element.28.refs_2_.refs_3_), custom_call_target="tpu_custom_call" | custom-call | flops 8053063680 | tf_op jit(solution)/shard_map/pallas_call | solution.py:96
  28.0 1.0 %shard_map.69.refs_2_ = f32[1024,768]{1,0:T(8,128)S(1)} custom-call(bf16[272,768]{1,0:T(8,128)(2,1)S(1)} %shard_map.67.refs_0_, bf16[144,256]{1,0:T(8,128)(2,1)S(1)} %shard_map.68.refs_1_, bf16[400,768]{1,0:T(8,128)(2,1)S(1)} %collective-permute-done.12.refs_2_, f32[1024,768]{1,0:T(8,128)S(1)} %get-tuple-element.28.refs_2_.refs_3_), custom_call_target="tpu_custom_call" | custom-call | flops 402653184 | tf_op jit(solution)/shard_map/pallas_call | solution.py:96
  29.0 0.6 %shard_map.70.refs_1_ = bf16[144,256]{1,0:T(8,128)(2,1)S(1)} custom-call(bf16[272,768]{1,0:T(8,128)(2,1)S(1)} %collective-permute-done.11.refs_0_, bf16[1024,768]{1,0:T(8,128)(2,1)S(1)} %get-tuple-element.22.refs_5_.refs_1_, f32[1024,768]{1,0:T(8,128)S(1)} %shard_map.69.refs_2_), custom_call_target="tpu_custom_call" | custom-call | flops 402653184 | tf_op jit(solution)/shard_map/pallas_call | solution.py:96
  29.6 1.5 %shard_map.71 = (bf16[1024,768]{1,0:T(8,128)(2,1)}, s32[1,128]{1,0:T(1,128)S(1)}) custom-call(bf16[272,768]{1,0:T(8,128)(2,1)S(1)} %collective-permute-done.11.refs_0_, bf16[144,256]{1,0:T(8,128)(2,1)S(1)} %shard_map.70.refs_1_, f32[1024,768]{1,0:T(8,128)S(1)} %shard_map.69.refs_2_), custom_call_target="tpu_custom_call" | custom-call | tf_op jit(solution)/shard_map/pallas_call | solution.py:258
  31.1 2.1 %collective-permute-done.8.refs_3_ = bf16[32,768]{1,0:T(8,128)(2,1)S(1)} collective-permute-done((bf16[32,768]{1,0:T(8,128)(2,1)S(1)}, bf16[32,768]{1,0:T(8,128)(2,1)S(1)}, u32[]{:S(2)}, u32[]{:S(2)}) %collective-permute-start.8) | collective-permute-done | bytes 49184 | tf_op jit(solution)/shard_map/ppermute | solution.py:77
  33.2 0.7 %shard_map.72 = f32[32,768]{1,0:T(8,128)} custom-call(f32[32,768]{1,0:T(8,128)S(1)} %get-tuple-element.29.refs_2_.refs_0_, bf16[32,768]{1,0:T(8,128)(2,1)S(1)} %collective-permute-done.5.refs_1_, bf16[32,768]{1,0:T(8,128)(2,1)S(1)} %collective-permute-done.7.refs_2_, bf16[32,768]{1,0:T(8,128)(2,1)S(1)} %collective-permute-done.8.refs_3_, ...), custom_call_target="tpu_custom_call" | custom-call | tf_op jit(solution)/shard_map/pallas_call | solution.py:96
  (21 shorter events, 2.0 us)
Async XLA Ops:
  0.6 8.9 %collective-permute-start = (bf16[32,768]{1,0:T(8,128)(2,1)}, bf16[32,768]{1,0:T(8,128)(2,1)S(1)}, u32[]{:S(2)}, u32[]{:S(2)}) collective-permute-start(bf16[32,768]{1,0:T(8,128)(2,1)} %refs_0_.1), channel_id=1, source_target_pairs={{0,2},{1,3},{2,0},{3,1},{4,6},{5,7},{6,4},{7,5},{8,10},{9,11},{10,... | collective-permute-start | bytes 147464 | tf_op jit(solution)/shard_map/ppermute | solution.py:77
  3.7 6.7 %collective-permute-start.1 = (bf16[32,768]{1,0:T(8,128)(2,1)}, bf16[32,768]{1,0:T(8,128)(2,1)S(1)}, u32[]{:S(2)}, u32[]{:S(2)}) collective-permute-start(bf16[32,768]{1,0:T(8,128)(2,1)} %refs_0_.1), channel_id=1, source_target_pairs={{0,6},{1,7},{2,4},{3,5},{4,2},{5,3},{6,0},{7,1},{8,14},{9,15},{10,... | collective-permute-start | bytes 147464 | tf_op jit(solution)/shard_map/ppermute | solution.py:77
  6.2 5.7 %collective-permute-start.2 = (bf16[32,768]{1,0:T(8,128)(2,1)}, bf16[32,768]{1,0:T(8,128)(2,1)S(1)}, u32[]{:S(2)}, u32[]{:S(2)}) collective-permute-start(bf16[32,768]{1,0:T(8,128)(2,1)} %refs_0_.1), channel_id=1, source_target_pairs={{0,4},{1,5},{2,6},{3,7},{4,0},{5,1},{6,2},{7,3},{8,12},{9,13},{10,... | collective-permute-start | bytes 147464 | tf_op jit(solution)/shard_map/ppermute | solution.py:77
  7.0 1.4 %copy-start = (bf16[1024,768]{1,0:T(8,128)(2,1)S(1)}, bf16[1024,768]{1,0:T(8,128)(2,1)}, u32[]{:S(2)}) copy-start(bf16[1024,768]{1,0:T(8,128)(2,1)} %refs_1_.1) | copy-start | bytes 4718596
  8.4 0.8 %copy-start.1 = (bf16[32,768]{1,0:T(8,128)(2,1)S(1)}, bf16[32,768]{1,0:T(8,128)(2,1)}, u32[]{:S(2)}) copy-start(bf16[32,768]{1,0:T(8,128)(2,1)} %refs_0_.1) | copy-start | bytes 147460
  12.0 5.7 %collective-permute-start.4 = (bf16[128,768]{1,0:T(8,128)(2,1)S(1)}, bf16[128,768]{1,0:T(8,128)(2,1)S(1)}, u32[]{:S(2)}, u32[]{:S(2)}) collective-permute-start(bf16[128,768]{1,0:T(8,128)(2,1)S(1)} %get-tuple-element.23.refs_0_), channel_id=1, source_target_pairs={{0,1},{1,0},{2,3},{3,2},{4,5},{5,4},{6,7},{7,6},{8,9},{9,8},{10,11... | collective-permute-start | bytes 589832 | tf_op jit(solution)/shard_map/ppermute | solution.py:77
  13.5 12.5 %collective-permute-start.9 = (bf16[144,768]{1,0:T(8,128)(2,1)S(1)}, bf16[144,768]{1,0:T(8,128)(2,1)S(1)}, u32[]{:S(2)}, u32[]{:S(2)}) collective-permute-start(bf16[144,768]{1,0:T(8,128)(2,1)S(1)} %get-tuple-element.35), channel_id=1, source_target_pairs={{0,16},{8,24},{16,0},{24,8},{1,17},{9,25},{17,1},{25,9},{2,18},{10... | collective-permute-start | bytes 663560 | tf_op jit(solution)/shard_map/ppermute | solution.py:77
  16.4 9.7 %collective-permute-start.10 = (bf16[128,768]{1,0:T(8,128)(2,1)S(1)}, bf16[128,768]{1,0:T(8,128)(2,1)S(1)}, u32[]{:S(2)}, u32[]{:S(2)}) collective-permute-start(bf16[128,768]{1,0:T(8,128)(2,1)S(1)} %get-tuple-element.36), channel_id=1, source_target_pairs={{0,17},{1,16},{2,19},{3,18},{4,21},{5,20},{6,23},{7,22},{8,25},{9,... | collective-permute-start | bytes 589832 | tf_op jit(solution)/shard_map/ppermute | solution.py:87
  16.9 4.6 %collective-permute-start.3 = (bf16[64,768]{1,0:T(8,128)(2,1)S(1)}, bf16[64,768]{1,0:T(8,128)(2,1)S(1)}, u32[]{:S(2)}, u32[]{:S(2)}) collective-permute-start(bf16[64,768]{1,0:T(8,128)(2,1)S(1)} %get-tuple-element.25), channel_id=1, source_target_pairs={{0,2},{1,3},{2,0},{3,1},{4,6},{5,7},{6,4},{7,5},{8,10},{9,11},{10,... | collective-permute-start | bytes 294920 | tf_op jit(solution)/shard_map/ppermute | solution.py:77
  19.0 4.7 %collective-permute-start.6 = (bf16[64,768]{1,0:T(8,128)(2,1)S(1)}, bf16[64,768]{1,0:T(8,128)(2,1)S(1)}, u32[]{:S(2)}, u32[]{:S(2)}) collective-permute-start(bf16[64,768]{1,0:T(8,128)(2,1)S(1)} %get-tuple-element.32), channel_id=1, source_target_pairs={{0,2},{1,3},{2,0},{3,1},{4,6},{5,7},{6,4},{7,5},{8,10},{9,11},{10,... | collective-permute-start | bytes 294920 | tf_op jit(solution)/shard_map/ppermute | solution.py:77
  20.9 7.1 %collective-permute-start.12 = (bf16[400,768]{1,0:T(8,128)(2,1)S(1)}, bf16[400,768]{1,0:T(8,128)(2,1)S(1)}, u32[]{:S(2)}, u32[]{:S(2)}) collective-permute-start(bf16[400,768]{1,0:T(8,128)(2,1)S(1)} %get-tuple-element.37), channel_id=1, source_target_pairs={{0,8},{8,0},{16,24},{24,16},{1,9},{9,1},{17,25},{25,17},{2,10},{10... | collective-permute-start | bytes 1843208 | tf_op jit(solution)/shard_map/ppermute | solution.py:77
  21.6 9.5 %collective-permute-start.5 = (bf16[32,768]{1,0:T(8,128)(2,1)S(1)}, bf16[32,768]{1,0:T(8,128)(2,1)S(1)}, u32[]{:S(2)}, u32[]{:S(2)}) collective-permute-start(bf16[32,768]{1,0:T(8,128)(2,1)S(1)} %get-tuple-element.30), channel_id=1, source_target_pairs={{0,4},{1,5},{2,6},{3,7},{4,0},{5,1},{6,2},{7,3},{8,12},{9,13},{10,... | collective-permute-start | bytes 147464 | tf_op jit(solution)/shard_map/ppermute | solution.py:77
  23.7 7.4 %collective-permute-start.7 = (bf16[32,768]{1,0:T(8,128)(2,1)S(1)}, bf16[32,768]{1,0:T(8,128)(2,1)S(1)}, u32[]{:S(2)}, u32[]{:S(2)}) collective-permute-start(bf16[32,768]{1,0:T(8,128)(2,1)S(1)} %get-tuple-element.33.refs_2_), channel_id=1, source_target_pairs={{0,1},{1,0},{2,3},{3,2},{4,5},{5,4},{6,7},{7,6},{8,9},{9,8},{10,11... | collective-permute-start | bytes 147464 | tf_op jit(solution)/shard_map/ppermute | solution.py:77
  26.1 2.9 %collective-permute-start.11 = (bf16[272,768]{1,0:T(8,128)(2,1)S(1)}, bf16[272,768]{1,0:T(8,128)(2,1)S(1)}, u32[]{:S(2)}, u32[]{:S(2)}) collective-permute-start(bf16[272,768]{1,0:T(8,128)(2,1)S(1)} %shard_map.67.refs_0_), channel_id=1, source_target_pairs={{0,8},{8,0},{16,24},{24,16},{1,9},{9,1},{17,25},{25,17},{2,10},{10... | collective-permute-start | bytes 1253384 | tf_op jit(solution)/shard_map/ppermute | solution.py:77
  26.2 7.0 %collective-permute-start.8 = (bf16[32,768]{1,0:T(8,128)(2,1)S(1)}, bf16[32,768]{1,0:T(8,128)(2,1)S(1)}, u32[]{:S(2)}, u32[]{:S(2)}) collective-permute-start(bf16[32,768]{1,0:T(8,128)(2,1)S(1)} %get-tuple-element.34), channel_id=1, source_target_pairs={{0,5},{1,4},{2,7},{3,6},{4,1},{5,0},{6,3},{7,2},{8,13},{9,12},{10,... | collective-permute-start | bytes 147464 | tf_op jit(solution)/shard_map/ppermute | solution.py:77

commit v25 on v24

--- a/solution.py
+++ b/solution.py
@@ -360,9 +360,9 @@
     far_sent, far_across = local_call(
         fold_body, [sent, sent], [far_kept, far_came], 0, [near_kept, acc]
     )
-    far_came, far_across = swap(far_sent, "lab", 1), swap(far_across, "lab", 5)
+    far_came, far_over = swap(far_sent, "lab", 1), swap(far_across, "lab", 5)
     cross = local_call(
-        stack_body, [like(qcount + NOTE, width, bf16)], [cross_near, cross_far], 0, [far_sent]
+        stack_body, [like(qcount + NOTE, width, bf16)], [cross_near, cross_far], 0, [far_across]
     )[0]
     cross_mate = swap(cross, "pb", 1)
     grown = like(lab_dev, width, f32)
@@ -376,7 +376,7 @@
     )[0]
     weight_grad, mark = late(groups, cross_mate, slope, acc)
     query_grad = local_call(
-        sum_body, [home], [near_kept, near_came, far_came, far_across], 0, [mark]
+        sum_body, [home], [near_kept, near_came, far_came, far_over], 0, [mark]
     )[0]
     return (query_grad, weight_grad)
 

time: 34.1 us -> 32.1 us (0.941)
  waiting for transfers between devices: 6.33 us -> 4.37 us
    ppermute x12, waiting for transfers between devices: 6.32 us -> 4.37 us  [swap(): return lax.ppermute(value, axis, [(i, i ^ bit) for i in range(count)])]
  transfers between devices with their start and end apart: 13 -> 13, of which waited for: 6 -> 6; matrix products, arithmetic and copies ran while one was open for 2% -> 2% of each run, Pallas kernels for 22% -> 23%
where the time goes in v25:
time: 32.1 us; the launch traced here: 31.9 us
  starting transfers between devices  15.9 us (50%)
  Pallas kernels  7.97 us (25%)
  waiting for transfers between devices  4.37 us (14%)
  local copies, waits for them, and re-layouts  2.21 us (7%)
  between operations  0.75 us (2%)
  other arithmetic  0.72 us (2%)
    ppermute x12, starting transfers between devices, swap(): return lax.ppermute(value, axis, [(i, i ^ bit) for i in range(count)])  15.3 us
    pallas_call x13, Pallas kernels, local_call(): pl.pallas_call(lambda *refs: body(*refs[:given], *refs[later:]), out_shap...  6.5 us
    ppermute x12, waiting for transfers between devices, swap(): return lax.ppermute(value, axis, [(i, i ^ bit) for i in range(count)])  4.37 us
    unnamed x4, local copies, waits for them, and re-layouts  2.21 us
    pallas_call x1, Pallas kernels, late(): pl.pallas_call(lambda *refs: late_body(groups, *refs), out_shape=[out, li...  1.48 us
    convert_element_type x1, other arithmetic, dense_shards(): jnp.concatenate([sibling_blocks.T, positive_slot[None]], axis=0).astype(f32)  0.72 us
  transfers between devices with their start and end apart: 13, of which 6 were waited for; matrix products, arithmetic and copies ran while one was open for 2% of the time, Pallas kernels for 23%

profile of v25, /device:TPU:0, one launch (start us, length us, event | category | flops | bytes accessed | tf_op | source)
XLA Modules:
  0.0 31.9 jit_solution(12590969011835320909)
XLA Ops:
  0.6 3.1 %collective-permute-start = (bf16[32,768]{1,0:T(8,128)(2,1)}, bf16[32,768]{1,0:T(8,128)(2,1)S(1)}, u32[]{:S(2)}, u32[]{:S(2)}) collective-permute-start(bf16[32,768]{1,0:T(8,128)(2,1)} %refs_0_.1), channel_id=1, source_target_pairs={{0,2},{1,3},{2,0},{3,1},{4,6},{5,7},{6,4},{7,5},{8,10},{9,11},{10,... | collective-permute-start | bytes 147464 | tf_op jit(solution)/shard_map/ppermute | solution.py:77
  3.7 2.5 %collective-permute-start.1 = (bf16[32,768]{1,0:T(8,128)(2,1)}, bf16[32,768]{1,0:T(8,128)(2,1)S(1)}, u32[]{:S(2)}, u32[]{:S(2)}) collective-permute-start(bf16[32,768]{1,0:T(8,128)(2,1)} %refs_0_.1), channel_id=1, source_target_pairs={{0,6},{1,7},{2,4},{3,5},{4,2},{5,3},{6,0},{7,1},{8,14},{9,15},{10,... | collective-permute-start | bytes 147464 | tf_op jit(solution)/shard_map/ppermute | solution.py:77
  6.3 0.7 %add_convert_fusion.refs_1_ = f32[9,256]{1,0:T(8,128)S(1)} fusion(s32[1,256]{1,0:T(1,128)} %bitcast.4, s32[8,256]{1,0:T(8,128)} %bitcast.3), kind=kLoop, calls=%fused_computation | loop fusion | flops 4608 | bytes 18432 | tf_op jit(solution)/shard_map/convert_element_type | solution.py:319
  7.0 1.4 %copy-done = bf16[1024,768]{1,0:T(8,128)(2,1)S(1)} copy-done((bf16[1024,768]{1,0:T(8,128)(2,1)S(1)}, bf16[1024,768]{1,0:T(8,128)(2,1)}, u32[]{:S(2)}) %copy-start) | copy-done | bytes 1572888
  8.4 0.8 %copy-done.1 = bf16[32,768]{1,0:T(8,128)(2,1)S(1)} copy-done((bf16[32,768]{1,0:T(8,128)(2,1)S(1)}, bf16[32,768]{1,0:T(8,128)(2,1)}, u32[]{:S(2)}) %copy-start.1) | copy-done | bytes 49176
  9.5 0.9 %collective-permute-done.1.refs_2_ = bf16[32,768]{1,0:T(8,128)(2,1)S(1)} collective-permute-done((bf16[32,768]{1,0:T(8,128)(2,1)}, bf16[32,768]{1,0:T(8,128)(2,1)S(1)}, u32[]{:S(2)}, u32[]{:S(2)}) %collective-permute-start.1) | collective-permute-done | bytes 49184 | tf_op jit(solution)/shard_map/ppermute | solution.py:77
  10.4 1.5 %collective-permute-done.2.refs_3_ = bf16[32,768]{1,0:T(8,128)(2,1)S(1)} collective-permute-done((bf16[32,768]{1,0:T(8,128)(2,1)}, bf16[32,768]{1,0:T(8,128)(2,1)S(1)}, u32[]{:S(2)}, u32[]{:S(2)}) %collective-permute-start.2) | collective-permute-done | bytes 49184 | tf_op jit(solution)/shard_map/ppermute | solution.py:77
  12.0 1.6 %collective-permute-start.4 = (bf16[128,768]{1,0:T(8,128)(2,1)S(1)}, bf16[128,768]{1,0:T(8,128)(2,1)S(1)}, u32[]{:S(2)}, u32[]{:S(2)}) collective-permute-start(bf16[128,768]{1,0:T(8,128)(2,1)S(1)} %get-tuple-element.23.refs_0_), channel_id=1, source_target_pairs={{0,1},{1,0},{2,3},{3,2},{4,5},{5,4},{6,7},{7,6},{8,9},{9,8},{10,11... | collective-permute-start | bytes 589832 | tf_op jit(solution)/shard_map/ppermute | solution.py:77
  13.5 1.5 %collective-permute-start.9 = (bf16[144,768]{1,0:T(8,128)(2,1)S(1)}, bf16[144,768]{1,0:T(8,128)(2,1)S(1)}, u32[]{:S(2)}, u32[]{:S(2)}) collective-permute-start(bf16[144,768]{1,0:T(8,128)(2,1)S(1)} %get-tuple-element.35), channel_id=1, source_target_pairs={{0,16},{8,24},{16,0},{24,8},{1,17},{9,25},{17,1},{25,9},{2,18},{10... | collective-permute-start | bytes 663560 | tf_op jit(solution)/shard_map/ppermute | solution.py:77
  15.0 1.3 %shard_map.62 = (f32[64,768]{1,0:T(8,128)S(1)}, bf16[64,768]{1,0:T(8,128)(2,1)S(1)}, bf16[144,128]{1,0:T(8,128)(2,1)S(1)}, bf16[128,768]{1,0:T(8,128)(2,1)S(1)}) custom-call(bf16[128,768]{1,0:T(8,128)(2,1)S(1)} %get-tuple-element.23.refs_0_, bf16[1024,768]{1,0:T(8,128)(2,1)S(1)} %get-tuple-element.22.refs_5_.refs_1_, ...), custom_call_target="tpu_custom_call" | custom-call | flops 402653184 | tf_op jit(solution)/shard_map/pallas_call | solution.py:96
  16.4 0.5 %collective-permute-start.10 = (bf16[128,768]{1,0:T(8,128)(2,1)S(1)}, bf16[128,768]{1,0:T(8,128)(2,1)S(1)}, u32[]{:S(2)}, u32[]{:S(2)}) collective-permute-start(bf16[128,768]{1,0:T(8,128)(2,1)S(1)} %get-tuple-element.36), channel_id=1, source_target_pairs={{0,17},{1,16},{2,19},{3,18},{4,21},{5,20},{6,23},{7,22},{8,25},{9,... | collective-permute-start | bytes 589832 | tf_op jit(solution)/shard_map/ppermute | solution.py:87
  17.7 1.3 %shard_map.63 = (f32[64,768]{1,0:T(8,128)S(1)}, bf16[64,768]{1,0:T(8,128)(2,1)S(1)}, bf16[144,128]{1,0:T(8,128)(2,1)S(1)}) custom-call(bf16[128,768]{1,0:T(8,128)(2,1)S(1)} %collective-permute-done.4.refs_0_.refs_1_, bf16[1024,768]{1,0:T(8,128)(2,1)S(1)} %get-tuple-element.22.refs_5_.refs_1_, bf16[16,768]{1,0:T(8,128)(2,1)S(1)} %shard_map.60.refs_4_.refs_2_, ...), custom_call_target="tpu_custom_call" | custom-call | flops 402653184 | tf_op jit(solution)/shard_map/pallas_call | solution.py:96
  19.0 1.3 %collective-permute-start.6 = (bf16[64,768]{1,0:T(8,128)(2,1)S(1)}, bf16[64,768]{1,0:T(8,128)(2,1)S(1)}, u32[]{:S(2)}, u32[]{:S(2)}) collective-permute-start(bf16[64,768]{1,0:T(8,128)(2,1)S(1)} %get-tuple-element.32), channel_id=1, source_target_pairs={{0,2},{1,3},{2,0},{3,1},{4,6},{5,7},{6,4},{7,5},{8,10},{9,11},{10,... | collective-permute-start | bytes 294920 | tf_op jit(solution)/shard_map/ppermute | solution.py:77
  20.3 0.6 %shard_map.64 = (f32[1024,768]{1,0:T(8,128)S(1)}, bf16[400,768]{1,0:T(8,128)(2,1)S(1)}) custom-call(bf16[128,768]{1,0:T(8,128)(2,1)S(1)} %get-tuple-element.23.refs_0_, bf16[128,768]{1,0:T(8,128)(2,1)S(1)} %collective-permute-done.4.refs_0_.refs_1_, bf16[144,128]{1,0:T(8,128)(2,1)S(1)} %get-tuple-element.26.refs_3_.refs_2_, ...), custom_call_target="tpu_custom_call" | custom-call | flops 402653184 | tf_op jit(solution)/shard_map/pallas_call | solution.py:96
  21.0 0.5 %collective-permute-done.3.refs_1_ = bf16[64,768]{1,0:T(8,128)(2,1)S(1)} collective-permute-done((bf16[64,768]{1,0:T(8,128)(2,1)S(1)}, bf16[64,768]{1,0:T(8,128)(2,1)S(1)}, u32[]{:S(2)}, u32[]{:S(2)}) %collective-permute-start.3) | collective-permute-done | bytes 98336 | tf_op jit(solution)/shard_map/ppermute | solution.py:77
  21.6 1.4 %collective-permute-start.5 = (bf16[32,768]{1,0:T(8,128)(2,1)S(1)}, bf16[32,768]{1,0:T(8,128)(2,1)S(1)}, u32[]{:S(2)}, u32[]{:S(2)}) collective-permute-start(bf16[32,768]{1,0:T(8,128)(2,1)S(1)} %get-tuple-element.30), channel_id=1, source_target_pairs={{0,4},{1,5},{2,6},{3,7},{4,0},{5,1},{6,2},{7,3},{8,12},{9,13},{10,... | collective-permute-start | bytes 147464 | tf_op jit(solution)/shard_map/ppermute | solution.py:77
  22.9 0.8 %collective-permute-done.6.refs_1_ = bf16[64,768]{1,0:T(8,128)(2,1)S(1)} collective-permute-done((bf16[64,768]{1,0:T(8,128)(2,1)S(1)}, bf16[64,768]{1,0:T(8,128)(2,1)S(1)}, u32[]{:S(2)}, u32[]{:S(2)}) %collective-permute-start.6) | collective-permute-done | bytes 98336 | tf_op jit(solution)/shard_map/ppermute | solution.py:77
  23.7 2.9 %collective-permute-start.8 = (bf16[32,768]{1,0:T(8,128)(2,1)S(1)}, bf16[32,768]{1,0:T(8,128)(2,1)S(1)}, u32[]{:S(2)}, u32[]{:S(2)}) collective-permute-start(bf16[32,768]{1,0:T(8,128)(2,1)S(1)} %get-tuple-element.34.refs_2_), channel_id=1, source_target_pairs={{0,5},{1,4},{2,7},{3,6},{4,1},{5,0},{6,3},{7,2},{8,13},{9,12},{10,... | collective-permute-start | bytes 147464 | tf_op jit(solution)/shard_map/ppermute | solution.py:77
  26.8 0.6 %collective-permute-start.7 = (bf16[32,768]{1,0:T(8,128)(2,1)S(1)}, bf16[32,768]{1,0:T(8,128)(2,1)S(1)}, u32[]{:S(2)}, u32[]{:S(2)}) collective-permute-start(bf16[32,768]{1,0:T(8,128)(2,1)S(1)} %get-tuple-element.33), channel_id=1, source_target_pairs={{0,1},{1,0},{2,3},{3,2},{4,5},{5,4},{6,7},{7,6},{8,9},{9,8},{10,11... | collective-permute-start | bytes 147464 | tf_op jit(solution)/shard_map/ppermute | solution.py:77
  27.3 0.6 %shard_map.68.refs_1_ = bf16[144,256]{1,0:T(8,128)(2,1)S(1)} custom-call(bf16[272,768]{1,0:T(8,128)(2,1)S(1)} %shard_map.67.refs_0_, bf16[1024,768]{1,0:T(8,128)(2,1)S(1)} %get-tuple-element.22.refs_5_.refs_1_, f32[1024,768]{1,0:T(8,128)S(1)} %get-tuple-element.28.refs_2_.refs_3_), custom_call_target="tpu_custom_call" | custom-call | flops 8053063680 | tf_op jit(solution)/shard_map/pallas_call | solution.py:96
  28.0 1.0 %shard_map.69.refs_2_ = f32[1024,768]{1,0:T(8,128)S(1)} custom-call(bf16[272,768]{1,0:T(8,128)(2,1)S(1)} %shard_map.67.refs_0_, bf16[144,256]{1,0:T(8,128)(2,1)S(1)} %shard_map.68.refs_1_, bf16[400,768]{1,0:T(8,128)(2,1)S(1)} %collective-permute-done.12.refs_2_, f32[1024,768]{1,0:T(8,128)S(1)} %get-tuple-element.28.refs_2_.refs_3_), custom_call_target="tpu_custom_call" | custom-call | flops 402653184 | tf_op jit(solution)/shard_map/pallas_call | solution.py:96
  29.0 0.6 %shard_map.70.refs_1_ = bf16[144,256]{1,0:T(8,128)(2,1)S(1)} custom-call(bf16[272,768]{1,0:T(8,128)(2,1)S(1)} %collective-permute-done.11.refs_0_, bf16[1024,768]{1,0:T(8,128)(2,1)S(1)} %get-tuple-element.22.refs_5_.refs_1_, f32[1024,768]{1,0:T(8,128)S(1)} %shard_map.69.refs_2_), custom_call_target="tpu_custom_call" | custom-call | flops 402653184 | tf_op jit(solution)/shard_map/pallas_call | solution.py:96
  29.6 1.5 %shard_map.71 = (bf16[1024,768]{1,0:T(8,128)(2,1)}, s32[1,128]{1,0:T(1,128)S(1)}) custom-call(bf16[272,768]{1,0:T(8,128)(2,1)S(1)} %collective-permute-done.11.refs_0_, bf16[144,256]{1,0:T(8,128)(2,1)S(1)} %shard_map.70.refs_1_, f32[1024,768]{1,0:T(8,128)S(1)} %shard_map.69.refs_2_), custom_call_target="tpu_custom_call" | custom-call | tf_op jit(solution)/shard_map/pallas_call | solution.py:258
  31.2 0.7 %shard_map.72 = f32[32,768]{1,0:T(8,128)} custom-call(f32[32,768]{1,0:T(8,128)S(1)} %get-tuple-element.29.refs_2_.refs_0_, bf16[32,768]{1,0:T(8,128)(2,1)S(1)} %collective-permute-done.5.refs_1_, bf16[32,768]{1,0:T(8,128)(2,1)S(1)} %collective-permute-done.7.refs_2_, bf16[32,768]{1,0:T(8,128)(2,1)S(1)} %collective-permute-done.8.refs_3_, ...), custom_call_target="tpu_custom_call" | custom-call | tf_op jit(solution)/shard_map/pallas_call | solution.py:96
  (21 shorter events, 1.5 us)
Async XLA Ops:
  0.6 8.9 %collective-permute-start = (bf16[32,768]{1,0:T(8,128)(2,1)}, bf16[32,768]{1,0:T(8,128)(2,1)S(1)}, u32[]{:S(2)}, u32[]{:S(2)}) collective-permute-start(bf16[32,768]{1,0:T(8,128)(2,1)} %refs_0_.1), channel_id=1, source_target_pairs={{0,2},{1,3},{2,0},{3,1},{4,6},{5,7},{6,4},{7,5},{8,10},{9,11},{10,... | collective-permute-start | bytes 147464 | tf_op jit(solution)/shard_map/ppermute | solution.py:77
  3.7 6.7 %collective-permute-start.1 = (bf16[32,768]{1,0:T(8,128)(2,1)}, bf16[32,768]{1,0:T(8,128)(2,1)S(1)}, u32[]{:S(2)}, u32[]{:S(2)}) collective-permute-start(bf16[32,768]{1,0:T(8,128)(2,1)} %refs_0_.1), channel_id=1, source_target_pairs={{0,6},{1,7},{2,4},{3,5},{4,2},{5,3},{6,0},{7,1},{8,14},{9,15},{10,... | collective-permute-start | bytes 147464 | tf_op jit(solution)/shard_map/ppermute | solution.py:77
  6.2 5.7 %collective-permute-start.2 = (bf16[32,768]{1,0:T(8,128)(2,1)}, bf16[32,768]{1,0:T(8,128)(2,1)S(1)}, u32[]{:S(2)}, u32[]{:S(2)}) collective-permute-start(bf16[32,768]{1,0:T(8,128)(2,1)} %refs_0_.1), channel_id=1, source_target_pairs={{0,4},{1,5},{2,6},{3,7},{4,0},{5,1},{6,2},{7,3},{8,12},{9,13},{10,... | collective-permute-start | bytes 147464 | tf_op jit(solution)/shard_map/ppermute | solution.py:77
  7.0 1.4 %copy-start = (bf16[1024,768]{1,0:T(8,128)(2,1)S(1)}, bf16[1024,768]{1,0:T(8,128)(2,1)}, u32[]{:S(2)}) copy-start(bf16[1024,768]{1,0:T(8,128)(2,1)} %refs_1_.1) | copy-start | bytes 4718596
  8.4 0.8 %copy-start.1 = (bf16[32,768]{1,0:T(8,128)(2,1)S(1)}, bf16[32,768]{1,0:T(8,128)(2,1)}, u32[]{:S(2)}) copy-start(bf16[32,768]{1,0:T(8,128)(2,1)} %refs_0_.1) | copy-start | bytes 147460
  12.0 5.7 %collective-permute-start.4 = (bf16[128,768]{1,0:T(8,128)(2,1)S(1)}, bf16[128,768]{1,0:T(8,128)(2,1)S(1)}, u32[]{:S(2)}, u32[]{:S(2)}) collective-permute-start(bf16[128,768]{1,0:T(8,128)(2,1)S(1)} %get-tuple-element.23.refs_0_), channel_id=1, source_target_pairs={{0,1},{1,0},{2,3},{3,2},{4,5},{5,4},{6,7},{7,6},{8,9},{9,8},{10,11... | collective-permute-start | bytes 589832 | tf_op jit(solution)/shard_map/ppermute | solution.py:77
  13.5 13.1 %collective-permute-start.9 = (bf16[144,768]{1,0:T(8,128)(2,1)S(1)}, bf16[144,768]{1,0:T(8,128)(2,1)S(1)}, u32[]{:S(2)}, u32[]{:S(2)}) collective-permute-start(bf16[144,768]{1,0:T(8,128)(2,1)S(1)} %get-tuple-element.35), channel_id=1, source_target_pairs={{0,16},{8,24},{16,0},{24,8},{1,17},{9,25},{17,1},{25,9},{2,18},{10... | collective-permute-start | bytes 663560 | tf_op jit(solution)/shard_map/ppermute | solution.py:77
  16.4 10.3 %collective-permute-start.10 = (bf16[128,768]{1,0:T(8,128)(2,1)S(1)}, bf16[128,768]{1,0:T(8,128)(2,1)S(1)}, u32[]{:S(2)}, u32[]{:S(2)}) collective-permute-start(bf16[128,768]{1,0:T(8,128)(2,1)S(1)} %get-tuple-element.36), channel_id=1, source_target_pairs={{0,17},{1,16},{2,19},{3,18},{4,21},{5,20},{6,23},{7,22},{8,25},{9,... | collective-permute-start | bytes 589832 | tf_op jit(solution)/shard_map/ppermute | solution.py:87
  16.9 4.6 %collective-permute-start.3 = (bf16[64,768]{1,0:T(8,128)(2,1)S(1)}, bf16[64,768]{1,0:T(8,128)(2,1)S(1)}, u32[]{:S(2)}, u32[]{:S(2)}) collective-permute-start(bf16[64,768]{1,0:T(8,128)(2,1)S(1)} %get-tuple-element.25), channel_id=1, source_target_pairs={{0,2},{1,3},{2,0},{3,1},{4,6},{5,7},{6,4},{7,5},{8,10},{9,11},{10,... | collective-permute-start | bytes 294920 | tf_op jit(solution)/shard_map/ppermute | solution.py:77
  19.0 4.7 %collective-permute-start.6 = (bf16[64,768]{1,0:T(8,128)(2,1)S(1)}, bf16[64,768]{1,0:T(8,128)(2,1)S(1)}, u32[]{:S(2)}, u32[]{:S(2)}) collective-permute-start(bf16[64,768]{1,0:T(8,128)(2,1)S(1)} %get-tuple-element.32), channel_id=1, source_target_pairs={{0,2},{1,3},{2,0},{3,1},{4,6},{5,7},{6,4},{7,5},{8,10},{9,11},{10,... | collective-permute-start | bytes 294920 | tf_op jit(solution)/shard_map/ppermute | solution.py:77
  20.9 7.1 %collective-permute-start.12 = (bf16[400,768]{1,0:T(8,128)(2,1)S(1)}, bf16[400,768]{1,0:T(8,128)(2,1)S(1)}, u32[]{:S(2)}, u32[]{:S(2)}) collective-permute-start(bf16[400,768]{1,0:T(8,128)(2,1)S(1)} %get-tuple-element.37), channel_id=1, source_target_pairs={{0,8},{8,0},{16,24},{24,16},{1,9},{9,1},{17,25},{25,17},{2,10},{10... | collective-permute-start | bytes 1843208 | tf_op jit(solution)/shard_map/ppermute | solution.py:77
  21.6 9.5 %collective-permute-start.5 = (bf16[32,768]{1,0:T(8,128)(2,1)S(1)}, bf16[32,768]{1,0:T(8,128)(2,1)S(1)}, u32[]{:S(2)}, u32[]{:S(2)}) collective-permute-start(bf16[32,768]{1,0:T(8,128)(2,1)S(1)} %get-tuple-element.30), channel_id=1, source_target_pairs={{0,4},{1,5},{2,6},{3,7},{4,0},{5,1},{6,2},{7,3},{8,12},{9,13},{10,... | collective-permute-start | bytes 147464 | tf_op jit(solution)/shard_map/ppermute | solution.py:77
  23.7 7.5 %collective-permute-start.8 = (bf16[32,768]{1,0:T(8,128)(2,1)S(1)}, bf16[32,768]{1,0:T(8,128)(2,1)S(1)}, u32[]{:S(2)}, u32[]{:S(2)}) collective-permute-start(bf16[32,768]{1,0:T(8,128)(2,1)S(1)} %get-tuple-element.34.refs_2_), channel_id=1, source_target_pairs={{0,5},{1,4},{2,7},{3,6},{4,1},{5,0},{6,3},{7,2},{8,13},{9,12},{10,... | collective-permute-start | bytes 147464 | tf_op jit(solution)/shard_map/ppermute | solution.py:77
  26.7 2.3 %collective-permute-start.11 = (bf16[272,768]{1,0:T(8,128)(2,1)S(1)}, bf16[272,768]{1,0:T(8,128)(2,1)S(1)}, u32[]{:S(2)}, u32[]{:S(2)}) collective-permute-start(bf16[272,768]{1,0:T(8,128)(2,1)S(1)} %shard_map.67.refs_0_), channel_id=1, source_target_pairs={{0,8},{8,0},{16,24},{24,16},{1,9},{9,1},{17,25},{25,17},{2,10},{10... | collective-permute-start | bytes 1253384 | tf_op jit(solution)/shard_map/ppermute | solution.py:77
  26.8 4.4 %collective-permute-start.7 = (bf16[32,768]{1,0:T(8,128)(2,1)S(1)}, bf16[32,768]{1,0:T(8,128)(2,1)S(1)}, u32[]{:S(2)}, u32[]{:S(2)}) collective-permute-start(bf16[32,768]{1,0:T(8,128)(2,1)S(1)} %get-tuple-element.33), channel_id=1, source_target_pairs={{0,1},{1,0},{2,3},{3,2},{4,5},{5,4},{6,7},{7,6},{8,9},{9,8},{10,11... | collective-permute-start | bytes 147464 | tf_op jit(solution)/shard_map/ppermute | solution.py:77

commit v26 on v25

--- a/solution.py
+++ b/solution.py
@@ -108,8 +108,8 @@
 
 
 def join_body(*refs):
-    own_ref, first_ref, *rest, note_ref, out_ref, noted_ref = refs
-    came_refs = [own_ref, first_ref, *rest[::-1]]
+    own_ref, *came_refs, note_ref, out_ref, noted_ref = refs
+    came_refs = [own_ref, *came_refs[::-1]]
     stack_body(*came_refs, out_ref)
     stack_body(*came_refs, note_ref, noted_ref)
 
@@ -254,7 +254,7 @@
 
 def late(groups, crossed, slope, acc):
     out = like(*acc.shape, crossed.dtype)
-    chunks = 4
+    chunks = 8
     return pl.pallas_call(
         lambda *refs: late_body(groups, *refs),
         out_shape=[out, like(1, BLOCK, jnp.int32)],
@@ -309,7 +309,7 @@
     groups = lax.axis_size("pb")
     f32, bf16 = jnp.float32, jnp.bfloat16
     me = jnp.reshape(lax.axis_index("lab"), (1,)).astype(jnp.int32)
-    far_bit = groups // 2
+    far_bit, next_bit, wide_bit = groups // 2, homes // 4, homes // 2
     came = [swap(queries, "lab", step) for step in range(2, homes, 2)]
     held, weights = local_call(
         hold_body,
@@ -325,7 +325,7 @@
     near, noted = local_call(
         join_body,
         [like(half, width, bf16), like(half + NOTE, width, bf16)],
-        [held, came[0], *came[:0:-1], note],
+        [held, *came[::-1], note],
         0,
         [weights],
     )
@@ -344,7 +344,7 @@
     far_kept, far_sent, far_slope = local_call(
         far_body, pair + [slope_like], [far, weights, note], work, [near_slope]
     )
-    far_came, near_came = swap(far_sent, "lab", 2), swap(near_sent, "lab", 2)
+    far_came, near_came = swap(far_sent, "lab", next_bit), swap(near_sent, "lab", next_bit)
     acc, own = local_call(
         own_body,
         [like(lab_dev, width, f32), like(qcount + BLOCK + NOTE, width, bf16)],
@@ -356,11 +356,11 @@
     near_kept, near_sent = local_call(
         fold_body, [home, sent], [near_kept, near_came], 0, [acc]
     )
-    near_came = swap(near_sent, "lab", 4)
+    near_came = swap(near_sent, "lab", wide_bit)
     far_sent, far_across = local_call(
         fold_body, [sent, sent], [far_kept, far_came], 0, [near_kept, acc]
     )
-    far_came, far_over = swap(far_sent, "lab", 1), swap(far_across, "lab", 5)
+    far_came, far_over = swap(far_sent, "lab", 1), swap(far_across, "lab", wide_bit + 1)
     cross = local_call(
         stack_body, [like(qcount + NOTE, width, bf16)], [cross_near, cross_far], 0, [far_across]
     )[0]

time: 32.1 us -> 33.1 us (1.031)
  starting transfers between devices: 15.9 us -> 18.4 us
  waiting for transfers between devices: 4.37 us -> 2.85 us
    ppermute x12, starting transfers between devices: 15.3 us -> 17.8 us  [swap(): return lax.ppermute(value, axis, [(i, i ^ bit) for i in range(count)])]
    ppermute x12, waiting for transfers between devices: 4.37 us -> 2.85 us  [swap(): return lax.ppermute(value, axis, [(i, i ^ bit) for i in range(count)])]
  transfers between devices with their start and end apart: 13 -> 13, of which waited for: 6 -> 4; matrix products, arithmetic and copies ran while one was open for 2% -> 2% of each run, Pallas kernels for 23% -> 22%
where the time goes in v26:
time: 33.1 us; the launch traced here: 32.8 us
  starting transfers between devices  18.4 us (56%)
  Pallas kernels  7.95 us (24%)
  waiting for transfers between devices  2.85 us (9%)
  local copies, waits for them, and re-layouts  2.21 us (7%)
  between operations  0.75 us (2%)
  other arithmetic  0.72 us (2%)
    ppermute x12, starting transfers between devices, swap(): return lax.ppermute(value, axis, [(i, i ^ bit) for i in range(count)])  17.8 us
    pallas_call x13, Pallas kernels, local_call(): pl.pallas_call(lambda *refs: body(*refs[:given], *refs[later:]), out_shap...  6.49 us
    ppermute x12, waiting for transfers between devices, swap(): return lax.ppermute(value, axis, [(i, i ^ bit) for i in range(count)])  2.85 us
    unnamed x4, local copies, waits for them, and re-layouts  2.21 us
    pallas_call x1, Pallas kernels, late(): pl.pallas_call(lambda *refs: late_body(groups, *refs), out_shape=[out, li...  1.46 us
    convert_element_type x1, other arithmetic, dense_shards(): jnp.concatenate([sibling_blocks.T, positive_slot[None]], axis=0).astype(f32)  0.72 us
  transfers between devices with their start and end apart: 13, of which 4 were waited for; matrix products, arithmetic and copies ran while one was open for 2% of the time, Pallas kernels for 22%

profile of v26, /device:TPU:0, one launch (start us, length us, event | category | flops | bytes accessed | tf_op | source)
XLA Modules:
  0.0 32.8 jit_solution(15332206918102237660)
XLA Ops:
  0.6 5.1 %collective-permute-start = (bf16[32,768]{1,0:T(8,128)(2,1)}, bf16[32,768]{1,0:T(8,128)(2,1)S(1)}, u32[]{:S(2)}, u32[]{:S(2)}) collective-permute-start(bf16[32,768]{1,0:T(8,128)(2,1)} %refs_0_.1), channel_id=1, source_target_pairs={{0,6},{1,7},{2,4},{3,5},{4,2},{5,3},{6,0},{7,1},{8,14},{9,15},{10,... | collective-permute-start | bytes 147464 | tf_op jit(solution)/shard_map/ppermute | solution.py:77
  5.7 0.6 %collective-permute-start.2 = (bf16[32,768]{1,0:T(8,128)(2,1)}, bf16[32,768]{1,0:T(8,128)(2,1)S(1)}, u32[]{:S(2)}, u32[]{:S(2)}) collective-permute-start(bf16[32,768]{1,0:T(8,128)(2,1)} %refs_0_.1), channel_id=1, source_target_pairs={{0,2},{1,3},{2,0},{3,1},{4,6},{5,7},{6,4},{7,5},{8,10},{9,11},{10,... | collective-permute-start | bytes 147464 | tf_op jit(solution)/shard_map/ppermute | solution.py:77
  6.4 0.7 %add_convert_fusion.refs_1_ = f32[9,256]{1,0:T(8,128)S(1)} fusion(s32[1,256]{1,0:T(1,128)} %bitcast.4, s32[8,256]{1,0:T(8,128)} %bitcast.3), kind=kLoop, calls=%fused_computation | loop fusion | flops 4608 | bytes 18432 | tf_op jit(solution)/shard_map/convert_element_type | solution.py:319
  7.1 1.4 %copy-done = bf16[1024,768]{1,0:T(8,128)(2,1)S(1)} copy-done((bf16[1024,768]{1,0:T(8,128)(2,1)S(1)}, bf16[1024,768]{1,0:T(8,128)(2,1)}, u32[]{:S(2)}) %copy-start) | copy-done | bytes 1572888
  8.5 0.8 %copy-done.1 = bf16[32,768]{1,0:T(8,128)(2,1)S(1)} copy-done((bf16[32,768]{1,0:T(8,128)(2,1)S(1)}, bf16[32,768]{1,0:T(8,128)(2,1)}, u32[]{:S(2)}) %copy-start.1) | copy-done | bytes 49176
  9.6 1.4 %collective-permute-done.1.refs_2_ = bf16[32,768]{1,0:T(8,128)(2,1)S(1)} collective-permute-done((bf16[32,768]{1,0:T(8,128)(2,1)}, bf16[32,768]{1,0:T(8,128)(2,1)S(1)}, u32[]{:S(2)}, u32[]{:S(2)}) %collective-permute-start.1) | collective-permute-done | bytes 49184 | tf_op jit(solution)/shard_map/ppermute | solution.py:77
  11.0 1.6 %collective-permute-start.4 = (bf16[128,768]{1,0:T(8,128)(2,1)S(1)}, bf16[128,768]{1,0:T(8,128)(2,1)S(1)}, u32[]{:S(2)}, u32[]{:S(2)}) collective-permute-start(bf16[128,768]{1,0:T(8,128)(2,1)S(1)} %get-tuple-element.23.refs_0_), channel_id=1, source_target_pairs={{0,1},{1,0},{2,3},{3,2},{4,5},{5,4},{6,7},{7,6},{8,9},{9,8},{10,11... | collective-permute-start | bytes 589832 | tf_op jit(solution)/shard_map/ppermute | solution.py:77
  12.6 1.5 %collective-permute-start.9 = (bf16[144,768]{1,0:T(8,128)(2,1)S(1)}, bf16[144,768]{1,0:T(8,128)(2,1)S(1)}, u32[]{:S(2)}, u32[]{:S(2)}) collective-permute-start(bf16[144,768]{1,0:T(8,128)(2,1)S(1)} %get-tuple-element.35), channel_id=1, source_target_pairs={{0,16},{8,24},{16,0},{24,8},{1,17},{9,25},{17,1},{25,9},{2,18},{10... | collective-permute-start | bytes 663560 | tf_op jit(solution)/shard_map/ppermute | solution.py:77
  14.1 1.3 %shard_map.62 = (f32[64,768]{1,0:T(8,128)S(1)}, bf16[64,768]{1,0:T(8,128)(2,1)S(1)}, bf16[144,128]{1,0:T(8,128)(2,1)S(1)}, bf16[128,768]{1,0:T(8,128)(2,1)S(1)}) custom-call(bf16[128,768]{1,0:T(8,128)(2,1)S(1)} %get-tuple-element.23.refs_0_, bf16[1024,768]{1,0:T(8,128)(2,1)S(1)} %get-tuple-element.22.refs_5_.refs_1_, ...), custom_call_target="tpu_custom_call" | custom-call | flops 402653184 | tf_op jit(solution)/shard_map/pallas_call | solution.py:96
  15.4 0.5 %collective-permute-start.10 = (bf16[128,768]{1,0:T(8,128)(2,1)S(1)}, bf16[128,768]{1,0:T(8,128)(2,1)S(1)}, u32[]{:S(2)}, u32[]{:S(2)}) collective-permute-start(bf16[128,768]{1,0:T(8,128)(2,1)S(1)} %get-tuple-element.36), channel_id=1, source_target_pairs={{0,17},{1,16},{2,19},{3,18},{4,21},{5,20},{6,23},{7,22},{8,25},{9,... | collective-permute-start | bytes 589832 | tf_op jit(solution)/shard_map/ppermute | solution.py:87
  15.9 0.6 %collective-permute-start.3 = (bf16[64,768]{1,0:T(8,128)(2,1)S(1)}, bf16[64,768]{1,0:T(8,128)(2,1)S(1)}, u32[]{:S(2)}, u32[]{:S(2)}) collective-permute-start(bf16[64,768]{1,0:T(8,128)(2,1)S(1)} %get-tuple-element.25), channel_id=1, source_target_pairs={{0,2},{1,3},{2,0},{3,1},{4,6},{5,7},{6,4},{7,5},{8,10},{9,11},{10,... | collective-permute-start | bytes 294920 | tf_op jit(solution)/shard_map/ppermute | solution.py:77
  16.6 0.2 collective-permute-done.4.refs_0_.refs_1_
  16.8 1.3 %shard_map.63 = (f32[64,768]{1,0:T(8,128)S(1)}, bf16[64,768]{1,0:T(8,128)(2,1)S(1)}, bf16[144,128]{1,0:T(8,128)(2,1)S(1)}) custom-call(bf16[128,768]{1,0:T(8,128)(2,1)S(1)} %collective-permute-done.4.refs_0_.refs_1_, bf16[1024,768]{1,0:T(8,128)(2,1)S(1)} %get-tuple-element.22.refs_5_.refs_1_, bf16[16,768]{1,0:T(8,128)(2,1)S(1)} %shard_map.60.refs_4_.refs_2_, ...), custom_call_target="tpu_custom_call" | custom-call | flops 402653184 | tf_op jit(solution)/shard_map/pallas_call | solution.py:96
  18.1 1.2 %collective-permute-start.6 = (bf16[64,768]{1,0:T(8,128)(2,1)S(1)}, bf16[64,768]{1,0:T(8,128)(2,1)S(1)}, u32[]{:S(2)}, u32[]{:S(2)}) collective-permute-start(bf16[64,768]{1,0:T(8,128)(2,1)S(1)} %get-tuple-element.32), channel_id=1, source_target_pairs={{0,2},{1,3},{2,0},{3,1},{4,6},{5,7},{6,4},{7,5},{8,10},{9,11},{10,... | collective-permute-start | bytes 294920 | tf_op jit(solution)/shard_map/ppermute | solution.py:77
  19.4 0.6 %shard_map.64 = (f32[1024,768]{1,0:T(8,128)S(1)}, bf16[400,768]{1,0:T(8,128)(2,1)S(1)}) custom-call(bf16[128,768]{1,0:T(8,128)(2,1)S(1)} %get-tuple-element.23.refs_0_, bf16[128,768]{1,0:T(8,128)(2,1)S(1)} %collective-permute-done.4.refs_0_.refs_1_, bf16[144,128]{1,0:T(8,128)(2,1)S(1)} %get-tuple-element.26.refs_3_.refs_2_, ...), custom_call_target="tpu_custom_call" | custom-call | flops 402653184 | tf_op jit(solution)/shard_map/pallas_call | solution.py:96
  20.0 0.9 %collective-permute-done.3.refs_1_ = bf16[64,768]{1,0:T(8,128)(2,1)S(1)} collective-permute-done((bf16[64,768]{1,0:T(8,128)(2,1)S(1)}, bf16[64,768]{1,0:T(8,128)(2,1)S(1)}, u32[]{:S(2)}, u32[]{:S(2)}) %collective-permute-start.3) | collective-permute-done | bytes 98336 | tf_op jit(solution)/shard_map/ppermute | solution.py:77
  21.0 2.0 %collective-permute-start.5 = (bf16[32,768]{1,0:T(8,128)(2,1)S(1)}, bf16[32,768]{1,0:T(8,128)(2,1)S(1)}, u32[]{:S(2)}, u32[]{:S(2)}) collective-permute-start(bf16[32,768]{1,0:T(8,128)(2,1)S(1)} %get-tuple-element.30), channel_id=1, source_target_pairs={{0,4},{1,5},{2,6},{3,7},{4,0},{5,1},{6,2},{7,3},{8,12},{9,13},{10,... | collective-permute-start | bytes 147464 | tf_op jit(solution)/shard_map/ppermute | solution.py:77
  23.0 4.9 %collective-permute-start.8 = (bf16[32,768]{1,0:T(8,128)(2,1)S(1)}, bf16[32,768]{1,0:T(8,128)(2,1)S(1)}, u32[]{:S(2)}, u32[]{:S(2)}) collective-permute-start(bf16[32,768]{1,0:T(8,128)(2,1)S(1)} %get-tuple-element.34.refs_2_), channel_id=1, source_target_pairs={{0,5},{1,4},{2,7},{3,6},{4,1},{5,0},{6,3},{7,2},{8,13},{9,12},{10,... | collective-permute-start | bytes 147464 | tf_op jit(solution)/shard_map/ppermute | solution.py:77
  28.1 0.6 %shard_map.68.refs_1_ = bf16[144,256]{1,0:T(8,128)(2,1)S(1)} custom-call(bf16[272,768]{1,0:T(8,128)(2,1)S(1)} %shard_map.67.refs_0_, bf16[1024,768]{1,0:T(8,128)(2,1)S(1)} %get-tuple-element.22.refs_5_.refs_1_, f32[1024,768]{1,0:T(8,128)S(1)} %get-tuple-element.28.refs_2_.refs_3_), custom_call_target="tpu_custom_call" | custom-call | flops 8053063680 | tf_op jit(solution)/shard_map/pallas_call | solution.py:96
  28.7 1.0 %shard_map.69.refs_2_ = f32[1024,768]{1,0:T(8,128)S(1)} custom-call(bf16[272,768]{1,0:T(8,128)(2,1)S(1)} %shard_map.67.refs_0_, bf16[144,256]{1,0:T(8,128)(2,1)S(1)} %shard_map.68.refs_1_, bf16[400,768]{1,0:T(8,128)(2,1)S(1)} %collective-permute-done.12.refs_2_, f32[1024,768]{1,0:T(8,128)S(1)} %get-tuple-element.28.refs_2_.refs_3_), custom_call_target="tpu_custom_call" | custom-call | flops 402653184 | tf_op jit(solution)/shard_map/pallas_call | solution.py:96
  29.7 0.6 %shard_map.70.refs_1_ = bf16[144,256]{1,0:T(8,128)(2,1)S(1)} custom-call(bf16[272,768]{1,0:T(8,128)(2,1)S(1)} %collective-permute-done.11.refs_0_, bf16[1024,768]{1,0:T(8,128)(2,1)S(1)} %get-tuple-element.22.refs_5_.refs_1_, f32[1024,768]{1,0:T(8,128)S(1)} %shard_map.69.refs_2_), custom_call_target="tpu_custom_call" | custom-call | flops 402653184 | tf_op jit(solution)/shard_map/pallas_call | solution.py:96
  30.4 1.5 %shard_map.71 = (bf16[1024,768]{1,0:T(8,128)(2,1)}, s32[1,128]{1,0:T(1,128)S(1)}) custom-call(bf16[272,768]{1,0:T(8,128)(2,1)S(1)} %collective-permute-done.11.refs_0_, bf16[144,256]{1,0:T(8,128)(2,1)S(1)} %shard_map.70.refs_1_, f32[1024,768]{1,0:T(8,128)S(1)} %shard_map.69.refs_2_), custom_call_target="tpu_custom_call" | custom-call | tf_op jit(solution)/shard_map/pallas_call | solution.py:258
  31.8 0.3 collective-permute-done.7.refs_2_
  32.2 0.7 %shard_map.72 = f32[32,768]{1,0:T(8,128)} custom-call(f32[32,768]{1,0:T(8,128)S(1)} %get-tuple-element.29.refs_2_.refs_0_, bf16[32,768]{1,0:T(8,128)(2,1)S(1)} %collective-permute-done.5.refs_1_, bf16[32,768]{1,0:T(8,128)(2,1)S(1)} %collective-permute-done.7.refs_2_, bf16[32,768]{1,0:T(8,128)(2,1)S(1)} %collective-permute-done.8.refs_3_, ...), custom_call_target="tpu_custom_call" | custom-call | tf_op jit(solution)/shard_map/pallas_call | solution.py:96
  (21 shorter events, 0.6 us)
Async XLA Ops:
  0.6 9.0 %collective-permute-start = (bf16[32,768]{1,0:T(8,128)(2,1)}, bf16[32,768]{1,0:T(8,128)(2,1)S(1)}, u32[]{:S(2)}, u32[]{:S(2)}) collective-permute-start(bf16[32,768]{1,0:T(8,128)(2,1)} %refs_0_.1), channel_id=1, source_target_pairs={{0,6},{1,7},{2,4},{3,5},{4,2},{5,3},{6,0},{7,1},{8,14},{9,15},{10,... | collective-permute-start | bytes 147464 | tf_op jit(solution)/shard_map/ppermute | solution.py:77
  5.7 5.2 %collective-permute-start.1 = (bf16[32,768]{1,0:T(8,128)(2,1)}, bf16[32,768]{1,0:T(8,128)(2,1)S(1)}, u32[]{:S(2)}, u32[]{:S(2)}) collective-permute-start(bf16[32,768]{1,0:T(8,128)(2,1)} %refs_0_.1), channel_id=1, source_target_pairs={{0,4},{1,5},{2,6},{3,7},{4,0},{5,1},{6,2},{7,3},{8,12},{9,13},{10,... | collective-permute-start | bytes 147464 | tf_op jit(solution)/shard_map/ppermute | solution.py:77
  5.7 5.2 %collective-permute-start.2 = (bf16[32,768]{1,0:T(8,128)(2,1)}, bf16[32,768]{1,0:T(8,128)(2,1)S(1)}, u32[]{:S(2)}, u32[]{:S(2)}) collective-permute-start(bf16[32,768]{1,0:T(8,128)(2,1)} %refs_0_.1), channel_id=1, source_target_pairs={{0,2},{1,3},{2,0},{3,1},{4,6},{5,7},{6,4},{7,5},{8,10},{9,11},{10,... | collective-permute-start | bytes 147464 | tf_op jit(solution)/shard_map/ppermute | solution.py:77
  7.1 1.4 %copy-start = (bf16[1024,768]{1,0:T(8,128)(2,1)S(1)}, bf16[1024,768]{1,0:T(8,128)(2,1)}, u32[]{:S(2)}) copy-start(bf16[1024,768]{1,0:T(8,128)(2,1)} %refs_1_.1) | copy-start | bytes 4718596
  8.5 0.8 %copy-start.1 = (bf16[32,768]{1,0:T(8,128)(2,1)S(1)}, bf16[32,768]{1,0:T(8,128)(2,1)}, u32[]{:S(2)}) copy-start(bf16[32,768]{1,0:T(8,128)(2,1)} %refs_0_.1) | copy-start | bytes 147460
  11.0 5.8 %collective-permute-start.4 = (bf16[128,768]{1,0:T(8,128)(2,1)S(1)}, bf16[128,768]{1,0:T(8,128)(2,1)S(1)}, u32[]{:S(2)}, u32[]{:S(2)}) collective-permute-start(bf16[128,768]{1,0:T(8,128)(2,1)S(1)} %get-tuple-element.23.refs_0_), channel_id=1, source_target_pairs={{0,1},{1,0},{2,3},{3,2},{4,5},{5,4},{6,7},{7,6},{8,9},{9,8},{10,11... | collective-permute-start | bytes 589832 | tf_op jit(solution)/shard_map/ppermute | solution.py:77
  12.6 15.3 %collective-permute-start.9 = (bf16[144,768]{1,0:T(8,128)(2,1)S(1)}, bf16[144,768]{1,0:T(8,128)(2,1)S(1)}, u32[]{:S(2)}, u32[]{:S(2)}) collective-permute-start(bf16[144,768]{1,0:T(8,128)(2,1)S(1)} %get-tuple-element.35), channel_id=1, source_target_pairs={{0,16},{8,24},{16,0},{24,8},{1,17},{9,25},{17,1},{25,9},{2,18},{10... | collective-permute-start | bytes 663560 | tf_op jit(solution)/shard_map/ppermute | solution.py:77
  15.4 12.5 %collective-permute-start.10 = (bf16[128,768]{1,0:T(8,128)(2,1)S(1)}, bf16[128,768]{1,0:T(8,128)(2,1)S(1)}, u32[]{:S(2)}, u32[]{:S(2)}) collective-permute-start(bf16[128,768]{1,0:T(8,128)(2,1)S(1)} %get-tuple-element.36), channel_id=1, source_target_pairs={{0,17},{1,16},{2,19},{3,18},{4,21},{5,20},{6,23},{7,22},{8,25},{9,... | collective-permute-start | bytes 589832 | tf_op jit(solution)/shard_map/ppermute | solution.py:87
  15.9 5.0 %collective-permute-start.3 = (bf16[64,768]{1,0:T(8,128)(2,1)S(1)}, bf16[64,768]{1,0:T(8,128)(2,1)S(1)}, u32[]{:S(2)}, u32[]{:S(2)}) collective-permute-start(bf16[64,768]{1,0:T(8,128)(2,1)S(1)} %get-tuple-element.25), channel_id=1, source_target_pairs={{0,2},{1,3},{2,0},{3,1},{4,6},{5,7},{6,4},{7,5},{8,10},{9,11},{10,... | collective-permute-start | bytes 294920 | tf_op jit(solution)/shard_map/ppermute | solution.py:77
  18.1 4.9 %collective-permute-start.6 = (bf16[64,768]{1,0:T(8,128)(2,1)S(1)}, bf16[64,768]{1,0:T(8,128)(2,1)S(1)}, u32[]{:S(2)}, u32[]{:S(2)}) collective-permute-start(bf16[64,768]{1,0:T(8,128)(2,1)S(1)} %get-tuple-element.32), channel_id=1, source_target_pairs={{0,2},{1,3},{2,0},{3,1},{4,6},{5,7},{6,4},{7,5},{8,10},{9,11},{10,... | collective-permute-start | bytes 294920 | tf_op jit(solution)/shard_map/ppermute | solution.py:77
  19.9 8.8 %collective-permute-start.12 = (bf16[400,768]{1,0:T(8,128)(2,1)S(1)}, bf16[400,768]{1,0:T(8,128)(2,1)S(1)}, u32[]{:S(2)}, u32[]{:S(2)}) collective-permute-start(bf16[400,768]{1,0:T(8,128)(2,1)S(1)} %get-tuple-element.37), channel_id=1, source_target_pairs={{0,8},{8,0},{16,24},{24,16},{1,9},{9,1},{17,25},{25,17},{2,10},{10... | collective-permute-start | bytes 1843208 | tf_op jit(solution)/shard_map/ppermute | solution.py:77
  21.0 10.9 %collective-permute-start.5 = (bf16[32,768]{1,0:T(8,128)(2,1)S(1)}, bf16[32,768]{1,0:T(8,128)(2,1)S(1)}, u32[]{:S(2)}, u32[]{:S(2)}) collective-permute-start(bf16[32,768]{1,0:T(8,128)(2,1)S(1)} %get-tuple-element.30), channel_id=1, source_target_pairs={{0,4},{1,5},{2,6},{3,7},{4,0},{5,1},{6,2},{7,3},{8,12},{9,13},{10,... | collective-permute-start | bytes 147464 | tf_op jit(solution)/shard_map/ppermute | solution.py:77
  23.0 9.1 %collective-permute-start.8 = (bf16[32,768]{1,0:T(8,128)(2,1)S(1)}, bf16[32,768]{1,0:T(8,128)(2,1)S(1)}, u32[]{:S(2)}, u32[]{:S(2)}) collective-permute-start(bf16[32,768]{1,0:T(8,128)(2,1)S(1)} %get-tuple-element.34.refs_2_), channel_id=1, source_target_pairs={{0,5},{1,4},{2,7},{3,6},{4,1},{5,0},{6,3},{7,2},{8,13},{9,12},{10,... | collective-permute-start | bytes 147464 | tf_op jit(solution)/shard_map/ppermute | solution.py:77
  27.9 1.8 %collective-permute-start.11 = (bf16[272,768]{1,0:T(8,128)(2,1)S(1)}, bf16[272,768]{1,0:T(8,128)(2,1)S(1)}, u32[]{:S(2)}, u32[]{:S(2)}) collective-permute-start(bf16[272,768]{1,0:T(8,128)(2,1)S(1)} %shard_map.67.refs_0_), channel_id=1, source_target_pairs={{0,8},{8,0},{16,24},{24,16},{1,9},{9,1},{17,25},{25,17},{2,10},{10... | collective-permute-start | bytes 1253384 | tf_op jit(solution)/shard_map/ppermute | solution.py:77
  28.0 4.2 %collective-permute-start.7 = (bf16[32,768]{1,0:T(8,128)(2,1)S(1)}, bf16[32,768]{1,0:T(8,128)(2,1)S(1)}, u32[]{:S(2)}, u32[]{:S(2)}) collective-permute-start(bf16[32,768]{1,0:T(8,128)(2,1)S(1)} %get-tuple-element.33), channel_id=1, source_target_pairs={{0,1},{1,0},{2,3},{3,2},{4,5},{5,4},{6,7},{7,6},{8,9},{9,8},{10,11... | collective-permute-start | bytes 147464 | tf_op jit(solution)/shard_map/ppermute | solution.py:77

commit v27 on v26

--- a/solution.py
+++ b/solution.py
@@ -109,7 +109,7 @@
 
 def join_body(*refs):
     own_ref, *came_refs, note_ref, out_ref, noted_ref = refs
-    came_refs = [own_ref, *came_refs[::-1]]
+    came_refs = [own_ref, *came_refs[1:], came_refs[0]]
     stack_body(*came_refs, out_ref)
     stack_body(*came_refs, note_ref, noted_ref)
 
@@ -254,7 +254,7 @@
 
 def late(groups, crossed, slope, acc):
     out = like(*acc.shape, crossed.dtype)
-    chunks = 8
+    chunks = 4
     return pl.pallas_call(
         lambda *refs: late_body(groups, *refs),
         out_shape=[out, like(1, BLOCK, jnp.int32)],
@@ -325,7 +325,7 @@
     near, noted = local_call(
         join_body,
         [like(half, width, bf16), like(half + NOTE, width, bf16)],
-        [held, *came[::-1], note],
+        [held, came[-1], *came[:-1], note],
         0,
         [weights],
     )

time: 33.1 us -> 32.8 us (level)
  starting transfers between devices: 18.4 us -> 16.8 us
  waiting for transfers between devices: 2.85 us -> 4.05 us
    ppermute x12, starting transfers between devices: 17.8 us -> 16.3 us  [swap(): return lax.ppermute(value, axis, [(i, i ^ bit) for i in range(count)])]
    ppermute x12, waiting for transfers between devices: 2.85 us -> 4.05 us  [swap(): return lax.ppermute(value, axis, [(i, i ^ bit) for i in range(count)])]
where the time goes in v27:
time: 32.8 us; the launch traced here: 32.5 us
  starting transfers between devices  16.8 us (51%)
  Pallas kernels  7.97 us (24%)
  waiting for transfers between devices  4.05 us (12%)
  local copies, waits for them, and re-layouts  2.21 us (7%)
  between operations  0.76 us (2%)
  other arithmetic  0.72 us (2%)
    ppermute x12, starting transfers between devices, swap(): return lax.ppermute(value, axis, [(i, i ^ bit) for i in range(count)])  16.3 us
    pallas_call x13, Pallas kernels, local_call(): pl.pallas_call(lambda *refs: body(*refs[:given], *refs[later:]), out_shap...  6.5 us
    ppermute x12, waiting for transfers between devices, swap(): return lax.ppermute(value, axis, [(i, i ^ bit) for i in range(count)])  4.05 us
    unnamed x4, local copies, waits for them, and re-layouts  2.21 us
    pallas_call x1, Pallas kernels, late(): pl.pallas_call(lambda *refs: late_body(groups, *refs), out_shape=[out, li...  1.48 us
    convert_element_type x1, other arithmetic, dense_shards(): jnp.concatenate([sibling_blocks.T, positive_slot[None]], axis=0).astype(f32)  0.72 us
  transfers between devices with their start and end apart: 13, of which 4 were waited for; matrix products, arithmetic and copies ran while one was open for 2% of the time, Pallas kernels for 22%

profile of v27, /device:TPU:0, one launch (start us, length us, event | category | flops | bytes accessed | tf_op | source)
XLA Modules:
  0.0 32.5 jit_solution(2791465705561496047)
XLA Ops:
  0.6 5.1 %collective-permute-start = (bf16[32,768]{1,0:T(8,128)(2,1)}, bf16[32,768]{1,0:T(8,128)(2,1)S(1)}, u32[]{:S(2)}, u32[]{:S(2)}) collective-permute-start(bf16[32,768]{1,0:T(8,128)(2,1)} %refs_0_.1), channel_id=1, source_target_pairs={{0,6},{1,7},{2,4},{3,5},{4,2},{5,3},{6,0},{7,1},{8,14},{9,15},{10,... | collective-permute-start | bytes 147464 | tf_op jit(solution)/shard_map/ppermute | solution.py:77
  5.7 0.6 %collective-permute-start.2 = (bf16[32,768]{1,0:T(8,128)(2,1)}, bf16[32,768]{1,0:T(8,128)(2,1)S(1)}, u32[]{:S(2)}, u32[]{:S(2)}) collective-permute-start(bf16[32,768]{1,0:T(8,128)(2,1)} %refs_0_.1), channel_id=1, source_target_pairs={{0,4},{1,5},{2,6},{3,7},{4,0},{5,1},{6,2},{7,3},{8,12},{9,13},{10,... | collective-permute-start | bytes 147464 | tf_op jit(solution)/shard_map/ppermute | solution.py:77
  6.4 0.7 %add_convert_fusion.refs_1_ = f32[9,256]{1,0:T(8,128)S(1)} fusion(s32[1,256]{1,0:T(1,128)} %bitcast.4, s32[8,256]{1,0:T(8,128)} %bitcast.3), kind=kLoop, calls=%fused_computation | loop fusion | flops 4608 | bytes 18432 | tf_op jit(solution)/shard_map/convert_element_type | solution.py:319
  7.1 1.4 %copy-done = bf16[1024,768]{1,0:T(8,128)(2,1)S(1)} copy-done((bf16[1024,768]{1,0:T(8,128)(2,1)S(1)}, bf16[1024,768]{1,0:T(8,128)(2,1)}, u32[]{:S(2)}) %copy-start) | copy-done | bytes 1572888
  8.5 0.8 %copy-done.1 = bf16[32,768]{1,0:T(8,128)(2,1)S(1)} copy-done((bf16[32,768]{1,0:T(8,128)(2,1)S(1)}, bf16[32,768]{1,0:T(8,128)(2,1)}, u32[]{:S(2)}) %copy-start.1) | copy-done | bytes 49176
  9.6 0.5 %collective-permute-done.1.refs_2_ = bf16[32,768]{1,0:T(8,128)(2,1)S(1)} collective-permute-done((bf16[32,768]{1,0:T(8,128)(2,1)}, bf16[32,768]{1,0:T(8,128)(2,1)S(1)}, u32[]{:S(2)}, u32[]{:S(2)}) %collective-permute-start.1) | collective-permute-done | bytes 49184 | tf_op jit(solution)/shard_map/ppermute | solution.py:77
  10.1 1.2 %collective-permute-done.2.refs_3_ = bf16[32,768]{1,0:T(8,128)(2,1)S(1)} collective-permute-done((bf16[32,768]{1,0:T(8,128)(2,1)}, bf16[32,768]{1,0:T(8,128)(2,1)S(1)}, u32[]{:S(2)}, u32[]{:S(2)}) %collective-permute-start.2) | collective-permute-done | bytes 49184 | tf_op jit(solution)/shard_map/ppermute | solution.py:77
  11.3 1.6 %collective-permute-start.4 = (bf16[128,768]{1,0:T(8,128)(2,1)S(1)}, bf16[128,768]{1,0:T(8,128)(2,1)S(1)}, u32[]{:S(2)}, u32[]{:S(2)}) collective-permute-start(bf16[128,768]{1,0:T(8,128)(2,1)S(1)} %get-tuple-element.23.refs_0_), channel_id=1, source_target_pairs={{0,1},{1,0},{2,3},{3,2},{4,5},{5,4},{6,7},{7,6},{8,9},{9,8},{10,11... | collective-permute-start | bytes 589832 | tf_op jit(solution)/shard_map/ppermute | solution.py:77
  12.9 1.5 %collective-permute-start.9 = (bf16[144,768]{1,0:T(8,128)(2,1)S(1)}, bf16[144,768]{1,0:T(8,128)(2,1)S(1)}, u32[]{:S(2)}, u32[]{:S(2)}) collective-permute-start(bf16[144,768]{1,0:T(8,128)(2,1)S(1)} %get-tuple-element.35), channel_id=1, source_target_pairs={{0,16},{8,24},{16,0},{24,8},{1,17},{9,25},{17,1},{25,9},{2,18},{10... | collective-permute-start | bytes 663560 | tf_op jit(solution)/shard_map/ppermute | solution.py:77
  14.3 1.3 %shard_map.62 = (f32[64,768]{1,0:T(8,128)S(1)}, bf16[64,768]{1,0:T(8,128)(2,1)S(1)}, bf16[144,128]{1,0:T(8,128)(2,1)S(1)}, bf16[128,768]{1,0:T(8,128)(2,1)S(1)}) custom-call(bf16[128,768]{1,0:T(8,128)(2,1)S(1)} %get-tuple-element.23.refs_0_, bf16[1024,768]{1,0:T(8,128)(2,1)S(1)} %get-tuple-element.22.refs_5_.refs_1_, ...), custom_call_target="tpu_custom_call" | custom-call | flops 402653184 | tf_op jit(solution)/shard_map/pallas_call | solution.py:96
  15.7 0.5 %collective-permute-start.10 = (bf16[128,768]{1,0:T(8,128)(2,1)S(1)}, bf16[128,768]{1,0:T(8,128)(2,1)S(1)}, u32[]{:S(2)}, u32[]{:S(2)}) collective-permute-start(bf16[128,768]{1,0:T(8,128)(2,1)S(1)} %get-tuple-element.36), channel_id=1, source_target_pairs={{0,17},{1,16},{2,19},{3,18},{4,21},{5,20},{6,23},{7,22},{8,25},{9,... | collective-permute-start | bytes 589832 | tf_op jit(solution)/shard_map/ppermute | solution.py:87
  16.2 1.7 %collective-permute-start.3 = (bf16[64,768]{1,0:T(8,128)(2,1)S(1)}, bf16[64,768]{1,0:T(8,128)(2,1)S(1)}, u32[]{:S(2)}, u32[]{:S(2)}) collective-permute-start(bf16[64,768]{1,0:T(8,128)(2,1)S(1)} %get-tuple-element.25), channel_id=1, source_target_pairs={{0,2},{1,3},{2,0},{3,1},{4,6},{5,7},{6,4},{7,5},{8,10},{9,11},{10,... | collective-permute-start | bytes 294920 | tf_op jit(solution)/shard_map/ppermute | solution.py:77
  18.0 1.3 %shard_map.63 = (f32[64,768]{1,0:T(8,128)S(1)}, bf16[64,768]{1,0:T(8,128)(2,1)S(1)}, bf16[144,128]{1,0:T(8,128)(2,1)S(1)}) custom-call(bf16[128,768]{1,0:T(8,128)(2,1)S(1)} %collective-permute-done.4.refs_0_.refs_1_, bf16[1024,768]{1,0:T(8,128)(2,1)S(1)} %get-tuple-element.22.refs_5_.refs_1_, bf16[16,768]{1,0:T(8,128)(2,1)S(1)} %shard_map.60.refs_4_.refs_2_, ...), custom_call_target="tpu_custom_call" | custom-call | flops 402653184 | tf_op jit(solution)/shard_map/pallas_call | solution.py:96
  19.3 1.4 %collective-permute-start.6 = (bf16[64,768]{1,0:T(8,128)(2,1)S(1)}, bf16[64,768]{1,0:T(8,128)(2,1)S(1)}, u32[]{:S(2)}, u32[]{:S(2)}) collective-permute-start(bf16[64,768]{1,0:T(8,128)(2,1)S(1)} %get-tuple-element.32), channel_id=1, source_target_pairs={{0,2},{1,3},{2,0},{3,1},{4,6},{5,7},{6,4},{7,5},{8,10},{9,11},{10,... | collective-permute-start | bytes 294920 | tf_op jit(solution)/shard_map/ppermute | solution.py:77
  20.7 0.6 %shard_map.64 = (f32[1024,768]{1,0:T(8,128)S(1)}, bf16[400,768]{1,0:T(8,128)(2,1)S(1)}) custom-call(bf16[128,768]{1,0:T(8,128)(2,1)S(1)} %get-tuple-element.23.refs_0_, bf16[128,768]{1,0:T(8,128)(2,1)S(1)} %collective-permute-done.4.refs_0_.refs_1_, bf16[144,128]{1,0:T(8,128)(2,1)S(1)} %get-tuple-element.26.refs_3_.refs_2_, ...), custom_call_target="tpu_custom_call" | custom-call | flops 402653184 | tf_op jit(solution)/shard_map/pallas_call | solution.py:96
  21.4 1.6 %collective-permute-start.5 = (bf16[32,768]{1,0:T(8,128)(2,1)S(1)}, bf16[32,768]{1,0:T(8,128)(2,1)S(1)}, u32[]{:S(2)}, u32[]{:S(2)}) collective-permute-start(bf16[32,768]{1,0:T(8,128)(2,1)S(1)} %get-tuple-element.30), channel_id=1, source_target_pairs={{0,4},{1,5},{2,6},{3,7},{4,0},{5,1},{6,2},{7,3},{8,12},{9,13},{10,... | collective-permute-start | bytes 147464 | tf_op jit(solution)/shard_map/ppermute | solution.py:77
  23.0 1.0 %collective-permute-done.6.refs_1_ = bf16[64,768]{1,0:T(8,128)(2,1)S(1)} collective-permute-done((bf16[64,768]{1,0:T(8,128)(2,1)S(1)}, bf16[64,768]{1,0:T(8,128)(2,1)S(1)}, u32[]{:S(2)}, u32[]{:S(2)}) %collective-permute-start.6) | collective-permute-done | bytes 98336 | tf_op jit(solution)/shard_map/ppermute | solution.py:77
  24.0 2.5 %collective-permute-start.8 = (bf16[32,768]{1,0:T(8,128)(2,1)S(1)}, bf16[32,768]{1,0:T(8,128)(2,1)S(1)}, u32[]{:S(2)}, u32[]{:S(2)}) collective-permute-start(bf16[32,768]{1,0:T(8,128)(2,1)S(1)} %get-tuple-element.34.refs_2_), channel_id=1, source_target_pairs={{0,5},{1,4},{2,7},{3,6},{4,1},{5,0},{6,3},{7,2},{8,13},{9,12},{10,... | collective-permute-start | bytes 147464 | tf_op jit(solution)/shard_map/ppermute | solution.py:77
  26.7 0.6 %shard_map.68.refs_1_ = bf16[144,256]{1,0:T(8,128)(2,1)S(1)} custom-call(bf16[272,768]{1,0:T(8,128)(2,1)S(1)} %shard_map.67.refs_0_, bf16[1024,768]{1,0:T(8,128)(2,1)S(1)} %get-tuple-element.22.refs_5_.refs_1_, f32[1024,768]{1,0:T(8,128)S(1)} %get-tuple-element.28.refs_2_.refs_3_), custom_call_target="tpu_custom_call" | custom-call | flops 8053063680 | tf_op jit(solution)/shard_map/pallas_call | solution.py:96
  27.4 1.0 %shard_map.69.refs_2_ = f32[1024,768]{1,0:T(8,128)S(1)} custom-call(bf16[272,768]{1,0:T(8,128)(2,1)S(1)} %shard_map.67.refs_0_, bf16[144,256]{1,0:T(8,128)(2,1)S(1)} %shard_map.68.refs_1_, bf16[400,768]{1,0:T(8,128)(2,1)S(1)} %collective-permute-done.12.refs_2_, f32[1024,768]{1,0:T(8,128)S(1)} %get-tuple-element.28.refs_2_.refs_3_), custom_call_target="tpu_custom_call" | custom-call | flops 402653184 | tf_op jit(solution)/shard_map/pallas_call | solution.py:96
  28.4 0.6 %shard_map.70.refs_1_ = bf16[144,256]{1,0:T(8,128)(2,1)S(1)} custom-call(bf16[272,768]{1,0:T(8,128)(2,1)S(1)} %collective-permute-done.11.refs_0_, bf16[1024,768]{1,0:T(8,128)(2,1)S(1)} %get-tuple-element.22.refs_5_.refs_1_, f32[1024,768]{1,0:T(8,128)S(1)} %shard_map.69.refs_2_), custom_call_target="tpu_custom_call" | custom-call | flops 402653184 | tf_op jit(solution)/shard_map/pallas_call | solution.py:96
  29.0 1.5 %shard_map.71 = (bf16[1024,768]{1,0:T(8,128)(2,1)}, s32[1,128]{1,0:T(1,128)S(1)}) custom-call(bf16[272,768]{1,0:T(8,128)(2,1)S(1)} %collective-permute-done.11.refs_0_, bf16[144,256]{1,0:T(8,128)(2,1)S(1)} %shard_map.70.refs_1_, f32[1024,768]{1,0:T(8,128)S(1)} %shard_map.69.refs_2_), custom_call_target="tpu_custom_call" | custom-call | tf_op jit(solution)/shard_map/pallas_call | solution.py:258
  30.5 1.3 %collective-permute-done.7.refs_2_ = bf16[32,768]{1,0:T(8,128)(2,1)S(1)} collective-permute-done((bf16[32,768]{1,0:T(8,128)(2,1)S(1)}, bf16[32,768]{1,0:T(8,128)(2,1)S(1)}, u32[]{:S(2)}, u32[]{:S(2)}) %collective-permute-start.7) | collective-permute-done | bytes 49184 | tf_op jit(solution)/shard_map/ppermute | solution.py:77
  31.9 0.7 %shard_map.72 = f32[32,768]{1,0:T(8,128)} custom-call(f32[32,768]{1,0:T(8,128)S(1)} %get-tuple-element.29.refs_2_.refs_0_, bf16[32,768]{1,0:T(8,128)(2,1)S(1)} %collective-permute-done.5.refs_1_, bf16[32,768]{1,0:T(8,128)(2,1)S(1)} %collective-permute-done.7.refs_2_, bf16[32,768]{1,0:T(8,128)(2,1)S(1)} %collective-permute-done.8.refs_3_, ...), custom_call_target="tpu_custom_call" | custom-call | tf_op jit(solution)/shard_map/pallas_call | solution.py:96
  (21 shorter events, 0.6 us)
Async XLA Ops:
  0.6 9.0 %collective-permute-start = (bf16[32,768]{1,0:T(8,128)(2,1)}, bf16[32,768]{1,0:T(8,128)(2,1)S(1)}, u32[]{:S(2)}, u32[]{:S(2)}) collective-permute-start(bf16[32,768]{1,0:T(8,128)(2,1)} %refs_0_.1), channel_id=1, source_target_pairs={{0,6},{1,7},{2,4},{3,5},{4,2},{5,3},{6,0},{7,1},{8,14},{9,15},{10,... | collective-permute-start | bytes 147464 | tf_op jit(solution)/shard_map/ppermute | solution.py:77
  5.7 4.3 %collective-permute-start.1 = (bf16[32,768]{1,0:T(8,128)(2,1)}, bf16[32,768]{1,0:T(8,128)(2,1)S(1)}, u32[]{:S(2)}, u32[]{:S(2)}) collective-permute-start(bf16[32,768]{1,0:T(8,128)(2,1)} %refs_0_.1), channel_id=1, source_target_pairs={{0,2},{1,3},{2,0},{3,1},{4,6},{5,7},{6,4},{7,5},{8,10},{9,11},{10,... | collective-permute-start | bytes 147464 | tf_op jit(solution)/shard_map/ppermute | solution.py:77
  5.7 5.5 %collective-permute-start.2 = (bf16[32,768]{1,0:T(8,128)(2,1)}, bf16[32,768]{1,0:T(8,128)(2,1)S(1)}, u32[]{:S(2)}, u32[]{:S(2)}) collective-permute-start(bf16[32,768]{1,0:T(8,128)(2,1)} %refs_0_.1), channel_id=1, source_target_pairs={{0,4},{1,5},{2,6},{3,7},{4,0},{5,1},{6,2},{7,3},{8,12},{9,13},{10,... | collective-permute-start | bytes 147464 | tf_op jit(solution)/shard_map/ppermute | solution.py:77
  7.1 1.4 %copy-start = (bf16[1024,768]{1,0:T(8,128)(2,1)S(1)}, bf16[1024,768]{1,0:T(8,128)(2,1)}, u32[]{:S(2)}) copy-start(bf16[1024,768]{1,0:T(8,128)(2,1)} %refs_1_.1) | copy-start | bytes 4718596
  8.5 0.8 %copy-start.1 = (bf16[32,768]{1,0:T(8,128)(2,1)S(1)}, bf16[32,768]{1,0:T(8,128)(2,1)}, u32[]{:S(2)}) copy-start(bf16[32,768]{1,0:T(8,128)(2,1)} %refs_0_.1) | copy-start | bytes 147460
  11.3 6.7 %collective-permute-start.4 = (bf16[128,768]{1,0:T(8,128)(2,1)S(1)}, bf16[128,768]{1,0:T(8,128)(2,1)S(1)}, u32[]{:S(2)}, u32[]{:S(2)}) collective-permute-start(bf16[128,768]{1,0:T(8,128)(2,1)S(1)} %get-tuple-element.23.refs_0_), channel_id=1, source_target_pairs={{0,1},{1,0},{2,3},{3,2},{4,5},{5,4},{6,7},{7,6},{8,9},{9,8},{10,11... | collective-permute-start | bytes 589832 | tf_op jit(solution)/shard_map/ppermute | solution.py:77
  12.9 13.7 %collective-permute-start.9 = (bf16[144,768]{1,0:T(8,128)(2,1)S(1)}, bf16[144,768]{1,0:T(8,128)(2,1)S(1)}, u32[]{:S(2)}, u32[]{:S(2)}) collective-permute-start(bf16[144,768]{1,0:T(8,128)(2,1)S(1)} %get-tuple-element.35), channel_id=1, source_target_pairs={{0,16},{8,24},{16,0},{24,8},{1,17},{9,25},{17,1},{25,9},{2,18},{10... | collective-permute-start | bytes 663560 | tf_op jit(solution)/shard_map/ppermute | solution.py:77
  15.7 10.9 %collective-permute-start.10 = (bf16[128,768]{1,0:T(8,128)(2,1)S(1)}, bf16[128,768]{1,0:T(8,128)(2,1)S(1)}, u32[]{:S(2)}, u32[]{:S(2)}) collective-permute-start(bf16[128,768]{1,0:T(8,128)(2,1)S(1)} %get-tuple-element.36), channel_id=1, source_target_pairs={{0,17},{1,16},{2,19},{3,18},{4,21},{5,20},{6,23},{7,22},{8,25},{9,... | collective-permute-start | bytes 589832 | tf_op jit(solution)/shard_map/ppermute | solution.py:87
  16.2 5.1 %collective-permute-start.3 = (bf16[64,768]{1,0:T(8,128)(2,1)S(1)}, bf16[64,768]{1,0:T(8,128)(2,1)S(1)}, u32[]{:S(2)}, u32[]{:S(2)}) collective-permute-start(bf16[64,768]{1,0:T(8,128)(2,1)S(1)} %get-tuple-element.25), channel_id=1, source_target_pairs={{0,2},{1,3},{2,0},{3,1},{4,6},{5,7},{6,4},{7,5},{8,10},{9,11},{10,... | collective-permute-start | bytes 294920 | tf_op jit(solution)/shard_map/ppermute | solution.py:77
  19.3 4.7 %collective-permute-start.6 = (bf16[64,768]{1,0:T(8,128)(2,1)S(1)}, bf16[64,768]{1,0:T(8,128)(2,1)S(1)}, u32[]{:S(2)}, u32[]{:S(2)}) collective-permute-start(bf16[64,768]{1,0:T(8,128)(2,1)S(1)} %get-tuple-element.32), channel_id=1, source_target_pairs={{0,2},{1,3},{2,0},{3,1},{4,6},{5,7},{6,4},{7,5},{8,10},{9,11},{10,... | collective-permute-start | bytes 294920 | tf_op jit(solution)/shard_map/ppermute | solution.py:77
  21.3 6.1 %collective-permute-start.12 = (bf16[400,768]{1,0:T(8,128)(2,1)S(1)}, bf16[400,768]{1,0:T(8,128)(2,1)S(1)}, u32[]{:S(2)}, u32[]{:S(2)}) collective-permute-start(bf16[400,768]{1,0:T(8,128)(2,1)S(1)} %get-tuple-element.37), channel_id=1, source_target_pairs={{0,8},{8,0},{16,24},{24,16},{1,9},{9,1},{17,25},{25,17},{2,10},{10... | collective-permute-start | bytes 1843208 | tf_op jit(solution)/shard_map/ppermute | solution.py:77
  21.4 9.1 %collective-permute-start.5 = (bf16[32,768]{1,0:T(8,128)(2,1)S(1)}, bf16[32,768]{1,0:T(8,128)(2,1)S(1)}, u32[]{:S(2)}, u32[]{:S(2)}) collective-permute-start(bf16[32,768]{1,0:T(8,128)(2,1)S(1)} %get-tuple-element.30), channel_id=1, source_target_pairs={{0,4},{1,5},{2,6},{3,7},{4,0},{5,1},{6,2},{7,3},{8,12},{9,13},{10,... | collective-permute-start | bytes 147464 | tf_op jit(solution)/shard_map/ppermute | solution.py:77
  24.0 7.9 %collective-permute-start.8 = (bf16[32,768]{1,0:T(8,128)(2,1)S(1)}, bf16[32,768]{1,0:T(8,128)(2,1)S(1)}, u32[]{:S(2)}, u32[]{:S(2)}) collective-permute-start(bf16[32,768]{1,0:T(8,128)(2,1)S(1)} %get-tuple-element.34.refs_2_), channel_id=1, source_target_pairs={{0,5},{1,4},{2,7},{3,6},{4,1},{5,0},{6,3},{7,2},{8,13},{9,12},{10,... | collective-permute-start | bytes 147464 | tf_op jit(solution)/shard_map/ppermute | solution.py:77
  26.6 1.8 %collective-permute-start.11 = (bf16[272,768]{1,0:T(8,128)(2,1)S(1)}, bf16[272,768]{1,0:T(8,128)(2,1)S(1)}, u32[]{:S(2)}, u32[]{:S(2)}) collective-permute-start(bf16[272,768]{1,0:T(8,128)(2,1)S(1)} %shard_map.67.refs_0_), channel_id=1, source_target_pairs={{0,8},{8,0},{16,24},{24,16},{1,9},{9,1},{17,25},{25,17},{2,10},{10... | collective-permute-start | bytes 1253384 | tf_op jit(solution)/shard_map/ppermute | solution.py:77
  26.7 5.2 %collective-permute-start.7 = (bf16[32,768]{1,0:T(8,128)(2,1)S(1)}, bf16[32,768]{1,0:T(8,128)(2,1)S(1)}, u32[]{:S(2)}, u32[]{:S(2)}) collective-permute-start(bf16[32,768]{1,0:T(8,128)(2,1)S(1)} %get-tuple-element.33), channel_id=1, source_target_pairs={{0,1},{1,0},{2,3},{3,2},{4,5},{5,4},{6,7},{7,6},{8,9},{9,8},{10,11... | collective-permute-start | bytes 147464 | tf_op jit(solution)/shard_map/ppermute | solution.py:77
